TPU v7x, 32 devices: a whole 2x2x4 slice. The times are simulated.
32 devices in a mesh: seq: 8 (over z, y), head: 4 (over x, core).
Axes of the slice: x: 2, y: 2, z: 4, core: 2. Of those that a mesh axis runs over, the one named last changes fastest.
Arguments:
- queries: bfloat16 [1024, 2048], P('seq', 'head'), may hold values from -1.25 to 1.25
- key_vectors: bfloat16 [1024, 2048], P('seq', 'head'), may hold values from -1.25 to 1.25
- value_vectors: bfloat16 [1024, 2048], P('seq', 'head'), may hold values from -4 to 4
- feature_proj: bfloat16 [16, 128, 256], P('head'), may hold values from -2.5 to 2.5
- out_weight: bfloat16 [2048, 2048], P('head'), may hold values from -0.1875 to 0.1875
- grad_output: bfloat16 [1024, 2048], P('seq', 'head'), may hold values from -4 to 4
Outputs:
- layer_out: bfloat16 [1024, 2048], P('seq', 'head')
- grad_queries: bfloat16 [1024, 2048], P('seq', 'head')
- grad_keys: bfloat16 [1024, 2048], P('seq', 'head')
- grad_values: bfloat16 [1024, 2048], P('seq', 'head')
All inputs are finite; a program needn't handle non-finite values.
Results may differ from a plain program's by a relative error of at most 0.025.
Values may be sent and summed in bfloat16 or wider, within the bound.
No kernel may reach another device: no remote copies, remote signals or barrier semaphores. Data moves between devices by JAX's collectives and lax.ppermute only.
A program may use at most 128 MiB of HBM per device.

v0:
```python
import jax
import jax.numpy as jnp
from jax import lax
from jax.sharding import PartitionSpec as P

BLOCK = 128


epsilon = 1e-05


def entering(array, axis, combine, identity, reverse):
    devices, here = (lax.axis_size(axis), lax.axis_index(axis))
    everything = lax.all_gather(array, axis)
    start = jnp.broadcast_to(jnp.asarray(identity, array.dtype), array.shape)

    def hop(k, before):
        at = devices - 1 - k if reverse else k
        reached = at > here if reverse else at < here
        new = combine(before, everything[at])
        return jnp.where(reached, new, before)

    return lax.fori_loop(0, devices, hop, start)


def lower_mask(width):
    row_ids = lax.broadcasted_iota(jnp.int32, (width, width), 0)
    col_ids = lax.broadcasted_iota(jnp.int32, (width, width), 1)
    return col_ids <= row_ids


def add_arrays(earlier, after_part):
    return earlier + after_part


def key_states(key_feats, value_blocks):
    states = jnp.einsum(
        "hncm,hncd->hnmd", key_feats, value_blocks, preferred_element_type=jnp.float32
    )
    running = jnp.cumsum(states, axis=1)
    before_sum = jnp.concatenate([jnp.zeros_like(states), running[:, :-1]], axis=1)
    return (before_sum, running[:, -1])


def head_major(matrix, head_count, head_width):
    tok_rows = matrix.shape[0]
    return jnp.transpose(matrix.reshape(tok_rows, head_count, head_width), (1, 0, 2))


def token_major(stacked):
    head_count, tok_rows, head_width = stacked.shape
    return jnp.transpose(stacked, (1, 0, 2)).reshape(tok_rows, head_count * head_width)


def local(queries, key_vectors, value_vectors, feature_proj, out_weight, grad_output):
    head_count = feature_proj.shape[0]
    head_width = feature_proj.shape[1]
    feat_count = feature_proj.shape[2]
    tok_rows = queries.shape[0]
    n_blocks = tok_rows // BLOCK
    feat_scale = head_width ** (-0.25)
    causal = lower_mask(BLOCK)[None, None]
    q_heads = head_major(queries, head_count, head_width)
    k_heads = head_major(key_vectors, head_count, head_width)
    v_blocks = head_major(value_vectors, head_count, head_width).reshape(
        head_count, n_blocks, BLOCK, head_width
    )
    q_feat32 = jnp.exp(
        jnp.einsum("htd,hdm->htm", q_heads, feature_proj, preferred_element_type=jnp.float32)
        * feat_scale
    )
    k_wide = k_heads.astype(jnp.float32)
    half_sq = jnp.sum(k_wide * k_wide, axis=2, keepdims=True) * (feat_scale * feat_scale * 0.5)
    k_logits = jnp.einsum("htd,hdm->htm", k_heads, feature_proj, preferred_element_type=jnp.float32)
    k_feat32 = jnp.exp(k_logits * feat_scale - half_sq)
    q_feat = q_feat32.astype(jnp.bfloat16).reshape(head_count, n_blocks, BLOCK, feat_count)
    k_feat = k_feat32.astype(jnp.bfloat16).reshape(head_count, n_blocks, BLOCK, feat_count)
    before_sum, local_total = key_states(k_feat, v_blocks)
    prefix_sum = entering(local_total, "seq", add_arrays, jnp.zeros_like(local_total), False)
    carried_b = (prefix_sum[:, None] + before_sum).astype(jnp.bfloat16)
    scores = jnp.einsum("hnim,hnjm->hnij", q_feat, k_feat, preferred_element_type=jnp.float32)
    scores_b = jnp.where(causal, scores, 0.0).astype(jnp.bfloat16)
    numerator = jnp.einsum(
        "hnij,hnjd->hnid", scores_b, v_blocks, preferred_element_type=jnp.float32
    )
    numerator = numerator + jnp.einsum(
        "hnim,hnmd->hnid", q_feat, carried_b, preferred_element_type=jnp.float32
    )
    row_root = jnp.sqrt(jnp.mean(numerator * numerator, axis=3, keepdims=True) + epsilon)
    normed = numerator / row_root
    mixed = token_major(normed.astype(jnp.bfloat16).reshape(head_count, tok_rows, head_width))
    slabs = lax.all_to_all(out_weight, "head", split_axis=1, concat_axis=0, tiled=True)
    w_part = slabs
    layer_out = jnp.dot(
        lax.all_gather(mixed, "head", axis=1, tiled=True),
        w_part,
        preferred_element_type=jnp.float32,
    ).astype(jnp.bfloat16)
    w_part = out_weight
    grad_flat = lax.dot_general(
        lax.all_gather(grad_output, "head", axis=1, tiled=True),
        w_part,
        (((1,), (1,)), ((), ())),
        preferred_element_type=jnp.float32,
    )
    grad_mixed = head_major(grad_flat, head_count, head_width).reshape(
        head_count, n_blocks, BLOCK, head_width
    )
    grad_numer = (
        (grad_mixed - normed * jnp.mean(grad_mixed * normed, axis=3, keepdims=True)) / row_root
    ).astype(jnp.bfloat16)
    later_terms = jnp.einsum(
        "hnim,hnid->hnmd", q_feat, grad_numer, preferred_element_type=jnp.float32
    )
    backward_sum = jnp.cumsum(later_terms[:, ::-1], axis=1)[:, ::-1]
    after_local = jnp.concatenate([backward_sum[:, 1:], jnp.zeros_like(later_terms)], axis=1)
    suffix_sum = entering(
        backward_sum[:, 0], "seq", add_arrays, jnp.zeros_like(backward_sum[:, 0]), True
    )
    after_b = (suffix_sum[:, None] + after_local).astype(jnp.bfloat16)
    grad_scores = jnp.einsum(
        "hnid,hnjd->hnij", grad_numer, v_blocks, preferred_element_type=jnp.float32
    )
    grad_scores = jnp.where(causal, grad_scores, 0.0).astype(jnp.bfloat16)
    grad_v = jnp.einsum("hnij,hnid->hnjd", scores_b, grad_numer, preferred_element_type=jnp.float32)
    grad_v = grad_v + jnp.einsum(
        "hnjm,hnmd->hnjd", k_feat, after_b, preferred_element_type=jnp.float32
    )
    grad_qf = jnp.einsum("hnij,hnjm->hnim", grad_scores, k_feat, preferred_element_type=jnp.float32)
    grad_qf = grad_qf + jnp.einsum(
        "hnid,hnmd->hnim", grad_numer, carried_b, preferred_element_type=jnp.float32
    )
    grad_kf = jnp.einsum("hnij,hnim->hnjm", grad_scores, q_feat, preferred_element_type=jnp.float32)
    grad_kf = grad_kf + jnp.einsum(
        "hnjd,hnmd->hnjm", v_blocks, after_b, preferred_element_type=jnp.float32
    )
    query_terms = (grad_qf.reshape(head_count, tok_rows, feat_count) * q_feat32).astype(
        jnp.bfloat16
    )
    key_terms = (grad_kf.reshape(head_count, tok_rows, feat_count) * k_feat32).astype(jnp.bfloat16)
    grad_q = (
        jnp.einsum("htm,hdm->htd", query_terms, feature_proj, preferred_element_type=jnp.float32)
        * feat_scale
    )
    key_total = jnp.sum(key_terms.astype(jnp.float32), axis=2, keepdims=True)
    grad_k = (
        jnp.einsum("htm,hdm->htd", key_terms, feature_proj, preferred_element_type=jnp.float32)
        * feat_scale
    )
    grad_k = grad_k - key_total * k_wide * (feat_scale * feat_scale)
    return (
        layer_out,
        token_major(grad_q.astype(jnp.bfloat16)),
        token_major(grad_k.astype(jnp.bfloat16)),
        token_major(grad_v.reshape(head_count, tok_rows, head_width).astype(jnp.bfloat16)),
    )


def solution(mesh):
    placed = (
        P("seq", "head"),
        P("seq", "head"),
        P("seq", "head"),
        P("head", None, None),
        P("head", None),
        P("seq", "head"),
    )
    return jax.shard_map(
        local,
        mesh=mesh,
        in_specs=placed,
        out_specs=(P("seq", "head"), P("seq", "head"), P("seq", "head"), P("seq", "head")),
        check_vma=False,
    )
```

profile of v0, /device:TPU:0, one launch (start us, length us, event | category | flops | bytes accessed | tf_op | source)
XLA Modules:
  0.0 193.4 jit_solution(14623215960825400027)
XLA Ops:
  7.2 1.1 copy.65
  8.4 1.1 fusion.33
  9.5 2.1 %fusion.18 = f32[4,256,128]{2,1,0:T(8,128)} fusion(bf16[4,128,256]{2,1,0:T(8,128)(2,1)S(1)} %get-tuple-element.261, bf16[128,512]{1,0:T(8,128)(2,1)} %param.12), kind=kOutput, calls=%fused_computation.37 | convolution fusion | flops 33554432 | bytes 917504 | tf_op jit(solution)/shard_map/hncm,hncd->hnmd/dot_general | solution.py:37
  11.7 9.1 %all_gather.14 = bf16[128,2048]{1,0:T(8,128)(2,1)} all-gather(bf16[128,512]{1,0:T(8,128)(2,1)S(1)} %copy-done.16), channel_id=1, replica_groups=mesh['seq'=8,'head'=4] {'head'}, dimensions={1}, use_global_device_ids=true | all-gather | bytes 655360 | tf_op jit(solution)/shard_map/all_gather | solution.py:101
  20.8 1.0 fusion.32
  22.4 65.5 %all-gather.5.cloned.1.call-done = f32[32,256,128]{2,1,0:T(8,128)} async-done(((f32[4,256,128]{2,1,0:T(8,128)}), f32[32,256,128]{2,1,0:T(8,128)}) %all-gather.5.cloned.1.call-update) | async-done | bytes 4194320 | tf_op jit(solution)/shard_map/all_gather | solution.py:14
  87.9 10.1 %while.30 = (s32[]{:T(128)}, f32[4,256,128]{2,1,0:T(8,128)S(1)}, s32[]{:T(128)}, f32[8,4,256,128]{3,2,1,0:T(8,128)}, s32[]{:T(128)}, /*index=5*/s32[]{:T(128)}) while((s32[]{:T(128)}, f32[4,256,128]{2,1,0:T(8,128)S(1)}, s32[]{:T(128)}, f32[8,4,256,128]{3,2,1,0:T(8,128)}, s32[]{:T(128)}, /*index=5*/s32[]{:T(128)}) %tuple.92), condition=%wide.region_2.3_spmd.clone, body=%wide.region_1.0_spmd.clone.sunk | while | flops 393220 | bytes 1572965 | solution.py:23
  87.9 1.4 add_select_fusion.4
  89.3 1.2 add_select_fusion.4
  90.5 1.2 add_select_fusion.4
  91.8 1.2 add_select_fusion.4
  93.0 1.2 add_select_fusion.4
  94.2 1.2 add_select_fusion.4
  95.5 1.2 add_select_fusion.4
  96.7 1.2 add_select_fusion.4
  97.9 0.3 multiply_reduce_fusion.1
  98.2 0.6 add_sqrt_fusion
  98.9 1.8 multiply_reduce_fusion
  100.7 1.1 fusion.36
  101.8 2.5 %copy.71 = bf16[512,2048]{0,1:T(8,128)(2,1)} copy(bf16[512,2048]{1,0:T(8,128)(2,1)S(1)} %copy-done.1) | data formatting | bytes 4194304 | tf_op args[4]
  104.4 3.6 %all-to-all-start = ((bf16[512,4,512]{0,2,1:T(8,128)(2,1)}), bf16[512,4,512]{0,2,1:T(8,128)(2,1)S(1)}, u32[]{:S(2)}, u32[]{:S(2)}) async-start(bf16[512,4,512]{0,2,1:T(8,128)(2,1)} %bitcast.124), calls=%async_computation | async-start | bytes 4194304 | tf_op jit(solution)/shard_map/all_to_all | solution.py:92
  108.0 25.7 %all-to-all-done = bf16[512,4,512]{0,2,1:T(8,128)(2,1)S(1)} async-done(((bf16[512,4,512]{0,2,1:T(8,128)(2,1)}), bf16[512,4,512]{0,2,1:T(8,128)(2,1)S(1)}, u32[]{:S(2)}, u32[]{:S(2)}) %all-to-all-start) | async-done | bytes 2097184 | tf_op jit(solution)/shard_map/all_to_all | solution.py:92
  133.7 1.3 copy-done.2
  135.0 2.8 %copy.72 = bf16[4,512,512]{2,1,0:T(8,128)(2,1)S(1)} copy(bf16[4,512,512]{1,2,0:T(8,128)(2,1)} %bitcast.123) | data formatting | bytes 4194304 | tf_op jit(solution)/shard_map/all_to_all | solution.py:92
  137.8 1.1 fusion.13
  139.0 0.6 copy-done.15
  139.6 2.0 %fusion.34 = f32[4,128,256]{2,1,0:T(8,128)} fusion(bf16[4,128,128]{2,1,0:T(8,128)(2,1)S(1)} %fusion.13, bf16[4,128,256]{2,1,0:T(8,128)(2,1)} %copy-done.4), kind=kOutput, calls=%fused_computation.58 | convolution fusion | flops 33554432 | bytes 917504 | tf_op jit(solution)/shard_map/hnij,hnjm->hnim/dot_general | solution.py:129
  141.6 2.3 %fusion.16 = bf16[4,128,128]{1,2,0:T(8,128)(2,1)} fusion(bf16[4,128,256]{2,1,0:T(8,128)(2,1)S(1)} %copy-done, f32[4,128,256]{2,1,0:T(8,128)} %get-tuple-element.260, f32[4,128,256]{2,1,0:T(8,128)} %fusion.34, bf16[4,128,128]{1,2,0:T(8,128)(2,1)S(1)} %divide_convert_fusion, f32[4,256,128]{2,1,0:T(8,128)S(1)} %get-tuple-element.193), kind=kOutput, calls=%fused_computation.28 | convolution fusion | flops 67764224 | bytes 2097152 | tf_op jit(solution)/shard_map/htm,hdm->htd/dot_general | solution.py:142
  143.9 1.7 copy.81
  145.6 1.0 fusion.17
  146.6 6.6 %all_gather.13 = bf16[128,2048]{0,1:T(8,128)(2,1)S(1)} all-gather(bf16[128,512]{0,1:T(8,128)(2,1)S(1)} %bitcast.129), channel_id=1, replica_groups=mesh['seq'=8,'head'=4] {'head'}, dimensions={1}, use_global_device_ids=true | all-gather | bytes 655360 | tf_op jit(solution)/shard_map/all_gather | solution.py:95
  153.2 2.1 %fusion.35 = f32[4,128,256]{2,1,0:T(8,128)} fusion(bf16[4,128,128]{2,1,0:T(8,128)(2,1)} %copy-done.15, bf16[4,128,256]{2,1,0:T(8,128)(2,1)} %copy-done.3), kind=kOutput, calls=%fused_computation.59 | convolution fusion | flops 33554432 | bytes 917504 | tf_op jit(solution)/shard_map/hnij,hnim->hnjm/dot_general | solution.py:133
  155.3 1.1 convolution_convert_fusion
  156.4 17.3 %all-gather.7.cloned.1.call-done = f32[32,256,128]{2,1,0:T(8,128)} async-done(((f32[4,256,128]{2,1,0:T(8,128)}), f32[32,256,128]{2,1,0:T(8,128)}) %all-gather.7.cloned.1.call-update) | async-done | bytes 4194320 | tf_op jit(solution)/shard_map/all_gather | solution.py:14
  173.7 10.1 %while.31 = (s32[]{:T(128)}, f32[4,256,128]{2,1,0:T(8,128)S(1)}, s32[]{:T(128)}, f32[8,4,256,128]{3,2,1,0:T(8,128)}, s32[]{:T(128)}, /*index=5*/s32[]{:T(128)}, s32[]{:T(128)}, s32[]{:T(128)}) while((s32[]{:T(128)}, f32[4,256,128]{2,1,0:T(8,128)S(1)}, s32[]{:T(128)}, f32[8,4,256,128]{3,2,1,0:T(8,128)}, s32[]{:T(128)}, ...), condition=%wide.region_6.7_spmd.clone, body=%wide.region_5.6_spmd.clone.sunk | while | flops 393224 | bytes 1573027 | solution.py:23
  173.7 1.3 add_select_fusion.5
  175.0 1.2 add_select_fusion.5
  176.3 1.2 add_select_fusion.5
  177.5 1.2 add_select_fusion.5
  178.8 1.2 add_select_fusion.5
  180.0 1.2 add_select_fusion.5
  181.3 1.2 add_select_fusion.5
  182.5 1.2 add_select_fusion.5
  183.8 0.3 fusion.21
  184.1 0.3 convert_reduce_fusion
  184.4 0.3 copy-done.12
  184.9 0.8 copy.82
  185.8 0.8 copy.83
  (50 shorter events, 1.2 us)
Async XLA Ops:
  7.2 1.2 copy-start
  7.2 4.5 %copy-start.16 = (bf16[128,512]{1,0:T(8,128)(2,1)S(1)}, bf16[128,512]{1,0:T(8,128)(2,1)}, u32[]{:S(2)}) copy-start(bf16[128,512]{1,0:T(8,128)(2,1)} %param.15) | copy-start | bytes 393220
  7.2 13.6 %copy-start.17 = (bf16[128,512]{1,0:T(8,128)(2,1)S(1)}, bf16[128,512]{1,0:T(8,128)(2,1)}, u32[]{:S(2)}) copy-start(bf16[128,512]{1,0:T(8,128)(2,1)} %param.10) | copy-start | bytes 393220
  7.2 80.7 %all-gather.5.cloned.1.call-start = ((), (), s32[]{:S(2)}) async-start(), calls=%async_computation.1 | async-start | bytes 4718592 | tf_op jit(solution)/shard_map/all_gather | solution.py:14
  8.3 3.3 %copy-start.11 = (bf16[128,512]{0,1:T(8,128)(2,1)}, bf16[128,512]{0,1:T(8,128)(2,1)S(1)}, u32[]{:S(2)}) copy-start(bf16[128,512]{0,1:T(8,128)(2,1)S(1)} %copy.65) | copy-start | bytes 393220
  9.5 12.8 %copy-start.4 = (bf16[4,128,256]{2,1,0:T(8,128)(2,1)}, bf16[4,128,256]{2,1,0:T(8,128)(2,1)S(1)}, u32[]{:S(2)}) copy-start(bf16[4,128,256]{2,1,0:T(8,128)(2,1)S(1)} %get-tuple-element.261) | copy-start | bytes 786436
  9.5 12.6 %copy-start.9 = (bf16[128,512]{1,0:T(8,128)(2,1)S(1)}, bf16[128,512]{1,0:T(8,128)(2,1)}, u32[]{:S(2)}) copy-start(bf16[128,512]{1,0:T(8,128)(2,1)} %param.12) | copy-start | bytes 393220
  11.6 162.0 %all-gather.7.cloned.1.call-start = ((), (), s32[]{:S(2)}) async-start(), calls=%async_computation.2 | async-start | bytes 4718592 | tf_op jit(solution)/shard_map/all_gather | solution.py:14
  21.8 78.9 %copy-start.3 = (bf16[4,128,256]{2,1,0:T(8,128)(2,1)}, bf16[4,128,256]{2,1,0:T(8,128)(2,1)S(1)}, u32[]{:S(2)}) copy-start(bf16[4,128,256]{2,1,0:T(8,128)(2,1)S(1)} %get-tuple-element.259) | copy-start | bytes 786436
  22.1 65.8 %copy-start.13 = (bf16[4,128,128]{2,1,0:T(8,128)(2,1)}, bf16[4,128,128]{2,1,0:T(8,128)(2,1)S(1)}, u32[]{:S(2)}) copy-start(bf16[4,128,128]{2,1,0:T(8,128)(2,1)S(1)} %fusion.12) | copy-start | bytes 393220
  87.9 11.0 %copy-start.1 = (bf16[512,2048]{1,0:T(8,128)(2,1)S(1)}, bf16[512,2048]{1,0:T(8,128)(2,1)}, u32[]{:S(2)}) copy-start(bf16[512,2048]{1,0:T(8,128)(2,1)} %param.14) | copy-start | bytes 6291460
  98.2 2.4 %copy-start.6 = (f32[4,128,128]{1,2,0:T(8,128)}, f32[4,128,128]{1,2,0:T(8,128)S(1)}, u32[]{:S(2)}) copy-start(f32[4,128,128]{1,2,0:T(8,128)S(1)} %get-tuple-element.264) | copy-start | bytes 786436
  104.4 29.3 %all-to-all-start = ((bf16[512,4,512]{0,2,1:T(8,128)(2,1)}), bf16[512,4,512]{0,2,1:T(8,128)(2,1)S(1)}, u32[]{:S(2)}, u32[]{:S(2)}) async-start(bf16[512,4,512]{0,2,1:T(8,128)(2,1)} %bitcast.124), calls=%async_computation | async-start | bytes 4194304 | tf_op jit(solution)/shard_map/all_to_all | solution.py:92
  133.7 1.3 copy-start.2
  139.0 0.7 copy-start.15
  139.6 6.0 %copy-start.18 = (f32[128,4]{0,1:T(4,128)S(1)}, f32[128,4]{0,1:T(4,128)}, u32[]{:S(2)}) copy-start(f32[128,4]{0,1:T(4,128)} %get-tuple-element.258) | copy-start | bytes 6148
  173.7 10.1 %copy-start.5 = (bf16[4,128,256]{2,1,0:T(8,128)(2,1)S(1)}, bf16[4,128,256]{2,1,0:T(8,128)(2,1)}, u32[]{:S(2)}) copy-start(bf16[4,128,256]{2,1,0:T(8,128)(2,1)} %copy-done.4) | copy-start | bytes 786436
  173.7 10.4 %copy-start.7 = (f32[4,128,256]{2,1,0:T(8,128)S(1)}, f32[4,128,256]{2,1,0:T(8,128)}, u32[]{:S(2)}) copy-start(f32[4,128,256]{2,1,0:T(8,128)} %fusion.35) | copy-start | bytes 1572868
  173.7 10.4 %copy-start.8 = (f32[4,128,256]{2,1,0:T(8,128)S(1)}, f32[4,128,256]{2,1,0:T(8,128)}, u32[]{:S(2)}) copy-start(f32[4,128,256]{2,1,0:T(8,128)} %get-tuple-element.262) | copy-start | bytes 1572868
  173.7 10.4 %copy-start.10 = (bf16[128,512]{1,0:T(8,128)(2,1)S(1)}, bf16[128,512]{1,0:T(8,128)(2,1)}, u32[]{:S(2)}) copy-start(bf16[128,512]{1,0:T(8,128)(2,1)} %param.12) | copy-start | bytes 393220
  183.7 0.9 copy-start.12
  183.7 1.9 copy-start.14
Sparse Core Ops, SparseCore 0:
  11.8 76.0 all-gather.4
  102.0 71.6 all-gather.6
where the time goes:
time: 195 us; the launch traced here: 193 us
  waiting for transfers between devices  108 us (55%)
  other arithmetic  21.5 us (11%)
  matrix products  17.4 us (9%)
  blocking collectives  15.7 us (8%)
  between operations  14.3 us (7%)
  local copies, waits for them, and re-layouts  11.9 us (6%)
  starting transfers between devices  3.72 us (2%)
    all_gather x2, waiting for transfers between devices, entering(): everything = lax.all_gather(array, axis)  82.8 us
    all_to_all x1, waiting for transfers between devices, local(): lax.all_to_all(out_weight, 'head', split_axis=1, concat_axis=0, tiled=True)  25.7 us
    select_n x16, other arithmetic, hop(): return jnp.where(reached, new, before)  19.7 us
    unnamed x43, local copies, waits for them, and re-layouts  9.14 us
    all_gather x1, blocking collectives, local(): lax.all_gather(grad_output, 'head', axis=1, tiled=True)  9.08 us
    all_gather x1, blocking collectives, local(): lax.all_gather(mixed, 'head', axis=1, tiled=True)  6.63 us
  transfers between devices with their start and end apart: 3, of which 3 were waited for; matrix products, arithmetic and copies ran while one was open for 9% of the time, Pallas kernels for 0%

commit v1 on v0

v1 whole, which is shorter than its diff:
```python
import functools

import jax
import jax.numpy as jnp
from jax import lax
from jax.experimental import pallas as pl
from jax.experimental.pallas import tpu as pltpu
from jax.sharding import PartitionSpec as P

EPSILON = 1e-05
VMEM = pl.BlockSpec(memory_space=pltpu.VMEM)
SMEM = pl.BlockSpec(memory_space=pltpu.SMEM)
NN = (((1,), (0,)), ((), ()))
NT = (((1,), (1,)), ((), ()))
TN = (((0,), (0,)), ((), ()))


def mm(a, b, dims=NN):
    return lax.dot_general(a, b, dims, preferred_element_type=jnp.float32)


def bf(x):
    return x.astype(jnp.bfloat16)


def call(body, outs, *args, flops=0, specs=None):
    size = sum(a.size * a.dtype.itemsize for a in args)
    size += sum(o.size * o.dtype.itemsize for o in outs)
    return pl.pallas_call(
        body,
        out_shape=outs,
        in_specs=specs or [VMEM] * len(args),
        out_specs=[VMEM] * len(outs),
        cost_estimate=pl.CostEstimate(flops=flops, bytes_accessed=size, transcendentals=0),
        compiler_params=pltpu.CompilerParams(vmem_limit_bytes=32 * 1024 * 1024),
    )(*args)


def struct(shape, dtype=jnp.bfloat16):
    return jax.ShapeDtypeStruct(shape, dtype)


def causal_mask(rows):
    row = lax.broadcasted_iota(jnp.int32, (rows, rows), 0)
    col = lax.broadcasted_iota(jnp.int32, (rows, rows), 1)
    return col <= row


def key_kernel(heads, k_ref, v_ref, om_ref, kf_ref, state_ref):
    dim, feats = om_ref.shape[1:]
    scale = dim ** (-0.25)
    for h in range(heads):
        cols, fcols = pl.ds(h * dim, dim), pl.ds(h * feats, feats)
        k = k_ref[:, cols]
        wide = k.astype(jnp.float32)
        half_sq = jnp.sum(wide * wide, axis=1, keepdims=True) * (scale * scale * 0.5)
        kf = bf(jnp.exp(mm(k, om_ref[h]) * scale - half_sq))
        kf_ref[:, fcols] = kf
        state_ref[cols, :] = bf(mm(v_ref[:, cols], kf, TN))


def local_kernel(heads, offsets, me_ref, q_ref, v_ref, om_ref, kf_ref, go_ref, w_ref,
                 qf_ref, scores_ref, num_ref, gm_ref):
    rows = q_ref.shape[0]
    dim, feats = om_ref.shape[1:]
    width = go_ref.shape[2]
    scale = dim ** (-0.25)
    causal = causal_mask(rows)
    for h in range(heads):
        cols, fcols = pl.ds(h * dim, dim), pl.ds(h * feats, feats)
        qf = bf(jnp.exp(mm(q_ref[:, cols], om_ref[h]) * scale))
        qf_ref[:, fcols] = qf
        scores = bf(jnp.where(causal, mm(qf, kf_ref[:, fcols], NT), 0.0))
        scores_ref[h] = scores
        num_ref[:, cols] = mm(scores, v_ref[:, cols])
    total = None
    for at, offset in enumerate(offsets):
        block = me_ref[0] ^ offset
        part = mm(go_ref[at], w_ref[:, pl.ds(pl.multiple_of(block * width, 128), width)], NT)
        total = part if total is None else total + part
    gm_ref[...] = total


def middle_kernel(heads, qf_ref, num_ref, gm_ref, carried_ref, mixed_ref, gn_ref, later_ref):
    dim = carried_ref.shape[0] // heads
    feats = carried_ref.shape[1]
    for h in range(heads):
        cols, fcols = pl.ds(h * dim, dim), pl.ds(h * feats, feats)
        qf = qf_ref[:, fcols]
        num = num_ref[:, cols] + mm(qf, carried_ref[cols, :], NT)
        inv = lax.rsqrt(jnp.mean(num * num, axis=1, keepdims=True) + EPSILON)
        normed = num * inv
        mixed_ref[:, cols] = bf(normed)
        gm = gm_ref[:, cols]
        gn = bf((gm - normed * jnp.mean(gm * normed, axis=1, keepdims=True)) * inv)
        gn_ref[:, cols] = gn
        later_ref[cols, :] = bf(mm(gn, qf, TN))


def project_kernel(offsets, me_ref, mixed_ref, w_ref, own_ref, sent_ref):
    width = own_ref.shape[2]
    half = len(offsets) // 2
    mixed = mixed_ref[...]
    for at, offset in enumerate(offsets):
        block = me_ref[0] ^ offset
        part = bf(mm(mixed, w_ref[:, pl.ds(pl.multiple_of(block * width, 128), width)]))
        if at < half:
            own_ref[at] = part
        else:
            sent_ref[at - half] = part


def query_kernel(heads, qf_ref, kf_ref, v_ref, om_ref, scores_ref, gn_ref, carried_ref,
                 gq_ref, gv_ref, gkf_ref):
    rows = qf_ref.shape[0]
    dim, feats = om_ref.shape[1:]
    scale = dim ** (-0.25)
    causal = causal_mask(rows)
    for h in range(heads):
        cols, fcols = pl.ds(h * dim, dim), pl.ds(h * feats, feats)
        qf, kf, gn = qf_ref[:, fcols], kf_ref[:, fcols], gn_ref[:, cols]
        gs = bf(jnp.where(causal, mm(gn, v_ref[:, cols], NT), 0.0))
        gqf = mm(gs, kf) + mm(gn, carried_ref[cols, :])
        terms = bf(gqf * qf.astype(jnp.float32))
        gq_ref[:, cols] = bf(mm(terms, om_ref[h], NT) * scale)
        gv_ref[:, cols] = mm(scores_ref[h], gn, TN)
        gkf_ref[:, fcols] = mm(gs, qf, TN)


def last_kernel(heads, k_ref, v_ref, om_ref, kf_ref, gv_in_ref, gkf_ref, after_ref,
                gk_ref, gv_ref):
    dim, feats = om_ref.shape[1:]
    scale = dim ** (-0.25)
    for h in range(heads):
        cols, fcols = pl.ds(h * dim, dim), pl.ds(h * feats, feats)
        kf, after = kf_ref[:, fcols], after_ref[cols, :]
        gv_ref[:, cols] = bf(gv_in_ref[:, cols] + mm(kf, after, NT))
        gkf = gkf_ref[:, fcols] + mm(v_ref[:, cols], after)
        terms = bf(gkf * kf.astype(jnp.float32))
        total = jnp.sum(terms.astype(jnp.float32), axis=1, keepdims=True)
        wide = k_ref[:, cols].astype(jnp.float32)
        gk_ref[:, cols] = bf(
            mm(terms, om_ref[h], NT) * scale - total * wide * (scale * scale)
        )


def prefix_kernel(in_ref, out_ref):
    total = jnp.zeros(in_ref.shape[1:], jnp.float32)
    for at in range(in_ref.shape[0]):
        out_ref[at] = bf(total)
        total = total + in_ref[at].astype(jnp.float32)


def swap(array, axis, bit):
    size = lax.axis_size(axis)
    return lax.ppermute(array, axis, [(i, i ^ bit) for i in range(size)])


def bits_of(size):
    return [1 << b for b in range(size.bit_length() - 1)]


def before(state, axis):
    size = lax.axis_size(axis)
    parts = state.reshape((size, state.shape[0] // size) + state.shape[1:])
    mine = lax.all_to_all(parts, axis, 0, 0)
    (sums,) = call(prefix_kernel, [struct(mine.shape)], mine)
    return lax.all_to_all(sums, axis, 0, 0).reshape(state.shape)


def after(state, axis):
    size = lax.axis_size(axis)
    step, inclusive, exclusive = 1, state.astype(jnp.float32), None
    while step < size:
        got = lax.ppermute(
            bf(inclusive), axis, [(i, i - step) for i in range(step, size)]
        ).astype(jnp.float32)
        exclusive = got if exclusive is None else exclusive + got
        inclusive = inclusive + got
        step *= 2
    return bf(exclusive)


def local(queries, key_vectors, value_vectors, feature_proj, out_weight, grad_output):
    heads, dim, feats = feature_proj.shape
    rows, width = grad_output.shape
    split = lax.axis_size("head")
    bits = bits_of(split)
    me = lax.axis_index("head").astype(jnp.int32).reshape(1)
    macs = rows * dim * feats * heads * 2

    kf, state = call(
        functools.partial(key_kernel, heads),
        [struct((rows, heads * feats)), struct((heads * dim, feats))],
        key_vectors, value_vectors, feature_proj, flops=2 * macs,
    )
    carried = before(state, "seq")

    offsets, gathered = [0], grad_output[None]
    for bit in reversed(bits):
        gathered = jnp.concatenate([gathered, swap(gathered, "head", bit)], axis=0)
        offsets = offsets + [o ^ bit for o in offsets]
    qf, scores, num, gm = call(
        functools.partial(local_kernel, heads, offsets),
        [
            struct((rows, heads * feats)),
            struct((heads, rows, rows)),
            struct((rows, heads * dim), jnp.float32),
            struct((rows, heads * dim), jnp.float32),
        ],
        me, queries, value_vectors, feature_proj, kf, gathered, out_weight,
        flops=3 * macs + 2 * rows * out_weight.size, specs=[SMEM] + [VMEM] * 6,
    )
    mixed, gn, later = call(
        functools.partial(middle_kernel, heads),
        [
            struct((rows, heads * dim)),
            struct((rows, heads * dim)),
            struct((heads * dim, feats)),
        ],
        qf, num, gm, carried, flops=2 * macs,
    )
    after_b = after(later, "seq")

    order = [o for o in range(split) if not o & 1] + [o for o in range(split) if o & 1]
    own, sent = call(
        functools.partial(project_kernel, order),
        [struct((split // 2, rows, width))] * 2,
        me, mixed, out_weight, flops=2 * rows * out_weight.size, specs=[SMEM, VMEM, VMEM],
    )
    total = own.astype(jnp.float32) + swap(sent, "head", 1).astype(jnp.float32)
    for bit in bits[1:]:
        pairs = total.reshape((total.shape[0] // 2, 2) + total.shape[1:])
        total = pairs[:, 0] + swap(bf(pairs[:, 1]), "head", bit).astype(jnp.float32)
    layer_out = bf(total[0])

    gq, gv_part, gkf_part = call(
        functools.partial(query_kernel, heads),
        [
            struct((rows, heads * dim)),
            struct((rows, heads * dim), jnp.float32),
            struct((rows, heads * feats), jnp.float32),
        ],
        qf, kf, value_vectors, feature_proj, scores, gn, carried, flops=5 * macs,
    )
    gk, gv = call(
        functools.partial(last_kernel, heads),
        [struct((rows, heads * dim))] * 2,
        key_vectors, value_vectors, feature_proj, kf, gv_part, gkf_part, after_b,
        flops=3 * macs,
    )
    return layer_out, gq, gk, gv


def solution(mesh):
    placed = (
        P("seq", "head"),
        P("seq", "head"),
        P("seq", "head"),
        P("head", None, None),
        P("head", None),
        P("seq", "head"),
    )
    return jax.shard_map(
        local,
        mesh=mesh,
        in_specs=placed,
        out_specs=(P("seq", "head"),) * 4,
        check_vma=False,
    )
```

time: 195 us -> 72.1 us (0.37)
  waiting for transfers between devices: 108 us -> 35.2 us
  other arithmetic: 21.5 us -> 2.97 us
  matrix products: 17.4 us -> 0 us
  blocking collectives: 15.7 us -> 0 us
  starting transfers between devices: 3.72 us -> 17.9 us
  between operations: 14.3 us -> 0.84 us
  Pallas kernels: 0 us -> 8.45 us
  local copies, waits for them, and re-layouts: 11.9 us -> 6.15 us
    all_gather x2 -> x0, waiting for transfers between devices: 82.8 us -> none  [entering(): everything = lax.all_gather(array, axis)]
    ppermute x0 -> x7, waiting for transfers between devices: none -> 26.9 us  [the longest x3 25.2 us: after(): lax.ppermute(bf(inclusive), axis, [(i, i - step) for i in range(step, siz...]
    select_n x16 -> x0, other arithmetic: 19.7 us -> none  [hop(): return jnp.where(reached, new, before)]
    dot_general x17 -> x0, matrix products: 17.4 us -> none  [the longest x1 2.29 us: local(): jnp.einsum('htm,hdm->htd', query_terms, feature_proj, preferred_element_t...]
    all_to_all x1 -> x2, waiting for transfers between devices: 25.7 us -> 8.29 us  [the longest x1 7.43 us: before(): mine = lax.all_to_all(parts, axis, 0, 0)]
    all_gather x2 -> x0, blocking collectives: 15.7 us -> none  [the longest x1 9.08 us: local(): lax.all_gather(grad_output, 'head', axis=1, tiled=True)]
    pallas_call x0 -> x7, Pallas kernels: none -> 8.45 us  [call(): pl.pallas_call(body, out_shape=outs, in_specs=specs or [VMEM] * len(args)...]
    all_to_all x1 -> x2, starting transfers between devices: 3.64 us -> 10.9 us  [the longest x1 7.28 us: before(): mine = lax.all_to_all(parts, axis, 0, 0)]
  transfers between devices with their start and end apart: 3 -> 9, of which waited for: 3 -> 6; matrix products, arithmetic and copies ran while one was open for 9% -> 4% of each run, Pallas kernels for 0% -> 7%
where the time goes in v1:
time: 72.1 us; the launch traced here: 71.5 us
  waiting for transfers between devices  35.2 us (49%)
  starting transfers between devices  17.9 us (25%)
  Pallas kernels  8.45 us (12%)
  local copies, waits for them, and re-layouts  6.15 us (9%)
  other arithmetic  2.97 us (4%)
  between operations  0.84 us (1%)
    ppermute x3, waiting for transfers between devices, after(): lax.ppermute(bf(inclusive), axis, [(i, i - step) for i in range(step, siz...  25.2 us
    pallas_call x7, Pallas kernels, call(): pl.pallas_call(body, out_shape=outs, in_specs=specs or [VMEM] * len(args)...  8.45 us
    all_to_all x1, waiting for transfers between devices, before(): mine = lax.all_to_all(parts, axis, 0, 0)  7.43 us
    all_to_all x1, starting transfers between devices, before(): mine = lax.all_to_all(parts, axis, 0, 0)  7.28 us
    unnamed x26, local copies, waits for them, and re-layouts  6.13 us
    ppermute x3, starting transfers between devices, after(): lax.ppermute(bf(inclusive), axis, [(i, i - step) for i in range(step, siz...  3.88 us
    all_to_all x1, starting transfers between devices, before(): return lax.all_to_all(sums, axis, 0, 0).reshape(state.shape)  3.59 us
    ppermute x4, starting transfers between devices, swap(): return lax.ppermute(array, axis, [(i, i ^ bit) for i in range(size)])  3.19 us
  transfers between devices with their start and end apart: 9, of which 6 were waited for; matrix products, arithmetic and copies ran while one was open for 4% of the time, Pallas kernels for 7%

profile of v1, /device:TPU:0, one launch (start us, length us, event | category | flops | bytes accessed | tf_op | source)
XLA Modules:
  0.0 71.5 jit_solution(15771470615554688487)
XLA Ops:
  0.6 0.0 copy-start
  0.6 0.0 copy-start.1
  0.7 1.1 %copy-done.1 = bf16[4,128,256]{2,1,0:T(8,128)(2,1)S(1)} copy-done((bf16[4,128,256]{2,1,0:T(8,128)(2,1)S(1)}, bf16[4,128,256]{2,1,0:T(8,128)(2,1)}, u32[]{:S(2)}) %copy-start.1) | copy-done | bytes 262168
  1.7 0.9 %copy-done.3 = bf16[128,512]{1,0:T(8,128)(2,1)S(1)} copy-done((bf16[128,512]{1,0:T(8,128)(2,1)S(1)}, bf16[128,512]{1,0:T(8,128)(2,1)}, u32[]{:S(2)}) %copy-start.3) | copy-done | bytes 131096
  2.6 0.9 %copy-done.5 = bf16[128,512]{1,0:T(8,128)(2,1)S(1)} copy-done((bf16[128,512]{1,0:T(8,128)(2,1)S(1)}, bf16[128,512]{1,0:T(8,128)(2,1)}, u32[]{:S(2)}) %copy-start.5) | copy-done | bytes 131096
  3.6 1.1 %shard_map.93 = (bf16[128,1024]{1,0:T(8,128)(2,1)S(1)}, bf16[512,256]{1,0:T(8,128)(2,1)}) custom-call(bf16[128,512]{1,0:T(8,128)(2,1)S(1)} %copy-done.5, bf16[128,512]{1,0:T(8,128)(2,1)S(1)} %copy-done.3, bf16[4,128,256]{2,1,0:T(8,128)(2,1)S(1)} %copy-done.1), custom_call_target="tpu_custom_call" | custom-call | flops 67108864 | bytes 1048576 | tf_op jit(solution)/shard_map/pallas_call | solution.py:29
  4.7 7.3 %all-to-all-start = ((bf16[8,64,256]{2,1,0:T(8,128)(2,1)}), bf16[8,64,256]{2,1,0:T(8,128)(2,1)S(1)}, u32[]{:S(2)}, u32[]{:S(2)}) async-start(bf16[8,64,256]{2,1,0:T(8,128)(2,1)} %bitcast.2), calls=%async_computation | async-start | bytes 524288 | tf_op jit(solution)/shard_map/all_to_all | solution.py:166
  12.0 1.5 %collective-permute-start = (bf16[1,128,512]{2,1,0:T(8,128)(2,1)}, bf16[1,128,512]{2,1,0:T(8,128)(2,1)S(1)}, u32[]{:S(2)}, u32[]{:S(2)}) collective-permute-start(bf16[1,128,512]{2,1,0:T(8,128)(2,1)} %bitcast.20), channel_id=1, source_target_pairs={{0,2},{1,3},{2,0},{3,1},{4,6},{5,7},{6,4},{7,5},{8,10},{9,11},{10,... | collective-permute-start | bytes 393224 | tf_op jit(solution)/shard_map/ppermute | solution.py:156
  13.5 7.4 %all-to-all-done.in_ref = bf16[8,64,256]{2,1,0:T(8,128)(2,1)S(1)} async-done(((bf16[8,64,256]{2,1,0:T(8,128)(2,1)}), bf16[8,64,256]{2,1,0:T(8,128)(2,1)S(1)}, u32[]{:S(2)}, u32[]{:S(2)}) %all-to-all-start) | async-done | bytes 262176 | tf_op jit(solution)/shard_map/all_to_all | solution.py:166
  20.9 0.7 %shard_map.95 = bf16[8,64,256]{2,1,0:T(8,128)(2,1)} custom-call(bf16[8,64,256]{2,1,0:T(8,128)(2,1)S(1)} %all-to-all-done.in_ref), custom_call_target="tpu_custom_call" | custom-call | bytes 524288 | tf_op jit(solution)/shard_map/pallas_call | solution.py:29
  21.6 3.6 %all-to-all-start.1 = ((bf16[8,64,256]{2,1,0:T(8,128)(2,1)}), bf16[8,64,256]{2,1,0:T(8,128)(2,1)S(1)}, u32[]{:S(2)}, u32[]{:S(2)}) async-start(bf16[8,64,256]{2,1,0:T(8,128)(2,1)} %shard_map.95), calls=%async_computation.1 | async-start | bytes 524288 | tf_op jit(solution)/shard_map/all_to_all | solution.py:168
  25.2 0.0 collective-permute-done
  25.2 0.9 %pad_maximum_fusion.1 = bf16[2,128,512]{2,1,0:T(8,128)(2,1)S(1)} fusion(bf16[1,128,512]{2,1,0:T(8,128)(2,1)S(1)} %collective-permute-done, bf16[1,128,512]{2,1,0:T(8,128)(2,1)} %bitcast.21), kind=kLoop, calls=%fused_computation.13 | loop fusion | flops 131072 | bytes 524288 | tf_op jit(solution)/shard_map/concatenate | solution.py:201
  26.1 0.1 collective-permute-start.1
  26.2 1.6 %collective-permute-done.1 = bf16[2,128,512]{2,1,0:T(8,128)(2,1)} collective-permute-done((bf16[2,128,512]{2,1,0:T(8,128)(2,1)S(1)}, bf16[2,128,512]{2,1,0:T(8,128)(2,1)}, u32[]{:S(2)}, u32[]{:S(2)}) %collective-permute-start.1) | collective-permute-done | bytes 262176 | tf_op jit(solution)/shard_map/ppermute | solution.py:156
  27.9 1.0 %pad_maximum_fusion.go_ref = bf16[4,128,512]{2,1,0:T(8,128)(2,1)S(1)} fusion(bf16[2,128,512]{2,1,0:T(8,128)(2,1)} %collective-permute-done.1, bf16[1,128,512]{2,1,0:T(8,128)(2,1)S(1)} %collective-permute-done, bf16[1,128,512]{2,1,0:T(8,128)(2,1)S(1)} %bitcast.22), kind=kLoop, calls=%fused_computation.6 | loop fusion | flops 524288 | bytes 1048576 | tf_op jit(solution)/shard_map/concatenate | solution.py:201
  28.9 0.0 copy-done
  28.9 0.0 copy-done.2
  28.9 0.0 copy-done.4
  28.9 0.0 copy-start.9
  28.9 0.9 %copy-done.9 = bf16[128,512]{1,0:T(8,128)(2,1)S(1)} copy-done((bf16[128,512]{1,0:T(8,128)(2,1)S(1)}, bf16[128,512]{1,0:T(8,128)(2,1)}, u32[]{:S(2)}) %copy-start.9) | copy-done | bytes 131096
  29.8 1.7 %shard_map.94 = (bf16[128,1024]{1,0:T(8,128)(2,1)S(1)}, bf16[4,128,128]{2,1,0:T(8,128)(2,1)S(1)}, f32[128,512]{1,0:T(8,128)S(1)}, f32[128,512]{1,0:T(8,128)S(1)}) custom-call(s32[1]{0:T(128)} %bitcast.me_ref, bf16[128,512]{1,0:T(8,128)(2,1)S(1)} %copy-done.9, bf16[128,512]{1,0:T(8,128)(2,1)S(1)} %copy-done.4, bf16[4,128,256]{2,1,0:T(8,128)(2,1)S(1)} %copy-done.2, ...), custom_call_target="tpu_custom_call" | custom-call | flops 369098752 | bytes 4325380 | tf_op jit(solution)/shard_map/pallas_call | solution.py:29
  31.5 0.0 copy-start.7
  31.6 0.7 copy-done.7
  32.3 0.7 copy-done.10
  32.9 0.9 %all-to-all-done.1 = bf16[8,64,256]{2,1,0:T(8,128)(2,1)S(1)} async-done(((bf16[8,64,256]{2,1,0:T(8,128)(2,1)}), bf16[8,64,256]{2,1,0:T(8,128)(2,1)S(1)}, u32[]{:S(2)}, u32[]{:S(2)}) %all-to-all-start.1) | async-done | bytes 262176 | tf_op jit(solution)/shard_map/all_to_all | solution.py:168
  33.8 0.9 %copy-done.8 = f32[128,512]{1,0:T(8,128)S(1)} copy-done((f32[128,512]{1,0:T(8,128)S(1)}, f32[128,512]{1,0:T(8,128)}, u32[]{:S(2)}) %copy-start.8) | copy-done | bytes 262168
  34.7 1.0 %shard_map.96 = (bf16[128,512]{1,0:T(8,128)(2,1)S(1)}, bf16[128,512]{1,0:T(8,128)(2,1)S(1)}, bf16[512,256]{1,0:T(8,128)(2,1)S(1)}) custom-call(bf16[128,1024]{1,0:T(8,128)(2,1)S(1)} %get-tuple-element.21.qf_ref, f32[128,512]{1,0:T(8,128)S(1)} %get-tuple-element.22.num_ref, f32[128,512]{1,0:T(8,128)S(1)} %copy-done.8, bf16[512,256]{1,0:T(8,128)(2,1)S(1)} %bitcast.18), custom_call_target="tpu_custom_call" | custom-call | flops 67108864 | bytes 1572864 | tf_op jit(solution)/shard_map/pallas_call | solution.py:29
  35.7 1.3 %collective-permute-start.4 = (bf16[512,256]{1,0:T(8,128)(2,1)S(1)}, bf16[512,256]{1,0:T(8,128)(2,1)S(1)}, u32[]{:S(2)}, u32[]{:S(2)}) collective-permute-start(bf16[512,256]{1,0:T(8,128)(2,1)S(1)} %get-tuple-element.33), channel_id=1, source_target_pairs={{4,0},{8,4},{12,8},{16,12},{20,16},{24,20},{28,24},{5,1},{9,5},{13... | collective-permute-start | bytes 786440 | tf_op jit(solution)/shard_map/ppermute | solution.py:175
  37.0 0.5 shard_map.97
  37.5 0.0 copy-start.11
  37.5 0.1 collective-permute-start.2
  37.6 7.8 %collective-permute-done.4 = bf16[512,256]{1,0:T(8,128)(2,1)S(1)} collective-permute-done((bf16[512,256]{1,0:T(8,128)(2,1)S(1)}, bf16[512,256]{1,0:T(8,128)(2,1)S(1)}, u32[]{:S(2)}, u32[]{:S(2)}) %collective-permute-start.4) | collective-permute-done | bytes 262176 | tf_op jit(solution)/shard_map/ppermute | solution.py:175
  45.4 0.1 fusion.3
  45.4 1.3 %collective-permute-start.5 = (bf16[512,256]{1,0:T(8,128)(2,1)S(1)}, bf16[512,256]{1,0:T(8,128)(2,1)S(1)}, u32[]{:S(2)}, u32[]{:S(2)}) collective-permute-start(bf16[512,256]{1,0:T(8,128)(2,1)S(1)} %fusion.3), channel_id=1, source_target_pairs={{8,0},{12,4},{16,8},{20,12},{24,16},{28,20},{9,1},{13,5},{17,9},{2... | collective-permute-start | bytes 786440 | tf_op jit(solution)/shard_map/ppermute | solution.py:175
  46.7 0.0 collective-permute-done.2
  46.8 0.1 add_bitcast_fusion
  46.9 0.0 copy-start.6
  46.9 1.6 %collective-permute-start.3 = (bf16[1,128,512]{2,1,0:T(8,128)(2,1)S(1)}, bf16[1,128,512]{2,1,0:T(8,128)(2,1)S(1)}, u32[]{:S(2)}, u32[]{:S(2)}) collective-permute-start(bf16[1,128,512]{2,1,0:T(8,128)(2,1)S(1)} %fusion.7), channel_id=1, source_target_pairs={{0,2},{1,3},{2,0},{3,1},{4,6},{5,7},{6,4},{7,5},{8,10},{9,11},{10,... | collective-permute-start | bytes 393224 | tf_op jit(solution)/shard_map/ppermute | solution.py:156
  48.4 6.4 %collective-permute-done.5 = bf16[512,256]{1,0:T(8,128)(2,1)S(1)} collective-permute-done((bf16[512,256]{1,0:T(8,128)(2,1)S(1)}, bf16[512,256]{1,0:T(8,128)(2,1)S(1)}, u32[]{:S(2)}, u32[]{:S(2)}) %collective-permute-start.5) | collective-permute-done | bytes 262176 | tf_op jit(solution)/shard_map/ppermute | solution.py:175
  54.9 0.1 fusion.2
  55.0 1.3 %collective-permute-start.6 = (bf16[512,256]{1,0:T(8,128)(2,1)S(1)}, bf16[512,256]{1,0:T(8,128)(2,1)S(1)}, u32[]{:S(2)}, u32[]{:S(2)}) collective-permute-start(bf16[512,256]{1,0:T(8,128)(2,1)S(1)} %fusion.2), channel_id=1, source_target_pairs={{16,0},{20,4},{24,8},{28,12},{17,1},{21,5},{25,9},{29,13},{18,2},{... | collective-permute-start | bytes 786440 | tf_op jit(solution)/shard_map/ppermute | solution.py:175
  56.3 2.0 %shard_map.98 = (bf16[128,512]{1,0:T(8,128)(2,1)}, f32[128,512]{1,0:T(8,128)S(1)}, f32[128,1024]{1,0:T(8,128)S(1)}) custom-call(bf16[128,1024]{1,0:T(8,128)(2,1)S(1)} %get-tuple-element.21.qf_ref, bf16[128,1024]{1,0:T(8,128)(2,1)S(1)} %get-tuple-element.20.kf_ref, bf16[128,512]{1,0:T(8,128)(2,1)S(1)} %copy-done.4, bf16[4,128,256]{2,1,0:T(8,128)(2,1)S(1)} %copy-done.2, ...), custom_call_target="tpu_custom_call" | custom-call | flops 167772160 | bytes 2359296 | tf_op jit(solution)/shard_map/pallas_call | solution.py:29
  58.3 0.0 collective-permute-done.3
  58.3 0.7 fusion.6
  59.0 11.0 %collective-permute-done.6 = bf16[512,256]{1,0:T(8,128)(2,1)S(1)} collective-permute-done((bf16[512,256]{1,0:T(8,128)(2,1)S(1)}, bf16[512,256]{1,0:T(8,128)(2,1)S(1)}, u32[]{:S(2)}, u32[]{:S(2)}) %collective-permute-start.6) | collective-permute-done | bytes 262176 | tf_op jit(solution)/shard_map/ppermute | solution.py:175
  70.0 0.1 fusion.1.after_ref
  70.1 1.4 %shard_map.99 = (bf16[128,512]{1,0:T(8,128)(2,1)}, bf16[128,512]{1,0:T(8,128)(2,1)}) custom-call(bf16[128,512]{1,0:T(8,128)(2,1)S(1)} %copy-done.6, bf16[128,512]{1,0:T(8,128)(2,1)S(1)} %copy-done.4, bf16[4,128,256]{2,1,0:T(8,128)(2,1)S(1)} %copy-done.2, bf16[128,1024]{1,0:T(8,128)(2,1)S(1)} %get-tuple-element.20.kf_ref, ...), custom_call_target="tpu_custom_call" | custom-call | flops 100663296 | bytes 2097152 | tf_op jit(solution)/shard_map/pallas_call | solution.py:29
  (11 shorter events, 0.0 us)
Async XLA Ops:
  0.6 28.3 %copy-start = (bf16[512,2048]{1,0:T(8,128)(2,1)S(1)}, bf16[512,2048]{1,0:T(8,128)(2,1)}, u32[]{:S(2)}) copy-start(bf16[512,2048]{1,0:T(8,128)(2,1)} %w_ref.3) | copy-start | bytes 6291460
  0.6 1.1 %copy-start.1 = (bf16[4,128,256]{2,1,0:T(8,128)(2,1)S(1)}, bf16[4,128,256]{2,1,0:T(8,128)(2,1)}, u32[]{:S(2)}) copy-start(bf16[4,128,256]{2,1,0:T(8,128)(2,1)} %om_ref.7) | copy-start | bytes 786436
  1.7 0.9 %copy-start.3 = (bf16[128,512]{1,0:T(8,128)(2,1)S(1)}, bf16[128,512]{1,0:T(8,128)(2,1)}, u32[]{:S(2)}) copy-start(bf16[128,512]{1,0:T(8,128)(2,1)} %v_ref.7) | copy-start | bytes 393220
  2.6 0.9 %copy-start.5 = (bf16[128,512]{1,0:T(8,128)(2,1)S(1)}, bf16[128,512]{1,0:T(8,128)(2,1)}, u32[]{:S(2)}) copy-start(bf16[128,512]{1,0:T(8,128)(2,1)} %k_ref.3) | copy-start | bytes 393220
  3.5 24.3 %copy-start.12 = (bf16[128,512]{1,0:T(8,128)(2,1)S(1)}, bf16[128,512]{1,0:T(8,128)(2,1)}, u32[]{:S(2)}) copy-start(bf16[128,512]{1,0:T(8,128)(2,1)} %param.11) | copy-start | bytes 393220
  3.6 25.4 %copy-start.2 = (bf16[4,128,256]{2,1,0:T(8,128)(2,1)S(1)}, bf16[4,128,256]{2,1,0:T(8,128)(2,1)}, u32[]{:S(2)}) copy-start(bf16[4,128,256]{2,1,0:T(8,128)(2,1)} %om_ref.7) | copy-start | bytes 786436
  3.6 25.4 %copy-start.4 = (bf16[128,512]{1,0:T(8,128)(2,1)S(1)}, bf16[128,512]{1,0:T(8,128)(2,1)}, u32[]{:S(2)}) copy-start(bf16[128,512]{1,0:T(8,128)(2,1)} %v_ref.7) | copy-start | bytes 393220
  4.7 16.2 %all-to-all-start = ((bf16[8,64,256]{2,1,0:T(8,128)(2,1)}), bf16[8,64,256]{2,1,0:T(8,128)(2,1)S(1)}, u32[]{:S(2)}, u32[]{:S(2)}) async-start(bf16[8,64,256]{2,1,0:T(8,128)(2,1)} %bitcast.2), calls=%async_computation | async-start | bytes 524288 | tf_op jit(solution)/shard_map/all_to_all | solution.py:166
  12.0 13.2 %collective-permute-start = (bf16[1,128,512]{2,1,0:T(8,128)(2,1)}, bf16[1,128,512]{2,1,0:T(8,128)(2,1)S(1)}, u32[]{:S(2)}, u32[]{:S(2)}) collective-permute-start(bf16[1,128,512]{2,1,0:T(8,128)(2,1)} %bitcast.20), channel_id=1, source_target_pairs={{0,2},{1,3},{2,0},{3,1},{4,6},{5,7},{6,4},{7,5},{8,10},{9,11},{10,... | collective-permute-start | bytes 393224 | tf_op jit(solution)/shard_map/ppermute | solution.py:156
  21.6 12.2 %all-to-all-start.1 = ((bf16[8,64,256]{2,1,0:T(8,128)(2,1)}), bf16[8,64,256]{2,1,0:T(8,128)(2,1)S(1)}, u32[]{:S(2)}, u32[]{:S(2)}) async-start(bf16[8,64,256]{2,1,0:T(8,128)(2,1)} %shard_map.95), calls=%async_computation.1 | async-start | bytes 524288 | tf_op jit(solution)/shard_map/all_to_all | solution.py:168
  26.1 1.7 %collective-permute-start.1 = (bf16[2,128,512]{2,1,0:T(8,128)(2,1)S(1)}, bf16[2,128,512]{2,1,0:T(8,128)(2,1)}, u32[]{:S(2)}, u32[]{:S(2)}) collective-permute-start(bf16[2,128,512]{2,1,0:T(8,128)(2,1)S(1)} %pad_maximum_fusion.1), channel_id=1, source_target_pairs={{0,1},{1,0},{2,3},{3,2},{4,5},{5,4},{6,7},{7,6},{8,9},{9,8},{10,11... | collective-permute-start | bytes 786440 | tf_op jit(solution)/shard_map/ppermute | solution.py:156
  28.9 0.9 %copy-start.9 = (bf16[128,512]{1,0:T(8,128)(2,1)S(1)}, bf16[128,512]{1,0:T(8,128)(2,1)}, u32[]{:S(2)}) copy-start(bf16[128,512]{1,0:T(8,128)(2,1)} %q_ref.1) | copy-start | bytes 393220
  31.5 0.7 copy-start.7
  32.3 0.7 copy-start.10
  33.8 1.0 %copy-start.8 = (f32[128,512]{1,0:T(8,128)S(1)}, f32[128,512]{1,0:T(8,128)}, u32[]{:S(2)}) copy-start(f32[128,512]{1,0:T(8,128)} %copy-done.7) | copy-start | bytes 786436
  35.7 9.7 %collective-permute-start.4 = (bf16[512,256]{1,0:T(8,128)(2,1)S(1)}, bf16[512,256]{1,0:T(8,128)(2,1)S(1)}, u32[]{:S(2)}, u32[]{:S(2)}) collective-permute-start(bf16[512,256]{1,0:T(8,128)(2,1)S(1)} %get-tuple-element.33), channel_id=1, source_target_pairs={{4,0},{8,4},{12,8},{16,12},{20,16},{24,20},{28,24},{5,1},{9,5},{13... | collective-permute-start | bytes 786440 | tf_op jit(solution)/shard_map/ppermute | solution.py:175
  37.5 18.8 %copy-start.11 = (bf16[4,128,128]{2,1,0:T(8,128)(2,1)S(1)}, bf16[4,128,128]{2,1,0:T(8,128)(2,1)}, u32[]{:S(2)}) copy-start(bf16[4,128,128]{2,1,0:T(8,128)(2,1)} %copy-done.10) | copy-start | bytes 393220
  37.5 9.3 %collective-permute-start.2 = (bf16[2,128,512]{2,1,0:T(8,128)(2,1)S(1)}, bf16[2,128,512]{2,1,0:T(8,128)(2,1)S(1)}, u32[]{:S(2)}, u32[]{:S(2)}) collective-permute-start(bf16[2,128,512]{2,1,0:T(8,128)(2,1)S(1)} %get-tuple-element.27), channel_id=1, source_target_pairs={{0,1},{1,0},{2,3},{3,2},{4,5},{5,4},{6,7},{7,6},{8,9},{9,8},{10,11... | collective-permute-start | bytes 786440 | tf_op jit(solution)/shard_map/ppermute | solution.py:156
  45.4 9.4 %collective-permute-start.5 = (bf16[512,256]{1,0:T(8,128)(2,1)S(1)}, bf16[512,256]{1,0:T(8,128)(2,1)S(1)}, u32[]{:S(2)}, u32[]{:S(2)}) collective-permute-start(bf16[512,256]{1,0:T(8,128)(2,1)S(1)} %fusion.3), channel_id=1, source_target_pairs={{8,0},{12,4},{16,8},{20,12},{24,16},{28,20},{9,1},{13,5},{17,9},{2... | collective-permute-start | bytes 786440 | tf_op jit(solution)/shard_map/ppermute | solution.py:175
  46.9 23.2 %copy-start.6 = (bf16[128,512]{1,0:T(8,128)(2,1)S(1)}, bf16[128,512]{1,0:T(8,128)(2,1)}, u32[]{:S(2)}) copy-start(bf16[128,512]{1,0:T(8,128)(2,1)} %k_ref.3) | copy-start | bytes 393220
  46.9 11.4 %collective-permute-start.3 = (bf16[1,128,512]{2,1,0:T(8,128)(2,1)S(1)}, bf16[1,128,512]{2,1,0:T(8,128)(2,1)S(1)}, u32[]{:S(2)}, u32[]{:S(2)}) collective-permute-start(bf16[1,128,512]{2,1,0:T(8,128)(2,1)S(1)} %fusion.7), channel_id=1, source_target_pairs={{0,2},{1,3},{2,0},{3,1},{4,6},{5,7},{6,4},{7,5},{8,10},{9,11},{10,... | collective-permute-start | bytes 393224 | tf_op jit(solution)/shard_map/ppermute | solution.py:156
  55.0 15.0 %collective-permute-start.6 = (bf16[512,256]{1,0:T(8,128)(2,1)S(1)}, bf16[512,256]{1,0:T(8,128)(2,1)S(1)}, u32[]{:S(2)}, u32[]{:S(2)}) collective-permute-start(bf16[512,256]{1,0:T(8,128)(2,1)S(1)} %fusion.2), channel_id=1, source_target_pairs={{16,0},{20,4},{24,8},{28,12},{17,1},{21,5},{25,9},{29,13},{18,2},{... | collective-permute-start | bytes 786440 | tf_op jit(solution)/shard_map/ppermute | solution.py:175

commit v2 on v1

--- a/solution.py
+++ b/solution.py
@@ -10,6 +10,7 @@
 EPSILON = 1e-05
 VMEM = pl.BlockSpec(memory_space=pltpu.VMEM)
 SMEM = pl.BlockSpec(memory_space=pltpu.SMEM)
+HBM = pl.BlockSpec(memory_space=pltpu.HBM)
 NN = (((1,), (0,)), ((), ()))
 NT = (((1,), (1,)), ((), ()))
 TN = (((0,), (0,)), ((), ()))
@@ -23,7 +24,7 @@
     return x.astype(jnp.bfloat16)
 
 
-def call(body, outs, *args, flops=0, specs=None):
+def call(body, outs, *args, flops=0, specs=None, scratch=()):
     size = sum(a.size * a.dtype.itemsize for a in args)
     size += sum(o.size * o.dtype.itemsize for o in outs)
     return pl.pallas_call(
@@ -31,6 +32,7 @@
         out_shape=outs,
         in_specs=specs or [VMEM] * len(args),
         out_specs=[VMEM] * len(outs),
+        scratch_shapes=list(scratch),
         cost_estimate=pl.CostEstimate(flops=flops, bytes_accessed=size, transcendentals=0),
         compiler_params=pltpu.CompilerParams(vmem_limit_bytes=32 * 1024 * 1024),
     )(*args)
@@ -181,7 +183,15 @@
     return bf(exclusive)
 
 
-def local(queries, key_vectors, value_vectors, feature_proj, out_weight, grad_output):
+def reduce_blocks(own, sent, bits):
+    total = own.astype(jnp.float32) + swap(sent, "head", 1).astype(jnp.float32)
+    for bit in bits[1:]:
+        pairs = total.reshape((total.shape[0] // 2, 2) + total.shape[1:])
+        total = pairs[:, 0] + swap(bf(pairs[:, 1]), "head", bit).astype(jnp.float32)
+    return bf(total[0])
+
+
+def scanned(queries, key_vectors, value_vectors, feature_proj, out_weight, grad_output):
     heads, dim, feats = feature_proj.shape
     rows, width = grad_output.shape
     split = lax.axis_size("head")
@@ -228,11 +238,7 @@
         [struct((split // 2, rows, width))] * 2,
         me, mixed, out_weight, flops=2 * rows * out_weight.size, specs=[SMEM, VMEM, VMEM],
     )
-    total = own.astype(jnp.float32) + swap(sent, "head", 1).astype(jnp.float32)
-    for bit in bits[1:]:
-        pairs = total.reshape((total.shape[0] // 2, 2) + total.shape[1:])
-        total = pairs[:, 0] + swap(bf(pairs[:, 1]), "head", bit).astype(jnp.float32)
-    layer_out = bf(total[0])
+    layer_out = reduce_blocks(own, sent, bits)
 
     gq, gv_part, gkf_part = call(
         functools.partial(query_kernel, heads),
@@ -252,6 +258,289 @@
     return layer_out, gq, gk, gv
 
 
+def spot():
+    s, h = lax.axis_index("seq"), lax.axis_index("head")
+    return s, h
+
+
+def routes(k, n, seq, head):
+    out = []
+    for s in range(seq):
+        for h in range(head):
+            to = (n * (h % 2) + (s + k) % n) * head + 2 * (h // 2) + s // n
+            out.append((s * head + h, to))
+    return out
+
+
+def scatter(parts):
+    n, seq, head = len(parts), lax.axis_size("seq"), lax.axis_size("head")
+    return [lax.ppermute(p, ("seq", "head"), routes(k, n, seq, head)) for k, p in enumerate(parts)]
+
+
+def gather(parts):
+    n, seq, head = len(parts), lax.axis_size("seq"), lax.axis_size("head")
+    return [
+        lax.ppermute(p, ("seq", "head"), [(b, a) for a, b in routes(k, n, seq, head)])
+        for k, p in enumerate(parts)
+    ]
+
+
+def pass_on(array, forward):
+    pairs = [(h, h + 1) if forward else (h + 1, h) for h in range(0, lax.axis_size("head"), 2)]
+    return lax.ppermute(array, "head", pairs)
+
+
+def lane(index, width):
+    return pl.ds(pl.multiple_of(index * width, 128), width)
+
+
+def pack_kernel(n, q_ref, k_ref, v_ref, om_ref, *rest):
+    outs, om_out, sems = rest[:n], rest[n], rest[n + 1]
+    s, _ = spot()
+    dim = om_ref.shape[1]
+    copies = []
+    for k in range(n):
+        cols = lane(lax.rem(s + k, n), dim)
+        for at, ref in enumerate((q_ref, k_ref, v_ref)):
+            copies.append((ref.at[:, cols], outs[k].at[at]))
+    copies.append((om_ref.at[lax.rem(s, n)], om_out))
+    started = [pltpu.make_async_copy(a, b, sems.at[i]) for i, (a, b) in enumerate(copies)]
+    for copy in started:
+        copy.start()
+    for copy in started:
+        copy.wait()
+
+
+def grad_mixed_kernel(n, offsets, *refs):
+    blocks, w_ref = refs[: len(offsets)], refs[len(offsets)]
+    outs, scr = refs[len(offsets) + 1 : -1], refs[-1]
+    s, h = spot()
+    width = blocks[0].shape[1]
+    dim = outs[0].shape[1]
+    total = None
+    for offset, ref in zip(offsets, blocks):
+        part = mm(ref[...], w_ref[:, lane(h ^ offset, width)], NT)
+        total = part if total is None else total + part
+    scr[...] = bf(total)
+    for k in range(n):
+        outs[k][...] = scr[:, lane(lax.rem(s + k, n), dim)]
+
+
+def first_kernel(n, *refs):
+    got, own_om_ref, om_in_ref = refs[:n], refs[n], refs[n + 1]
+    qkv_ref, om_ref, kf_ref, state_ref, total_ref = refs[n + 2 :]
+    s, h = spot()
+    rows, dim = got[0].shape[1:]
+    scale = dim ** (-0.25)
+    for k in range(n):
+        at = pl.ds(pl.multiple_of(lax.rem(s + n - k, n) * rows, 128), rows)
+        qkv_ref[:, at, :] = got[k][...]
+    mine = lax.div(s, n) == lax.rem(h, 2)
+    om = jnp.where(mine, own_om_ref[lax.rem(s, n)], om_in_ref[...])
+    om_ref[...] = om
+    k_all = qkv_ref[1]
+    wide = k_all.astype(jnp.float32)
+    half_sq = jnp.sum(wide * wide, axis=1, keepdims=True) * (scale * scale * 0.5)
+    kf = bf(jnp.exp(mm(k_all, om) * scale - half_sq))
+    kf_ref[...] = kf
+    total = jnp.zeros(total_ref.shape, jnp.float32)
+    for t in range(n):
+        at = pl.ds(t * rows, rows)
+        state_ref[t] = bf(total)
+        total = total + mm(qkv_ref[2, at, :], kf[t * rows : (t + 1) * rows], TN)
+    total_ref[...] = bf(total)
+
+
+def inner_kernel(n, qkv_ref, om_ref, kf_ref, state_ref, qf_ref, scores_ref, num_ref):
+    dim = om_ref.shape[0]
+    rows = scores_ref.shape[1]
+    scale = dim ** (-0.25)
+    causal = causal_mask(rows)
+    qf_ref[...] = bf(jnp.exp(mm(qkv_ref[0], om_ref[...]) * scale))
+    for t in range(n):
+        at = pl.ds(t * rows, rows)
+        qf = qf_ref[at, :]
+        scores = bf(jnp.where(causal, mm(qf, kf_ref[at, :], NT), 0.0))
+        scores_ref[t] = scores
+        num_ref[at, :] = mm(scores, qkv_ref[2, at, :]) + mm(qf, state_ref[t], NT)
+
+
+def turn_kernel(n, *refs):
+    gm_in, (qf_ref, num_ref, carried_ref) = refs[:n], refs[n : n + 3]
+    gn_ref, state_ref, total_ref = refs[n + 3 : n + 6]
+    outs, scr = refs[n + 6 : -1], refs[-1]
+    s, _ = spot()
+    rows = gm_in[0].shape[0]
+    places = [
+        pl.ds(pl.multiple_of(lax.rem(s + n - k, n) * rows, 128), rows) for k in range(n)
+    ]
+    for k in range(n):
+        scr[places[k], :] = gm_in[k][...]
+    num = num_ref[...] + mm(qf_ref[...], carried_ref[...], NT)
+    inv = lax.rsqrt(jnp.mean(num * num, axis=1, keepdims=True) + EPSILON)
+    normed = num * inv
+    gm = scr[...].astype(jnp.float32)
+    gn = bf((gm - normed * jnp.mean(gm * normed, axis=1, keepdims=True)) * inv)
+    gn_ref[...] = gn
+    scr[...] = bf(normed)
+    for k in range(n):
+        outs[k][...] = scr[places[k], :]
+    total = jnp.zeros(total_ref.shape, jnp.float32)
+    for t in reversed(range(n)):
+        state_ref[t] = bf(total)
+        at = pl.ds(t * rows, rows)
+        total = total + mm(gn[t * rows : (t + 1) * rows], qf_ref[at, :], TN)
+    total_ref[...] = bf(total)
+
+
+def back_kernel(n, qkv_ref, om_ref, kf_ref, qf_ref, scores_ref, gn_ref, state_ref, carried_ref,
+                later_ref, gq_ref, gv_ref, gkf_ref, gqf_scr):
+    dim = om_ref.shape[0]
+    rows = scores_ref.shape[1]
+    scale = dim ** (-0.25)
+    causal = causal_mask(rows)
+    gqf_scr[...] = mm(gn_ref[...], carried_ref[...])
+    for t in range(n):
+        at = pl.ds(t * rows, rows)
+        qf, kf, gn, v = qf_ref[at, :], kf_ref[at, :], gn_ref[at, :], qkv_ref[2, at, :]
+        gs = bf(jnp.where(causal, mm(gn, v, NT), 0.0))
+        gqf = gqf_scr[at, :] + mm(gs, kf) + mm(gn, state_ref[t])
+        terms = bf(gqf * qf.astype(jnp.float32))
+        gq_ref[at, :] = bf(mm(terms, om_ref[...], NT) * scale)
+        later = later_ref[t]
+        gv_ref[at, :] = mm(scores_ref[t], gn, TN) + mm(kf, later, NT)
+        gkf_ref[at, :] = mm(gs, qf, TN) + mm(v, later)
+
+
+def end_kernel(n, qkv_ref, om_ref, kf_ref, gq_ref, gv_ref, gkf_ref, after_ref, *rest):
+    outs, gk_scr, gv_scr = rest[:n], rest[n], rest[n + 1]
+    s, _ = spot()
+    dim = om_ref.shape[0]
+    rows = outs[0].shape[1]
+    scale = dim ** (-0.25)
+    kf, after = kf_ref[...], after_ref[...]
+    gv_scr[...] = bf(gv_ref[...] + mm(kf, after, NT))
+    gkf = gkf_ref[...] + mm(qkv_ref[2], after)
+    terms = bf(gkf * kf.astype(jnp.float32))
+    total = jnp.sum(terms.astype(jnp.float32), axis=1, keepdims=True)
+    wide = qkv_ref[1].astype(jnp.float32)
+    gk_scr[...] = bf(mm(terms, om_ref[...], NT) * scale - total * wide * (scale * scale))
+    for k in range(n):
+        at = pl.ds(pl.multiple_of(lax.rem(s + n - k, n) * rows, 128), rows)
+        outs[k][0] = gq_ref[at, :]
+        outs[k][1] = gk_scr[at, :]
+        outs[k][2] = gv_scr[at, :]
+
+
+def mixed_project_kernel(n, offsets, *refs):
+    mixed_in, w_ref, own_ref, sent_ref, scr = refs[:n], *refs[n:]
+    s, h = spot()
+    width = own_ref.shape[2]
+    dim = mixed_in[0].shape[1]
+    half = len(offsets) // 2
+    for k in range(n):
+        scr[:, lane(lax.rem(s + k, n), dim)] = mixed_in[k][...]
+    mixed = scr[...]
+    for at, offset in enumerate(offsets):
+        part = bf(mm(mixed, w_ref[:, lane(h ^ offset, width)]))
+        if at < half:
+            own_ref[at] = part
+        else:
+            sent_ref[at - half] = part
+
+
+def unpack_kernel(n, *refs):
+    got, outs = refs[:n], refs[n:]
+    s, _ = spot()
+    dim = got[0].shape[2]
+    for k in range(n):
+        cols = lane(lax.rem(s + k, n), dim)
+        for at, out in enumerate(outs):
+            out[:, cols] = got[k][at]
+
+
+def head_per_pair(queries, key_vectors, value_vectors, feature_proj, out_weight, grad_output):
+    n, dim, feats = feature_proj.shape
+    rows, width = grad_output.shape
+    split = lax.axis_size("head")
+    bits = bits_of(split)
+    long = n * rows
+    macs = long * dim * feats * 2
+    f32 = jnp.float32
+
+    *sends, om_sent = call(
+        functools.partial(pack_kernel, n),
+        [struct((3, rows, dim))] * n + [struct((dim, feats))],
+        queries, key_vectors, value_vectors, feature_proj,
+        specs=[HBM] * 4, scratch=[pltpu.SemaphoreType.DMA((3 * n + 1,))],
+    )
+    offsets, blocks = [0], [grad_output]
+    for bit in reversed(bits):
+        blocks = blocks + [swap(b, "head", bit) for b in blocks]
+        offsets = offsets + [o ^ bit for o in offsets]
+    om_in = swap(om_sent, "head", 1)
+    got = scatter(sends)
+    gm_parts = call(
+        functools.partial(grad_mixed_kernel, n, offsets),
+        [struct((rows, dim))] * n,
+        *blocks, out_weight, flops=2 * rows * out_weight.size,
+        scratch=[pltpu.VMEM((rows, n * dim), jnp.bfloat16)],
+    )
+    gm_in = scatter(gm_parts)
+    qkv, om, kf, state, total = call(
+        functools.partial(first_kernel, n),
+        [
+            struct((3, long, dim)),
+            struct((dim, feats)),
+            struct((long, feats)),
+            struct((n, dim, feats)),
+            struct((dim, feats)),
+        ],
+        *got, feature_proj, om_in, flops=2 * macs,
+    )
+    carried = pass_on(total, True)
+    qf, scores, num = call(
+        functools.partial(inner_kernel, n),
+        [struct((long, feats)), struct((n, rows, rows)), struct((long, dim), f32)],
+        qkv, om, kf, state, flops=4 * macs,
+    )
+    gn, later, later_total, *mixed_parts = call(
+        functools.partial(turn_kernel, n),
+        [struct((long, dim)), struct((n, dim, feats)), struct((dim, feats))]
+        + [struct((rows, dim))] * n,
+        *gm_in, qf, num, carried, flops=2 * macs,
+        scratch=[pltpu.VMEM((long, dim), jnp.bfloat16)],
+    )
+    after_b = pass_on(later_total, False)
+    mixed_in = gather(mixed_parts)
+    gq, gv_part, gkf_part = call(
+        functools.partial(back_kernel, n),
+        [struct((long, dim)), struct((long, dim), f32), struct((long, feats), f32)],
+        qkv, om, kf, qf, scores, gn, state, carried, later, flops=8 * macs,
+        scratch=[pltpu.VMEM((long, feats), f32)],
+    )
+    grads = call(
+        functools.partial(end_kernel, n),
+        [struct((3, rows, dim))] * n,
+        qkv, om, kf, gq, gv_part, gkf_part, after_b, flops=3 * macs,
+        scratch=[pltpu.VMEM((long, dim), jnp.bfloat16)] * 2,
+    )
+    grads_in = gather(grads)
+
+    order = [o for o in range(split) if not o & 1] + [o for o in range(split) if o & 1]
+    own, sent = call(
+        functools.partial(mixed_project_kernel, n, order),
+        [struct((split // 2, rows, width))] * 2,
+        *mixed_in, out_weight, flops=2 * rows * out_weight.size,
+        scratch=[pltpu.VMEM((rows, n * dim), jnp.bfloat16)],
+    )
+    layer_out = reduce_blocks(own, sent, bits)
+    gq, gk, gv = call(
+        functools.partial(unpack_kernel, n), [struct((rows, n * dim))] * 3, *grads_in
+    )
+    return layer_out, gq, gk, gv
+
+
 def solution(mesh):
     placed = (
         P("seq", "head"),
@@ -261,6 +550,14 @@
         P("head", None),
         P("seq", "head"),
     )
+
+    def local(queries, key_vectors, value_vectors, feature_proj, out_weight, grad_output):
+        paired = mesh.shape["seq"] == 2 * feature_proj.shape[0] and mesh.shape["head"] % 2 == 0
+        body = head_per_pair if paired else scanned
+        return body(
+            queries, key_vectors, value_vectors, feature_proj, out_weight, grad_output
+        )
+
     return jax.shard_map(
         local,
         mesh=mesh,

time: 72.1 us -> 75.6 us (1.049)
  the two profiles are of different devices: /device:TPU:0 before, /device:TPU:1 now
where the time goes in v2:
time: 75.6 us; the launch traced here: 75.2 us
  starting transfers between devices  40 us (53%)
  waiting for transfers between devices  20 us (26%)
  local copies, waits for them, and re-layouts  7.12 us (9%)
  Pallas kernels  6.51 us (9%)
  between operations  0.84 us (1%)
    ppermute x8, starting transfers between devices, scatter(): lax.ppermute(p, ('seq', 'head'), routes(k, n, seq, head))  21.8 us
    ppermute x8, waiting for transfers between devices, gather(): lax.ppermute(p, ('seq', 'head'), [(b, a) for a, b in routes(k, n, seq, he...  12.7 us
    ppermute x8, starting transfers between devices, gather(): lax.ppermute(p, ('seq', 'head'), [(b, a) for a, b in routes(k, n, seq, he...  11.3 us
    ppermute x8, waiting for transfers between devices, scatter(): lax.ppermute(p, ('seq', 'head'), routes(k, n, seq, head))  7.26 us
    unnamed x16, local copies, waits for them, and re-layouts  7.1 us
    pallas_call x9, Pallas kernels, call(): pl.pallas_call(body, out_shape=outs, in_specs=specs or [VMEM] * len(args)...  6.51 us
    ppermute x2, starting transfers between devices, pass_on(): return lax.ppermute(array, 'head', pairs)  3.68 us
    ppermute x6, starting transfers between devices, swap(): return lax.ppermute(array, axis, [(i, i ^ bit) for i in range(size)])  3.14 us
  transfers between devices with their start and end apart: 24, of which 11 were waited for; matrix products, arithmetic and copies ran while one was open for 0% of the time, Pallas kernels for 7%

profile of v2, /device:TPU:1, one launch (start us, length us, event | category | flops | bytes accessed | tf_op | source)
XLA Modules:
  0.0 75.2 jit_solution(15275373133385494526)
XLA Ops:
  0.6 2.1 %collective-permute-start = (bf16[128,512]{1,0:T(8,128)(2,1)}, bf16[128,512]{1,0:T(8,128)(2,1)S(1)}, u32[]{:S(2)}, u32[]{:S(2)}) collective-permute-start(bf16[128,512]{1,0:T(8,128)(2,1)} %refs_0_.1), channel_id=1, source_target_pairs={{0,2},{1,3},{2,0},{3,1},{4,6},{5,7},{6,4},{7,5},{8,10},{9,11},{10,... | collective-permute-start | bytes 393224 | tf_op jit(solution)/shard_map/ppermute | solution.py:158
  2.7 0.9 %copy-done.2 = bf16[4,128,256]{2,1,0:T(8,128)(2,1)S(1)} copy-done((bf16[4,128,256]{2,1,0:T(8,128)(2,1)S(1)}, bf16[4,128,256]{2,1,0:T(8,128)(2,1)}, u32[]{:S(2)}) %copy-start.2) | copy-done | bytes 262168
  3.7 0.9 %copy-done.4 = bf16[128,512]{1,0:T(8,128)(2,1)S(1)} copy-done((bf16[128,512]{1,0:T(8,128)(2,1)S(1)}, bf16[128,512]{1,0:T(8,128)(2,1)}, u32[]{:S(2)}) %copy-start.4) | copy-done | bytes 131096
  4.6 0.9 %copy-done.5 = bf16[128,512]{1,0:T(8,128)(2,1)S(1)} copy-done((bf16[128,512]{1,0:T(8,128)(2,1)S(1)}, bf16[128,512]{1,0:T(8,128)(2,1)}, u32[]{:S(2)}) %copy-start.5) | copy-done | bytes 131096
  5.5 0.9 %copy-done.6 = bf16[128,512]{1,0:T(8,128)(2,1)S(1)} copy-done((bf16[128,512]{1,0:T(8,128)(2,1)S(1)}, bf16[128,512]{1,0:T(8,128)(2,1)}, u32[]{:S(2)}) %copy-start.6) | copy-done | bytes 131096
  6.4 0.3 shard_map.94
  6.7 5.1 %collective-permute-start.7 = (bf16[3,128,128]{2,1,0:T(8,128)(2,1)S(1)}, bf16[3,128,128]{2,1,0:T(8,128)(2,1)S(1)}, u32[]{:S(2)}, u32[]{:S(2)}) collective-permute-start(bf16[3,128,128]{2,1,0:T(8,128)(2,1)S(1)} %get-tuple-element.44), channel_id=1, source_target_pairs={{0,0},{1,16},{2,2},{3,18},{4,4},{5,20},{6,6},{7,22},{8,8},{9,24},{... | collective-permute-start | bytes 294920 | tf_op jit(solution)/shard_map/ppermute | solution.py:277
  11.9 0.5 collective-permute-start.1
  12.4 1.0 %collective-permute-start.8 = (bf16[3,128,128]{2,1,0:T(8,128)(2,1)S(1)}, bf16[3,128,128]{2,1,0:T(8,128)(2,1)S(1)}, u32[]{:S(2)}, u32[]{:S(2)}) collective-permute-start(bf16[3,128,128]{2,1,0:T(8,128)(2,1)S(1)} %get-tuple-element.45), channel_id=1, source_target_pairs={{0,4},{1,20},{2,6},{3,22},{4,8},{5,24},{6,10},{7,26},{8,12},{9,28}... | collective-permute-start | bytes 294920 | tf_op jit(solution)/shard_map/ppermute | solution.py:277
  13.4 3.6 %collective-permute-start.9 = (bf16[3,128,128]{2,1,0:T(8,128)(2,1)S(1)}, bf16[3,128,128]{2,1,0:T(8,128)(2,1)S(1)}, u32[]{:S(2)}, u32[]{:S(2)}) collective-permute-start(bf16[3,128,128]{2,1,0:T(8,128)(2,1)S(1)} %get-tuple-element.46), channel_id=1, source_target_pairs={{0,8},{1,24},{2,10},{3,26},{4,12},{5,28},{6,14},{7,30},{8,0},{9,16... | collective-permute-start | bytes 294920 | tf_op jit(solution)/shard_map/ppermute | solution.py:277
  17.1 3.7 %collective-permute-start.10 = (bf16[3,128,128]{2,1,0:T(8,128)(2,1)S(1)}, bf16[3,128,128]{2,1,0:T(8,128)(2,1)S(1)}, u32[]{:S(2)}, u32[]{:S(2)}) collective-permute-start(bf16[3,128,128]{2,1,0:T(8,128)(2,1)S(1)} %get-tuple-element.47), channel_id=1, source_target_pairs={{0,12},{1,28},{2,14},{3,30},{4,0},{5,16},{6,2},{7,18},{8,4},{9,20}... | collective-permute-start | bytes 294920 | tf_op jit(solution)/shard_map/ppermute | solution.py:277
  20.8 3.2 %collective-permute-done.10.refs_3_ = bf16[3,128,128]{2,1,0:T(8,128)(2,1)S(1)} collective-permute-done((bf16[3,128,128]{2,1,0:T(8,128)(2,1)S(1)}, bf16[3,128,128]{2,1,0:T(8,128)(2,1)S(1)}, u32[]{:S(2)}, u32[]{:S(2)}) %collective-permute-start.10) | collective-permute-done | bytes 98336 | tf_op jit(solution)/shard_map/ppermute | solution.py:277
  24.0 0.9 %copy-done.3 = bf16[4,128,256]{2,1,0:T(8,128)(2,1)S(1)} copy-done((bf16[4,128,256]{2,1,0:T(8,128)(2,1)S(1)}, bf16[4,128,256]{2,1,0:T(8,128)(2,1)}, u32[]{:S(2)}) %copy-start.3) | copy-done | bytes 262168
  24.9 0.5 shard_map.95
  25.4 1.3 %collective-permute-start.12 = (bf16[128,256]{1,0:T(8,128)(2,1)S(1)}, bf16[128,256]{1,0:T(8,128)(2,1)S(1)}, u32[]{:S(2)}, u32[]{:S(2)}) collective-permute-start(bf16[128,256]{1,0:T(8,128)(2,1)S(1)} %get-tuple-element.55), channel_id=1, source_target_pairs={{0,1},{2,3},{4,5},{6,7},{8,9},{10,11},{12,13},{14,15},{16,17},{18,... | collective-permute-start | bytes 196616 | tf_op jit(solution)/shard_map/ppermute | solution.py:290
  26.7 1.6 %copy-done = bf16[512,2048]{1,0:T(8,128)(2,1)S(1)} copy-done((bf16[512,2048]{1,0:T(8,128)(2,1)S(1)}, bf16[512,2048]{1,0:T(8,128)(2,1)}, u32[]{:S(2)}) %copy-start) | copy-done | bytes 2097176
  28.3 0.9 %copy-done.7 = bf16[128,512]{1,0:T(8,128)(2,1)S(1)} copy-done((bf16[128,512]{1,0:T(8,128)(2,1)S(1)}, bf16[128,512]{1,0:T(8,128)(2,1)}, u32[]{:S(2)}) %copy-start.7) | copy-done | bytes 131096
  29.2 0.9 %shard_map.93 = (bf16[128,128]{1,0:T(8,128)(2,1)S(1)}, bf16[128,128]{1,0:T(8,128)(2,1)S(1)}, bf16[128,128]{1,0:T(8,128)(2,1)S(1)}, bf16[128,128]{1,0:T(8,128)(2,1)S(1)}) custom-call(bf16[128,512]{1,0:T(8,128)(2,1)S(1)} %copy-done.7, bf16[128,512]{1,0:T(8,128)(2,1)S(1)} %collective-permute-done.refs_1_, bf16[128,512]{1,0:T(8,128)(2,1)S(1)} %collective-permute-done.1.refs_2_, ...), custom_call_target="tpu_custom_call" | custom-call | flops 268435456 | bytes 2752512 | tf_op jit(solution)/shard_map/pallas_call | solution.py:30
  30.1 1.9 %collective-permute-start.3 = (bf16[128,128]{1,0:T(8,128)(2,1)S(1)}, bf16[128,128]{1,0:T(8,128)(2,1)S(1)}, u32[]{:S(2)}, u32[]{:S(2)}) collective-permute-start(bf16[128,128]{1,0:T(8,128)(2,1)S(1)} %get-tuple-element.40), channel_id=1, source_target_pairs={{0,0},{1,16},{2,2},{3,18},{4,4},{5,20},{6,6},{7,22},{8,8},{9,24},{... | collective-permute-start | bytes 98312 | tf_op jit(solution)/shard_map/ppermute | solution.py:277
  32.0 2.5 %collective-permute-start.4 = (bf16[128,128]{1,0:T(8,128)(2,1)S(1)}, bf16[128,128]{1,0:T(8,128)(2,1)S(1)}, u32[]{:S(2)}, u32[]{:S(2)}) collective-permute-start(bf16[128,128]{1,0:T(8,128)(2,1)S(1)} %get-tuple-element.41), channel_id=1, source_target_pairs={{0,4},{1,20},{2,6},{3,22},{4,8},{5,24},{6,10},{7,26},{8,12},{9,28}... | collective-permute-start | bytes 98312 | tf_op jit(solution)/shard_map/ppermute | solution.py:277
  34.4 3.8 %collective-permute-start.5 = (bf16[128,128]{1,0:T(8,128)(2,1)S(1)}, bf16[128,128]{1,0:T(8,128)(2,1)S(1)}, u32[]{:S(2)}, u32[]{:S(2)}) collective-permute-start(bf16[128,128]{1,0:T(8,128)(2,1)S(1)} %get-tuple-element.42), channel_id=1, source_target_pairs={{0,8},{1,24},{2,10},{3,26},{4,12},{5,28},{6,14},{7,30},{8,0},{9,16... | collective-permute-start | bytes 98312 | tf_op jit(solution)/shard_map/ppermute | solution.py:277
  38.2 0.3 collective-permute-start.6
  38.5 0.8 %shard_map.96 = (bf16[512,256]{1,0:T(8,128)(2,1)S(1)}, bf16[4,128,128]{2,1,0:T(8,128)(2,1)S(1)}, f32[512,128]{1,0:T(8,128)S(1)}) custom-call(bf16[3,512,128]{2,1,0:T(8,128)(2,1)S(1)} %get-tuple-element.49.qkv_ref, bf16[128,256]{1,0:T(8,128)(2,1)S(1)} %get-tuple-element.50.om_ref, bf16[512,256]{1,0:T(8,128)(2,1)S(1)} %get-tuple-element.51.kf_ref, ...), custom_call_target="tpu_custom_call" | custom-call | flops 134217728 | bytes 1638400 | tf_op jit(solution)/shard_map/pallas_call | solution.py:30
  39.3 0.9 %collective-permute-done.5.refs_2_ = bf16[128,128]{1,0:T(8,128)(2,1)S(1)} collective-permute-done((bf16[128,128]{1,0:T(8,128)(2,1)S(1)}, bf16[128,128]{1,0:T(8,128)(2,1)S(1)}, u32[]{:S(2)}, u32[]{:S(2)}) %collective-permute-start.5) | collective-permute-done | bytes 32800 | tf_op jit(solution)/shard_map/ppermute | solution.py:277
  40.2 3.1 %collective-permute-done.6.refs_3_ = bf16[128,128]{1,0:T(8,128)(2,1)S(1)} collective-permute-done((bf16[128,128]{1,0:T(8,128)(2,1)S(1)}, bf16[128,128]{1,0:T(8,128)(2,1)S(1)}, u32[]{:S(2)}, u32[]{:S(2)}) %collective-permute-start.6) | collective-permute-done | bytes 32800 | tf_op jit(solution)/shard_map/ppermute | solution.py:277
  43.4 0.8 %shard_map.97 = (bf16[512,128]{1,0:T(8,128)(2,1)S(1)}, bf16[4,128,256]{2,1,0:T(8,128)(2,1)S(1)}, bf16[128,256]{1,0:T(8,128)(2,1)S(1)}, bf16[128,128]{1,0:T(8,128...) custom-call(bf16[128,128]{1,0:T(8,128)(2,1)S(1)} %collective-permute-done.3.ref, ...), custom_call_target="tpu_custom_call" | custom-call | flops 67108864 | bytes 1310720 | tf_op jit(solution)/shard_map/pallas_call | solution.py:30
  44.1 1.9 %collective-permute-start.13 = (bf16[128,128]{1,0:T(8,128)(2,1)S(1)}, bf16[128,128]{1,0:T(8,128)(2,1)S(1)}, u32[]{:S(2)}, u32[]{:S(2)}) collective-permute-start(bf16[128,128]{1,0:T(8,128)(2,1)S(1)} %get-tuple-element.56), channel_id=1, source_target_pairs={{0,0},{16,1},{2,2},{18,3},{4,4},{20,5},{6,6},{22,7},{8,8},{24,9},{... | collective-permute-start | bytes 98312 | tf_op jit(solution)/shard_map/ppermute | solution.py:283
  46.1 1.3 %collective-permute-start.14 = (bf16[128,128]{1,0:T(8,128)(2,1)S(1)}, bf16[128,128]{1,0:T(8,128)(2,1)S(1)}, u32[]{:S(2)}, u32[]{:S(2)}) collective-permute-start(bf16[128,128]{1,0:T(8,128)(2,1)S(1)} %get-tuple-element.57), channel_id=1, source_target_pairs={{4,0},{20,1},{6,2},{22,3},{8,4},{24,5},{10,6},{26,7},{12,8},{28,9}... | collective-permute-start | bytes 98312 | tf_op jit(solution)/shard_map/ppermute | solution.py:283
  47.4 2.3 %collective-permute-start.15 = (bf16[128,128]{1,0:T(8,128)(2,1)S(1)}, bf16[128,128]{1,0:T(8,128)(2,1)S(1)}, u32[]{:S(2)}, u32[]{:S(2)}) collective-permute-start(bf16[128,128]{1,0:T(8,128)(2,1)S(1)} %get-tuple-element.58), channel_id=1, source_target_pairs={{8,0},{24,1},{10,2},{26,3},{12,4},{28,5},{14,6},{30,7},{0,8},{16,9... | collective-permute-start | bytes 98312 | tf_op jit(solution)/shard_map/ppermute | solution.py:283
  49.7 0.6 collective-permute-done.13.refs_0_
  50.3 1.0 %collective-permute-done.14.refs_1_ = bf16[128,128]{1,0:T(8,128)(2,1)S(1)} collective-permute-done((bf16[128,128]{1,0:T(8,128)(2,1)S(1)}, bf16[128,128]{1,0:T(8,128)(2,1)S(1)}, u32[]{:S(2)}, u32[]{:S(2)}) %collective-permute-start.14) | collective-permute-done | bytes 32800 | tf_op jit(solution)/shard_map/ppermute | solution.py:283
  51.3 1.2 %collective-permute-done.15.refs_2_ = bf16[128,128]{1,0:T(8,128)(2,1)S(1)} collective-permute-done((bf16[128,128]{1,0:T(8,128)(2,1)S(1)}, bf16[128,128]{1,0:T(8,128)(2,1)S(1)}, u32[]{:S(2)}, u32[]{:S(2)}) %collective-permute-start.15) | collective-permute-done | bytes 32800 | tf_op jit(solution)/shard_map/ppermute | solution.py:283
  52.5 3.2 %collective-permute-done.16.refs_3_ = bf16[128,128]{1,0:T(8,128)(2,1)S(1)} collective-permute-done((bf16[128,128]{1,0:T(8,128)(2,1)S(1)}, bf16[128,128]{1,0:T(8,128)(2,1)S(1)}, u32[]{:S(2)}, u32[]{:S(2)}) %collective-permute-start.16) | collective-permute-done | bytes 32800 | tf_op jit(solution)/shard_map/ppermute | solution.py:283
  55.7 0.5 shard_map.98
  56.2 2.4 %collective-permute-start.19 = (bf16[128,256]{1,0:T(8,128)(2,1)S(1)}, bf16[128,256]{1,0:T(8,128)(2,1)S(1)}, u32[]{:S(2)}, u32[]{:S(2)}) collective-permute-start(bf16[128,256]{1,0:T(8,128)(2,1)S(1)} %get-tuple-element.68), channel_id=1, source_target_pairs={{1,0},{3,2},{5,4},{7,6},{9,8},{11,10},{13,12},{15,14},{17,16},{19,... | collective-permute-start | bytes 196616 | tf_op jit(solution)/shard_map/ppermute | solution.py:290
  58.8 0.3 collective-permute-start.18
  59.1 1.5 %shard_map.99 = (bf16[512,128]{1,0:T(8,128)(2,1)S(1)}, f32[512,128]{1,0:T(8,128)S(1)}, f32[512,256]{1,0:T(8,128)S(1)}) custom-call(bf16[3,512,128]{2,1,0:T(8,128)(2,1)S(1)} %get-tuple-element.49.qkv_ref, bf16[128,256]{1,0:T(8,128)(2,1)S(1)} %get-tuple-element.50.om_ref, bf16[512,256]{1,0:T(8,128)(2,1)S(1)} %get-tuple-element.51.kf_ref, ...), custom_call_target="tpu_custom_call" | custom-call | flops 268435456 | bytes 2752512 | tf_op jit(solution)/shard_map/pallas_call | solution.py:30
  60.6 0.6 shard_map.100
  61.2 1.9 %collective-permute-start.20 = (bf16[3,128,128]{2,1,0:T(8,128)(2,1)S(1)}, bf16[3,128,128]{2,1,0:T(8,128)(2,1)S(1)}, u32[]{:S(2)}, u32[]{:S(2)}) collective-permute-start(bf16[3,128,128]{2,1,0:T(8,128)(2,1)S(1)} %get-tuple-element.69), channel_id=1, source_target_pairs={{0,0},{16,1},{2,2},{18,3},{4,4},{20,5},{6,6},{22,7},{8,8},{24,9},{... | collective-permute-start | bytes 294920 | tf_op jit(solution)/shard_map/ppermute | solution.py:283
  63.1 2.1 %collective-permute-start.21 = (bf16[3,128,128]{2,1,0:T(8,128)(2,1)S(1)}, bf16[3,128,128]{2,1,0:T(8,128)(2,1)S(1)}, u32[]{:S(2)}, u32[]{:S(2)}) collective-permute-start(bf16[3,128,128]{2,1,0:T(8,128)(2,1)S(1)} %get-tuple-element.70), channel_id=1, source_target_pairs={{4,0},{20,1},{6,2},{22,3},{8,4},{24,5},{10,6},{26,7},{12,8},{28,9}... | collective-permute-start | bytes 294920 | tf_op jit(solution)/shard_map/ppermute | solution.py:283
  65.2 1.0 %collective-permute-start.22 = (bf16[3,128,128]{2,1,0:T(8,128)(2,1)S(1)}, bf16[3,128,128]{2,1,0:T(8,128)(2,1)S(1)}, u32[]{:S(2)}, u32[]{:S(2)}) collective-permute-start(bf16[3,128,128]{2,1,0:T(8,128)(2,1)S(1)} %get-tuple-element.71), channel_id=1, source_target_pairs={{8,0},{24,1},{10,2},{26,3},{12,4},{28,5},{14,6},{30,7},{0,8},{16,9... | collective-permute-start | bytes 294920 | tf_op jit(solution)/shard_map/ppermute | solution.py:283
  66.2 0.8 %collective-permute-start.23 = (bf16[3,128,128]{2,1,0:T(8,128)(2,1)S(1)}, bf16[3,128,128]{2,1,0:T(8,128)(2,1)S(1)}, u32[]{:S(2)}, u32[]{:S(2)}) collective-permute-start(bf16[3,128,128]{2,1,0:T(8,128)(2,1)S(1)} %get-tuple-element.72), channel_id=1, source_target_pairs={{12,0},{28,1},{14,2},{30,3},{0,4},{16,5},{2,6},{18,7},{4,8},{20,9}... | collective-permute-start | bytes 294920 | tf_op jit(solution)/shard_map/ppermute | solution.py:283
  67.0 2.4 %collective-permute-done.20.refs_0_ = bf16[3,128,128]{2,1,0:T(8,128)(2,1)S(1)} collective-permute-done((bf16[3,128,128]{2,1,0:T(8,128)(2,1)S(1)}, bf16[3,128,128]{2,1,0:T(8,128)(2,1)S(1)}, u32[]{:S(2)}, u32[]{:S(2)}) %collective-permute-start.20) | collective-permute-done | bytes 98336 | tf_op jit(solution)/shard_map/ppermute | solution.py:283
  69.4 1.2 %collective-permute-done.21.refs_1_ = bf16[3,128,128]{2,1,0:T(8,128)(2,1)S(1)} collective-permute-done((bf16[3,128,128]{2,1,0:T(8,128)(2,1)S(1)}, bf16[3,128,128]{2,1,0:T(8,128)(2,1)S(1)}, u32[]{:S(2)}, u32[]{:S(2)}) %collective-permute-start.21) | collective-permute-done | bytes 98336 | tf_op jit(solution)/shard_map/ppermute | solution.py:283
  70.6 0.5 collective-permute-done.22.refs_2_
  71.1 2.6 %collective-permute-done.23.refs_3_ = bf16[3,128,128]{2,1,0:T(8,128)(2,1)S(1)} collective-permute-done((bf16[3,128,128]{2,1,0:T(8,128)(2,1)S(1)}, bf16[3,128,128]{2,1,0:T(8,128)(2,1)S(1)}, u32[]{:S(2)}, u32[]{:S(2)}) %collective-permute-start.23) | collective-permute-done | bytes 98336 | tf_op jit(solution)/shard_map/ppermute | solution.py:283
  73.7 0.8 %shard_map.101 = (bf16[128,512]{1,0:T(8,128)(2,1)}, bf16[128,512]{1,0:T(8,128)(2,1)}, bf16[128,512]{1,0:T(8,128)(2,1)}) custom-call(bf16[3,128,128]{2,1,0:T(8,128)(2,1)S(1)} %collective-permute-done.20.refs_0_, bf16[3,128,128]{2,1,0:T(8,128)(2,1)S(1)} %collective-permute-done.21.refs_1_, bf16[3,128,128]{2,1,0:T(8,128)(2,1)S(1)} %collective-permute-done.22.refs_2_, ...), custom_call_target="tpu_custom_call" | custom-call | bytes 786432 | tf_op jit(solution)/shard_map/pallas_call | solution.py:30
  74.5 0.7 fusion.2
  (28 shorter events, 0.4 us)
Async XLA Ops:
  0.6 11.7 %collective-permute-start = (bf16[128,512]{1,0:T(8,128)(2,1)}, bf16[128,512]{1,0:T(8,128)(2,1)S(1)}, u32[]{:S(2)}, u32[]{:S(2)}) collective-permute-start(bf16[128,512]{1,0:T(8,128)(2,1)} %refs_0_.1), channel_id=1, source_target_pairs={{0,2},{1,3},{2,0},{3,1},{4,6},{5,7},{6,4},{7,5},{8,10},{9,11},{10,... | collective-permute-start | bytes 393224 | tf_op jit(solution)/shard_map/ppermute | solution.py:158
  2.7 0.9 %copy-start.2 = (bf16[4,128,256]{2,1,0:T(8,128)(2,1)S(1)}, bf16[4,128,256]{2,1,0:T(8,128)(2,1)}, u32[]{:S(2)}) copy-start(bf16[4,128,256]{2,1,0:T(8,128)(2,1)} %refs_4_.4) | copy-start | bytes 786436
  3.7 0.9 %copy-start.4 = (bf16[128,512]{1,0:T(8,128)(2,1)S(1)}, bf16[128,512]{1,0:T(8,128)(2,1)}, u32[]{:S(2)}) copy-start(bf16[128,512]{1,0:T(8,128)(2,1)} %q_ref.1) | copy-start | bytes 393220
  4.6 0.9 %copy-start.5 = (bf16[128,512]{1,0:T(8,128)(2,1)S(1)}, bf16[128,512]{1,0:T(8,128)(2,1)}, u32[]{:S(2)}) copy-start(bf16[128,512]{1,0:T(8,128)(2,1)} %k_ref.1) | copy-start | bytes 393220
  5.5 0.9 %copy-start.6 = (bf16[128,512]{1,0:T(8,128)(2,1)S(1)}, bf16[128,512]{1,0:T(8,128)(2,1)}, u32[]{:S(2)}) copy-start(bf16[128,512]{1,0:T(8,128)(2,1)} %v_ref.1) | copy-start | bytes 393220
  6.7 10.3 %collective-permute-start.7 = (bf16[3,128,128]{2,1,0:T(8,128)(2,1)S(1)}, bf16[3,128,128]{2,1,0:T(8,128)(2,1)S(1)}, u32[]{:S(2)}, u32[]{:S(2)}) collective-permute-start(bf16[3,128,128]{2,1,0:T(8,128)(2,1)S(1)} %get-tuple-element.44), channel_id=1, source_target_pairs={{0,0},{1,16},{2,2},{3,18},{4,4},{5,20},{6,6},{7,22},{8,8},{9,24},{... | collective-permute-start | bytes 294920 | tf_op jit(solution)/shard_map/ppermute | solution.py:277
  11.8 1.6 %collective-permute-start.11 = (bf16[128,256]{1,0:T(8,128)(2,1)S(1)}, bf16[128,256]{1,0:T(8,128)(2,1)S(1)}, u32[]{:S(2)}, u32[]{:S(2)}) collective-permute-start(bf16[128,256]{1,0:T(8,128)(2,1)S(1)} %get-tuple-element.48), channel_id=1, source_target_pairs={{0,1},{1,0},{2,3},{3,2},{4,5},{5,4},{6,7},{7,6},{8,9},{9,8},{10,11... | collective-permute-start | bytes 196616 | tf_op jit(solution)/shard_map/ppermute | solution.py:158
  11.9 14.8 %collective-permute-start.1 = (bf16[128,512]{1,0:T(8,128)(2,1)}, bf16[128,512]{1,0:T(8,128)(2,1)S(1)}, u32[]{:S(2)}, u32[]{:S(2)}) collective-permute-start(bf16[128,512]{1,0:T(8,128)(2,1)} %refs_0_.1), channel_id=1, source_target_pairs={{0,1},{1,0},{2,3},{3,2},{4,5},{5,4},{6,7},{7,6},{8,9},{9,8},{10,11... | collective-permute-start | bytes 393224 | tf_op jit(solution)/shard_map/ppermute | solution.py:158
  12.4 14.3 %collective-permute-start.2 = (bf16[128,512]{1,0:T(8,128)(2,1)S(1)}, bf16[128,512]{1,0:T(8,128)(2,1)S(1)}, u32[]{:S(2)}, u32[]{:S(2)}) collective-permute-start(bf16[128,512]{1,0:T(8,128)(2,1)S(1)} %collective-permute-done.refs_1_), channel_id=1, source_target_pairs={{0,1},{1,0},{2,3},{3,2},{4,5},{5,4},{6,7},{7,6},{8,9},{9,8},{10,11... | collective-permute-start | bytes 393224 | tf_op jit(solution)/shard_map/ppermute | solution.py:158
  12.4 8.3 %collective-permute-start.8 = (bf16[3,128,128]{2,1,0:T(8,128)(2,1)S(1)}, bf16[3,128,128]{2,1,0:T(8,128)(2,1)S(1)}, u32[]{:S(2)}, u32[]{:S(2)}) collective-permute-start(bf16[3,128,128]{2,1,0:T(8,128)(2,1)S(1)} %get-tuple-element.45), channel_id=1, source_target_pairs={{0,4},{1,20},{2,6},{3,22},{4,8},{5,24},{6,10},{7,26},{8,12},{9,28}... | collective-permute-start | bytes 294920 | tf_op jit(solution)/shard_map/ppermute | solution.py:277
  13.4 7.4 %collective-permute-start.9 = (bf16[3,128,128]{2,1,0:T(8,128)(2,1)S(1)}, bf16[3,128,128]{2,1,0:T(8,128)(2,1)S(1)}, u32[]{:S(2)}, u32[]{:S(2)}) collective-permute-start(bf16[3,128,128]{2,1,0:T(8,128)(2,1)S(1)} %get-tuple-element.46), channel_id=1, source_target_pairs={{0,8},{1,24},{2,10},{3,26},{4,12},{5,28},{6,14},{7,30},{8,0},{9,16... | collective-permute-start | bytes 294920 | tf_op jit(solution)/shard_map/ppermute | solution.py:277
  17.1 6.9 %collective-permute-start.10 = (bf16[3,128,128]{2,1,0:T(8,128)(2,1)S(1)}, bf16[3,128,128]{2,1,0:T(8,128)(2,1)S(1)}, u32[]{:S(2)}, u32[]{:S(2)}) collective-permute-start(bf16[3,128,128]{2,1,0:T(8,128)(2,1)S(1)} %get-tuple-element.47), channel_id=1, source_target_pairs={{0,12},{1,28},{2,14},{3,30},{4,0},{5,16},{6,2},{7,18},{8,4},{9,20}... | collective-permute-start | bytes 294920 | tf_op jit(solution)/shard_map/ppermute | solution.py:277
  24.0 1.0 %copy-start.3 = (bf16[4,128,256]{2,1,0:T(8,128)(2,1)S(1)}, bf16[4,128,256]{2,1,0:T(8,128)(2,1)}, u32[]{:S(2)}) copy-start(bf16[4,128,256]{2,1,0:T(8,128)(2,1)} %refs_4_.4) | copy-start | bytes 786436
  25.4 13.9 %collective-permute-start.12 = (bf16[128,256]{1,0:T(8,128)(2,1)S(1)}, bf16[128,256]{1,0:T(8,128)(2,1)S(1)}, u32[]{:S(2)}, u32[]{:S(2)}) collective-permute-start(bf16[128,256]{1,0:T(8,128)(2,1)S(1)} %get-tuple-element.55), channel_id=1, source_target_pairs={{0,1},{2,3},{4,5},{6,7},{8,9},{10,11},{12,13},{14,15},{16,17},{18,... | collective-permute-start | bytes 196616 | tf_op jit(solution)/shard_map/ppermute | solution.py:290
  26.7 1.6 %copy-start = (bf16[512,2048]{1,0:T(8,128)(2,1)S(1)}, bf16[512,2048]{1,0:T(8,128)(2,1)}, u32[]{:S(2)}) copy-start(bf16[512,2048]{1,0:T(8,128)(2,1)} %refs_4_.5) | copy-start | bytes 6291460
  28.3 0.9 %copy-start.7 = (bf16[128,512]{1,0:T(8,128)(2,1)S(1)}, bf16[128,512]{1,0:T(8,128)(2,1)}, u32[]{:S(2)}) copy-start(bf16[128,512]{1,0:T(8,128)(2,1)} %refs_0_.1) | copy-start | bytes 393220
  29.2 26.5 %copy-start.1 = (bf16[512,2048]{1,0:T(8,128)(2,1)S(1)}, bf16[512,2048]{1,0:T(8,128)(2,1)}, u32[]{:S(2)}) copy-start(bf16[512,2048]{1,0:T(8,128)(2,1)} %refs_4_.5) | copy-start | bytes 6291460
  30.1 9.2 %collective-permute-start.3 = (bf16[128,128]{1,0:T(8,128)(2,1)S(1)}, bf16[128,128]{1,0:T(8,128)(2,1)S(1)}, u32[]{:S(2)}, u32[]{:S(2)}) collective-permute-start(bf16[128,128]{1,0:T(8,128)(2,1)S(1)} %get-tuple-element.40), channel_id=1, source_target_pairs={{0,0},{1,16},{2,2},{3,18},{4,4},{5,20},{6,6},{7,22},{8,8},{9,24},{... | collective-permute-start | bytes 98312 | tf_op jit(solution)/shard_map/ppermute | solution.py:277
  32.0 7.3 %collective-permute-start.4 = (bf16[128,128]{1,0:T(8,128)(2,1)S(1)}, bf16[128,128]{1,0:T(8,128)(2,1)S(1)}, u32[]{:S(2)}, u32[]{:S(2)}) collective-permute-start(bf16[128,128]{1,0:T(8,128)(2,1)S(1)} %get-tuple-element.41), channel_id=1, source_target_pairs={{0,4},{1,20},{2,6},{3,22},{4,8},{5,24},{6,10},{7,26},{8,12},{9,28}... | collective-permute-start | bytes 98312 | tf_op jit(solution)/shard_map/ppermute | solution.py:277
  34.4 5.8 %collective-permute-start.5 = (bf16[128,128]{1,0:T(8,128)(2,1)S(1)}, bf16[128,128]{1,0:T(8,128)(2,1)S(1)}, u32[]{:S(2)}, u32[]{:S(2)}) collective-permute-start(bf16[128,128]{1,0:T(8,128)(2,1)S(1)} %get-tuple-element.42), channel_id=1, source_target_pairs={{0,8},{1,24},{2,10},{3,26},{4,12},{5,28},{6,14},{7,30},{8,0},{9,16... | collective-permute-start | bytes 98312 | tf_op jit(solution)/shard_map/ppermute | solution.py:277
  38.2 5.1 %collective-permute-start.6 = (bf16[128,128]{1,0:T(8,128)(2,1)S(1)}, bf16[128,128]{1,0:T(8,128)(2,1)S(1)}, u32[]{:S(2)}, u32[]{:S(2)}) collective-permute-start(bf16[128,128]{1,0:T(8,128)(2,1)S(1)} %get-tuple-element.43), channel_id=1, source_target_pairs={{0,12},{1,28},{2,14},{3,30},{4,0},{5,16},{6,2},{7,18},{8,4},{9,20}... | collective-permute-start | bytes 98312 | tf_op jit(solution)/shard_map/ppermute | solution.py:277
  44.1 6.1 %collective-permute-start.13 = (bf16[128,128]{1,0:T(8,128)(2,1)S(1)}, bf16[128,128]{1,0:T(8,128)(2,1)S(1)}, u32[]{:S(2)}, u32[]{:S(2)}) collective-permute-start(bf16[128,128]{1,0:T(8,128)(2,1)S(1)} %get-tuple-element.56), channel_id=1, source_target_pairs={{0,0},{16,1},{2,2},{18,3},{4,4},{20,5},{6,6},{22,7},{8,8},{24,9},{... | collective-permute-start | bytes 98312 | tf_op jit(solution)/shard_map/ppermute | solution.py:283
  46.1 5.2 %collective-permute-start.14 = (bf16[128,128]{1,0:T(8,128)(2,1)S(1)}, bf16[128,128]{1,0:T(8,128)(2,1)S(1)}, u32[]{:S(2)}, u32[]{:S(2)}) collective-permute-start(bf16[128,128]{1,0:T(8,128)(2,1)S(1)} %get-tuple-element.57), channel_id=1, source_target_pairs={{4,0},{20,1},{6,2},{22,3},{8,4},{24,5},{10,6},{26,7},{12,8},{28,9}... | collective-permute-start | bytes 98312 | tf_op jit(solution)/shard_map/ppermute | solution.py:283
  47.4 5.1 %collective-permute-start.15 = (bf16[128,128]{1,0:T(8,128)(2,1)S(1)}, bf16[128,128]{1,0:T(8,128)(2,1)S(1)}, u32[]{:S(2)}, u32[]{:S(2)}) collective-permute-start(bf16[128,128]{1,0:T(8,128)(2,1)S(1)} %get-tuple-element.58), channel_id=1, source_target_pairs={{8,0},{24,1},{10,2},{26,3},{12,4},{28,5},{14,6},{30,7},{0,8},{16,9... | collective-permute-start | bytes 98312 | tf_op jit(solution)/shard_map/ppermute | solution.py:283
  49.7 6.0 %collective-permute-start.16 = (bf16[128,128]{1,0:T(8,128)(2,1)S(1)}, bf16[128,128]{1,0:T(8,128)(2,1)S(1)}, u32[]{:S(2)}, u32[]{:S(2)}) collective-permute-start(bf16[128,128]{1,0:T(8,128)(2,1)S(1)} %get-tuple-element.59), channel_id=1, source_target_pairs={{12,0},{28,1},{14,2},{30,3},{0,4},{16,5},{2,6},{18,7},{4,8},{20,9}... | collective-permute-start | bytes 98312 | tf_op jit(solution)/shard_map/ppermute | solution.py:283
  56.2 2.5 %collective-permute-start.17 = (bf16[2,128,512]{2,1,0:T(8,128)(2,1)S(1)}, bf16[2,128,512]{2,1,0:T(8,128)(2,1)S(1)}, u32[]{:S(2)}, u32[]{:S(2)}) collective-permute-start(bf16[2,128,512]{2,1,0:T(8,128)(2,1)S(1)} %get-tuple-element.61), channel_id=1, source_target_pairs={{0,1},{1,0},{2,3},{3,2},{4,5},{5,4},{6,7},{7,6},{8,9},{9,8},{10,11... | collective-permute-start | bytes 786440 | tf_op jit(solution)/shard_map/ppermute | solution.py:158
  56.2 4.3 %collective-permute-start.19 = (bf16[128,256]{1,0:T(8,128)(2,1)S(1)}, bf16[128,256]{1,0:T(8,128)(2,1)S(1)}, u32[]{:S(2)}, u32[]{:S(2)}) collective-permute-start(bf16[128,256]{1,0:T(8,128)(2,1)S(1)} %get-tuple-element.68), channel_id=1, source_target_pairs={{1,0},{3,2},{5,4},{7,6},{9,8},{11,10},{13,12},{15,14},{17,16},{19,... | collective-permute-start | bytes 196616 | tf_op jit(solution)/shard_map/ppermute | solution.py:290
  58.8 15.7 %collective-permute-start.18 = (bf16[1,128,512]{2,1,0:T(8,128)(2,1)S(1)}, bf16[1,128,512]{2,1,0:T(8,128)(2,1)S(1)}, u32[]{:S(2)}, u32[]{:S(2)}) collective-permute-start(bf16[1,128,512]{2,1,0:T(8,128)(2,1)S(1)} %fusion.3), channel_id=1, source_target_pairs={{0,2},{1,3},{2,0},{3,1},{4,6},{5,7},{6,4},{7,5},{8,10},{9,11},{10,... | collective-permute-start | bytes 393224 | tf_op jit(solution)/shard_map/ppermute | solution.py:158
  61.2 8.2 %collective-permute-start.20 = (bf16[3,128,128]{2,1,0:T(8,128)(2,1)S(1)}, bf16[3,128,128]{2,1,0:T(8,128)(2,1)S(1)}, u32[]{:S(2)}, u32[]{:S(2)}) collective-permute-start(bf16[3,128,128]{2,1,0:T(8,128)(2,1)S(1)} %get-tuple-element.69), channel_id=1, source_target_pairs={{0,0},{16,1},{2,2},{18,3},{4,4},{20,5},{6,6},{22,7},{8,8},{24,9},{... | collective-permute-start | bytes 294920 | tf_op jit(solution)/shard_map/ppermute | solution.py:283
  63.1 7.5 %collective-permute-start.21 = (bf16[3,128,128]{2,1,0:T(8,128)(2,1)S(1)}, bf16[3,128,128]{2,1,0:T(8,128)(2,1)S(1)}, u32[]{:S(2)}, u32[]{:S(2)}) collective-permute-start(bf16[3,128,128]{2,1,0:T(8,128)(2,1)S(1)} %get-tuple-element.70), channel_id=1, source_target_pairs={{4,0},{20,1},{6,2},{22,3},{8,4},{24,5},{10,6},{26,7},{12,8},{28,9}... | collective-permute-start | bytes 294920 | tf_op jit(solution)/shard_map/ppermute | solution.py:283
  65.2 5.9 %collective-permute-start.22 = (bf16[3,128,128]{2,1,0:T(8,128)(2,1)S(1)}, bf16[3,128,128]{2,1,0:T(8,128)(2,1)S(1)}, u32[]{:S(2)}, u32[]{:S(2)}) collective-permute-start(bf16[3,128,128]{2,1,0:T(8,128)(2,1)S(1)} %get-tuple-element.71), channel_id=1, source_target_pairs={{8,0},{24,1},{10,2},{26,3},{12,4},{28,5},{14,6},{30,7},{0,8},{16,9... | collective-permute-start | bytes 294920 | tf_op jit(solution)/shard_map/ppermute | solution.py:283
  66.2 7.5 %collective-permute-start.23 = (bf16[3,128,128]{2,1,0:T(8,128)(2,1)S(1)}, bf16[3,128,128]{2,1,0:T(8,128)(2,1)S(1)}, u32[]{:S(2)}, u32[]{:S(2)}) collective-permute-start(bf16[3,128,128]{2,1,0:T(8,128)(2,1)S(1)} %get-tuple-element.72), channel_id=1, source_target_pairs={{12,0},{28,1},{14,2},{30,3},{0,4},{16,5},{2,6},{18,7},{4,8},{20,9}... | collective-permute-start | bytes 294920 | tf_op jit(solution)/shard_map/ppermute | solution.py:283

commit v3 on v2

--- a/solution.py
+++ b/solution.py
@@ -10,6 +10,7 @@
 EPSILON = 1e-05
 VMEM = pl.BlockSpec(memory_space=pltpu.VMEM)
 SMEM = pl.BlockSpec(memory_space=pltpu.SMEM)
+ANY = pl.BlockSpec(memory_space=pl.ANY)
 HBM = pl.BlockSpec(memory_space=pltpu.HBM)
 NN = (((1,), (0,)), ((), ()))
 NT = (((1,), (1,)), ((), ()))
@@ -24,7 +25,7 @@
     return x.astype(jnp.bfloat16)
 
 
-def call(body, outs, *args, flops=0, specs=None, scratch=()):
+def call(body, outs, *args, flops=0, specs=None, scratch=(), vmem=32):
     size = sum(a.size * a.dtype.itemsize for a in args)
     size += sum(o.size * o.dtype.itemsize for o in outs)
     return pl.pallas_call(
@@ -34,7 +35,7 @@
         out_specs=[VMEM] * len(outs),
         scratch_shapes=list(scratch),
         cost_estimate=pl.CostEstimate(flops=flops, bytes_accessed=size, transcendentals=0),
-        compiler_params=pltpu.CompilerParams(vmem_limit_bytes=32 * 1024 * 1024),
+        compiler_params=pltpu.CompilerParams(vmem_limit_bytes=vmem * 1024 * 1024),
     )(*args)
 
 
@@ -184,11 +185,12 @@
 
 
 def reduce_blocks(own, sent, bits):
-    total = own.astype(jnp.float32) + swap(sent, "head", 1).astype(jnp.float32)
+    got = swap(sent, "head", 1)
     for bit in bits[1:]:
+        total = own.astype(jnp.float32) + got.astype(jnp.float32)
         pairs = total.reshape((total.shape[0] // 2, 2) + total.shape[1:])
-        total = pairs[:, 0] + swap(bf(pairs[:, 1]), "head", bit).astype(jnp.float32)
-    return bf(total[0])
+        own, got = pairs[:, 0], swap(bf(pairs[:, 1]), "head", bit)
+    return own[0].astype(jnp.float32), got[0]
 
 
 def scanned(queries, key_vectors, value_vectors, feature_proj, out_weight, grad_output):
@@ -238,7 +240,8 @@
         [struct((split // 2, rows, width))] * 2,
         me, mixed, out_weight, flops=2 * rows * out_weight.size, specs=[SMEM, VMEM, VMEM],
     )
-    layer_out = reduce_blocks(own, sent, bits)
+    part, last = reduce_blocks(own, sent, bits)
+    layer_out = bf(part + last.astype(jnp.float32))
 
     gq, gv_part, gkf_part = call(
         functools.partial(query_kernel, heads),
@@ -294,11 +297,11 @@
     return pl.ds(pl.multiple_of(index * width, 128), width)
 
 
-def pack_kernel(n, q_ref, k_ref, v_ref, om_ref, *rest):
-    outs, om_out, sems = rest[:n], rest[n], rest[n + 1]
+def pack_kernel(n, q_ref, k_ref, v_ref, om_ref, go_ref, *rest):
+    outs, om_out, go_out, sems = rest[:n], rest[n], rest[n + 1], rest[n + 2]
     s, _ = spot()
     dim = om_ref.shape[1]
-    copies = []
+    copies = [(go_ref, go_out)]
     for k in range(n):
         cols = lane(lax.rem(s + k, n), dim)
         for at, ref in enumerate((q_ref, k_ref, v_ref)):
@@ -313,13 +316,20 @@
 
 def grad_mixed_kernel(n, offsets, *refs):
     blocks, w_ref = refs[: len(offsets)], refs[len(offsets)]
-    outs, scr = refs[len(offsets) + 1 : -1], refs[-1]
+    outs, (scr, w_scr, sems) = refs[len(offsets) + 1 : -3], refs[-3:]
     s, h = spot()
     width = blocks[0].shape[1]
     dim = outs[0].shape[1]
+    copies = [
+        pltpu.make_async_copy(w_ref.at[:, lane(h ^ offset, width)], w_scr.at[at], sems.at[at])
+        for at, offset in enumerate(offsets)
+    ]
+    for copy in copies:
+        copy.start()
     total = None
-    for offset, ref in zip(offsets, blocks):
-        part = mm(ref[...], w_ref[:, lane(h ^ offset, width)], NT)
+    for at, ref in enumerate(blocks):
+        copies[at].wait()
+        part = mm(ref[...], w_scr[at], NT)
         total = part if total is None else total + part
     scr[...] = bf(total)
     for k in range(n):
@@ -328,7 +338,7 @@
 
 def first_kernel(n, *refs):
     got, own_om_ref, om_in_ref = refs[:n], refs[n], refs[n + 1]
-    qkv_ref, om_ref, kf_ref, state_ref, total_ref = refs[n + 2 :]
+    qkv_ref, om_ref, kf_ref, state_ref, total_ref = refs[n + 3 :]
     s, h = spot()
     rows, dim = got[0].shape[1:]
     scale = dim ** (-0.25)
@@ -336,7 +346,7 @@
         at = pl.ds(pl.multiple_of(lax.rem(s + n - k, n) * rows, 128), rows)
         qkv_ref[:, at, :] = got[k][...]
     mine = lax.div(s, n) == lax.rem(h, 2)
-    om = jnp.where(mine, own_om_ref[lax.rem(s, n)], om_in_ref[...])
+    om = jnp.where(mine, own_om_ref[...], om_in_ref[...])
     om_ref[...] = om
     k_all = qkv_ref[1]
     wide = k_all.astype(jnp.float32)
@@ -433,7 +443,7 @@
 
 
 def mixed_project_kernel(n, offsets, *refs):
-    mixed_in, w_ref, own_ref, sent_ref, scr = refs[:n], *refs[n:]
+    mixed_in, (w_ref, _, own_ref, sent_ref, scr) = refs[:n], refs[n:]
     s, h = spot()
     width = own_ref.shape[2]
     dim = mixed_in[0].shape[1]
@@ -450,9 +460,10 @@
 
 
 def unpack_kernel(n, *refs):
-    got, outs = refs[:n], refs[n:]
+    got, (part_ref, last_ref), (out_ref, *outs) = refs[:n], refs[n : n + 2], refs[n + 2 :]
     s, _ = spot()
     dim = got[0].shape[2]
+    out_ref[...] = bf(part_ref[...] + last_ref[...].astype(jnp.float32))
     for k in range(n):
         cols = lane(lax.rem(s + k, n), dim)
         for at, out in enumerate(outs):
@@ -468,23 +479,28 @@
     macs = long * dim * feats * 2
     f32 = jnp.float32
 
-    *sends, om_sent = call(
+    *sends, om_own, go = call(
         functools.partial(pack_kernel, n),
-        [struct((3, rows, dim))] * n + [struct((dim, feats))],
-        queries, key_vectors, value_vectors, feature_proj,
-        specs=[HBM] * 4, scratch=[pltpu.SemaphoreType.DMA((3 * n + 1,))],
-    )
-    offsets, blocks = [0], [grad_output]
+        [struct((3, rows, dim))] * n + [struct((dim, feats)), struct(grad_output.shape)],
+        queries, key_vectors, value_vectors, feature_proj, grad_output,
+        specs=[HBM] * 5, scratch=[pltpu.SemaphoreType.DMA((3 * n + 2,))], vmem=60,
+    )
+    offsets, blocks = [0], [go]
     for bit in reversed(bits):
         blocks = blocks + [swap(b, "head", bit) for b in blocks]
         offsets = offsets + [o ^ bit for o in offsets]
-    om_in = swap(om_sent, "head", 1)
+    om_in = swap(om_own, "head", 1)
     got = scatter(sends)
     gm_parts = call(
         functools.partial(grad_mixed_kernel, n, offsets),
         [struct((rows, dim))] * n,
         *blocks, out_weight, flops=2 * rows * out_weight.size,
-        scratch=[pltpu.VMEM((rows, n * dim), jnp.bfloat16)],
+        specs=[VMEM] * split + [HBM], vmem=59,
+        scratch=[
+            pltpu.VMEM((rows, n * dim), jnp.bfloat16),
+            pltpu.VMEM((split, n * dim, width), jnp.bfloat16),
+            pltpu.SemaphoreType.DMA((split,)),
+        ],
     )
     gm_in = scatter(gm_parts)
     qkv, om, kf, state, total = call(
@@ -496,7 +512,8 @@
             struct((n, dim, feats)),
             struct((dim, feats)),
         ],
-        *got, feature_proj, om_in, flops=2 * macs,
+        *got, om_own, om_in, gm_parts[0], flops=2 * macs,
+        specs=[VMEM] * (n + 2) + [ANY],
     )
     carried = pass_on(total, True)
     qf, scores, num = call(
@@ -531,14 +548,16 @@
     own, sent = call(
         functools.partial(mixed_project_kernel, n, order),
         [struct((split // 2, rows, width))] * 2,
-        *mixed_in, out_weight, flops=2 * rows * out_weight.size,
+        *mixed_in, out_weight, grads[0], flops=2 * rows * out_weight.size,
+        specs=[VMEM] * (n + 1) + [ANY],
         scratch=[pltpu.VMEM((rows, n * dim), jnp.bfloat16)],
     )
-    layer_out = reduce_blocks(own, sent, bits)
-    gq, gk, gv = call(
-        functools.partial(unpack_kernel, n), [struct((rows, n * dim))] * 3, *grads_in
-    )
-    return layer_out, gq, gk, gv
+    part, last = reduce_blocks(own, sent, bits)
+    return call(
+        functools.partial(unpack_kernel, n),
+        [struct((rows, width))] + [struct((rows, n * dim))] * 3,
+        *grads_in, part, last,
+    )
 
 
 def solution(mesh):

time: 75.6 us -> 69.8 us (0.923)
  the two profiles are of different devices: /device:TPU:1 before, /device:TPU:5 now
where the time goes in v3:
time: 69.8 us; the launch traced here: 69.4 us
  starting transfers between devices  44 us (63%)
  waiting for transfers between devices  11.6 us (17%)
  Pallas kernels  11.4 us (16%)
  local copies, waits for them, and re-layouts  1.45 us (2%)
  between operations  0.87 us (1%)
    ppermute x8, starting transfers between devices, gather(): lax.ppermute(p, ('seq', 'head'), [(b, a) for a, b in routes(k, n, seq, he...  19.2 us
    ppermute x8, starting transfers between devices, scatter(): lax.ppermute(p, ('seq', 'head'), routes(k, n, seq, head))  17.2 us
    pallas_call x9, Pallas kernels, call(): pl.pallas_call(body, out_shape=outs, in_specs=specs or [VMEM] * len(args)...  11.4 us
    ppermute x8, waiting for transfers between devices, gather(): lax.ppermute(p, ('seq', 'head'), [(b, a) for a, b in routes(k, n, seq, he...  6.04 us
    ppermute x6, starting transfers between devices, swap(): return lax.ppermute(array, axis, [(i, i ^ bit) for i in range(size)])  5.13 us
    ppermute x8, waiting for transfers between devices, scatter(): lax.ppermute(p, ('seq', 'head'), routes(k, n, seq, head))  3.17 us
    ppermute x2, starting transfers between devices, pass_on(): return lax.ppermute(array, 'head', pairs)  2.59 us
    ppermute x6, waiting for transfers between devices, swap(): return lax.ppermute(array, axis, [(i, i ^ bit) for i in range(size)])  2.42 us
  transfers between devices with their start and end apart: 24, of which 7 were waited for; matrix products, arithmetic and copies ran while one was open for 0% of the time, Pallas kernels for 10%

profile of v3, /device:TPU:5, one launch (start us, length us, event | category | flops | bytes accessed | tf_op | source)
XLA Modules:
  0.0 69.4 jit_solution(16837326513230114743)
XLA Ops:
  0.6 2.0 %shard_map.93 = (bf16[3,128,128]{2,1,0:T(8,128)(2,1)}, bf16[3,128,128]{2,1,0:T(8,128)(2,1)}, bf16[3,128,128]{2,1,0:T(8,128)(2,1)}, bf16[3,128,128]{2,1,0:T(8,128...) custom-call(bf16[128,512]{1,0:T(8,128)(2,1)} %q_ref.1, bf16[128,512]{1,0:T(8,128)(2,1)} %k_ref.1, ...), custom_call_target="tpu_custom_call" | custom-call | bytes 1376256 | tf_op jit(solution)/shard_map/pallas_call | solution.py:31
  2.7 1.3 %collective-permute-start.5 = (bf16[128,512]{1,0:T(8,128)(2,1)}, bf16[128,512]{1,0:T(8,128)(2,1)S(1)}, u32[]{:S(2)}, u32[]{:S(2)}) collective-permute-start(bf16[128,512]{1,0:T(8,128)(2,1)} %get-tuple-element.43.refs_0_), channel_id=1, source_target_pairs={{0,2},{1,3},{2,0},{3,1},{4,6},{5,7},{6,4},{7,5},{8,10},{9,11},{10,... | collective-permute-start | bytes 393224 | tf_op jit(solution)/shard_map/ppermute | solution.py:159
  4.0 1.0 %collective-permute-start.6 = (bf16[128,512]{1,0:T(8,128)(2,1)}, bf16[128,512]{1,0:T(8,128)(2,1)S(1)}, u32[]{:S(2)}, u32[]{:S(2)}) collective-permute-start(bf16[128,512]{1,0:T(8,128)(2,1)} %get-tuple-element.43.refs_0_), channel_id=1, source_target_pairs={{0,1},{1,0},{2,3},{3,2},{4,5},{5,4},{6,7},{7,6},{8,9},{9,8},{10,11... | collective-permute-start | bytes 393224 | tf_op jit(solution)/shard_map/ppermute | solution.py:159
  4.9 2.4 %collective-permute-done.5.refs_1_ = bf16[128,512]{1,0:T(8,128)(2,1)S(1)} collective-permute-done((bf16[128,512]{1,0:T(8,128)(2,1)}, bf16[128,512]{1,0:T(8,128)(2,1)S(1)}, u32[]{:S(2)}, u32[]{:S(2)}) %collective-permute-start.5) | collective-permute-done | bytes 131104 | tf_op jit(solution)/shard_map/ppermute | solution.py:159
  7.3 1.5 %collective-permute-start.7 = (bf16[128,512]{1,0:T(8,128)(2,1)S(1)}, bf16[128,512]{1,0:T(8,128)(2,1)S(1)}, u32[]{:S(2)}, u32[]{:S(2)}) collective-permute-start(bf16[128,512]{1,0:T(8,128)(2,1)S(1)} %collective-permute-done.5.refs_1_), channel_id=1, source_target_pairs={{0,1},{1,0},{2,3},{3,2},{4,5},{5,4},{6,7},{7,6},{8,9},{9,8},{10,11... | collective-permute-start | bytes 393224 | tf_op jit(solution)/shard_map/ppermute | solution.py:159
  8.9 4.1 %collective-permute-start = (bf16[3,128,128]{2,1,0:T(8,128)(2,1)}, bf16[3,128,128]{2,1,0:T(8,128)(2,1)S(1)}, u32[]{:S(2)}, u32[]{:S(2)}) collective-permute-start(bf16[3,128,128]{2,1,0:T(8,128)(2,1)} %get-tuple-element.38), channel_id=1, source_target_pairs={{0,0},{1,16},{2,2},{3,18},{4,4},{5,20},{6,6},{7,22},{8,8},{9,24},{... | collective-permute-start | bytes 294920 | tf_op jit(solution)/shard_map/ppermute | solution.py:280
  13.0 1.5 %collective-permute-start.1 = (bf16[3,128,128]{2,1,0:T(8,128)(2,1)}, bf16[3,128,128]{2,1,0:T(8,128)(2,1)S(1)}, u32[]{:S(2)}, u32[]{:S(2)}) collective-permute-start(bf16[3,128,128]{2,1,0:T(8,128)(2,1)} %get-tuple-element.39), channel_id=1, source_target_pairs={{0,4},{1,20},{2,6},{3,22},{4,8},{5,24},{6,10},{7,26},{8,12},{9,28}... | collective-permute-start | bytes 294920 | tf_op jit(solution)/shard_map/ppermute | solution.py:280
  14.4 2.1 %collective-permute-start.2 = (bf16[3,128,128]{2,1,0:T(8,128)(2,1)}, bf16[3,128,128]{2,1,0:T(8,128)(2,1)S(1)}, u32[]{:S(2)}, u32[]{:S(2)}) collective-permute-start(bf16[3,128,128]{2,1,0:T(8,128)(2,1)} %get-tuple-element.40), channel_id=1, source_target_pairs={{0,8},{1,24},{2,10},{3,26},{4,12},{5,28},{6,14},{7,30},{8,0},{9,16... | collective-permute-start | bytes 294920 | tf_op jit(solution)/shard_map/ppermute | solution.py:280
  16.5 0.0 collective-permute-done.6.refs_2_
  16.5 0.6 collective-permute-start.3
  17.2 0.0 collective-permute-done.7.refs_3_
  17.2 0.0 collective-permute-start.4
  17.2 0.0 copy-done.4
  17.2 0.6 copy-done.5
  17.8 3.9 %shard_map.94 = (bf16[128,128]{1,0:T(8,128)(2,1)}, bf16[128,128]{1,0:T(8,128)(2,1)}, bf16[128,128]{1,0:T(8,128)(2,1)}, bf16[128,128]{1,0:T(8,128)(2,1)}) custom-call(bf16[128,512]{1,0:T(8,128)(2,1)} %get-tuple-element.43.refs_0_, bf16[128,512]{1,0:T(8,128)(2,1)} %copy-done.3, bf16[128,512]{1,0:T(8,128)(2,1)} %copy-done.4, bf16[128,512]{1,0:T(8,128)(2,1)} %copy-done.5, ...), custom_call_target="tpu_custom_call" | custom-call | flops 268435456 | bytes 2752512 | tf_op jit(solution)/shard_map/pallas_call | solution.py:31
  21.7 0.0 collective-permute-done.refs_0_
  21.7 0.0 collective-permute-done.1.refs_1_
  21.8 1.8 %collective-permute-done.3.refs_3_ = bf16[3,128,128]{2,1,0:T(8,128)(2,1)S(1)} collective-permute-done((bf16[3,128,128]{2,1,0:T(8,128)(2,1)}, bf16[3,128,128]{2,1,0:T(8,128)(2,1)S(1)}, u32[]{:S(2)}, u32[]{:S(2)}) %collective-permute-start.3) | collective-permute-done | bytes 98336 | tf_op jit(solution)/shard_map/ppermute | solution.py:280
  23.6 0.8 %copy-done.2 = bf16[128,128]{1,0:T(8,128)(2,1)S(1)} copy-done((bf16[128,128]{1,0:T(8,128)(2,1)S(1)}, bf16[128,128]{1,0:T(8,128)(2,1)}, u32[]{:S(2)}) %copy-start.2) | copy-done | bytes 32792
  24.4 0.5 shard_map.95
  24.8 1.3 %collective-permute-start.12 = (bf16[128,256]{1,0:T(8,128)(2,1)S(1)}, bf16[128,256]{1,0:T(8,128)(2,1)S(1)}, u32[]{:S(2)}, u32[]{:S(2)}) collective-permute-start(bf16[128,256]{1,0:T(8,128)(2,1)S(1)} %get-tuple-element.55), channel_id=1, source_target_pairs={{0,1},{2,3},{4,5},{6,7},{8,9},{10,11},{12,13},{14,15},{16,17},{18,... | collective-permute-start | bytes 196616 | tf_op jit(solution)/shard_map/ppermute | solution.py:293
  26.1 3.8 %collective-permute-start.9 = (bf16[128,128]{1,0:T(8,128)(2,1)}, bf16[128,128]{1,0:T(8,128)(2,1)S(1)}, u32[]{:S(2)}, u32[]{:S(2)}) collective-permute-start(bf16[128,128]{1,0:T(8,128)(2,1)} %get-tuple-element.51), channel_id=1, source_target_pairs={{0,4},{1,20},{2,6},{3,22},{4,8},{5,24},{6,10},{7,26},{8,12},{9,28}... | collective-permute-start | bytes 98312 | tf_op jit(solution)/shard_map/ppermute | solution.py:280
  29.9 1.0 %collective-permute-start.10 = (bf16[128,128]{1,0:T(8,128)(2,1)}, bf16[128,128]{1,0:T(8,128)(2,1)S(1)}, u32[]{:S(2)}, u32[]{:S(2)}) collective-permute-start(bf16[128,128]{1,0:T(8,128)(2,1)} %get-tuple-element.52), channel_id=1, source_target_pairs={{0,8},{1,24},{2,10},{3,26},{4,12},{5,28},{6,14},{7,30},{8,0},{9,16... | collective-permute-start | bytes 98312 | tf_op jit(solution)/shard_map/ppermute | solution.py:280
  30.9 0.0 collective-permute-start.11
  30.9 4.1 %collective-permute-start.8 = (bf16[128,128]{1,0:T(8,128)(2,1)S(1)}, bf16[128,128]{1,0:T(8,128)(2,1)S(1)}, u32[]{:S(2)}, u32[]{:S(2)}) collective-permute-start(bf16[128,128]{1,0:T(8,128)(2,1)S(1)} %copy-done.2), channel_id=1, source_target_pairs={{0,0},{1,16},{2,2},{3,18},{4,4},{5,20},{6,6},{7,22},{8,8},{9,24},{... | collective-permute-start | bytes 98312 | tf_op jit(solution)/shard_map/ppermute | solution.py:280
  35.0 0.8 %shard_map.96 = (bf16[512,256]{1,0:T(8,128)(2,1)S(1)}, bf16[4,128,128]{2,1,0:T(8,128)(2,1)S(1)}, f32[512,128]{1,0:T(8,128)S(1)}) custom-call(bf16[3,512,128]{2,1,0:T(8,128)(2,1)S(1)} %get-tuple-element.45.qkv_ref, bf16[128,256]{1,0:T(8,128)(2,1)S(1)} %get-tuple-element.46.om_ref, bf16[512,256]{1,0:T(8,128)(2,1)S(1)} %get-tuple-element.47.kf_ref, ...), custom_call_target="tpu_custom_call" | custom-call | flops 134217728 | bytes 1638400 | tf_op jit(solution)/shard_map/pallas_call | solution.py:31
  35.8 1.3 %collective-permute-done.11.refs_3_ = bf16[128,128]{1,0:T(8,128)(2,1)S(1)} collective-permute-done((bf16[128,128]{1,0:T(8,128)(2,1)}, bf16[128,128]{1,0:T(8,128)(2,1)S(1)}, u32[]{:S(2)}, u32[]{:S(2)}) %collective-permute-start.11) | collective-permute-done | bytes 32800 | tf_op jit(solution)/shard_map/ppermute | solution.py:280
  37.2 0.8 %shard_map.97 = (bf16[512,128]{1,0:T(8,128)(2,1)S(1)}, bf16[4,128,256]{2,1,0:T(8,128)(2,1)S(1)}, bf16[128,256]{1,0:T(8,128)(2,1)S(1)}, bf16[128,128]{1,0:T(8,128...) custom-call(bf16[128,128]{1,0:T(8,128)(2,1)S(1)} %collective-permute-done.8.ref, ...), custom_call_target="tpu_custom_call" | custom-call | flops 67108864 | bytes 1310720 | tf_op jit(solution)/shard_map/pallas_call | solution.py:31
  37.9 1.3 %collective-permute-start.13 = (bf16[128,256]{1,0:T(8,128)(2,1)S(1)}, bf16[128,256]{1,0:T(8,128)(2,1)S(1)}, u32[]{:S(2)}, u32[]{:S(2)}) collective-permute-start(bf16[128,256]{1,0:T(8,128)(2,1)S(1)} %get-tuple-element.61), channel_id=1, source_target_pairs={{1,0},{3,2},{5,4},{7,6},{9,8},{11,10},{13,12},{15,14},{17,16},{19,... | collective-permute-start | bytes 196616 | tf_op jit(solution)/shard_map/ppermute | solution.py:293
  39.2 4.0 %collective-permute-start.18 = (bf16[128,128]{1,0:T(8,128)(2,1)S(1)}, bf16[128,128]{1,0:T(8,128)(2,1)S(1)}, u32[]{:S(2)}, u32[]{:S(2)}) collective-permute-start(bf16[128,128]{1,0:T(8,128)(2,1)S(1)} %get-tuple-element.66), channel_id=1, source_target_pairs={{0,0},{16,1},{2,2},{18,3},{4,4},{20,5},{6,6},{22,7},{8,8},{24,9},{... | collective-permute-start | bytes 98312 | tf_op jit(solution)/shard_map/ppermute | solution.py:286
  43.2 3.9 %collective-permute-start.19 = (bf16[128,128]{1,0:T(8,128)(2,1)S(1)}, bf16[128,128]{1,0:T(8,128)(2,1)S(1)}, u32[]{:S(2)}, u32[]{:S(2)}) collective-permute-start(bf16[128,128]{1,0:T(8,128)(2,1)S(1)} %get-tuple-element.67), channel_id=1, source_target_pairs={{4,0},{20,1},{6,2},{22,3},{8,4},{24,5},{10,6},{26,7},{12,8},{28,9}... | collective-permute-start | bytes 98312 | tf_op jit(solution)/shard_map/ppermute | solution.py:286
  47.2 1.3 %collective-permute-start.20 = (bf16[128,128]{1,0:T(8,128)(2,1)S(1)}, bf16[128,128]{1,0:T(8,128)(2,1)S(1)}, u32[]{:S(2)}, u32[]{:S(2)}) collective-permute-start(bf16[128,128]{1,0:T(8,128)(2,1)S(1)} %get-tuple-element.68), channel_id=1, source_target_pairs={{8,0},{24,1},{10,2},{26,3},{12,4},{28,5},{14,6},{30,7},{0,8},{16,9... | collective-permute-start | bytes 98312 | tf_op jit(solution)/shard_map/ppermute | solution.py:286
  48.4 1.3 %collective-permute-start.21 = (bf16[128,128]{1,0:T(8,128)(2,1)S(1)}, bf16[128,128]{1,0:T(8,128)(2,1)S(1)}, u32[]{:S(2)}, u32[]{:S(2)}) collective-permute-start(bf16[128,128]{1,0:T(8,128)(2,1)S(1)} %get-tuple-element.69), channel_id=1, source_target_pairs={{12,0},{28,1},{14,2},{30,3},{0,4},{16,5},{2,6},{18,7},{4,8},{20,9}... | collective-permute-start | bytes 98312 | tf_op jit(solution)/shard_map/ppermute | solution.py:286
  49.7 1.5 %shard_map.98 = (bf16[512,128]{1,0:T(8,128)(2,1)S(1)}, f32[512,128]{1,0:T(8,128)S(1)}, f32[512,256]{1,0:T(8,128)S(1)}) custom-call(bf16[3,512,128]{2,1,0:T(8,128)(2,1)S(1)} %get-tuple-element.45.qkv_ref, bf16[128,256]{1,0:T(8,128)(2,1)S(1)} %get-tuple-element.46.om_ref, bf16[512,256]{1,0:T(8,128)(2,1)S(1)} %get-tuple-element.47.kf_ref, ...), custom_call_target="tpu_custom_call" | custom-call | flops 268435456 | bytes 2752512 | tf_op jit(solution)/shard_map/pallas_call | solution.py:31
  51.2 0.6 shard_map.99
  51.8 0.5 collective-permute-done.20.refs_2_
  52.3 1.3 %collective-permute-done.21.refs_3_ = bf16[128,128]{1,0:T(8,128)(2,1)S(1)} collective-permute-done((bf16[128,128]{1,0:T(8,128)(2,1)S(1)}, bf16[128,128]{1,0:T(8,128)(2,1)S(1)}, u32[]{:S(2)}, u32[]{:S(2)}) %collective-permute-start.21) | collective-permute-done | bytes 32800 | tf_op jit(solution)/shard_map/ppermute | solution.py:286
  53.6 0.5 shard_map.100
  54.1 0.1 collective-permute-start.22
  54.1 1.9 %collective-permute-start.14 = (bf16[3,128,128]{2,1,0:T(8,128)(2,1)S(1)}, bf16[3,128,128]{2,1,0:T(8,128)(2,1)S(1)}, u32[]{:S(2)}, u32[]{:S(2)}) collective-permute-start(bf16[3,128,128]{2,1,0:T(8,128)(2,1)S(1)} %get-tuple-element.62.refs_5_), channel_id=1, source_target_pairs={{0,0},{16,1},{2,2},{18,3},{4,4},{20,5},{6,6},{22,7},{8,8},{24,9},{... | collective-permute-start | bytes 294920 | tf_op jit(solution)/shard_map/ppermute | solution.py:286
  56.1 2.9 %collective-permute-start.15 = (bf16[3,128,128]{2,1,0:T(8,128)(2,1)S(1)}, bf16[3,128,128]{2,1,0:T(8,128)(2,1)S(1)}, u32[]{:S(2)}, u32[]{:S(2)}) collective-permute-start(bf16[3,128,128]{2,1,0:T(8,128)(2,1)S(1)} %get-tuple-element.63), channel_id=1, source_target_pairs={{4,0},{20,1},{6,2},{22,3},{8,4},{24,5},{10,6},{26,7},{12,8},{28,9}... | collective-permute-start | bytes 294920 | tf_op jit(solution)/shard_map/ppermute | solution.py:286
  59.0 2.0 %collective-permute-start.16 = (bf16[3,128,128]{2,1,0:T(8,128)(2,1)S(1)}, bf16[3,128,128]{2,1,0:T(8,128)(2,1)S(1)}, u32[]{:S(2)}, u32[]{:S(2)}) collective-permute-start(bf16[3,128,128]{2,1,0:T(8,128)(2,1)S(1)} %get-tuple-element.64), channel_id=1, source_target_pairs={{8,0},{24,1},{10,2},{26,3},{12,4},{28,5},{14,6},{30,7},{0,8},{16,9... | collective-permute-start | bytes 294920 | tf_op jit(solution)/shard_map/ppermute | solution.py:286
  60.9 1.9 %collective-permute-start.17 = (bf16[3,128,128]{2,1,0:T(8,128)(2,1)S(1)}, bf16[3,128,128]{2,1,0:T(8,128)(2,1)S(1)}, u32[]{:S(2)}, u32[]{:S(2)}) collective-permute-start(bf16[3,128,128]{2,1,0:T(8,128)(2,1)S(1)} %get-tuple-element.65), channel_id=1, source_target_pairs={{12,0},{28,1},{14,2},{30,3},{0,4},{16,5},{2,6},{18,7},{4,8},{20,9}... | collective-permute-start | bytes 294920 | tf_op jit(solution)/shard_map/ppermute | solution.py:286
  62.8 0.1 add_bitcast_fusion
  62.9 1.3 %collective-permute-start.23 = (bf16[1,128,512]{2,1,0:T(8,128)(2,1)S(1)}, bf16[1,128,512]{2,1,0:T(8,128)(2,1)S(1)}, u32[]{:S(2)}, u32[]{:S(2)}) collective-permute-start(bf16[1,128,512]{2,1,0:T(8,128)(2,1)S(1)} %fusion), channel_id=1, source_target_pairs={{0,2},{1,3},{2,0},{3,1},{4,6},{5,7},{6,4},{7,5},{8,10},{9,11},{10,... | collective-permute-start | bytes 393224 | tf_op jit(solution)/shard_map/ppermute | solution.py:159
  64.3 0.5 collective-permute-done.16.refs_2_
  64.8 3.7 %collective-permute-done.17.refs_3_ = bf16[3,128,128]{2,1,0:T(8,128)(2,1)S(1)} collective-permute-done((bf16[3,128,128]{2,1,0:T(8,128)(2,1)S(1)}, bf16[3,128,128]{2,1,0:T(8,128)(2,1)S(1)}, u32[]{:S(2)}, u32[]{:S(2)}) %collective-permute-start.17) | collective-permute-done | bytes 98336 | tf_op jit(solution)/shard_map/ppermute | solution.py:286
  68.6 0.9 %shard_map.101 = (bf16[128,512]{1,0:T(8,128)(2,1)}, bf16[128,512]{1,0:T(8,128)(2,1)}, bf16[128,512]{1,0:T(8,128)(2,1)}, bf16[128,512]{1,0:T(8,128)(2,1)}) custom-call(bf16[3,128,128]{2,1,0:T(8,128)(2,1)S(1)} %collective-permute-done.14.refs_0_, bf16[3,128,128]{2,1,0:T(8,128)(2,1)S(1)} %collective-permute-done.15.refs_1_, ...), custom_call_target="tpu_custom_call" | custom-call | bytes 1310720 | tf_op jit(solution)/shard_map/pallas_call | solution.py:31
  (24 shorter events, 0.1 us)
Async XLA Ops:
  2.7 20.9 %copy-start.1 = (bf16[128,256]{1,0:T(8,128)(2,1)S(1)}, bf16[128,256]{1,0:T(8,128)(2,1)}, u32[]{:S(2)}) copy-start(bf16[128,256]{1,0:T(8,128)(2,1)} %get-tuple-element.42.refs_4_) | copy-start | bytes 196612
  2.7 4.6 %collective-permute-start.5 = (bf16[128,512]{1,0:T(8,128)(2,1)}, bf16[128,512]{1,0:T(8,128)(2,1)S(1)}, u32[]{:S(2)}, u32[]{:S(2)}) collective-permute-start(bf16[128,512]{1,0:T(8,128)(2,1)} %get-tuple-element.43.refs_0_), channel_id=1, source_target_pairs={{0,2},{1,3},{2,0},{3,1},{4,6},{5,7},{6,4},{7,5},{8,10},{9,11},{10,... | collective-permute-start | bytes 393224 | tf_op jit(solution)/shard_map/ppermute | solution.py:159
  4.0 12.6 %collective-permute-start.6 = (bf16[128,512]{1,0:T(8,128)(2,1)}, bf16[128,512]{1,0:T(8,128)(2,1)S(1)}, u32[]{:S(2)}, u32[]{:S(2)}) collective-permute-start(bf16[128,512]{1,0:T(8,128)(2,1)} %get-tuple-element.43.refs_0_), channel_id=1, source_target_pairs={{0,1},{1,0},{2,3},{3,2},{4,5},{5,4},{6,7},{7,6},{8,9},{9,8},{10,11... | collective-permute-start | bytes 393224 | tf_op jit(solution)/shard_map/ppermute | solution.py:159
  7.3 9.8 %copy-start.3 = (bf16[128,512]{1,0:T(8,128)(2,1)}, bf16[128,512]{1,0:T(8,128)(2,1)S(1)}, u32[]{:S(2)}) copy-start(bf16[128,512]{1,0:T(8,128)(2,1)S(1)} %collective-permute-done.5.refs_1_) | copy-start | bytes 393220
  7.3 9.8 %collective-permute-start.7 = (bf16[128,512]{1,0:T(8,128)(2,1)S(1)}, bf16[128,512]{1,0:T(8,128)(2,1)S(1)}, u32[]{:S(2)}, u32[]{:S(2)}) collective-permute-start(bf16[128,512]{1,0:T(8,128)(2,1)S(1)} %collective-permute-done.5.refs_1_), channel_id=1, source_target_pairs={{0,1},{1,0},{2,3},{3,2},{4,5},{5,4},{6,7},{7,6},{8,9},{9,8},{10,11... | collective-permute-start | bytes 393224 | tf_op jit(solution)/shard_map/ppermute | solution.py:159
  8.9 12.9 %collective-permute-start = (bf16[3,128,128]{2,1,0:T(8,128)(2,1)}, bf16[3,128,128]{2,1,0:T(8,128)(2,1)S(1)}, u32[]{:S(2)}, u32[]{:S(2)}) collective-permute-start(bf16[3,128,128]{2,1,0:T(8,128)(2,1)} %get-tuple-element.38), channel_id=1, source_target_pairs={{0,0},{1,16},{2,2},{3,18},{4,4},{5,20},{6,6},{7,22},{8,8},{9,24},{... | collective-permute-start | bytes 294920 | tf_op jit(solution)/shard_map/ppermute | solution.py:280
  13.0 8.8 %collective-permute-start.1 = (bf16[3,128,128]{2,1,0:T(8,128)(2,1)}, bf16[3,128,128]{2,1,0:T(8,128)(2,1)S(1)}, u32[]{:S(2)}, u32[]{:S(2)}) collective-permute-start(bf16[3,128,128]{2,1,0:T(8,128)(2,1)} %get-tuple-element.39), channel_id=1, source_target_pairs={{0,4},{1,20},{2,6},{3,22},{4,8},{5,24},{6,10},{7,26},{8,12},{9,28}... | collective-permute-start | bytes 294920 | tf_op jit(solution)/shard_map/ppermute | solution.py:280
  14.4 7.3 %collective-permute-start.2 = (bf16[3,128,128]{2,1,0:T(8,128)(2,1)}, bf16[3,128,128]{2,1,0:T(8,128)(2,1)S(1)}, u32[]{:S(2)}, u32[]{:S(2)}) collective-permute-start(bf16[3,128,128]{2,1,0:T(8,128)(2,1)} %get-tuple-element.40), channel_id=1, source_target_pairs={{0,8},{1,24},{2,10},{3,26},{4,12},{5,28},{6,14},{7,30},{8,0},{9,16... | collective-permute-start | bytes 294920 | tf_op jit(solution)/shard_map/ppermute | solution.py:280
  16.5 0.7 copy-start.4
  16.5 7.1 %collective-permute-start.3 = (bf16[3,128,128]{2,1,0:T(8,128)(2,1)}, bf16[3,128,128]{2,1,0:T(8,128)(2,1)S(1)}, u32[]{:S(2)}, u32[]{:S(2)}) collective-permute-start(bf16[3,128,128]{2,1,0:T(8,128)(2,1)} %get-tuple-element.41), channel_id=1, source_target_pairs={{0,12},{1,28},{2,14},{3,30},{4,0},{5,16},{6,2},{7,18},{8,4},{9,20}... | collective-permute-start | bytes 294920 | tf_op jit(solution)/shard_map/ppermute | solution.py:280
  17.2 0.7 copy-start.5
  17.2 4.6 %collective-permute-start.4 = (bf16[128,256]{1,0:T(8,128)(2,1)}, bf16[128,256]{1,0:T(8,128)(2,1)S(1)}, u32[]{:S(2)}, u32[]{:S(2)}) collective-permute-start(bf16[128,256]{1,0:T(8,128)(2,1)} %get-tuple-element.42.refs_4_), channel_id=1, source_target_pairs={{0,1},{1,0},{2,3},{3,2},{4,5},{5,4},{6,7},{7,6},{8,9},{9,8},{10,11... | collective-permute-start | bytes 196616 | tf_op jit(solution)/shard_map/ppermute | solution.py:159
  23.6 0.8 %copy-start.2 = (bf16[128,128]{1,0:T(8,128)(2,1)S(1)}, bf16[128,128]{1,0:T(8,128)(2,1)}, u32[]{:S(2)}) copy-start(bf16[128,128]{1,0:T(8,128)(2,1)} %get-tuple-element.44.refs_6_) | copy-start | bytes 98308
  24.8 12.3 %collective-permute-start.12 = (bf16[128,256]{1,0:T(8,128)(2,1)S(1)}, bf16[128,256]{1,0:T(8,128)(2,1)S(1)}, u32[]{:S(2)}, u32[]{:S(2)}) collective-permute-start(bf16[128,256]{1,0:T(8,128)(2,1)S(1)} %get-tuple-element.55), channel_id=1, source_target_pairs={{0,1},{2,3},{4,5},{6,7},{8,9},{10,11},{12,13},{14,15},{16,17},{18,... | collective-permute-start | bytes 196616 | tf_op jit(solution)/shard_map/ppermute | solution.py:293
  26.1 9.7 %collective-permute-start.9 = (bf16[128,128]{1,0:T(8,128)(2,1)}, bf16[128,128]{1,0:T(8,128)(2,1)S(1)}, u32[]{:S(2)}, u32[]{:S(2)}) collective-permute-start(bf16[128,128]{1,0:T(8,128)(2,1)} %get-tuple-element.51), channel_id=1, source_target_pairs={{0,4},{1,20},{2,6},{3,22},{4,8},{5,24},{6,10},{7,26},{8,12},{9,28}... | collective-permute-start | bytes 98312 | tf_op jit(solution)/shard_map/ppermute | solution.py:280
  29.9 5.9 %collective-permute-start.10 = (bf16[128,128]{1,0:T(8,128)(2,1)}, bf16[128,128]{1,0:T(8,128)(2,1)S(1)}, u32[]{:S(2)}, u32[]{:S(2)}) collective-permute-start(bf16[128,128]{1,0:T(8,128)(2,1)} %get-tuple-element.52), channel_id=1, source_target_pairs={{0,8},{1,24},{2,10},{3,26},{4,12},{5,28},{6,14},{7,30},{8,0},{9,16... | collective-permute-start | bytes 98312 | tf_op jit(solution)/shard_map/ppermute | solution.py:280
  30.9 6.2 %collective-permute-start.11 = (bf16[128,128]{1,0:T(8,128)(2,1)}, bf16[128,128]{1,0:T(8,128)(2,1)S(1)}, u32[]{:S(2)}, u32[]{:S(2)}) collective-permute-start(bf16[128,128]{1,0:T(8,128)(2,1)} %get-tuple-element.53), channel_id=1, source_target_pairs={{0,12},{1,28},{2,14},{3,30},{4,0},{5,16},{6,2},{7,18},{8,4},{9,20}... | collective-permute-start | bytes 98312 | tf_op jit(solution)/shard_map/ppermute | solution.py:280
  30.9 6.2 %collective-permute-start.8 = (bf16[128,128]{1,0:T(8,128)(2,1)S(1)}, bf16[128,128]{1,0:T(8,128)(2,1)S(1)}, u32[]{:S(2)}, u32[]{:S(2)}) collective-permute-start(bf16[128,128]{1,0:T(8,128)(2,1)S(1)} %copy-done.2), channel_id=1, source_target_pairs={{0,0},{1,16},{2,2},{3,18},{4,4},{5,20},{6,6},{7,22},{8,8},{9,24},{... | collective-permute-start | bytes 98312 | tf_op jit(solution)/shard_map/ppermute | solution.py:280
  37.2 16.4 %copy-start = (bf16[512,2048]{1,0:T(8,128)(2,1)S(1)}, bf16[512,2048]{1,0:T(8,128)(2,1)}, u32[]{:S(2)}) copy-start(bf16[512,2048]{1,0:T(8,128)(2,1)} %refs_4_.3) | copy-start | bytes 6291460
  37.9 13.3 %collective-permute-start.13 = (bf16[128,256]{1,0:T(8,128)(2,1)S(1)}, bf16[128,256]{1,0:T(8,128)(2,1)S(1)}, u32[]{:S(2)}, u32[]{:S(2)}) collective-permute-start(bf16[128,256]{1,0:T(8,128)(2,1)S(1)} %get-tuple-element.61), channel_id=1, source_target_pairs={{1,0},{3,2},{5,4},{7,6},{9,8},{11,10},{13,12},{15,14},{17,16},{19,... | collective-permute-start | bytes 196616 | tf_op jit(solution)/shard_map/ppermute | solution.py:293
  39.2 12.6 %collective-permute-start.18 = (bf16[128,128]{1,0:T(8,128)(2,1)S(1)}, bf16[128,128]{1,0:T(8,128)(2,1)S(1)}, u32[]{:S(2)}, u32[]{:S(2)}) collective-permute-start(bf16[128,128]{1,0:T(8,128)(2,1)S(1)} %get-tuple-element.66), channel_id=1, source_target_pairs={{0,0},{16,1},{2,2},{18,3},{4,4},{20,5},{6,6},{22,7},{8,8},{24,9},{... | collective-permute-start | bytes 98312 | tf_op jit(solution)/shard_map/ppermute | solution.py:286
  43.2 8.6 %collective-permute-start.19 = (bf16[128,128]{1,0:T(8,128)(2,1)S(1)}, bf16[128,128]{1,0:T(8,128)(2,1)S(1)}, u32[]{:S(2)}, u32[]{:S(2)}) collective-permute-start(bf16[128,128]{1,0:T(8,128)(2,1)S(1)} %get-tuple-element.67), channel_id=1, source_target_pairs={{4,0},{20,1},{6,2},{22,3},{8,4},{24,5},{10,6},{26,7},{12,8},{28,9}... | collective-permute-start | bytes 98312 | tf_op jit(solution)/shard_map/ppermute | solution.py:286
  47.2 5.1 %collective-permute-start.20 = (bf16[128,128]{1,0:T(8,128)(2,1)S(1)}, bf16[128,128]{1,0:T(8,128)(2,1)S(1)}, u32[]{:S(2)}, u32[]{:S(2)}) collective-permute-start(bf16[128,128]{1,0:T(8,128)(2,1)S(1)} %get-tuple-element.68), channel_id=1, source_target_pairs={{8,0},{24,1},{10,2},{26,3},{12,4},{28,5},{14,6},{30,7},{0,8},{16,9... | collective-permute-start | bytes 98312 | tf_op jit(solution)/shard_map/ppermute | solution.py:286
  48.4 5.1 %collective-permute-start.21 = (bf16[128,128]{1,0:T(8,128)(2,1)S(1)}, bf16[128,128]{1,0:T(8,128)(2,1)S(1)}, u32[]{:S(2)}, u32[]{:S(2)}) collective-permute-start(bf16[128,128]{1,0:T(8,128)(2,1)S(1)} %get-tuple-element.69), channel_id=1, source_target_pairs={{12,0},{28,1},{14,2},{30,3},{0,4},{16,5},{2,6},{18,7},{4,8},{20,9}... | collective-permute-start | bytes 98312 | tf_op jit(solution)/shard_map/ppermute | solution.py:286
  54.1 8.8 %collective-permute-start.22 = (bf16[2,128,512]{2,1,0:T(8,128)(2,1)S(1)}, bf16[2,128,512]{2,1,0:T(8,128)(2,1)S(1)}, u32[]{:S(2)}, u32[]{:S(2)}) collective-permute-start(bf16[2,128,512]{2,1,0:T(8,128)(2,1)S(1)} %get-tuple-element.71), channel_id=1, source_target_pairs={{0,1},{1,0},{2,3},{3,2},{4,5},{5,4},{6,7},{7,6},{8,9},{9,8},{10,11... | collective-permute-start | bytes 786440 | tf_op jit(solution)/shard_map/ppermute | solution.py:159
  54.1 14.4 %collective-permute-start.14 = (bf16[3,128,128]{2,1,0:T(8,128)(2,1)S(1)}, bf16[3,128,128]{2,1,0:T(8,128)(2,1)S(1)}, u32[]{:S(2)}, u32[]{:S(2)}) collective-permute-start(bf16[3,128,128]{2,1,0:T(8,128)(2,1)S(1)} %get-tuple-element.62.refs_5_), channel_id=1, source_target_pairs={{0,0},{16,1},{2,2},{18,3},{4,4},{20,5},{6,6},{22,7},{8,8},{24,9},{... | collective-permute-start | bytes 294920 | tf_op jit(solution)/shard_map/ppermute | solution.py:286
  56.1 8.2 %collective-permute-start.15 = (bf16[3,128,128]{2,1,0:T(8,128)(2,1)S(1)}, bf16[3,128,128]{2,1,0:T(8,128)(2,1)S(1)}, u32[]{:S(2)}, u32[]{:S(2)}) collective-permute-start(bf16[3,128,128]{2,1,0:T(8,128)(2,1)S(1)} %get-tuple-element.63), channel_id=1, source_target_pairs={{4,0},{20,1},{6,2},{22,3},{8,4},{24,5},{10,6},{26,7},{12,8},{28,9}... | collective-permute-start | bytes 294920 | tf_op jit(solution)/shard_map/ppermute | solution.py:286
  59.0 5.8 %collective-permute-start.16 = (bf16[3,128,128]{2,1,0:T(8,128)(2,1)S(1)}, bf16[3,128,128]{2,1,0:T(8,128)(2,1)S(1)}, u32[]{:S(2)}, u32[]{:S(2)}) collective-permute-start(bf16[3,128,128]{2,1,0:T(8,128)(2,1)S(1)} %get-tuple-element.64), channel_id=1, source_target_pairs={{8,0},{24,1},{10,2},{26,3},{12,4},{28,5},{14,6},{30,7},{0,8},{16,9... | collective-permute-start | bytes 294920 | tf_op jit(solution)/shard_map/ppermute | solution.py:286
  60.9 7.6 %collective-permute-start.17 = (bf16[3,128,128]{2,1,0:T(8,128)(2,1)S(1)}, bf16[3,128,128]{2,1,0:T(8,128)(2,1)S(1)}, u32[]{:S(2)}, u32[]{:S(2)}) collective-permute-start(bf16[3,128,128]{2,1,0:T(8,128)(2,1)S(1)} %get-tuple-element.65), channel_id=1, source_target_pairs={{12,0},{28,1},{14,2},{30,3},{0,4},{16,5},{2,6},{18,7},{4,8},{20,9}... | collective-permute-start | bytes 294920 | tf_op jit(solution)/shard_map/ppermute | solution.py:286
  62.9 5.6 %collective-permute-start.23 = (bf16[1,128,512]{2,1,0:T(8,128)(2,1)S(1)}, bf16[1,128,512]{2,1,0:T(8,128)(2,1)S(1)}, u32[]{:S(2)}, u32[]{:S(2)}) collective-permute-start(bf16[1,128,512]{2,1,0:T(8,128)(2,1)S(1)} %fusion), channel_id=1, source_target_pairs={{0,2},{1,3},{2,0},{3,1},{4,6},{5,7},{6,4},{7,5},{8,10},{9,11},{10,... | collective-permute-start | bytes 393224 | tf_op jit(solution)/shard_map/ppermute | solution.py:159

commit v4 on v3

--- a/solution.py
+++ b/solution.py
@@ -11,7 +11,6 @@
 VMEM = pl.BlockSpec(memory_space=pltpu.VMEM)
 SMEM = pl.BlockSpec(memory_space=pltpu.SMEM)
 ANY = pl.BlockSpec(memory_space=pl.ANY)
-HBM = pl.BlockSpec(memory_space=pltpu.HBM)
 NN = (((1,), (0,)), ((), ()))
 NT = (((1,), (1,)), ((), ()))
 TN = (((0,), (0,)), ((), ()))
@@ -25,14 +24,14 @@
     return x.astype(jnp.bfloat16)
 
 
-def call(body, outs, *args, flops=0, specs=None, scratch=(), vmem=32):
+def call(body, outs, *args, flops=0, specs=None, out_specs=None, scratch=(), vmem=32):
     size = sum(a.size * a.dtype.itemsize for a in args)
     size += sum(o.size * o.dtype.itemsize for o in outs)
     return pl.pallas_call(
         body,
         out_shape=outs,
         in_specs=specs or [VMEM] * len(args),
-        out_specs=[VMEM] * len(outs),
+        out_specs=out_specs or [VMEM] * len(outs),
         scratch_shapes=list(scratch),
         cost_estimate=pl.CostEstimate(flops=flops, bytes_accessed=size, transcendentals=0),
         compiler_params=pltpu.CompilerParams(vmem_limit_bytes=vmem * 1024 * 1024),
@@ -314,22 +313,14 @@
         copy.wait()
 
 
-def grad_mixed_kernel(n, offsets, *refs):
-    blocks, w_ref = refs[: len(offsets)], refs[len(offsets)]
-    outs, (scr, w_scr, sems) = refs[len(offsets) + 1 : -3], refs[-3:]
+def grad_mixed_kernel(n, *refs):
+    blocks, w_ref, outs, scr = refs[: -n - 2], refs[-n - 2], refs[-n - 1 : -1], refs[-1]
     s, h = spot()
     width = blocks[0].shape[1]
     dim = outs[0].shape[1]
-    copies = [
-        pltpu.make_async_copy(w_ref.at[:, lane(h ^ offset, width)], w_scr.at[at], sems.at[at])
-        for at, offset in enumerate(offsets)
-    ]
-    for copy in copies:
-        copy.start()
     total = None
-    for at, ref in enumerate(blocks):
-        copies[at].wait()
-        part = mm(ref[...], w_scr[at], NT)
+    for offset, ref in enumerate(blocks):
+        part = mm(ref[...], w_ref[:, lane(h ^ offset, width)], NT)
         total = part if total is None else total + part
     scr[...] = bf(total)
     for k in range(n):
@@ -483,24 +474,17 @@
         functools.partial(pack_kernel, n),
         [struct((3, rows, dim))] * n + [struct((dim, feats)), struct(grad_output.shape)],
         queries, key_vectors, value_vectors, feature_proj, grad_output,
-        specs=[HBM] * 5, scratch=[pltpu.SemaphoreType.DMA((3 * n + 2,))], vmem=60,
-    )
-    offsets, blocks = [0], [go]
-    for bit in reversed(bits):
-        blocks = blocks + [swap(b, "head", bit) for b in blocks]
-        offsets = offsets + [o ^ bit for o in offsets]
+        specs=[ANY] * 5, out_specs=[ANY] * (n + 2),
+        scratch=[pltpu.SemaphoreType.DMA((3 * n + 2,))], vmem=60,
+    )
+    blocks = [go] + [swap(go, "head", offset) for offset in range(1, split)]
     om_in = swap(om_own, "head", 1)
     got = scatter(sends)
     gm_parts = call(
-        functools.partial(grad_mixed_kernel, n, offsets),
+        functools.partial(grad_mixed_kernel, n),
         [struct((rows, dim))] * n,
         *blocks, out_weight, flops=2 * rows * out_weight.size,
-        specs=[VMEM] * split + [HBM], vmem=59,
-        scratch=[
-            pltpu.VMEM((rows, n * dim), jnp.bfloat16),
-            pltpu.VMEM((split, n * dim, width), jnp.bfloat16),
-            pltpu.SemaphoreType.DMA((split,)),
-        ],
+        scratch=[pltpu.VMEM((rows, n * dim), jnp.bfloat16)],
     )
     gm_in = scatter(gm_parts)
     qkv, om, kf, state, total = call(

time: 69.8 us -> 82.4 us (1.18)
  Pallas kernels: 11.4 us -> 25.4 us
  waiting for transfers between devices: 11.6 us -> 9.22 us
  local copies, waits for them, and re-layouts: 1.45 us -> 2.54 us
    pallas_call x9, Pallas kernels: 11.4 us -> 25.4 us  [call(): pl.pallas_call(body, out_shape=outs, in_specs=specs or [VMEM] * len(args)...]
    ppermute x6, waiting for transfers between devices: 2.42 us -> 0.02 us  [swap(): return lax.ppermute(array, axis, [(i, i ^ bit) for i in range(size)])]
    ppermute x6, starting transfers between devices: 5.13 us -> 3.66 us  [swap(): return lax.ppermute(array, axis, [(i, i ^ bit) for i in range(size)])]
    ppermute x8, starting transfers between devices: 17.2 us -> 18.3 us  [scatter(): lax.ppermute(p, ('seq', 'head'), routes(k, n, seq, head))]
    unnamed x12 -> x8, local copies, waits for them, and re-layouts: 1.41 us -> 2.5 us
  transfers between devices with their start and end apart: 24 -> 24, of which waited for: 7 -> 7; matrix products, arithmetic and copies ran while one was open for 0% -> 0% of each run, Pallas kernels for 10% -> 5%
where the time goes in v4:
time: 82.4 us; the launch traced here: 82.1 us
  starting transfers between devices  44.1 us (54%)
  Pallas kernels  25.4 us (31%)
  waiting for transfers between devices  9.22 us (11%)
  local copies, waits for them, and re-layouts  2.54 us (3%)
  between operations  0.85 us (1%)
    pallas_call x9, Pallas kernels, call(): pl.pallas_call(body, out_shape=outs, in_specs=specs or [VMEM] * len(args)...  25.4 us
    ppermute x8, starting transfers between devices, gather(): lax.ppermute(p, ('seq', 'head'), [(b, a) for a, b in routes(k, n, seq, he...  19.5 us
    ppermute x8, starting transfers between devices, scatter(): lax.ppermute(p, ('seq', 'head'), routes(k, n, seq, head))  18.3 us
    ppermute x8, waiting for transfers between devices, gather(): lax.ppermute(p, ('seq', 'head'), [(b, a) for a, b in routes(k, n, seq, he...  5.37 us
    ppermute x8, waiting for transfers between devices, scatter(): lax.ppermute(p, ('seq', 'head'), routes(k, n, seq, head))  3.84 us
    ppermute x6, starting transfers between devices, swap(): return lax.ppermute(array, axis, [(i, i ^ bit) for i in range(size)])  3.66 us
    ppermute x2, starting transfers between devices, pass_on(): return lax.ppermute(array, 'head', pairs)  2.59 us
    unnamed x8, local copies, waits for them, and re-layouts  2.5 us
  transfers between devices with their start and end apart: 24, of which 7 were waited for; matrix products, arithmetic and copies ran while one was open for 0% of the time, Pallas kernels for 5%

profile of v4, /device:TPU:5, one launch (start us, length us, event | category | flops | bytes accessed | tf_op | source)
XLA Modules:
  0.0 82.1 jit_solution(776092227284767543)
XLA Ops:
  0.6 19.1 %shard_map.93 = (bf16[3,128,128]{2,1,0:T(8,128)(2,1)}, bf16[3,128,128]{2,1,0:T(8,128)(2,1)}, bf16[3,128,128]{2,1,0:T(8,128)(2,1)}, bf16[3,128,128]{2,1,0:T(8,128...) custom-call(bf16[128,512]{1,0:T(8,128)(2,1)} %q_ref.1, bf16[128,512]{1,0:T(8,128)(2,1)} %k_ref.1, ...), custom_call_target="tpu_custom_call" | custom-call | bytes 1376256 | tf_op jit(solution)/shard_map/pallas_call | solution.py:30
  19.7 1.8 %collective-permute-start.7 = (bf16[128,512]{1,0:T(8,128)(2,1)}, bf16[128,512]{1,0:T(8,128)(2,1)S(1)}, u32[]{:S(2)}, u32[]{:S(2)}) collective-permute-start(bf16[128,512]{1,0:T(8,128)(2,1)} %get-tuple-element.43.refs_0_), channel_id=1, source_target_pairs={{0,3},{1,2},{2,1},{3,0},{4,7},{5,6},{6,5},{7,4},{8,11},{9,10},{10,... | collective-permute-start | bytes 393224 | tf_op jit(solution)/shard_map/ppermute | solution.py:158
  21.6 0.3 collective-permute-start.6
  21.8 0.2 collective-permute-start.5
  22.0 4.4 %collective-permute-start = (bf16[3,128,128]{2,1,0:T(8,128)(2,1)}, bf16[3,128,128]{2,1,0:T(8,128)(2,1)S(1)}, u32[]{:S(2)}, u32[]{:S(2)}) collective-permute-start(bf16[3,128,128]{2,1,0:T(8,128)(2,1)} %get-tuple-element.38), channel_id=1, source_target_pairs={{0,0},{1,16},{2,2},{3,18},{4,4},{5,20},{6,6},{7,22},{8,8},{9,24},{... | collective-permute-start | bytes 294920 | tf_op jit(solution)/shard_map/ppermute | solution.py:279
  26.4 1.2 %collective-permute-start.1 = (bf16[3,128,128]{2,1,0:T(8,128)(2,1)}, bf16[3,128,128]{2,1,0:T(8,128)(2,1)S(1)}, u32[]{:S(2)}, u32[]{:S(2)}) collective-permute-start(bf16[3,128,128]{2,1,0:T(8,128)(2,1)} %get-tuple-element.39), channel_id=1, source_target_pairs={{0,4},{1,20},{2,6},{3,22},{4,8},{5,24},{6,10},{7,26},{8,12},{9,28}... | collective-permute-start | bytes 294920 | tf_op jit(solution)/shard_map/ppermute | solution.py:279
  27.6 0.0 collective-permute-done.7.refs_3_
  27.6 2.4 %collective-permute-start.2 = (bf16[3,128,128]{2,1,0:T(8,128)(2,1)}, bf16[3,128,128]{2,1,0:T(8,128)(2,1)S(1)}, u32[]{:S(2)}, u32[]{:S(2)}) collective-permute-start(bf16[3,128,128]{2,1,0:T(8,128)(2,1)} %get-tuple-element.40), channel_id=1, source_target_pairs={{0,8},{1,24},{2,10},{3,26},{4,12},{5,28},{6,14},{7,30},{8,0},{9,16... | collective-permute-start | bytes 294920 | tf_op jit(solution)/shard_map/ppermute | solution.py:279
  30.0 1.4 %collective-permute-start.3 = (bf16[3,128,128]{2,1,0:T(8,128)(2,1)}, bf16[3,128,128]{2,1,0:T(8,128)(2,1)S(1)}, u32[]{:S(2)}, u32[]{:S(2)}) collective-permute-start(bf16[3,128,128]{2,1,0:T(8,128)(2,1)} %get-tuple-element.41), channel_id=1, source_target_pairs={{0,12},{1,28},{2,14},{3,30},{4,0},{5,16},{6,2},{7,18},{8,4},{9,20}... | collective-permute-start | bytes 294920 | tf_op jit(solution)/shard_map/ppermute | solution.py:279
  31.4 0.0 collective-permute-done.5.refs_1_
  31.4 0.0 collective-permute-start.4
  31.4 1.6 %copy-done = bf16[512,2048]{1,0:T(8,128)(2,1)S(1)} copy-done((bf16[512,2048]{1,0:T(8,128)(2,1)S(1)}, bf16[512,2048]{1,0:T(8,128)(2,1)}, u32[]{:S(2)}) %copy-start) | copy-done | bytes 2097176
  33.0 0.9 %copy-done.2 = bf16[128,512]{1,0:T(8,128)(2,1)S(1)} copy-done((bf16[128,512]{1,0:T(8,128)(2,1)S(1)}, bf16[128,512]{1,0:T(8,128)(2,1)}, u32[]{:S(2)}) %copy-start.2) | copy-done | bytes 131096
  33.9 0.9 %shard_map.94 = (bf16[128,128]{1,0:T(8,128)(2,1)S(1)}, bf16[128,128]{1,0:T(8,128)(2,1)S(1)}, bf16[128,128]{1,0:T(8,128)(2,1)S(1)}, bf16[128,128]{1,0:T(8,128)(2,1)S(1)}) custom-call(bf16[128,512]{1,0:T(8,128)(2,1)S(1)} %copy-done.2, bf16[128,512]{1,0:T(8,128)(2,1)S(1)} %collective-permute-done.5.refs_1_, ...), custom_call_target="tpu_custom_call" | custom-call | flops 268435456 | bytes 2752512 | tf_op jit(solution)/shard_map/pallas_call | solution.py:30
  34.8 0.0 collective-permute-done.refs_0_
  34.8 0.0 collective-permute-done.1.refs_1_
  34.8 2.2 %collective-permute-done.3.refs_3_ = bf16[3,128,128]{2,1,0:T(8,128)(2,1)S(1)} collective-permute-done((bf16[3,128,128]{2,1,0:T(8,128)(2,1)}, bf16[3,128,128]{2,1,0:T(8,128)(2,1)S(1)}, u32[]{:S(2)}, u32[]{:S(2)}) %collective-permute-start.3) | collective-permute-done | bytes 98336 | tf_op jit(solution)/shard_map/ppermute | solution.py:279
  37.0 0.5 shard_map.95
  37.5 1.3 %collective-permute-start.12 = (bf16[128,256]{1,0:T(8,128)(2,1)S(1)}, bf16[128,256]{1,0:T(8,128)(2,1)S(1)}, u32[]{:S(2)}, u32[]{:S(2)}) collective-permute-start(bf16[128,256]{1,0:T(8,128)(2,1)S(1)} %get-tuple-element.55), channel_id=1, source_target_pairs={{0,1},{2,3},{4,5},{6,7},{8,9},{10,11},{12,13},{14,15},{16,17},{18,... | collective-permute-start | bytes 196616 | tf_op jit(solution)/shard_map/ppermute | solution.py:292
  38.8 3.8 %collective-permute-start.9 = (bf16[128,128]{1,0:T(8,128)(2,1)S(1)}, bf16[128,128]{1,0:T(8,128)(2,1)S(1)}, u32[]{:S(2)}, u32[]{:S(2)}) collective-permute-start(bf16[128,128]{1,0:T(8,128)(2,1)S(1)} %get-tuple-element.51), channel_id=1, source_target_pairs={{0,4},{1,20},{2,6},{3,22},{4,8},{5,24},{6,10},{7,26},{8,12},{9,28}... | collective-permute-start | bytes 98312 | tf_op jit(solution)/shard_map/ppermute | solution.py:279
  42.7 0.6 collective-permute-start.10
  43.2 0.8 collective-permute-start.11
  44.0 3.7 %collective-permute-start.8 = (bf16[128,128]{1,0:T(8,128)(2,1)S(1)}, bf16[128,128]{1,0:T(8,128)(2,1)S(1)}, u32[]{:S(2)}, u32[]{:S(2)}) collective-permute-start(bf16[128,128]{1,0:T(8,128)(2,1)S(1)} %get-tuple-element.44.refs_6_), channel_id=1, source_target_pairs={{0,0},{1,16},{2,2},{3,18},{4,4},{5,20},{6,6},{7,22},{8,8},{9,24},{... | collective-permute-start | bytes 98312 | tf_op jit(solution)/shard_map/ppermute | solution.py:279
  47.7 0.8 shard_map.96
  48.5 0.0 collective-permute-done.9.refs_1_
  48.5 0.8 collective-permute-done.11.refs_3_
  49.3 0.9 %collective-permute-done.8.refs_0_ = bf16[128,128]{1,0:T(8,128)(2,1)S(1)} collective-permute-done((bf16[128,128]{1,0:T(8,128)(2,1)S(1)}, bf16[128,128]{1,0:T(8,128)(2,1)S(1)}, u32[]{:S(2)}, u32[]{:S(2)}) %collective-permute-start.8) | collective-permute-done | bytes 32800 | tf_op jit(solution)/shard_map/ppermute | solution.py:279
  50.2 0.8 shard_map.97
  50.9 1.3 %collective-permute-start.13 = (bf16[128,256]{1,0:T(8,128)(2,1)S(1)}, bf16[128,256]{1,0:T(8,128)(2,1)S(1)}, u32[]{:S(2)}, u32[]{:S(2)}) collective-permute-start(bf16[128,256]{1,0:T(8,128)(2,1)S(1)} %get-tuple-element.61), channel_id=1, source_target_pairs={{1,0},{3,2},{5,4},{7,6},{9,8},{11,10},{13,12},{15,14},{17,16},{19,... | collective-permute-start | bytes 196616 | tf_op jit(solution)/shard_map/ppermute | solution.py:292
  52.2 3.7 %collective-permute-start.18 = (bf16[128,128]{1,0:T(8,128)(2,1)S(1)}, bf16[128,128]{1,0:T(8,128)(2,1)S(1)}, u32[]{:S(2)}, u32[]{:S(2)}) collective-permute-start(bf16[128,128]{1,0:T(8,128)(2,1)S(1)} %get-tuple-element.66), channel_id=1, source_target_pairs={{0,0},{16,1},{2,2},{18,3},{4,4},{20,5},{6,6},{22,7},{8,8},{24,9},{... | collective-permute-start | bytes 98312 | tf_op jit(solution)/shard_map/ppermute | solution.py:285
  55.9 4.0 %collective-permute-start.19 = (bf16[128,128]{1,0:T(8,128)(2,1)S(1)}, bf16[128,128]{1,0:T(8,128)(2,1)S(1)}, u32[]{:S(2)}, u32[]{:S(2)}) collective-permute-start(bf16[128,128]{1,0:T(8,128)(2,1)S(1)} %get-tuple-element.67), channel_id=1, source_target_pairs={{4,0},{20,1},{6,2},{22,3},{8,4},{24,5},{10,6},{26,7},{12,8},{28,9}... | collective-permute-start | bytes 98312 | tf_op jit(solution)/shard_map/ppermute | solution.py:285
  59.9 0.6 collective-permute-start.20
  60.5 1.9 %collective-permute-start.21 = (bf16[128,128]{1,0:T(8,128)(2,1)S(1)}, bf16[128,128]{1,0:T(8,128)(2,1)S(1)}, u32[]{:S(2)}, u32[]{:S(2)}) collective-permute-start(bf16[128,128]{1,0:T(8,128)(2,1)S(1)} %get-tuple-element.69), channel_id=1, source_target_pairs={{12,0},{28,1},{14,2},{30,3},{0,4},{16,5},{2,6},{18,7},{4,8},{20,9}... | collective-permute-start | bytes 98312 | tf_op jit(solution)/shard_map/ppermute | solution.py:285
  62.4 1.5 %shard_map.98 = (bf16[512,128]{1,0:T(8,128)(2,1)S(1)}, f32[512,128]{1,0:T(8,128)S(1)}, f32[512,256]{1,0:T(8,128)S(1)}) custom-call(bf16[3,512,128]{2,1,0:T(8,128)(2,1)S(1)} %get-tuple-element.45.qkv_ref, bf16[128,256]{1,0:T(8,128)(2,1)S(1)} %get-tuple-element.46.om_ref, bf16[512,256]{1,0:T(8,128)(2,1)S(1)} %get-tuple-element.47.kf_ref, ...), custom_call_target="tpu_custom_call" | custom-call | flops 268435456 | bytes 2752512 | tf_op jit(solution)/shard_map/pallas_call | solution.py:30
  63.9 0.6 shard_map.99
  64.5 0.5 collective-permute-done.20.refs_2_
  65.0 0.6 collective-permute-done.21.refs_3_
  65.6 0.5 shard_map.100
  66.1 0.1 collective-permute-start.22
  66.2 1.9 %collective-permute-start.14 = (bf16[3,128,128]{2,1,0:T(8,128)(2,1)S(1)}, bf16[3,128,128]{2,1,0:T(8,128)(2,1)S(1)}, u32[]{:S(2)}, u32[]{:S(2)}) collective-permute-start(bf16[3,128,128]{2,1,0:T(8,128)(2,1)S(1)} %get-tuple-element.62.refs_5_), channel_id=1, source_target_pairs={{0,0},{16,1},{2,2},{18,3},{4,4},{20,5},{6,6},{22,7},{8,8},{24,9},{... | collective-permute-start | bytes 294920 | tf_op jit(solution)/shard_map/ppermute | solution.py:285
  68.1 3.5 %collective-permute-start.15 = (bf16[3,128,128]{2,1,0:T(8,128)(2,1)S(1)}, bf16[3,128,128]{2,1,0:T(8,128)(2,1)S(1)}, u32[]{:S(2)}, u32[]{:S(2)}) collective-permute-start(bf16[3,128,128]{2,1,0:T(8,128)(2,1)S(1)} %get-tuple-element.63), channel_id=1, source_target_pairs={{4,0},{20,1},{6,2},{22,3},{8,4},{24,5},{10,6},{26,7},{12,8},{28,9}... | collective-permute-start | bytes 294920 | tf_op jit(solution)/shard_map/ppermute | solution.py:285
  71.6 2.0 %collective-permute-start.16 = (bf16[3,128,128]{2,1,0:T(8,128)(2,1)S(1)}, bf16[3,128,128]{2,1,0:T(8,128)(2,1)S(1)}, u32[]{:S(2)}, u32[]{:S(2)}) collective-permute-start(bf16[3,128,128]{2,1,0:T(8,128)(2,1)S(1)} %get-tuple-element.64), channel_id=1, source_target_pairs={{8,0},{24,1},{10,2},{26,3},{12,4},{28,5},{14,6},{30,7},{0,8},{16,9... | collective-permute-start | bytes 294920 | tf_op jit(solution)/shard_map/ppermute | solution.py:285
  73.6 2.0 %collective-permute-start.17 = (bf16[3,128,128]{2,1,0:T(8,128)(2,1)S(1)}, bf16[3,128,128]{2,1,0:T(8,128)(2,1)S(1)}, u32[]{:S(2)}, u32[]{:S(2)}) collective-permute-start(bf16[3,128,128]{2,1,0:T(8,128)(2,1)S(1)} %get-tuple-element.65), channel_id=1, source_target_pairs={{12,0},{28,1},{14,2},{30,3},{0,4},{16,5},{2,6},{18,7},{4,8},{20,9}... | collective-permute-start | bytes 294920 | tf_op jit(solution)/shard_map/ppermute | solution.py:285
  75.6 0.1 add_bitcast_fusion
  75.7 1.3 %collective-permute-start.23 = (bf16[1,128,512]{2,1,0:T(8,128)(2,1)S(1)}, bf16[1,128,512]{2,1,0:T(8,128)(2,1)S(1)}, u32[]{:S(2)}, u32[]{:S(2)}) collective-permute-start(bf16[1,128,512]{2,1,0:T(8,128)(2,1)S(1)} %fusion), channel_id=1, source_target_pairs={{0,2},{1,3},{2,0},{3,1},{4,6},{5,7},{6,4},{7,5},{8,10},{9,11},{10,... | collective-permute-start | bytes 393224 | tf_op jit(solution)/shard_map/ppermute | solution.py:158
  77.0 0.5 collective-permute-done.16.refs_2_
  77.5 3.7 %collective-permute-done.17.refs_3_ = bf16[3,128,128]{2,1,0:T(8,128)(2,1)S(1)} collective-permute-done((bf16[3,128,128]{2,1,0:T(8,128)(2,1)S(1)}, bf16[3,128,128]{2,1,0:T(8,128)(2,1)S(1)}, u32[]{:S(2)}, u32[]{:S(2)}) %collective-permute-start.17) | collective-permute-done | bytes 98336 | tf_op jit(solution)/shard_map/ppermute | solution.py:285
  81.2 0.9 %shard_map.101 = (bf16[128,512]{1,0:T(8,128)(2,1)}, bf16[128,512]{1,0:T(8,128)(2,1)}, bf16[128,512]{1,0:T(8,128)(2,1)}, bf16[128,512]{1,0:T(8,128)(2,1)}) custom-call(bf16[3,128,128]{2,1,0:T(8,128)(2,1)S(1)} %collective-permute-done.14.refs_0_, bf16[3,128,128]{2,1,0:T(8,128)(2,1)S(1)} %collective-permute-done.15.refs_1_, ...), custom_call_target="tpu_custom_call" | custom-call | bytes 1310720 | tf_op jit(solution)/shard_map/pallas_call | solution.py:30
  (20 shorter events, 0.1 us)
Async XLA Ops:
  19.7 7.9 %collective-permute-start.7 = (bf16[128,512]{1,0:T(8,128)(2,1)}, bf16[128,512]{1,0:T(8,128)(2,1)S(1)}, u32[]{:S(2)}, u32[]{:S(2)}) collective-permute-start(bf16[128,512]{1,0:T(8,128)(2,1)} %get-tuple-element.43.refs_0_), channel_id=1, source_target_pairs={{0,3},{1,2},{2,1},{3,0},{4,7},{5,6},{6,5},{7,4},{8,11},{9,10},{10,... | collective-permute-start | bytes 393224 | tf_op jit(solution)/shard_map/ppermute | solution.py:158
  21.6 8.4 %collective-permute-start.6 = (bf16[128,512]{1,0:T(8,128)(2,1)}, bf16[128,512]{1,0:T(8,128)(2,1)S(1)}, u32[]{:S(2)}, u32[]{:S(2)}) collective-permute-start(bf16[128,512]{1,0:T(8,128)(2,1)} %get-tuple-element.43.refs_0_), channel_id=1, source_target_pairs={{0,2},{1,3},{2,0},{3,1},{4,6},{5,7},{6,4},{7,5},{8,10},{9,11},{10,... | collective-permute-start | bytes 393224 | tf_op jit(solution)/shard_map/ppermute | solution.py:158
  21.8 9.6 %collective-permute-start.5 = (bf16[128,512]{1,0:T(8,128)(2,1)}, bf16[128,512]{1,0:T(8,128)(2,1)S(1)}, u32[]{:S(2)}, u32[]{:S(2)}) collective-permute-start(bf16[128,512]{1,0:T(8,128)(2,1)} %get-tuple-element.43.refs_0_), channel_id=1, source_target_pairs={{0,1},{1,0},{2,3},{3,2},{4,5},{5,4},{6,7},{7,6},{8,9},{9,8},{10,11... | collective-permute-start | bytes 393224 | tf_op jit(solution)/shard_map/ppermute | solution.py:158
  22.0 12.8 %collective-permute-start = (bf16[3,128,128]{2,1,0:T(8,128)(2,1)}, bf16[3,128,128]{2,1,0:T(8,128)(2,1)S(1)}, u32[]{:S(2)}, u32[]{:S(2)}) collective-permute-start(bf16[3,128,128]{2,1,0:T(8,128)(2,1)} %get-tuple-element.38), channel_id=1, source_target_pairs={{0,0},{1,16},{2,2},{3,18},{4,4},{5,20},{6,6},{7,22},{8,8},{9,24},{... | collective-permute-start | bytes 294920 | tf_op jit(solution)/shard_map/ppermute | solution.py:279
  26.4 8.4 %collective-permute-start.1 = (bf16[3,128,128]{2,1,0:T(8,128)(2,1)}, bf16[3,128,128]{2,1,0:T(8,128)(2,1)S(1)}, u32[]{:S(2)}, u32[]{:S(2)}) collective-permute-start(bf16[3,128,128]{2,1,0:T(8,128)(2,1)} %get-tuple-element.39), channel_id=1, source_target_pairs={{0,4},{1,20},{2,6},{3,22},{4,8},{5,24},{6,10},{7,26},{8,12},{9,28}... | collective-permute-start | bytes 294920 | tf_op jit(solution)/shard_map/ppermute | solution.py:279
  27.6 7.2 %collective-permute-start.2 = (bf16[3,128,128]{2,1,0:T(8,128)(2,1)}, bf16[3,128,128]{2,1,0:T(8,128)(2,1)S(1)}, u32[]{:S(2)}, u32[]{:S(2)}) collective-permute-start(bf16[3,128,128]{2,1,0:T(8,128)(2,1)} %get-tuple-element.40), channel_id=1, source_target_pairs={{0,8},{1,24},{2,10},{3,26},{4,12},{5,28},{6,14},{7,30},{8,0},{9,16... | collective-permute-start | bytes 294920 | tf_op jit(solution)/shard_map/ppermute | solution.py:279
  30.0 7.0 %collective-permute-start.3 = (bf16[3,128,128]{2,1,0:T(8,128)(2,1)}, bf16[3,128,128]{2,1,0:T(8,128)(2,1)S(1)}, u32[]{:S(2)}, u32[]{:S(2)}) collective-permute-start(bf16[3,128,128]{2,1,0:T(8,128)(2,1)} %get-tuple-element.41), channel_id=1, source_target_pairs={{0,12},{1,28},{2,14},{3,30},{4,0},{5,16},{6,2},{7,18},{8,4},{9,20}... | collective-permute-start | bytes 294920 | tf_op jit(solution)/shard_map/ppermute | solution.py:279
  31.4 3.4 %collective-permute-start.4 = (bf16[128,256]{1,0:T(8,128)(2,1)}, bf16[128,256]{1,0:T(8,128)(2,1)S(1)}, u32[]{:S(2)}, u32[]{:S(2)}) collective-permute-start(bf16[128,256]{1,0:T(8,128)(2,1)} %get-tuple-element.42.refs_4_), channel_id=1, source_target_pairs={{0,1},{1,0},{2,3},{3,2},{4,5},{5,4},{6,7},{7,6},{8,9},{9,8},{10,11... | collective-permute-start | bytes 196616 | tf_op jit(solution)/shard_map/ppermute | solution.py:158
  31.4 1.6 %copy-start = (bf16[512,2048]{1,0:T(8,128)(2,1)S(1)}, bf16[512,2048]{1,0:T(8,128)(2,1)}, u32[]{:S(2)}) copy-start(bf16[512,2048]{1,0:T(8,128)(2,1)} %refs_4_.3) | copy-start | bytes 6291460
  33.0 0.9 %copy-start.2 = (bf16[128,512]{1,0:T(8,128)(2,1)S(1)}, bf16[128,512]{1,0:T(8,128)(2,1)}, u32[]{:S(2)}) copy-start(bf16[128,512]{1,0:T(8,128)(2,1)} %get-tuple-element.43.refs_0_) | copy-start | bytes 393220
  33.9 3.1 %copy-start.3 = (bf16[128,256]{1,0:T(8,128)(2,1)S(1)}, bf16[128,256]{1,0:T(8,128)(2,1)}, u32[]{:S(2)}) copy-start(bf16[128,256]{1,0:T(8,128)(2,1)} %get-tuple-element.42.refs_4_) | copy-start | bytes 196612
  37.5 12.6 %collective-permute-start.12 = (bf16[128,256]{1,0:T(8,128)(2,1)S(1)}, bf16[128,256]{1,0:T(8,128)(2,1)S(1)}, u32[]{:S(2)}, u32[]{:S(2)}) collective-permute-start(bf16[128,256]{1,0:T(8,128)(2,1)S(1)} %get-tuple-element.55), channel_id=1, source_target_pairs={{0,1},{2,3},{4,5},{6,7},{8,9},{10,11},{12,13},{14,15},{16,17},{18,... | collective-permute-start | bytes 196616 | tf_op jit(solution)/shard_map/ppermute | solution.py:292
  38.8 9.7 %collective-permute-start.9 = (bf16[128,128]{1,0:T(8,128)(2,1)S(1)}, bf16[128,128]{1,0:T(8,128)(2,1)S(1)}, u32[]{:S(2)}, u32[]{:S(2)}) collective-permute-start(bf16[128,128]{1,0:T(8,128)(2,1)S(1)} %get-tuple-element.51), channel_id=1, source_target_pairs={{0,4},{1,20},{2,6},{3,22},{4,8},{5,24},{6,10},{7,26},{8,12},{9,28}... | collective-permute-start | bytes 98312 | tf_op jit(solution)/shard_map/ppermute | solution.py:279
  42.7 5.8 %collective-permute-start.10 = (bf16[128,128]{1,0:T(8,128)(2,1)S(1)}, bf16[128,128]{1,0:T(8,128)(2,1)S(1)}, u32[]{:S(2)}, u32[]{:S(2)}) collective-permute-start(bf16[128,128]{1,0:T(8,128)(2,1)S(1)} %get-tuple-element.52), channel_id=1, source_target_pairs={{0,8},{1,24},{2,10},{3,26},{4,12},{5,28},{6,14},{7,30},{8,0},{9,16... | collective-permute-start | bytes 98312 | tf_op jit(solution)/shard_map/ppermute | solution.py:279
  43.2 6.0 %collective-permute-start.11 = (bf16[128,128]{1,0:T(8,128)(2,1)S(1)}, bf16[128,128]{1,0:T(8,128)(2,1)S(1)}, u32[]{:S(2)}, u32[]{:S(2)}) collective-permute-start(bf16[128,128]{1,0:T(8,128)(2,1)S(1)} %get-tuple-element.53), channel_id=1, source_target_pairs={{0,12},{1,28},{2,14},{3,30},{4,0},{5,16},{6,2},{7,18},{8,4},{9,20}... | collective-permute-start | bytes 98312 | tf_op jit(solution)/shard_map/ppermute | solution.py:279
  44.0 6.1 %collective-permute-start.8 = (bf16[128,128]{1,0:T(8,128)(2,1)S(1)}, bf16[128,128]{1,0:T(8,128)(2,1)S(1)}, u32[]{:S(2)}, u32[]{:S(2)}) collective-permute-start(bf16[128,128]{1,0:T(8,128)(2,1)S(1)} %get-tuple-element.44.refs_6_), channel_id=1, source_target_pairs={{0,0},{1,16},{2,2},{3,18},{4,4},{5,20},{6,6},{7,22},{8,8},{9,24},{... | collective-permute-start | bytes 98312 | tf_op jit(solution)/shard_map/ppermute | solution.py:279
  50.1 15.5 %copy-start.1 = (bf16[512,2048]{1,0:T(8,128)(2,1)S(1)}, bf16[512,2048]{1,0:T(8,128)(2,1)}, u32[]{:S(2)}) copy-start(bf16[512,2048]{1,0:T(8,128)(2,1)} %refs_4_.3) | copy-start | bytes 6291460
  50.9 13.0 %collective-permute-start.13 = (bf16[128,256]{1,0:T(8,128)(2,1)S(1)}, bf16[128,256]{1,0:T(8,128)(2,1)S(1)}, u32[]{:S(2)}, u32[]{:S(2)}) collective-permute-start(bf16[128,256]{1,0:T(8,128)(2,1)S(1)} %get-tuple-element.61), channel_id=1, source_target_pairs={{1,0},{3,2},{5,4},{7,6},{9,8},{11,10},{13,12},{15,14},{17,16},{19,... | collective-permute-start | bytes 196616 | tf_op jit(solution)/shard_map/ppermute | solution.py:292
  52.2 12.3 %collective-permute-start.18 = (bf16[128,128]{1,0:T(8,128)(2,1)S(1)}, bf16[128,128]{1,0:T(8,128)(2,1)S(1)}, u32[]{:S(2)}, u32[]{:S(2)}) collective-permute-start(bf16[128,128]{1,0:T(8,128)(2,1)S(1)} %get-tuple-element.66), channel_id=1, source_target_pairs={{0,0},{16,1},{2,2},{18,3},{4,4},{20,5},{6,6},{22,7},{8,8},{24,9},{... | collective-permute-start | bytes 98312 | tf_op jit(solution)/shard_map/ppermute | solution.py:285
  55.9 8.6 %collective-permute-start.19 = (bf16[128,128]{1,0:T(8,128)(2,1)S(1)}, bf16[128,128]{1,0:T(8,128)(2,1)S(1)}, u32[]{:S(2)}, u32[]{:S(2)}) collective-permute-start(bf16[128,128]{1,0:T(8,128)(2,1)S(1)} %get-tuple-element.67), channel_id=1, source_target_pairs={{4,0},{20,1},{6,2},{22,3},{8,4},{24,5},{10,6},{26,7},{12,8},{28,9}... | collective-permute-start | bytes 98312 | tf_op jit(solution)/shard_map/ppermute | solution.py:285
  59.9 5.1 %collective-permute-start.20 = (bf16[128,128]{1,0:T(8,128)(2,1)S(1)}, bf16[128,128]{1,0:T(8,128)(2,1)S(1)}, u32[]{:S(2)}, u32[]{:S(2)}) collective-permute-start(bf16[128,128]{1,0:T(8,128)(2,1)S(1)} %get-tuple-element.68), channel_id=1, source_target_pairs={{8,0},{24,1},{10,2},{26,3},{12,4},{28,5},{14,6},{30,7},{0,8},{16,9... | collective-permute-start | bytes 98312 | tf_op jit(solution)/shard_map/ppermute | solution.py:285
  60.5 5.1 %collective-permute-start.21 = (bf16[128,128]{1,0:T(8,128)(2,1)S(1)}, bf16[128,128]{1,0:T(8,128)(2,1)S(1)}, u32[]{:S(2)}, u32[]{:S(2)}) collective-permute-start(bf16[128,128]{1,0:T(8,128)(2,1)S(1)} %get-tuple-element.69), channel_id=1, source_target_pairs={{12,0},{28,1},{14,2},{30,3},{0,4},{16,5},{2,6},{18,7},{4,8},{20,9}... | collective-permute-start | bytes 98312 | tf_op jit(solution)/shard_map/ppermute | solution.py:285
  66.1 9.5 %collective-permute-start.22 = (bf16[2,128,512]{2,1,0:T(8,128)(2,1)S(1)}, bf16[2,128,512]{2,1,0:T(8,128)(2,1)S(1)}, u32[]{:S(2)}, u32[]{:S(2)}) collective-permute-start(bf16[2,128,512]{2,1,0:T(8,128)(2,1)S(1)} %get-tuple-element.71), channel_id=1, source_target_pairs={{0,1},{1,0},{2,3},{3,2},{4,5},{5,4},{6,7},{7,6},{8,9},{9,8},{10,11... | collective-permute-start | bytes 786440 | tf_op jit(solution)/shard_map/ppermute | solution.py:158
  66.2 15.0 %collective-permute-start.14 = (bf16[3,128,128]{2,1,0:T(8,128)(2,1)S(1)}, bf16[3,128,128]{2,1,0:T(8,128)(2,1)S(1)}, u32[]{:S(2)}, u32[]{:S(2)}) collective-permute-start(bf16[3,128,128]{2,1,0:T(8,128)(2,1)S(1)} %get-tuple-element.62.refs_5_), channel_id=1, source_target_pairs={{0,0},{16,1},{2,2},{18,3},{4,4},{20,5},{6,6},{22,7},{8,8},{24,9},{... | collective-permute-start | bytes 294920 | tf_op jit(solution)/shard_map/ppermute | solution.py:285
  68.1 8.9 %collective-permute-start.15 = (bf16[3,128,128]{2,1,0:T(8,128)(2,1)S(1)}, bf16[3,128,128]{2,1,0:T(8,128)(2,1)S(1)}, u32[]{:S(2)}, u32[]{:S(2)}) collective-permute-start(bf16[3,128,128]{2,1,0:T(8,128)(2,1)S(1)} %get-tuple-element.63), channel_id=1, source_target_pairs={{4,0},{20,1},{6,2},{22,3},{8,4},{24,5},{10,6},{26,7},{12,8},{28,9}... | collective-permute-start | bytes 294920 | tf_op jit(solution)/shard_map/ppermute | solution.py:285
  71.6 5.9 %collective-permute-start.16 = (bf16[3,128,128]{2,1,0:T(8,128)(2,1)S(1)}, bf16[3,128,128]{2,1,0:T(8,128)(2,1)S(1)}, u32[]{:S(2)}, u32[]{:S(2)}) collective-permute-start(bf16[3,128,128]{2,1,0:T(8,128)(2,1)S(1)} %get-tuple-element.64), channel_id=1, source_target_pairs={{8,0},{24,1},{10,2},{26,3},{12,4},{28,5},{14,6},{30,7},{0,8},{16,9... | collective-permute-start | bytes 294920 | tf_op jit(solution)/shard_map/ppermute | solution.py:285
  73.6 7.6 %collective-permute-start.17 = (bf16[3,128,128]{2,1,0:T(8,128)(2,1)S(1)}, bf16[3,128,128]{2,1,0:T(8,128)(2,1)S(1)}, u32[]{:S(2)}, u32[]{:S(2)}) collective-permute-start(bf16[3,128,128]{2,1,0:T(8,128)(2,1)S(1)} %get-tuple-element.65), channel_id=1, source_target_pairs={{12,0},{28,1},{14,2},{30,3},{0,4},{16,5},{2,6},{18,7},{4,8},{20,9}... | collective-permute-start | bytes 294920 | tf_op jit(solution)/shard_map/ppermute | solution.py:285
  75.7 5.6 %collective-permute-start.23 = (bf16[1,128,512]{2,1,0:T(8,128)(2,1)S(1)}, bf16[1,128,512]{2,1,0:T(8,128)(2,1)S(1)}, u32[]{:S(2)}, u32[]{:S(2)}) collective-permute-start(bf16[1,128,512]{2,1,0:T(8,128)(2,1)S(1)} %fusion), channel_id=1, source_target_pairs={{0,2},{1,3},{2,0},{3,1},{4,6},{5,7},{6,4},{7,5},{8,10},{9,11},{10,... | collective-permute-start | bytes 393224 | tf_op jit(solution)/shard_map/ppermute | solution.py:158

commit v5 on v4

v5 whole, which is shorter than its diff:
```python
import functools

import jax
import jax.numpy as jnp
from jax import lax
from jax.experimental import pallas as pl
from jax.experimental.pallas import tpu as pltpu
from jax.sharding import PartitionSpec as P

EPSILON = 1e-05
VMEM = pl.BlockSpec(memory_space=pltpu.VMEM)
ANY = pl.BlockSpec(memory_space=pl.ANY)
NN = (((1,), (0,)), ((), ()))
NT = (((1,), (1,)), ((), ()))
TN = (((0,), (0,)), ((), ()))


def mm(a, b, dims=NN):
    return lax.dot_general(a, b, dims, preferred_element_type=jnp.float32)


def bf(x):
    return x.astype(jnp.bfloat16)


def call(body, outs, *args, flops=0, specs=None, scratch=(), vmem=32):
    size = sum(a.size * a.dtype.itemsize for a in args)
    size += sum(o.size * o.dtype.itemsize for o in outs)
    return pl.pallas_call(
        body,
        out_shape=outs,
        in_specs=specs or [VMEM] * len(args),
        out_specs=[VMEM] * len(outs),
        scratch_shapes=list(scratch),
        cost_estimate=pl.CostEstimate(flops=flops, bytes_accessed=size, transcendentals=0),
        compiler_params=pltpu.CompilerParams(vmem_limit_bytes=vmem * 1024 * 1024),
    )(*args)


def struct(shape, dtype=jnp.bfloat16):
    return jax.ShapeDtypeStruct(shape, dtype)


def causal_mask(rows):
    row = lax.broadcasted_iota(jnp.int32, (rows, rows), 0)
    col = lax.broadcasted_iota(jnp.int32, (rows, rows), 1)
    return col <= row


def swap(array, axis, bit):
    size = lax.axis_size(axis)
    return lax.ppermute(array, axis, [(i, i ^ bit) for i in range(size)])


def bits_of(size):
    return [1 << b for b in range(size.bit_length() - 1)]


def reduce_blocks(own, sent, bits):
    got = swap(sent, "head", 1)
    for bit in bits[1:]:
        total = own.astype(jnp.float32) + got.astype(jnp.float32)
        pairs = total.reshape((total.shape[0] // 2, 2) + total.shape[1:])
        own, got = pairs[:, 0], swap(bf(pairs[:, 1]), "head", bit)
    return own[0].astype(jnp.float32), got[0]


def member(n):
    return lax.rem(lax.axis_index("seq"), n)


def exchange(parts):
    n, size = len(parts), lax.axis_size("seq")
    return [parts[0]] + [
        lax.ppermute(parts[k], "seq", [(i, i ^ k) for i in range(size)]) for k in range(1, n)
    ]


def from_groups(total, n, forward):
    size, step, exclusive = lax.axis_size("seq"), n, None
    inclusive = total.astype(jnp.float32)
    while step < size:
        pairs = [(i, i + step) for i in range(size - step)]
        if not forward:
            pairs = [(b, a) for a, b in pairs]
        got = lax.ppermute(bf(inclusive), "seq", pairs).astype(jnp.float32)
        exclusive = got if exclusive is None else exclusive + got
        inclusive = inclusive + got
        step *= 2
    return jnp.zeros_like(total) if exclusive is None else bf(exclusive)


def lane(index, width):
    return pl.ds(pl.multiple_of(index * width, 128), width)


def pack_kernel(n, q_ref, k_ref, v_ref, om_ref, go_ref, *rest):
    outs, om_out, go_out, sems = rest[:n], rest[n], rest[n + 1], rest[n + 2]
    r = member(n)
    dim = om_ref.shape[1]
    copies = [(go_ref, go_out)]
    for k in range(n):
        cols = lane(r ^ k, dim)
        for at, ref in enumerate((q_ref, k_ref, v_ref)):
            copies.append((ref.at[:, cols], outs[k].at[at]))
    copies.append((om_ref.at[r], om_out))
    started = [pltpu.make_async_copy(a, b, sems.at[i]) for i, (a, b) in enumerate(copies)]
    for copy in started:
        copy.start()
    for copy in started:
        copy.wait()


def grad_mixed_kernel(n, *refs):
    blocks, w_ref, outs, scr = refs[: -n - 2], refs[-n - 2], refs[-n - 1 : -1], refs[-1]
    r, h = member(n), lax.axis_index("head")
    width = blocks[0].shape[1]
    dim = outs[0].shape[1]
    total = None
    for offset, ref in enumerate(blocks):
        part = mm(ref[...], w_ref[:, lane(h ^ offset, width)], NT)
        total = part if total is None else total + part
    scr[...] = bf(total)
    for k in range(n):
        outs[k][...] = scr[:, lane(r ^ k, dim)]


def first_kernel(n, *refs):
    got, om_ref, (qkv_ref, kf_ref, state_ref, total_ref) = refs[:n], refs[n], refs[n + 2 :]
    r = member(n)
    rows, dim = got[0].shape[1:]
    scale = dim ** (-0.25)
    for k in range(n):
        at = pl.ds(pl.multiple_of((r ^ k) * rows, 128), rows)
        qkv_ref[:, at, :] = got[k][...]
    k_all = qkv_ref[1]
    wide = k_all.astype(jnp.float32)
    half_sq = jnp.sum(wide * wide, axis=1, keepdims=True) * (scale * scale * 0.5)
    kf = bf(jnp.exp(mm(k_all, om_ref[...]) * scale - half_sq))
    kf_ref[...] = kf
    total = jnp.zeros(total_ref.shape, jnp.float32)
    for t in range(n):
        at = pl.ds(t * rows, rows)
        state_ref[t] = bf(total)
        total = total + mm(qkv_ref[2, at, :], kf[t * rows : (t + 1) * rows], TN)
    total_ref[...] = bf(total)


def inner_kernel(n, qkv_ref, om_ref, kf_ref, state_ref, qf_ref, scores_ref, num_ref):
    dim = om_ref.shape[0]
    rows = scores_ref.shape[1]
    scale = dim ** (-0.25)
    causal = causal_mask(rows)
    qf_ref[...] = bf(jnp.exp(mm(qkv_ref[0], om_ref[...]) * scale))
    for t in range(n):
        at = pl.ds(t * rows, rows)
        qf = qf_ref[at, :]
        scores = bf(jnp.where(causal, mm(qf, kf_ref[at, :], NT), 0.0))
        scores_ref[t] = scores
        num_ref[at, :] = mm(scores, qkv_ref[2, at, :]) + mm(qf, state_ref[t], NT)


def turn_kernel(n, *refs):
    gm_in, (qf_ref, num_ref, carried_ref) = refs[:n], refs[n : n + 3]
    gn_ref, state_ref, total_ref = refs[n + 3 : n + 6]
    outs, scr = refs[n + 6 : -1], refs[-1]
    r = member(n)
    rows = gm_in[0].shape[0]
    places = [
        pl.ds(pl.multiple_of((r ^ k) * rows, 128), rows) for k in range(n)
    ]
    for k in range(n):
        scr[places[k], :] = gm_in[k][...]
    num = num_ref[...] + mm(qf_ref[...], carried_ref[...], NT)
    inv = lax.rsqrt(jnp.mean(num * num, axis=1, keepdims=True) + EPSILON)
    normed = num * inv
    gm = scr[...].astype(jnp.float32)
    gn = bf((gm - normed * jnp.mean(gm * normed, axis=1, keepdims=True)) * inv)
    gn_ref[...] = gn
    scr[...] = bf(normed)
    for k in range(n):
        outs[k][...] = scr[places[k], :]
    total = jnp.zeros(total_ref.shape, jnp.float32)
    for t in reversed(range(n)):
        state_ref[t] = bf(total)
        at = pl.ds(t * rows, rows)
        total = total + mm(gn[t * rows : (t + 1) * rows], qf_ref[at, :], TN)
    total_ref[...] = bf(total)


def back_kernel(n, qkv_ref, om_ref, kf_ref, qf_ref, scores_ref, gn_ref, state_ref, carried_ref,
                later_ref, gq_ref, gv_ref, gkf_ref, gqf_scr):
    dim = om_ref.shape[0]
    rows = scores_ref.shape[1]
    scale = dim ** (-0.25)
    causal = causal_mask(rows)
    gqf_scr[...] = mm(gn_ref[...], carried_ref[...])
    for t in range(n):
        at = pl.ds(t * rows, rows)
        qf, kf, gn, v = qf_ref[at, :], kf_ref[at, :], gn_ref[at, :], qkv_ref[2, at, :]
        gs = bf(jnp.where(causal, mm(gn, v, NT), 0.0))
        gqf = gqf_scr[at, :] + mm(gs, kf) + mm(gn, state_ref[t])
        terms = bf(gqf * qf.astype(jnp.float32))
        gq_ref[at, :] = bf(mm(terms, om_ref[...], NT) * scale)
        later = later_ref[t]
        gv_ref[at, :] = mm(scores_ref[t], gn, TN) + mm(kf, later, NT)
        gkf_ref[at, :] = mm(gs, qf, TN) + mm(v, later)


def end_kernel(n, qkv_ref, om_ref, kf_ref, gq_ref, gv_ref, gkf_ref, after_ref, *rest):
    outs, gk_scr, gv_scr = rest[:n], rest[n], rest[n + 1]
    r = member(n)
    dim = om_ref.shape[0]
    rows = outs[0].shape[1]
    scale = dim ** (-0.25)
    kf, after = kf_ref[...], after_ref[...]
    gv_scr[...] = bf(gv_ref[...] + mm(kf, after, NT))
    gkf = gkf_ref[...] + mm(qkv_ref[2], after)
    terms = bf(gkf * kf.astype(jnp.float32))
    total = jnp.sum(terms.astype(jnp.float32), axis=1, keepdims=True)
    wide = qkv_ref[1].astype(jnp.float32)
    gk_scr[...] = bf(mm(terms, om_ref[...], NT) * scale - total * wide * (scale * scale))
    for k in range(n):
        at = pl.ds(pl.multiple_of((r ^ k) * rows, 128), rows)
        outs[k][0] = gq_ref[at, :]
        outs[k][1] = gk_scr[at, :]
        outs[k][2] = gv_scr[at, :]


def mixed_project_kernel(n, offsets, *refs):
    mixed_in, (w_ref, _, own_ref, sent_ref, scr) = refs[:n], refs[n:]
    r, h = member(n), lax.axis_index("head")
    width = own_ref.shape[2]
    dim = mixed_in[0].shape[1]
    half = len(offsets) // 2
    for k in range(n):
        scr[:, lane(r ^ k, dim)] = mixed_in[k][...]
    mixed = scr[...]
    for at, offset in enumerate(offsets):
        part = bf(mm(mixed, w_ref[:, lane(h ^ offset, width)]))
        if at < half:
            own_ref[at] = part
        else:
            sent_ref[at - half] = part


def unpack_kernel(n, *refs):
    got, (part_ref, last_ref), (out_ref, *outs) = refs[:n], refs[n : n + 2], refs[n + 2 :]
    r = member(n)
    dim = got[0].shape[2]
    out_ref[...] = bf(part_ref[...] + last_ref[...].astype(jnp.float32))
    for k in range(n):
        cols = lane(r ^ k, dim)
        for at, out in enumerate(outs):
            out[:, cols] = got[k][at]


def local(queries, key_vectors, value_vectors, feature_proj, out_weight, grad_output):
    n, dim, feats = feature_proj.shape
    rows, width = grad_output.shape
    split = lax.axis_size("head")
    bits = bits_of(split)
    long = n * rows
    macs = long * dim * feats * 2
    f32 = jnp.float32

    *sends, om, go = call(
        functools.partial(pack_kernel, n),
        [struct((3, rows, dim))] * n + [struct((dim, feats)), struct(grad_output.shape)],
        queries, key_vectors, value_vectors, feature_proj, grad_output,
        specs=[ANY] * 5, scratch=[pltpu.SemaphoreType.DMA((3 * n + 2,))], vmem=60,
    )
    blocks = [go] + [swap(go, "head", offset) for offset in range(1, split)]
    got = exchange(sends)
    gm_parts = call(
        functools.partial(grad_mixed_kernel, n),
        [struct((rows, dim))] * n,
        *blocks, out_weight, flops=2 * rows * out_weight.size,
        scratch=[pltpu.VMEM((rows, n * dim), jnp.bfloat16)],
    )
    gm_in = exchange(gm_parts)
    qkv, kf, state, total = call(
        functools.partial(first_kernel, n),
        [
            struct((3, long, dim)),
            struct((long, feats)),
            struct((n, dim, feats)),
            struct((dim, feats)),
        ],
        *got, om, gm_parts[0], flops=2 * macs, specs=[VMEM] * (n + 1) + [ANY],
    )
    carried = from_groups(total, n, True)
    qf, scores, num = call(
        functools.partial(inner_kernel, n),
        [struct((long, feats)), struct((n, rows, rows)), struct((long, dim), f32)],
        qkv, om, kf, state, flops=4 * macs,
    )
    gn, later, later_total, *mixed_parts = call(
        functools.partial(turn_kernel, n),
        [struct((long, dim)), struct((n, dim, feats)), struct((dim, feats))]
        + [struct((rows, dim))] * n,
        *gm_in, qf, num, carried, flops=2 * macs,
        scratch=[pltpu.VMEM((long, dim), jnp.bfloat16)],
    )
    after_b = from_groups(later_total, n, False)
    mixed_in = exchange(mixed_parts)
    gq, gv_part, gkf_part = call(
        functools.partial(back_kernel, n),
        [struct((long, dim)), struct((long, dim), f32), struct((long, feats), f32)],
        qkv, om, kf, qf, scores, gn, state, carried, later, flops=8 * macs,
        scratch=[pltpu.VMEM((long, feats), f32)],
    )
    grads = call(
        functools.partial(end_kernel, n),
        [struct((3, rows, dim))] * n,
        qkv, om, kf, gq, gv_part, gkf_part, after_b, flops=3 * macs,
        scratch=[pltpu.VMEM((long, dim), jnp.bfloat16)] * 2,
    )
    grads_in = exchange(grads)

    order = [o for o in range(split) if not o & 1] + [o for o in range(split) if o & 1]
    own, sent = call(
        functools.partial(mixed_project_kernel, n, order),
        [struct((split // 2, rows, width))] * 2,
        *mixed_in, out_weight, grads[0], flops=2 * rows * out_weight.size,
        specs=[VMEM] * (n + 1) + [ANY],
        scratch=[pltpu.VMEM((rows, n * dim), jnp.bfloat16)],
    )
    part, last = reduce_blocks(own, sent, bits)
    return call(
        functools.partial(unpack_kernel, n),
        [struct((rows, width))] + [struct((rows, n * dim))] * 3,
        *grads_in, part, last,
    )


def solution(mesh):
    placed = (
        P("seq", "head"),
        P("seq", "head"),
        P("seq", "head"),
        P("head", None, None),
        P("head", None),
        P("seq", "head"),
    )
    return jax.shard_map(
        local,
        mesh=mesh,
        in_specs=placed,
        out_specs=(P("seq", "head"),) * 4,
        check_vma=False,
    )
```

time: 82.4 us -> 48.9 us (0.59)
  the two profiles are of different devices: /device:TPU:5 before, /device:TPU:0 now
where the time goes in v5:
time: 48.9 us; the launch traced here: 48.6 us
  starting transfers between devices  28.2 us (58%)
  waiting for transfers between devices  8.68 us (18%)
  Pallas kernels  8.25 us (17%)
  local copies, waits for them, and re-layouts  2.56 us (5%)
  between operations  0.82 us (2%)
    ppermute x12, starting transfers between devices, exchange(): lax.ppermute(parts[k], 'seq', [(i, i ^ k) for i in range(size)])  17.4 us
    pallas_call x9, Pallas kernels, call(): pl.pallas_call(body, out_shape=outs, in_specs=specs or [VMEM] * len(args)...  8.25 us
    ppermute x12, waiting for transfers between devices, exchange(): lax.ppermute(parts[k], 'seq', [(i, i ^ k) for i in range(size)])  6.92 us
    ppermute x2, starting transfers between devices, from_groups(): got = lax.ppermute(bf(inclusive), 'seq', pairs).astype(jnp.float32)  6.11 us
    ppermute x5, starting transfers between devices, swap(): return lax.ppermute(array, axis, [(i, i ^ bit) for i in range(size)])  4.75 us
    unnamed x10, local copies, waits for them, and re-layouts  2.52 us
    ppermute x2, waiting for transfers between devices, from_groups(): got = lax.ppermute(bf(inclusive), 'seq', pairs).astype(jnp.float32)  1.34 us
  transfers between devices with their start and end apart: 19, of which 7 were waited for; matrix products, arithmetic and copies ran while one was open for 0% of the time, Pallas kernels for 8%

profile of v5, /device:TPU:0, one launch (start us, length us, event | category | flops | bytes accessed | tf_op | source)
XLA Modules:
  0.0 48.6 jit_solution(5385701806905437482)
XLA Ops:
  0.6 2.0 %shard_map.93 = (bf16[3,128,128]{2,1,0:T(8,128)(2,1)}, bf16[3,128,128]{2,1,0:T(8,128)(2,1)}, bf16[3,128,128]{2,1,0:T(8,128)(2,1)}, bf16[3,128,128]{2,1,0:T(8,128...) custom-call(bf16[128,512]{1,0:T(8,128)(2,1)} %q_ref.1, bf16[128,512]{1,0:T(8,128)(2,1)} %k_ref.1, ...), custom_call_target="tpu_custom_call" | custom-call | bytes 1376256 | tf_op jit(solution)/shard_map/pallas_call | solution.py:29
  2.7 2.4 %collective-permute-start.5 = (bf16[128,512]{1,0:T(8,128)(2,1)}, bf16[128,512]{1,0:T(8,128)(2,1)S(1)}, u32[]{:S(2)}, u32[]{:S(2)}) collective-permute-start(bf16[128,512]{1,0:T(8,128)(2,1)} %get-tuple-element.42.refs_0_), channel_id=1, source_target_pairs={{0,3},{1,2},{2,1},{3,0},{4,7},{5,6},{6,5},{7,4},{8,11},{9,10},{10,... | collective-permute-start | bytes 393224 | tf_op jit(solution)/shard_map/ppermute | solution.py:52
  5.1 0.6 %collective-permute-start.4 = (bf16[128,512]{1,0:T(8,128)(2,1)}, bf16[128,512]{1,0:T(8,128)(2,1)S(1)}, u32[]{:S(2)}, u32[]{:S(2)}) collective-permute-start(bf16[128,512]{1,0:T(8,128)(2,1)} %get-tuple-element.42.refs_0_), channel_id=1, source_target_pairs={{0,2},{1,3},{2,0},{3,1},{4,6},{5,7},{6,4},{7,5},{8,10},{9,11},{10,... | collective-permute-start | bytes 393224 | tf_op jit(solution)/shard_map/ppermute | solution.py:52
  5.8 0.0 collective-permute-start.3
  5.8 1.8 %collective-permute-start = (bf16[3,128,128]{2,1,0:T(8,128)(2,1)}, bf16[3,128,128]{2,1,0:T(8,128)(2,1)S(1)}, u32[]{:S(2)}, u32[]{:S(2)}) collective-permute-start(bf16[3,128,128]{2,1,0:T(8,128)(2,1)} %get-tuple-element.38), channel_id=1, source_target_pairs={{0,4},{4,0},{8,12},{12,8},{16,20},{20,16},{24,28},{28,24},{1,5},{5... | collective-permute-start | bytes 294920 | tf_op jit(solution)/shard_map/ppermute | solution.py:75
  7.6 1.6 %collective-permute-start.1 = (bf16[3,128,128]{2,1,0:T(8,128)(2,1)}, bf16[3,128,128]{2,1,0:T(8,128)(2,1)S(1)}, u32[]{:S(2)}, u32[]{:S(2)}) collective-permute-start(bf16[3,128,128]{2,1,0:T(8,128)(2,1)} %get-tuple-element.39), channel_id=1, source_target_pairs={{0,8},{4,12},{8,0},{12,4},{16,24},{20,28},{24,16},{28,20},{1,9},{5... | collective-permute-start | bytes 294920 | tf_op jit(solution)/shard_map/ppermute | solution.py:75
  9.2 0.2 collective-permute-done.5.refs_3_
  9.3 3.4 %collective-permute-start.2 = (bf16[3,128,128]{2,1,0:T(8,128)(2,1)}, bf16[3,128,128]{2,1,0:T(8,128)(2,1)S(1)}, u32[]{:S(2)}, u32[]{:S(2)}) collective-permute-start(bf16[3,128,128]{2,1,0:T(8,128)(2,1)} %get-tuple-element.40), channel_id=1, source_target_pairs={{0,12},{4,8},{8,4},{12,0},{16,28},{20,24},{24,20},{28,16},{1,13},{... | collective-permute-start | bytes 294920 | tf_op jit(solution)/shard_map/ppermute | solution.py:75
  12.7 0.0 collective-permute-done.4.refs_2_
  12.7 0.0 collective-permute-done.3.refs_1_
  12.7 1.6 %copy-done = bf16[512,2048]{1,0:T(8,128)(2,1)S(1)} copy-done((bf16[512,2048]{1,0:T(8,128)(2,1)S(1)}, bf16[512,2048]{1,0:T(8,128)(2,1)}, u32[]{:S(2)}) %copy-start) | copy-done | bytes 2097176
  14.3 0.9 %copy-done.3 = bf16[128,512]{1,0:T(8,128)(2,1)S(1)} copy-done((bf16[128,512]{1,0:T(8,128)(2,1)S(1)}, bf16[128,512]{1,0:T(8,128)(2,1)}, u32[]{:S(2)}) %copy-start.3) | copy-done | bytes 131096
  15.2 0.9 %shard_map.94 = (bf16[128,128]{1,0:T(8,128)(2,1)S(1)}, bf16[128,128]{1,0:T(8,128)(2,1)S(1)}, bf16[128,128]{1,0:T(8,128)(2,1)S(1)}, bf16[128,128]{1,0:T(8,128)(2,1)S(1)}) custom-call(bf16[128,512]{1,0:T(8,128)(2,1)S(1)} %copy-done.3, bf16[128,512]{1,0:T(8,128)(2,1)S(1)} %collective-permute-done.3.refs_1_, ...), custom_call_target="tpu_custom_call" | custom-call | flops 268435456 | bytes 2752512 | tf_op jit(solution)/shard_map/pallas_call | solution.py:29
  16.1 0.0 collective-permute-done.refs_1_
  16.1 0.0 collective-permute-done.1.refs_2_
  16.1 0.0 collective-permute-done.2.refs_3_
  16.1 0.0 copy-done.4
  16.1 0.4 shard_map.95
  16.6 4.8 %collective-permute-start.9 = (bf16[128,256]{1,0:T(8,128)(2,1)S(1)}, bf16[128,256]{1,0:T(8,128)(2,1)S(1)}, u32[]{:S(2)}, u32[]{:S(2)}) collective-permute-start(bf16[128,256]{1,0:T(8,128)(2,1)S(1)} %get-tuple-element.53), channel_id=1, source_target_pairs={{0,16},{4,20},{8,24},{12,28},{1,17},{5,21},{9,25},{13,29},{2,18},{... | collective-permute-start | bytes 196616 | tf_op jit(solution)/shard_map/ppermute | solution.py:86
  21.4 1.6 %collective-permute-start.6 = (bf16[128,128]{1,0:T(8,128)(2,1)S(1)}, bf16[128,128]{1,0:T(8,128)(2,1)S(1)}, u32[]{:S(2)}, u32[]{:S(2)}) collective-permute-start(bf16[128,128]{1,0:T(8,128)(2,1)S(1)} %get-tuple-element.49), channel_id=1, source_target_pairs={{0,4},{4,0},{8,12},{12,8},{16,20},{20,16},{24,28},{28,24},{1,5},{5... | collective-permute-start | bytes 98312 | tf_op jit(solution)/shard_map/ppermute | solution.py:75
  23.0 1.6 %collective-permute-start.7 = (bf16[128,128]{1,0:T(8,128)(2,1)S(1)}, bf16[128,128]{1,0:T(8,128)(2,1)S(1)}, u32[]{:S(2)}, u32[]{:S(2)}) collective-permute-start(bf16[128,128]{1,0:T(8,128)(2,1)S(1)} %get-tuple-element.50), channel_id=1, source_target_pairs={{0,8},{4,12},{8,0},{12,4},{16,24},{20,28},{24,16},{28,20},{1,9},{5... | collective-permute-start | bytes 98312 | tf_op jit(solution)/shard_map/ppermute | solution.py:75
  24.6 0.4 collective-permute-start.8
  25.0 0.8 %shard_map.96 = (bf16[512,256]{1,0:T(8,128)(2,1)S(1)}, bf16[4,128,128]{2,1,0:T(8,128)(2,1)S(1)}, f32[512,128]{1,0:T(8,128)S(1)}) custom-call(bf16[3,512,128]{2,1,0:T(8,128)(2,1)S(1)} %get-tuple-element.44.qkv_ref, bf16[128,256]{1,0:T(8,128)(2,1)S(1)} %copy-done.2, bf16[512,256]{1,0:T(8,128)(2,1)S(1)} %get-tuple-element.45.kf_ref, ...), custom_call_target="tpu_custom_call" | custom-call | flops 134217728 | bytes 1638400 | tf_op jit(solution)/shard_map/pallas_call | solution.py:29
  25.7 0.0 collective-permute-done.6.refs_1_
  25.7 1.3 %collective-permute-done.7.refs_2_ = bf16[128,128]{1,0:T(8,128)(2,1)S(1)} collective-permute-done((bf16[128,128]{1,0:T(8,128)(2,1)S(1)}, bf16[128,128]{1,0:T(8,128)(2,1)S(1)}, u32[]{:S(2)}, u32[]{:S(2)}) %collective-permute-start.7) | collective-permute-done | bytes 32800 | tf_op jit(solution)/shard_map/ppermute | solution.py:75
  27.0 2.4 %collective-permute-done.8.refs_3_ = bf16[128,128]{1,0:T(8,128)(2,1)S(1)} collective-permute-done((bf16[128,128]{1,0:T(8,128)(2,1)S(1)}, bf16[128,128]{1,0:T(8,128)(2,1)S(1)}, u32[]{:S(2)}, u32[]{:S(2)}) %collective-permute-start.8) | collective-permute-done | bytes 32800 | tf_op jit(solution)/shard_map/ppermute | solution.py:75
  29.4 0.0 collective-permute-done.9.refs_6_.carried_ref
  29.4 0.8 %shard_map.97 = (bf16[512,128]{1,0:T(8,128)(2,1)S(1)}, bf16[4,128,256]{2,1,0:T(8,128)(2,1)S(1)}, bf16[128,256]{1,0:T(8,128)(2,1)S(1)}, bf16[128,128]{1,0:T(8,128...) custom-call(bf16[128,128]{1,0:T(8,128)(2,1)S(1)} %get-tuple-element.43.refs_5_., ...), custom_call_target="tpu_custom_call" | custom-call | flops 67108864 | bytes 1310720 | tf_op jit(solution)/shard_map/pallas_call | solution.py:29
  30.1 1.3 %collective-permute-start.10 = (bf16[128,256]{1,0:T(8,128)(2,1)S(1)}, bf16[128,256]{1,0:T(8,128)(2,1)S(1)}, u32[]{:S(2)}, u32[]{:S(2)}) collective-permute-start(bf16[128,256]{1,0:T(8,128)(2,1)S(1)} %get-tuple-element.59), channel_id=1, source_target_pairs={{16,0},{20,4},{24,8},{28,12},{17,1},{21,5},{25,9},{29,13},{18,2},{... | collective-permute-start | bytes 196616 | tf_op jit(solution)/shard_map/ppermute | solution.py:86
  31.4 0.6 %collective-permute-start.14 = (bf16[128,128]{1,0:T(8,128)(2,1)S(1)}, bf16[128,128]{1,0:T(8,128)(2,1)S(1)}, u32[]{:S(2)}, u32[]{:S(2)}) collective-permute-start(bf16[128,128]{1,0:T(8,128)(2,1)S(1)} %get-tuple-element.65), channel_id=1, source_target_pairs={{0,4},{4,0},{8,12},{12,8},{16,20},{20,16},{24,28},{28,24},{1,5},{5... | collective-permute-start | bytes 98312 | tf_op jit(solution)/shard_map/ppermute | solution.py:75
  32.0 0.4 collective-permute-start.15
  32.5 2.5 %collective-permute-start.16 = (bf16[128,128]{1,0:T(8,128)(2,1)S(1)}, bf16[128,128]{1,0:T(8,128)(2,1)S(1)}, u32[]{:S(2)}, u32[]{:S(2)}) collective-permute-start(bf16[128,128]{1,0:T(8,128)(2,1)S(1)} %get-tuple-element.67), channel_id=1, source_target_pairs={{0,12},{4,8},{8,4},{12,0},{16,28},{20,24},{24,20},{28,16},{1,13},{... | collective-permute-start | bytes 98312 | tf_op jit(solution)/shard_map/ppermute | solution.py:75
  35.0 1.5 %shard_map.98 = (bf16[512,128]{1,0:T(8,128)(2,1)S(1)}, f32[512,128]{1,0:T(8,128)S(1)}, f32[512,256]{1,0:T(8,128)S(1)}) custom-call(bf16[3,512,128]{2,1,0:T(8,128)(2,1)S(1)} %get-tuple-element.44.qkv_ref, bf16[128,256]{1,0:T(8,128)(2,1)S(1)} %copy-done.2, bf16[512,256]{1,0:T(8,128)(2,1)S(1)} %get-tuple-element.45.kf_ref, ...), custom_call_target="tpu_custom_call" | custom-call | flops 268435456 | bytes 2752512 | tf_op jit(solution)/shard_map/pallas_call | solution.py:29
  36.5 1.3 %collective-permute-done.10.after_ref = bf16[128,256]{1,0:T(8,128)(2,1)S(1)} collective-permute-done((bf16[128,256]{1,0:T(8,128)(2,1)S(1)}, bf16[128,256]{1,0:T(8,128)(2,1)S(1)}, u32[]{:S(2)}, u32[]{:S(2)}) %collective-permute-start.10) | collective-permute-done | bytes 65568 | tf_op jit(solution)/shard_map/ppermute | solution.py:86
  37.8 0.6 %shard_map.99 = (bf16[3,128,128]{2,1,0:T(8,128)(2,1)S(1)}, bf16[3,128,128]{2,1,0:T(8,128)(2,1)S(1)}, bf16[3,128,128]{2,1,0:T(8,128)(2,1)S(1)}, bf16[3,128,128]{2,1,0:T(8,128)(2,1)S(1)}) custom-call(bf16[3,512,128]{2,1,0:T(8,128)(2,1)S(1)} %get-tuple-element.44.qkv_ref, bf16[128,256]{1,0:T(8,128)(2,1)S(1)} %copy-done.2, ...), custom_call_target="tpu_custom_call" | custom-call | flops 100663296 | bytes 2097152 | tf_op jit(solution)/shard_map/pallas_call | solution.py:29
  38.4 0.0 collective-permute-done.16.refs_3_
  38.4 0.5 shard_map.100
  38.9 0.1 collective-permute-start.17
  39.0 0.6 %collective-permute-start.11 = (bf16[3,128,128]{2,1,0:T(8,128)(2,1)S(1)}, bf16[3,128,128]{2,1,0:T(8,128)(2,1)S(1)}, u32[]{:S(2)}, u32[]{:S(2)}) collective-permute-start(bf16[3,128,128]{2,1,0:T(8,128)(2,1)S(1)} %get-tuple-element.61), channel_id=1, source_target_pairs={{0,4},{4,0},{8,12},{12,8},{16,20},{20,16},{24,28},{28,24},{1,5},{5... | collective-permute-start | bytes 294920 | tf_op jit(solution)/shard_map/ppermute | solution.py:75
  39.6 1.4 %collective-permute-start.12 = (bf16[3,128,128]{2,1,0:T(8,128)(2,1)S(1)}, bf16[3,128,128]{2,1,0:T(8,128)(2,1)S(1)}, u32[]{:S(2)}, u32[]{:S(2)}) collective-permute-start(bf16[3,128,128]{2,1,0:T(8,128)(2,1)S(1)} %get-tuple-element.62), channel_id=1, source_target_pairs={{0,8},{4,12},{8,0},{12,4},{16,24},{20,28},{24,16},{28,20},{1,9},{5... | collective-permute-start | bytes 294920 | tf_op jit(solution)/shard_map/ppermute | solution.py:75
  41.0 1.6 %collective-permute-start.13 = (bf16[3,128,128]{2,1,0:T(8,128)(2,1)S(1)}, bf16[3,128,128]{2,1,0:T(8,128)(2,1)S(1)}, u32[]{:S(2)}, u32[]{:S(2)}) collective-permute-start(bf16[3,128,128]{2,1,0:T(8,128)(2,1)S(1)} %get-tuple-element.63), channel_id=1, source_target_pairs={{0,12},{4,8},{8,4},{12,0},{16,28},{20,24},{24,20},{28,16},{1,13},{... | collective-permute-start | bytes 294920 | tf_op jit(solution)/shard_map/ppermute | solution.py:75
  42.6 0.1 add_bitcast_fusion
  42.7 1.6 %collective-permute-start.18 = (bf16[1,128,512]{2,1,0:T(8,128)(2,1)S(1)}, bf16[1,128,512]{2,1,0:T(8,128)(2,1)S(1)}, u32[]{:S(2)}, u32[]{:S(2)}) collective-permute-start(bf16[1,128,512]{2,1,0:T(8,128)(2,1)S(1)} %fusion), channel_id=1, source_target_pairs={{0,2},{1,3},{2,0},{3,1},{4,6},{5,7},{6,4},{7,5},{8,10},{9,11},{10,... | collective-permute-start | bytes 393224 | tf_op jit(solution)/shard_map/ppermute | solution.py:52
  44.2 0.0 collective-permute-done.11.refs_1_
  44.2 1.0 %collective-permute-done.12.refs_2_ = bf16[3,128,128]{2,1,0:T(8,128)(2,1)S(1)} collective-permute-done((bf16[3,128,128]{2,1,0:T(8,128)(2,1)S(1)}, bf16[3,128,128]{2,1,0:T(8,128)(2,1)S(1)}, u32[]{:S(2)}, u32[]{:S(2)}) %collective-permute-start.12) | collective-permute-done | bytes 98336 | tf_op jit(solution)/shard_map/ppermute | solution.py:75
  45.2 2.3 %collective-permute-done.13.refs_3_ = bf16[3,128,128]{2,1,0:T(8,128)(2,1)S(1)} collective-permute-done((bf16[3,128,128]{2,1,0:T(8,128)(2,1)S(1)}, bf16[3,128,128]{2,1,0:T(8,128)(2,1)S(1)}, u32[]{:S(2)}, u32[]{:S(2)}) %collective-permute-start.13) | collective-permute-done | bytes 98336 | tf_op jit(solution)/shard_map/ppermute | solution.py:75
  47.5 0.2 collective-permute-done.18
  47.7 0.9 %shard_map.101 = (bf16[128,512]{1,0:T(8,128)(2,1)}, bf16[128,512]{1,0:T(8,128)(2,1)}, bf16[128,512]{1,0:T(8,128)(2,1)}, bf16[128,512]{1,0:T(8,128)(2,1)}) custom-call(bf16[3,128,128]{2,1,0:T(8,128)(2,1)S(1)} %get-tuple-element.60.refs_5_.refs_0_, bf16[3,128,128]{2,1,0:T(8,128)(2,1)S(1)} %collective-permute-done.11.refs_1_, ...), custom_call_target="tpu_custom_call" | custom-call | bytes 1310720 | tf_op jit(solution)/shard_map/pallas_call | solution.py:29
  (12 shorter events, 0.1 us)
Async XLA Ops:
  2.7 6.6 %collective-permute-start.5 = (bf16[128,512]{1,0:T(8,128)(2,1)}, bf16[128,512]{1,0:T(8,128)(2,1)S(1)}, u32[]{:S(2)}, u32[]{:S(2)}) collective-permute-start(bf16[128,512]{1,0:T(8,128)(2,1)} %get-tuple-element.42.refs_0_), channel_id=1, source_target_pairs={{0,3},{1,2},{2,1},{3,0},{4,7},{5,6},{6,5},{7,4},{8,11},{9,10},{10,... | collective-permute-start | bytes 393224 | tf_op jit(solution)/shard_map/ppermute | solution.py:52
  5.1 7.6 %collective-permute-start.4 = (bf16[128,512]{1,0:T(8,128)(2,1)}, bf16[128,512]{1,0:T(8,128)(2,1)S(1)}, u32[]{:S(2)}, u32[]{:S(2)}) collective-permute-start(bf16[128,512]{1,0:T(8,128)(2,1)} %get-tuple-element.42.refs_0_), channel_id=1, source_target_pairs={{0,2},{1,3},{2,0},{3,1},{4,6},{5,7},{6,4},{7,5},{8,10},{9,11},{10,... | collective-permute-start | bytes 393224 | tf_op jit(solution)/shard_map/ppermute | solution.py:52
  5.8 6.9 %collective-permute-start.3 = (bf16[128,512]{1,0:T(8,128)(2,1)}, bf16[128,512]{1,0:T(8,128)(2,1)S(1)}, u32[]{:S(2)}, u32[]{:S(2)}) collective-permute-start(bf16[128,512]{1,0:T(8,128)(2,1)} %get-tuple-element.42.refs_0_), channel_id=1, source_target_pairs={{0,1},{1,0},{2,3},{3,2},{4,5},{5,4},{6,7},{7,6},{8,9},{9,8},{10,11... | collective-permute-start | bytes 393224 | tf_op jit(solution)/shard_map/ppermute | solution.py:52
  5.8 10.3 %collective-permute-start = (bf16[3,128,128]{2,1,0:T(8,128)(2,1)}, bf16[3,128,128]{2,1,0:T(8,128)(2,1)S(1)}, u32[]{:S(2)}, u32[]{:S(2)}) collective-permute-start(bf16[3,128,128]{2,1,0:T(8,128)(2,1)} %get-tuple-element.38), channel_id=1, source_target_pairs={{0,4},{4,0},{8,12},{12,8},{16,20},{20,16},{24,28},{28,24},{1,5},{5... | collective-permute-start | bytes 294920 | tf_op jit(solution)/shard_map/ppermute | solution.py:75
  7.6 8.5 %collective-permute-start.1 = (bf16[3,128,128]{2,1,0:T(8,128)(2,1)}, bf16[3,128,128]{2,1,0:T(8,128)(2,1)S(1)}, u32[]{:S(2)}, u32[]{:S(2)}) collective-permute-start(bf16[3,128,128]{2,1,0:T(8,128)(2,1)} %get-tuple-element.39), channel_id=1, source_target_pairs={{0,8},{4,12},{8,0},{12,4},{16,24},{20,28},{24,16},{28,20},{1,9},{5... | collective-permute-start | bytes 294920 | tf_op jit(solution)/shard_map/ppermute | solution.py:75
  9.3 6.8 %collective-permute-start.2 = (bf16[3,128,128]{2,1,0:T(8,128)(2,1)}, bf16[3,128,128]{2,1,0:T(8,128)(2,1)S(1)}, u32[]{:S(2)}, u32[]{:S(2)}) collective-permute-start(bf16[3,128,128]{2,1,0:T(8,128)(2,1)} %get-tuple-element.40), channel_id=1, source_target_pairs={{0,12},{4,8},{8,4},{12,0},{16,28},{20,24},{24,20},{28,16},{1,13},{... | collective-permute-start | bytes 294920 | tf_op jit(solution)/shard_map/ppermute | solution.py:75
  12.7 1.6 %copy-start = (bf16[512,2048]{1,0:T(8,128)(2,1)S(1)}, bf16[512,2048]{1,0:T(8,128)(2,1)}, u32[]{:S(2)}) copy-start(bf16[512,2048]{1,0:T(8,128)(2,1)} %refs_4_.3) | copy-start | bytes 6291460
  14.3 0.9 %copy-start.3 = (bf16[128,512]{1,0:T(8,128)(2,1)S(1)}, bf16[128,512]{1,0:T(8,128)(2,1)}, u32[]{:S(2)}) copy-start(bf16[128,512]{1,0:T(8,128)(2,1)} %get-tuple-element.42.refs_0_) | copy-start | bytes 393220
  15.2 0.9 %copy-start.2 = (bf16[128,256]{1,0:T(8,128)(2,1)S(1)}, bf16[128,256]{1,0:T(8,128)(2,1)}, u32[]{:S(2)}) copy-start(bf16[128,256]{1,0:T(8,128)(2,1)} %get-tuple-element.41.refs_4_.om_ref) | copy-start | bytes 196612
  15.2 0.9 %copy-start.4 = (bf16[3,128,128]{2,1,0:T(8,128)(2,1)S(1)}, bf16[3,128,128]{2,1,0:T(8,128)(2,1)}, u32[]{:S(2)}) copy-start(bf16[3,128,128]{2,1,0:T(8,128)(2,1)} %get-tuple-element.37.refs_0_) | copy-start | bytes 294916
  16.6 12.8 %collective-permute-start.9 = (bf16[128,256]{1,0:T(8,128)(2,1)S(1)}, bf16[128,256]{1,0:T(8,128)(2,1)S(1)}, u32[]{:S(2)}, u32[]{:S(2)}) collective-permute-start(bf16[128,256]{1,0:T(8,128)(2,1)S(1)} %get-tuple-element.53), channel_id=1, source_target_pairs={{0,16},{4,20},{8,24},{12,28},{1,17},{5,21},{9,25},{13,29},{2,18},{... | collective-permute-start | bytes 196616 | tf_op jit(solution)/shard_map/ppermute | solution.py:86
  21.4 4.3 %collective-permute-start.6 = (bf16[128,128]{1,0:T(8,128)(2,1)S(1)}, bf16[128,128]{1,0:T(8,128)(2,1)S(1)}, u32[]{:S(2)}, u32[]{:S(2)}) collective-permute-start(bf16[128,128]{1,0:T(8,128)(2,1)S(1)} %get-tuple-element.49), channel_id=1, source_target_pairs={{0,4},{4,0},{8,12},{12,8},{16,20},{20,16},{24,28},{28,24},{1,5},{5... | collective-permute-start | bytes 98312 | tf_op jit(solution)/shard_map/ppermute | solution.py:75
  23.0 4.0 %collective-permute-start.7 = (bf16[128,128]{1,0:T(8,128)(2,1)S(1)}, bf16[128,128]{1,0:T(8,128)(2,1)S(1)}, u32[]{:S(2)}, u32[]{:S(2)}) collective-permute-start(bf16[128,128]{1,0:T(8,128)(2,1)S(1)} %get-tuple-element.50), channel_id=1, source_target_pairs={{0,8},{4,12},{8,0},{12,4},{16,24},{20,28},{24,16},{28,20},{1,9},{5... | collective-permute-start | bytes 98312 | tf_op jit(solution)/shard_map/ppermute | solution.py:75
  24.6 4.8 %collective-permute-start.8 = (bf16[128,128]{1,0:T(8,128)(2,1)S(1)}, bf16[128,128]{1,0:T(8,128)(2,1)S(1)}, u32[]{:S(2)}, u32[]{:S(2)}) collective-permute-start(bf16[128,128]{1,0:T(8,128)(2,1)S(1)} %get-tuple-element.51), channel_id=1, source_target_pairs={{0,12},{4,8},{8,4},{12,0},{16,28},{20,24},{24,20},{28,16},{1,13},{... | collective-permute-start | bytes 98312 | tf_op jit(solution)/shard_map/ppermute | solution.py:75
  29.4 9.1 %copy-start.1 = (bf16[512,2048]{1,0:T(8,128)(2,1)S(1)}, bf16[512,2048]{1,0:T(8,128)(2,1)}, u32[]{:S(2)}) copy-start(bf16[512,2048]{1,0:T(8,128)(2,1)} %refs_4_.3) | copy-start | bytes 6291460
  30.1 7.7 %collective-permute-start.10 = (bf16[128,256]{1,0:T(8,128)(2,1)S(1)}, bf16[128,256]{1,0:T(8,128)(2,1)S(1)}, u32[]{:S(2)}, u32[]{:S(2)}) collective-permute-start(bf16[128,256]{1,0:T(8,128)(2,1)S(1)} %get-tuple-element.59), channel_id=1, source_target_pairs={{16,0},{20,4},{24,8},{28,12},{17,1},{21,5},{25,9},{29,13},{18,2},{... | collective-permute-start | bytes 196616 | tf_op jit(solution)/shard_map/ppermute | solution.py:86
  31.4 7.0 %collective-permute-start.14 = (bf16[128,128]{1,0:T(8,128)(2,1)S(1)}, bf16[128,128]{1,0:T(8,128)(2,1)S(1)}, u32[]{:S(2)}, u32[]{:S(2)}) collective-permute-start(bf16[128,128]{1,0:T(8,128)(2,1)S(1)} %get-tuple-element.65), channel_id=1, source_target_pairs={{0,4},{4,0},{8,12},{12,8},{16,20},{20,16},{24,28},{28,24},{1,5},{5... | collective-permute-start | bytes 98312 | tf_op jit(solution)/shard_map/ppermute | solution.py:75
  32.0 6.4 %collective-permute-start.15 = (bf16[128,128]{1,0:T(8,128)(2,1)S(1)}, bf16[128,128]{1,0:T(8,128)(2,1)S(1)}, u32[]{:S(2)}, u32[]{:S(2)}) collective-permute-start(bf16[128,128]{1,0:T(8,128)(2,1)S(1)} %get-tuple-element.66), channel_id=1, source_target_pairs={{0,8},{4,12},{8,0},{12,4},{16,24},{20,28},{24,16},{28,20},{1,9},{5... | collective-permute-start | bytes 98312 | tf_op jit(solution)/shard_map/ppermute | solution.py:75
  32.5 6.0 %collective-permute-start.16 = (bf16[128,128]{1,0:T(8,128)(2,1)S(1)}, bf16[128,128]{1,0:T(8,128)(2,1)S(1)}, u32[]{:S(2)}, u32[]{:S(2)}) collective-permute-start(bf16[128,128]{1,0:T(8,128)(2,1)S(1)} %get-tuple-element.67), channel_id=1, source_target_pairs={{0,12},{4,8},{8,4},{12,0},{16,28},{20,24},{24,20},{28,16},{1,13},{... | collective-permute-start | bytes 98312 | tf_op jit(solution)/shard_map/ppermute | solution.py:75
  38.9 3.6 %collective-permute-start.17 = (bf16[2,128,512]{2,1,0:T(8,128)(2,1)S(1)}, bf16[2,128,512]{2,1,0:T(8,128)(2,1)S(1)}, u32[]{:S(2)}, u32[]{:S(2)}) collective-permute-start(bf16[2,128,512]{2,1,0:T(8,128)(2,1)S(1)} %get-tuple-element.69), channel_id=1, source_target_pairs={{0,1},{1,0},{2,3},{3,2},{4,5},{5,4},{6,7},{7,6},{8,9},{9,8},{10,11... | collective-permute-start | bytes 786440 | tf_op jit(solution)/shard_map/ppermute | solution.py:52
  39.0 5.2 %collective-permute-start.11 = (bf16[3,128,128]{2,1,0:T(8,128)(2,1)S(1)}, bf16[3,128,128]{2,1,0:T(8,128)(2,1)S(1)}, u32[]{:S(2)}, u32[]{:S(2)}) collective-permute-start(bf16[3,128,128]{2,1,0:T(8,128)(2,1)S(1)} %get-tuple-element.61), channel_id=1, source_target_pairs={{0,4},{4,0},{8,12},{12,8},{16,20},{20,16},{24,28},{28,24},{1,5},{5... | collective-permute-start | bytes 294920 | tf_op jit(solution)/shard_map/ppermute | solution.py:75
  39.6 5.6 %collective-permute-start.12 = (bf16[3,128,128]{2,1,0:T(8,128)(2,1)S(1)}, bf16[3,128,128]{2,1,0:T(8,128)(2,1)S(1)}, u32[]{:S(2)}, u32[]{:S(2)}) collective-permute-start(bf16[3,128,128]{2,1,0:T(8,128)(2,1)S(1)} %get-tuple-element.62), channel_id=1, source_target_pairs={{0,8},{4,12},{8,0},{12,4},{16,24},{20,28},{24,16},{28,20},{1,9},{5... | collective-permute-start | bytes 294920 | tf_op jit(solution)/shard_map/ppermute | solution.py:75
  41.0 6.5 %collective-permute-start.13 = (bf16[3,128,128]{2,1,0:T(8,128)(2,1)S(1)}, bf16[3,128,128]{2,1,0:T(8,128)(2,1)S(1)}, u32[]{:S(2)}, u32[]{:S(2)}) collective-permute-start(bf16[3,128,128]{2,1,0:T(8,128)(2,1)S(1)} %get-tuple-element.63), channel_id=1, source_target_pairs={{0,12},{4,8},{8,4},{12,0},{16,28},{20,24},{24,20},{28,16},{1,13},{... | collective-permute-start | bytes 294920 | tf_op jit(solution)/shard_map/ppermute | solution.py:75
  42.7 5.1 %collective-permute-start.18 = (bf16[1,128,512]{2,1,0:T(8,128)(2,1)S(1)}, bf16[1,128,512]{2,1,0:T(8,128)(2,1)S(1)}, u32[]{:S(2)}, u32[]{:S(2)}) collective-permute-start(bf16[1,128,512]{2,1,0:T(8,128)(2,1)S(1)} %fusion), channel_id=1, source_target_pairs={{0,2},{1,3},{2,0},{3,1},{4,6},{5,7},{6,4},{7,5},{8,10},{9,11},{10,... | collective-permute-start | bytes 393224 | tf_op jit(solution)/shard_map/ppermute | solution.py:52

commit v6 on v5

--- a/solution.py
+++ b/solution.py
@@ -71,9 +71,11 @@
 
 def exchange(parts):
     n, size = len(parts), lax.axis_size("seq")
-    return [parts[0]] + [
-        lax.ppermute(parts[k], "seq", [(i, i ^ k) for i in range(size)]) for k in range(1, n)
+    got = [
+        lax.ppermute(parts[k], "seq", [(i, i ^ k) for i in range(size)])
+        for k in reversed(range(1, n))
     ]
+    return [parts[0]] + got[::-1]
 
 
 def from_groups(total, n, forward):
@@ -111,8 +113,12 @@
         copy.wait()
 
 
+def mark_kernel(_, out_ref):
+    out_ref[...] = jnp.zeros(out_ref.shape, out_ref.dtype)
+
+
 def grad_mixed_kernel(n, *refs):
-    blocks, w_ref, outs, scr = refs[: -n - 2], refs[-n - 2], refs[-n - 1 : -1], refs[-1]
+    blocks, w_ref, outs, scr = refs[: -n - 3], refs[-n - 3], refs[-n - 1 : -1], refs[-1]
     r, h = member(n), lax.axis_index("head")
     width = blocks[0].shape[1]
     dim = outs[0].shape[1]
@@ -272,10 +278,12 @@
     )
     blocks = [go] + [swap(go, "head", offset) for offset in range(1, split)]
     got = exchange(sends)
+    (mark,) = call(mark_kernel, [struct((8, 128), f32)], om, specs=[ANY], flops=10**10)
     gm_parts = call(
         functools.partial(grad_mixed_kernel, n),
         [struct((rows, dim))] * n,
-        *blocks, out_weight, flops=2 * rows * out_weight.size,
+        *blocks, out_weight, mark, flops=2 * rows * out_weight.size,
+        specs=[VMEM] * (split + 1) + [ANY],
         scratch=[pltpu.VMEM((rows, n * dim), jnp.bfloat16)],
     )
     gm_in = exchange(gm_parts)

time: 48.9 us -> 48.6 us (level)
    pallas_call x9 -> x10, Pallas kernels: 8.25 us -> 8.26 us  [call(): pl.pallas_call(body, out_shape=outs, in_specs=specs or [VMEM] * len(args)...]
  transfers between devices with their start and end apart: 19 -> 19, of which waited for: 7 -> 8; matrix products, arithmetic and copies ran while one was open for 0% -> 0% of each run, Pallas kernels for 8% -> 8%
where the time goes in v6:
time: 48.6 us; the launch traced here: 48.4 us
  starting transfers between devices  28 us (58%)
  waiting for transfers between devices  8.81 us (18%)
  Pallas kernels  8.26 us (17%)
  local copies, waits for them, and re-layouts  2.44 us (5%)
  between operations  0.82 us (2%)
    ppermute x12, starting transfers between devices, exchange(): lax.ppermute(parts[k], 'seq', [(i, i ^ k) for i in range(size)])  17.4 us
    pallas_call x10, Pallas kernels, call(): pl.pallas_call(body, out_shape=outs, in_specs=specs or [VMEM] * len(args)...  8.26 us
    ppermute x12, waiting for transfers between devices, exchange(): lax.ppermute(parts[k], 'seq', [(i, i ^ k) for i in range(size)])  7.02 us
    ppermute x2, starting transfers between devices, from_groups(): got = lax.ppermute(bf(inclusive), 'seq', pairs).astype(jnp.float32)  5.88 us
    ppermute x5, starting transfers between devices, swap(): return lax.ppermute(array, axis, [(i, i ^ bit) for i in range(size)])  4.72 us
    unnamed x10, local copies, waits for them, and re-layouts  2.4 us
    ppermute x2, waiting for transfers between devices, from_groups(): got = lax.ppermute(bf(inclusive), 'seq', pairs).astype(jnp.float32)  1.38 us
  transfers between devices with their start and end apart: 19, of which 8 were waited for; matrix products, arithmetic and copies ran while one was open for 0% of the time, Pallas kernels for 8%

profile of v6, /device:TPU:0, one launch (start us, length us, event | category | flops | bytes accessed | tf_op | source)
XLA Modules:
  0.0 48.4 jit_solution(7677372689278178)
XLA Ops:
  0.6 2.0 %shard_map.93 = (bf16[3,128,128]{2,1,0:T(8,128)(2,1)}, bf16[3,128,128]{2,1,0:T(8,128)(2,1)}, bf16[3,128,128]{2,1,0:T(8,128)(2,1)}, bf16[3,128,128]{2,1,0:T(8,128...) custom-call(bf16[128,512]{1,0:T(8,128)(2,1)} %q_ref.1, bf16[128,512]{1,0:T(8,128)(2,1)} %k_ref.1, ...), custom_call_target="tpu_custom_call" | custom-call | bytes 1376256 | tf_op jit(solution)/shard_map/pallas_call | solution.py:29
  2.7 2.4 %collective-permute-start.5 = (bf16[128,512]{1,0:T(8,128)(2,1)}, bf16[128,512]{1,0:T(8,128)(2,1)S(1)}, u32[]{:S(2)}, u32[]{:S(2)}) collective-permute-start(bf16[128,512]{1,0:T(8,128)(2,1)} %get-tuple-element.42.refs_0_), channel_id=1, source_target_pairs={{0,3},{1,2},{2,1},{3,0},{4,7},{5,6},{6,5},{7,4},{8,11},{9,10},{10,... | collective-permute-start | bytes 393224 | tf_op jit(solution)/shard_map/ppermute | solution.py:52
  5.1 0.6 %collective-permute-start.4 = (bf16[128,512]{1,0:T(8,128)(2,1)}, bf16[128,512]{1,0:T(8,128)(2,1)S(1)}, u32[]{:S(2)}, u32[]{:S(2)}) collective-permute-start(bf16[128,512]{1,0:T(8,128)(2,1)} %get-tuple-element.42.refs_0_), channel_id=1, source_target_pairs={{0,2},{1,3},{2,0},{3,1},{4,6},{5,7},{6,4},{7,5},{8,10},{9,11},{10,... | collective-permute-start | bytes 393224 | tf_op jit(solution)/shard_map/ppermute | solution.py:52
  5.8 0.0 collective-permute-start.3
  5.8 1.8 %collective-permute-start = (bf16[3,128,128]{2,1,0:T(8,128)(2,1)}, bf16[3,128,128]{2,1,0:T(8,128)(2,1)S(1)}, u32[]{:S(2)}, u32[]{:S(2)}) collective-permute-start(bf16[3,128,128]{2,1,0:T(8,128)(2,1)} %get-tuple-element.38), channel_id=1, source_target_pairs={{0,4},{4,0},{8,12},{12,8},{16,20},{20,16},{24,28},{28,24},{1,5},{5... | collective-permute-start | bytes 294920 | tf_op jit(solution)/shard_map/ppermute | solution.py:75
  7.6 1.6 %collective-permute-start.1 = (bf16[3,128,128]{2,1,0:T(8,128)(2,1)}, bf16[3,128,128]{2,1,0:T(8,128)(2,1)S(1)}, u32[]{:S(2)}, u32[]{:S(2)}) collective-permute-start(bf16[3,128,128]{2,1,0:T(8,128)(2,1)} %get-tuple-element.39), channel_id=1, source_target_pairs={{0,8},{4,12},{8,0},{12,4},{16,24},{20,28},{24,16},{28,20},{1,9},{5... | collective-permute-start | bytes 294920 | tf_op jit(solution)/shard_map/ppermute | solution.py:75
  9.2 0.2 collective-permute-done.5.refs_3_
  9.3 3.4 %collective-permute-start.2 = (bf16[3,128,128]{2,1,0:T(8,128)(2,1)}, bf16[3,128,128]{2,1,0:T(8,128)(2,1)S(1)}, u32[]{:S(2)}, u32[]{:S(2)}) collective-permute-start(bf16[3,128,128]{2,1,0:T(8,128)(2,1)} %get-tuple-element.40), channel_id=1, source_target_pairs={{0,12},{4,8},{8,4},{12,0},{16,28},{20,24},{24,20},{28,16},{1,13},{... | collective-permute-start | bytes 294920 | tf_op jit(solution)/shard_map/ppermute | solution.py:75
  12.7 0.8 %copy-done.1 = bf16[128,256]{1,0:T(8,128)(2,1)S(1)} copy-done((bf16[128,256]{1,0:T(8,128)(2,1)S(1)}, bf16[128,256]{1,0:T(8,128)(2,1)}, u32[]{:S(2)}) %copy-start.1) | copy-done | bytes 65560
  13.5 0.0 copy-start.4
  13.6 0.0 collective-permute-done.4.refs_2_
  13.6 0.0 collective-permute-done.3.refs_1_
  13.6 1.5 %copy-done = bf16[512,2048]{1,0:T(8,128)(2,1)S(1)} copy-done((bf16[512,2048]{1,0:T(8,128)(2,1)S(1)}, bf16[512,2048]{1,0:T(8,128)(2,1)}, u32[]{:S(2)}) %copy-start) | copy-done | bytes 2097176
  15.1 0.9 %shard_map.95 = (bf16[128,128]{1,0:T(8,128)(2,1)S(1)}, bf16[128,128]{1,0:T(8,128)(2,1)S(1)}, bf16[128,128]{1,0:T(8,128)(2,1)S(1)}, bf16[128,128]{1,0:T(8,128)(2,1)S(1)}) custom-call(bf16[128,512]{1,0:T(8,128)(2,1)S(1)} %copy-done.3, bf16[128,512]{1,0:T(8,128)(2,1)S(1)} %collective-permute-done.3.refs_1_, ...), custom_call_target="tpu_custom_call" | custom-call | flops 268435456 | bytes 2756608 | tf_op jit(solution)/shard_map/pallas_call | solution.py:29
  16.0 0.0 collective-permute-done.refs_1_
  16.0 0.0 collective-permute-done.1.refs_2_
  16.0 0.1 collective-permute-done.2.refs_3_
  16.1 0.4 shard_map.96
  16.5 4.6 %collective-permute-start.9 = (bf16[128,256]{1,0:T(8,128)(2,1)S(1)}, bf16[128,256]{1,0:T(8,128)(2,1)S(1)}, u32[]{:S(2)}, u32[]{:S(2)}) collective-permute-start(bf16[128,256]{1,0:T(8,128)(2,1)S(1)} %get-tuple-element.53), channel_id=1, source_target_pairs={{0,16},{4,20},{8,24},{12,28},{1,17},{5,21},{9,25},{13,29},{2,18},{... | collective-permute-start | bytes 196616 | tf_op jit(solution)/shard_map/ppermute | solution.py:88
  21.1 1.6 %collective-permute-start.6 = (bf16[128,128]{1,0:T(8,128)(2,1)S(1)}, bf16[128,128]{1,0:T(8,128)(2,1)S(1)}, u32[]{:S(2)}, u32[]{:S(2)}) collective-permute-start(bf16[128,128]{1,0:T(8,128)(2,1)S(1)} %get-tuple-element.49), channel_id=1, source_target_pairs={{0,4},{4,0},{8,12},{12,8},{16,20},{20,16},{24,28},{28,24},{1,5},{5... | collective-permute-start | bytes 98312 | tf_op jit(solution)/shard_map/ppermute | solution.py:75
  22.7 1.6 %collective-permute-start.7 = (bf16[128,128]{1,0:T(8,128)(2,1)S(1)}, bf16[128,128]{1,0:T(8,128)(2,1)S(1)}, u32[]{:S(2)}, u32[]{:S(2)}) collective-permute-start(bf16[128,128]{1,0:T(8,128)(2,1)S(1)} %get-tuple-element.50), channel_id=1, source_target_pairs={{0,8},{4,12},{8,0},{12,4},{16,24},{20,28},{24,16},{28,20},{1,9},{5... | collective-permute-start | bytes 98312 | tf_op jit(solution)/shard_map/ppermute | solution.py:75
  24.3 0.4 collective-permute-start.8
  24.7 0.8 %shard_map.97 = (bf16[512,256]{1,0:T(8,128)(2,1)S(1)}, bf16[4,128,128]{2,1,0:T(8,128)(2,1)S(1)}, f32[512,128]{1,0:T(8,128)S(1)}) custom-call(bf16[3,512,128]{2,1,0:T(8,128)(2,1)S(1)} %get-tuple-element.44.qkv_ref, bf16[128,256]{1,0:T(8,128)(2,1)S(1)} %copy-done.2, bf16[512,256]{1,0:T(8,128)(2,1)S(1)} %get-tuple-element.45.kf_ref, ...), custom_call_target="tpu_custom_call" | custom-call | flops 134217728 | bytes 1638400 | tf_op jit(solution)/shard_map/pallas_call | solution.py:29
  25.5 1.2 %collective-permute-done.7.refs_2_ = bf16[128,128]{1,0:T(8,128)(2,1)S(1)} collective-permute-done((bf16[128,128]{1,0:T(8,128)(2,1)S(1)}, bf16[128,128]{1,0:T(8,128)(2,1)S(1)}, u32[]{:S(2)}, u32[]{:S(2)}) %collective-permute-start.7) | collective-permute-done | bytes 32800 | tf_op jit(solution)/shard_map/ppermute | solution.py:75
  26.6 2.5 %collective-permute-done.8.refs_3_ = bf16[128,128]{1,0:T(8,128)(2,1)S(1)} collective-permute-done((bf16[128,128]{1,0:T(8,128)(2,1)S(1)}, bf16[128,128]{1,0:T(8,128)(2,1)S(1)}, u32[]{:S(2)}, u32[]{:S(2)}) %collective-permute-start.8) | collective-permute-done | bytes 32800 | tf_op jit(solution)/shard_map/ppermute | solution.py:75
  29.1 0.8 %shard_map.98 = (bf16[512,128]{1,0:T(8,128)(2,1)S(1)}, bf16[4,128,256]{2,1,0:T(8,128)(2,1)S(1)}, bf16[128,256]{1,0:T(8,128)(2,1)S(1)}, bf16[128,128]{1,0:T(8,128...) custom-call(bf16[128,128]{1,0:T(8,128)(2,1)S(1)} %get-tuple-element.43.refs_5_., ...), custom_call_target="tpu_custom_call" | custom-call | flops 67108864 | bytes 1310720 | tf_op jit(solution)/shard_map/pallas_call | solution.py:29
  29.9 1.3 %collective-permute-start.10 = (bf16[128,256]{1,0:T(8,128)(2,1)S(1)}, bf16[128,256]{1,0:T(8,128)(2,1)S(1)}, u32[]{:S(2)}, u32[]{:S(2)}) collective-permute-start(bf16[128,256]{1,0:T(8,128)(2,1)S(1)} %get-tuple-element.59), channel_id=1, source_target_pairs={{16,0},{20,4},{24,8},{28,12},{17,1},{21,5},{25,9},{29,13},{18,2},{... | collective-permute-start | bytes 196616 | tf_op jit(solution)/shard_map/ppermute | solution.py:88
  31.2 0.6 %collective-permute-start.14 = (bf16[128,128]{1,0:T(8,128)(2,1)S(1)}, bf16[128,128]{1,0:T(8,128)(2,1)S(1)}, u32[]{:S(2)}, u32[]{:S(2)}) collective-permute-start(bf16[128,128]{1,0:T(8,128)(2,1)S(1)} %get-tuple-element.65), channel_id=1, source_target_pairs={{0,4},{4,0},{8,12},{12,8},{16,20},{20,16},{24,28},{28,24},{1,5},{5... | collective-permute-start | bytes 98312 | tf_op jit(solution)/shard_map/ppermute | solution.py:75
  31.7 0.5 collective-permute-start.15
  32.2 2.5 %collective-permute-start.16 = (bf16[128,128]{1,0:T(8,128)(2,1)S(1)}, bf16[128,128]{1,0:T(8,128)(2,1)S(1)}, u32[]{:S(2)}, u32[]{:S(2)}) collective-permute-start(bf16[128,128]{1,0:T(8,128)(2,1)S(1)} %get-tuple-element.67), channel_id=1, source_target_pairs={{0,12},{4,8},{8,4},{12,0},{16,28},{20,24},{24,20},{28,16},{1,13},{... | collective-permute-start | bytes 98312 | tf_op jit(solution)/shard_map/ppermute | solution.py:75
  34.7 1.5 %shard_map.99 = (bf16[512,128]{1,0:T(8,128)(2,1)S(1)}, f32[512,128]{1,0:T(8,128)S(1)}, f32[512,256]{1,0:T(8,128)S(1)}) custom-call(bf16[3,512,128]{2,1,0:T(8,128)(2,1)S(1)} %get-tuple-element.44.qkv_ref, bf16[128,256]{1,0:T(8,128)(2,1)S(1)} %copy-done.2, bf16[512,256]{1,0:T(8,128)(2,1)S(1)} %get-tuple-element.45.kf_ref, ...), custom_call_target="tpu_custom_call" | custom-call | flops 268435456 | bytes 2752512 | tf_op jit(solution)/shard_map/pallas_call | solution.py:29
  36.2 1.4 %collective-permute-done.10.after_ref = bf16[128,256]{1,0:T(8,128)(2,1)S(1)} collective-permute-done((bf16[128,256]{1,0:T(8,128)(2,1)S(1)}, bf16[128,256]{1,0:T(8,128)(2,1)S(1)}, u32[]{:S(2)}, u32[]{:S(2)}) %collective-permute-start.10) | collective-permute-done | bytes 65568 | tf_op jit(solution)/shard_map/ppermute | solution.py:88
  37.6 0.6 %shard_map.100 = (bf16[3,128,128]{2,1,0:T(8,128)(2,1)S(1)}, bf16[3,128,128]{2,1,0:T(8,128)(2,1)S(1)}, bf16[3,128,128]{2,1,0:T(8,128)(2,1)S(1)}, bf16[3,128,128]{2,1,0:T(8,128)(2,1)S(1)}) custom-call(bf16[3,512,128]{2,1,0:T(8,128)(2,1)S(1)} %get-tuple-element.44.qkv_ref, bf16[128,256]{1,0:T(8,128)(2,1)S(1)} %copy-done.2, ...), custom_call_target="tpu_custom_call" | custom-call | flops 100663296 | bytes 2097152 | tf_op jit(solution)/shard_map/pallas_call | solution.py:29
  38.2 0.0 collective-permute-done.14.refs_1_
  38.2 0.0 collective-permute-done.16.refs_3_
  38.2 0.5 shard_map.101
  38.7 0.1 collective-permute-start.17
  38.8 1.0 %collective-permute-start.11 = (bf16[3,128,128]{2,1,0:T(8,128)(2,1)S(1)}, bf16[3,128,128]{2,1,0:T(8,128)(2,1)S(1)}, u32[]{:S(2)}, u32[]{:S(2)}) collective-permute-start(bf16[3,128,128]{2,1,0:T(8,128)(2,1)S(1)} %get-tuple-element.61), channel_id=1, source_target_pairs={{0,4},{4,0},{8,12},{12,8},{16,20},{20,16},{24,28},{28,24},{1,5},{5... | collective-permute-start | bytes 294920 | tf_op jit(solution)/shard_map/ppermute | solution.py:75
  39.8 0.9 %collective-permute-start.12 = (bf16[3,128,128]{2,1,0:T(8,128)(2,1)S(1)}, bf16[3,128,128]{2,1,0:T(8,128)(2,1)S(1)}, u32[]{:S(2)}, u32[]{:S(2)}) collective-permute-start(bf16[3,128,128]{2,1,0:T(8,128)(2,1)S(1)} %get-tuple-element.62), channel_id=1, source_target_pairs={{0,8},{4,12},{8,0},{12,4},{16,24},{20,28},{24,16},{28,20},{1,9},{5... | collective-permute-start | bytes 294920 | tf_op jit(solution)/shard_map/ppermute | solution.py:75
  40.7 1.6 %collective-permute-start.13 = (bf16[3,128,128]{2,1,0:T(8,128)(2,1)S(1)}, bf16[3,128,128]{2,1,0:T(8,128)(2,1)S(1)}, u32[]{:S(2)}, u32[]{:S(2)}) collective-permute-start(bf16[3,128,128]{2,1,0:T(8,128)(2,1)S(1)} %get-tuple-element.63), channel_id=1, source_target_pairs={{0,12},{4,8},{8,4},{12,0},{16,28},{20,24},{24,20},{28,16},{1,13},{... | collective-permute-start | bytes 294920 | tf_op jit(solution)/shard_map/ppermute | solution.py:75
  42.3 0.0 collective-permute-done.17
  42.3 0.1 add_bitcast_fusion
  42.4 1.5 %collective-permute-start.18 = (bf16[1,128,512]{2,1,0:T(8,128)(2,1)S(1)}, bf16[1,128,512]{2,1,0:T(8,128)(2,1)S(1)}, u32[]{:S(2)}, u32[]{:S(2)}) collective-permute-start(bf16[1,128,512]{2,1,0:T(8,128)(2,1)S(1)} %fusion), channel_id=1, source_target_pairs={{0,2},{1,3},{2,0},{3,1},{4,6},{5,7},{6,4},{7,5},{8,10},{9,11},{10,... | collective-permute-start | bytes 393224 | tf_op jit(solution)/shard_map/ppermute | solution.py:52
  44.0 0.0 collective-permute-done.11.refs_1_
  44.0 1.4 %collective-permute-done.12.refs_2_ = bf16[3,128,128]{2,1,0:T(8,128)(2,1)S(1)} collective-permute-done((bf16[3,128,128]{2,1,0:T(8,128)(2,1)S(1)}, bf16[3,128,128]{2,1,0:T(8,128)(2,1)S(1)}, u32[]{:S(2)}, u32[]{:S(2)}) %collective-permute-start.12) | collective-permute-done | bytes 98336 | tf_op jit(solution)/shard_map/ppermute | solution.py:75
  45.4 1.8 %collective-permute-done.13.refs_3_ = bf16[3,128,128]{2,1,0:T(8,128)(2,1)S(1)} collective-permute-done((bf16[3,128,128]{2,1,0:T(8,128)(2,1)S(1)}, bf16[3,128,128]{2,1,0:T(8,128)(2,1)S(1)}, u32[]{:S(2)}, u32[]{:S(2)}) %collective-permute-start.13) | collective-permute-done | bytes 98336 | tf_op jit(solution)/shard_map/ppermute | solution.py:75
  47.3 0.2 collective-permute-done.18
  47.5 0.9 %shard_map.102 = (bf16[128,512]{1,0:T(8,128)(2,1)}, bf16[128,512]{1,0:T(8,128)(2,1)}, bf16[128,512]{1,0:T(8,128)(2,1)}, bf16[128,512]{1,0:T(8,128)(2,1)}) custom-call(bf16[3,128,128]{2,1,0:T(8,128)(2,1)S(1)} %get-tuple-element.60.refs_5_.refs_0_, bf16[3,128,128]{2,1,0:T(8,128)(2,1)S(1)} %collective-permute-done.11.refs_1_, ...), custom_call_target="tpu_custom_call" | custom-call | bytes 1310720 | tf_op jit(solution)/shard_map/pallas_call | solution.py:29
  (13 shorter events, 0.1 us)
Async XLA Ops:
  2.7 6.6 %collective-permute-start.5 = (bf16[128,512]{1,0:T(8,128)(2,1)}, bf16[128,512]{1,0:T(8,128)(2,1)S(1)}, u32[]{:S(2)}, u32[]{:S(2)}) collective-permute-start(bf16[128,512]{1,0:T(8,128)(2,1)} %get-tuple-element.42.refs_0_), channel_id=1, source_target_pairs={{0,3},{1,2},{2,1},{3,0},{4,7},{5,6},{6,5},{7,4},{8,11},{9,10},{10,... | collective-permute-start | bytes 393224 | tf_op jit(solution)/shard_map/ppermute | solution.py:52
  5.1 8.4 %collective-permute-start.4 = (bf16[128,512]{1,0:T(8,128)(2,1)}, bf16[128,512]{1,0:T(8,128)(2,1)S(1)}, u32[]{:S(2)}, u32[]{:S(2)}) collective-permute-start(bf16[128,512]{1,0:T(8,128)(2,1)} %get-tuple-element.42.refs_0_), channel_id=1, source_target_pairs={{0,2},{1,3},{2,0},{3,1},{4,6},{5,7},{6,4},{7,5},{8,10},{9,11},{10,... | collective-permute-start | bytes 393224 | tf_op jit(solution)/shard_map/ppermute | solution.py:52
  5.8 7.8 %collective-permute-start.3 = (bf16[128,512]{1,0:T(8,128)(2,1)}, bf16[128,512]{1,0:T(8,128)(2,1)S(1)}, u32[]{:S(2)}, u32[]{:S(2)}) collective-permute-start(bf16[128,512]{1,0:T(8,128)(2,1)} %get-tuple-element.42.refs_0_), channel_id=1, source_target_pairs={{0,1},{1,0},{2,3},{3,2},{4,5},{5,4},{6,7},{7,6},{8,9},{9,8},{10,11... | collective-permute-start | bytes 393224 | tf_op jit(solution)/shard_map/ppermute | solution.py:52
  5.8 10.2 %collective-permute-start = (bf16[3,128,128]{2,1,0:T(8,128)(2,1)}, bf16[3,128,128]{2,1,0:T(8,128)(2,1)S(1)}, u32[]{:S(2)}, u32[]{:S(2)}) collective-permute-start(bf16[3,128,128]{2,1,0:T(8,128)(2,1)} %get-tuple-element.38), channel_id=1, source_target_pairs={{0,4},{4,0},{8,12},{12,8},{16,20},{20,16},{24,28},{28,24},{1,5},{5... | collective-permute-start | bytes 294920 | tf_op jit(solution)/shard_map/ppermute | solution.py:75
  7.6 8.4 %collective-permute-start.1 = (bf16[3,128,128]{2,1,0:T(8,128)(2,1)}, bf16[3,128,128]{2,1,0:T(8,128)(2,1)S(1)}, u32[]{:S(2)}, u32[]{:S(2)}) collective-permute-start(bf16[3,128,128]{2,1,0:T(8,128)(2,1)} %get-tuple-element.39), channel_id=1, source_target_pairs={{0,8},{4,12},{8,0},{12,4},{16,24},{20,28},{24,16},{28,20},{1,9},{5... | collective-permute-start | bytes 294920 | tf_op jit(solution)/shard_map/ppermute | solution.py:75
  9.3 6.8 %collective-permute-start.2 = (bf16[3,128,128]{2,1,0:T(8,128)(2,1)}, bf16[3,128,128]{2,1,0:T(8,128)(2,1)S(1)}, u32[]{:S(2)}, u32[]{:S(2)}) collective-permute-start(bf16[3,128,128]{2,1,0:T(8,128)(2,1)} %get-tuple-element.40), channel_id=1, source_target_pairs={{0,12},{4,8},{8,4},{12,0},{16,28},{20,24},{24,20},{28,16},{1,13},{... | collective-permute-start | bytes 294920 | tf_op jit(solution)/shard_map/ppermute | solution.py:75
  12.7 0.8 %copy-start.1 = (bf16[128,256]{1,0:T(8,128)(2,1)S(1)}, bf16[128,256]{1,0:T(8,128)(2,1)}, u32[]{:S(2)}) copy-start(bf16[128,256]{1,0:T(8,128)(2,1)} %get-tuple-element.41._.refs_4_.om_ref) | copy-start | bytes 196612
  13.5 1.6 %copy-start = (bf16[512,2048]{1,0:T(8,128)(2,1)S(1)}, bf16[512,2048]{1,0:T(8,128)(2,1)}, u32[]{:S(2)}) copy-start(bf16[512,2048]{1,0:T(8,128)(2,1)} %refs_4_.3) | copy-start | bytes 6291460
  13.5 1.6 %copy-start.3 = (bf16[128,512]{1,0:T(8,128)(2,1)S(1)}, bf16[128,512]{1,0:T(8,128)(2,1)}, u32[]{:S(2)}) copy-start(bf16[128,512]{1,0:T(8,128)(2,1)} %get-tuple-element.42.refs_0_) | copy-start | bytes 393220
  13.5 2.6 %copy-start.2 = (bf16[128,256]{1,0:T(8,128)(2,1)S(1)}, bf16[128,256]{1,0:T(8,128)(2,1)}, u32[]{:S(2)}) copy-start(bf16[128,256]{1,0:T(8,128)(2,1)} %get-tuple-element.41._.refs_4_.om_ref) | copy-start | bytes 196612
  13.5 2.5 %copy-start.4 = (bf16[3,128,128]{2,1,0:T(8,128)(2,1)S(1)}, bf16[3,128,128]{2,1,0:T(8,128)(2,1)}, u32[]{:S(2)}) copy-start(bf16[3,128,128]{2,1,0:T(8,128)(2,1)} %get-tuple-element.37.refs_0_) | copy-start | bytes 294916
  16.5 12.6 %collective-permute-start.9 = (bf16[128,256]{1,0:T(8,128)(2,1)S(1)}, bf16[128,256]{1,0:T(8,128)(2,1)S(1)}, u32[]{:S(2)}, u32[]{:S(2)}) collective-permute-start(bf16[128,256]{1,0:T(8,128)(2,1)S(1)} %get-tuple-element.53), channel_id=1, source_target_pairs={{0,16},{4,20},{8,24},{12,28},{1,17},{5,21},{9,25},{13,29},{2,18},{... | collective-permute-start | bytes 196616 | tf_op jit(solution)/shard_map/ppermute | solution.py:88
  21.1 4.3 %collective-permute-start.6 = (bf16[128,128]{1,0:T(8,128)(2,1)S(1)}, bf16[128,128]{1,0:T(8,128)(2,1)S(1)}, u32[]{:S(2)}, u32[]{:S(2)}) collective-permute-start(bf16[128,128]{1,0:T(8,128)(2,1)S(1)} %get-tuple-element.49), channel_id=1, source_target_pairs={{0,4},{4,0},{8,12},{12,8},{16,20},{20,16},{24,28},{28,24},{1,5},{5... | collective-permute-start | bytes 98312 | tf_op jit(solution)/shard_map/ppermute | solution.py:75
  22.7 3.9 %collective-permute-start.7 = (bf16[128,128]{1,0:T(8,128)(2,1)S(1)}, bf16[128,128]{1,0:T(8,128)(2,1)S(1)}, u32[]{:S(2)}, u32[]{:S(2)}) collective-permute-start(bf16[128,128]{1,0:T(8,128)(2,1)S(1)} %get-tuple-element.50), channel_id=1, source_target_pairs={{0,8},{4,12},{8,0},{12,4},{16,24},{20,28},{24,16},{28,20},{1,9},{5... | collective-permute-start | bytes 98312 | tf_op jit(solution)/shard_map/ppermute | solution.py:75
  24.3 4.8 %collective-permute-start.8 = (bf16[128,128]{1,0:T(8,128)(2,1)S(1)}, bf16[128,128]{1,0:T(8,128)(2,1)S(1)}, u32[]{:S(2)}, u32[]{:S(2)}) collective-permute-start(bf16[128,128]{1,0:T(8,128)(2,1)S(1)} %get-tuple-element.51), channel_id=1, source_target_pairs={{0,12},{4,8},{8,4},{12,0},{16,28},{20,24},{24,20},{28,16},{1,13},{... | collective-permute-start | bytes 98312 | tf_op jit(solution)/shard_map/ppermute | solution.py:75
  29.9 7.7 %collective-permute-start.10 = (bf16[128,256]{1,0:T(8,128)(2,1)S(1)}, bf16[128,256]{1,0:T(8,128)(2,1)S(1)}, u32[]{:S(2)}, u32[]{:S(2)}) collective-permute-start(bf16[128,256]{1,0:T(8,128)(2,1)S(1)} %get-tuple-element.59), channel_id=1, source_target_pairs={{16,0},{20,4},{24,8},{28,12},{17,1},{21,5},{25,9},{29,13},{18,2},{... | collective-permute-start | bytes 196616 | tf_op jit(solution)/shard_map/ppermute | solution.py:88
  31.2 7.0 %collective-permute-start.14 = (bf16[128,128]{1,0:T(8,128)(2,1)S(1)}, bf16[128,128]{1,0:T(8,128)(2,1)S(1)}, u32[]{:S(2)}, u32[]{:S(2)}) collective-permute-start(bf16[128,128]{1,0:T(8,128)(2,1)S(1)} %get-tuple-element.65), channel_id=1, source_target_pairs={{0,4},{4,0},{8,12},{12,8},{16,20},{20,16},{24,28},{28,24},{1,5},{5... | collective-permute-start | bytes 98312 | tf_op jit(solution)/shard_map/ppermute | solution.py:75
  31.7 6.5 %collective-permute-start.15 = (bf16[128,128]{1,0:T(8,128)(2,1)S(1)}, bf16[128,128]{1,0:T(8,128)(2,1)S(1)}, u32[]{:S(2)}, u32[]{:S(2)}) collective-permute-start(bf16[128,128]{1,0:T(8,128)(2,1)S(1)} %get-tuple-element.66), channel_id=1, source_target_pairs={{0,8},{4,12},{8,0},{12,4},{16,24},{20,28},{24,16},{28,20},{1,9},{5... | collective-permute-start | bytes 98312 | tf_op jit(solution)/shard_map/ppermute | solution.py:75
  32.2 6.0 %collective-permute-start.16 = (bf16[128,128]{1,0:T(8,128)(2,1)S(1)}, bf16[128,128]{1,0:T(8,128)(2,1)S(1)}, u32[]{:S(2)}, u32[]{:S(2)}) collective-permute-start(bf16[128,128]{1,0:T(8,128)(2,1)S(1)} %get-tuple-element.67), channel_id=1, source_target_pairs={{0,12},{4,8},{8,4},{12,0},{16,28},{20,24},{24,20},{28,16},{1,13},{... | collective-permute-start | bytes 98312 | tf_op jit(solution)/shard_map/ppermute | solution.py:75
  38.7 3.6 %collective-permute-start.17 = (bf16[2,128,512]{2,1,0:T(8,128)(2,1)S(1)}, bf16[2,128,512]{2,1,0:T(8,128)(2,1)S(1)}, u32[]{:S(2)}, u32[]{:S(2)}) collective-permute-start(bf16[2,128,512]{2,1,0:T(8,128)(2,1)S(1)} %get-tuple-element.69), channel_id=1, source_target_pairs={{0,1},{1,0},{2,3},{3,2},{4,5},{5,4},{6,7},{7,6},{8,9},{9,8},{10,11... | collective-permute-start | bytes 786440 | tf_op jit(solution)/shard_map/ppermute | solution.py:52
  38.8 5.2 %collective-permute-start.11 = (bf16[3,128,128]{2,1,0:T(8,128)(2,1)S(1)}, bf16[3,128,128]{2,1,0:T(8,128)(2,1)S(1)}, u32[]{:S(2)}, u32[]{:S(2)}) collective-permute-start(bf16[3,128,128]{2,1,0:T(8,128)(2,1)S(1)} %get-tuple-element.61), channel_id=1, source_target_pairs={{0,4},{4,0},{8,12},{12,8},{16,20},{20,16},{24,28},{28,24},{1,5},{5... | collective-permute-start | bytes 294920 | tf_op jit(solution)/shard_map/ppermute | solution.py:75
  39.8 5.6 %collective-permute-start.12 = (bf16[3,128,128]{2,1,0:T(8,128)(2,1)S(1)}, bf16[3,128,128]{2,1,0:T(8,128)(2,1)S(1)}, u32[]{:S(2)}, u32[]{:S(2)}) collective-permute-start(bf16[3,128,128]{2,1,0:T(8,128)(2,1)S(1)} %get-tuple-element.62), channel_id=1, source_target_pairs={{0,8},{4,12},{8,0},{12,4},{16,24},{20,28},{24,16},{28,20},{1,9},{5... | collective-permute-start | bytes 294920 | tf_op jit(solution)/shard_map/ppermute | solution.py:75
  40.7 6.5 %collective-permute-start.13 = (bf16[3,128,128]{2,1,0:T(8,128)(2,1)S(1)}, bf16[3,128,128]{2,1,0:T(8,128)(2,1)S(1)}, u32[]{:S(2)}, u32[]{:S(2)}) collective-permute-start(bf16[3,128,128]{2,1,0:T(8,128)(2,1)S(1)} %get-tuple-element.63), channel_id=1, source_target_pairs={{0,12},{4,8},{8,4},{12,0},{16,28},{20,24},{24,20},{28,16},{1,13},{... | collective-permute-start | bytes 294920 | tf_op jit(solution)/shard_map/ppermute | solution.py:75
  42.4 5.1 %collective-permute-start.18 = (bf16[1,128,512]{2,1,0:T(8,128)(2,1)S(1)}, bf16[1,128,512]{2,1,0:T(8,128)(2,1)S(1)}, u32[]{:S(2)}, u32[]{:S(2)}) collective-permute-start(bf16[1,128,512]{2,1,0:T(8,128)(2,1)S(1)} %fusion), channel_id=1, source_target_pairs={{0,2},{1,3},{2,0},{3,1},{4,6},{5,7},{6,4},{7,5},{8,10},{9,11},{10,... | collective-permute-start | bytes 393224 | tf_op jit(solution)/shard_map/ppermute | solution.py:52

commit v7 on v6

--- a/solution.py
+++ b/solution.py
@@ -71,11 +71,10 @@
 
 def exchange(parts):
     n, size = len(parts), lax.axis_size("seq")
-    got = [
+    return [
         lax.ppermute(parts[k], "seq", [(i, i ^ k) for i in range(size)])
         for k in reversed(range(1, n))
-    ]
-    return [parts[0]] + got[::-1]
+    ] + [parts[0]]
 
 
 def from_groups(total, n, forward):
@@ -96,16 +95,15 @@
     return pl.ds(pl.multiple_of(index * width, 128), width)
 
 
-def pack_kernel(n, q_ref, k_ref, v_ref, om_ref, go_ref, *rest):
-    outs, om_out, go_out, sems = rest[:n], rest[n], rest[n + 1], rest[n + 2]
+def pack_kernel(n, q_ref, k_ref, v_ref, *rest):
+    outs, sems = rest[:n], rest[n]
     r = member(n)
-    dim = om_ref.shape[1]
-    copies = [(go_ref, go_out)]
+    dim = outs[0].shape[2]
+    copies = []
     for k in range(n):
         cols = lane(r ^ k, dim)
         for at, ref in enumerate((q_ref, k_ref, v_ref)):
             copies.append((ref.at[:, cols], outs[k].at[at]))
-    copies.append((om_ref.at[r], om_out))
     started = [pltpu.make_async_copy(a, b, sems.at[i]) for i, (a, b) in enumerate(copies)]
     for copy in started:
         copy.start()
@@ -117,13 +115,13 @@
     out_ref[...] = jnp.zeros(out_ref.shape, out_ref.dtype)
 
 
-def grad_mixed_kernel(n, *refs):
+def grad_mixed_kernel(n, offsets, *refs):
     blocks, w_ref, outs, scr = refs[: -n - 3], refs[-n - 3], refs[-n - 1 : -1], refs[-1]
     r, h = member(n), lax.axis_index("head")
     width = blocks[0].shape[1]
     dim = outs[0].shape[1]
     total = None
-    for offset, ref in enumerate(blocks):
+    for offset, ref in zip(offsets, blocks):
         part = mm(ref[...], w_ref[:, lane(h ^ offset, width)], NT)
         total = part if total is None else total + part
     scr[...] = bf(total)
@@ -132,7 +130,8 @@
 
 
 def first_kernel(n, *refs):
-    got, om_ref, (qkv_ref, kf_ref, state_ref, total_ref) = refs[:n], refs[n], refs[n + 2 :]
+    got, om_ref = refs[:n][::-1], refs[n]
+    qkv_ref, kf_ref, state_ref, total_ref = refs[n + 2 :]
     r = member(n)
     rows, dim = got[0].shape[1:]
     scale = dim ** (-0.25)
@@ -142,7 +141,7 @@
     k_all = qkv_ref[1]
     wide = k_all.astype(jnp.float32)
     half_sq = jnp.sum(wide * wide, axis=1, keepdims=True) * (scale * scale * 0.5)
-    kf = bf(jnp.exp(mm(k_all, om_ref[...]) * scale - half_sq))
+    kf = bf(jnp.exp(mm(k_all, om_ref[r]) * scale - half_sq))
     kf_ref[...] = kf
     total = jnp.zeros(total_ref.shape, jnp.float32)
     for t in range(n):
@@ -153,11 +152,11 @@
 
 
 def inner_kernel(n, qkv_ref, om_ref, kf_ref, state_ref, qf_ref, scores_ref, num_ref):
-    dim = om_ref.shape[0]
+    r, dim = member(n), om_ref.shape[1]
     rows = scores_ref.shape[1]
     scale = dim ** (-0.25)
     causal = causal_mask(rows)
-    qf_ref[...] = bf(jnp.exp(mm(qkv_ref[0], om_ref[...]) * scale))
+    qf_ref[...] = bf(jnp.exp(mm(qkv_ref[0], om_ref[r]) * scale))
     for t in range(n):
         at = pl.ds(t * rows, rows)
         qf = qf_ref[at, :]
@@ -167,7 +166,7 @@
 
 
 def turn_kernel(n, *refs):
-    gm_in, (qf_ref, num_ref, carried_ref) = refs[:n], refs[n : n + 3]
+    gm_in, (qf_ref, num_ref, carried_ref) = refs[:n][::-1], refs[n : n + 3]
     gn_ref, state_ref, total_ref = refs[n + 3 : n + 6]
     outs, scr = refs[n + 6 : -1], refs[-1]
     r = member(n)
@@ -196,7 +195,7 @@
 
 def back_kernel(n, qkv_ref, om_ref, kf_ref, qf_ref, scores_ref, gn_ref, state_ref, carried_ref,
                 later_ref, gq_ref, gv_ref, gkf_ref, gqf_scr):
-    dim = om_ref.shape[0]
+    r, dim = member(n), om_ref.shape[1]
     rows = scores_ref.shape[1]
     scale = dim ** (-0.25)
     causal = causal_mask(rows)
@@ -207,7 +206,7 @@
         gs = bf(jnp.where(causal, mm(gn, v, NT), 0.0))
         gqf = gqf_scr[at, :] + mm(gs, kf) + mm(gn, state_ref[t])
         terms = bf(gqf * qf.astype(jnp.float32))
-        gq_ref[at, :] = bf(mm(terms, om_ref[...], NT) * scale)
+        gq_ref[at, :] = bf(mm(terms, om_ref[r], NT) * scale)
         later = later_ref[t]
         gv_ref[at, :] = mm(scores_ref[t], gn, TN) + mm(kf, later, NT)
         gkf_ref[at, :] = mm(gs, qf, TN) + mm(v, later)
@@ -215,8 +214,7 @@
 
 def end_kernel(n, qkv_ref, om_ref, kf_ref, gq_ref, gv_ref, gkf_ref, after_ref, *rest):
     outs, gk_scr, gv_scr = rest[:n], rest[n], rest[n + 1]
-    r = member(n)
-    dim = om_ref.shape[0]
+    r, dim = member(n), om_ref.shape[1]
     rows = outs[0].shape[1]
     scale = dim ** (-0.25)
     kf, after = kf_ref[...], after_ref[...]
@@ -225,7 +223,7 @@
     terms = bf(gkf * kf.astype(jnp.float32))
     total = jnp.sum(terms.astype(jnp.float32), axis=1, keepdims=True)
     wide = qkv_ref[1].astype(jnp.float32)
-    gk_scr[...] = bf(mm(terms, om_ref[...], NT) * scale - total * wide * (scale * scale))
+    gk_scr[...] = bf(mm(terms, om_ref[r], NT) * scale - total * wide * (scale * scale))
     for k in range(n):
         at = pl.ds(pl.multiple_of((r ^ k) * rows, 128), rows)
         outs[k][0] = gq_ref[at, :]
@@ -234,7 +232,7 @@
 
 
 def mixed_project_kernel(n, offsets, *refs):
-    mixed_in, (w_ref, _, own_ref, sent_ref, scr) = refs[:n], refs[n:]
+    mixed_in, (w_ref, _, own_ref, sent_ref, scr) = refs[:n][::-1], refs[n:]
     r, h = member(n), lax.axis_index("head")
     width = own_ref.shape[2]
     dim = mixed_in[0].shape[1]
@@ -251,7 +249,8 @@
 
 
 def unpack_kernel(n, *refs):
-    got, (part_ref, last_ref), (out_ref, *outs) = refs[:n], refs[n : n + 2], refs[n + 2 :]
+    got, (part_ref, last_ref) = refs[:n][::-1], refs[n : n + 2]
+    out_ref, *outs = refs[n + 2 :]
     r = member(n)
     dim = got[0].shape[2]
     out_ref[...] = bf(part_ref[...] + last_ref[...].astype(jnp.float32))
@@ -270,17 +269,20 @@
     macs = long * dim * feats * 2
     f32 = jnp.float32
 
-    *sends, om, go = call(
+    offsets, blocks = [0], [grad_output]
+    for bit in reversed(bits):
+        blocks = blocks + [swap(b, "head", bit) for b in blocks]
+        offsets = offsets + [o ^ bit for o in offsets]
+    sends = call(
         functools.partial(pack_kernel, n),
-        [struct((3, rows, dim))] * n + [struct((dim, feats)), struct(grad_output.shape)],
-        queries, key_vectors, value_vectors, feature_proj, grad_output,
-        specs=[ANY] * 5, scratch=[pltpu.SemaphoreType.DMA((3 * n + 2,))], vmem=60,
-    )
-    blocks = [go] + [swap(go, "head", offset) for offset in range(1, split)]
+        [struct((3, rows, dim))] * n,
+        queries, key_vectors, value_vectors,
+        specs=[ANY] * 3, scratch=[pltpu.SemaphoreType.DMA((3 * n,))], vmem=60,
+    )
     got = exchange(sends)
-    (mark,) = call(mark_kernel, [struct((8, 128), f32)], om, specs=[ANY], flops=10**10)
+    (mark,) = call(mark_kernel, [struct((8, 128), f32)], blocks[offsets.index(1)], specs=[ANY], flops=10**10)
     gm_parts = call(
-        functools.partial(grad_mixed_kernel, n),
+        functools.partial(grad_mixed_kernel, n, offsets),
         [struct((rows, dim))] * n,
         *blocks, out_weight, mark, flops=2 * rows * out_weight.size,
         specs=[VMEM] * (split + 1) + [ANY],
@@ -295,13 +297,13 @@
             struct((n, dim, feats)),
             struct((dim, feats)),
         ],
-        *got, om, gm_parts[0], flops=2 * macs, specs=[VMEM] * (n + 1) + [ANY],
+        *got, feature_proj, gm_parts[0], flops=2 * macs, specs=[VMEM] * (n + 1) + [ANY],
     )
     carried = from_groups(total, n, True)
     qf, scores, num = call(
         functools.partial(inner_kernel, n),
         [struct((long, feats)), struct((n, rows, rows)), struct((long, dim), f32)],
-        qkv, om, kf, state, flops=4 * macs,
+        qkv, feature_proj, kf, state, flops=4 * macs,
     )
     gn, later, later_total, *mixed_parts = call(
         functools.partial(turn_kernel, n),
@@ -315,13 +317,13 @@
     gq, gv_part, gkf_part = call(
         functools.partial(back_kernel, n),
         [struct((long, dim)), struct((long, dim), f32), struct((long, feats), f32)],
-        qkv, om, kf, qf, scores, gn, state, carried, later, flops=8 * macs,
+        qkv, feature_proj, kf, qf, scores, gn, state, carried, later, flops=8 * macs,
         scratch=[pltpu.VMEM((long, feats), f32)],
     )
     grads = call(
         functools.partial(end_kernel, n),
         [struct((3, rows, dim))] * n,
-        qkv, om, kf, gq, gv_part, gkf_part, after_b, flops=3 * macs,
+        qkv, feature_proj, kf, gq, gv_part, gkf_part, after_b, flops=3 * macs,
         scratch=[pltpu.VMEM((long, dim), jnp.bfloat16)] * 2,
     )
     grads_in = exchange(grads)

time: 48.6 us -> 44.7 us (0.920)
  starting transfers between devices: 28 us -> 23.7 us
  waiting for transfers between devices: 8.81 us -> 11.9 us
  local copies, waits for them, and re-layouts: 2.44 us -> 0.06 us
    ppermute x12, starting transfers between devices: 17.4 us -> 14.2 us  [exchange(): lax.ppermute(parts[k], 'seq', [(i, i ^ k) for i in range(size)])]
    unnamed x10 -> x8, local copies, waits for them, and re-layouts: 2.4 us -> 0.02 us
    ppermute x12, waiting for transfers between devices: 7.02 us -> 9.26 us  [exchange(): lax.ppermute(parts[k], 'seq', [(i, i ^ k) for i in range(size)])]
    ppermute x5, waiting for transfers between devices: 0.42 us -> 1.83 us  [swap(): return lax.ppermute(array, axis, [(i, i ^ bit) for i in range(size)])]
    ppermute x5, starting transfers between devices: 4.72 us -> 3.69 us  [swap(): return lax.ppermute(array, axis, [(i, i ^ bit) for i in range(size)])]
    ppermute x2, waiting for transfers between devices: 1.38 us -> 0.76 us  [from_groups(): got = lax.ppermute(bf(inclusive), 'seq', pairs).astype(jnp.float32)]
  transfers between devices with their start and end apart: 19 -> 19, of which waited for: 8 -> 11; matrix products, arithmetic and copies ran while one was open for 0% -> 0% of each run, Pallas kernels for 8% -> 12%
where the time goes in v7:
time: 44.7 us; the launch traced here: 44.5 us
  starting transfers between devices  23.7 us (53%)
  waiting for transfers between devices  11.9 us (27%)
  Pallas kernels  8 us (18%)
  between operations  0.8 us (2%)
    ppermute x12, starting transfers between devices, exchange(): lax.ppermute(parts[k], 'seq', [(i, i ^ k) for i in range(size)])  14.2 us
    ppermute x12, waiting for transfers between devices, exchange(): lax.ppermute(parts[k], 'seq', [(i, i ^ k) for i in range(size)])  9.26 us
    pallas_call x10, Pallas kernels, call(): pl.pallas_call(body, out_shape=outs, in_specs=specs or [VMEM] * len(args)...  8 us
    ppermute x2, starting transfers between devices, from_groups(): got = lax.ppermute(bf(inclusive), 'seq', pairs).astype(jnp.float32)  5.79 us
    ppermute x5, starting transfers between devices, swap(): return lax.ppermute(array, axis, [(i, i ^ bit) for i in range(size)])  3.69 us
    ppermute x5, waiting for transfers between devices, swap(): return lax.ppermute(array, axis, [(i, i ^ bit) for i in range(size)])  1.83 us
  transfers between devices with their start and end apart: 19, of which 11 were waited for; matrix products, arithmetic and copies ran while one was open for 0% of the time, Pallas kernels for 12%

profile of v7, /device:TPU:0, one launch (start us, length us, event | category | flops | bytes accessed | tf_op | source)
XLA Modules:
  0.0 44.5 jit_solution(861252744545882523)
XLA Ops:
  0.6 3.0 %collective-permute-start.3 = (bf16[128,512]{1,0:T(8,128)(2,1)}, bf16[128,512]{1,0:T(8,128)(2,1)S(1)}, u32[]{:S(2)}, u32[]{:S(2)}) collective-permute-start(bf16[128,512]{1,0:T(8,128)(2,1)} %refs_0_.1), channel_id=1, source_target_pairs={{0,2},{1,3},{2,0},{3,1},{4,6},{5,7},{6,4},{7,5},{8,10},{9,11},{10,... | collective-permute-start | bytes 393224 | tf_op jit(solution)/shard_map/ppermute | solution.py:52
  3.6 1.8 %shard_map.93 = (bf16[3,128,128]{2,1,0:T(8,128)(2,1)}, bf16[3,128,128]{2,1,0:T(8,128)(2,1)}, bf16[3,128,128]{2,1,0:T(8,128)(2,1)}, bf16[3,128,128]{2,1,0:T(8,128)(2,1)}) custom-call(bf16[128,512]{1,0:T(8,128)(2,1)} %q_ref.1, bf16[128,512]{1,0:T(8,128)(2,1)} %k_ref.1, bf16[128,512]{1,0:T(8,128)(2,1)} %v_ref.1), custom_call_target="tpu_custom_call" | custom-call | bytes 786432 | tf_op jit(solution)/shard_map/pallas_call | solution.py:29
  5.4 2.6 %collective-permute-start = (bf16[3,128,128]{2,1,0:T(8,128)(2,1)}, bf16[3,128,128]{2,1,0:T(8,128)(2,1)S(1)}, u32[]{:S(2)}, u32[]{:S(2)}) collective-permute-start(bf16[3,128,128]{2,1,0:T(8,128)(2,1)} %get-tuple-element.35), channel_id=1, source_target_pairs={{0,12},{4,8},{8,4},{12,0},{16,28},{20,24},{24,20},{28,16},{1,13},{... | collective-permute-start | bytes 294920 | tf_op jit(solution)/shard_map/ppermute | solution.py:75
  8.0 0.4 %collective-permute-start.1 = (bf16[3,128,128]{2,1,0:T(8,128)(2,1)}, bf16[3,128,128]{2,1,0:T(8,128)(2,1)S(1)}, u32[]{:S(2)}, u32[]{:S(2)}) collective-permute-start(bf16[3,128,128]{2,1,0:T(8,128)(2,1)} %get-tuple-element.36), channel_id=1, source_target_pairs={{0,8},{4,12},{8,0},{12,4},{16,24},{20,28},{24,16},{28,20},{1,9},{5... | collective-permute-start | bytes 294920 | tf_op jit(solution)/shard_map/ppermute | solution.py:75
  8.5 0.5 %collective-permute-start.2 = (bf16[3,128,128]{2,1,0:T(8,128)(2,1)}, bf16[3,128,128]{2,1,0:T(8,128)(2,1)S(1)}, u32[]{:S(2)}, u32[]{:S(2)}) collective-permute-start(bf16[3,128,128]{2,1,0:T(8,128)(2,1)} %get-tuple-element.37), channel_id=1, source_target_pairs={{0,4},{4,0},{8,12},{12,8},{16,20},{20,16},{24,28},{28,24},{1,5},{5... | collective-permute-start | bytes 294920 | tf_op jit(solution)/shard_map/ppermute | solution.py:75
  9.0 0.0 collective-permute-done.3.refs_1_
  9.0 0.0 collective-permute-start.5
  9.0 0.0 collective-permute-done.4._.refs_2_
  9.0 0.0 copy-start.1
  9.0 0.0 copy-start.3
  9.0 1.3 %collective-permute-done.5.refs_3_ = bf16[128,512]{1,0:T(8,128)(2,1)S(1)} collective-permute-done((bf16[128,512]{1,0:T(8,128)(2,1)S(1)}, bf16[128,512]{1,0:T(8,128)(2,1)S(1)}, u32[]{:S(2)}, u32[]{:S(2)}) %collective-permute-start.5) | collective-permute-done | bytes 131104 | tf_op jit(solution)/shard_map/ppermute | solution.py:52
  10.3 0.9 %shard_map.95 = (bf16[128,128]{1,0:T(8,128)(2,1)S(1)}, bf16[128,128]{1,0:T(8,128)(2,1)S(1)}, bf16[128,128]{1,0:T(8,128)(2,1)S(1)}, bf16[128,128]{1,0:T(8,128)(2,1)S(1)}) custom-call(bf16[128,512]{1,0:T(8,128)(2,1)S(1)} %copy-done.2, bf16[128,512]{1,0:T(8,128)(2,1)S(1)} %collective-permute-done.3.refs_1_, ...), custom_call_target="tpu_custom_call" | custom-call | flops 268435456 | bytes 2756608 | tf_op jit(solution)/shard_map/pallas_call | solution.py:29
  11.2 1.0 %collective-permute-done.refs_0_ = bf16[3,128,128]{2,1,0:T(8,128)(2,1)S(1)} collective-permute-done((bf16[3,128,128]{2,1,0:T(8,128)(2,1)}, bf16[3,128,128]{2,1,0:T(8,128)(2,1)S(1)}, u32[]{:S(2)}, u32[]{:S(2)}) %collective-permute-start) | collective-permute-done | bytes 98336 | tf_op jit(solution)/shard_map/ppermute | solution.py:75
  12.2 1.8 %collective-permute-done.1.refs_1_ = bf16[3,128,128]{2,1,0:T(8,128)(2,1)S(1)} collective-permute-done((bf16[3,128,128]{2,1,0:T(8,128)(2,1)}, bf16[3,128,128]{2,1,0:T(8,128)(2,1)S(1)}, u32[]{:S(2)}, u32[]{:S(2)}) %collective-permute-start.1) | collective-permute-done | bytes 98336 | tf_op jit(solution)/shard_map/ppermute | solution.py:75
  14.0 0.0 collective-permute-done.2.refs_2_
  14.0 0.4 %shard_map.96 = (bf16[3,512,128]{2,1,0:T(8,128)(2,1)S(1)}, bf16[512,256]{1,0:T(8,128)(2,1)S(1)}, bf16[4,128,256]{2,1,0:T(8,128)(2,1)S(1)}, bf16[128,256]{1,0:T(8,128)(2,1)S(1)}) custom-call(bf16[3,128,128]{2,1,0:T(8,128)(2,1)S(1)} %collective-permute-done.refs_0_, bf16[3,128,128]{2,1,0:T(8,128)(2,1)S(1)} %collective-permute-done.1.refs_1_, ...), custom_call_target="tpu_custom_call" | custom-call | flops 67108864 | bytes 1671168 | tf_op jit(solution)/shard_map/pallas_call | solution.py:29
  14.4 4.5 %collective-permute-start.9 = (bf16[128,256]{1,0:T(8,128)(2,1)S(1)}, bf16[128,256]{1,0:T(8,128)(2,1)S(1)}, u32[]{:S(2)}, u32[]{:S(2)}) collective-permute-start(bf16[128,256]{1,0:T(8,128)(2,1)S(1)} %get-tuple-element.49), channel_id=1, source_target_pairs={{0,16},{4,20},{8,24},{12,28},{1,17},{5,21},{9,25},{13,29},{2,18},{... | collective-permute-start | bytes 196616 | tf_op jit(solution)/shard_map/ppermute | solution.py:87
  18.9 2.5 %collective-permute-start.6 = (bf16[128,128]{1,0:T(8,128)(2,1)S(1)}, bf16[128,128]{1,0:T(8,128)(2,1)S(1)}, u32[]{:S(2)}, u32[]{:S(2)}) collective-permute-start(bf16[128,128]{1,0:T(8,128)(2,1)S(1)} %get-tuple-element.45), channel_id=1, source_target_pairs={{0,12},{4,8},{8,4},{12,0},{16,28},{20,24},{24,20},{28,16},{1,13},{... | collective-permute-start | bytes 98312 | tf_op jit(solution)/shard_map/ppermute | solution.py:75
  21.5 0.4 %collective-permute-start.7 = (bf16[128,128]{1,0:T(8,128)(2,1)S(1)}, bf16[128,128]{1,0:T(8,128)(2,1)S(1)}, u32[]{:S(2)}, u32[]{:S(2)}) collective-permute-start(bf16[128,128]{1,0:T(8,128)(2,1)S(1)} %get-tuple-element.46), channel_id=1, source_target_pairs={{0,8},{4,12},{8,0},{12,4},{16,24},{20,28},{24,16},{28,20},{1,9},{5... | collective-permute-start | bytes 98312 | tf_op jit(solution)/shard_map/ppermute | solution.py:75
  21.9 0.6 %collective-permute-start.8 = (bf16[128,128]{1,0:T(8,128)(2,1)S(1)}, bf16[128,128]{1,0:T(8,128)(2,1)S(1)}, u32[]{:S(2)}, u32[]{:S(2)}) collective-permute-start(bf16[128,128]{1,0:T(8,128)(2,1)S(1)} %get-tuple-element.47), channel_id=1, source_target_pairs={{0,4},{4,0},{8,12},{12,8},{16,20},{20,16},{24,28},{28,24},{1,5},{5... | collective-permute-start | bytes 98312 | tf_op jit(solution)/shard_map/ppermute | solution.py:75
  22.5 0.8 %shard_map.97 = (bf16[512,256]{1,0:T(8,128)(2,1)S(1)}, bf16[4,128,128]{2,1,0:T(8,128)(2,1)S(1)}, f32[512,128]{1,0:T(8,128)S(1)}) custom-call(bf16[3,512,128]{2,1,0:T(8,128)(2,1)S(1)} %get-tuple-element.40.qkv_ref, bf16[4,128,256]{2,1,0:T(8,128)(2,1)S(1)} %copy-done.1, bf16[512,256]{1,0:T(8,128)(2,1)S(1)} %get-tuple-element.41.kf_ref, ...), custom_call_target="tpu_custom_call" | custom-call | flops 134217728 | bytes 1835008 | tf_op jit(solution)/shard_map/pallas_call | solution.py:29
  23.3 0.8 %collective-permute-done.6.refs_0_ = bf16[128,128]{1,0:T(8,128)(2,1)S(1)} collective-permute-done((bf16[128,128]{1,0:T(8,128)(2,1)S(1)}, bf16[128,128]{1,0:T(8,128)(2,1)S(1)}, u32[]{:S(2)}, u32[]{:S(2)}) %collective-permute-start.6) | collective-permute-done | bytes 32800 | tf_op jit(solution)/shard_map/ppermute | solution.py:75
  24.1 1.3 %collective-permute-done.7.refs_1_ = bf16[128,128]{1,0:T(8,128)(2,1)S(1)} collective-permute-done((bf16[128,128]{1,0:T(8,128)(2,1)S(1)}, bf16[128,128]{1,0:T(8,128)(2,1)S(1)}, u32[]{:S(2)}, u32[]{:S(2)}) %collective-permute-start.7) | collective-permute-done | bytes 32800 | tf_op jit(solution)/shard_map/ppermute | solution.py:75
  25.4 0.4 %collective-permute-done.8.refs_2_ = bf16[128,128]{1,0:T(8,128)(2,1)S(1)} collective-permute-done((bf16[128,128]{1,0:T(8,128)(2,1)S(1)}, bf16[128,128]{1,0:T(8,128)(2,1)S(1)}, u32[]{:S(2)}, u32[]{:S(2)}) %collective-permute-start.8) | collective-permute-done | bytes 32800 | tf_op jit(solution)/shard_map/ppermute | solution.py:75
  25.8 0.0 collective-permute-done.9.refs_6_.carried_ref
  25.8 0.8 %shard_map.98 = (bf16[512,128]{1,0:T(8,128)(2,1)S(1)}, bf16[4,128,256]{2,1,0:T(8,128)(2,1)S(1)}, bf16[128,256]{1,0:T(8,128)(2,1)S(1)}, bf16[128,128]{1,0:T(8,128...) custom-call(bf16[128,128]{1,0:T(8,128)(2,1)S(1)} %collective-permute-done.6.ref, ...), custom_call_target="tpu_custom_call" | custom-call | flops 67108864 | bytes 1310720 | tf_op jit(solution)/shard_map/pallas_call | solution.py:29
  26.6 1.3 %collective-permute-start.10 = (bf16[128,256]{1,0:T(8,128)(2,1)S(1)}, bf16[128,256]{1,0:T(8,128)(2,1)S(1)}, u32[]{:S(2)}, u32[]{:S(2)}) collective-permute-start(bf16[128,256]{1,0:T(8,128)(2,1)S(1)} %get-tuple-element.55), channel_id=1, source_target_pairs={{16,0},{20,4},{24,8},{28,12},{17,1},{21,5},{25,9},{29,13},{18,2},{... | collective-permute-start | bytes 196616 | tf_op jit(solution)/shard_map/ppermute | solution.py:87
  27.9 1.6 %collective-permute-start.14 = (bf16[128,128]{1,0:T(8,128)(2,1)S(1)}, bf16[128,128]{1,0:T(8,128)(2,1)S(1)}, u32[]{:S(2)}, u32[]{:S(2)}) collective-permute-start(bf16[128,128]{1,0:T(8,128)(2,1)S(1)} %get-tuple-element.60), channel_id=1, source_target_pairs={{0,12},{4,8},{8,4},{12,0},{16,28},{20,24},{24,20},{28,16},{1,13},{... | collective-permute-start | bytes 98312 | tf_op jit(solution)/shard_map/ppermute | solution.py:75
  29.5 0.5 %collective-permute-start.15 = (bf16[128,128]{1,0:T(8,128)(2,1)S(1)}, bf16[128,128]{1,0:T(8,128)(2,1)S(1)}, u32[]{:S(2)}, u32[]{:S(2)}) collective-permute-start(bf16[128,128]{1,0:T(8,128)(2,1)S(1)} %get-tuple-element.61), channel_id=1, source_target_pairs={{0,8},{4,12},{8,0},{12,4},{16,24},{20,28},{24,16},{28,20},{1,9},{5... | collective-permute-start | bytes 98312 | tf_op jit(solution)/shard_map/ppermute | solution.py:75
  30.0 1.5 %collective-permute-start.16 = (bf16[128,128]{1,0:T(8,128)(2,1)S(1)}, bf16[128,128]{1,0:T(8,128)(2,1)S(1)}, u32[]{:S(2)}, u32[]{:S(2)}) collective-permute-start(bf16[128,128]{1,0:T(8,128)(2,1)S(1)} %get-tuple-element.62), channel_id=1, source_target_pairs={{0,4},{4,0},{8,12},{12,8},{16,20},{20,16},{24,28},{28,24},{1,5},{5... | collective-permute-start | bytes 98312 | tf_op jit(solution)/shard_map/ppermute | solution.py:75
  31.5 1.5 %shard_map.99 = (bf16[512,128]{1,0:T(8,128)(2,1)S(1)}, f32[512,128]{1,0:T(8,128)S(1)}, f32[512,256]{1,0:T(8,128)S(1)}) custom-call(bf16[3,512,128]{2,1,0:T(8,128)(2,1)S(1)} %get-tuple-element.40.qkv_ref, bf16[4,128,256]{2,1,0:T(8,128)(2,1)S(1)} %copy-done.1, bf16[512,256]{1,0:T(8,128)(2,1)S(1)} %get-tuple-element.41.kf_ref, ...), custom_call_target="tpu_custom_call" | custom-call | flops 268435456 | bytes 2949120 | tf_op jit(solution)/shard_map/pallas_call | solution.py:29
  33.0 0.8 %collective-permute-done.10.after_ref = bf16[128,256]{1,0:T(8,128)(2,1)S(1)} collective-permute-done((bf16[128,256]{1,0:T(8,128)(2,1)S(1)}, bf16[128,256]{1,0:T(8,128)(2,1)S(1)}, u32[]{:S(2)}, u32[]{:S(2)}) %collective-permute-start.10) | collective-permute-done | bytes 65568 | tf_op jit(solution)/shard_map/ppermute | solution.py:87
  33.7 0.6 %shard_map.100 = (bf16[3,128,128]{2,1,0:T(8,128)(2,1)S(1)}, bf16[3,128,128]{2,1,0:T(8,128)(2,1)S(1)}, bf16[3,128,128]{2,1,0:T(8,128)(2,1)S(1)}, bf16[3,128,128]{2,1,0:T(8,128)(2,1)S(1)}) custom-call(bf16[3,512,128]{2,1,0:T(8,128)(2,1)S(1)} %get-tuple-element.40.qkv_ref, bf16[4,128,256]{2,1,0:T(8,128)(2,1)S(1)} %copy-done.1, ...), custom_call_target="tpu_custom_call" | custom-call | flops 100663296 | bytes 2293760 | tf_op jit(solution)/shard_map/pallas_call | solution.py:29
  34.3 0.0 collective-permute-done.14.refs_0_
  34.3 0.0 collective-permute-done.16.refs_2_
  34.3 0.5 %shard_map.101 = (bf16[2,128,512]{2,1,0:T(8,128)(2,1)S(1)}, bf16[2,128,512]{2,1,0:T(8,128)(2,1)S(1)}) custom-call(bf16[128,128]{1,0:T(8,128)(2,1)S(1)} %collective-permute-done.14.refs_0_, bf16[128,128]{1,0:T(8,128)(2,1)S(1)} %collective-permute-done.15.refs_1_, bf16[128,128]{1,0:T(8,128)(2,1)S(1)} %collective-permute-done.16.refs_2_, ...), custom_call_target="tpu_custom_call" | custom-call | flops 268435456 | bytes 2850816 | tf_op jit(solution)/shard_map/pallas_call | solution.py:29
  34.8 0.1 collective-permute-start.17
  34.9 2.1 %collective-permute-start.11 = (bf16[3,128,128]{2,1,0:T(8,128)(2,1)S(1)}, bf16[3,128,128]{2,1,0:T(8,128)(2,1)S(1)}, u32[]{:S(2)}, u32[]{:S(2)}) collective-permute-start(bf16[3,128,128]{2,1,0:T(8,128)(2,1)S(1)} %get-tuple-element.56), channel_id=1, source_target_pairs={{0,12},{4,8},{8,4},{12,0},{16,28},{20,24},{24,20},{28,16},{1,13},{... | collective-permute-start | bytes 294920 | tf_op jit(solution)/shard_map/ppermute | solution.py:75
  37.0 0.5 %collective-permute-start.12 = (bf16[3,128,128]{2,1,0:T(8,128)(2,1)S(1)}, bf16[3,128,128]{2,1,0:T(8,128)(2,1)S(1)}, u32[]{:S(2)}, u32[]{:S(2)}) collective-permute-start(bf16[3,128,128]{2,1,0:T(8,128)(2,1)S(1)} %get-tuple-element.57), channel_id=1, source_target_pairs={{0,8},{4,12},{8,0},{12,4},{16,24},{20,28},{24,16},{28,20},{1,9},{5... | collective-permute-start | bytes 294920 | tf_op jit(solution)/shard_map/ppermute | solution.py:75
  37.4 1.0 %collective-permute-start.13 = (bf16[3,128,128]{2,1,0:T(8,128)(2,1)S(1)}, bf16[3,128,128]{2,1,0:T(8,128)(2,1)S(1)}, u32[]{:S(2)}, u32[]{:S(2)}) collective-permute-start(bf16[3,128,128]{2,1,0:T(8,128)(2,1)S(1)} %get-tuple-element.58), channel_id=1, source_target_pairs={{0,4},{4,0},{8,12},{12,8},{16,20},{20,16},{24,28},{28,24},{1,5},{5... | collective-permute-start | bytes 294920 | tf_op jit(solution)/shard_map/ppermute | solution.py:75
  38.4 0.0 collective-permute-done.17
  38.4 0.1 add_bitcast_fusion
  38.5 0.6 %collective-permute-start.18 = (bf16[1,128,512]{2,1,0:T(8,128)(2,1)S(1)}, bf16[1,128,512]{2,1,0:T(8,128)(2,1)S(1)}, u32[]{:S(2)}, u32[]{:S(2)}) collective-permute-start(bf16[1,128,512]{2,1,0:T(8,128)(2,1)S(1)} %fusion), channel_id=1, source_target_pairs={{0,2},{1,3},{2,0},{3,1},{4,6},{5,7},{6,4},{7,5},{8,10},{9,11},{10,... | collective-permute-start | bytes 393224 | tf_op jit(solution)/shard_map/ppermute | solution.py:52
  39.1 2.3 %collective-permute-done.11.refs_0_ = bf16[3,128,128]{2,1,0:T(8,128)(2,1)S(1)} collective-permute-done((bf16[3,128,128]{2,1,0:T(8,128)(2,1)S(1)}, bf16[3,128,128]{2,1,0:T(8,128)(2,1)S(1)}, u32[]{:S(2)}, u32[]{:S(2)}) %collective-permute-start.11) | collective-permute-done | bytes 98336 | tf_op jit(solution)/shard_map/ppermute | solution.py:75
  41.4 1.2 %collective-permute-done.12.refs_1_ = bf16[3,128,128]{2,1,0:T(8,128)(2,1)S(1)} collective-permute-done((bf16[3,128,128]{2,1,0:T(8,128)(2,1)S(1)}, bf16[3,128,128]{2,1,0:T(8,128)(2,1)S(1)}, u32[]{:S(2)}, u32[]{:S(2)}) %collective-permute-start.12) | collective-permute-done | bytes 98336 | tf_op jit(solution)/shard_map/ppermute | solution.py:75
  42.7 0.4 collective-permute-done.13.refs_2_
  43.1 0.5 %collective-permute-done.18 = bf16[1,128,512]{2,1,0:T(8,128)(2,1)S(1)} collective-permute-done((bf16[1,128,512]{2,1,0:T(8,128)(2,1)S(1)}, bf16[1,128,512]{2,1,0:T(8,128)(2,1)S(1)}, u32[]{:S(2)}, u32[]{:S(2)}) %collective-permute-start.18) | collective-permute-done | bytes 131104 | tf_op jit(solution)/shard_map/ppermute | solution.py:52
  43.6 0.9 %shard_map.102 = (bf16[128,512]{1,0:T(8,128)(2,1)}, bf16[128,512]{1,0:T(8,128)(2,1)}, bf16[128,512]{1,0:T(8,128)(2,1)}, bf16[128,512]{1,0:T(8,128)(2,1)}) custom-call(bf16[3,128,128]{2,1,0:T(8,128)(2,1)S(1)} %collective-permute-done.11.refs_0_, bf16[3,128,128]{2,1,0:T(8,128)(2,1)S(1)} %collective-permute-done.12.refs_1_, ...), custom_call_target="tpu_custom_call" | custom-call | bytes 1310720 | tf_op jit(solution)/shard_map/pallas_call | solution.py:29
  (11 shorter events, 0.1 us)
Async XLA Ops:
  0.6 8.4 %collective-permute-start.3 = (bf16[128,512]{1,0:T(8,128)(2,1)}, bf16[128,512]{1,0:T(8,128)(2,1)S(1)}, u32[]{:S(2)}, u32[]{:S(2)}) collective-permute-start(bf16[128,512]{1,0:T(8,128)(2,1)} %refs_0_.1), channel_id=1, source_target_pairs={{0,2},{1,3},{2,0},{3,1},{4,6},{5,7},{6,4},{7,5},{8,10},{9,11},{10,... | collective-permute-start | bytes 393224 | tf_op jit(solution)/shard_map/ppermute | solution.py:52
  3.6 5.4 %collective-permute-start.4 = (bf16[128,512]{1,0:T(8,128)(2,1)}, bf16[128,512]{1,0:T(8,128)(2,1)S(1)}, u32[]{:S(2)}, u32[]{:S(2)}) collective-permute-start(bf16[128,512]{1,0:T(8,128)(2,1)} %refs_0_.1), channel_id=1, source_target_pairs={{0,1},{1,0},{2,3},{3,2},{4,5},{5,4},{6,7},{7,6},{8,9},{9,8},{10,11... | collective-permute-start | bytes 393224 | tf_op jit(solution)/shard_map/ppermute | solution.py:52
  5.4 6.8 %collective-permute-start = (bf16[3,128,128]{2,1,0:T(8,128)(2,1)}, bf16[3,128,128]{2,1,0:T(8,128)(2,1)S(1)}, u32[]{:S(2)}, u32[]{:S(2)}) collective-permute-start(bf16[3,128,128]{2,1,0:T(8,128)(2,1)} %get-tuple-element.35), channel_id=1, source_target_pairs={{0,12},{4,8},{8,4},{12,0},{16,28},{20,24},{24,20},{28,16},{1,13},{... | collective-permute-start | bytes 294920 | tf_op jit(solution)/shard_map/ppermute | solution.py:75
  8.0 5.9 %collective-permute-start.1 = (bf16[3,128,128]{2,1,0:T(8,128)(2,1)}, bf16[3,128,128]{2,1,0:T(8,128)(2,1)S(1)}, u32[]{:S(2)}, u32[]{:S(2)}) collective-permute-start(bf16[3,128,128]{2,1,0:T(8,128)(2,1)} %get-tuple-element.36), channel_id=1, source_target_pairs={{0,8},{4,12},{8,0},{12,4},{16,24},{20,28},{24,16},{28,20},{1,9},{5... | collective-permute-start | bytes 294920 | tf_op jit(solution)/shard_map/ppermute | solution.py:75
  8.5 1.9 %copy-start = (bf16[512,2048]{1,0:T(8,128)(2,1)S(1)}, bf16[512,2048]{1,0:T(8,128)(2,1)}, u32[]{:S(2)}) copy-start(bf16[512,2048]{1,0:T(8,128)(2,1)} %refs_4_.5) | copy-start | bytes 6291460
  8.5 1.9 %copy-start.2 = (bf16[128,512]{1,0:T(8,128)(2,1)S(1)}, bf16[128,512]{1,0:T(8,128)(2,1)}, u32[]{:S(2)}) copy-start(bf16[128,512]{1,0:T(8,128)(2,1)} %refs_0_.1) | copy-start | bytes 393220
  8.5 5.5 %collective-permute-start.2 = (bf16[3,128,128]{2,1,0:T(8,128)(2,1)}, bf16[3,128,128]{2,1,0:T(8,128)(2,1)S(1)}, u32[]{:S(2)}, u32[]{:S(2)}) collective-permute-start(bf16[3,128,128]{2,1,0:T(8,128)(2,1)} %get-tuple-element.37), channel_id=1, source_target_pairs={{0,4},{4,0},{8,12},{12,8},{16,20},{20,16},{24,28},{28,24},{1,5},{5... | collective-permute-start | bytes 294920 | tf_op jit(solution)/shard_map/ppermute | solution.py:75
  9.0 1.3 %collective-permute-start.5 = (bf16[128,512]{1,0:T(8,128)(2,1)S(1)}, bf16[128,512]{1,0:T(8,128)(2,1)S(1)}, u32[]{:S(2)}, u32[]{:S(2)}) collective-permute-start(bf16[128,512]{1,0:T(8,128)(2,1)S(1)} %collective-permute-done.3.refs_1_), channel_id=1, source_target_pairs={{0,1},{1,0},{2,3},{3,2},{4,5},{5,4},{6,7},{7,6},{8,9},{9,8},{10,11... | collective-permute-start | bytes 393224 | tf_op jit(solution)/shard_map/ppermute | solution.py:52
  9.0 5.0 %copy-start.1 = (bf16[4,128,256]{2,1,0:T(8,128)(2,1)S(1)}, bf16[4,128,256]{2,1,0:T(8,128)(2,1)}, u32[]{:S(2)}) copy-start(bf16[4,128,256]{2,1,0:T(8,128)(2,1)} %om_ref.5) | copy-start | bytes 786436
  9.0 5.0 %copy-start.3 = (bf16[3,128,128]{2,1,0:T(8,128)(2,1)S(1)}, bf16[3,128,128]{2,1,0:T(8,128)(2,1)}, u32[]{:S(2)}) copy-start(bf16[3,128,128]{2,1,0:T(8,128)(2,1)} %get-tuple-element.38.refs_3_) | copy-start | bytes 294916
  14.4 11.4 %collective-permute-start.9 = (bf16[128,256]{1,0:T(8,128)(2,1)S(1)}, bf16[128,256]{1,0:T(8,128)(2,1)S(1)}, u32[]{:S(2)}, u32[]{:S(2)}) collective-permute-start(bf16[128,256]{1,0:T(8,128)(2,1)S(1)} %get-tuple-element.49), channel_id=1, source_target_pairs={{0,16},{4,20},{8,24},{12,28},{1,17},{5,21},{9,25},{13,29},{2,18},{... | collective-permute-start | bytes 196616 | tf_op jit(solution)/shard_map/ppermute | solution.py:87
  18.9 5.1 %collective-permute-start.6 = (bf16[128,128]{1,0:T(8,128)(2,1)S(1)}, bf16[128,128]{1,0:T(8,128)(2,1)S(1)}, u32[]{:S(2)}, u32[]{:S(2)}) collective-permute-start(bf16[128,128]{1,0:T(8,128)(2,1)S(1)} %get-tuple-element.45), channel_id=1, source_target_pairs={{0,12},{4,8},{8,4},{12,0},{16,28},{20,24},{24,20},{28,16},{1,13},{... | collective-permute-start | bytes 98312 | tf_op jit(solution)/shard_map/ppermute | solution.py:75
  21.5 3.9 %collective-permute-start.7 = (bf16[128,128]{1,0:T(8,128)(2,1)S(1)}, bf16[128,128]{1,0:T(8,128)(2,1)S(1)}, u32[]{:S(2)}, u32[]{:S(2)}) collective-permute-start(bf16[128,128]{1,0:T(8,128)(2,1)S(1)} %get-tuple-element.46), channel_id=1, source_target_pairs={{0,8},{4,12},{8,0},{12,4},{16,24},{20,28},{24,16},{28,20},{1,9},{5... | collective-permute-start | bytes 98312 | tf_op jit(solution)/shard_map/ppermute | solution.py:75
  21.9 3.9 %collective-permute-start.8 = (bf16[128,128]{1,0:T(8,128)(2,1)S(1)}, bf16[128,128]{1,0:T(8,128)(2,1)S(1)}, u32[]{:S(2)}, u32[]{:S(2)}) collective-permute-start(bf16[128,128]{1,0:T(8,128)(2,1)S(1)} %get-tuple-element.47), channel_id=1, source_target_pairs={{0,4},{4,0},{8,12},{12,8},{16,20},{20,16},{24,28},{28,24},{1,5},{5... | collective-permute-start | bytes 98312 | tf_op jit(solution)/shard_map/ppermute | solution.py:75
  26.6 7.1 %collective-permute-start.10 = (bf16[128,256]{1,0:T(8,128)(2,1)S(1)}, bf16[128,256]{1,0:T(8,128)(2,1)S(1)}, u32[]{:S(2)}, u32[]{:S(2)}) collective-permute-start(bf16[128,256]{1,0:T(8,128)(2,1)S(1)} %get-tuple-element.55), channel_id=1, source_target_pairs={{16,0},{20,4},{24,8},{28,12},{17,1},{21,5},{25,9},{29,13},{18,2},{... | collective-permute-start | bytes 196616 | tf_op jit(solution)/shard_map/ppermute | solution.py:87
  27.9 6.4 %collective-permute-start.14 = (bf16[128,128]{1,0:T(8,128)(2,1)S(1)}, bf16[128,128]{1,0:T(8,128)(2,1)S(1)}, u32[]{:S(2)}, u32[]{:S(2)}) collective-permute-start(bf16[128,128]{1,0:T(8,128)(2,1)S(1)} %get-tuple-element.60), channel_id=1, source_target_pairs={{0,12},{4,8},{8,4},{12,0},{16,28},{20,24},{24,20},{28,16},{1,13},{... | collective-permute-start | bytes 98312 | tf_op jit(solution)/shard_map/ppermute | solution.py:75
  29.5 4.7 %collective-permute-start.15 = (bf16[128,128]{1,0:T(8,128)(2,1)S(1)}, bf16[128,128]{1,0:T(8,128)(2,1)S(1)}, u32[]{:S(2)}, u32[]{:S(2)}) collective-permute-start(bf16[128,128]{1,0:T(8,128)(2,1)S(1)} %get-tuple-element.61), channel_id=1, source_target_pairs={{0,8},{4,12},{8,0},{12,4},{16,24},{20,28},{24,16},{28,20},{1,9},{5... | collective-permute-start | bytes 98312 | tf_op jit(solution)/shard_map/ppermute | solution.py:75
  30.0 4.3 %collective-permute-start.16 = (bf16[128,128]{1,0:T(8,128)(2,1)S(1)}, bf16[128,128]{1,0:T(8,128)(2,1)S(1)}, u32[]{:S(2)}, u32[]{:S(2)}) collective-permute-start(bf16[128,128]{1,0:T(8,128)(2,1)S(1)} %get-tuple-element.62), channel_id=1, source_target_pairs={{0,4},{4,0},{8,12},{12,8},{16,20},{20,16},{24,28},{28,24},{1,5},{5... | collective-permute-start | bytes 98312 | tf_op jit(solution)/shard_map/ppermute | solution.py:75
  34.8 3.6 %collective-permute-start.17 = (bf16[2,128,512]{2,1,0:T(8,128)(2,1)S(1)}, bf16[2,128,512]{2,1,0:T(8,128)(2,1)S(1)}, u32[]{:S(2)}, u32[]{:S(2)}) collective-permute-start(bf16[2,128,512]{2,1,0:T(8,128)(2,1)S(1)} %get-tuple-element.65), channel_id=1, source_target_pairs={{0,1},{1,0},{2,3},{3,2},{4,5},{5,4},{6,7},{7,6},{8,9},{9,8},{10,11... | collective-permute-start | bytes 786440 | tf_op jit(solution)/shard_map/ppermute | solution.py:52
  34.9 6.6 %collective-permute-start.11 = (bf16[3,128,128]{2,1,0:T(8,128)(2,1)S(1)}, bf16[3,128,128]{2,1,0:T(8,128)(2,1)S(1)}, u32[]{:S(2)}, u32[]{:S(2)}) collective-permute-start(bf16[3,128,128]{2,1,0:T(8,128)(2,1)S(1)} %get-tuple-element.56), channel_id=1, source_target_pairs={{0,12},{4,8},{8,4},{12,0},{16,28},{20,24},{24,20},{28,16},{1,13},{... | collective-permute-start | bytes 294920 | tf_op jit(solution)/shard_map/ppermute | solution.py:75
  37.0 5.7 %collective-permute-start.12 = (bf16[3,128,128]{2,1,0:T(8,128)(2,1)S(1)}, bf16[3,128,128]{2,1,0:T(8,128)(2,1)S(1)}, u32[]{:S(2)}, u32[]{:S(2)}) collective-permute-start(bf16[3,128,128]{2,1,0:T(8,128)(2,1)S(1)} %get-tuple-element.57), channel_id=1, source_target_pairs={{0,8},{4,12},{8,0},{12,4},{16,24},{20,28},{24,16},{28,20},{1,9},{5... | collective-permute-start | bytes 294920 | tf_op jit(solution)/shard_map/ppermute | solution.py:75
  37.4 5.6 %collective-permute-start.13 = (bf16[3,128,128]{2,1,0:T(8,128)(2,1)S(1)}, bf16[3,128,128]{2,1,0:T(8,128)(2,1)S(1)}, u32[]{:S(2)}, u32[]{:S(2)}) collective-permute-start(bf16[3,128,128]{2,1,0:T(8,128)(2,1)S(1)} %get-tuple-element.58), channel_id=1, source_target_pairs={{0,4},{4,0},{8,12},{12,8},{16,20},{20,16},{24,28},{28,24},{1,5},{5... | collective-permute-start | bytes 294920 | tf_op jit(solution)/shard_map/ppermute | solution.py:75
  38.5 5.1 %collective-permute-start.18 = (bf16[1,128,512]{2,1,0:T(8,128)(2,1)S(1)}, bf16[1,128,512]{2,1,0:T(8,128)(2,1)S(1)}, u32[]{:S(2)}, u32[]{:S(2)}) collective-permute-start(bf16[1,128,512]{2,1,0:T(8,128)(2,1)S(1)} %fusion), channel_id=1, source_target_pairs={{0,2},{1,3},{2,0},{3,1},{4,6},{5,7},{6,4},{7,5},{8,10},{9,11},{10,... | collective-permute-start | bytes 393224 | tf_op jit(solution)/shard_map/ppermute | solution.py:52

commit v8 on v7

--- a/solution.py
+++ b/solution.py
@@ -70,25 +70,26 @@
 
 
 def exchange(parts):
-    n, size = len(parts), lax.axis_size("seq")
-    return [
-        lax.ppermute(parts[k], "seq", [(i, i ^ k) for i in range(size)])
-        for k in reversed(range(1, n))
-    ] + [parts[0]]
-
-
-def from_groups(total, n, forward):
-    size, step, exclusive = lax.axis_size("seq"), n, None
-    inclusive = total.astype(jnp.float32)
+    return [swap(part, "seq", k) for k, part in enumerate(parts, 1)][::-1]
+
+
+def swap_totals(total, n):
+    size, step, got = lax.axis_size("seq"), n, []
     while step < size:
-        pairs = [(i, i + step) for i in range(size - step)]
-        if not forward:
-            pairs = [(b, a) for a, b in pairs]
-        got = lax.ppermute(bf(inclusive), "seq", pairs).astype(jnp.float32)
-        exclusive = got if exclusive is None else exclusive + got
-        inclusive = inclusive + got
+        got.append(swap(bf(total), "seq", step))
+        total = total.astype(jnp.float32) + got[-1].astype(jnp.float32)
         step *= 2
-    return jnp.zeros_like(total) if exclusive is None else bf(exclusive)
+    return got
+
+
+def sum_of_side(refs, n, earlier):
+    group = lax.div(lax.axis_index("seq"), n)
+    total = jnp.zeros(refs[0].shape, jnp.float32)
+    for at, ref in enumerate(refs):
+        from_earlier = lax.rem(lax.shift_right_logical(group, at), 2) == 1
+        keep = from_earlier if earlier else jnp.logical_not(from_earlier)
+        total = total + jnp.where(keep, ref[...].astype(jnp.float32), 0.0)
+    return bf(total)
 
 
 def lane(index, width):
@@ -96,14 +97,13 @@
 
 
 def pack_kernel(n, q_ref, k_ref, v_ref, *rest):
-    outs, sems = rest[:n], rest[n]
+    outs, sems = rest[:-1], rest[-1]
     r = member(n)
     dim = outs[0].shape[2]
     copies = []
-    for k in range(n):
-        cols = lane(r ^ k, dim)
+    for k, out in enumerate(outs, 1):
         for at, ref in enumerate((q_ref, k_ref, v_ref)):
-            copies.append((ref.at[:, cols], outs[k].at[at]))
+            copies.append((ref.at[:, lane(r ^ k, dim)], out.at[at]))
     started = [pltpu.make_async_copy(a, b, sems.at[i]) for i, (a, b) in enumerate(copies)]
     for copy in started:
         copy.start()
@@ -130,14 +130,18 @@
 
 
 def first_kernel(n, *refs):
-    got, om_ref = refs[:n][::-1], refs[n]
-    qkv_ref, kf_ref, state_ref, total_ref = refs[n + 2 :]
+    got, own, om_ref = refs[: n - 1][::-1], refs[n - 1 : n + 2], refs[n + 2]
+    qkv_ref, kf_ref, state_ref, total_ref = refs[n + 4 :]
     r = member(n)
-    rows, dim = got[0].shape[1:]
+    rows, dim = own[0].shape[0], om_ref.shape[1]
     scale = dim ** (-0.25)
     for k in range(n):
         at = pl.ds(pl.multiple_of((r ^ k) * rows, 128), rows)
-        qkv_ref[:, at, :] = got[k][...]
+        if k:
+            qkv_ref[:, at, :] = got[k - 1][...]
+        else:
+            for i, ref in enumerate(own):
+                qkv_ref[i, at, :] = ref[:, lane(r, dim)]
     k_all = qkv_ref[1]
     wide = k_all.astype(jnp.float32)
     half_sq = jnp.sum(wide * wide, axis=1, keepdims=True) * (scale * scale * 0.5)
@@ -166,9 +170,9 @@
 
 
 def turn_kernel(n, *refs):
-    gm_in, (qf_ref, num_ref, carried_ref) = refs[:n][::-1], refs[n : n + 3]
-    gn_ref, state_ref, total_ref = refs[n + 3 : n + 6]
-    outs, scr = refs[n + 6 : -1], refs[-1]
+    gm_in, (qf_ref, num_ref), earlier = refs[:n][::-1], refs[n : n + 2], refs[n + 2 : -n - 5]
+    carried_ref, gn_ref, state_ref, total_ref = refs[-n - 5 : -n - 1]
+    outs, scr = refs[-n - 1 : -1], refs[-1]
     r = member(n)
     rows = gm_in[0].shape[0]
     places = [
@@ -176,7 +180,9 @@
     ]
     for k in range(n):
         scr[places[k], :] = gm_in[k][...]
-    num = num_ref[...] + mm(qf_ref[...], carried_ref[...], NT)
+    carried = sum_of_side(earlier, n, True)
+    carried_ref[...] = carried
+    num = num_ref[...] + mm(qf_ref[...], carried, NT)
     inv = lax.rsqrt(jnp.mean(num * num, axis=1, keepdims=True) + EPSILON)
     normed = num * inv
     gm = scr[...].astype(jnp.float32)
@@ -212,12 +218,12 @@
         gkf_ref[at, :] = mm(gs, qf, TN) + mm(v, later)
 
 
-def end_kernel(n, qkv_ref, om_ref, kf_ref, gq_ref, gv_ref, gkf_ref, after_ref, *rest):
-    outs, gk_scr, gv_scr = rest[:n], rest[n], rest[n + 1]
+def end_kernel(n, qkv_ref, om_ref, kf_ref, gq_ref, gv_ref, gkf_ref, *rest):
+    later, outs, (gk_scr, gv_scr) = rest[: -n - 2], rest[-n - 2 : -2], rest[-2:]
     r, dim = member(n), om_ref.shape[1]
     rows = outs[0].shape[1]
     scale = dim ** (-0.25)
-    kf, after = kf_ref[...], after_ref[...]
+    kf, after = kf_ref[...], sum_of_side(later, n, False)
     gv_scr[...] = bf(gv_ref[...] + mm(kf, after, NT))
     gkf = gkf_ref[...] + mm(qkv_ref[2], after)
     terms = bf(gkf * kf.astype(jnp.float32))
@@ -275,9 +281,9 @@
         offsets = offsets + [o ^ bit for o in offsets]
     sends = call(
         functools.partial(pack_kernel, n),
-        [struct((3, rows, dim))] * n,
+        [struct((3, rows, dim))] * (n - 1),
         queries, key_vectors, value_vectors,
-        specs=[ANY] * 3, scratch=[pltpu.SemaphoreType.DMA((3 * n,))], vmem=60,
+        specs=[ANY] * 3, scratch=[pltpu.SemaphoreType.DMA((3 * n - 3,))], vmem=60,
     )
     got = exchange(sends)
     (mark,) = call(mark_kernel, [struct((8, 128), f32)], blocks[offsets.index(1)], specs=[ANY], flops=10**10)
@@ -288,7 +294,7 @@
         specs=[VMEM] * (split + 1) + [ANY],
         scratch=[pltpu.VMEM((rows, n * dim), jnp.bfloat16)],
     )
-    gm_in = exchange(gm_parts)
+    gm_in = exchange(gm_parts[1:]) + [gm_parts[0]]
     qkv, kf, state, total = call(
         functools.partial(first_kernel, n),
         [
@@ -297,23 +303,29 @@
             struct((n, dim, feats)),
             struct((dim, feats)),
         ],
-        *got, feature_proj, gm_parts[0], flops=2 * macs, specs=[VMEM] * (n + 1) + [ANY],
-    )
-    carried = from_groups(total, n, True)
+        *got, queries, key_vectors, value_vectors, feature_proj, gm_parts[0],
+        flops=2 * macs, specs=[VMEM] * (n + 3) + [ANY],
+    )
+    earlier = swap_totals(total, n)
     qf, scores, num = call(
         functools.partial(inner_kernel, n),
         [struct((long, feats)), struct((n, rows, rows)), struct((long, dim), f32)],
         qkv, feature_proj, kf, state, flops=4 * macs,
     )
-    gn, later, later_total, *mixed_parts = call(
+    carried, gn, later, later_total, *mixed_parts = call(
         functools.partial(turn_kernel, n),
-        [struct((long, dim)), struct((n, dim, feats)), struct((dim, feats))]
+        [
+            struct((dim, feats)),
+            struct((long, dim)),
+            struct((n, dim, feats)),
+            struct((dim, feats)),
+        ]
         + [struct((rows, dim))] * n,
-        *gm_in, qf, num, carried, flops=2 * macs,
+        *gm_in, qf, num, *earlier, flops=2 * macs,
         scratch=[pltpu.VMEM((long, dim), jnp.bfloat16)],
     )
-    after_b = from_groups(later_total, n, False)
-    mixed_in = exchange(mixed_parts)
+    after = swap_totals(later_total, n)
+    mixed_in = exchange(mixed_parts[1:]) + [mixed_parts[0]]
     gq, gv_part, gkf_part = call(
         functools.partial(back_kernel, n),
         [struct((long, dim)), struct((long, dim), f32), struct((long, feats), f32)],
@@ -323,10 +335,10 @@
     grads = call(
         functools.partial(end_kernel, n),
         [struct((3, rows, dim))] * n,
-        qkv, feature_proj, kf, gq, gv_part, gkf_part, after_b, flops=3 * macs,
+        qkv, feature_proj, kf, gq, gv_part, gkf_part, *after, flops=3 * macs,
         scratch=[pltpu.VMEM((long, dim), jnp.bfloat16)] * 2,
     )
-    grads_in = exchange(grads)
+    grads_in = exchange(grads[1:]) + [grads[0]]
 
     order = [o for o in range(split) if not o & 1] + [o for o in range(split) if o & 1]
     own, sent = call(

time: 44.7 us -> 41.3 us (0.924)
  starting transfers between devices: 23.7 us -> 20.8 us
  waiting for transfers between devices: 11.9 us -> 11.4 us
    ppermute x14 -> x0, starting transfers between devices: 20 us -> none  [the longest x12 14.2 us: exchange(): lax.ppermute(parts[k], 'seq', [(i, i ^ k) for i in range(size)])]
    ppermute x5 -> x19, starting transfers between devices: 3.69 us -> 20.8 us  [swap(): return lax.ppermute(array, axis, [(i, i ^ bit) for i in range(size)])]
    ppermute x14 -> x0, waiting for transfers between devices: 10 us -> none  [the longest x12 9.26 us: exchange(): lax.ppermute(parts[k], 'seq', [(i, i ^ k) for i in range(size)])]
    ppermute x5 -> x19, waiting for transfers between devices: 1.83 us -> 11.4 us  [swap(): return lax.ppermute(array, axis, [(i, i ^ bit) for i in range(size)])]
  transfers between devices with their start and end apart: 19 -> 19, of which waited for: 11 -> 10; matrix products, arithmetic and copies ran while one was open for 0% -> 0% of each run, Pallas kernels for 12% -> 13%
where the time goes in v8:
time: 41.3 us; the launch traced here: 41.1 us
  starting transfers between devices  20.8 us (50%)
  waiting for transfers between devices  11.4 us (28%)
  Pallas kernels  7.94 us (19%)
  between operations  0.81 us (2%)
    ppermute x19, starting transfers between devices, swap(): return lax.ppermute(array, axis, [(i, i ^ bit) for i in range(size)])  20.8 us
    ppermute x19, waiting for transfers between devices, swap(): return lax.ppermute(array, axis, [(i, i ^ bit) for i in range(size)])  11.4 us
    pallas_call x10, Pallas kernels, call(): pl.pallas_call(body, out_shape=outs, in_specs=specs or [VMEM] * len(args)...  7.94 us
  transfers between devices with their start and end apart: 19, of which 10 were waited for; matrix products, arithmetic and copies ran while one was open for 0% of the time, Pallas kernels for 13%

profile of v8, /device:TPU:0, one launch (start us, length us, event | category | flops | bytes accessed | tf_op | source)
XLA Modules:
  0.0 41.1 jit_solution(14454632799102775929)
XLA Ops:
  0.6 3.0 %collective-permute-start.3 = (bf16[128,512]{1,0:T(8,128)(2,1)}, bf16[128,512]{1,0:T(8,128)(2,1)S(1)}, u32[]{:S(2)}, u32[]{:S(2)}) collective-permute-start(bf16[128,512]{1,0:T(8,128)(2,1)} %refs_0_.1), channel_id=1, source_target_pairs={{0,2},{1,3},{2,0},{3,1},{4,6},{5,7},{6,4},{7,5},{8,10},{9,11},{10,... | collective-permute-start | bytes 393224 | tf_op jit(solution)/shard_map/ppermute | solution.py:52
  3.6 0.0 collective-permute-start.4
  3.6 1.7 %shard_map.93 = (bf16[3,128,128]{2,1,0:T(8,128)(2,1)}, bf16[3,128,128]{2,1,0:T(8,128)(2,1)}, bf16[3,128,128]{2,1,0:T(8,128)(2,1)}) custom-call(bf16[128,512]{1,0:T(8,128)(2,1)} %refs_3_.1, bf16[128,512]{1,0:T(8,128)(2,1)} %refs_4_.4, bf16[128,512]{1,0:T(8,128)(2,1)} %refs_5_.1), custom_call_target="tpu_custom_call" | custom-call | bytes 688128 | tf_op jit(solution)/shard_map/pallas_call | solution.py:29
  5.3 2.6 %collective-permute-start = (bf16[3,128,128]{2,1,0:T(8,128)(2,1)}, bf16[3,128,128]{2,1,0:T(8,128)(2,1)S(1)}, u32[]{:S(2)}, u32[]{:S(2)}) collective-permute-start(bf16[3,128,128]{2,1,0:T(8,128)(2,1)} %get-tuple-element.35), channel_id=1, source_target_pairs={{0,12},{4,8},{8,4},{12,0},{16,28},{20,24},{24,20},{28,16},{1,13},{... | collective-permute-start | bytes 294920 | tf_op jit(solution)/shard_map/ppermute | solution.py:52
  7.9 0.4 %collective-permute-start.1 = (bf16[3,128,128]{2,1,0:T(8,128)(2,1)}, bf16[3,128,128]{2,1,0:T(8,128)(2,1)S(1)}, u32[]{:S(2)}, u32[]{:S(2)}) collective-permute-start(bf16[3,128,128]{2,1,0:T(8,128)(2,1)} %get-tuple-element.36), channel_id=1, source_target_pairs={{0,8},{4,12},{8,0},{12,4},{16,24},{20,28},{24,16},{28,20},{1,9},{5... | collective-permute-start | bytes 294920 | tf_op jit(solution)/shard_map/ppermute | solution.py:52
  8.4 0.5 %collective-permute-start.2 = (bf16[3,128,128]{2,1,0:T(8,128)(2,1)}, bf16[3,128,128]{2,1,0:T(8,128)(2,1)S(1)}, u32[]{:S(2)}, u32[]{:S(2)}) collective-permute-start(bf16[3,128,128]{2,1,0:T(8,128)(2,1)} %get-tuple-element.37), channel_id=1, source_target_pairs={{0,4},{4,0},{8,12},{12,8},{16,20},{20,16},{24,28},{28,24},{1,5},{5... | collective-permute-start | bytes 294920 | tf_op jit(solution)/shard_map/ppermute | solution.py:52
  8.9 0.0 collective-permute-done.3.refs_1_
  8.9 0.0 collective-permute-start.5
  8.9 0.0 collective-permute-done.4._.refs_2_
  8.9 0.0 copy-start.1
  8.9 0.0 copy-start.2
  8.9 0.0 copy-start.3
  8.9 0.0 copy-start.4
  8.9 1.3 %collective-permute-done.5.refs_3_ = bf16[128,512]{1,0:T(8,128)(2,1)S(1)} collective-permute-done((bf16[128,512]{1,0:T(8,128)(2,1)S(1)}, bf16[128,512]{1,0:T(8,128)(2,1)S(1)}, u32[]{:S(2)}, u32[]{:S(2)}) %collective-permute-start.5) | collective-permute-done | bytes 131104 | tf_op jit(solution)/shard_map/ppermute | solution.py:52
  10.2 0.9 %shard_map.95 = (bf16[128,128]{1,0:T(8,128)(2,1)S(1)}, bf16[128,128]{1,0:T(8,128)(2,1)S(1)}, bf16[128,128]{1,0:T(8,128)(2,1)S(1)}, bf16[128,128]{1,0:T(8,128)(2,1)S(1)}) custom-call(bf16[128,512]{1,0:T(8,128)(2,1)S(1)} %copy-done.5, bf16[128,512]{1,0:T(8,128)(2,1)S(1)} %collective-permute-done.3.refs_1_, ...), custom_call_target="tpu_custom_call" | custom-call | flops 268435456 | bytes 2756608 | tf_op jit(solution)/shard_map/pallas_call | solution.py:29
  11.1 1.0 %collective-permute-done.refs_0_ = bf16[3,128,128]{2,1,0:T(8,128)(2,1)S(1)} collective-permute-done((bf16[3,128,128]{2,1,0:T(8,128)(2,1)}, bf16[3,128,128]{2,1,0:T(8,128)(2,1)S(1)}, u32[]{:S(2)}, u32[]{:S(2)}) %collective-permute-start) | collective-permute-done | bytes 98336 | tf_op jit(solution)/shard_map/ppermute | solution.py:52
  12.1 1.8 %collective-permute-done.1.refs_1_ = bf16[3,128,128]{2,1,0:T(8,128)(2,1)S(1)} collective-permute-done((bf16[3,128,128]{2,1,0:T(8,128)(2,1)}, bf16[3,128,128]{2,1,0:T(8,128)(2,1)S(1)}, u32[]{:S(2)}, u32[]{:S(2)}) %collective-permute-start.1) | collective-permute-done | bytes 98336 | tf_op jit(solution)/shard_map/ppermute | solution.py:52
  13.9 0.0 collective-permute-done.2.refs_2_
  13.9 0.5 %shard_map.96 = (bf16[3,512,128]{2,1,0:T(8,128)(2,1)S(1)}, bf16[512,256]{1,0:T(8,128)(2,1)S(1)}, bf16[4,128,256]{2,1,0:T(8,128)(2,1)S(1)}, bf16[128,256]{1,0:T(8,128)(2,1)S(1)}) custom-call(bf16[3,128,128]{2,1,0:T(8,128)(2,1)S(1)} %collective-permute-done.refs_0_, bf16[3,128,128]{2,1,0:T(8,128)(2,1)S(1)} %collective-permute-done.1.refs_1_, ...), custom_call_target="tpu_custom_call" | custom-call | flops 67108864 | bytes 1966080 | tf_op jit(solution)/shard_map/pallas_call | solution.py:29
  14.4 2.7 %collective-permute-start.9 = (bf16[128,256]{1,0:T(8,128)(2,1)S(1)}, bf16[128,256]{1,0:T(8,128)(2,1)S(1)}, u32[]{:S(2)}, u32[]{:S(2)}) collective-permute-start(bf16[128,256]{1,0:T(8,128)(2,1)S(1)} %get-tuple-element.48), channel_id=1, source_target_pairs={{0,16},{4,20},{8,24},{12,28},{16,0},{20,4},{24,8},{28,12},{1,17},{... | collective-permute-start | bytes 196616 | tf_op jit(solution)/shard_map/ppermute | solution.py:52
  17.0 2.5 %collective-permute-start.6 = (bf16[128,128]{1,0:T(8,128)(2,1)S(1)}, bf16[128,128]{1,0:T(8,128)(2,1)S(1)}, u32[]{:S(2)}, u32[]{:S(2)}) collective-permute-start(bf16[128,128]{1,0:T(8,128)(2,1)S(1)} %get-tuple-element.44), channel_id=1, source_target_pairs={{0,12},{4,8},{8,4},{12,0},{16,28},{20,24},{24,20},{28,16},{1,13},{... | collective-permute-start | bytes 98312 | tf_op jit(solution)/shard_map/ppermute | solution.py:52
  19.5 0.4 %collective-permute-start.7 = (bf16[128,128]{1,0:T(8,128)(2,1)S(1)}, bf16[128,128]{1,0:T(8,128)(2,1)S(1)}, u32[]{:S(2)}, u32[]{:S(2)}) collective-permute-start(bf16[128,128]{1,0:T(8,128)(2,1)S(1)} %get-tuple-element.45), channel_id=1, source_target_pairs={{0,8},{4,12},{8,0},{12,4},{16,24},{20,28},{24,16},{28,20},{1,9},{5... | collective-permute-start | bytes 98312 | tf_op jit(solution)/shard_map/ppermute | solution.py:52
  19.9 0.6 %collective-permute-start.8 = (bf16[128,128]{1,0:T(8,128)(2,1)S(1)}, bf16[128,128]{1,0:T(8,128)(2,1)S(1)}, u32[]{:S(2)}, u32[]{:S(2)}) collective-permute-start(bf16[128,128]{1,0:T(8,128)(2,1)S(1)} %get-tuple-element.46), channel_id=1, source_target_pairs={{0,4},{4,0},{8,12},{12,8},{16,20},{20,16},{24,28},{28,24},{1,5},{5... | collective-permute-start | bytes 98312 | tf_op jit(solution)/shard_map/ppermute | solution.py:52
  20.5 0.8 %shard_map.97 = (bf16[512,256]{1,0:T(8,128)(2,1)S(1)}, bf16[4,128,128]{2,1,0:T(8,128)(2,1)S(1)}, f32[512,128]{1,0:T(8,128)S(1)}) custom-call(bf16[3,512,128]{2,1,0:T(8,128)(2,1)S(1)} %get-tuple-element.39.qkv_ref, bf16[4,128,256]{2,1,0:T(8,128)(2,1)S(1)} %copy-done.1, bf16[512,256]{1,0:T(8,128)(2,1)S(1)} %get-tuple-element.40.kf_ref, ...), custom_call_target="tpu_custom_call" | custom-call | flops 134217728 | bytes 1835008 | tf_op jit(solution)/shard_map/pallas_call | solution.py:29
  21.3 1.0 %collective-permute-done.6.refs_0_ = bf16[128,128]{1,0:T(8,128)(2,1)S(1)} collective-permute-done((bf16[128,128]{1,0:T(8,128)(2,1)S(1)}, bf16[128,128]{1,0:T(8,128)(2,1)S(1)}, u32[]{:S(2)}, u32[]{:S(2)}) %collective-permute-start.6) | collective-permute-done | bytes 32800 | tf_op jit(solution)/shard_map/ppermute | solution.py:52
  22.3 1.2 %collective-permute-done.7.refs_1_ = bf16[128,128]{1,0:T(8,128)(2,1)S(1)} collective-permute-done((bf16[128,128]{1,0:T(8,128)(2,1)S(1)}, bf16[128,128]{1,0:T(8,128)(2,1)S(1)}, u32[]{:S(2)}, u32[]{:S(2)}) %collective-permute-start.7) | collective-permute-done | bytes 32800 | tf_op jit(solution)/shard_map/ppermute | solution.py:52
  23.4 0.4 %collective-permute-done.8.refs_2_ = bf16[128,128]{1,0:T(8,128)(2,1)S(1)} collective-permute-done((bf16[128,128]{1,0:T(8,128)(2,1)S(1)}, bf16[128,128]{1,0:T(8,128)(2,1)S(1)}, u32[]{:S(2)}, u32[]{:S(2)}) %collective-permute-start.8) | collective-permute-done | bytes 32800 | tf_op jit(solution)/shard_map/ppermute | solution.py:52
  23.9 0.0 collective-permute-done.9.refs_6_
  23.9 0.8 %shard_map.98 = (bf16[128,256]{1,0:T(8,128)(2,1)S(1)}, bf16[512,128]{1,0:T(8,128)(2,1)S(1)}, bf16[4,128,256]{2,1,0:T(8,128)(2,1)S(1)}, bf16[128,256]{1,0:T(8,128...) custom-call(bf16[128,128]{1,0:T(8,128)(2,1)S(1)} %collective-permute, ...), custom_call_target="tpu_custom_call" | custom-call | flops 67108864 | bytes 1376256 | tf_op jit(solution)/shard_map/pallas_call | solution.py:29
  24.6 0.4 collective-permute-start.10
  25.0 1.6 %collective-permute-start.14 = (bf16[128,128]{1,0:T(8,128)(2,1)S(1)}, bf16[128,128]{1,0:T(8,128)(2,1)S(1)}, u32[]{:S(2)}, u32[]{:S(2)}) collective-permute-start(bf16[128,128]{1,0:T(8,128)(2,1)S(1)} %get-tuple-element.60), channel_id=1, source_target_pairs={{0,12},{4,8},{8,4},{12,0},{16,28},{20,24},{24,20},{28,16},{1,13},{... | collective-permute-start | bytes 98312 | tf_op jit(solution)/shard_map/ppermute | solution.py:52
  26.6 0.5 %collective-permute-start.15 = (bf16[128,128]{1,0:T(8,128)(2,1)S(1)}, bf16[128,128]{1,0:T(8,128)(2,1)S(1)}, u32[]{:S(2)}, u32[]{:S(2)}) collective-permute-start(bf16[128,128]{1,0:T(8,128)(2,1)S(1)} %get-tuple-element.61), channel_id=1, source_target_pairs={{0,8},{4,12},{8,0},{12,4},{16,24},{20,28},{24,16},{28,20},{1,9},{5... | collective-permute-start | bytes 98312 | tf_op jit(solution)/shard_map/ppermute | solution.py:52
  27.1 1.5 %collective-permute-start.16 = (bf16[128,128]{1,0:T(8,128)(2,1)S(1)}, bf16[128,128]{1,0:T(8,128)(2,1)S(1)}, u32[]{:S(2)}, u32[]{:S(2)}) collective-permute-start(bf16[128,128]{1,0:T(8,128)(2,1)S(1)} %get-tuple-element.62), channel_id=1, source_target_pairs={{0,4},{4,0},{8,12},{12,8},{16,20},{20,16},{24,28},{28,24},{1,5},{5... | collective-permute-start | bytes 98312 | tf_op jit(solution)/shard_map/ppermute | solution.py:52
  28.5 1.5 %shard_map.99 = (bf16[512,128]{1,0:T(8,128)(2,1)S(1)}, f32[512,128]{1,0:T(8,128)S(1)}, f32[512,256]{1,0:T(8,128)S(1)}) custom-call(bf16[3,512,128]{2,1,0:T(8,128)(2,1)S(1)} %get-tuple-element.39.qkv_ref, bf16[4,128,256]{2,1,0:T(8,128)(2,1)S(1)} %copy-done.1, bf16[512,256]{1,0:T(8,128)(2,1)S(1)} %get-tuple-element.40.kf_ref, ...), custom_call_target="tpu_custom_call" | custom-call | flops 268435456 | bytes 2949120 | tf_op jit(solution)/shard_map/pallas_call | solution.py:29
  30.0 0.0 collective-permute-done.10.rest_0_
  30.0 0.6 %shard_map.100 = (bf16[3,128,128]{2,1,0:T(8,128)(2,1)S(1)}, bf16[3,128,128]{2,1,0:T(8,128)(2,1)S(1)}, bf16[3,128,128]{2,1,0:T(8,128)(2,1)S(1)}, bf16[3,128,128]{2,1,0:T(8,128)(2,1)S(1)}) custom-call(bf16[3,512,128]{2,1,0:T(8,128)(2,1)S(1)} %get-tuple-element.39.qkv_ref, bf16[4,128,256]{2,1,0:T(8,128)(2,1)S(1)} %copy-done.1, ...), custom_call_target="tpu_custom_call" | custom-call | flops 100663296 | bytes 2293760 | tf_op jit(solution)/shard_map/pallas_call | solution.py:29
  30.6 0.3 collective-permute-done.16.refs_2_
  31.0 0.4 %shard_map.101 = (bf16[2,128,512]{2,1,0:T(8,128)(2,1)S(1)}, bf16[2,128,512]{2,1,0:T(8,128)(2,1)S(1)}) custom-call(bf16[128,128]{1,0:T(8,128)(2,1)S(1)} %collective-permute-done.14.refs_0_, bf16[128,128]{1,0:T(8,128)(2,1)S(1)} %collective-permute-done.15.refs_1_, bf16[128,128]{1,0:T(8,128)(2,1)S(1)} %collective-permute-done.16.refs_2_, ...), custom_call_target="tpu_custom_call" | custom-call | flops 268435456 | bytes 2850816 | tf_op jit(solution)/shard_map/pallas_call | solution.py:29
  31.4 0.1 collective-permute-start.17
  31.5 2.5 %collective-permute-start.11 = (bf16[3,128,128]{2,1,0:T(8,128)(2,1)S(1)}, bf16[3,128,128]{2,1,0:T(8,128)(2,1)S(1)}, u32[]{:S(2)}, u32[]{:S(2)}) collective-permute-start(bf16[3,128,128]{2,1,0:T(8,128)(2,1)S(1)} %get-tuple-element.56), channel_id=1, source_target_pairs={{0,12},{4,8},{8,4},{12,0},{16,28},{20,24},{24,20},{28,16},{1,13},{... | collective-permute-start | bytes 294920 | tf_op jit(solution)/shard_map/ppermute | solution.py:52
  34.0 0.5 %collective-permute-start.12 = (bf16[3,128,128]{2,1,0:T(8,128)(2,1)S(1)}, bf16[3,128,128]{2,1,0:T(8,128)(2,1)S(1)}, u32[]{:S(2)}, u32[]{:S(2)}) collective-permute-start(bf16[3,128,128]{2,1,0:T(8,128)(2,1)S(1)} %get-tuple-element.57), channel_id=1, source_target_pairs={{0,8},{4,12},{8,0},{12,4},{16,24},{20,28},{24,16},{28,20},{1,9},{5... | collective-permute-start | bytes 294920 | tf_op jit(solution)/shard_map/ppermute | solution.py:52
  34.5 0.6 %collective-permute-start.13 = (bf16[3,128,128]{2,1,0:T(8,128)(2,1)S(1)}, bf16[3,128,128]{2,1,0:T(8,128)(2,1)S(1)}, u32[]{:S(2)}, u32[]{:S(2)}) collective-permute-start(bf16[3,128,128]{2,1,0:T(8,128)(2,1)S(1)} %get-tuple-element.58), channel_id=1, source_target_pairs={{0,4},{4,0},{8,12},{12,8},{16,20},{20,16},{24,28},{28,24},{1,5},{5... | collective-permute-start | bytes 294920 | tf_op jit(solution)/shard_map/ppermute | solution.py:52
  35.1 0.1 add_bitcast_fusion
  35.2 0.6 %collective-permute-start.18 = (bf16[1,128,512]{2,1,0:T(8,128)(2,1)S(1)}, bf16[1,128,512]{2,1,0:T(8,128)(2,1)S(1)}, u32[]{:S(2)}, u32[]{:S(2)}) collective-permute-start(bf16[1,128,512]{2,1,0:T(8,128)(2,1)S(1)} %fusion), channel_id=1, source_target_pairs={{0,2},{1,3},{2,0},{3,1},{4,6},{5,7},{6,4},{7,5},{8,10},{9,11},{10,... | collective-permute-start | bytes 393224 | tf_op jit(solution)/shard_map/ppermute | solution.py:52
  35.8 2.3 %collective-permute-done.11.refs_0_ = bf16[3,128,128]{2,1,0:T(8,128)(2,1)S(1)} collective-permute-done((bf16[3,128,128]{2,1,0:T(8,128)(2,1)S(1)}, bf16[3,128,128]{2,1,0:T(8,128)(2,1)S(1)}, u32[]{:S(2)}, u32[]{:S(2)}) %collective-permute-start.11) | collective-permute-done | bytes 98336 | tf_op jit(solution)/shard_map/ppermute | solution.py:52
  38.1 1.7 %collective-permute-done.12.refs_1_ = bf16[3,128,128]{2,1,0:T(8,128)(2,1)S(1)} collective-permute-done((bf16[3,128,128]{2,1,0:T(8,128)(2,1)S(1)}, bf16[3,128,128]{2,1,0:T(8,128)(2,1)S(1)}, u32[]{:S(2)}, u32[]{:S(2)}) %collective-permute-start.12) | collective-permute-done | bytes 98336 | tf_op jit(solution)/shard_map/ppermute | solution.py:52
  39.7 0.5 %collective-permute-done.18 = bf16[1,128,512]{2,1,0:T(8,128)(2,1)S(1)} collective-permute-done((bf16[1,128,512]{2,1,0:T(8,128)(2,1)S(1)}, bf16[1,128,512]{2,1,0:T(8,128)(2,1)S(1)}, u32[]{:S(2)}, u32[]{:S(2)}) %collective-permute-start.18) | collective-permute-done | bytes 131104 | tf_op jit(solution)/shard_map/ppermute | solution.py:52
  40.2 0.9 %shard_map.102 = (bf16[128,512]{1,0:T(8,128)(2,1)}, bf16[128,512]{1,0:T(8,128)(2,1)}, bf16[128,512]{1,0:T(8,128)(2,1)}, bf16[128,512]{1,0:T(8,128)(2,1)}) custom-call(bf16[3,128,128]{2,1,0:T(8,128)(2,1)S(1)} %collective-permute-done.11.refs_0_, bf16[3,128,128]{2,1,0:T(8,128)(2,1)S(1)} %collective-permute-done.12.refs_1_, ...), custom_call_target="tpu_custom_call" | custom-call | bytes 1310720 | tf_op jit(solution)/shard_map/pallas_call | solution.py:29
  (15 shorter events, 0.1 us)
Async XLA Ops:
  0.6 8.2 %collective-permute-start.3 = (bf16[128,512]{1,0:T(8,128)(2,1)}, bf16[128,512]{1,0:T(8,128)(2,1)S(1)}, u32[]{:S(2)}, u32[]{:S(2)}) collective-permute-start(bf16[128,512]{1,0:T(8,128)(2,1)} %refs_0_.1), channel_id=1, source_target_pairs={{0,2},{1,3},{2,0},{3,1},{4,6},{5,7},{6,4},{7,5},{8,10},{9,11},{10,... | collective-permute-start | bytes 393224 | tf_op jit(solution)/shard_map/ppermute | solution.py:52
  3.6 5.3 %collective-permute-start.4 = (bf16[128,512]{1,0:T(8,128)(2,1)}, bf16[128,512]{1,0:T(8,128)(2,1)S(1)}, u32[]{:S(2)}, u32[]{:S(2)}) collective-permute-start(bf16[128,512]{1,0:T(8,128)(2,1)} %refs_0_.1), channel_id=1, source_target_pairs={{0,1},{1,0},{2,3},{3,2},{4,5},{5,4},{6,7},{7,6},{8,9},{9,8},{10,11... | collective-permute-start | bytes 393224 | tf_op jit(solution)/shard_map/ppermute | solution.py:52
  5.3 6.8 %collective-permute-start = (bf16[3,128,128]{2,1,0:T(8,128)(2,1)}, bf16[3,128,128]{2,1,0:T(8,128)(2,1)S(1)}, u32[]{:S(2)}, u32[]{:S(2)}) collective-permute-start(bf16[3,128,128]{2,1,0:T(8,128)(2,1)} %get-tuple-element.35), channel_id=1, source_target_pairs={{0,12},{4,8},{8,4},{12,0},{16,28},{20,24},{24,20},{28,16},{1,13},{... | collective-permute-start | bytes 294920 | tf_op jit(solution)/shard_map/ppermute | solution.py:52
  7.9 5.9 %collective-permute-start.1 = (bf16[3,128,128]{2,1,0:T(8,128)(2,1)}, bf16[3,128,128]{2,1,0:T(8,128)(2,1)S(1)}, u32[]{:S(2)}, u32[]{:S(2)}) collective-permute-start(bf16[3,128,128]{2,1,0:T(8,128)(2,1)} %get-tuple-element.36), channel_id=1, source_target_pairs={{0,8},{4,12},{8,0},{12,4},{16,24},{20,28},{24,16},{28,20},{1,9},{5... | collective-permute-start | bytes 294920 | tf_op jit(solution)/shard_map/ppermute | solution.py:52
  8.4 1.9 %copy-start = (bf16[512,2048]{1,0:T(8,128)(2,1)S(1)}, bf16[512,2048]{1,0:T(8,128)(2,1)}, u32[]{:S(2)}) copy-start(bf16[512,2048]{1,0:T(8,128)(2,1)} %refs_4_.5) | copy-start | bytes 6291460
  8.4 1.9 %copy-start.5 = (bf16[128,512]{1,0:T(8,128)(2,1)S(1)}, bf16[128,512]{1,0:T(8,128)(2,1)}, u32[]{:S(2)}) copy-start(bf16[128,512]{1,0:T(8,128)(2,1)} %refs_0_.1) | copy-start | bytes 393220
  8.4 5.5 %collective-permute-start.2 = (bf16[3,128,128]{2,1,0:T(8,128)(2,1)}, bf16[3,128,128]{2,1,0:T(8,128)(2,1)S(1)}, u32[]{:S(2)}, u32[]{:S(2)}) collective-permute-start(bf16[3,128,128]{2,1,0:T(8,128)(2,1)} %get-tuple-element.37), channel_id=1, source_target_pairs={{0,4},{4,0},{8,12},{12,8},{16,20},{20,16},{24,28},{28,24},{1,5},{5... | collective-permute-start | bytes 294920 | tf_op jit(solution)/shard_map/ppermute | solution.py:52
  8.9 1.3 %collective-permute-start.5 = (bf16[128,512]{1,0:T(8,128)(2,1)S(1)}, bf16[128,512]{1,0:T(8,128)(2,1)S(1)}, u32[]{:S(2)}, u32[]{:S(2)}) collective-permute-start(bf16[128,512]{1,0:T(8,128)(2,1)S(1)} %collective-permute-done.3.refs_1_), channel_id=1, source_target_pairs={{0,1},{1,0},{2,3},{3,2},{4,5},{5,4},{6,7},{7,6},{8,9},{9,8},{10,11... | collective-permute-start | bytes 393224 | tf_op jit(solution)/shard_map/ppermute | solution.py:52
  8.9 5.0 %copy-start.1 = (bf16[4,128,256]{2,1,0:T(8,128)(2,1)S(1)}, bf16[4,128,256]{2,1,0:T(8,128)(2,1)}, u32[]{:S(2)}) copy-start(bf16[4,128,256]{2,1,0:T(8,128)(2,1)} %om_ref.5) | copy-start | bytes 786436
  8.9 5.0 %copy-start.2 = (bf16[128,512]{1,0:T(8,128)(2,1)S(1)}, bf16[128,512]{1,0:T(8,128)(2,1)}, u32[]{:S(2)}) copy-start(bf16[128,512]{1,0:T(8,128)(2,1)} %refs_3_.1) | copy-start | bytes 393220
  8.9 5.0 %copy-start.3 = (bf16[128,512]{1,0:T(8,128)(2,1)S(1)}, bf16[128,512]{1,0:T(8,128)(2,1)}, u32[]{:S(2)}) copy-start(bf16[128,512]{1,0:T(8,128)(2,1)} %refs_4_.4) | copy-start | bytes 393220
  8.9 5.0 %copy-start.4 = (bf16[128,512]{1,0:T(8,128)(2,1)S(1)}, bf16[128,512]{1,0:T(8,128)(2,1)}, u32[]{:S(2)}) copy-start(bf16[128,512]{1,0:T(8,128)(2,1)} %refs_5_.1) | copy-start | bytes 393220
  14.4 9.5 %collective-permute-start.9 = (bf16[128,256]{1,0:T(8,128)(2,1)S(1)}, bf16[128,256]{1,0:T(8,128)(2,1)S(1)}, u32[]{:S(2)}, u32[]{:S(2)}) collective-permute-start(bf16[128,256]{1,0:T(8,128)(2,1)S(1)} %get-tuple-element.48), channel_id=1, source_target_pairs={{0,16},{4,20},{8,24},{12,28},{16,0},{20,4},{24,8},{28,12},{1,17},{... | collective-permute-start | bytes 196616 | tf_op jit(solution)/shard_map/ppermute | solution.py:52
  17.0 5.2 %collective-permute-start.6 = (bf16[128,128]{1,0:T(8,128)(2,1)S(1)}, bf16[128,128]{1,0:T(8,128)(2,1)S(1)}, u32[]{:S(2)}, u32[]{:S(2)}) collective-permute-start(bf16[128,128]{1,0:T(8,128)(2,1)S(1)} %get-tuple-element.44), channel_id=1, source_target_pairs={{0,12},{4,8},{8,4},{12,0},{16,28},{20,24},{24,20},{28,16},{1,13},{... | collective-permute-start | bytes 98312 | tf_op jit(solution)/shard_map/ppermute | solution.py:52
  19.5 3.9 %collective-permute-start.7 = (bf16[128,128]{1,0:T(8,128)(2,1)S(1)}, bf16[128,128]{1,0:T(8,128)(2,1)S(1)}, u32[]{:S(2)}, u32[]{:S(2)}) collective-permute-start(bf16[128,128]{1,0:T(8,128)(2,1)S(1)} %get-tuple-element.45), channel_id=1, source_target_pairs={{0,8},{4,12},{8,0},{12,4},{16,24},{20,28},{24,16},{28,20},{1,9},{5... | collective-permute-start | bytes 98312 | tf_op jit(solution)/shard_map/ppermute | solution.py:52
  19.9 3.9 %collective-permute-start.8 = (bf16[128,128]{1,0:T(8,128)(2,1)S(1)}, bf16[128,128]{1,0:T(8,128)(2,1)S(1)}, u32[]{:S(2)}, u32[]{:S(2)}) collective-permute-start(bf16[128,128]{1,0:T(8,128)(2,1)S(1)} %get-tuple-element.46), channel_id=1, source_target_pairs={{0,4},{4,0},{8,12},{12,8},{16,20},{20,16},{24,28},{28,24},{1,5},{5... | collective-permute-start | bytes 98312 | tf_op jit(solution)/shard_map/ppermute | solution.py:52
  24.6 5.4 %collective-permute-start.10 = (bf16[128,256]{1,0:T(8,128)(2,1)S(1)}, bf16[128,256]{1,0:T(8,128)(2,1)S(1)}, u32[]{:S(2)}, u32[]{:S(2)}) collective-permute-start(bf16[128,256]{1,0:T(8,128)(2,1)S(1)} %get-tuple-element.55), channel_id=1, source_target_pairs={{0,16},{4,20},{8,24},{12,28},{16,0},{20,4},{24,8},{28,12},{1,17},{... | collective-permute-start | bytes 196616 | tf_op jit(solution)/shard_map/ppermute | solution.py:52
  25.0 5.6 %collective-permute-start.14 = (bf16[128,128]{1,0:T(8,128)(2,1)S(1)}, bf16[128,128]{1,0:T(8,128)(2,1)S(1)}, u32[]{:S(2)}, u32[]{:S(2)}) collective-permute-start(bf16[128,128]{1,0:T(8,128)(2,1)S(1)} %get-tuple-element.60), channel_id=1, source_target_pairs={{0,12},{4,8},{8,4},{12,0},{16,28},{20,24},{24,20},{28,16},{1,13},{... | collective-permute-start | bytes 98312 | tf_op jit(solution)/shard_map/ppermute | solution.py:52
  26.6 4.0 %collective-permute-start.15 = (bf16[128,128]{1,0:T(8,128)(2,1)S(1)}, bf16[128,128]{1,0:T(8,128)(2,1)S(1)}, u32[]{:S(2)}, u32[]{:S(2)}) collective-permute-start(bf16[128,128]{1,0:T(8,128)(2,1)S(1)} %get-tuple-element.61), channel_id=1, source_target_pairs={{0,8},{4,12},{8,0},{12,4},{16,24},{20,28},{24,16},{28,20},{1,9},{5... | collective-permute-start | bytes 98312 | tf_op jit(solution)/shard_map/ppermute | solution.py:52
  27.1 3.9 %collective-permute-start.16 = (bf16[128,128]{1,0:T(8,128)(2,1)S(1)}, bf16[128,128]{1,0:T(8,128)(2,1)S(1)}, u32[]{:S(2)}, u32[]{:S(2)}) collective-permute-start(bf16[128,128]{1,0:T(8,128)(2,1)S(1)} %get-tuple-element.62), channel_id=1, source_target_pairs={{0,4},{4,0},{8,12},{12,8},{16,20},{20,16},{24,28},{28,24},{1,5},{5... | collective-permute-start | bytes 98312 | tf_op jit(solution)/shard_map/ppermute | solution.py:52
  31.4 3.6 %collective-permute-start.17 = (bf16[2,128,512]{2,1,0:T(8,128)(2,1)S(1)}, bf16[2,128,512]{2,1,0:T(8,128)(2,1)S(1)}, u32[]{:S(2)}, u32[]{:S(2)}) collective-permute-start(bf16[2,128,512]{2,1,0:T(8,128)(2,1)S(1)} %get-tuple-element.65), channel_id=1, source_target_pairs={{0,1},{1,0},{2,3},{3,2},{4,5},{5,4},{6,7},{7,6},{8,9},{9,8},{10,11... | collective-permute-start | bytes 786440 | tf_op jit(solution)/shard_map/ppermute | solution.py:52
  31.5 6.6 %collective-permute-start.11 = (bf16[3,128,128]{2,1,0:T(8,128)(2,1)S(1)}, bf16[3,128,128]{2,1,0:T(8,128)(2,1)S(1)}, u32[]{:S(2)}, u32[]{:S(2)}) collective-permute-start(bf16[3,128,128]{2,1,0:T(8,128)(2,1)S(1)} %get-tuple-element.56), channel_id=1, source_target_pairs={{0,12},{4,8},{8,4},{12,0},{16,28},{20,24},{24,20},{28,16},{1,13},{... | collective-permute-start | bytes 294920 | tf_op jit(solution)/shard_map/ppermute | solution.py:52
  34.0 5.7 %collective-permute-start.12 = (bf16[3,128,128]{2,1,0:T(8,128)(2,1)S(1)}, bf16[3,128,128]{2,1,0:T(8,128)(2,1)S(1)}, u32[]{:S(2)}, u32[]{:S(2)}) collective-permute-start(bf16[3,128,128]{2,1,0:T(8,128)(2,1)S(1)} %get-tuple-element.57), channel_id=1, source_target_pairs={{0,8},{4,12},{8,0},{12,4},{16,24},{20,28},{24,16},{28,20},{1,9},{5... | collective-permute-start | bytes 294920 | tf_op jit(solution)/shard_map/ppermute | solution.py:52
  34.5 5.2 %collective-permute-start.13 = (bf16[3,128,128]{2,1,0:T(8,128)(2,1)S(1)}, bf16[3,128,128]{2,1,0:T(8,128)(2,1)S(1)}, u32[]{:S(2)}, u32[]{:S(2)}) collective-permute-start(bf16[3,128,128]{2,1,0:T(8,128)(2,1)S(1)} %get-tuple-element.58), channel_id=1, source_target_pairs={{0,4},{4,0},{8,12},{12,8},{16,20},{20,16},{24,28},{28,24},{1,5},{5... | collective-permute-start | bytes 294920 | tf_op jit(solution)/shard_map/ppermute | solution.py:52
  35.2 5.1 %collective-permute-start.18 = (bf16[1,128,512]{2,1,0:T(8,128)(2,1)S(1)}, bf16[1,128,512]{2,1,0:T(8,128)(2,1)S(1)}, u32[]{:S(2)}, u32[]{:S(2)}) collective-permute-start(bf16[1,128,512]{2,1,0:T(8,128)(2,1)S(1)} %fusion), channel_id=1, source_target_pairs={{0,2},{1,3},{2,0},{3,1},{4,6},{5,7},{6,4},{7,5},{8,10},{9,11},{10,... | collective-permute-start | bytes 393224 | tf_op jit(solution)/shard_map/ppermute | solution.py:52

commit v9 on v8

v9 whole, which is shorter than its diff:
```python
import functools

import jax
import jax.numpy as jnp
from jax import lax
from jax.experimental import pallas as pl
from jax.experimental.pallas import tpu as pltpu
from jax.sharding import PartitionSpec as P

EPSILON = 1e-05
VMEM = pl.BlockSpec(memory_space=pltpu.VMEM)
ANY = pl.BlockSpec(memory_space=pl.ANY)
NN = (((1,), (0,)), ((), ()))
NT = (((1,), (1,)), ((), ()))
TN = (((0,), (0,)), ((), ()))


def mm(a, b, dims=NN):
    return lax.dot_general(a, b, dims, preferred_element_type=jnp.float32)


def bf(x):
    return x.astype(jnp.bfloat16)


def call(body, outs, *args, flops=0, specs=None, scratch=(), vmem=32):
    size = sum(a.size * a.dtype.itemsize for a in args)
    size += sum(o.size * o.dtype.itemsize for o in outs)
    return pl.pallas_call(
        body,
        out_shape=outs,
        in_specs=specs or [VMEM] * len(args),
        out_specs=[VMEM] * len(outs),
        scratch_shapes=list(scratch),
        cost_estimate=pl.CostEstimate(flops=flops, bytes_accessed=size, transcendentals=0),
        compiler_params=pltpu.CompilerParams(vmem_limit_bytes=vmem * 1024 * 1024),
    )(*args)


def struct(shape, dtype=jnp.bfloat16):
    return jax.ShapeDtypeStruct(shape, dtype)


def causal_mask(rows):
    row = lax.broadcasted_iota(jnp.int32, (rows, rows), 0)
    col = lax.broadcasted_iota(jnp.int32, (rows, rows), 1)
    return col <= row


def swap(array, axis, bit):
    size = lax.axis_size(axis)
    return lax.ppermute(array, axis, [(i, i ^ bit) for i in range(size)])


def bits_of(size):
    return [1 << b for b in range(size.bit_length() - 1)]


def reduce_blocks(own, sent, bits):
    got = swap(sent, "head", 1)
    for bit in bits[1:]:
        total = own.astype(jnp.float32) + got.astype(jnp.float32)
        pairs = total.reshape((total.shape[0] // 2, 2) + total.shape[1:])
        own, got = pairs[:, 0], swap(bf(pairs[:, 1]), "head", bit)
    return own[0].astype(jnp.float32), got[0]


def exchange(parts):
    return lax.all_to_all(parts, "member", 0, 0)


def swap_totals(total):
    got = []
    for bit in bits_of(lax.axis_size("group")):
        got.append(swap(bf(total), "group", bit))
        total = total.astype(jnp.float32) + got[-1].astype(jnp.float32)
    return got


def sum_of_side(refs, shape, earlier):
    group = lax.axis_index("group")
    total = jnp.zeros(shape, jnp.float32)
    for at, ref in enumerate(refs):
        from_earlier = lax.rem(lax.shift_right_logical(group, at), 2) == 1
        keep = from_earlier if earlier else jnp.logical_not(from_earlier)
        total = total + jnp.where(keep, ref[...].astype(jnp.float32), 0.0)
    return bf(total)


def lane(index, width):
    return pl.ds(pl.multiple_of(index * width, 128), width)


def pack_kernel(q_ref, k_ref, v_ref, out_ref, sems):
    n, _, _, dim = out_ref.shape
    copies = [
        pltpu.make_async_copy(
            ref.at[:, pl.ds(j * dim, dim)], out_ref.at[j, at], sems.at[j, at]
        )
        for j in range(n)
        for at, ref in enumerate((q_ref, k_ref, v_ref))
    ]
    for copy in copies:
        copy.start()
    for copy in copies:
        copy.wait()


def mark_kernel(_, out_ref):
    out_ref[...] = jnp.zeros(out_ref.shape, out_ref.dtype)


def grad_mixed_kernel(n, offsets, *refs):
    blocks, w_ref, out_ref = refs[:-3], refs[-3], refs[-1]
    h = lax.axis_index("head")
    width = blocks[0].shape[1]
    dim = out_ref.shape[2]
    total = None
    for offset, ref in zip(offsets, blocks):
        part = mm(ref[...], w_ref[:, lane(h ^ offset, width)], NT)
        total = part if total is None else total + part
    for j in range(n):
        out_ref[j] = bf(total[:, j * dim : (j + 1) * dim])


def first_kernel(n, got_ref, om_ref, _, qkv_ref, kf_ref, state_ref, total_ref):
    rows, dim = got_ref.shape[2:]
    r = lax.axis_index("member")
    scale = dim ** (-0.25)
    for t in range(n):
        qkv_ref[:, t * rows : (t + 1) * rows, :] = got_ref[t]
    k_all = qkv_ref[1]
    wide = k_all.astype(jnp.float32)
    half_sq = jnp.sum(wide * wide, axis=1, keepdims=True) * (scale * scale * 0.5)
    kf = bf(jnp.exp(mm(k_all, om_ref[r]) * scale - half_sq))
    kf_ref[...] = kf
    total = jnp.zeros(total_ref.shape, jnp.float32)
    for t in range(n):
        at = pl.ds(t * rows, rows)
        state_ref[t] = bf(total)
        total = total + mm(qkv_ref[2, at, :], kf[t * rows : (t + 1) * rows], TN)
    total_ref[...] = bf(total)


def inner_kernel(n, qkv_ref, om_ref, kf_ref, state_ref, qf_ref, scores_ref, num_ref):
    r, dim = lax.axis_index("member"), om_ref.shape[1]
    rows = scores_ref.shape[1]
    scale = dim ** (-0.25)
    causal = causal_mask(rows)
    qf_ref[...] = bf(jnp.exp(mm(qkv_ref[0], om_ref[r]) * scale))
    for t in range(n):
        at = pl.ds(t * rows, rows)
        qf = qf_ref[at, :]
        scores = bf(jnp.where(causal, mm(qf, kf_ref[at, :], NT), 0.0))
        scores_ref[t] = scores
        num_ref[at, :] = mm(scores, qkv_ref[2, at, :]) + mm(qf, state_ref[t], NT)


def turn_kernel(n, gm_ref, qf_ref, num_ref, *refs):
    earlier, (carried_ref, gn_ref, state_ref, total_ref, out_ref) = refs[:-5], refs[-5:]
    rows, dim = gm_ref.shape[1:]
    carried = sum_of_side(earlier, total_ref.shape, True)
    carried_ref[...] = carried
    num = num_ref[...] + mm(qf_ref[...], carried, NT)
    inv = lax.rsqrt(jnp.mean(num * num, axis=1, keepdims=True) + EPSILON)
    normed = num * inv
    gm = gm_ref[...].reshape(n * rows, dim).astype(jnp.float32)
    gn = bf((gm - normed * jnp.mean(gm * normed, axis=1, keepdims=True)) * inv)
    gn_ref[...] = gn
    out_ref[...] = bf(normed).reshape(out_ref.shape)
    total = jnp.zeros(total_ref.shape, jnp.float32)
    for t in reversed(range(n)):
        state_ref[t] = bf(total)
        at = pl.ds(t * rows, rows)
        total = total + mm(gn[t * rows : (t + 1) * rows], qf_ref[at, :], TN)
    total_ref[...] = bf(total)


def back_kernel(n, qkv_ref, om_ref, kf_ref, qf_ref, scores_ref, gn_ref, state_ref, carried_ref,
                later_ref, gq_ref, gv_ref, gkf_ref, gqf_scr):
    r, dim = lax.axis_index("member"), om_ref.shape[1]
    rows = scores_ref.shape[1]
    scale = dim ** (-0.25)
    causal = causal_mask(rows)
    gqf_scr[...] = mm(gn_ref[...], carried_ref[...])
    for t in range(n):
        at = pl.ds(t * rows, rows)
        qf, kf, gn, v = qf_ref[at, :], kf_ref[at, :], gn_ref[at, :], qkv_ref[2, at, :]
        gs = bf(jnp.where(causal, mm(gn, v, NT), 0.0))
        gqf = gqf_scr[at, :] + mm(gs, kf) + mm(gn, state_ref[t])
        terms = bf(gqf * qf.astype(jnp.float32))
        gq_ref[at, :] = bf(mm(terms, om_ref[r], NT) * scale)
        later = later_ref[t]
        gv_ref[at, :] = mm(scores_ref[t], gn, TN) + mm(kf, later, NT)
        gkf_ref[at, :] = mm(gs, qf, TN) + mm(v, later)


def end_kernel(n, qkv_ref, om_ref, kf_ref, gq_ref, gv_ref, gkf_ref, *rest):
    later, out_ref = rest[:-1], rest[-1]
    r, dim = lax.axis_index("member"), om_ref.shape[1]
    rows = out_ref.shape[2]
    scale = dim ** (-0.25)
    kf, after = kf_ref[...], sum_of_side(later, om_ref.shape[1:], False)
    gv = bf(gv_ref[...] + mm(kf, after, NT))
    gkf = gkf_ref[...] + mm(qkv_ref[2], after)
    terms = bf(gkf * kf.astype(jnp.float32))
    total = jnp.sum(terms.astype(jnp.float32), axis=1, keepdims=True)
    wide = qkv_ref[1].astype(jnp.float32)
    gk = bf(mm(terms, om_ref[r], NT) * scale - total * wide * (scale * scale))
    for t in range(n):
        at = slice(t * rows, (t + 1) * rows)
        out_ref[t, 0] = gq_ref[at, :]
        out_ref[t, 1] = gk[at]
        out_ref[t, 2] = gv[at]


def mixed_project_kernel(n, offsets, mixed_ref, w_ref, _, own_ref, sent_ref):
    h = lax.axis_index("head")
    width = own_ref.shape[2]
    half = len(offsets) // 2
    mixed = jnp.concatenate([mixed_ref[j] for j in range(n)], axis=1)
    for at, offset in enumerate(offsets):
        part = bf(mm(mixed, w_ref[:, lane(h ^ offset, width)]))
        if at < half:
            own_ref[at] = part
        else:
            sent_ref[at - half] = part


def unpack_kernel(n, got_ref, part_ref, last_ref, out_ref, *outs):
    dim = got_ref.shape[3]
    out_ref[...] = bf(part_ref[...] + last_ref[...].astype(jnp.float32))
    for j in range(n):
        for at, out in enumerate(outs):
            out[:, j * dim : (j + 1) * dim] = got_ref[j, at]


def local(queries, key_vectors, value_vectors, feature_proj, out_weight, grad_output):
    n, dim, feats = feature_proj.shape
    rows, width = grad_output.shape
    split = lax.axis_size("head")
    bits = bits_of(split)
    long = n * rows
    macs = long * dim * feats * 2
    f32 = jnp.float32

    offsets, blocks = [0], [grad_output]
    for bit in reversed(bits):
        blocks = blocks + [swap(b, "head", bit) for b in blocks]
        offsets = offsets + [o ^ bit for o in offsets]
    (packed,) = call(
        pack_kernel,
        [struct((n, 3, rows, dim))],
        queries, key_vectors, value_vectors,
        specs=[ANY] * 3, scratch=[pltpu.SemaphoreType.DMA((n, 3))], vmem=60,
    )
    got = exchange(packed)
    (mark,) = call(mark_kernel, [struct((8, 128), f32)], blocks[offsets.index(1)], specs=[ANY], flops=10**10)
    (gm_sent,) = call(
        functools.partial(grad_mixed_kernel, n, offsets),
        [struct((n, rows, dim))],
        *blocks, out_weight, mark, flops=2 * rows * out_weight.size,
        specs=[VMEM] * (split + 1) + [ANY],
    )
    gm = exchange(gm_sent)
    qkv, kf, state, total = call(
        functools.partial(first_kernel, n),
        [
            struct((3, long, dim)),
            struct((long, feats)),
            struct((n, dim, feats)),
            struct((dim, feats)),
        ],
        got, feature_proj, gm_sent, flops=2 * macs, specs=[VMEM, VMEM, ANY],
    )
    earlier = swap_totals(total)
    qf, scores, num = call(
        functools.partial(inner_kernel, n),
        [struct((long, feats)), struct((n, rows, rows)), struct((long, dim), f32)],
        qkv, feature_proj, kf, state, flops=4 * macs,
    )
    carried, gn, later, later_total, mixed_sent = call(
        functools.partial(turn_kernel, n),
        [
            struct((dim, feats)),
            struct((long, dim)),
            struct((n, dim, feats)),
            struct((dim, feats)),
            struct((n, rows, dim)),
        ],
        gm, qf, num, *earlier, flops=2 * macs,
    )
    after = swap_totals(later_total)
    mixed = exchange(mixed_sent)
    gq, gv_part, gkf_part = call(
        functools.partial(back_kernel, n),
        [struct((long, dim)), struct((long, dim), f32), struct((long, feats), f32)],
        qkv, feature_proj, kf, qf, scores, gn, state, carried, later, flops=8 * macs,
        scratch=[pltpu.VMEM((long, feats), f32)],
    )
    (grads_sent,) = call(
        functools.partial(end_kernel, n),
        [struct((n, 3, rows, dim))],
        qkv, feature_proj, kf, gq, gv_part, gkf_part, *after, flops=3 * macs,
    )
    grads = exchange(grads_sent)

    order = [o for o in range(split) if not o & 1] + [o for o in range(split) if o & 1]
    own, sent = call(
        functools.partial(mixed_project_kernel, n, order),
        [struct((split // 2, rows, width))] * 2,
        mixed, out_weight, grads_sent, flops=2 * rows * out_weight.size,
        specs=[VMEM, VMEM, ANY],
    )
    part, last = reduce_blocks(own, sent, bits)
    return call(
        functools.partial(unpack_kernel, n),
        [struct((rows, width))] + [struct((rows, n * dim))] * 3,
        grads, part, last,
    )


def solution(mesh):
    placed = (
        P(("group", "member"), "head"),
        P(("group", "member"), "head"),
        P(("group", "member"), "head"),
        P("head", None, None),
        P("head", None),
        P(("group", "member"), "head"),
    )

    def whole(*arrays):
        seq, head = mesh.shape["seq"], mesh.shape["head"]
        members = arrays[3].shape[0] // head
        split = jax.sharding.Mesh(
            mesh.devices.reshape(seq // members, members, head), ("group", "member", "head")
        )
        return jax.shard_map(
            local,
            mesh=split,
            in_specs=placed,
            out_specs=(P(("group", "member"), "head"),) * 4,
            check_vma=False,
        )(*arrays)

    return whole
```

time: 41.3 us -> 61.3 us (1.48)
  local copies, waits for them, and re-layouts: 0.07 us -> 12.5 us
  starting transfers between devices: 20.8 us -> 24.7 us
  Pallas kernels: 7.94 us -> 10 us
  waiting for transfers between devices: 11.4 us -> 12.4 us
    all_to_all x0 -> x4, starting transfers between devices: none -> 14.9 us  [exchange(): return lax.all_to_all(parts, 'member', 0, 0)]
    unnamed x12 -> x38, local copies, waits for them, and re-layouts: 0.03 us -> 12.4 us
    ppermute x19 -> x7, starting transfers between devices: 20.8 us -> 9.79 us  [swap(): return lax.ppermute(array, axis, [(i, i ^ bit) for i in range(size)])]
    all_to_all x0 -> x4, waiting for transfers between devices: none -> 5.71 us  [exchange(): return lax.all_to_all(parts, 'member', 0, 0)]
    ppermute x19 -> x7, waiting for transfers between devices: 11.4 us -> 6.74 us  [swap(): return lax.ppermute(array, axis, [(i, i ^ bit) for i in range(size)])]
    pallas_call x10, Pallas kernels: 7.94 us -> 10 us  [call(): pl.pallas_call(body, out_shape=outs, in_specs=specs or [VMEM] * len(args)...]
  transfers between devices with their start and end apart: 19 -> 11, of which waited for: 10 -> 5; matrix products, arithmetic and copies ran while one was open for 0% -> 0% of each run, Pallas kernels for 13% -> 13%
where the time goes in v9:
time: 61.3 us; the launch traced here: 60.5 us
  starting transfers between devices  24.7 us (40%)
  local copies, waits for them, and re-layouts  12.5 us (20%)
  waiting for transfers between devices  12.4 us (20%)
  Pallas kernels  10 us (16%)
  between operations  0.76 us (1%)
    all_to_all x4, starting transfers between devices, exchange(): return lax.all_to_all(parts, 'member', 0, 0)  14.9 us
    unnamed x38, local copies, waits for them, and re-layouts  12.4 us
    pallas_call x10, Pallas kernels, call(): pl.pallas_call(body, out_shape=outs, in_specs=specs or [VMEM] * len(args)...  10 us
    ppermute x7, starting transfers between devices, swap(): return lax.ppermute(array, axis, [(i, i ^ bit) for i in range(size)])  9.79 us
    ppermute x7, waiting for transfers between devices, swap(): return lax.ppermute(array, axis, [(i, i ^ bit) for i in range(size)])  6.74 us
    all_to_all x4, waiting for transfers between devices, exchange(): return lax.all_to_all(parts, 'member', 0, 0)  5.71 us
  transfers between devices with their start and end apart: 11, of which 5 were waited for; matrix products, arithmetic and copies ran while one was open for 0% of the time, Pallas kernels for 13%

profile of v9, /device:TPU:0, one launch (start us, length us, event | category | flops | bytes accessed | tf_op | source)
XLA Modules:
  0.0 60.5 jit_solution(176737293428858801)
XLA Ops:
  0.6 3.0 %collective-permute-start = (bf16[128,512]{1,0:T(8,128)(2,1)}, bf16[128,512]{1,0:T(8,128)(2,1)S(1)}, u32[]{:S(2)}, u32[]{:S(2)}) collective-permute-start(bf16[128,512]{1,0:T(8,128)(2,1)} %refs_0_.1), channel_id=1, source_target_pairs={{0,2},{1,3},{2,0},{3,1},{4,6},{5,7},{6,4},{7,5},{8,10},{9,11},{10,... | collective-permute-start | bytes 393224 | tf_op jit(solution)/shard_map/ppermute | solution.py:52
  3.6 0.0 collective-permute-start.1
  3.6 1.8 %shard_map.93 = bf16[4,3,128,128]{3,2,1,0:T(8,128)(2,1)} custom-call(bf16[128,512]{1,0:T(8,128)(2,1)} %q_ref.1, bf16[128,512]{1,0:T(8,128)(2,1)} %k_ref.1, bf16[128,512]{1,0:T(8,128)(2,1)} %v_ref.1), custom_call_target="tpu_custom_call" | custom-call | bytes 786432 | tf_op jit(solution)/shard_map/pallas_call | solution.py:29
  5.4 3.8 %all-to-all-start = ((bf16[4,3,128,128]{3,2,1,0:T(8,128)(2,1)}), bf16[4,3,128,128]{3,2,1,0:T(8,128)(2,1)S(1)}, u32[]{:S(2)}, u32[]{:S(2)}) async-start(bf16[4,3,128,128]{3,2,1,0:T(8,128)(2,1)} %shard_map.93), calls=%async_computation | async-start | bytes 786432 | tf_op jit(solution)/shard_map/all_to_all | solution.py:69
  9.3 0.0 collective-permute-done.refs_1_
  9.3 0.3 collective-permute-start.2
  9.6 0.0 collective-permute-done.1._.refs_2_
  9.6 1.1 %collective-permute-done.2.refs_3_ = bf16[128,512]{1,0:T(8,128)(2,1)S(1)} collective-permute-done((bf16[128,512]{1,0:T(8,128)(2,1)S(1)}, bf16[128,512]{1,0:T(8,128)(2,1)S(1)}, u32[]{:S(2)}, u32[]{:S(2)}) %collective-permute-start.2) | collective-permute-done | bytes 131104 | tf_op jit(solution)/shard_map/ppermute | solution.py:52
  10.7 0.2 copy-done
  10.9 1.5 %shard_map.95._ = bf16[4,128,128]{2,1,0:T(8,128)(2,1)} custom-call(bf16[128,512]{1,0:T(8,128)(2,1)S(1)} %copy-done.13, bf16[128,512]{1,0:T(8,128)(2,1)S(1)} %collective-permute-done.refs_1_, bf16[128,512]{1,0:T(8,128)(2,1)S(1)} %collective-permute-done.1._.refs_2_, bf16[128,512]{1,0:T(8,128)(2,1)S(1)} %collective-permute-done.2.refs_3_, ...), custom_call_target="tpu_custom_call" | custom-call | flops 268435456 | bytes 2756608 | tf_op jit(solution)/shard_map/pallas_call | solution.py:29
  12.3 4.2 %all-to-all-done.got_ref = bf16[4,3,128,128]{3,2,1,0:T(8,128)(2,1)S(1)} async-done(((bf16[4,3,128,128]{3,2,1,0:T(8,128)(2,1)}), bf16[4,3,128,128]{3,2,1,0:T(8,128)(2,1)S(1)}, u32[]{:S(2)}, u32[]{:S(2)}) %all-to-all-start) | async-done | bytes 393248 | tf_op jit(solution)/shard_map/all_to_all | solution.py:69
  16.6 3.3 %all-to-all-start.1 = ((bf16[4,128,128]{2,1,0:T(8,128)(2,1)}), bf16[4,128,128]{2,1,0:T(8,128)(2,1)S(1)}, u32[]{:S(2)}, u32[]{:S(2)}) async-start(bf16[4,128,128]{2,1,0:T(8,128)(2,1)} %shard_map.95._), calls=%async_computation.1 | async-start | bytes 262144 | tf_op jit(solution)/shard_map/all_to_all | solution.py:69
  19.9 1.1 %shard_map.96 = (bf16[3,512,128]{2,1,0:T(8,128)(2,1)S(1)}, bf16[512,256]{1,0:T(8,128)(2,1)S(1)}, bf16[4,128,256]{2,1,0:T(8,128)(2,1)S(1)}, bf16[128,256]{1,0:T(8,128)(2,1)}) custom-call(bf16[4,3,128,128]{3,2,1,0:T(8,128)(2,1)S(1)} %all-to-all-done.got_ref, bf16[4,128,256]{2,1,0:T(8,128)(2,1)S(1)} %copy-done.1, bf16[4,128,128]{2,1,0:T(8,128)(2,1)} %shard_map.95._), custom_call_target="tpu_custom_call" | custom-call | flops 67108864 | bytes 1769472 | tf_op jit(solution)/shard_map/pallas_call | solution.py:29
  21.0 2.6 %collective-permute-start.3 = (bf16[128,256]{1,0:T(8,128)(2,1)}, bf16[128,256]{1,0:T(8,128)(2,1)S(1)}, u32[]{:S(2)}, u32[]{:S(2)}) collective-permute-start(bf16[128,256]{1,0:T(8,128)(2,1)} %get-tuple-element.27), channel_id=1, source_target_pairs={{0,16},{16,0},{1,17},{17,1},{2,18},{18,2},{3,19},{19,3},{4,20},{20... | collective-permute-start | bytes 196616 | tf_op jit(solution)/shard_map/ppermute | solution.py:52
  23.6 0.8 %shard_map.97 = (bf16[512,256]{1,0:T(8,128)(2,1)S(1)}, bf16[4,128,128]{2,1,0:T(8,128)(2,1)S(1)}, f32[512,128]{1,0:T(8,128)S(1)}) custom-call(bf16[3,512,128]{2,1,0:T(8,128)(2,1)S(1)} %get-tuple-element.21.qkv_ref, bf16[4,128,256]{2,1,0:T(8,128)(2,1)S(1)} %copy-done.1, bf16[512,256]{1,0:T(8,128)(2,1)S(1)} %get-tuple-element.22.kf_ref, ...), custom_call_target="tpu_custom_call" | custom-call | flops 134217728 | bytes 1835008 | tf_op jit(solution)/shard_map/pallas_call | solution.py:29
  24.4 0.7 %copy-done.2 = bf16[4,128,256]{2,1,0:T(8,128)(2,1)} copy-done((bf16[4,128,256]{2,1,0:T(8,128)(2,1)}, bf16[4,128,256]{2,1,0:T(8,128)(2,1)S(1)}, u32[]{:S(2)}) %copy-start.2) | copy-done | bytes 262168
  25.1 0.7 %copy-done.4 = f32[512,128]{1,0:T(8,128)} copy-done((f32[512,128]{1,0:T(8,128)}, f32[512,128]{1,0:T(8,128)S(1)}, u32[]{:S(2)}) %copy-start.4) | copy-done | bytes 262168
  25.8 0.7 %copy-done.8 = bf16[4,128,128]{2,1,0:T(8,128)(2,1)} copy-done((bf16[4,128,128]{2,1,0:T(8,128)(2,1)}, bf16[4,128,128]{2,1,0:T(8,128)(2,1)S(1)}, u32[]{:S(2)}) %copy-start.8) | copy-done | bytes 131096
  26.4 0.0 all-to-all-done.1.gm_ref
  26.4 0.6 collective-permute-done.3.refs_0_
  27.0 0.6 %copy-done.16 = bf16[128,256]{1,0:T(8,128)(2,1)} copy-done((bf16[128,256]{1,0:T(8,128)(2,1)}, bf16[128,256]{1,0:T(8,128)(2,1)S(1)}, u32[]{:S(2)}) %copy-start.16) | copy-done | bytes 65560
  27.6 0.9 %copy-done.5 = f32[512,128]{1,0:T(8,128)S(1)} copy-done((f32[512,128]{1,0:T(8,128)S(1)}, f32[512,128]{1,0:T(8,128)}, u32[]{:S(2)}) %copy-start.5) | copy-done | bytes 262168
  28.6 0.8 %copy-done.17 = bf16[128,256]{1,0:T(8,128)(2,1)S(1)} copy-done((bf16[128,256]{1,0:T(8,128)(2,1)S(1)}, bf16[128,256]{1,0:T(8,128)(2,1)}, u32[]{:S(2)}) %copy-start.17) | copy-done | bytes 65560
  29.4 0.8 %shard_map.98 = (bf16[128,256]{1,0:T(8,128)(2,1)S(1)}, bf16[512,128]{1,0:T(8,128)(2,1)S(1)}, bf16[4,128,256]{2,1,0:T(8,128)(2,1)S(1)}, bf16[128,256]{1,0:T(8,128)(2,1)S(1)}, bf16[4,128,128]{2,1,0:T(8,128)(2,1)S(1)}) custom-call(bf16[4,128,128]{2,1,0:T(8,128)(2,1)S(1)} %all-to-all-done.1.gm_ref, bf16[512,256]{1,0:T(8,128)(2,1)S(1)} %get-tuple-element.24.qf_ref, ...), custom_call_target="tpu_custom_call" | custom-call | flops 67108864 | bytes 1376256 | tf_op jit(solution)/shard_map/pallas_call | solution.py:29
  30.2 0.7 %copy-done.6 = bf16[4,128,256]{2,1,0:T(8,128)(2,1)} copy-done((bf16[4,128,256]{2,1,0:T(8,128)(2,1)}, bf16[4,128,256]{2,1,0:T(8,128)(2,1)S(1)}, u32[]{:S(2)}) %copy-start.6) | copy-done | bytes 262168
  30.9 0.7 %copy-done.10 = bf16[512,128]{1,0:T(8,128)(2,1)} copy-done((bf16[512,128]{1,0:T(8,128)(2,1)}, bf16[512,128]{1,0:T(8,128)(2,1)S(1)}, u32[]{:S(2)}) %copy-start.10) | copy-done | bytes 131096
  31.5 0.7 %copy-done.12 = bf16[4,128,128]{2,1,0:T(8,128)(2,1)} copy-done((bf16[4,128,128]{2,1,0:T(8,128)(2,1)}, bf16[4,128,128]{2,1,0:T(8,128)(2,1)S(1)}, u32[]{:S(2)}) %copy-start.12) | copy-done | bytes 131096
  32.2 0.6 %copy-done.14 = bf16[128,256]{1,0:T(8,128)(2,1)} copy-done((bf16[128,256]{1,0:T(8,128)(2,1)}, bf16[128,256]{1,0:T(8,128)(2,1)S(1)}, u32[]{:S(2)}) %copy-start.14) | copy-done | bytes 65560
  32.8 0.6 %copy-done.18 = bf16[128,256]{1,0:T(8,128)(2,1)} copy-done((bf16[128,256]{1,0:T(8,128)(2,1)}, bf16[128,256]{1,0:T(8,128)(2,1)S(1)}, u32[]{:S(2)}) %copy-start.18) | copy-done | bytes 65560
  33.4 3.6 %all-to-all-start.3 = ((bf16[4,128,128]{2,1,0:T(8,128)(2,1)}), bf16[4,128,128]{2,1,0:T(8,128)(2,1)S(1)}, u32[]{:S(2)}, u32[]{:S(2)}) async-start(bf16[4,128,128]{2,1,0:T(8,128)(2,1)} %copy-done.12), calls=%async_computation.3 | async-start | bytes 262144 | tf_op jit(solution)/shard_map/all_to_all | solution.py:69
  37.0 3.2 %collective-permute-start.4 = (bf16[128,256]{1,0:T(8,128)(2,1)}, bf16[128,256]{1,0:T(8,128)(2,1)S(1)}, u32[]{:S(2)}, u32[]{:S(2)}) collective-permute-start(bf16[128,256]{1,0:T(8,128)(2,1)} %copy-done.18), channel_id=1, source_target_pairs={{0,16},{16,0},{1,17},{17,1},{2,18},{18,2},{3,19},{19,3},{4,20},{20... | collective-permute-start | bytes 196616 | tf_op jit(solution)/shard_map/ppermute | solution.py:52
  40.2 0.9 %copy-done.3 = bf16[4,128,256]{2,1,0:T(8,128)(2,1)S(1)} copy-done((bf16[4,128,256]{2,1,0:T(8,128)(2,1)S(1)}, bf16[4,128,256]{2,1,0:T(8,128)(2,1)}, u32[]{:S(2)}) %copy-start.3) | copy-done | bytes 262168
  41.2 0.9 %copy-done.7 = bf16[4,128,256]{2,1,0:T(8,128)(2,1)S(1)} copy-done((bf16[4,128,256]{2,1,0:T(8,128)(2,1)S(1)}, bf16[4,128,256]{2,1,0:T(8,128)(2,1)}, u32[]{:S(2)}) %copy-start.7) | copy-done | bytes 262168
  42.1 0.9 %copy-done.9 = bf16[4,128,128]{2,1,0:T(8,128)(2,1)S(1)} copy-done((bf16[4,128,128]{2,1,0:T(8,128)(2,1)S(1)}, bf16[4,128,128]{2,1,0:T(8,128)(2,1)}, u32[]{:S(2)}) %copy-start.9) | copy-done | bytes 131096
  43.0 0.9 %copy-done.11 = bf16[512,128]{1,0:T(8,128)(2,1)S(1)} copy-done((bf16[512,128]{1,0:T(8,128)(2,1)S(1)}, bf16[512,128]{1,0:T(8,128)(2,1)}, u32[]{:S(2)}) %copy-start.11) | copy-done | bytes 131096
  43.9 0.8 %copy-done.15 = bf16[128,256]{1,0:T(8,128)(2,1)S(1)} copy-done((bf16[128,256]{1,0:T(8,128)(2,1)S(1)}, bf16[128,256]{1,0:T(8,128)(2,1)}, u32[]{:S(2)}) %copy-start.15) | copy-done | bytes 65560
  44.8 1.5 %shard_map.99 = (bf16[512,128]{1,0:T(8,128)(2,1)S(1)}, f32[512,128]{1,0:T(8,128)S(1)}, f32[512,256]{1,0:T(8,128)S(1)}) custom-call(bf16[3,512,128]{2,1,0:T(8,128)(2,1)S(1)} %get-tuple-element.21.qkv_ref, bf16[4,128,256]{2,1,0:T(8,128)(2,1)S(1)} %copy-done.1, bf16[512,256]{1,0:T(8,128)(2,1)S(1)} %get-tuple-element.22.kf_ref, ...), custom_call_target="tpu_custom_call" | custom-call | flops 268435456 | bytes 2949120 | tf_op jit(solution)/shard_map/pallas_call | solution.py:29
  46.3 0.0 collective-permute-done.4.rest_0_
  46.3 1.3 %shard_map.100._ = bf16[4,3,128,128]{3,2,1,0:T(8,128)(2,1)} custom-call(bf16[3,512,128]{2,1,0:T(8,128)(2,1)S(1)} %get-tuple-element.21.qkv_ref, bf16[4,128,256]{2,1,0:T(8,128)(2,1)S(1)} %copy-done.1, bf16[512,256]{1,0:T(8,128)(2,1)S(1)} %get-tuple-element.22.kf_ref, bf16[512,128]{1,0:T(8,128)(2,1)S(1)} %get-tuple-element.31.gq_ref, ...), custom_call_target="tpu_custom_call" | custom-call | flops 100663296 | bytes 2293760 | tf_op jit(solution)/shard_map/pallas_call | solution.py:29
  47.6 0.0 all-to-all-done.3.mixed_ref
  47.6 0.5 shard_map.101
  48.1 0.1 collective-permute-start.5
  48.2 4.2 %all-to-all-start.2 = ((bf16[4,3,128,128]{3,2,1,0:T(8,128)(2,1)}), bf16[4,3,128,128]{3,2,1,0:T(8,128)(2,1)S(1)}, u32[]{:S(2)}, u32[]{:S(2)}) async-start(bf16[4,3,128,128]{3,2,1,0:T(8,128)(2,1)} %shard_map.100._), calls=%async_computation.2 | async-start | bytes 786432 | tf_op jit(solution)/shard_map/all_to_all | solution.py:69
  52.4 0.1 add_bitcast_fusion
  52.5 0.6 collective-permute-start.6
  53.1 5.0 %collective-permute-done.6 = bf16[1,128,512]{2,1,0:T(8,128)(2,1)S(1)} collective-permute-done((bf16[1,128,512]{2,1,0:T(8,128)(2,1)S(1)}, bf16[1,128,512]{2,1,0:T(8,128)(2,1)S(1)}, u32[]{:S(2)}, u32[]{:S(2)}) %collective-permute-start.6) | collective-permute-done | bytes 131104 | tf_op jit(solution)/shard_map/ppermute | solution.py:52
  58.2 1.5 %all-to-all-done.2.got_ref = bf16[4,3,128,128]{3,2,1,0:T(8,128)(2,1)S(1)} async-done(((bf16[4,3,128,128]{3,2,1,0:T(8,128)(2,1)}), bf16[4,3,128,128]{3,2,1,0:T(8,128)(2,1)S(1)}, u32[]{:S(2)}, u32[]{:S(2)}) %all-to-all-start.2) | async-done | bytes 393248 | tf_op jit(solution)/shard_map/all_to_all | solution.py:69
  59.6 0.9 %shard_map.102 = (bf16[128,512]{1,0:T(8,128)(2,1)}, bf16[128,512]{1,0:T(8,128)(2,1)}, bf16[128,512]{1,0:T(8,128)(2,1)}, bf16[128,512]{1,0:T(8,128)(2,1)}) custom-call(bf16[4,3,128,128]{3,2,1,0:T(8,128)(2,1)S(1)} %all-to-all-done.2.got_ref, f32[128,512]{1,0:T(8,128)S(1)} %slice_bitcast_fusion.part_ref, bf16[128,512]{1,0:T(8,128)(2,1)S(1)} %bitcast.7), custom_call_target="tpu_custom_call" | custom-call | bytes 1310720 | tf_op jit(solution)/shard_map/pallas_call | solution.py:29
  (25 shorter events, 0.1 us)
Async XLA Ops:
  0.6 8.6 %collective-permute-start = (bf16[128,512]{1,0:T(8,128)(2,1)}, bf16[128,512]{1,0:T(8,128)(2,1)S(1)}, u32[]{:S(2)}, u32[]{:S(2)}) collective-permute-start(bf16[128,512]{1,0:T(8,128)(2,1)} %refs_0_.1), channel_id=1, source_target_pairs={{0,2},{1,3},{2,0},{3,1},{4,6},{5,7},{6,4},{7,5},{8,10},{9,11},{10,... | collective-permute-start | bytes 393224 | tf_op jit(solution)/shard_map/ppermute | solution.py:52
  3.6 5.9 %collective-permute-start.1 = (bf16[128,512]{1,0:T(8,128)(2,1)}, bf16[128,512]{1,0:T(8,128)(2,1)S(1)}, u32[]{:S(2)}, u32[]{:S(2)}) collective-permute-start(bf16[128,512]{1,0:T(8,128)(2,1)} %refs_0_.1), channel_id=1, source_target_pairs={{0,1},{1,0},{2,3},{3,2},{4,5},{5,4},{6,7},{7,6},{8,9},{9,8},{10,11... | collective-permute-start | bytes 393224 | tf_op jit(solution)/shard_map/ppermute | solution.py:52
  5.4 11.1 %all-to-all-start = ((bf16[4,3,128,128]{3,2,1,0:T(8,128)(2,1)}), bf16[4,3,128,128]{3,2,1,0:T(8,128)(2,1)S(1)}, u32[]{:S(2)}, u32[]{:S(2)}) async-start(bf16[4,3,128,128]{3,2,1,0:T(8,128)(2,1)} %shard_map.93), calls=%async_computation | async-start | bytes 786432 | tf_op jit(solution)/shard_map/all_to_all | solution.py:69
  9.3 1.6 %copy-start = (bf16[512,2048]{1,0:T(8,128)(2,1)S(1)}, bf16[512,2048]{1,0:T(8,128)(2,1)}, u32[]{:S(2)}) copy-start(bf16[512,2048]{1,0:T(8,128)(2,1)} %w_ref.1) | copy-start | bytes 6291460
  9.3 1.6 %copy-start.13 = (bf16[128,512]{1,0:T(8,128)(2,1)S(1)}, bf16[128,512]{1,0:T(8,128)(2,1)}, u32[]{:S(2)}) copy-start(bf16[128,512]{1,0:T(8,128)(2,1)} %refs_0_.1) | copy-start | bytes 393220
  9.3 1.4 %collective-permute-start.2 = (bf16[128,512]{1,0:T(8,128)(2,1)S(1)}, bf16[128,512]{1,0:T(8,128)(2,1)S(1)}, u32[]{:S(2)}, u32[]{:S(2)}) collective-permute-start(bf16[128,512]{1,0:T(8,128)(2,1)S(1)} %collective-permute-done.refs_1_), channel_id=1, source_target_pairs={{0,1},{1,0},{2,3},{3,2},{4,5},{5,4},{6,7},{7,6},{8,9},{9,8},{10,11... | collective-permute-start | bytes 393224 | tf_op jit(solution)/shard_map/ppermute | solution.py:52
  9.6 10.3 %copy-start.1 = (bf16[4,128,256]{2,1,0:T(8,128)(2,1)S(1)}, bf16[4,128,256]{2,1,0:T(8,128)(2,1)}, u32[]{:S(2)}) copy-start(bf16[4,128,256]{2,1,0:T(8,128)(2,1)} %om_ref.7) | copy-start | bytes 786436
  16.6 9.9 %all-to-all-start.1 = ((bf16[4,128,128]{2,1,0:T(8,128)(2,1)}), bf16[4,128,128]{2,1,0:T(8,128)(2,1)S(1)}, u32[]{:S(2)}, u32[]{:S(2)}) async-start(bf16[4,128,128]{2,1,0:T(8,128)(2,1)} %shard_map.95._), calls=%async_computation.1 | async-start | bytes 262144 | tf_op jit(solution)/shard_map/all_to_all | solution.py:69
  21.0 6.0 %collective-permute-start.3 = (bf16[128,256]{1,0:T(8,128)(2,1)}, bf16[128,256]{1,0:T(8,128)(2,1)S(1)}, u32[]{:S(2)}, u32[]{:S(2)}) collective-permute-start(bf16[128,256]{1,0:T(8,128)(2,1)} %get-tuple-element.27), channel_id=1, source_target_pairs={{0,16},{16,0},{1,17},{17,1},{2,18},{18,2},{3,19},{19,3},{4,20},{20... | collective-permute-start | bytes 196616 | tf_op jit(solution)/shard_map/ppermute | solution.py:52
  24.3 0.7 %copy-start.2 = (bf16[4,128,256]{2,1,0:T(8,128)(2,1)}, bf16[4,128,256]{2,1,0:T(8,128)(2,1)S(1)}, u32[]{:S(2)}) copy-start(bf16[4,128,256]{2,1,0:T(8,128)(2,1)S(1)} %get-tuple-element.23.state_ref) | copy-start | bytes 786436
  25.1 0.7 %copy-start.4 = (f32[512,128]{1,0:T(8,128)}, f32[512,128]{1,0:T(8,128)S(1)}, u32[]{:S(2)}) copy-start(f32[512,128]{1,0:T(8,128)S(1)} %get-tuple-element.26.num_ref) | copy-start | bytes 786436
  25.8 0.7 %copy-start.8 = (bf16[4,128,128]{2,1,0:T(8,128)(2,1)}, bf16[4,128,128]{2,1,0:T(8,128)(2,1)S(1)}, u32[]{:S(2)}) copy-start(bf16[4,128,128]{2,1,0:T(8,128)(2,1)S(1)} %get-tuple-element.25.scores_ref) | copy-start | bytes 393220
  27.0 0.6 %copy-start.16 = (bf16[128,256]{1,0:T(8,128)(2,1)}, bf16[128,256]{1,0:T(8,128)(2,1)S(1)}, u32[]{:S(2)}) copy-start(bf16[128,256]{1,0:T(8,128)(2,1)S(1)} %collective-permute-done.3.refs_0_) | copy-start | bytes 196612
  27.6 0.9 %copy-start.5 = (f32[512,128]{1,0:T(8,128)S(1)}, f32[512,128]{1,0:T(8,128)}, u32[]{:S(2)}) copy-start(f32[512,128]{1,0:T(8,128)} %copy-done.4) | copy-start | bytes 786436
  28.6 0.8 %copy-start.17 = (bf16[128,256]{1,0:T(8,128)(2,1)S(1)}, bf16[128,256]{1,0:T(8,128)(2,1)}, u32[]{:S(2)}) copy-start(bf16[128,256]{1,0:T(8,128)(2,1)} %copy-done.16) | copy-start | bytes 196612
  30.2 0.7 %copy-start.6 = (bf16[4,128,256]{2,1,0:T(8,128)(2,1)}, bf16[4,128,256]{2,1,0:T(8,128)(2,1)S(1)}, u32[]{:S(2)}) copy-start(bf16[4,128,256]{2,1,0:T(8,128)(2,1)S(1)} %get-tuple-element.30.later_ref) | copy-start | bytes 786436
  30.9 0.7 %copy-start.10 = (bf16[512,128]{1,0:T(8,128)(2,1)}, bf16[512,128]{1,0:T(8,128)(2,1)S(1)}, u32[]{:S(2)}) copy-start(bf16[512,128]{1,0:T(8,128)(2,1)S(1)} %get-tuple-element.28.gn_ref) | copy-start | bytes 393220
  31.5 0.7 %copy-start.12 = (bf16[4,128,128]{2,1,0:T(8,128)(2,1)}, bf16[4,128,128]{2,1,0:T(8,128)(2,1)S(1)}, u32[]{:S(2)}) copy-start(bf16[4,128,128]{2,1,0:T(8,128)(2,1)S(1)} %get-tuple-element.35) | copy-start | bytes 393220
  32.2 0.6 %copy-start.14 = (bf16[128,256]{1,0:T(8,128)(2,1)}, bf16[128,256]{1,0:T(8,128)(2,1)S(1)}, u32[]{:S(2)}) copy-start(bf16[128,256]{1,0:T(8,128)(2,1)S(1)} %get-tuple-element.29.carried_ref) | copy-start | bytes 196612
  32.8 0.6 %copy-start.18 = (bf16[128,256]{1,0:T(8,128)(2,1)}, bf16[128,256]{1,0:T(8,128)(2,1)S(1)}, u32[]{:S(2)}) copy-start(bf16[128,256]{1,0:T(8,128)(2,1)S(1)} %get-tuple-element.34) | copy-start | bytes 196612
  33.4 14.2 %all-to-all-start.3 = ((bf16[4,128,128]{2,1,0:T(8,128)(2,1)}), bf16[4,128,128]{2,1,0:T(8,128)(2,1)S(1)}, u32[]{:S(2)}, u32[]{:S(2)}) async-start(bf16[4,128,128]{2,1,0:T(8,128)(2,1)} %copy-done.12), calls=%async_computation.3 | async-start | bytes 262144 | tf_op jit(solution)/shard_map/all_to_all | solution.py:69
  37.0 9.3 %collective-permute-start.4 = (bf16[128,256]{1,0:T(8,128)(2,1)}, bf16[128,256]{1,0:T(8,128)(2,1)S(1)}, u32[]{:S(2)}, u32[]{:S(2)}) collective-permute-start(bf16[128,256]{1,0:T(8,128)(2,1)} %copy-done.18), channel_id=1, source_target_pairs={{0,16},{16,0},{1,17},{17,1},{2,18},{18,2},{3,19},{19,3},{4,20},{20... | collective-permute-start | bytes 196616 | tf_op jit(solution)/shard_map/ppermute | solution.py:52
  40.2 0.9 %copy-start.3 = (bf16[4,128,256]{2,1,0:T(8,128)(2,1)S(1)}, bf16[4,128,256]{2,1,0:T(8,128)(2,1)}, u32[]{:S(2)}) copy-start(bf16[4,128,256]{2,1,0:T(8,128)(2,1)} %copy-done.2) | copy-start | bytes 786436
  41.2 0.9 %copy-start.7 = (bf16[4,128,256]{2,1,0:T(8,128)(2,1)S(1)}, bf16[4,128,256]{2,1,0:T(8,128)(2,1)}, u32[]{:S(2)}) copy-start(bf16[4,128,256]{2,1,0:T(8,128)(2,1)} %copy-done.6) | copy-start | bytes 786436
  42.1 0.9 %copy-start.9 = (bf16[4,128,128]{2,1,0:T(8,128)(2,1)S(1)}, bf16[4,128,128]{2,1,0:T(8,128)(2,1)}, u32[]{:S(2)}) copy-start(bf16[4,128,128]{2,1,0:T(8,128)(2,1)} %copy-done.8) | copy-start | bytes 393220
  43.0 0.9 %copy-start.11 = (bf16[512,128]{1,0:T(8,128)(2,1)S(1)}, bf16[512,128]{1,0:T(8,128)(2,1)}, u32[]{:S(2)}) copy-start(bf16[512,128]{1,0:T(8,128)(2,1)} %copy-done.10) | copy-start | bytes 393220
  43.9 0.8 %copy-start.15 = (bf16[128,256]{1,0:T(8,128)(2,1)S(1)}, bf16[128,256]{1,0:T(8,128)(2,1)}, u32[]{:S(2)}) copy-start(bf16[128,256]{1,0:T(8,128)(2,1)} %copy-done.14) | copy-start | bytes 196612
  48.1 4.3 %collective-permute-start.5 = (bf16[2,128,512]{2,1,0:T(8,128)(2,1)S(1)}, bf16[2,128,512]{2,1,0:T(8,128)(2,1)S(1)}, u32[]{:S(2)}, u32[]{:S(2)}) collective-permute-start(bf16[2,128,512]{2,1,0:T(8,128)(2,1)S(1)} %get-tuple-element.37), channel_id=1, source_target_pairs={{0,1},{1,0},{2,3},{3,2},{4,5},{5,4},{6,7},{7,6},{8,9},{9,8},{10,11... | collective-permute-start | bytes 786440 | tf_op jit(solution)/shard_map/ppermute | solution.py:52
  48.2 11.5 %all-to-all-start.2 = ((bf16[4,3,128,128]{3,2,1,0:T(8,128)(2,1)}), bf16[4,3,128,128]{3,2,1,0:T(8,128)(2,1)S(1)}, u32[]{:S(2)}, u32[]{:S(2)}) async-start(bf16[4,3,128,128]{3,2,1,0:T(8,128)(2,1)} %shard_map.100._), calls=%async_computation.2 | async-start | bytes 786432 | tf_op jit(solution)/shard_map/all_to_all | solution.py:69
  52.5 5.7 %collective-permute-start.6 = (bf16[1,128,512]{2,1,0:T(8,128)(2,1)S(1)}, bf16[1,128,512]{2,1,0:T(8,128)(2,1)S(1)}, u32[]{:S(2)}, u32[]{:S(2)}) collective-permute-start(bf16[1,128,512]{2,1,0:T(8,128)(2,1)S(1)} %fusion), channel_id=1, source_target_pairs={{0,2},{1,3},{2,0},{3,1},{4,6},{5,7},{6,4},{7,5},{8,10},{9,11},{10,... | collective-permute-start | bytes 393224 | tf_op jit(solution)/shard_map/ppermute | solution.py:52

commit v10 on v8

--- a/solution.py
+++ b/solution.py
@@ -23,14 +23,14 @@
     return x.astype(jnp.bfloat16)
 
 
-def call(body, outs, *args, flops=0, specs=None, scratch=(), vmem=32):
+def call(body, outs, *args, flops=0, specs=None, out_specs=None, scratch=(), vmem=32):
     size = sum(a.size * a.dtype.itemsize for a in args)
     size += sum(o.size * o.dtype.itemsize for o in outs)
     return pl.pallas_call(
         body,
         out_shape=outs,
         in_specs=specs or [VMEM] * len(args),
-        out_specs=[VMEM] * len(outs),
+        out_specs=out_specs or [VMEM] * len(outs),
         scratch_shapes=list(scratch),
         cost_estimate=pl.CostEstimate(flops=flops, bytes_accessed=size, transcendentals=0),
         compiler_params=pltpu.CompilerParams(vmem_limit_bytes=vmem * 1024 * 1024),
@@ -41,10 +41,38 @@
     return jax.ShapeDtypeStruct(shape, dtype)
 
 
-def causal_mask(rows):
-    row = lax.broadcasted_iota(jnp.int32, (rows, rows), 0)
-    col = lax.broadcasted_iota(jnp.int32, (rows, rows), 1)
-    return col <= row
+def tiles(long, rows):
+    size = 256 if long % 256 == 0 else rows
+    return [(at, at + size) for at in range(0, long, size)]
+
+
+def causal(scores):
+    row = lax.broadcasted_iota(jnp.int32, scores.shape, 0)
+    col = lax.broadcasted_iota(jnp.int32, scores.shape, 1)
+    return jnp.where(col <= row, scores, 0.0)
+
+
+def lower(left, right, spans):
+    out = {}
+    for i, (a, b) in enumerate(spans):
+        for j, (c, d) in enumerate(spans[: i + 1]):
+            tile = mm(left[a:b], right[c:d], NT)
+            out[i, j] = bf(causal(tile) if i == j else tile)
+    return out
+
+
+def times(tile_at, right, spans):
+    return [
+        sum(mm(tile_at(i, j), right[c:d]) for j, (c, d) in enumerate(spans[: i + 1]))
+        for i in range(len(spans))
+    ]
+
+
+def transposed_times(tile_at, right, spans):
+    return [
+        sum(mm(tile_at(i, j), right[a:b], TN) for i, (a, b) in enumerate(spans) if i >= j)
+        for j in range(len(spans))
+    ]
 
 
 def swap(array, axis, bit):
@@ -97,18 +125,24 @@
 
 
 def pack_kernel(n, q_ref, k_ref, v_ref, *rest):
-    outs, sems = rest[:-1], rest[-1]
+    outs, (scr, in_sems, out_sems) = rest[:-3], rest[-3:]
     r = member(n)
-    dim = outs[0].shape[2]
-    copies = []
+    dim = scr.shape[3]
+    loads, stores = [], []
     for k, out in enumerate(outs, 1):
         for at, ref in enumerate((q_ref, k_ref, v_ref)):
-            copies.append((ref.at[:, lane(r ^ k, dim)], out.at[at]))
-    started = [pltpu.make_async_copy(a, b, sems.at[i]) for i, (a, b) in enumerate(copies)]
-    for copy in started:
-        copy.start()
-    for copy in started:
-        copy.wait()
+            here = scr.at[k - 1, at]
+            loads.append(
+                pltpu.make_async_copy(ref.at[:, lane(r ^ k, dim)], here, in_sems.at[k - 1, at])
+            )
+            stores.append(pltpu.make_async_copy(here, out.at[at], out_sems.at[k - 1, at]))
+    for load in loads:
+        load.start()
+    for load, store in zip(loads, stores):
+        load.wait()
+        store.start()
+    for store in stores:
+        store.wait()
 
 
 def mark_kernel(_, out_ref):
@@ -131,7 +165,7 @@
 
 def first_kernel(n, *refs):
     got, own, om_ref = refs[: n - 1][::-1], refs[n - 1 : n + 2], refs[n + 2]
-    qkv_ref, kf_ref, state_ref, total_ref = refs[n + 4 :]
+    qkv_ref, kf_ref, total_ref = refs[n + 4 :]
     r = member(n)
     rows, dim = own[0].shape[0], om_ref.shape[1]
     scale = dim ** (-0.25)
@@ -147,31 +181,26 @@
     half_sq = jnp.sum(wide * wide, axis=1, keepdims=True) * (scale * scale * 0.5)
     kf = bf(jnp.exp(mm(k_all, om_ref[r]) * scale - half_sq))
     kf_ref[...] = kf
-    total = jnp.zeros(total_ref.shape, jnp.float32)
-    for t in range(n):
-        at = pl.ds(t * rows, rows)
-        state_ref[t] = bf(total)
-        total = total + mm(qkv_ref[2, at, :], kf[t * rows : (t + 1) * rows], TN)
-    total_ref[...] = bf(total)
-
-
-def inner_kernel(n, qkv_ref, om_ref, kf_ref, state_ref, qf_ref, scores_ref, num_ref):
-    r, dim = member(n), om_ref.shape[1]
-    rows = scores_ref.shape[1]
+    total_ref[...] = bf(mm(qkv_ref[2], kf, TN))
+
+
+def inner_kernel(rows, qkv_ref, om_ref, kf_ref, qf_ref, scores_ref, num_ref):
+    long, dim = num_ref.shape
+    n = long // rows
     scale = dim ** (-0.25)
-    causal = causal_mask(rows)
-    qf_ref[...] = bf(jnp.exp(mm(qkv_ref[0], om_ref[r]) * scale))
-    for t in range(n):
-        at = pl.ds(t * rows, rows)
-        qf = qf_ref[at, :]
-        scores = bf(jnp.where(causal, mm(qf, kf_ref[at, :], NT), 0.0))
-        scores_ref[t] = scores
-        num_ref[at, :] = mm(scores, qkv_ref[2, at, :]) + mm(qf, state_ref[t], NT)
+    spans = tiles(long, rows)
+    qf = bf(jnp.exp(mm(qkv_ref[0], om_ref[member(n)]) * scale))
+    qf_ref[...] = qf
+    scores = lower(qf, kf_ref[...], spans)
+    for (i, j), tile in scores.items():
+        scores_ref[slice(*spans[i]), slice(*spans[j])] = tile
+    for (a, b), part in zip(spans, times(lambda i, j: scores[i, j], qkv_ref[2], spans)):
+        num_ref[a:b, :] = part
 
 
 def turn_kernel(n, *refs):
-    gm_in, (qf_ref, num_ref), earlier = refs[:n][::-1], refs[n : n + 2], refs[n + 2 : -n - 5]
-    carried_ref, gn_ref, state_ref, total_ref = refs[-n - 5 : -n - 1]
+    gm_in, (qf_ref, num_ref), earlier = refs[:n][::-1], refs[n : n + 2], refs[n + 2 : -n - 4]
+    carried_ref, gn_ref, total_ref = refs[-n - 4 : -n - 1]
     outs, scr = refs[-n - 1 : -1], refs[-1]
     r = member(n)
     rows = gm_in[0].shape[0]
@@ -191,31 +220,29 @@
     scr[...] = bf(normed)
     for k in range(n):
         outs[k][...] = scr[places[k], :]
-    total = jnp.zeros(total_ref.shape, jnp.float32)
-    for t in reversed(range(n)):
-        state_ref[t] = bf(total)
-        at = pl.ds(t * rows, rows)
-        total = total + mm(gn[t * rows : (t + 1) * rows], qf_ref[at, :], TN)
-    total_ref[...] = bf(total)
-
-
-def back_kernel(n, qkv_ref, om_ref, kf_ref, qf_ref, scores_ref, gn_ref, state_ref, carried_ref,
-                later_ref, gq_ref, gv_ref, gkf_ref, gqf_scr):
-    r, dim = member(n), om_ref.shape[1]
-    rows = scores_ref.shape[1]
+    total_ref[...] = bf(mm(gn, qf_ref[...], TN))
+
+
+def back_kernel(rows, qkv_ref, om_ref, kf_ref, qf_ref, scores_ref, gn_ref, carried_ref,
+                gq_ref, gv_ref, gkf_ref):
+    long, dim = gn_ref.shape
+    r = member(long // rows)
     scale = dim ** (-0.25)
-    causal = causal_mask(rows)
-    gqf_scr[...] = mm(gn_ref[...], carried_ref[...])
-    for t in range(n):
-        at = pl.ds(t * rows, rows)
-        qf, kf, gn, v = qf_ref[at, :], kf_ref[at, :], gn_ref[at, :], qkv_ref[2, at, :]
-        gs = bf(jnp.where(causal, mm(gn, v, NT), 0.0))
-        gqf = gqf_scr[at, :] + mm(gs, kf) + mm(gn, state_ref[t])
-        terms = bf(gqf * qf.astype(jnp.float32))
-        gq_ref[at, :] = bf(mm(terms, om_ref[r], NT) * scale)
-        later = later_ref[t]
-        gv_ref[at, :] = mm(scores_ref[t], gn, TN) + mm(kf, later, NT)
-        gkf_ref[at, :] = mm(gs, qf, TN) + mm(v, later)
+    spans = tiles(long, rows)
+    gn, qf = gn_ref[...], qf_ref[...]
+    gs = lower(gn, qkv_ref[2], spans)
+    cross = mm(gn, carried_ref[...])
+    for (a, b), part in zip(spans, times(lambda i, j: gs[i, j], kf_ref[...], spans)):
+        terms = bf((cross[a:b] + part) * qf[a:b].astype(jnp.float32))
+        gq_ref[a:b, :] = bf(mm(terms, om_ref[r], NT) * scale)
+    for (a, b), part in zip(spans, transposed_times(lambda i, j: gs[i, j], qf, spans)):
+        gkf_ref[a:b, :] = part
+
+    def scores_at(i, j):
+        return scores_ref[slice(*spans[i]), slice(*spans[j])]
+
+    for (a, b), part in zip(spans, transposed_times(scores_at, gn, spans)):
+        gv_ref[a:b, :] = part
 
 
 def end_kernel(n, qkv_ref, om_ref, kf_ref, gq_ref, gv_ref, gkf_ref, *rest):
@@ -256,14 +283,21 @@
 
 def unpack_kernel(n, *refs):
     got, (part_ref, last_ref) = refs[:n][::-1], refs[n : n + 2]
-    out_ref, *outs = refs[n + 2 :]
+    (out_ref, *outs), (scr, sems, last_sem) = refs[n + 2 : -3], refs[-3:]
     r = member(n)
     dim = got[0].shape[2]
-    out_ref[...] = bf(part_ref[...] + last_ref[...].astype(jnp.float32))
-    for k in range(n):
-        cols = lane(r ^ k, dim)
-        for at, out in enumerate(outs):
-            out[:, cols] = got[k][at]
+    copies = [
+        pltpu.make_async_copy(got[k].at[at], out.at[:, lane(r ^ k, dim)], sems.at[k, at])
+        for k in range(n)
+        for at, out in enumerate(outs)
+    ]
+    for copy in copies:
+        copy.start()
+    scr[...] = bf(part_ref[...] + last_ref[...].astype(jnp.float32))
+    copies.append(pltpu.make_async_copy(scr, out_ref, last_sem))
+    copies[-1].start()
+    for copy in copies:
+        copy.wait()
 
 
 def local(queries, key_vectors, value_vectors, feature_proj, out_weight, grad_output):
@@ -283,7 +317,12 @@
         functools.partial(pack_kernel, n),
         [struct((3, rows, dim))] * (n - 1),
         queries, key_vectors, value_vectors,
-        specs=[ANY] * 3, scratch=[pltpu.SemaphoreType.DMA((3 * n - 3,))], vmem=60,
+        specs=[ANY] * 3, out_specs=[ANY] * (n - 1), vmem=60,
+        scratch=[
+            pltpu.VMEM((n - 1, 3, rows, dim), jnp.bfloat16),
+            pltpu.SemaphoreType.DMA((n - 1, 3)),
+            pltpu.SemaphoreType.DMA((n - 1, 3)),
+        ],
     )
     got = exchange(sends)
     (mark,) = call(mark_kernel, [struct((8, 128), f32)], blocks[offsets.index(1)], specs=[ANY], flops=10**10)
@@ -295,12 +334,11 @@
         scratch=[pltpu.VMEM((rows, n * dim), jnp.bfloat16)],
     )
     gm_in = exchange(gm_parts[1:]) + [gm_parts[0]]
-    qkv, kf, state, total = call(
+    qkv, kf, total = call(
         functools.partial(first_kernel, n),
         [
             struct((3, long, dim)),
             struct((long, feats)),
-            struct((n, dim, feats)),
             struct((dim, feats)),
         ],
         *got, queries, key_vectors, value_vectors, feature_proj, gm_parts[0],
@@ -308,16 +346,15 @@
     )
     earlier = swap_totals(total, n)
     qf, scores, num = call(
-        functools.partial(inner_kernel, n),
-        [struct((long, feats)), struct((n, rows, rows)), struct((long, dim), f32)],
-        qkv, feature_proj, kf, state, flops=4 * macs,
-    )
-    carried, gn, later, later_total, *mixed_parts = call(
+        functools.partial(inner_kernel, rows),
+        [struct((long, feats)), struct((long, long)), struct((long, dim), f32)],
+        qkv, feature_proj, kf, flops=4 * macs,
+    )
+    carried, gn, later_total, *mixed_parts = call(
         functools.partial(turn_kernel, n),
         [
             struct((dim, feats)),
             struct((long, dim)),
-            struct((n, dim, feats)),
             struct((dim, feats)),
         ]
         + [struct((rows, dim))] * n,
@@ -327,10 +364,9 @@
     after = swap_totals(later_total, n)
     mixed_in = exchange(mixed_parts[1:]) + [mixed_parts[0]]
     gq, gv_part, gkf_part = call(
-        functools.partial(back_kernel, n),
+        functools.partial(back_kernel, rows),
         [struct((long, dim)), struct((long, dim), f32), struct((long, feats), f32)],
-        qkv, feature_proj, kf, qf, scores, gn, state, carried, later, flops=8 * macs,
-        scratch=[pltpu.VMEM((long, feats), f32)],
+        qkv, feature_proj, kf, qf, scores, gn, carried, flops=8 * macs,
     )
     grads = call(
         functools.partial(end_kernel, n),
@@ -353,6 +389,12 @@
         functools.partial(unpack_kernel, n),
         [struct((rows, width))] + [struct((rows, n * dim))] * 3,
         *grads_in, part, last,
+        out_specs=[ANY] * 4,
+        scratch=[
+            pltpu.VMEM((rows, width), jnp.bfloat16),
+            pltpu.SemaphoreType.DMA((n, 3)),
+            pltpu.SemaphoreType.DMA,
+        ],
     )
 
 

time: 41.3 us -> 41.2 us (level)
  Pallas kernels: 7.94 us -> 7.05 us
  waiting for transfers between devices: 11.4 us -> 12.2 us
    pallas_call x10, Pallas kernels: 7.94 us -> 7.05 us  [call(): pl.pallas_call(body, out_shape=outs, in_specs=specs or [VMEM] * len(args)...]
    ppermute x19, waiting for transfers between devices: 11.4 us -> 12.2 us  [swap(): return lax.ppermute(array, axis, [(i, i ^ bit) for i in range(size)])]
  transfers between devices with their start and end apart: 19 -> 19, of which waited for: 10 -> 12; matrix products, arithmetic and copies ran while one was open for 0% -> 0% of each run, Pallas kernels for 13% -> 11%
where the time goes in v10:
time: 41.2 us; the launch traced here: 41 us
  starting transfers between devices  20.8 us (50%)
  waiting for transfers between devices  12.2 us (30%)
  Pallas kernels  7.05 us (17%)
  between operations  0.8 us (2%)
    ppermute x19, starting transfers between devices, swap(): return lax.ppermute(array, axis, [(i, i ^ bit) for i in range(size)])  20.8 us
    ppermute x19, waiting for transfers between devices, swap(): return lax.ppermute(array, axis, [(i, i ^ bit) for i in range(size)])  12.2 us
    pallas_call x10, Pallas kernels, call(): pl.pallas_call(body, out_shape=outs, in_specs=specs or [VMEM] * len(args)...  7.05 us
  transfers between devices with their start and end apart: 19, of which 12 were waited for; matrix products, arithmetic and copies ran while one was open for 0% of the time, Pallas kernels for 11%

profile of v10, /device:TPU:0, one launch (start us, length us, event | category | flops | bytes accessed | tf_op | source)
XLA Modules:
  0.0 41.0 jit_solution(1794863277608429826)
XLA Ops:
  0.6 3.0 %collective-permute-start.3 = (bf16[128,512]{1,0:T(8,128)(2,1)}, bf16[128,512]{1,0:T(8,128)(2,1)S(1)}, u32[]{:S(2)}, u32[]{:S(2)}) collective-permute-start(bf16[128,512]{1,0:T(8,128)(2,1)} %refs_0_.1), channel_id=1, source_target_pairs={{0,2},{1,3},{2,0},{3,1},{4,6},{5,7},{6,4},{7,5},{8,10},{9,11},{10,... | collective-permute-start | bytes 393224 | tf_op jit(solution)/shard_map/ppermute | solution.py:80
  3.6 0.0 collective-permute-start.4
  3.6 1.7 %shard_map.93 = (bf16[3,128,128]{2,1,0:T(8,128)(2,1)}, bf16[3,128,128]{2,1,0:T(8,128)(2,1)}, bf16[3,128,128]{2,1,0:T(8,128)(2,1)}) custom-call(bf16[128,512]{1,0:T(8,128)(2,1)} %refs_3_.1, bf16[128,512]{1,0:T(8,128)(2,1)} %refs_4_.4, bf16[128,512]{1,0:T(8,128)(2,1)} %refs_5_.1), custom_call_target="tpu_custom_call" | custom-call | bytes 688128 | tf_op jit(solution)/shard_map/pallas_call | solution.py:29
  5.3 2.6 %collective-permute-start = (bf16[3,128,128]{2,1,0:T(8,128)(2,1)}, bf16[3,128,128]{2,1,0:T(8,128)(2,1)S(1)}, u32[]{:S(2)}, u32[]{:S(2)}) collective-permute-start(bf16[3,128,128]{2,1,0:T(8,128)(2,1)} %get-tuple-element.33), channel_id=1, source_target_pairs={{0,12},{4,8},{8,4},{12,0},{16,28},{20,24},{24,20},{28,16},{1,13},{... | collective-permute-start | bytes 294920 | tf_op jit(solution)/shard_map/ppermute | solution.py:80
  7.9 0.4 %collective-permute-start.1 = (bf16[3,128,128]{2,1,0:T(8,128)(2,1)}, bf16[3,128,128]{2,1,0:T(8,128)(2,1)S(1)}, u32[]{:S(2)}, u32[]{:S(2)}) collective-permute-start(bf16[3,128,128]{2,1,0:T(8,128)(2,1)} %get-tuple-element.34), channel_id=1, source_target_pairs={{0,8},{4,12},{8,0},{12,4},{16,24},{20,28},{24,16},{28,20},{1,9},{5... | collective-permute-start | bytes 294920 | tf_op jit(solution)/shard_map/ppermute | solution.py:80
  8.4 0.5 %collective-permute-start.2 = (bf16[3,128,128]{2,1,0:T(8,128)(2,1)}, bf16[3,128,128]{2,1,0:T(8,128)(2,1)S(1)}, u32[]{:S(2)}, u32[]{:S(2)}) collective-permute-start(bf16[3,128,128]{2,1,0:T(8,128)(2,1)} %get-tuple-element.35), channel_id=1, source_target_pairs={{0,4},{4,0},{8,12},{12,8},{16,20},{20,16},{24,28},{28,24},{1,5},{5... | collective-permute-start | bytes 294920 | tf_op jit(solution)/shard_map/ppermute | solution.py:80
  8.9 0.0 collective-permute-done.3.refs_1_
  8.9 0.0 copy-start.1
  8.9 0.0 copy-start.2
  8.9 0.0 copy-start.3
  8.9 0.0 copy-start.4
  8.9 1.3 %collective-permute-done.5.refs_3_ = bf16[128,512]{1,0:T(8,128)(2,1)S(1)} collective-permute-done((bf16[128,512]{1,0:T(8,128)(2,1)S(1)}, bf16[128,512]{1,0:T(8,128)(2,1)S(1)}, u32[]{:S(2)}, u32[]{:S(2)}) %collective-permute-start.5) | collective-permute-done | bytes 131104 | tf_op jit(solution)/shard_map/ppermute | solution.py:80
  10.2 0.9 %shard_map.95 = (bf16[128,128]{1,0:T(8,128)(2,1)S(1)}, bf16[128,128]{1,0:T(8,128)(2,1)S(1)}, bf16[128,128]{1,0:T(8,128)(2,1)S(1)}, bf16[128,128]{1,0:T(8,128)(2,1)S(1)}) custom-call(bf16[128,512]{1,0:T(8,128)(2,1)S(1)} %copy-done.5, bf16[128,512]{1,0:T(8,128)(2,1)S(1)} %collective-permute-done.3.refs_1_, ...), custom_call_target="tpu_custom_call" | custom-call | flops 268435456 | bytes 2756608 | tf_op jit(solution)/shard_map/pallas_call | solution.py:29
  11.1 1.0 %collective-permute-done.refs_0_ = bf16[3,128,128]{2,1,0:T(8,128)(2,1)S(1)} collective-permute-done((bf16[3,128,128]{2,1,0:T(8,128)(2,1)}, bf16[3,128,128]{2,1,0:T(8,128)(2,1)S(1)}, u32[]{:S(2)}, u32[]{:S(2)}) %collective-permute-start) | collective-permute-done | bytes 98336 | tf_op jit(solution)/shard_map/ppermute | solution.py:80
  12.1 1.8 %collective-permute-done.1.refs_1_ = bf16[3,128,128]{2,1,0:T(8,128)(2,1)S(1)} collective-permute-done((bf16[3,128,128]{2,1,0:T(8,128)(2,1)}, bf16[3,128,128]{2,1,0:T(8,128)(2,1)S(1)}, u32[]{:S(2)}, u32[]{:S(2)}) %collective-permute-start.1) | collective-permute-done | bytes 98336 | tf_op jit(solution)/shard_map/ppermute | solution.py:80
  13.9 0.5 %shard_map.96 = (bf16[3,512,128]{2,1,0:T(8,128)(2,1)S(1)}, bf16[512,256]{1,0:T(8,128)(2,1)S(1)}, bf16[128,256]{1,0:T(8,128)(2,1)S(1)}) custom-call(bf16[3,128,128]{2,1,0:T(8,128)(2,1)S(1)} %collective-permute-done.refs_0_, bf16[3,128,128]{2,1,0:T(8,128)(2,1)S(1)} %collective-permute-done.1.refs_1_, bf16[3,128,128]{2,1,0:T(8,128)(2,1)S(1)} %collective-permute-done.2.refs_2_, ...), custom_call_target="tpu_custom_call" | custom-call | flops 67108864 | bytes 1703936 | tf_op jit(solution)/shard_map/pallas_call | solution.py:29
  14.4 2.7 %collective-permute-start.9 = (bf16[128,256]{1,0:T(8,128)(2,1)S(1)}, bf16[128,256]{1,0:T(8,128)(2,1)S(1)}, u32[]{:S(2)}, u32[]{:S(2)}) collective-permute-start(bf16[128,256]{1,0:T(8,128)(2,1)S(1)} %get-tuple-element.45), channel_id=1, source_target_pairs={{0,16},{4,20},{8,24},{12,28},{16,0},{20,4},{24,8},{28,12},{1,17},{... | collective-permute-start | bytes 196616 | tf_op jit(solution)/shard_map/ppermute | solution.py:80
  17.0 2.5 %collective-permute-start.6 = (bf16[128,128]{1,0:T(8,128)(2,1)S(1)}, bf16[128,128]{1,0:T(8,128)(2,1)S(1)}, u32[]{:S(2)}, u32[]{:S(2)}) collective-permute-start(bf16[128,128]{1,0:T(8,128)(2,1)S(1)} %get-tuple-element.41), channel_id=1, source_target_pairs={{0,12},{4,8},{8,4},{12,0},{16,28},{20,24},{24,20},{28,16},{1,13},{... | collective-permute-start | bytes 98312 | tf_op jit(solution)/shard_map/ppermute | solution.py:80
  19.5 0.4 %collective-permute-start.7 = (bf16[128,128]{1,0:T(8,128)(2,1)S(1)}, bf16[128,128]{1,0:T(8,128)(2,1)S(1)}, u32[]{:S(2)}, u32[]{:S(2)}) collective-permute-start(bf16[128,128]{1,0:T(8,128)(2,1)S(1)} %get-tuple-element.42), channel_id=1, source_target_pairs={{0,8},{4,12},{8,0},{12,4},{16,24},{20,28},{24,16},{28,20},{1,9},{5... | collective-permute-start | bytes 98312 | tf_op jit(solution)/shard_map/ppermute | solution.py:80
  19.9 0.6 %collective-permute-start.8 = (bf16[128,128]{1,0:T(8,128)(2,1)S(1)}, bf16[128,128]{1,0:T(8,128)(2,1)S(1)}, u32[]{:S(2)}, u32[]{:S(2)}) collective-permute-start(bf16[128,128]{1,0:T(8,128)(2,1)S(1)} %get-tuple-element.43), channel_id=1, source_target_pairs={{0,4},{4,0},{8,12},{12,8},{16,20},{20,16},{24,28},{28,24},{1,5},{5... | collective-permute-start | bytes 98312 | tf_op jit(solution)/shard_map/ppermute | solution.py:80
  20.5 0.5 %shard_map.97 = (bf16[512,256]{1,0:T(8,128)(2,1)S(1)}, bf16[512,512]{1,0:T(8,128)(2,1)S(1)}, f32[512,128]{1,0:T(8,128)S(1)}) custom-call(bf16[3,512,128]{2,1,0:T(8,128)(2,1)S(1)} %get-tuple-element.37.qkv_ref, bf16[4,128,256]{2,1,0:T(8,128)(2,1)S(1)} %copy-done.1, bf16[512,256]{1,0:T(8,128)(2,1)S(1)} %get-tuple-element.38.kf_ref), custom_call_target="tpu_custom_call" | custom-call | flops 134217728 | bytes 1966080 | tf_op jit(solution)/shard_map/pallas_call | solution.py:29
  21.0 1.2 %collective-permute-done.6.refs_0_ = bf16[128,128]{1,0:T(8,128)(2,1)S(1)} collective-permute-done((bf16[128,128]{1,0:T(8,128)(2,1)S(1)}, bf16[128,128]{1,0:T(8,128)(2,1)S(1)}, u32[]{:S(2)}, u32[]{:S(2)}) %collective-permute-start.6) | collective-permute-done | bytes 32800 | tf_op jit(solution)/shard_map/ppermute | solution.py:80
  22.3 1.1 %collective-permute-done.7.refs_1_ = bf16[128,128]{1,0:T(8,128)(2,1)S(1)} collective-permute-done((bf16[128,128]{1,0:T(8,128)(2,1)S(1)}, bf16[128,128]{1,0:T(8,128)(2,1)S(1)}, u32[]{:S(2)}, u32[]{:S(2)}) %collective-permute-start.7) | collective-permute-done | bytes 32800 | tf_op jit(solution)/shard_map/ppermute | solution.py:80
  23.4 0.4 %collective-permute-done.8.refs_2_ = bf16[128,128]{1,0:T(8,128)(2,1)S(1)} collective-permute-done((bf16[128,128]{1,0:T(8,128)(2,1)S(1)}, bf16[128,128]{1,0:T(8,128)(2,1)S(1)}, u32[]{:S(2)}, u32[]{:S(2)}) %collective-permute-start.8) | collective-permute-done | bytes 32800 | tf_op jit(solution)/shard_map/ppermute | solution.py:80
  23.9 0.0 collective-permute-done.9.refs_6_
  23.9 0.6 %shard_map.98 = (bf16[128,256]{1,0:T(8,128)(2,1)S(1)}, bf16[512,128]{1,0:T(8,128)(2,1)S(1)}, bf16[128,256]{1,0:T(8,128)(2,1)S(1)}, bf16[128,128]{1,0:T(8,128)(2,...) custom-call(bf16[128,128]{1,0:T(8,128)(2,1)S(1)} %collective-permute-done.6.refs_0_, ...), custom_call_target="tpu_custom_call" | custom-call | flops 67108864 | bytes 1114112 | tf_op jit(solution)/shard_map/pallas_call | solution.py:29
  24.5 0.4 collective-permute-start.10
  24.9 1.6 %collective-permute-start.14 = (bf16[128,128]{1,0:T(8,128)(2,1)S(1)}, bf16[128,128]{1,0:T(8,128)(2,1)S(1)}, u32[]{:S(2)}, u32[]{:S(2)}) collective-permute-start(bf16[128,128]{1,0:T(8,128)(2,1)S(1)} %get-tuple-element.56), channel_id=1, source_target_pairs={{0,12},{4,8},{8,4},{12,0},{16,28},{20,24},{24,20},{28,16},{1,13},{... | collective-permute-start | bytes 98312 | tf_op jit(solution)/shard_map/ppermute | solution.py:80
  26.5 0.4 %collective-permute-start.15 = (bf16[128,128]{1,0:T(8,128)(2,1)S(1)}, bf16[128,128]{1,0:T(8,128)(2,1)S(1)}, u32[]{:S(2)}, u32[]{:S(2)}) collective-permute-start(bf16[128,128]{1,0:T(8,128)(2,1)S(1)} %get-tuple-element.57), channel_id=1, source_target_pairs={{0,8},{4,12},{8,0},{12,4},{16,24},{20,28},{24,16},{28,20},{1,9},{5... | collective-permute-start | bytes 98312 | tf_op jit(solution)/shard_map/ppermute | solution.py:80
  26.9 1.5 %collective-permute-start.16 = (bf16[128,128]{1,0:T(8,128)(2,1)S(1)}, bf16[128,128]{1,0:T(8,128)(2,1)S(1)}, u32[]{:S(2)}, u32[]{:S(2)}) collective-permute-start(bf16[128,128]{1,0:T(8,128)(2,1)S(1)} %get-tuple-element.58), channel_id=1, source_target_pairs={{0,4},{4,0},{8,12},{12,8},{16,20},{20,16},{24,28},{28,24},{1,5},{5... | collective-permute-start | bytes 98312 | tf_op jit(solution)/shard_map/ppermute | solution.py:80
  28.4 1.0 %shard_map.99 = (bf16[512,128]{1,0:T(8,128)(2,1)S(1)}, f32[512,128]{1,0:T(8,128)S(1)}, f32[512,256]{1,0:T(8,128)S(1)}) custom-call(bf16[3,512,128]{2,1,0:T(8,128)(2,1)S(1)} %get-tuple-element.37.qkv_ref, bf16[4,128,256]{2,1,0:T(8,128)(2,1)S(1)} %copy-done.1, bf16[512,256]{1,0:T(8,128)(2,1)S(1)} %get-tuple-element.38.kf_ref, ...), custom_call_target="tpu_custom_call" | custom-call | flops 268435456 | bytes 2818048 | tf_op jit(solution)/shard_map/pallas_call | solution.py:29
  29.4 0.4 collective-permute-done.10.rest_0_
  29.7 0.6 %shard_map.100 = (bf16[3,128,128]{2,1,0:T(8,128)(2,1)S(1)}, bf16[3,128,128]{2,1,0:T(8,128)(2,1)S(1)}, bf16[3,128,128]{2,1,0:T(8,128)(2,1)S(1)}, bf16[3,128,128]{2,1,0:T(8,128)(2,1)S(1)}) custom-call(bf16[3,512,128]{2,1,0:T(8,128)(2,1)S(1)} %get-tuple-element.37.qkv_ref, bf16[4,128,256]{2,1,0:T(8,128)(2,1)S(1)} %copy-done.1, ...), custom_call_target="tpu_custom_call" | custom-call | flops 100663296 | bytes 2293760 | tf_op jit(solution)/shard_map/pallas_call | solution.py:29
  30.3 0.1 collective-permute-done.15.refs_1_
  30.4 0.4 %collective-permute-done.16.refs_2_ = bf16[128,128]{1,0:T(8,128)(2,1)S(1)} collective-permute-done((bf16[128,128]{1,0:T(8,128)(2,1)S(1)}, bf16[128,128]{1,0:T(8,128)(2,1)S(1)}, u32[]{:S(2)}, u32[]{:S(2)}) %collective-permute-start.16) | collective-permute-done | bytes 32800 | tf_op jit(solution)/shard_map/ppermute | solution.py:80
  30.8 0.5 %shard_map.101 = (bf16[2,128,512]{2,1,0:T(8,128)(2,1)S(1)}, bf16[2,128,512]{2,1,0:T(8,128)(2,1)S(1)}) custom-call(bf16[128,128]{1,0:T(8,128)(2,1)S(1)} %collective-permute-done.14.refs_0_, bf16[128,128]{1,0:T(8,128)(2,1)S(1)} %collective-permute-done.15.refs_1_, bf16[128,128]{1,0:T(8,128)(2,1)S(1)} %collective-permute-done.16.refs_2_, ...), custom_call_target="tpu_custom_call" | custom-call | flops 268435456 | bytes 2850816 | tf_op jit(solution)/shard_map/pallas_call | solution.py:29
  31.3 0.1 collective-permute-start.17
  31.4 2.5 %collective-permute-start.11 = (bf16[3,128,128]{2,1,0:T(8,128)(2,1)S(1)}, bf16[3,128,128]{2,1,0:T(8,128)(2,1)S(1)}, u32[]{:S(2)}, u32[]{:S(2)}) collective-permute-start(bf16[3,128,128]{2,1,0:T(8,128)(2,1)S(1)} %get-tuple-element.52), channel_id=1, source_target_pairs={{0,12},{4,8},{8,4},{12,0},{16,28},{20,24},{24,20},{28,16},{1,13},{... | collective-permute-start | bytes 294920 | tf_op jit(solution)/shard_map/ppermute | solution.py:80
  33.9 0.4 %collective-permute-start.12 = (bf16[3,128,128]{2,1,0:T(8,128)(2,1)S(1)}, bf16[3,128,128]{2,1,0:T(8,128)(2,1)S(1)}, u32[]{:S(2)}, u32[]{:S(2)}) collective-permute-start(bf16[3,128,128]{2,1,0:T(8,128)(2,1)S(1)} %get-tuple-element.53), channel_id=1, source_target_pairs={{0,8},{4,12},{8,0},{12,4},{16,24},{20,28},{24,16},{28,20},{1,9},{5... | collective-permute-start | bytes 294920 | tf_op jit(solution)/shard_map/ppermute | solution.py:80
  34.4 0.6 %collective-permute-start.13 = (bf16[3,128,128]{2,1,0:T(8,128)(2,1)S(1)}, bf16[3,128,128]{2,1,0:T(8,128)(2,1)S(1)}, u32[]{:S(2)}, u32[]{:S(2)}) collective-permute-start(bf16[3,128,128]{2,1,0:T(8,128)(2,1)S(1)} %get-tuple-element.54), channel_id=1, source_target_pairs={{0,4},{4,0},{8,12},{12,8},{16,20},{20,16},{24,28},{28,24},{1,5},{5... | collective-permute-start | bytes 294920 | tf_op jit(solution)/shard_map/ppermute | solution.py:80
  34.9 0.0 collective-permute-done.17
  34.9 0.1 add_bitcast_fusion
  35.0 0.6 %collective-permute-start.18 = (bf16[1,128,512]{2,1,0:T(8,128)(2,1)S(1)}, bf16[1,128,512]{2,1,0:T(8,128)(2,1)S(1)}, u32[]{:S(2)}, u32[]{:S(2)}) collective-permute-start(bf16[1,128,512]{2,1,0:T(8,128)(2,1)S(1)} %fusion), channel_id=1, source_target_pairs={{0,2},{1,3},{2,0},{3,1},{4,6},{5,7},{6,4},{7,5},{8,10},{9,11},{10,... | collective-permute-start | bytes 393224 | tf_op jit(solution)/shard_map/ppermute | solution.py:80
  35.7 2.3 %collective-permute-done.11.refs_0_ = bf16[3,128,128]{2,1,0:T(8,128)(2,1)S(1)} collective-permute-done((bf16[3,128,128]{2,1,0:T(8,128)(2,1)S(1)}, bf16[3,128,128]{2,1,0:T(8,128)(2,1)S(1)}, u32[]{:S(2)}, u32[]{:S(2)}) %collective-permute-start.11) | collective-permute-done | bytes 98336 | tf_op jit(solution)/shard_map/ppermute | solution.py:80
  37.9 1.6 %collective-permute-done.12.refs_1_ = bf16[3,128,128]{2,1,0:T(8,128)(2,1)S(1)} collective-permute-done((bf16[3,128,128]{2,1,0:T(8,128)(2,1)S(1)}, bf16[3,128,128]{2,1,0:T(8,128)(2,1)S(1)}, u32[]{:S(2)}, u32[]{:S(2)}) %collective-permute-start.12) | collective-permute-done | bytes 98336 | tf_op jit(solution)/shard_map/ppermute | solution.py:80
  39.6 0.0 collective-permute-done.13.refs_2_
  39.6 0.5 %collective-permute-done.18 = bf16[1,128,512]{2,1,0:T(8,128)(2,1)S(1)} collective-permute-done((bf16[1,128,512]{2,1,0:T(8,128)(2,1)S(1)}, bf16[1,128,512]{2,1,0:T(8,128)(2,1)S(1)}, u32[]{:S(2)}, u32[]{:S(2)}) %collective-permute-start.18) | collective-permute-done | bytes 131104 | tf_op jit(solution)/shard_map/ppermute | solution.py:80
  40.1 0.9 %shard_map.102 = (bf16[128,512]{1,0:T(8,128)(2,1)}, bf16[128,512]{1,0:T(8,128)(2,1)}, bf16[128,512]{1,0:T(8,128)(2,1)}, bf16[128,512]{1,0:T(8,128)(2,1)}) custom-call(bf16[3,128,128]{2,1,0:T(8,128)(2,1)S(1)} %collective-permute-done.11.refs_0_, bf16[3,128,128]{2,1,0:T(8,128)(2,1)S(1)} %collective-permute-done.12.refs_1_, ...), custom_call_target="tpu_custom_call" | custom-call | bytes 1310720 | tf_op jit(solution)/shard_map/pallas_call | solution.py:29
  (15 shorter events, 0.1 us)
Async XLA Ops:
  0.6 8.2 %collective-permute-start.3 = (bf16[128,512]{1,0:T(8,128)(2,1)}, bf16[128,512]{1,0:T(8,128)(2,1)S(1)}, u32[]{:S(2)}, u32[]{:S(2)}) collective-permute-start(bf16[128,512]{1,0:T(8,128)(2,1)} %refs_0_.1), channel_id=1, source_target_pairs={{0,2},{1,3},{2,0},{3,1},{4,6},{5,7},{6,4},{7,5},{8,10},{9,11},{10,... | collective-permute-start | bytes 393224 | tf_op jit(solution)/shard_map/ppermute | solution.py:80
  3.6 5.2 %collective-permute-start.4 = (bf16[128,512]{1,0:T(8,128)(2,1)}, bf16[128,512]{1,0:T(8,128)(2,1)S(1)}, u32[]{:S(2)}, u32[]{:S(2)}) collective-permute-start(bf16[128,512]{1,0:T(8,128)(2,1)} %refs_0_.1), channel_id=1, source_target_pairs={{0,1},{1,0},{2,3},{3,2},{4,5},{5,4},{6,7},{7,6},{8,9},{9,8},{10,11... | collective-permute-start | bytes 393224 | tf_op jit(solution)/shard_map/ppermute | solution.py:80
  5.3 6.8 %collective-permute-start = (bf16[3,128,128]{2,1,0:T(8,128)(2,1)}, bf16[3,128,128]{2,1,0:T(8,128)(2,1)S(1)}, u32[]{:S(2)}, u32[]{:S(2)}) collective-permute-start(bf16[3,128,128]{2,1,0:T(8,128)(2,1)} %get-tuple-element.33), channel_id=1, source_target_pairs={{0,12},{4,8},{8,4},{12,0},{16,28},{20,24},{24,20},{28,16},{1,13},{... | collective-permute-start | bytes 294920 | tf_op jit(solution)/shard_map/ppermute | solution.py:80
  7.9 5.9 %collective-permute-start.1 = (bf16[3,128,128]{2,1,0:T(8,128)(2,1)}, bf16[3,128,128]{2,1,0:T(8,128)(2,1)S(1)}, u32[]{:S(2)}, u32[]{:S(2)}) collective-permute-start(bf16[3,128,128]{2,1,0:T(8,128)(2,1)} %get-tuple-element.34), channel_id=1, source_target_pairs={{0,8},{4,12},{8,0},{12,4},{16,24},{20,28},{24,16},{28,20},{1,9},{5... | collective-permute-start | bytes 294920 | tf_op jit(solution)/shard_map/ppermute | solution.py:80
  8.4 1.9 %copy-start = (bf16[512,2048]{1,0:T(8,128)(2,1)S(1)}, bf16[512,2048]{1,0:T(8,128)(2,1)}, u32[]{:S(2)}) copy-start(bf16[512,2048]{1,0:T(8,128)(2,1)} %refs_4_.5) | copy-start | bytes 6291460
  8.4 1.9 %copy-start.5 = (bf16[128,512]{1,0:T(8,128)(2,1)S(1)}, bf16[128,512]{1,0:T(8,128)(2,1)}, u32[]{:S(2)}) copy-start(bf16[128,512]{1,0:T(8,128)(2,1)} %refs_0_.1) | copy-start | bytes 393220
  8.4 5.5 %collective-permute-start.2 = (bf16[3,128,128]{2,1,0:T(8,128)(2,1)}, bf16[3,128,128]{2,1,0:T(8,128)(2,1)S(1)}, u32[]{:S(2)}, u32[]{:S(2)}) collective-permute-start(bf16[3,128,128]{2,1,0:T(8,128)(2,1)} %get-tuple-element.35), channel_id=1, source_target_pairs={{0,4},{4,0},{8,12},{12,8},{16,20},{20,16},{24,28},{28,24},{1,5},{5... | collective-permute-start | bytes 294920 | tf_op jit(solution)/shard_map/ppermute | solution.py:80
  8.9 1.3 %collective-permute-start.5 = (bf16[128,512]{1,0:T(8,128)(2,1)S(1)}, bf16[128,512]{1,0:T(8,128)(2,1)S(1)}, u32[]{:S(2)}, u32[]{:S(2)}) collective-permute-start(bf16[128,512]{1,0:T(8,128)(2,1)S(1)} %collective-permute-done.3.refs_1_), channel_id=1, source_target_pairs={{0,1},{1,0},{2,3},{3,2},{4,5},{5,4},{6,7},{7,6},{8,9},{9,8},{10,11... | collective-permute-start | bytes 393224 | tf_op jit(solution)/shard_map/ppermute | solution.py:80
  8.9 5.0 %copy-start.1 = (bf16[4,128,256]{2,1,0:T(8,128)(2,1)S(1)}, bf16[4,128,256]{2,1,0:T(8,128)(2,1)}, u32[]{:S(2)}) copy-start(bf16[4,128,256]{2,1,0:T(8,128)(2,1)} %om_ref.5) | copy-start | bytes 786436
  8.9 5.0 %copy-start.2 = (bf16[128,512]{1,0:T(8,128)(2,1)S(1)}, bf16[128,512]{1,0:T(8,128)(2,1)}, u32[]{:S(2)}) copy-start(bf16[128,512]{1,0:T(8,128)(2,1)} %refs_3_.1) | copy-start | bytes 393220
  8.9 5.0 %copy-start.3 = (bf16[128,512]{1,0:T(8,128)(2,1)S(1)}, bf16[128,512]{1,0:T(8,128)(2,1)}, u32[]{:S(2)}) copy-start(bf16[128,512]{1,0:T(8,128)(2,1)} %refs_4_.4) | copy-start | bytes 393220
  8.9 5.0 %copy-start.4 = (bf16[128,512]{1,0:T(8,128)(2,1)S(1)}, bf16[128,512]{1,0:T(8,128)(2,1)}, u32[]{:S(2)}) copy-start(bf16[128,512]{1,0:T(8,128)(2,1)} %refs_5_.1) | copy-start | bytes 393220
  14.4 9.5 %collective-permute-start.9 = (bf16[128,256]{1,0:T(8,128)(2,1)S(1)}, bf16[128,256]{1,0:T(8,128)(2,1)S(1)}, u32[]{:S(2)}, u32[]{:S(2)}) collective-permute-start(bf16[128,256]{1,0:T(8,128)(2,1)S(1)} %get-tuple-element.45), channel_id=1, source_target_pairs={{0,16},{4,20},{8,24},{12,28},{16,0},{20,4},{24,8},{28,12},{1,17},{... | collective-permute-start | bytes 196616 | tf_op jit(solution)/shard_map/ppermute | solution.py:80
  17.0 5.2 %collective-permute-start.6 = (bf16[128,128]{1,0:T(8,128)(2,1)S(1)}, bf16[128,128]{1,0:T(8,128)(2,1)S(1)}, u32[]{:S(2)}, u32[]{:S(2)}) collective-permute-start(bf16[128,128]{1,0:T(8,128)(2,1)S(1)} %get-tuple-element.41), channel_id=1, source_target_pairs={{0,12},{4,8},{8,4},{12,0},{16,28},{20,24},{24,20},{28,16},{1,13},{... | collective-permute-start | bytes 98312 | tf_op jit(solution)/shard_map/ppermute | solution.py:80
  19.5 3.9 %collective-permute-start.7 = (bf16[128,128]{1,0:T(8,128)(2,1)S(1)}, bf16[128,128]{1,0:T(8,128)(2,1)S(1)}, u32[]{:S(2)}, u32[]{:S(2)}) collective-permute-start(bf16[128,128]{1,0:T(8,128)(2,1)S(1)} %get-tuple-element.42), channel_id=1, source_target_pairs={{0,8},{4,12},{8,0},{12,4},{16,24},{20,28},{24,16},{28,20},{1,9},{5... | collective-permute-start | bytes 98312 | tf_op jit(solution)/shard_map/ppermute | solution.py:80
  19.9 3.9 %collective-permute-start.8 = (bf16[128,128]{1,0:T(8,128)(2,1)S(1)}, bf16[128,128]{1,0:T(8,128)(2,1)S(1)}, u32[]{:S(2)}, u32[]{:S(2)}) collective-permute-start(bf16[128,128]{1,0:T(8,128)(2,1)S(1)} %get-tuple-element.43), channel_id=1, source_target_pairs={{0,4},{4,0},{8,12},{12,8},{16,20},{20,16},{24,28},{28,24},{1,5},{5... | collective-permute-start | bytes 98312 | tf_op jit(solution)/shard_map/ppermute | solution.py:80
  24.5 5.2 %collective-permute-start.10 = (bf16[128,256]{1,0:T(8,128)(2,1)S(1)}, bf16[128,256]{1,0:T(8,128)(2,1)S(1)}, u32[]{:S(2)}, u32[]{:S(2)}) collective-permute-start(bf16[128,256]{1,0:T(8,128)(2,1)S(1)} %get-tuple-element.51), channel_id=1, source_target_pairs={{0,16},{4,20},{8,24},{12,28},{16,0},{20,4},{24,8},{28,12},{1,17},{... | collective-permute-start | bytes 196616 | tf_op jit(solution)/shard_map/ppermute | solution.py:80
  24.9 5.4 %collective-permute-start.14 = (bf16[128,128]{1,0:T(8,128)(2,1)S(1)}, bf16[128,128]{1,0:T(8,128)(2,1)S(1)}, u32[]{:S(2)}, u32[]{:S(2)}) collective-permute-start(bf16[128,128]{1,0:T(8,128)(2,1)S(1)} %get-tuple-element.56), channel_id=1, source_target_pairs={{0,12},{4,8},{8,4},{12,0},{16,28},{20,24},{24,20},{28,16},{1,13},{... | collective-permute-start | bytes 98312 | tf_op jit(solution)/shard_map/ppermute | solution.py:80
  26.5 3.9 %collective-permute-start.15 = (bf16[128,128]{1,0:T(8,128)(2,1)S(1)}, bf16[128,128]{1,0:T(8,128)(2,1)S(1)}, u32[]{:S(2)}, u32[]{:S(2)}) collective-permute-start(bf16[128,128]{1,0:T(8,128)(2,1)S(1)} %get-tuple-element.57), channel_id=1, source_target_pairs={{0,8},{4,12},{8,0},{12,4},{16,24},{20,28},{24,16},{28,20},{1,9},{5... | collective-permute-start | bytes 98312 | tf_op jit(solution)/shard_map/ppermute | solution.py:80
  26.9 3.9 %collective-permute-start.16 = (bf16[128,128]{1,0:T(8,128)(2,1)S(1)}, bf16[128,128]{1,0:T(8,128)(2,1)S(1)}, u32[]{:S(2)}, u32[]{:S(2)}) collective-permute-start(bf16[128,128]{1,0:T(8,128)(2,1)S(1)} %get-tuple-element.58), channel_id=1, source_target_pairs={{0,4},{4,0},{8,12},{12,8},{16,20},{20,16},{24,28},{28,24},{1,5},{5... | collective-permute-start | bytes 98312 | tf_op jit(solution)/shard_map/ppermute | solution.py:80
  31.3 3.6 %collective-permute-start.17 = (bf16[2,128,512]{2,1,0:T(8,128)(2,1)S(1)}, bf16[2,128,512]{2,1,0:T(8,128)(2,1)S(1)}, u32[]{:S(2)}, u32[]{:S(2)}) collective-permute-start(bf16[2,128,512]{2,1,0:T(8,128)(2,1)S(1)} %get-tuple-element.61), channel_id=1, source_target_pairs={{0,1},{1,0},{2,3},{3,2},{4,5},{5,4},{6,7},{7,6},{8,9},{9,8},{10,11... | collective-permute-start | bytes 786440 | tf_op jit(solution)/shard_map/ppermute | solution.py:80
  31.4 6.6 %collective-permute-start.11 = (bf16[3,128,128]{2,1,0:T(8,128)(2,1)S(1)}, bf16[3,128,128]{2,1,0:T(8,128)(2,1)S(1)}, u32[]{:S(2)}, u32[]{:S(2)}) collective-permute-start(bf16[3,128,128]{2,1,0:T(8,128)(2,1)S(1)} %get-tuple-element.52), channel_id=1, source_target_pairs={{0,12},{4,8},{8,4},{12,0},{16,28},{20,24},{24,20},{28,16},{1,13},{... | collective-permute-start | bytes 294920 | tf_op jit(solution)/shard_map/ppermute | solution.py:80
  33.9 5.7 %collective-permute-start.12 = (bf16[3,128,128]{2,1,0:T(8,128)(2,1)S(1)}, bf16[3,128,128]{2,1,0:T(8,128)(2,1)S(1)}, u32[]{:S(2)}, u32[]{:S(2)}) collective-permute-start(bf16[3,128,128]{2,1,0:T(8,128)(2,1)S(1)} %get-tuple-element.53), channel_id=1, source_target_pairs={{0,8},{4,12},{8,0},{12,4},{16,24},{20,28},{24,16},{28,20},{1,9},{5... | collective-permute-start | bytes 294920 | tf_op jit(solution)/shard_map/ppermute | solution.py:80
  34.4 5.2 %collective-permute-start.13 = (bf16[3,128,128]{2,1,0:T(8,128)(2,1)S(1)}, bf16[3,128,128]{2,1,0:T(8,128)(2,1)S(1)}, u32[]{:S(2)}, u32[]{:S(2)}) collective-permute-start(bf16[3,128,128]{2,1,0:T(8,128)(2,1)S(1)} %get-tuple-element.54), channel_id=1, source_target_pairs={{0,4},{4,0},{8,12},{12,8},{16,20},{20,16},{24,28},{28,24},{1,5},{5... | collective-permute-start | bytes 294920 | tf_op jit(solution)/shard_map/ppermute | solution.py:80
  35.0 5.1 %collective-permute-start.18 = (bf16[1,128,512]{2,1,0:T(8,128)(2,1)S(1)}, bf16[1,128,512]{2,1,0:T(8,128)(2,1)S(1)}, u32[]{:S(2)}, u32[]{:S(2)}) collective-permute-start(bf16[1,128,512]{2,1,0:T(8,128)(2,1)S(1)} %fusion), channel_id=1, source_target_pairs={{0,2},{1,3},{2,0},{3,1},{4,6},{5,7},{6,4},{7,5},{8,10},{9,11},{10,... | collective-permute-start | bytes 393224 | tf_op jit(solution)/shard_map/ppermute | solution.py:80

commit v11 on v10

--- a/solution.py
+++ b/solution.py
@@ -33,7 +33,7 @@
         out_specs=out_specs or [VMEM] * len(outs),
         scratch_shapes=list(scratch),
         cost_estimate=pl.CostEstimate(flops=flops, bytes_accessed=size, transcendentals=0),
-        compiler_params=pltpu.CompilerParams(vmem_limit_bytes=vmem * 1024 * 1024),
+        compiler_params=pltpu.CompilerParams(vmem_limit_bytes=int(vmem * 1024 * 1024)),
     )(*args)
 
 
@@ -125,24 +125,18 @@
 
 
 def pack_kernel(n, q_ref, k_ref, v_ref, *rest):
-    outs, (scr, in_sems, out_sems) = rest[:-3], rest[-3:]
+    outs, sems = rest[:-1], rest[-1]
     r = member(n)
-    dim = scr.shape[3]
-    loads, stores = [], []
-    for k, out in enumerate(outs, 1):
-        for at, ref in enumerate((q_ref, k_ref, v_ref)):
-            here = scr.at[k - 1, at]
-            loads.append(
-                pltpu.make_async_copy(ref.at[:, lane(r ^ k, dim)], here, in_sems.at[k - 1, at])
-            )
-            stores.append(pltpu.make_async_copy(here, out.at[at], out_sems.at[k - 1, at]))
-    for load in loads:
-        load.start()
-    for load, store in zip(loads, stores):
-        load.wait()
-        store.start()
-    for store in stores:
-        store.wait()
+    dim = outs[0].shape[2]
+    copies = [
+        pltpu.make_async_copy(ref.at[:, lane(r ^ k, dim)], out.at[at], sems.at[k - 1, at])
+        for k, out in enumerate(outs, 1)
+        for at, ref in enumerate((q_ref, k_ref, v_ref))
+    ]
+    for copy in copies:
+        copy.start()
+    for copy in copies:
+        copy.wait()
 
 
 def mark_kernel(_, out_ref):
@@ -317,12 +311,7 @@
         functools.partial(pack_kernel, n),
         [struct((3, rows, dim))] * (n - 1),
         queries, key_vectors, value_vectors,
-        specs=[ANY] * 3, out_specs=[ANY] * (n - 1), vmem=60,
-        scratch=[
-            pltpu.VMEM((n - 1, 3, rows, dim), jnp.bfloat16),
-            pltpu.SemaphoreType.DMA((n - 1, 3)),
-            pltpu.SemaphoreType.DMA((n - 1, 3)),
-        ],
+        specs=[ANY] * 3, scratch=[pltpu.SemaphoreType.DMA((n - 1, 3))], vmem=53.62,
     )
     got = exchange(sends)
     (mark,) = call(mark_kernel, [struct((8, 128), f32)], blocks[offsets.index(1)], specs=[ANY], flops=10**10)

time: 41.2 us -> 40.3 us (0.978)
  Pallas kernels: 7.05 us -> 6.35 us
    pallas_call x10, Pallas kernels: 7.05 us -> 6.35 us  [call(): pl.pallas_call(body, out_shape=outs, in_specs=specs or [VMEM] * len(args)...]
  transfers between devices with their start and end apart: 19 -> 19, of which waited for: 12 -> 12; matrix products, arithmetic and copies ran while one was open for 0% -> 0% of each run, Pallas kernels for 11% -> 10%
where the time goes in v11:
time: 40.3 us; the launch traced here: 40.1 us
  starting transfers between devices  20.8 us (52%)
  waiting for transfers between devices  12 us (30%)
  Pallas kernels  6.35 us (16%)
  between operations  0.8 us (2%)
    ppermute x19, starting transfers between devices, swap(): return lax.ppermute(array, axis, [(i, i ^ bit) for i in range(size)])  20.8 us
    ppermute x19, waiting for transfers between devices, swap(): return lax.ppermute(array, axis, [(i, i ^ bit) for i in range(size)])  12 us
    pallas_call x10, Pallas kernels, call(): pl.pallas_call(body, out_shape=outs, in_specs=specs or [VMEM] * len(args)...  6.35 us
  transfers between devices with their start and end apart: 19, of which 12 were waited for; matrix products, arithmetic and copies ran while one was open for 0% of the time, Pallas kernels for 10%

profile of v11, /device:TPU:0, one launch (start us, length us, event | category | flops | bytes accessed | tf_op | source)
XLA Modules:
  0.0 40.1 jit_solution(808796090387294581)
XLA Ops:
  0.6 3.0 %collective-permute-start.3 = (bf16[128,512]{1,0:T(8,128)(2,1)}, bf16[128,512]{1,0:T(8,128)(2,1)S(1)}, u32[]{:S(2)}, u32[]{:S(2)}) collective-permute-start(bf16[128,512]{1,0:T(8,128)(2,1)} %refs_0_.1), channel_id=1, source_target_pairs={{0,2},{1,3},{2,0},{3,1},{4,6},{5,7},{6,4},{7,5},{8,10},{9,11},{10,... | collective-permute-start | bytes 393224 | tf_op jit(solution)/shard_map/ppermute | solution.py:80
  3.6 0.0 collective-permute-start.4
  3.6 1.0 %shard_map.93 = (bf16[3,128,128]{2,1,0:T(8,128)(2,1)S(1)}, bf16[3,128,128]{2,1,0:T(8,128)(2,1)S(1)}, bf16[3,128,128]{2,1,0:T(8,128)(2,1)S(1)}) custom-call(bf16[128,512]{1,0:T(8,128)(2,1)} %refs_3_.1, bf16[128,512]{1,0:T(8,128)(2,1)} %refs_4_.4, bf16[128,512]{1,0:T(8,128)(2,1)} %refs_5_.1), custom_call_target="tpu_custom_call" | custom-call | bytes 688128 | tf_op jit(solution)/shard_map/pallas_call | solution.py:29
  4.6 2.6 %collective-permute-start = (bf16[3,128,128]{2,1,0:T(8,128)(2,1)S(1)}, bf16[3,128,128]{2,1,0:T(8,128)(2,1)S(1)}, u32[]{:S(2)}, u32[]{:S(2)}) collective-permute-start(bf16[3,128,128]{2,1,0:T(8,128)(2,1)S(1)} %get-tuple-element.33), channel_id=1, source_target_pairs={{0,12},{4,8},{8,4},{12,0},{16,28},{20,24},{24,20},{28,16},{1,13},{... | collective-permute-start | bytes 294920 | tf_op jit(solution)/shard_map/ppermute | solution.py:80
  7.2 0.4 %collective-permute-start.1 = (bf16[3,128,128]{2,1,0:T(8,128)(2,1)S(1)}, bf16[3,128,128]{2,1,0:T(8,128)(2,1)S(1)}, u32[]{:S(2)}, u32[]{:S(2)}) collective-permute-start(bf16[3,128,128]{2,1,0:T(8,128)(2,1)S(1)} %get-tuple-element.34), channel_id=1, source_target_pairs={{0,8},{4,12},{8,0},{12,4},{16,24},{20,28},{24,16},{28,20},{1,9},{5... | collective-permute-start | bytes 294920 | tf_op jit(solution)/shard_map/ppermute | solution.py:80
  7.7 0.5 %collective-permute-start.2 = (bf16[3,128,128]{2,1,0:T(8,128)(2,1)S(1)}, bf16[3,128,128]{2,1,0:T(8,128)(2,1)S(1)}, u32[]{:S(2)}, u32[]{:S(2)}) collective-permute-start(bf16[3,128,128]{2,1,0:T(8,128)(2,1)S(1)} %get-tuple-element.35), channel_id=1, source_target_pairs={{0,4},{4,0},{8,12},{12,8},{16,20},{20,16},{24,28},{28,24},{1,5},{5... | collective-permute-start | bytes 294920 | tf_op jit(solution)/shard_map/ppermute | solution.py:80
  8.2 0.0 collective-permute-done.3.refs_1_
  8.2 0.0 collective-permute-start.5
  8.2 0.0 collective-permute-done.4._.refs_2_
  8.2 0.0 copy-start.1
  8.2 0.0 copy-start.2
  8.2 0.0 copy-start.3
  8.2 0.0 copy-start.4
  8.2 1.3 %collective-permute-done.5.refs_3_ = bf16[128,512]{1,0:T(8,128)(2,1)S(1)} collective-permute-done((bf16[128,512]{1,0:T(8,128)(2,1)S(1)}, bf16[128,512]{1,0:T(8,128)(2,1)S(1)}, u32[]{:S(2)}, u32[]{:S(2)}) %collective-permute-start.5) | collective-permute-done | bytes 131104 | tf_op jit(solution)/shard_map/ppermute | solution.py:80
  9.5 0.9 %shard_map.95 = (bf16[128,128]{1,0:T(8,128)(2,1)S(1)}, bf16[128,128]{1,0:T(8,128)(2,1)S(1)}, bf16[128,128]{1,0:T(8,128)(2,1)S(1)}, bf16[128,128]{1,0:T(8,128)(2,1)S(1)}) custom-call(bf16[128,512]{1,0:T(8,128)(2,1)S(1)} %copy-done.5, bf16[128,512]{1,0:T(8,128)(2,1)S(1)} %collective-permute-done.3.refs_1_, ...), custom_call_target="tpu_custom_call" | custom-call | flops 268435456 | bytes 2756608 | tf_op jit(solution)/shard_map/pallas_call | solution.py:29
  10.4 0.8 %collective-permute-done.refs_0_ = bf16[3,128,128]{2,1,0:T(8,128)(2,1)S(1)} collective-permute-done((bf16[3,128,128]{2,1,0:T(8,128)(2,1)S(1)}, bf16[3,128,128]{2,1,0:T(8,128)(2,1)S(1)}, u32[]{:S(2)}, u32[]{:S(2)}) %collective-permute-start) | collective-permute-done | bytes 98336 | tf_op jit(solution)/shard_map/ppermute | solution.py:80
  11.2 1.8 %collective-permute-done.1.refs_1_ = bf16[3,128,128]{2,1,0:T(8,128)(2,1)S(1)} collective-permute-done((bf16[3,128,128]{2,1,0:T(8,128)(2,1)S(1)}, bf16[3,128,128]{2,1,0:T(8,128)(2,1)S(1)}, u32[]{:S(2)}, u32[]{:S(2)}) %collective-permute-start.1) | collective-permute-done | bytes 98336 | tf_op jit(solution)/shard_map/ppermute | solution.py:80
  13.0 0.5 %shard_map.96 = (bf16[3,512,128]{2,1,0:T(8,128)(2,1)S(1)}, bf16[512,256]{1,0:T(8,128)(2,1)S(1)}, bf16[128,256]{1,0:T(8,128)(2,1)S(1)}) custom-call(bf16[3,128,128]{2,1,0:T(8,128)(2,1)S(1)} %collective-permute-done.refs_0_, bf16[3,128,128]{2,1,0:T(8,128)(2,1)S(1)} %collective-permute-done.1.refs_1_, bf16[3,128,128]{2,1,0:T(8,128)(2,1)S(1)} %collective-permute-done.2.refs_2_, ...), custom_call_target="tpu_custom_call" | custom-call | flops 67108864 | bytes 1703936 | tf_op jit(solution)/shard_map/pallas_call | solution.py:29
  13.5 2.7 %collective-permute-start.9 = (bf16[128,256]{1,0:T(8,128)(2,1)S(1)}, bf16[128,256]{1,0:T(8,128)(2,1)S(1)}, u32[]{:S(2)}, u32[]{:S(2)}) collective-permute-start(bf16[128,256]{1,0:T(8,128)(2,1)S(1)} %get-tuple-element.45), channel_id=1, source_target_pairs={{0,16},{4,20},{8,24},{12,28},{16,0},{20,4},{24,8},{28,12},{1,17},{... | collective-permute-start | bytes 196616 | tf_op jit(solution)/shard_map/ppermute | solution.py:80
  16.1 2.5 %collective-permute-start.6 = (bf16[128,128]{1,0:T(8,128)(2,1)S(1)}, bf16[128,128]{1,0:T(8,128)(2,1)S(1)}, u32[]{:S(2)}, u32[]{:S(2)}) collective-permute-start(bf16[128,128]{1,0:T(8,128)(2,1)S(1)} %get-tuple-element.41), channel_id=1, source_target_pairs={{0,12},{4,8},{8,4},{12,0},{16,28},{20,24},{24,20},{28,16},{1,13},{... | collective-permute-start | bytes 98312 | tf_op jit(solution)/shard_map/ppermute | solution.py:80
  18.6 0.5 %collective-permute-start.7 = (bf16[128,128]{1,0:T(8,128)(2,1)S(1)}, bf16[128,128]{1,0:T(8,128)(2,1)S(1)}, u32[]{:S(2)}, u32[]{:S(2)}) collective-permute-start(bf16[128,128]{1,0:T(8,128)(2,1)S(1)} %get-tuple-element.42), channel_id=1, source_target_pairs={{0,8},{4,12},{8,0},{12,4},{16,24},{20,28},{24,16},{28,20},{1,9},{5... | collective-permute-start | bytes 98312 | tf_op jit(solution)/shard_map/ppermute | solution.py:80
  19.0 0.6 %collective-permute-start.8 = (bf16[128,128]{1,0:T(8,128)(2,1)S(1)}, bf16[128,128]{1,0:T(8,128)(2,1)S(1)}, u32[]{:S(2)}, u32[]{:S(2)}) collective-permute-start(bf16[128,128]{1,0:T(8,128)(2,1)S(1)} %get-tuple-element.43), channel_id=1, source_target_pairs={{0,4},{4,0},{8,12},{12,8},{16,20},{20,16},{24,28},{28,24},{1,5},{5... | collective-permute-start | bytes 98312 | tf_op jit(solution)/shard_map/ppermute | solution.py:80
  19.6 0.5 %shard_map.97 = (bf16[512,256]{1,0:T(8,128)(2,1)S(1)}, bf16[512,512]{1,0:T(8,128)(2,1)S(1)}, f32[512,128]{1,0:T(8,128)S(1)}) custom-call(bf16[3,512,128]{2,1,0:T(8,128)(2,1)S(1)} %get-tuple-element.37.qkv_ref, bf16[4,128,256]{2,1,0:T(8,128)(2,1)S(1)} %copy-done.1, bf16[512,256]{1,0:T(8,128)(2,1)S(1)} %get-tuple-element.38.kf_ref), custom_call_target="tpu_custom_call" | custom-call | flops 134217728 | bytes 1966080 | tf_op jit(solution)/shard_map/pallas_call | solution.py:29
  20.1 1.2 %collective-permute-done.6.refs_0_ = bf16[128,128]{1,0:T(8,128)(2,1)S(1)} collective-permute-done((bf16[128,128]{1,0:T(8,128)(2,1)S(1)}, bf16[128,128]{1,0:T(8,128)(2,1)S(1)}, u32[]{:S(2)}, u32[]{:S(2)}) %collective-permute-start.6) | collective-permute-done | bytes 32800 | tf_op jit(solution)/shard_map/ppermute | solution.py:80
  21.3 1.1 %collective-permute-done.7.refs_1_ = bf16[128,128]{1,0:T(8,128)(2,1)S(1)} collective-permute-done((bf16[128,128]{1,0:T(8,128)(2,1)S(1)}, bf16[128,128]{1,0:T(8,128)(2,1)S(1)}, u32[]{:S(2)}, u32[]{:S(2)}) %collective-permute-start.7) | collective-permute-done | bytes 32800 | tf_op jit(solution)/shard_map/ppermute | solution.py:80
  22.5 0.5 %collective-permute-done.8.refs_2_ = bf16[128,128]{1,0:T(8,128)(2,1)S(1)} collective-permute-done((bf16[128,128]{1,0:T(8,128)(2,1)S(1)}, bf16[128,128]{1,0:T(8,128)(2,1)S(1)}, u32[]{:S(2)}, u32[]{:S(2)}) %collective-permute-start.8) | collective-permute-done | bytes 32800 | tf_op jit(solution)/shard_map/ppermute | solution.py:80
  22.9 0.6 %shard_map.98 = (bf16[128,256]{1,0:T(8,128)(2,1)S(1)}, bf16[512,128]{1,0:T(8,128)(2,1)S(1)}, bf16[128,256]{1,0:T(8,128)(2,1)S(1)}, bf16[128,128]{1,0:T(8,128)(2,...) custom-call(bf16[128,128]{1,0:T(8,128)(2,1)S(1)} %collective-permute-done.6.refs_0_, ...), custom_call_target="tpu_custom_call" | custom-call | flops 67108864 | bytes 1114112 | tf_op jit(solution)/shard_map/pallas_call | solution.py:29
  23.6 0.4 collective-permute-start.10
  24.0 1.6 %collective-permute-start.14 = (bf16[128,128]{1,0:T(8,128)(2,1)S(1)}, bf16[128,128]{1,0:T(8,128)(2,1)S(1)}, u32[]{:S(2)}, u32[]{:S(2)}) collective-permute-start(bf16[128,128]{1,0:T(8,128)(2,1)S(1)} %get-tuple-element.56), channel_id=1, source_target_pairs={{0,12},{4,8},{8,4},{12,0},{16,28},{20,24},{24,20},{28,16},{1,13},{... | collective-permute-start | bytes 98312 | tf_op jit(solution)/shard_map/ppermute | solution.py:80
  25.6 0.4 %collective-permute-start.15 = (bf16[128,128]{1,0:T(8,128)(2,1)S(1)}, bf16[128,128]{1,0:T(8,128)(2,1)S(1)}, u32[]{:S(2)}, u32[]{:S(2)}) collective-permute-start(bf16[128,128]{1,0:T(8,128)(2,1)S(1)} %get-tuple-element.57), channel_id=1, source_target_pairs={{0,8},{4,12},{8,0},{12,4},{16,24},{20,28},{24,16},{28,20},{1,9},{5... | collective-permute-start | bytes 98312 | tf_op jit(solution)/shard_map/ppermute | solution.py:80
  26.0 1.5 %collective-permute-start.16 = (bf16[128,128]{1,0:T(8,128)(2,1)S(1)}, bf16[128,128]{1,0:T(8,128)(2,1)S(1)}, u32[]{:S(2)}, u32[]{:S(2)}) collective-permute-start(bf16[128,128]{1,0:T(8,128)(2,1)S(1)} %get-tuple-element.58), channel_id=1, source_target_pairs={{0,4},{4,0},{8,12},{12,8},{16,20},{20,16},{24,28},{28,24},{1,5},{5... | collective-permute-start | bytes 98312 | tf_op jit(solution)/shard_map/ppermute | solution.py:80
  27.5 1.0 %shard_map.99 = (bf16[512,128]{1,0:T(8,128)(2,1)S(1)}, f32[512,128]{1,0:T(8,128)S(1)}, f32[512,256]{1,0:T(8,128)S(1)}) custom-call(bf16[3,512,128]{2,1,0:T(8,128)(2,1)S(1)} %get-tuple-element.37.qkv_ref, bf16[4,128,256]{2,1,0:T(8,128)(2,1)S(1)} %copy-done.1, bf16[512,256]{1,0:T(8,128)(2,1)S(1)} %get-tuple-element.38.kf_ref, ...), custom_call_target="tpu_custom_call" | custom-call | flops 268435456 | bytes 2818048 | tf_op jit(solution)/shard_map/pallas_call | solution.py:29
  28.4 0.4 collective-permute-done.10.rest_0_
  28.8 0.6 %shard_map.100 = (bf16[3,128,128]{2,1,0:T(8,128)(2,1)S(1)}, bf16[3,128,128]{2,1,0:T(8,128)(2,1)S(1)}, bf16[3,128,128]{2,1,0:T(8,128)(2,1)S(1)}, bf16[3,128,128]{2,1,0:T(8,128)(2,1)S(1)}) custom-call(bf16[3,512,128]{2,1,0:T(8,128)(2,1)S(1)} %get-tuple-element.37.qkv_ref, bf16[4,128,256]{2,1,0:T(8,128)(2,1)S(1)} %copy-done.1, ...), custom_call_target="tpu_custom_call" | custom-call | flops 100663296 | bytes 2293760 | tf_op jit(solution)/shard_map/pallas_call | solution.py:29
  29.4 0.1 collective-permute-done.15.refs_1_
  29.5 0.4 %collective-permute-done.16.refs_2_ = bf16[128,128]{1,0:T(8,128)(2,1)S(1)} collective-permute-done((bf16[128,128]{1,0:T(8,128)(2,1)S(1)}, bf16[128,128]{1,0:T(8,128)(2,1)S(1)}, u32[]{:S(2)}, u32[]{:S(2)}) %collective-permute-start.16) | collective-permute-done | bytes 32800 | tf_op jit(solution)/shard_map/ppermute | solution.py:80
  29.9 0.5 %shard_map.101 = (bf16[2,128,512]{2,1,0:T(8,128)(2,1)S(1)}, bf16[2,128,512]{2,1,0:T(8,128)(2,1)S(1)}) custom-call(bf16[128,128]{1,0:T(8,128)(2,1)S(1)} %collective-permute-done.14.refs_0_, bf16[128,128]{1,0:T(8,128)(2,1)S(1)} %collective-permute-done.15.refs_1_, bf16[128,128]{1,0:T(8,128)(2,1)S(1)} %collective-permute-done.16.refs_2_, ...), custom_call_target="tpu_custom_call" | custom-call | flops 268435456 | bytes 2850816 | tf_op jit(solution)/shard_map/pallas_call | solution.py:29
  30.4 0.1 collective-permute-start.17
  30.5 2.5 %collective-permute-start.11 = (bf16[3,128,128]{2,1,0:T(8,128)(2,1)S(1)}, bf16[3,128,128]{2,1,0:T(8,128)(2,1)S(1)}, u32[]{:S(2)}, u32[]{:S(2)}) collective-permute-start(bf16[3,128,128]{2,1,0:T(8,128)(2,1)S(1)} %get-tuple-element.52), channel_id=1, source_target_pairs={{0,12},{4,8},{8,4},{12,0},{16,28},{20,24},{24,20},{28,16},{1,13},{... | collective-permute-start | bytes 294920 | tf_op jit(solution)/shard_map/ppermute | solution.py:80
  33.0 0.4 %collective-permute-start.12 = (bf16[3,128,128]{2,1,0:T(8,128)(2,1)S(1)}, bf16[3,128,128]{2,1,0:T(8,128)(2,1)S(1)}, u32[]{:S(2)}, u32[]{:S(2)}) collective-permute-start(bf16[3,128,128]{2,1,0:T(8,128)(2,1)S(1)} %get-tuple-element.53), channel_id=1, source_target_pairs={{0,8},{4,12},{8,0},{12,4},{16,24},{20,28},{24,16},{28,20},{1,9},{5... | collective-permute-start | bytes 294920 | tf_op jit(solution)/shard_map/ppermute | solution.py:80
  33.4 0.6 %collective-permute-start.13 = (bf16[3,128,128]{2,1,0:T(8,128)(2,1)S(1)}, bf16[3,128,128]{2,1,0:T(8,128)(2,1)S(1)}, u32[]{:S(2)}, u32[]{:S(2)}) collective-permute-start(bf16[3,128,128]{2,1,0:T(8,128)(2,1)S(1)} %get-tuple-element.54), channel_id=1, source_target_pairs={{0,4},{4,0},{8,12},{12,8},{16,20},{20,16},{24,28},{28,24},{1,5},{5... | collective-permute-start | bytes 294920 | tf_op jit(solution)/shard_map/ppermute | solution.py:80
  34.0 0.1 add_bitcast_fusion
  34.1 0.6 %collective-permute-start.18 = (bf16[1,128,512]{2,1,0:T(8,128)(2,1)S(1)}, bf16[1,128,512]{2,1,0:T(8,128)(2,1)S(1)}, u32[]{:S(2)}, u32[]{:S(2)}) collective-permute-start(bf16[1,128,512]{2,1,0:T(8,128)(2,1)S(1)} %fusion), channel_id=1, source_target_pairs={{0,2},{1,3},{2,0},{3,1},{4,6},{5,7},{6,4},{7,5},{8,10},{9,11},{10,... | collective-permute-start | bytes 393224 | tf_op jit(solution)/shard_map/ppermute | solution.py:80
  34.8 2.3 %collective-permute-done.11.refs_0_ = bf16[3,128,128]{2,1,0:T(8,128)(2,1)S(1)} collective-permute-done((bf16[3,128,128]{2,1,0:T(8,128)(2,1)S(1)}, bf16[3,128,128]{2,1,0:T(8,128)(2,1)S(1)}, u32[]{:S(2)}, u32[]{:S(2)}) %collective-permute-start.11) | collective-permute-done | bytes 98336 | tf_op jit(solution)/shard_map/ppermute | solution.py:80
  37.0 1.6 %collective-permute-done.12.refs_1_ = bf16[3,128,128]{2,1,0:T(8,128)(2,1)S(1)} collective-permute-done((bf16[3,128,128]{2,1,0:T(8,128)(2,1)S(1)}, bf16[3,128,128]{2,1,0:T(8,128)(2,1)S(1)}, u32[]{:S(2)}, u32[]{:S(2)}) %collective-permute-start.12) | collective-permute-done | bytes 98336 | tf_op jit(solution)/shard_map/ppermute | solution.py:80
  38.7 0.0 collective-permute-done.13.refs_2_
  38.7 0.5 %collective-permute-done.18 = bf16[1,128,512]{2,1,0:T(8,128)(2,1)S(1)} collective-permute-done((bf16[1,128,512]{2,1,0:T(8,128)(2,1)S(1)}, bf16[1,128,512]{2,1,0:T(8,128)(2,1)S(1)}, u32[]{:S(2)}, u32[]{:S(2)}) %collective-permute-start.18) | collective-permute-done | bytes 131104 | tf_op jit(solution)/shard_map/ppermute | solution.py:80
  39.2 0.9 %shard_map.102 = (bf16[128,512]{1,0:T(8,128)(2,1)}, bf16[128,512]{1,0:T(8,128)(2,1)}, bf16[128,512]{1,0:T(8,128)(2,1)}, bf16[128,512]{1,0:T(8,128)(2,1)}) custom-call(bf16[3,128,128]{2,1,0:T(8,128)(2,1)S(1)} %collective-permute-done.11.refs_0_, bf16[3,128,128]{2,1,0:T(8,128)(2,1)S(1)} %collective-permute-done.12.refs_1_, ...), custom_call_target="tpu_custom_call" | custom-call | bytes 1310720 | tf_op jit(solution)/shard_map/pallas_call | solution.py:29
  (15 shorter events, 0.1 us)
Async XLA Ops:
  0.6 7.5 %collective-permute-start.3 = (bf16[128,512]{1,0:T(8,128)(2,1)}, bf16[128,512]{1,0:T(8,128)(2,1)S(1)}, u32[]{:S(2)}, u32[]{:S(2)}) collective-permute-start(bf16[128,512]{1,0:T(8,128)(2,1)} %refs_0_.1), channel_id=1, source_target_pairs={{0,2},{1,3},{2,0},{3,1},{4,6},{5,7},{6,4},{7,5},{8,10},{9,11},{10,... | collective-permute-start | bytes 393224 | tf_op jit(solution)/shard_map/ppermute | solution.py:80
  3.6 4.5 %collective-permute-start.4 = (bf16[128,512]{1,0:T(8,128)(2,1)}, bf16[128,512]{1,0:T(8,128)(2,1)S(1)}, u32[]{:S(2)}, u32[]{:S(2)}) collective-permute-start(bf16[128,512]{1,0:T(8,128)(2,1)} %refs_0_.1), channel_id=1, source_target_pairs={{0,1},{1,0},{2,3},{3,2},{4,5},{5,4},{6,7},{7,6},{8,9},{9,8},{10,11... | collective-permute-start | bytes 393224 | tf_op jit(solution)/shard_map/ppermute | solution.py:80
  4.6 6.6 %collective-permute-start = (bf16[3,128,128]{2,1,0:T(8,128)(2,1)S(1)}, bf16[3,128,128]{2,1,0:T(8,128)(2,1)S(1)}, u32[]{:S(2)}, u32[]{:S(2)}) collective-permute-start(bf16[3,128,128]{2,1,0:T(8,128)(2,1)S(1)} %get-tuple-element.33), channel_id=1, source_target_pairs={{0,12},{4,8},{8,4},{12,0},{16,28},{20,24},{24,20},{28,16},{1,13},{... | collective-permute-start | bytes 294920 | tf_op jit(solution)/shard_map/ppermute | solution.py:80
  7.2 5.7 %collective-permute-start.1 = (bf16[3,128,128]{2,1,0:T(8,128)(2,1)S(1)}, bf16[3,128,128]{2,1,0:T(8,128)(2,1)S(1)}, u32[]{:S(2)}, u32[]{:S(2)}) collective-permute-start(bf16[3,128,128]{2,1,0:T(8,128)(2,1)S(1)} %get-tuple-element.34), channel_id=1, source_target_pairs={{0,8},{4,12},{8,0},{12,4},{16,24},{20,28},{24,16},{28,20},{1,9},{5... | collective-permute-start | bytes 294920 | tf_op jit(solution)/shard_map/ppermute | solution.py:80
  7.7 1.9 %copy-start = (bf16[512,2048]{1,0:T(8,128)(2,1)S(1)}, bf16[512,2048]{1,0:T(8,128)(2,1)}, u32[]{:S(2)}) copy-start(bf16[512,2048]{1,0:T(8,128)(2,1)} %refs_4_.5) | copy-start | bytes 6291460
  7.7 1.9 %copy-start.5 = (bf16[128,512]{1,0:T(8,128)(2,1)S(1)}, bf16[128,512]{1,0:T(8,128)(2,1)}, u32[]{:S(2)}) copy-start(bf16[128,512]{1,0:T(8,128)(2,1)} %refs_0_.1) | copy-start | bytes 393220
  7.7 5.3 %collective-permute-start.2 = (bf16[3,128,128]{2,1,0:T(8,128)(2,1)S(1)}, bf16[3,128,128]{2,1,0:T(8,128)(2,1)S(1)}, u32[]{:S(2)}, u32[]{:S(2)}) collective-permute-start(bf16[3,128,128]{2,1,0:T(8,128)(2,1)S(1)} %get-tuple-element.35), channel_id=1, source_target_pairs={{0,4},{4,0},{8,12},{12,8},{16,20},{20,16},{24,28},{28,24},{1,5},{5... | collective-permute-start | bytes 294920 | tf_op jit(solution)/shard_map/ppermute | solution.py:80
  8.2 1.3 %collective-permute-start.5 = (bf16[128,512]{1,0:T(8,128)(2,1)S(1)}, bf16[128,512]{1,0:T(8,128)(2,1)S(1)}, u32[]{:S(2)}, u32[]{:S(2)}) collective-permute-start(bf16[128,512]{1,0:T(8,128)(2,1)S(1)} %collective-permute-done.3.refs_1_), channel_id=1, source_target_pairs={{0,1},{1,0},{2,3},{3,2},{4,5},{5,4},{6,7},{7,6},{8,9},{9,8},{10,11... | collective-permute-start | bytes 393224 | tf_op jit(solution)/shard_map/ppermute | solution.py:80
  8.2 4.8 %copy-start.1 = (bf16[4,128,256]{2,1,0:T(8,128)(2,1)S(1)}, bf16[4,128,256]{2,1,0:T(8,128)(2,1)}, u32[]{:S(2)}) copy-start(bf16[4,128,256]{2,1,0:T(8,128)(2,1)} %om_ref.5) | copy-start | bytes 786436
  8.2 4.7 %copy-start.2 = (bf16[128,512]{1,0:T(8,128)(2,1)S(1)}, bf16[128,512]{1,0:T(8,128)(2,1)}, u32[]{:S(2)}) copy-start(bf16[128,512]{1,0:T(8,128)(2,1)} %refs_3_.1) | copy-start | bytes 393220
  8.2 4.7 %copy-start.3 = (bf16[128,512]{1,0:T(8,128)(2,1)S(1)}, bf16[128,512]{1,0:T(8,128)(2,1)}, u32[]{:S(2)}) copy-start(bf16[128,512]{1,0:T(8,128)(2,1)} %refs_4_.4) | copy-start | bytes 393220
  8.2 4.7 %copy-start.4 = (bf16[128,512]{1,0:T(8,128)(2,1)S(1)}, bf16[128,512]{1,0:T(8,128)(2,1)}, u32[]{:S(2)}) copy-start(bf16[128,512]{1,0:T(8,128)(2,1)} %refs_5_.1) | copy-start | bytes 393220
  13.5 9.5 %collective-permute-start.9 = (bf16[128,256]{1,0:T(8,128)(2,1)S(1)}, bf16[128,256]{1,0:T(8,128)(2,1)S(1)}, u32[]{:S(2)}, u32[]{:S(2)}) collective-permute-start(bf16[128,256]{1,0:T(8,128)(2,1)S(1)} %get-tuple-element.45), channel_id=1, source_target_pairs={{0,16},{4,20},{8,24},{12,28},{16,0},{20,4},{24,8},{28,12},{1,17},{... | collective-permute-start | bytes 196616 | tf_op jit(solution)/shard_map/ppermute | solution.py:80
  16.1 5.2 %collective-permute-start.6 = (bf16[128,128]{1,0:T(8,128)(2,1)S(1)}, bf16[128,128]{1,0:T(8,128)(2,1)S(1)}, u32[]{:S(2)}, u32[]{:S(2)}) collective-permute-start(bf16[128,128]{1,0:T(8,128)(2,1)S(1)} %get-tuple-element.41), channel_id=1, source_target_pairs={{0,12},{4,8},{8,4},{12,0},{16,28},{20,24},{24,20},{28,16},{1,13},{... | collective-permute-start | bytes 98312 | tf_op jit(solution)/shard_map/ppermute | solution.py:80
  18.6 3.9 %collective-permute-start.7 = (bf16[128,128]{1,0:T(8,128)(2,1)S(1)}, bf16[128,128]{1,0:T(8,128)(2,1)S(1)}, u32[]{:S(2)}, u32[]{:S(2)}) collective-permute-start(bf16[128,128]{1,0:T(8,128)(2,1)S(1)} %get-tuple-element.42), channel_id=1, source_target_pairs={{0,8},{4,12},{8,0},{12,4},{16,24},{20,28},{24,16},{28,20},{1,9},{5... | collective-permute-start | bytes 98312 | tf_op jit(solution)/shard_map/ppermute | solution.py:80
  19.0 3.9 %collective-permute-start.8 = (bf16[128,128]{1,0:T(8,128)(2,1)S(1)}, bf16[128,128]{1,0:T(8,128)(2,1)S(1)}, u32[]{:S(2)}, u32[]{:S(2)}) collective-permute-start(bf16[128,128]{1,0:T(8,128)(2,1)S(1)} %get-tuple-element.43), channel_id=1, source_target_pairs={{0,4},{4,0},{8,12},{12,8},{16,20},{20,16},{24,28},{28,24},{1,5},{5... | collective-permute-start | bytes 98312 | tf_op jit(solution)/shard_map/ppermute | solution.py:80
  23.6 5.2 %collective-permute-start.10 = (bf16[128,256]{1,0:T(8,128)(2,1)S(1)}, bf16[128,256]{1,0:T(8,128)(2,1)S(1)}, u32[]{:S(2)}, u32[]{:S(2)}) collective-permute-start(bf16[128,256]{1,0:T(8,128)(2,1)S(1)} %get-tuple-element.51), channel_id=1, source_target_pairs={{0,16},{4,20},{8,24},{12,28},{16,0},{20,4},{24,8},{28,12},{1,17},{... | collective-permute-start | bytes 196616 | tf_op jit(solution)/shard_map/ppermute | solution.py:80
  24.0 5.4 %collective-permute-start.14 = (bf16[128,128]{1,0:T(8,128)(2,1)S(1)}, bf16[128,128]{1,0:T(8,128)(2,1)S(1)}, u32[]{:S(2)}, u32[]{:S(2)}) collective-permute-start(bf16[128,128]{1,0:T(8,128)(2,1)S(1)} %get-tuple-element.56), channel_id=1, source_target_pairs={{0,12},{4,8},{8,4},{12,0},{16,28},{20,24},{24,20},{28,16},{1,13},{... | collective-permute-start | bytes 98312 | tf_op jit(solution)/shard_map/ppermute | solution.py:80
  25.6 3.9 %collective-permute-start.15 = (bf16[128,128]{1,0:T(8,128)(2,1)S(1)}, bf16[128,128]{1,0:T(8,128)(2,1)S(1)}, u32[]{:S(2)}, u32[]{:S(2)}) collective-permute-start(bf16[128,128]{1,0:T(8,128)(2,1)S(1)} %get-tuple-element.57), channel_id=1, source_target_pairs={{0,8},{4,12},{8,0},{12,4},{16,24},{20,28},{24,16},{28,20},{1,9},{5... | collective-permute-start | bytes 98312 | tf_op jit(solution)/shard_map/ppermute | solution.py:80
  26.0 3.9 %collective-permute-start.16 = (bf16[128,128]{1,0:T(8,128)(2,1)S(1)}, bf16[128,128]{1,0:T(8,128)(2,1)S(1)}, u32[]{:S(2)}, u32[]{:S(2)}) collective-permute-start(bf16[128,128]{1,0:T(8,128)(2,1)S(1)} %get-tuple-element.58), channel_id=1, source_target_pairs={{0,4},{4,0},{8,12},{12,8},{16,20},{20,16},{24,28},{28,24},{1,5},{5... | collective-permute-start | bytes 98312 | tf_op jit(solution)/shard_map/ppermute | solution.py:80
  30.4 3.6 %collective-permute-start.17 = (bf16[2,128,512]{2,1,0:T(8,128)(2,1)S(1)}, bf16[2,128,512]{2,1,0:T(8,128)(2,1)S(1)}, u32[]{:S(2)}, u32[]{:S(2)}) collective-permute-start(bf16[2,128,512]{2,1,0:T(8,128)(2,1)S(1)} %get-tuple-element.61), channel_id=1, source_target_pairs={{0,1},{1,0},{2,3},{3,2},{4,5},{5,4},{6,7},{7,6},{8,9},{9,8},{10,11... | collective-permute-start | bytes 786440 | tf_op jit(solution)/shard_map/ppermute | solution.py:80
  30.5 6.6 %collective-permute-start.11 = (bf16[3,128,128]{2,1,0:T(8,128)(2,1)S(1)}, bf16[3,128,128]{2,1,0:T(8,128)(2,1)S(1)}, u32[]{:S(2)}, u32[]{:S(2)}) collective-permute-start(bf16[3,128,128]{2,1,0:T(8,128)(2,1)S(1)} %get-tuple-element.52), channel_id=1, source_target_pairs={{0,12},{4,8},{8,4},{12,0},{16,28},{20,24},{24,20},{28,16},{1,13},{... | collective-permute-start | bytes 294920 | tf_op jit(solution)/shard_map/ppermute | solution.py:80
  33.0 5.7 %collective-permute-start.12 = (bf16[3,128,128]{2,1,0:T(8,128)(2,1)S(1)}, bf16[3,128,128]{2,1,0:T(8,128)(2,1)S(1)}, u32[]{:S(2)}, u32[]{:S(2)}) collective-permute-start(bf16[3,128,128]{2,1,0:T(8,128)(2,1)S(1)} %get-tuple-element.53), channel_id=1, source_target_pairs={{0,8},{4,12},{8,0},{12,4},{16,24},{20,28},{24,16},{28,20},{1,9},{5... | collective-permute-start | bytes 294920 | tf_op jit(solution)/shard_map/ppermute | solution.py:80
  33.4 5.2 %collective-permute-start.13 = (bf16[3,128,128]{2,1,0:T(8,128)(2,1)S(1)}, bf16[3,128,128]{2,1,0:T(8,128)(2,1)S(1)}, u32[]{:S(2)}, u32[]{:S(2)}) collective-permute-start(bf16[3,128,128]{2,1,0:T(8,128)(2,1)S(1)} %get-tuple-element.54), channel_id=1, source_target_pairs={{0,4},{4,0},{8,12},{12,8},{16,20},{20,16},{24,28},{28,24},{1,5},{5... | collective-permute-start | bytes 294920 | tf_op jit(solution)/shard_map/ppermute | solution.py:80
  34.1 5.1 %collective-permute-start.18 = (bf16[1,128,512]{2,1,0:T(8,128)(2,1)S(1)}, bf16[1,128,512]{2,1,0:T(8,128)(2,1)S(1)}, u32[]{:S(2)}, u32[]{:S(2)}) collective-permute-start(bf16[1,128,512]{2,1,0:T(8,128)(2,1)S(1)} %fusion), channel_id=1, source_target_pairs={{0,2},{1,3},{2,0},{3,1},{4,6},{5,7},{6,4},{7,5},{8,10},{9,11},{10,... | collective-permute-start | bytes 393224 | tf_op jit(solution)/shard_map/ppermute | solution.py:80

commit v12 on v11

--- a/solution.py
+++ b/solution.py
@@ -85,12 +85,12 @@
 
 
 def reduce_blocks(own, sent, bits):
-    got = swap(sent, "head", 1)
+    got = swap(sent, "head", bits[0])
     for bit in bits[1:]:
-        total = own.astype(jnp.float32) + got.astype(jnp.float32)
+        total = own + got.astype(jnp.float32)
         pairs = total.reshape((total.shape[0] // 2, 2) + total.shape[1:])
         own, got = pairs[:, 0], swap(bf(pairs[:, 1]), "head", bit)
-    return own[0].astype(jnp.float32), got[0]
+    return own[0], got[0]
 
 
 def member(n):
@@ -193,9 +193,8 @@
 
 
 def turn_kernel(n, *refs):
-    gm_in, (qf_ref, num_ref), earlier = refs[:n][::-1], refs[n : n + 2], refs[n + 2 : -n - 4]
-    carried_ref, gn_ref, total_ref = refs[-n - 4 : -n - 1]
-    outs, scr = refs[-n - 1 : -1], refs[-1]
+    gm_in, (qf_ref, num_ref), earlier = refs[:n][::-1], refs[n : n + 2], refs[n + 2 : -5]
+    carried_ref, gn_ref, total_ref, mixed_ref, scr = refs[-5:]
     r = member(n)
     rows = gm_in[0].shape[0]
     places = [
@@ -213,14 +212,17 @@
     gn_ref[...] = gn
     scr[...] = bf(normed)
     for k in range(n):
-        outs[k][...] = scr[places[k], :]
+        mixed_ref[k] = scr[places[k], :]
     total_ref[...] = bf(mm(gn, qf_ref[...], TN))
 
 
 def back_kernel(rows, qkv_ref, om_ref, kf_ref, qf_ref, scores_ref, gn_ref, carried_ref,
-                gq_ref, gv_ref, gkf_ref):
+                mixed_ref, other_ref, gq_ref, gv_ref, gkf_ref, *outs):
     long, dim = gn_ref.shape
     r = member(long // rows)
+    for k, out in enumerate(outs):
+        out[0] = mixed_ref[k]
+        out[1] = other_ref[k]
     scale = dim ** (-0.25)
     spans = tiles(long, rows)
     gn, qf = gn_ref[...], qf_ref[...]
@@ -259,25 +261,24 @@
 
 
 def mixed_project_kernel(n, offsets, *refs):
-    mixed_in, (w_ref, _, own_ref, sent_ref, scr) = refs[:n][::-1], refs[n:]
+    mixed_in, (w_ref, other_w_ref, _, own_ref, sent_ref, scr) = refs[:n][::-1], refs[n:]
     r, h = member(n), lax.axis_index("head")
     width = own_ref.shape[2]
-    dim = mixed_in[0].shape[1]
+    dim = mixed_in[0].shape[2]
     half = len(offsets) // 2
     for k in range(n):
-        scr[:, lane(r ^ k, dim)] = mixed_in[k][...]
-    mixed = scr[...]
+        scr[:, :, lane(r ^ k, dim)] = mixed_in[k][...]
     for at, offset in enumerate(offsets):
-        part = bf(mm(mixed, w_ref[:, lane(h ^ offset, width)]))
+        cols = lane(h ^ offset, width)
+        part = mm(scr[0], w_ref[:, cols]) + mm(scr[1], other_w_ref[:, cols])
         if at < half:
             own_ref[at] = part
         else:
-            sent_ref[at - half] = part
+            sent_ref[at - half] = bf(part)
 
 
 def unpack_kernel(n, *refs):
-    got, (part_ref, last_ref) = refs[:n][::-1], refs[n : n + 2]
-    (out_ref, *outs), (scr, sems, last_sem) = refs[n + 2 : -3], refs[-3:]
+    got, (*outs, mark_ref, sems) = refs[:n][::-1], refs[n:]
     r = member(n)
     dim = got[0].shape[2]
     copies = [
@@ -287,11 +288,13 @@
     ]
     for copy in copies:
         copy.start()
-    scr[...] = bf(part_ref[...] + last_ref[...].astype(jnp.float32))
-    copies.append(pltpu.make_async_copy(scr, out_ref, last_sem))
-    copies[-1].start()
+    mark_ref[...] = jnp.zeros(mark_ref.shape, mark_ref.dtype)
     for copy in copies:
         copy.wait()
+
+
+def add_kernel(part_ref, last_ref, _, out_ref):
+    out_ref[...] = bf(part_ref[...] + last_ref[...].astype(jnp.float32))
 
 
 def local(queries, key_vectors, value_vectors, feature_proj, out_weight, grad_output):
@@ -307,6 +310,7 @@
     for bit in reversed(bits):
         blocks = blocks + [swap(b, "head", bit) for b in blocks]
         offsets = offsets + [o ^ bit for o in offsets]
+    other_weight = swap(out_weight, "head", 1)
     sends = call(
         functools.partial(pack_kernel, n),
         [struct((3, rows, dim))] * (n - 1),
@@ -339,24 +343,26 @@
         [struct((long, feats)), struct((long, long)), struct((long, dim), f32)],
         qkv, feature_proj, kf, flops=4 * macs,
     )
-    carried, gn, later_total, *mixed_parts = call(
+    carried, gn, later_total, mixed = call(
         functools.partial(turn_kernel, n),
         [
             struct((dim, feats)),
             struct((long, dim)),
             struct((dim, feats)),
-        ]
-        + [struct((rows, dim))] * n,
+            struct((n, rows, dim)),
+        ],
         *gm_in, qf, num, *earlier, flops=2 * macs,
         scratch=[pltpu.VMEM((long, dim), jnp.bfloat16)],
     )
     after = swap_totals(later_total, n)
+    other_mixed = swap(mixed, "head", 1)
+    gq, gv_part, gkf_part, *mixed_parts = call(
+        functools.partial(back_kernel, rows),
+        [struct((long, dim)), struct((long, dim), f32), struct((long, feats), f32)]
+        + [struct((2, rows, dim))] * n,
+        qkv, feature_proj, kf, qf, scores, gn, carried, mixed, other_mixed, flops=8 * macs,
+    )
     mixed_in = exchange(mixed_parts[1:]) + [mixed_parts[0]]
-    gq, gv_part, gkf_part = call(
-        functools.partial(back_kernel, rows),
-        [struct((long, dim)), struct((long, dim), f32), struct((long, feats), f32)],
-        qkv, feature_proj, kf, qf, scores, gn, carried, flops=8 * macs,
-    )
     grads = call(
         functools.partial(end_kernel, n),
         [struct((3, rows, dim))] * n,
@@ -365,26 +371,25 @@
     )
     grads_in = exchange(grads[1:]) + [grads[0]]
 
-    order = [o for o in range(split) if not o & 1] + [o for o in range(split) if o & 1]
+    order = [o for o in range(0, split, 2) if not o & 2] + [o for o in range(2, split, 4)]
     own, sent = call(
         functools.partial(mixed_project_kernel, n, order),
-        [struct((split // 2, rows, width))] * 2,
-        *mixed_in, out_weight, grads[0], flops=2 * rows * out_weight.size,
-        specs=[VMEM] * (n + 1) + [ANY],
-        scratch=[pltpu.VMEM((rows, n * dim), jnp.bfloat16)],
-    )
-    part, last = reduce_blocks(own, sent, bits)
-    return call(
+        [struct((split // 4, rows, width), f32), struct((split // 4, rows, width))],
+        *mixed_in, out_weight, other_weight, grads[0], flops=2 * rows * out_weight.size,
+        specs=[VMEM] * (n + 2) + [ANY],
+        scratch=[pltpu.VMEM((2, rows, n * dim), jnp.bfloat16)],
+    )
+    part, last = reduce_blocks(own, sent, bits[1:])
+    gq, gk, gv, mark = call(
         functools.partial(unpack_kernel, n),
-        [struct((rows, width))] + [struct((rows, n * dim))] * 3,
-        *grads_in, part, last,
-        out_specs=[ANY] * 4,
-        scratch=[
-            pltpu.VMEM((rows, width), jnp.bfloat16),
-            pltpu.SemaphoreType.DMA((n, 3)),
-            pltpu.SemaphoreType.DMA,
-        ],
-    )
+        [struct((rows, n * dim))] * 3 + [struct((8, 128), f32)],
+        *grads_in, flops=8 * 10**8,
+        out_specs=[ANY] * 3 + [VMEM], scratch=[pltpu.SemaphoreType.DMA((n, 3))],
+    )
+    (layer_out,) = call(
+        add_kernel, [struct((rows, width))], part, last, mark, specs=[VMEM, VMEM, ANY]
+    )
+    return layer_out, gq, gk, gv
 
 
 def solution(mesh):

time: 40.3 us -> 41.2 us (1.022)
  starting transfers between devices: 20.8 us -> 23.2 us
  waiting for transfers between devices: 12 us -> 10 us
  Pallas kernels: 6.35 us -> 7.02 us
    ppermute x19 -> x20, starting transfers between devices: 20.8 us -> 23.2 us  [swap(): return lax.ppermute(array, axis, [(i, i ^ bit) for i in range(size)])]
    ppermute x19 -> x20, waiting for transfers between devices: 12 us -> 10 us  [swap(): return lax.ppermute(array, axis, [(i, i ^ bit) for i in range(size)])]
    pallas_call x10 -> x11, Pallas kernels: 6.35 us -> 7.02 us  [call(): pl.pallas_call(body, out_shape=outs, in_specs=specs or [VMEM] * len(args)...]
  transfers between devices with their start and end apart: 19 -> 20, of which waited for: 12 -> 12; matrix products, arithmetic and copies ran while one was open for 0% -> 0% of each run, Pallas kernels for 10% -> 15%
where the time goes in v12:
time: 41.2 us; the launch traced here: 41 us
  starting transfers between devices  23.2 us (56%)
  waiting for transfers between devices  10 us (24%)
  Pallas kernels  7.02 us (17%)
  between operations  0.78 us (2%)
    ppermute x20, starting transfers between devices, swap(): return lax.ppermute(array, axis, [(i, i ^ bit) for i in range(size)])  23.2 us
    ppermute x20, waiting for transfers between devices, swap(): return lax.ppermute(array, axis, [(i, i ^ bit) for i in range(size)])  10 us
    pallas_call x11, Pallas kernels, call(): pl.pallas_call(body, out_shape=outs, in_specs=specs or [VMEM] * len(args)...  7.02 us
  transfers between devices with their start and end apart: 20, of which 12 were waited for; matrix products, arithmetic and copies ran while one was open for 0% of the time, Pallas kernels for 15%

profile of v12, /device:TPU:0, one launch (start us, length us, event | category | flops | bytes accessed | tf_op | source)
XLA Modules:
  0.0 41.0 jit_solution(6791053026504215780)
XLA Ops:
  0.6 0.5 %collective-permute-start.14 = (bf16[512,2048]{1,0:T(8,128)(2,1)}, bf16[512,2048]{1,0:T(8,128)(2,1)S(1)}, u32[]{:S(2)}, u32[]{:S(2)}) collective-permute-start(bf16[512,2048]{1,0:T(8,128)(2,1)} %refs_4_.5), channel_id=1, source_target_pairs={{0,1},{1,0},{2,3},{3,2},{4,5},{5,4},{6,7},{7,6},{8,9},{9,8},{10,11... | collective-permute-start | bytes 6291464 | tf_op jit(solution)/shard_map/ppermute | solution.py:80
  1.1 2.6 %collective-permute-start.3 = (bf16[128,512]{1,0:T(8,128)(2,1)}, bf16[128,512]{1,0:T(8,128)(2,1)S(1)}, u32[]{:S(2)}, u32[]{:S(2)}) collective-permute-start(bf16[128,512]{1,0:T(8,128)(2,1)} %refs_0_.1), channel_id=1, source_target_pairs={{0,2},{1,3},{2,0},{3,1},{4,6},{5,7},{6,4},{7,5},{8,10},{9,11},{10,... | collective-permute-start | bytes 393224 | tf_op jit(solution)/shard_map/ppermute | solution.py:80
  3.7 0.2 collective-permute-start.4
  3.9 1.0 %shard_map.93 = (bf16[3,128,128]{2,1,0:T(8,128)(2,1)S(1)}, bf16[3,128,128]{2,1,0:T(8,128)(2,1)S(1)}, bf16[3,128,128]{2,1,0:T(8,128)(2,1)S(1)}) custom-call(bf16[128,512]{1,0:T(8,128)(2,1)} %refs_3_.1, bf16[128,512]{1,0:T(8,128)(2,1)} %refs_4_.4, bf16[128,512]{1,0:T(8,128)(2,1)} %refs_5_.1), custom_call_target="tpu_custom_call" | custom-call | bytes 688128 | tf_op jit(solution)/shard_map/pallas_call | solution.py:29
  4.9 2.6 %collective-permute-start = (bf16[3,128,128]{2,1,0:T(8,128)(2,1)S(1)}, bf16[3,128,128]{2,1,0:T(8,128)(2,1)S(1)}, u32[]{:S(2)}, u32[]{:S(2)}) collective-permute-start(bf16[3,128,128]{2,1,0:T(8,128)(2,1)S(1)} %get-tuple-element.38), channel_id=1, source_target_pairs={{0,12},{4,8},{8,4},{12,0},{16,28},{20,24},{24,20},{28,16},{1,13},{... | collective-permute-start | bytes 294920 | tf_op jit(solution)/shard_map/ppermute | solution.py:80
  7.5 0.4 %collective-permute-start.1 = (bf16[3,128,128]{2,1,0:T(8,128)(2,1)S(1)}, bf16[3,128,128]{2,1,0:T(8,128)(2,1)S(1)}, u32[]{:S(2)}, u32[]{:S(2)}) collective-permute-start(bf16[3,128,128]{2,1,0:T(8,128)(2,1)S(1)} %get-tuple-element.39), channel_id=1, source_target_pairs={{0,8},{4,12},{8,0},{12,4},{16,24},{20,28},{24,16},{28,20},{1,9},{5... | collective-permute-start | bytes 294920 | tf_op jit(solution)/shard_map/ppermute | solution.py:80
  7.9 0.1 collective-permute-done.3.refs_1_
  8.0 1.8 %collective-permute-start.2 = (bf16[3,128,128]{2,1,0:T(8,128)(2,1)S(1)}, bf16[3,128,128]{2,1,0:T(8,128)(2,1)S(1)}, u32[]{:S(2)}, u32[]{:S(2)}) collective-permute-start(bf16[3,128,128]{2,1,0:T(8,128)(2,1)S(1)} %get-tuple-element.40), channel_id=1, source_target_pairs={{0,4},{4,0},{8,12},{12,8},{16,20},{20,16},{24,28},{28,24},{1,5},{5... | collective-permute-start | bytes 294920 | tf_op jit(solution)/shard_map/ppermute | solution.py:80
  9.8 0.0 collective-permute-done.4._.refs_2_
  9.8 0.0 copy-start.1
  9.8 0.0 copy-start.2
  9.8 0.0 copy-start.3
  9.9 0.0 copy-start.4
  9.9 1.3 %collective-permute-done.5.refs_3_ = bf16[128,512]{1,0:T(8,128)(2,1)S(1)} collective-permute-done((bf16[128,512]{1,0:T(8,128)(2,1)S(1)}, bf16[128,512]{1,0:T(8,128)(2,1)S(1)}, u32[]{:S(2)}, u32[]{:S(2)}) %collective-permute-start.5) | collective-permute-done | bytes 131104 | tf_op jit(solution)/shard_map/ppermute | solution.py:80
  11.2 0.9 %shard_map.95 = (bf16[128,128]{1,0:T(8,128)(2,1)S(1)}, bf16[128,128]{1,0:T(8,128)(2,1)S(1)}, bf16[128,128]{1,0:T(8,128)(2,1)S(1)}, bf16[128,128]{1,0:T(8,128)(2,1)S(1)}) custom-call(bf16[128,512]{1,0:T(8,128)(2,1)S(1)} %copy-done.5, bf16[128,512]{1,0:T(8,128)(2,1)S(1)} %collective-permute-done.3.refs_1_, ...), custom_call_target="tpu_custom_call" | custom-call | flops 268435456 | bytes 2756608 | tf_op jit(solution)/shard_map/pallas_call | solution.py:29
  12.0 1.0 %collective-permute-done.1.refs_1_ = bf16[3,128,128]{2,1,0:T(8,128)(2,1)S(1)} collective-permute-done((bf16[3,128,128]{2,1,0:T(8,128)(2,1)S(1)}, bf16[3,128,128]{2,1,0:T(8,128)(2,1)S(1)}, u32[]{:S(2)}, u32[]{:S(2)}) %collective-permute-start.1) | collective-permute-done | bytes 98336 | tf_op jit(solution)/shard_map/ppermute | solution.py:80
  13.0 0.0 collective-permute-done.2.refs_2_
  13.1 0.5 %shard_map.96 = (bf16[3,512,128]{2,1,0:T(8,128)(2,1)S(1)}, bf16[512,256]{1,0:T(8,128)(2,1)S(1)}, bf16[128,256]{1,0:T(8,128)(2,1)S(1)}) custom-call(bf16[3,128,128]{2,1,0:T(8,128)(2,1)S(1)} %collective-permute-done.refs_0_, bf16[3,128,128]{2,1,0:T(8,128)(2,1)S(1)} %collective-permute-done.1.refs_1_, bf16[3,128,128]{2,1,0:T(8,128)(2,1)S(1)} %collective-permute-done.2.refs_2_, ...), custom_call_target="tpu_custom_call" | custom-call | flops 67108864 | bytes 1703936 | tf_op jit(solution)/shard_map/pallas_call | solution.py:29
  13.6 2.7 %collective-permute-start.9 = (bf16[128,256]{1,0:T(8,128)(2,1)S(1)}, bf16[128,256]{1,0:T(8,128)(2,1)S(1)}, u32[]{:S(2)}, u32[]{:S(2)}) collective-permute-start(bf16[128,256]{1,0:T(8,128)(2,1)S(1)} %get-tuple-element.50), channel_id=1, source_target_pairs={{0,16},{4,20},{8,24},{12,28},{16,0},{20,4},{24,8},{28,12},{1,17},{... | collective-permute-start | bytes 196616 | tf_op jit(solution)/shard_map/ppermute | solution.py:80
  16.3 2.5 %collective-permute-start.6 = (bf16[128,128]{1,0:T(8,128)(2,1)S(1)}, bf16[128,128]{1,0:T(8,128)(2,1)S(1)}, u32[]{:S(2)}, u32[]{:S(2)}) collective-permute-start(bf16[128,128]{1,0:T(8,128)(2,1)S(1)} %get-tuple-element.46), channel_id=1, source_target_pairs={{0,12},{4,8},{8,4},{12,0},{16,28},{20,24},{24,20},{28,16},{1,13},{... | collective-permute-start | bytes 98312 | tf_op jit(solution)/shard_map/ppermute | solution.py:80
  18.8 0.5 %collective-permute-start.7 = (bf16[128,128]{1,0:T(8,128)(2,1)S(1)}, bf16[128,128]{1,0:T(8,128)(2,1)S(1)}, u32[]{:S(2)}, u32[]{:S(2)}) collective-permute-start(bf16[128,128]{1,0:T(8,128)(2,1)S(1)} %get-tuple-element.47), channel_id=1, source_target_pairs={{0,8},{4,12},{8,0},{12,4},{16,24},{20,28},{24,16},{28,20},{1,9},{5... | collective-permute-start | bytes 98312 | tf_op jit(solution)/shard_map/ppermute | solution.py:80
  19.2 0.5 %collective-permute-start.8 = (bf16[128,128]{1,0:T(8,128)(2,1)S(1)}, bf16[128,128]{1,0:T(8,128)(2,1)S(1)}, u32[]{:S(2)}, u32[]{:S(2)}) collective-permute-start(bf16[128,128]{1,0:T(8,128)(2,1)S(1)} %get-tuple-element.48), channel_id=1, source_target_pairs={{0,4},{4,0},{8,12},{12,8},{16,20},{20,16},{24,28},{28,24},{1,5},{5... | collective-permute-start | bytes 98312 | tf_op jit(solution)/shard_map/ppermute | solution.py:80
  19.7 0.5 %shard_map.97 = (bf16[512,256]{1,0:T(8,128)(2,1)S(1)}, bf16[512,512]{1,0:T(8,128)(2,1)S(1)}, f32[512,128]{1,0:T(8,128)S(1)}) custom-call(bf16[3,512,128]{2,1,0:T(8,128)(2,1)S(1)} %get-tuple-element.42.qkv_ref, bf16[4,128,256]{2,1,0:T(8,128)(2,1)S(1)} %copy-done.1, bf16[512,256]{1,0:T(8,128)(2,1)S(1)} %get-tuple-element.43.kf_ref), custom_call_target="tpu_custom_call" | custom-call | flops 134217728 | bytes 1966080 | tf_op jit(solution)/shard_map/pallas_call | solution.py:29
  20.3 0.8 %collective-permute-done.6.refs_0_ = bf16[128,128]{1,0:T(8,128)(2,1)S(1)} collective-permute-done((bf16[128,128]{1,0:T(8,128)(2,1)S(1)}, bf16[128,128]{1,0:T(8,128)(2,1)S(1)}, u32[]{:S(2)}, u32[]{:S(2)}) %collective-permute-start.6) | collective-permute-done | bytes 32800 | tf_op jit(solution)/shard_map/ppermute | solution.py:80
  21.1 1.6 %collective-permute-done.7.refs_1_ = bf16[128,128]{1,0:T(8,128)(2,1)S(1)} collective-permute-done((bf16[128,128]{1,0:T(8,128)(2,1)S(1)}, bf16[128,128]{1,0:T(8,128)(2,1)S(1)}, u32[]{:S(2)}, u32[]{:S(2)}) %collective-permute-start.7) | collective-permute-done | bytes 32800 | tf_op jit(solution)/shard_map/ppermute | solution.py:80
  22.7 0.5 %collective-permute-done.8.refs_2_ = bf16[128,128]{1,0:T(8,128)(2,1)S(1)} collective-permute-done((bf16[128,128]{1,0:T(8,128)(2,1)S(1)}, bf16[128,128]{1,0:T(8,128)(2,1)S(1)}, u32[]{:S(2)}, u32[]{:S(2)}) %collective-permute-start.8) | collective-permute-done | bytes 32800 | tf_op jit(solution)/shard_map/ppermute | solution.py:80
  23.2 0.6 %shard_map.98 = (bf16[128,256]{1,0:T(8,128)(2,1)S(1)}, bf16[512,128]{1,0:T(8,128)(2,1)S(1)}, bf16[128,256]{1,0:T(8,128)(2,1)S(1)}, bf16[4,128,128]{2,1,0:T(8,128)(2,1)S(1)}) custom-call(bf16[128,128]{1,0:T(8,128)(2,1)S(1)} %collective-permute-done.6.refs_0_, bf16[128,128]{1,0:T(8,128)(2,1)S(1)} %collective-permute-done.7.refs_1_, ...), custom_call_target="tpu_custom_call" | custom-call | flops 67108864 | bytes 1114112 | tf_op jit(solution)/shard_map/pallas_call | solution.py:29
  23.8 0.1 collective-permute-start.10
  23.9 0.4 collective-permute-start.15
  24.3 0.9 %collective-permute-done.10.other_ref = bf16[4,128,128]{2,1,0:T(8,128)(2,1)S(1)} collective-permute-done((bf16[4,128,128]{2,1,0:T(8,128)(2,1)S(1)}, bf16[4,128,128]{2,1,0:T(8,128)(2,1)S(1)}, u32[]{:S(2)}, u32[]{:S(2)}) %collective-permute-start.10) | collective-permute-done | bytes 131104 | tf_op jit(solution)/shard_map/ppermute | solution.py:80
  25.2 1.0 %shard_map.99 = (bf16[512,128]{1,0:T(8,128)(2,1)S(1)}, f32[512,128]{1,0:T(8,128)S(1)}, f32[512,256]{1,0:T(8,128)S(1)}, bf16[2,128,128]{2,1,0:T(8,128)(2,1)S(1)},...) custom-call(bf16[3,512,128]{2,1,0:T(8,128)(2,1)S(1)} %get-tuple-element.42.qkv_, ...), custom_call_target="tpu_custom_call" | custom-call | flops 268435456 | bytes 3342336 | tf_op jit(solution)/shard_map/pallas_call | solution.py:29
  26.2 1.6 %collective-permute-start.11 = (bf16[2,128,128]{2,1,0:T(8,128)(2,1)S(1)}, bf16[2,128,128]{2,1,0:T(8,128)(2,1)S(1)}, u32[]{:S(2)}, u32[]{:S(2)}) collective-permute-start(bf16[2,128,128]{2,1,0:T(8,128)(2,1)S(1)} %get-tuple-element.54), channel_id=1, source_target_pairs={{0,12},{4,8},{8,4},{12,0},{16,28},{20,24},{24,20},{28,16},{1,13},{... | collective-permute-start | bytes 196616 | tf_op jit(solution)/shard_map/ppermute | solution.py:80
  27.8 0.5 %collective-permute-start.12 = (bf16[2,128,128]{2,1,0:T(8,128)(2,1)S(1)}, bf16[2,128,128]{2,1,0:T(8,128)(2,1)S(1)}, u32[]{:S(2)}, u32[]{:S(2)}) collective-permute-start(bf16[2,128,128]{2,1,0:T(8,128)(2,1)S(1)} %get-tuple-element.55), channel_id=1, source_target_pairs={{0,8},{4,12},{8,0},{12,4},{16,24},{20,28},{24,16},{28,20},{1,9},{5... | collective-permute-start | bytes 196616 | tf_op jit(solution)/shard_map/ppermute | solution.py:80
  28.2 1.5 %collective-permute-start.13 = (bf16[2,128,128]{2,1,0:T(8,128)(2,1)S(1)}, bf16[2,128,128]{2,1,0:T(8,128)(2,1)S(1)}, u32[]{:S(2)}, u32[]{:S(2)}) collective-permute-start(bf16[2,128,128]{2,1,0:T(8,128)(2,1)S(1)} %get-tuple-element.56), channel_id=1, source_target_pairs={{0,4},{4,0},{8,12},{12,8},{16,20},{20,16},{24,28},{28,24},{1,5},{5... | collective-permute-start | bytes 196616 | tf_op jit(solution)/shard_map/ppermute | solution.py:80
  29.7 0.9 %collective-permute-done.15.rest_0_ = bf16[128,256]{1,0:T(8,128)(2,1)S(1)} collective-permute-done((bf16[128,256]{1,0:T(8,128)(2,1)S(1)}, bf16[128,256]{1,0:T(8,128)(2,1)S(1)}, u32[]{:S(2)}, u32[]{:S(2)}) %collective-permute-start.15) | collective-permute-done | bytes 65568 | tf_op jit(solution)/shard_map/ppermute | solution.py:80
  30.6 0.6 %shard_map.100 = (bf16[3,128,128]{2,1,0:T(8,128)(2,1)S(1)}, bf16[3,128,128]{2,1,0:T(8,128)(2,1)S(1)}, bf16[3,128,128]{2,1,0:T(8,128)(2,1)S(1)}, bf16[3,128,128]{2,1,0:T(8,128)(2,1)S(1)}) custom-call(bf16[3,512,128]{2,1,0:T(8,128)(2,1)S(1)} %get-tuple-element.42.qkv_ref, bf16[4,128,256]{2,1,0:T(8,128)(2,1)S(1)} %copy-done.1, ...), custom_call_target="tpu_custom_call" | custom-call | flops 100663296 | bytes 2293760 | tf_op jit(solution)/shard_map/pallas_call | solution.py:29
  31.2 0.7 %collective-permute-start.17 = (bf16[3,128,128]{2,1,0:T(8,128)(2,1)S(1)}, bf16[3,128,128]{2,1,0:T(8,128)(2,1)S(1)}, u32[]{:S(2)}, u32[]{:S(2)}) collective-permute-start(bf16[3,128,128]{2,1,0:T(8,128)(2,1)S(1)} %get-tuple-element.65), channel_id=1, source_target_pairs={{0,12},{4,8},{8,4},{12,0},{16,28},{20,24},{24,20},{28,16},{1,13},{... | collective-permute-start | bytes 294920 | tf_op jit(solution)/shard_map/ppermute | solution.py:80
  31.9 0.0 collective-permute-done.11.refs_0_
  32.0 1.6 %collective-permute-start.18 = (bf16[3,128,128]{2,1,0:T(8,128)(2,1)S(1)}, bf16[3,128,128]{2,1,0:T(8,128)(2,1)S(1)}, u32[]{:S(2)}, u32[]{:S(2)}) collective-permute-start(bf16[3,128,128]{2,1,0:T(8,128)(2,1)S(1)} %get-tuple-element.66), channel_id=1, source_target_pairs={{0,8},{4,12},{8,0},{12,4},{16,24},{20,28},{24,16},{28,20},{1,9},{5... | collective-permute-start | bytes 294920 | tf_op jit(solution)/shard_map/ppermute | solution.py:80
  33.6 1.2 %collective-permute-start.19 = (bf16[3,128,128]{2,1,0:T(8,128)(2,1)S(1)}, bf16[3,128,128]{2,1,0:T(8,128)(2,1)S(1)}, u32[]{:S(2)}, u32[]{:S(2)}) collective-permute-start(bf16[3,128,128]{2,1,0:T(8,128)(2,1)S(1)} %get-tuple-element.67), channel_id=1, source_target_pairs={{0,4},{4,0},{8,12},{12,8},{16,20},{20,16},{24,28},{28,24},{1,5},{5... | collective-permute-start | bytes 294920 | tf_op jit(solution)/shard_map/ppermute | solution.py:80
  34.8 0.5 %shard_map.101 = (f32[1,128,512]{2,1,0:T(8,128)S(1)}, bf16[1,128,512]{2,1,0:T(8,128)(2,1)S(1)}) custom-call(bf16[2,128,128]{2,1,0:T(8,128)(2,1)S(1)} %collective-permute-done.11.refs_0_, bf16[2,128,128]{2,1,0:T(8,128)(2,1)S(1)} %collective-permute-done.12.refs_1_, bf16[2,128,128]{2,1,0:T(8,128)(2,1)S(1)} %collective-permute-done.13.refs_2_, ...), custom_call_target="tpu_custom_call" | custom-call | flops 268435456 | bytes 4947968 | tf_op jit(solution)/shard_map/pallas_call | solution.py:29
  35.3 1.4 %collective-permute-start.16 = (bf16[1,128,512]{2,1,0:T(8,128)(2,1)S(1)}, bf16[1,128,512]{2,1,0:T(8,128)(2,1)S(1)}, u32[]{:S(2)}, u32[]{:S(2)}) collective-permute-start(bf16[1,128,512]{2,1,0:T(8,128)(2,1)S(1)} %get-tuple-element.64), channel_id=1, source_target_pairs={{0,2},{1,3},{2,0},{3,1},{4,6},{5,7},{6,4},{7,5},{8,10},{9,11},{10,... | collective-permute-start | bytes 393224 | tf_op jit(solution)/shard_map/ppermute | solution.py:80
  36.7 0.1 collective-permute-done.17.refs_0_
  36.8 0.2 collective-permute-done.18.refs_1_
  37.0 1.2 %collective-permute-done.19.refs_2_ = bf16[3,128,128]{2,1,0:T(8,128)(2,1)S(1)} collective-permute-done((bf16[3,128,128]{2,1,0:T(8,128)(2,1)S(1)}, bf16[3,128,128]{2,1,0:T(8,128)(2,1)S(1)}, u32[]{:S(2)}, u32[]{:S(2)}) %collective-permute-start.19) | collective-permute-done | bytes 98336 | tf_op jit(solution)/shard_map/ppermute | solution.py:80
  38.2 0.8 %shard_map.102 = (bf16[128,512]{1,0:T(8,128)(2,1)}, bf16[128,512]{1,0:T(8,128)(2,1)}, bf16[128,512]{1,0:T(8,128)(2,1)}, f32[8,128]{1,0:T(8,128)S(1)}) custom-call(bf16[3,128,128]{2,1,0:T(8,128)(2,1)S(1)} %collective-permute-done.17.refs_0_, bf16[3,128,128]{2,1,0:T(8,128)(2,1)S(1)} %collective-permute-done.18.refs_1_, ...), custom_call_target="tpu_custom_call" | custom-call | flops 800000000 | bytes 790528 | tf_op jit(solution)/shard_map/pallas_call | solution.py:29
  39.0 1.3 %collective-permute-done.16 = bf16[1,128,512]{2,1,0:T(8,128)(2,1)S(1)} collective-permute-done((bf16[1,128,512]{2,1,0:T(8,128)(2,1)S(1)}, bf16[1,128,512]{2,1,0:T(8,128)(2,1)S(1)}, u32[]{:S(2)}, u32[]{:S(2)}) %collective-permute-start.16) | collective-permute-done | bytes 131104 | tf_op jit(solution)/shard_map/ppermute | solution.py:80
  40.3 0.7 %shard_map.103 = bf16[128,512]{1,0:T(8,128)(2,1)} custom-call(f32[128,512]{1,0:T(8,128)S(1)} %bitcast.2, bf16[128,512]{1,0:T(8,128)(2,1)S(1)} %bitcast.3, f32[8,128]{1,0:T(8,128)S(1)} %get-tuple-element.68._), custom_call_target="tpu_custom_call" | custom-call | bytes 528384 | tf_op jit(solution)/shard_map/pallas_call | solution.py:29
  (15 shorter events, 0.0 us)
Async XLA Ops:
  0.6 34.2 %collective-permute-start.14 = (bf16[512,2048]{1,0:T(8,128)(2,1)}, bf16[512,2048]{1,0:T(8,128)(2,1)S(1)}, u32[]{:S(2)}, u32[]{:S(2)}) collective-permute-start(bf16[512,2048]{1,0:T(8,128)(2,1)} %refs_4_.5), channel_id=1, source_target_pairs={{0,1},{1,0},{2,3},{3,2},{4,5},{5,4},{6,7},{7,6},{8,9},{9,8},{10,11... | collective-permute-start | bytes 6291464 | tf_op jit(solution)/shard_map/ppermute | solution.py:80
  1.1 6.9 %collective-permute-start.3 = (bf16[128,512]{1,0:T(8,128)(2,1)}, bf16[128,512]{1,0:T(8,128)(2,1)S(1)}, u32[]{:S(2)}, u32[]{:S(2)}) collective-permute-start(bf16[128,512]{1,0:T(8,128)(2,1)} %refs_0_.1), channel_id=1, source_target_pairs={{0,2},{1,3},{2,0},{3,1},{4,6},{5,7},{6,4},{7,5},{8,10},{9,11},{10,... | collective-permute-start | bytes 393224 | tf_op jit(solution)/shard_map/ppermute | solution.py:80
  3.7 6.1 %collective-permute-start.4 = (bf16[128,512]{1,0:T(8,128)(2,1)}, bf16[128,512]{1,0:T(8,128)(2,1)S(1)}, u32[]{:S(2)}, u32[]{:S(2)}) collective-permute-start(bf16[128,512]{1,0:T(8,128)(2,1)} %refs_0_.1), channel_id=1, source_target_pairs={{0,1},{1,0},{2,3},{3,2},{4,5},{5,4},{6,7},{7,6},{8,9},{9,8},{10,11... | collective-permute-start | bytes 393224 | tf_op jit(solution)/shard_map/ppermute | solution.py:80
  4.9 7.2 %collective-permute-start = (bf16[3,128,128]{2,1,0:T(8,128)(2,1)S(1)}, bf16[3,128,128]{2,1,0:T(8,128)(2,1)S(1)}, u32[]{:S(2)}, u32[]{:S(2)}) collective-permute-start(bf16[3,128,128]{2,1,0:T(8,128)(2,1)S(1)} %get-tuple-element.38), channel_id=1, source_target_pairs={{0,12},{4,8},{8,4},{12,0},{16,28},{20,24},{24,20},{28,16},{1,13},{... | collective-permute-start | bytes 294920 | tf_op jit(solution)/shard_map/ppermute | solution.py:80
  7.5 5.6 %collective-permute-start.1 = (bf16[3,128,128]{2,1,0:T(8,128)(2,1)S(1)}, bf16[3,128,128]{2,1,0:T(8,128)(2,1)S(1)}, u32[]{:S(2)}, u32[]{:S(2)}) collective-permute-start(bf16[3,128,128]{2,1,0:T(8,128)(2,1)S(1)} %get-tuple-element.39), channel_id=1, source_target_pairs={{0,8},{4,12},{8,0},{12,4},{16,24},{20,28},{24,16},{28,20},{1,9},{5... | collective-permute-start | bytes 294920 | tf_op jit(solution)/shard_map/ppermute | solution.py:80
  8.0 3.1 %copy-start = (bf16[512,2048]{1,0:T(8,128)(2,1)S(1)}, bf16[512,2048]{1,0:T(8,128)(2,1)}, u32[]{:S(2)}) copy-start(bf16[512,2048]{1,0:T(8,128)(2,1)} %refs_4_.5) | copy-start | bytes 6291460
  8.0 3.1 %copy-start.5 = (bf16[128,512]{1,0:T(8,128)(2,1)S(1)}, bf16[128,512]{1,0:T(8,128)(2,1)}, u32[]{:S(2)}) copy-start(bf16[128,512]{1,0:T(8,128)(2,1)} %refs_0_.1) | copy-start | bytes 393220
  8.0 5.0 %collective-permute-start.2 = (bf16[3,128,128]{2,1,0:T(8,128)(2,1)S(1)}, bf16[3,128,128]{2,1,0:T(8,128)(2,1)S(1)}, u32[]{:S(2)}, u32[]{:S(2)}) collective-permute-start(bf16[3,128,128]{2,1,0:T(8,128)(2,1)S(1)} %get-tuple-element.40), channel_id=1, source_target_pairs={{0,4},{4,0},{8,12},{12,8},{16,20},{20,16},{24,28},{28,24},{1,5},{5... | collective-permute-start | bytes 294920 | tf_op jit(solution)/shard_map/ppermute | solution.py:80
  9.8 1.3 %collective-permute-start.5 = (bf16[128,512]{1,0:T(8,128)(2,1)S(1)}, bf16[128,512]{1,0:T(8,128)(2,1)S(1)}, u32[]{:S(2)}, u32[]{:S(2)}) collective-permute-start(bf16[128,512]{1,0:T(8,128)(2,1)S(1)} %collective-permute-done.3.refs_1_), channel_id=1, source_target_pairs={{0,1},{1,0},{2,3},{3,2},{4,5},{5,4},{6,7},{7,6},{8,9},{9,8},{10,11... | collective-permute-start | bytes 393224 | tf_op jit(solution)/shard_map/ppermute | solution.py:80
  9.8 3.2 %copy-start.1 = (bf16[4,128,256]{2,1,0:T(8,128)(2,1)S(1)}, bf16[4,128,256]{2,1,0:T(8,128)(2,1)}, u32[]{:S(2)}) copy-start(bf16[4,128,256]{2,1,0:T(8,128)(2,1)} %om_ref.5) | copy-start | bytes 786436
  9.8 3.2 %copy-start.2 = (bf16[128,512]{1,0:T(8,128)(2,1)S(1)}, bf16[128,512]{1,0:T(8,128)(2,1)}, u32[]{:S(2)}) copy-start(bf16[128,512]{1,0:T(8,128)(2,1)} %refs_3_.1) | copy-start | bytes 393220
  9.8 3.2 %copy-start.3 = (bf16[128,512]{1,0:T(8,128)(2,1)S(1)}, bf16[128,512]{1,0:T(8,128)(2,1)}, u32[]{:S(2)}) copy-start(bf16[128,512]{1,0:T(8,128)(2,1)} %refs_4_.4) | copy-start | bytes 393220
  9.9 3.2 %copy-start.4 = (bf16[128,512]{1,0:T(8,128)(2,1)S(1)}, bf16[128,512]{1,0:T(8,128)(2,1)}, u32[]{:S(2)}) copy-start(bf16[128,512]{1,0:T(8,128)(2,1)} %refs_5_.1) | copy-start | bytes 393220
  13.6 9.6 %collective-permute-start.9 = (bf16[128,256]{1,0:T(8,128)(2,1)S(1)}, bf16[128,256]{1,0:T(8,128)(2,1)S(1)}, u32[]{:S(2)}, u32[]{:S(2)}) collective-permute-start(bf16[128,256]{1,0:T(8,128)(2,1)S(1)} %get-tuple-element.50), channel_id=1, source_target_pairs={{0,16},{4,20},{8,24},{12,28},{16,0},{20,4},{24,8},{28,12},{1,17},{... | collective-permute-start | bytes 196616 | tf_op jit(solution)/shard_map/ppermute | solution.py:80
  16.3 4.8 %collective-permute-start.6 = (bf16[128,128]{1,0:T(8,128)(2,1)S(1)}, bf16[128,128]{1,0:T(8,128)(2,1)S(1)}, u32[]{:S(2)}, u32[]{:S(2)}) collective-permute-start(bf16[128,128]{1,0:T(8,128)(2,1)S(1)} %get-tuple-element.46), channel_id=1, source_target_pairs={{0,12},{4,8},{8,4},{12,0},{16,28},{20,24},{24,20},{28,16},{1,13},{... | collective-permute-start | bytes 98312 | tf_op jit(solution)/shard_map/ppermute | solution.py:80
  18.8 3.9 %collective-permute-start.7 = (bf16[128,128]{1,0:T(8,128)(2,1)S(1)}, bf16[128,128]{1,0:T(8,128)(2,1)S(1)}, u32[]{:S(2)}, u32[]{:S(2)}) collective-permute-start(bf16[128,128]{1,0:T(8,128)(2,1)S(1)} %get-tuple-element.47), channel_id=1, source_target_pairs={{0,8},{4,12},{8,0},{12,4},{16,24},{20,28},{24,16},{28,20},{1,9},{5... | collective-permute-start | bytes 98312 | tf_op jit(solution)/shard_map/ppermute | solution.py:80
  19.2 3.9 %collective-permute-start.8 = (bf16[128,128]{1,0:T(8,128)(2,1)S(1)}, bf16[128,128]{1,0:T(8,128)(2,1)S(1)}, u32[]{:S(2)}, u32[]{:S(2)}) collective-permute-start(bf16[128,128]{1,0:T(8,128)(2,1)S(1)} %get-tuple-element.48), channel_id=1, source_target_pairs={{0,4},{4,0},{8,12},{12,8},{16,20},{20,16},{24,28},{28,24},{1,5},{5... | collective-permute-start | bytes 98312 | tf_op jit(solution)/shard_map/ppermute | solution.py:80
  23.8 1.4 %collective-permute-start.10 = (bf16[4,128,128]{2,1,0:T(8,128)(2,1)S(1)}, bf16[4,128,128]{2,1,0:T(8,128)(2,1)S(1)}, u32[]{:S(2)}, u32[]{:S(2)}) collective-permute-start(bf16[4,128,128]{2,1,0:T(8,128)(2,1)S(1)} %get-tuple-element.53.mixed_ref), channel_id=1, source_target_pairs={{0,1},{1,0},{2,3},{3,2},{4,5},{5,4},{6,7},{7,6},{8,9},{9,8},{10,11... | collective-permute-start | bytes 393224 | tf_op jit(solution)/shard_map/ppermute | solution.py:80
  23.9 6.8 %collective-permute-start.15 = (bf16[128,256]{1,0:T(8,128)(2,1)S(1)}, bf16[128,256]{1,0:T(8,128)(2,1)S(1)}, u32[]{:S(2)}, u32[]{:S(2)}) collective-permute-start(bf16[128,256]{1,0:T(8,128)(2,1)S(1)} %get-tuple-element.61), channel_id=1, source_target_pairs={{0,16},{4,20},{8,24},{12,28},{16,0},{20,4},{24,8},{28,12},{1,17},{... | collective-permute-start | bytes 196616 | tf_op jit(solution)/shard_map/ppermute | solution.py:80
  26.2 5.8 %collective-permute-start.11 = (bf16[2,128,128]{2,1,0:T(8,128)(2,1)S(1)}, bf16[2,128,128]{2,1,0:T(8,128)(2,1)S(1)}, u32[]{:S(2)}, u32[]{:S(2)}) collective-permute-start(bf16[2,128,128]{2,1,0:T(8,128)(2,1)S(1)} %get-tuple-element.54), channel_id=1, source_target_pairs={{0,12},{4,8},{8,4},{12,0},{16,28},{20,24},{24,20},{28,16},{1,13},{... | collective-permute-start | bytes 196616 | tf_op jit(solution)/shard_map/ppermute | solution.py:80
  27.8 5.8 %collective-permute-start.12 = (bf16[2,128,128]{2,1,0:T(8,128)(2,1)S(1)}, bf16[2,128,128]{2,1,0:T(8,128)(2,1)S(1)}, u32[]{:S(2)}, u32[]{:S(2)}) collective-permute-start(bf16[2,128,128]{2,1,0:T(8,128)(2,1)S(1)} %get-tuple-element.55), channel_id=1, source_target_pairs={{0,8},{4,12},{8,0},{12,4},{16,24},{20,28},{24,16},{28,20},{1,9},{5... | collective-permute-start | bytes 196616 | tf_op jit(solution)/shard_map/ppermute | solution.py:80
  28.2 6.6 %collective-permute-start.13 = (bf16[2,128,128]{2,1,0:T(8,128)(2,1)S(1)}, bf16[2,128,128]{2,1,0:T(8,128)(2,1)S(1)}, u32[]{:S(2)}, u32[]{:S(2)}) collective-permute-start(bf16[2,128,128]{2,1,0:T(8,128)(2,1)S(1)} %get-tuple-element.56), channel_id=1, source_target_pairs={{0,4},{4,0},{8,12},{12,8},{16,20},{20,16},{24,28},{28,24},{1,5},{5... | collective-permute-start | bytes 196616 | tf_op jit(solution)/shard_map/ppermute | solution.py:80
  31.2 5.6 %collective-permute-start.17 = (bf16[3,128,128]{2,1,0:T(8,128)(2,1)S(1)}, bf16[3,128,128]{2,1,0:T(8,128)(2,1)S(1)}, u32[]{:S(2)}, u32[]{:S(2)}) collective-permute-start(bf16[3,128,128]{2,1,0:T(8,128)(2,1)S(1)} %get-tuple-element.65), channel_id=1, source_target_pairs={{0,12},{4,8},{8,4},{12,0},{16,28},{20,24},{24,20},{28,16},{1,13},{... | collective-permute-start | bytes 294920 | tf_op jit(solution)/shard_map/ppermute | solution.py:80
  32.0 5.1 %collective-permute-start.18 = (bf16[3,128,128]{2,1,0:T(8,128)(2,1)S(1)}, bf16[3,128,128]{2,1,0:T(8,128)(2,1)S(1)}, u32[]{:S(2)}, u32[]{:S(2)}) collective-permute-start(bf16[3,128,128]{2,1,0:T(8,128)(2,1)S(1)} %get-tuple-element.66), channel_id=1, source_target_pairs={{0,8},{4,12},{8,0},{12,4},{16,24},{20,28},{24,16},{28,20},{1,9},{5... | collective-permute-start | bytes 294920 | tf_op jit(solution)/shard_map/ppermute | solution.py:80
  33.6 4.6 %collective-permute-start.19 = (bf16[3,128,128]{2,1,0:T(8,128)(2,1)S(1)}, bf16[3,128,128]{2,1,0:T(8,128)(2,1)S(1)}, u32[]{:S(2)}, u32[]{:S(2)}) collective-permute-start(bf16[3,128,128]{2,1,0:T(8,128)(2,1)S(1)} %get-tuple-element.67), channel_id=1, source_target_pairs={{0,4},{4,0},{8,12},{12,8},{16,20},{20,16},{24,28},{28,24},{1,5},{5... | collective-permute-start | bytes 294920 | tf_op jit(solution)/shard_map/ppermute | solution.py:80
  35.3 5.0 %collective-permute-start.16 = (bf16[1,128,512]{2,1,0:T(8,128)(2,1)S(1)}, bf16[1,128,512]{2,1,0:T(8,128)(2,1)S(1)}, u32[]{:S(2)}, u32[]{:S(2)}) collective-permute-start(bf16[1,128,512]{2,1,0:T(8,128)(2,1)S(1)} %get-tuple-element.64), channel_id=1, source_target_pairs={{0,2},{1,3},{2,0},{3,1},{4,6},{5,7},{6,4},{7,5},{8,10},{9,11},{10,... | collective-permute-start | bytes 393224 | tf_op jit(solution)/shard_map/ppermute | solution.py:80

commit v13 on v11

--- a/solution.py
+++ b/solution.py
@@ -178,12 +178,17 @@
     total_ref[...] = bf(mm(qkv_ref[2], kf, TN))
 
 
-def inner_kernel(rows, qkv_ref, om_ref, kf_ref, qf_ref, scores_ref, num_ref):
+def inner_kernel(n, *refs):
+    gm_in, (qkv_ref, om_ref, kf_ref) = refs[:n][::-1], refs[n : n + 3]
+    gm_ref, qf_ref, scores_ref, num_ref = refs[n + 3 :]
     long, dim = num_ref.shape
-    n = long // rows
+    rows = long // n
+    r = member(n)
+    for k in range(n):
+        gm_ref[pl.ds(pl.multiple_of((r ^ k) * rows, 128), rows), :] = gm_in[k][...]
     scale = dim ** (-0.25)
     spans = tiles(long, rows)
-    qf = bf(jnp.exp(mm(qkv_ref[0], om_ref[member(n)]) * scale))
+    qf = bf(jnp.exp(mm(qkv_ref[0], om_ref[r]) * scale))
     qf_ref[...] = qf
     scores = lower(qf, kf_ref[...], spans)
     for (i, j), tile in scores.items():
@@ -193,22 +198,20 @@
 
 
 def turn_kernel(n, *refs):
-    gm_in, (qf_ref, num_ref), earlier = refs[:n][::-1], refs[n : n + 2], refs[n + 2 : -n - 4]
+    gm_ref, qf_ref, num_ref, *earlier = refs[: -n - 4]
     carried_ref, gn_ref, total_ref = refs[-n - 4 : -n - 1]
     outs, scr = refs[-n - 1 : -1], refs[-1]
     r = member(n)
-    rows = gm_in[0].shape[0]
+    rows = outs[0].shape[0]
     places = [
         pl.ds(pl.multiple_of((r ^ k) * rows, 128), rows) for k in range(n)
     ]
-    for k in range(n):
-        scr[places[k], :] = gm_in[k][...]
     carried = sum_of_side(earlier, n, True)
     carried_ref[...] = carried
     num = num_ref[...] + mm(qf_ref[...], carried, NT)
     inv = lax.rsqrt(jnp.mean(num * num, axis=1, keepdims=True) + EPSILON)
     normed = num * inv
-    gm = scr[...].astype(jnp.float32)
+    gm = gm_ref[...].astype(jnp.float32)
     gn = bf((gm - normed * jnp.mean(gm * normed, axis=1, keepdims=True)) * inv)
     gn_ref[...] = gn
     scr[...] = bf(normed)
@@ -334,10 +337,10 @@
         flops=2 * macs, specs=[VMEM] * (n + 3) + [ANY],
     )
     earlier = swap_totals(total, n)
-    qf, scores, num = call(
-        functools.partial(inner_kernel, rows),
-        [struct((long, feats)), struct((long, long)), struct((long, dim), f32)],
-        qkv, feature_proj, kf, flops=4 * macs,
+    gm, qf, scores, num = call(
+        functools.partial(inner_kernel, n),
+        [struct((long, dim)), struct((long, feats)), struct((long, long)), struct((long, dim), f32)],
+        *gm_in, qkv, feature_proj, kf, flops=16 * macs,
     )
     carried, gn, later_total, *mixed_parts = call(
         functools.partial(turn_kernel, n),
@@ -347,7 +350,7 @@
             struct((dim, feats)),
         ]
         + [struct((rows, dim))] * n,
-        *gm_in, qf, num, *earlier, flops=2 * macs,
+        gm, qf, num, *earlier, flops=2 * macs,
         scratch=[pltpu.VMEM((long, dim), jnp.bfloat16)],
     )
     after = swap_totals(later_total, n)

time: 40.3 us -> 40.7 us (level)
  starting transfers between devices: 20.8 us -> 23.4 us
  waiting for transfers between devices: 12 us -> 9.74 us
    ppermute x19, starting transfers between devices: 20.8 us -> 23.4 us  [swap(): return lax.ppermute(array, axis, [(i, i ^ bit) for i in range(size)])]
    ppermute x19, waiting for transfers between devices: 12 us -> 9.74 us  [swap(): return lax.ppermute(array, axis, [(i, i ^ bit) for i in range(size)])]
  transfers between devices with their start and end apart: 19 -> 19, of which waited for: 12 -> 8; matrix products, arithmetic and copies ran while one was open for 0% -> 0% of each run, Pallas kernels for 10% -> 11%
where the time goes in v13:
time: 40.7 us; the launch traced here: 40.5 us
  starting transfers between devices  23.4 us (57%)
  waiting for transfers between devices  9.74 us (24%)
  Pallas kernels  6.35 us (16%)
  between operations  0.82 us (2%)
    ppermute x19, starting transfers between devices, swap(): return lax.ppermute(array, axis, [(i, i ^ bit) for i in range(size)])  23.4 us
    ppermute x19, waiting for transfers between devices, swap(): return lax.ppermute(array, axis, [(i, i ^ bit) for i in range(size)])  9.74 us
    pallas_call x10, Pallas kernels, call(): pl.pallas_call(body, out_shape=outs, in_specs=specs or [VMEM] * len(args)...  6.35 us
  transfers between devices with their start and end apart: 19, of which 8 were waited for; matrix products, arithmetic and copies ran while one was open for 0% of the time, Pallas kernels for 11%

profile of v13, /device:TPU:0, one launch (start us, length us, event | category | flops | bytes accessed | tf_op | source)
XLA Modules:
  0.0 40.5 jit_solution(11132411322935256550)
XLA Ops:
  0.6 3.0 %collective-permute-start.3 = (bf16[128,512]{1,0:T(8,128)(2,1)}, bf16[128,512]{1,0:T(8,128)(2,1)S(1)}, u32[]{:S(2)}, u32[]{:S(2)}) collective-permute-start(bf16[128,512]{1,0:T(8,128)(2,1)} %refs_0_.1), channel_id=1, source_target_pairs={{0,2},{1,3},{2,0},{3,1},{4,6},{5,7},{6,4},{7,5},{8,10},{9,11},{10,... | collective-permute-start | bytes 393224 | tf_op jit(solution)/shard_map/ppermute | solution.py:80
  3.6 0.0 collective-permute-start.4
  3.6 1.0 %shard_map.93 = (bf16[3,128,128]{2,1,0:T(8,128)(2,1)S(1)}, bf16[3,128,128]{2,1,0:T(8,128)(2,1)S(1)}, bf16[3,128,128]{2,1,0:T(8,128)(2,1)S(1)}) custom-call(bf16[128,512]{1,0:T(8,128)(2,1)} %refs_3_.1, bf16[128,512]{1,0:T(8,128)(2,1)} %refs_4_.4, bf16[128,512]{1,0:T(8,128)(2,1)} %refs_5_.2), custom_call_target="tpu_custom_call" | custom-call | bytes 688128 | tf_op jit(solution)/shard_map/pallas_call | solution.py:29
  4.6 2.6 %collective-permute-start = (bf16[3,128,128]{2,1,0:T(8,128)(2,1)S(1)}, bf16[3,128,128]{2,1,0:T(8,128)(2,1)S(1)}, u32[]{:S(2)}, u32[]{:S(2)}) collective-permute-start(bf16[3,128,128]{2,1,0:T(8,128)(2,1)S(1)} %get-tuple-element.34), channel_id=1, source_target_pairs={{0,12},{4,8},{8,4},{12,0},{16,28},{20,24},{24,20},{28,16},{1,13},{... | collective-permute-start | bytes 294920 | tf_op jit(solution)/shard_map/ppermute | solution.py:80
  7.2 0.4 %collective-permute-start.1 = (bf16[3,128,128]{2,1,0:T(8,128)(2,1)S(1)}, bf16[3,128,128]{2,1,0:T(8,128)(2,1)S(1)}, u32[]{:S(2)}, u32[]{:S(2)}) collective-permute-start(bf16[3,128,128]{2,1,0:T(8,128)(2,1)S(1)} %get-tuple-element.35), channel_id=1, source_target_pairs={{0,8},{4,12},{8,0},{12,4},{16,24},{20,28},{24,16},{28,20},{1,9},{5... | collective-permute-start | bytes 294920 | tf_op jit(solution)/shard_map/ppermute | solution.py:80
  7.7 0.5 %collective-permute-start.2 = (bf16[3,128,128]{2,1,0:T(8,128)(2,1)S(1)}, bf16[3,128,128]{2,1,0:T(8,128)(2,1)S(1)}, u32[]{:S(2)}, u32[]{:S(2)}) collective-permute-start(bf16[3,128,128]{2,1,0:T(8,128)(2,1)S(1)} %get-tuple-element.36), channel_id=1, source_target_pairs={{0,4},{4,0},{8,12},{12,8},{16,20},{20,16},{24,28},{28,24},{1,5},{5... | collective-permute-start | bytes 294920 | tf_op jit(solution)/shard_map/ppermute | solution.py:80
  8.2 0.0 collective-permute-done.3.refs_1_
  8.2 0.0 collective-permute-start.5
  8.2 0.0 collective-permute-done.4._.refs_2_
  8.2 0.0 copy-start.1
  8.2 0.0 copy-start.2
  8.2 0.0 copy-start.3
  8.2 0.0 copy-start.4
  8.2 1.3 %collective-permute-done.5.refs_3_ = bf16[128,512]{1,0:T(8,128)(2,1)S(1)} collective-permute-done((bf16[128,512]{1,0:T(8,128)(2,1)S(1)}, bf16[128,512]{1,0:T(8,128)(2,1)S(1)}, u32[]{:S(2)}, u32[]{:S(2)}) %collective-permute-start.5) | collective-permute-done | bytes 131104 | tf_op jit(solution)/shard_map/ppermute | solution.py:80
  9.5 0.9 %shard_map.95 = (bf16[128,128]{1,0:T(8,128)(2,1)S(1)}, bf16[128,128]{1,0:T(8,128)(2,1)S(1)}, bf16[128,128]{1,0:T(8,128)(2,1)S(1)}, bf16[128,128]{1,0:T(8,128)(2,1)S(1)}) custom-call(bf16[128,512]{1,0:T(8,128)(2,1)S(1)} %copy-done.5, bf16[128,512]{1,0:T(8,128)(2,1)S(1)} %collective-permute-done.3.refs_1_, ...), custom_call_target="tpu_custom_call" | custom-call | flops 268435456 | bytes 2756608 | tf_op jit(solution)/shard_map/pallas_call | solution.py:29
  10.4 2.6 %collective-permute-start.6 = (bf16[128,128]{1,0:T(8,128)(2,1)S(1)}, bf16[128,128]{1,0:T(8,128)(2,1)S(1)}, u32[]{:S(2)}, u32[]{:S(2)}) collective-permute-start(bf16[128,128]{1,0:T(8,128)(2,1)S(1)} %get-tuple-element.40), channel_id=1, source_target_pairs={{0,12},{4,8},{8,4},{12,0},{16,28},{20,24},{24,20},{28,16},{1,13},{... | collective-permute-start | bytes 98312 | tf_op jit(solution)/shard_map/ppermute | solution.py:80
  13.0 0.4 %collective-permute-start.7 = (bf16[128,128]{1,0:T(8,128)(2,1)S(1)}, bf16[128,128]{1,0:T(8,128)(2,1)S(1)}, u32[]{:S(2)}, u32[]{:S(2)}) collective-permute-start(bf16[128,128]{1,0:T(8,128)(2,1)S(1)} %get-tuple-element.41), channel_id=1, source_target_pairs={{0,8},{4,12},{8,0},{12,4},{16,24},{20,28},{24,16},{28,20},{1,9},{5... | collective-permute-start | bytes 98312 | tf_op jit(solution)/shard_map/ppermute | solution.py:80
  13.4 0.0 collective-permute-done.refs_0_
  13.4 0.5 %collective-permute-start.8 = (bf16[128,128]{1,0:T(8,128)(2,1)S(1)}, bf16[128,128]{1,0:T(8,128)(2,1)S(1)}, u32[]{:S(2)}, u32[]{:S(2)}) collective-permute-start(bf16[128,128]{1,0:T(8,128)(2,1)S(1)} %get-tuple-element.42), channel_id=1, source_target_pairs={{0,4},{4,0},{8,12},{12,8},{16,20},{20,16},{24,28},{28,24},{1,5},{5... | collective-permute-start | bytes 98312 | tf_op jit(solution)/shard_map/ppermute | solution.py:80
  14.0 0.0 collective-permute-done.1.refs_1_
  14.0 0.0 collective-permute-done.2.refs_2_
  14.0 0.5 %shard_map.96 = (bf16[3,512,128]{2,1,0:T(8,128)(2,1)S(1)}, bf16[512,256]{1,0:T(8,128)(2,1)S(1)}, bf16[128,256]{1,0:T(8,128)(2,1)S(1)}) custom-call(bf16[3,128,128]{2,1,0:T(8,128)(2,1)S(1)} %collective-permute-done.refs_0_, bf16[3,128,128]{2,1,0:T(8,128)(2,1)S(1)} %collective-permute-done.1.refs_1_, bf16[3,128,128]{2,1,0:T(8,128)(2,1)S(1)} %collective-permute-done.2.refs_2_, ...), custom_call_target="tpu_custom_call" | custom-call | flops 67108864 | bytes 1703936 | tf_op jit(solution)/shard_map/pallas_call | solution.py:29
  14.5 2.7 %collective-permute-start.9 = (bf16[128,256]{1,0:T(8,128)(2,1)S(1)}, bf16[128,256]{1,0:T(8,128)(2,1)S(1)}, u32[]{:S(2)}, u32[]{:S(2)}) collective-permute-start(bf16[128,256]{1,0:T(8,128)(2,1)S(1)} %get-tuple-element.47), channel_id=1, source_target_pairs={{0,16},{4,20},{8,24},{12,28},{16,0},{20,4},{24,8},{28,12},{1,17},{... | collective-permute-start | bytes 196616 | tf_op jit(solution)/shard_map/ppermute | solution.py:80
  17.1 0.0 collective-permute-done.6.refs_0_
  17.1 0.2 collective-permute-done.8.refs_2_
  17.4 0.5 %shard_map.97 = (bf16[512,128]{1,0:T(8,128)(2,1)S(1)}, bf16[512,256]{1,0:T(8,128)(2,1)S(1)}, bf16[512,512]{1,0:T(8,128)(2,1)S(1)}, f32[512,128]{1,0:T(8,128)S(1)}) custom-call(bf16[128,128]{1,0:T(8,128)(2,1)S(1)} %collective-permute-done.6.refs_0_, bf16[128,128]{1,0:T(8,128)(2,1)S(1)} %collective-permute-done.7.refs_1_, ...), custom_call_target="tpu_custom_call" | custom-call | flops 536870912 | bytes 2228224 | tf_op jit(solution)/shard_map/pallas_call | solution.py:29
  17.9 2.1 %collective-permute-done.9.refs_3_ = bf16[128,256]{1,0:T(8,128)(2,1)S(1)} collective-permute-done((bf16[128,256]{1,0:T(8,128)(2,1)S(1)}, bf16[128,256]{1,0:T(8,128)(2,1)S(1)}, u32[]{:S(2)}, u32[]{:S(2)}) %collective-permute-start.9) | collective-permute-done | bytes 65568 | tf_op jit(solution)/shard_map/ppermute | solution.py:80
  20.0 0.6 %shard_map.98 = (bf16[128,256]{1,0:T(8,128)(2,1)S(1)}, bf16[512,128]{1,0:T(8,128)(2,1)S(1)}, bf16[128,256]{1,0:T(8,128)(2,1)S(1)}, bf16[128,128]{1,0:T(8,128)(2,...) custom-call(bf16[512,128]{1,0:T(8,128)(2,1)S(1)} %get-tuple-element.45.refs_0_, ...), custom_call_target="tpu_custom_call" | custom-call | flops 67108864 | bytes 1114112 | tf_op jit(solution)/shard_map/pallas_call | solution.py:29
  20.6 2.4 %collective-permute-start.10 = (bf16[128,256]{1,0:T(8,128)(2,1)S(1)}, bf16[128,256]{1,0:T(8,128)(2,1)S(1)}, u32[]{:S(2)}, u32[]{:S(2)}) collective-permute-start(bf16[128,256]{1,0:T(8,128)(2,1)S(1)} %get-tuple-element.53), channel_id=1, source_target_pairs={{0,16},{4,20},{8,24},{12,28},{16,0},{20,4},{24,8},{28,12},{1,17},{... | collective-permute-start | bytes 196616 | tf_op jit(solution)/shard_map/ppermute | solution.py:80
  23.1 3.1 %collective-permute-start.14 = (bf16[128,128]{1,0:T(8,128)(2,1)S(1)}, bf16[128,128]{1,0:T(8,128)(2,1)S(1)}, u32[]{:S(2)}, u32[]{:S(2)}) collective-permute-start(bf16[128,128]{1,0:T(8,128)(2,1)S(1)} %get-tuple-element.58), channel_id=1, source_target_pairs={{0,12},{4,8},{8,4},{12,0},{16,28},{20,24},{24,20},{28,16},{1,13},{... | collective-permute-start | bytes 98312 | tf_op jit(solution)/shard_map/ppermute | solution.py:80
  26.1 0.0 collective-permute-start.15
  26.1 0.6 %collective-permute-start.16 = (bf16[128,128]{1,0:T(8,128)(2,1)S(1)}, bf16[128,128]{1,0:T(8,128)(2,1)S(1)}, u32[]{:S(2)}, u32[]{:S(2)}) collective-permute-start(bf16[128,128]{1,0:T(8,128)(2,1)S(1)} %get-tuple-element.60), channel_id=1, source_target_pairs={{0,4},{4,0},{8,12},{12,8},{16,20},{20,16},{24,28},{28,24},{1,5},{5... | collective-permute-start | bytes 98312 | tf_op jit(solution)/shard_map/ppermute | solution.py:80
  26.7 1.0 %shard_map.99 = (bf16[512,128]{1,0:T(8,128)(2,1)S(1)}, f32[512,128]{1,0:T(8,128)S(1)}, f32[512,256]{1,0:T(8,128)S(1)}) custom-call(bf16[3,512,128]{2,1,0:T(8,128)(2,1)S(1)} %get-tuple-element.38.refs_4_.qkv_ref, bf16[4,128,256]{2,1,0:T(8,128)(2,1)S(1)} %copy-done.1, bf16[512,256]{1,0:T(8,128)(2,1)S(1)} %get-tuple-element.39.refs_6_.kf_ref, ...), custom_call_target="tpu_custom_call" | custom-call | flops 268435456 | bytes 2818048 | tf_op jit(solution)/shard_map/pallas_call | solution.py:29
  27.6 0.0 collective-permute-done.10.rest_0_
  27.7 0.6 %shard_map.100 = (bf16[3,128,128]{2,1,0:T(8,128)(2,1)S(1)}, bf16[3,128,128]{2,1,0:T(8,128)(2,1)S(1)}, bf16[3,128,128]{2,1,0:T(8,128)(2,1)S(1)}, bf16[3,128,128]{2,1,0:T(8,128)(2,1)S(1)}) custom-call(bf16[3,512,128]{2,1,0:T(8,128)(2,1)S(1)} %get-tuple-element.38.refs_4_.qkv_ref, bf16[4,128,256]{2,1,0:T(8,128)(2,1)S(1)} %copy-done.1, ...), custom_call_target="tpu_custom_call" | custom-call | flops 100663296 | bytes 2293760 | tf_op jit(solution)/shard_map/pallas_call | solution.py:29
  28.3 1.8 %collective-permute-done.15.refs_1_ = bf16[128,128]{1,0:T(8,128)(2,1)S(1)} collective-permute-done((bf16[128,128]{1,0:T(8,128)(2,1)S(1)}, bf16[128,128]{1,0:T(8,128)(2,1)S(1)}, u32[]{:S(2)}, u32[]{:S(2)}) %collective-permute-start.15) | collective-permute-done | bytes 32800 | tf_op jit(solution)/shard_map/ppermute | solution.py:80
  30.0 0.4 %shard_map.101 = (bf16[2,128,512]{2,1,0:T(8,128)(2,1)S(1)}, bf16[2,128,512]{2,1,0:T(8,128)(2,1)S(1)}) custom-call(bf16[128,128]{1,0:T(8,128)(2,1)S(1)} %collective-permute-done.14.refs_0_, bf16[128,128]{1,0:T(8,128)(2,1)S(1)} %collective-permute-done.15.refs_1_, bf16[128,128]{1,0:T(8,128)(2,1)S(1)} %collective-permute-done.16.refs_2_, ...), custom_call_target="tpu_custom_call" | custom-call | flops 268435456 | bytes 2850816 | tf_op jit(solution)/shard_map/pallas_call | solution.py:29
  30.5 0.1 collective-permute-start.17
  30.6 2.0 %collective-permute-start.11 = (bf16[3,128,128]{2,1,0:T(8,128)(2,1)S(1)}, bf16[3,128,128]{2,1,0:T(8,128)(2,1)S(1)}, u32[]{:S(2)}, u32[]{:S(2)}) collective-permute-start(bf16[3,128,128]{2,1,0:T(8,128)(2,1)S(1)} %get-tuple-element.54), channel_id=1, source_target_pairs={{0,12},{4,8},{8,4},{12,0},{16,28},{20,24},{24,20},{28,16},{1,13},{... | collective-permute-start | bytes 294920 | tf_op jit(solution)/shard_map/ppermute | solution.py:80
  32.6 0.1 collective-permute-start.12
  32.7 1.4 %collective-permute-start.13 = (bf16[3,128,128]{2,1,0:T(8,128)(2,1)S(1)}, bf16[3,128,128]{2,1,0:T(8,128)(2,1)S(1)}, u32[]{:S(2)}, u32[]{:S(2)}) collective-permute-start(bf16[3,128,128]{2,1,0:T(8,128)(2,1)S(1)} %get-tuple-element.56), channel_id=1, source_target_pairs={{0,4},{4,0},{8,12},{12,8},{16,20},{20,16},{24,28},{28,24},{1,5},{5... | collective-permute-start | bytes 294920 | tf_op jit(solution)/shard_map/ppermute | solution.py:80
  34.1 0.1 add_bitcast_fusion
  34.2 1.0 %collective-permute-start.18 = (bf16[1,128,512]{2,1,0:T(8,128)(2,1)S(1)}, bf16[1,128,512]{2,1,0:T(8,128)(2,1)S(1)}, u32[]{:S(2)}, u32[]{:S(2)}) collective-permute-start(bf16[1,128,512]{2,1,0:T(8,128)(2,1)S(1)} %fusion), channel_id=1, source_target_pairs={{0,2},{1,3},{2,0},{3,1},{4,6},{5,7},{6,4},{7,5},{8,10},{9,11},{10,... | collective-permute-start | bytes 393224 | tf_op jit(solution)/shard_map/ppermute | solution.py:80
  35.2 1.8 %collective-permute-done.11.refs_0_ = bf16[3,128,128]{2,1,0:T(8,128)(2,1)S(1)} collective-permute-done((bf16[3,128,128]{2,1,0:T(8,128)(2,1)S(1)}, bf16[3,128,128]{2,1,0:T(8,128)(2,1)S(1)}, u32[]{:S(2)}, u32[]{:S(2)}) %collective-permute-start.11) | collective-permute-done | bytes 98336 | tf_op jit(solution)/shard_map/ppermute | solution.py:80
  37.0 1.1 %collective-permute-done.12.refs_1_ = bf16[3,128,128]{2,1,0:T(8,128)(2,1)S(1)} collective-permute-done((bf16[3,128,128]{2,1,0:T(8,128)(2,1)S(1)}, bf16[3,128,128]{2,1,0:T(8,128)(2,1)S(1)}, u32[]{:S(2)}, u32[]{:S(2)}) %collective-permute-start.12) | collective-permute-done | bytes 98336 | tf_op jit(solution)/shard_map/ppermute | solution.py:80
  38.1 0.6 %collective-permute-done.13.refs_2_ = bf16[3,128,128]{2,1,0:T(8,128)(2,1)S(1)} collective-permute-done((bf16[3,128,128]{2,1,0:T(8,128)(2,1)S(1)}, bf16[3,128,128]{2,1,0:T(8,128)(2,1)S(1)}, u32[]{:S(2)}, u32[]{:S(2)}) %collective-permute-start.13) | collective-permute-done | bytes 98336 | tf_op jit(solution)/shard_map/ppermute | solution.py:80
  38.8 0.8 %collective-permute-done.18 = bf16[1,128,512]{2,1,0:T(8,128)(2,1)S(1)} collective-permute-done((bf16[1,128,512]{2,1,0:T(8,128)(2,1)S(1)}, bf16[1,128,512]{2,1,0:T(8,128)(2,1)S(1)}, u32[]{:S(2)}, u32[]{:S(2)}) %collective-permute-start.18) | collective-permute-done | bytes 131104 | tf_op jit(solution)/shard_map/ppermute | solution.py:80
  39.6 0.9 %shard_map.102 = (bf16[128,512]{1,0:T(8,128)(2,1)}, bf16[128,512]{1,0:T(8,128)(2,1)}, bf16[128,512]{1,0:T(8,128)(2,1)}, bf16[128,512]{1,0:T(8,128)(2,1)}) custom-call(bf16[3,128,128]{2,1,0:T(8,128)(2,1)S(1)} %collective-permute-done.11.refs_0_, bf16[3,128,128]{2,1,0:T(8,128)(2,1)S(1)} %collective-permute-done.12.refs_1_, ...), custom_call_target="tpu_custom_call" | custom-call | bytes 1310720 | tf_op jit(solution)/shard_map/pallas_call | solution.py:29
  (15 shorter events, 0.1 us)
Async XLA Ops:
  0.6 7.5 %collective-permute-start.3 = (bf16[128,512]{1,0:T(8,128)(2,1)}, bf16[128,512]{1,0:T(8,128)(2,1)S(1)}, u32[]{:S(2)}, u32[]{:S(2)}) collective-permute-start(bf16[128,512]{1,0:T(8,128)(2,1)} %refs_0_.1), channel_id=1, source_target_pairs={{0,2},{1,3},{2,0},{3,1},{4,6},{5,7},{6,4},{7,5},{8,10},{9,11},{10,... | collective-permute-start | bytes 393224 | tf_op jit(solution)/shard_map/ppermute | solution.py:80
  3.6 4.5 %collective-permute-start.4 = (bf16[128,512]{1,0:T(8,128)(2,1)}, bf16[128,512]{1,0:T(8,128)(2,1)S(1)}, u32[]{:S(2)}, u32[]{:S(2)}) collective-permute-start(bf16[128,512]{1,0:T(8,128)(2,1)} %refs_0_.1), channel_id=1, source_target_pairs={{0,1},{1,0},{2,3},{3,2},{4,5},{5,4},{6,7},{7,6},{8,9},{9,8},{10,11... | collective-permute-start | bytes 393224 | tf_op jit(solution)/shard_map/ppermute | solution.py:80
  4.6 8.8 %collective-permute-start = (bf16[3,128,128]{2,1,0:T(8,128)(2,1)S(1)}, bf16[3,128,128]{2,1,0:T(8,128)(2,1)S(1)}, u32[]{:S(2)}, u32[]{:S(2)}) collective-permute-start(bf16[3,128,128]{2,1,0:T(8,128)(2,1)S(1)} %get-tuple-element.34), channel_id=1, source_target_pairs={{0,12},{4,8},{8,4},{12,0},{16,28},{20,24},{24,20},{28,16},{1,13},{... | collective-permute-start | bytes 294920 | tf_op jit(solution)/shard_map/ppermute | solution.py:80
  7.2 6.7 %collective-permute-start.1 = (bf16[3,128,128]{2,1,0:T(8,128)(2,1)S(1)}, bf16[3,128,128]{2,1,0:T(8,128)(2,1)S(1)}, u32[]{:S(2)}, u32[]{:S(2)}) collective-permute-start(bf16[3,128,128]{2,1,0:T(8,128)(2,1)S(1)} %get-tuple-element.35), channel_id=1, source_target_pairs={{0,8},{4,12},{8,0},{12,4},{16,24},{20,28},{24,16},{28,20},{1,9},{5... | collective-permute-start | bytes 294920 | tf_op jit(solution)/shard_map/ppermute | solution.py:80
  7.7 1.9 %copy-start = (bf16[512,2048]{1,0:T(8,128)(2,1)S(1)}, bf16[512,2048]{1,0:T(8,128)(2,1)}, u32[]{:S(2)}) copy-start(bf16[512,2048]{1,0:T(8,128)(2,1)} %refs_4_.5) | copy-start | bytes 6291460
  7.7 1.9 %copy-start.5 = (bf16[128,512]{1,0:T(8,128)(2,1)S(1)}, bf16[128,512]{1,0:T(8,128)(2,1)}, u32[]{:S(2)}) copy-start(bf16[128,512]{1,0:T(8,128)(2,1)} %refs_0_.1) | copy-start | bytes 393220
  7.7 6.3 %collective-permute-start.2 = (bf16[3,128,128]{2,1,0:T(8,128)(2,1)S(1)}, bf16[3,128,128]{2,1,0:T(8,128)(2,1)S(1)}, u32[]{:S(2)}, u32[]{:S(2)}) collective-permute-start(bf16[3,128,128]{2,1,0:T(8,128)(2,1)S(1)} %get-tuple-element.36), channel_id=1, source_target_pairs={{0,4},{4,0},{8,12},{12,8},{16,20},{20,16},{24,28},{28,24},{1,5},{5... | collective-permute-start | bytes 294920 | tf_op jit(solution)/shard_map/ppermute | solution.py:80
  8.2 1.3 %collective-permute-start.5 = (bf16[128,512]{1,0:T(8,128)(2,1)S(1)}, bf16[128,512]{1,0:T(8,128)(2,1)S(1)}, u32[]{:S(2)}, u32[]{:S(2)}) collective-permute-start(bf16[128,512]{1,0:T(8,128)(2,1)S(1)} %collective-permute-done.3.refs_1_), channel_id=1, source_target_pairs={{0,1},{1,0},{2,3},{3,2},{4,5},{5,4},{6,7},{7,6},{8,9},{9,8},{10,11... | collective-permute-start | bytes 393224 | tf_op jit(solution)/shard_map/ppermute | solution.py:80
  8.2 5.8 %copy-start.1 = (bf16[4,128,256]{2,1,0:T(8,128)(2,1)S(1)}, bf16[4,128,256]{2,1,0:T(8,128)(2,1)}, u32[]{:S(2)}) copy-start(bf16[4,128,256]{2,1,0:T(8,128)(2,1)} %om_ref.3) | copy-start | bytes 786436
  8.2 5.8 %copy-start.2 = (bf16[128,512]{1,0:T(8,128)(2,1)S(1)}, bf16[128,512]{1,0:T(8,128)(2,1)}, u32[]{:S(2)}) copy-start(bf16[128,512]{1,0:T(8,128)(2,1)} %refs_3_.1) | copy-start | bytes 393220
  8.2 5.8 %copy-start.3 = (bf16[128,512]{1,0:T(8,128)(2,1)S(1)}, bf16[128,512]{1,0:T(8,128)(2,1)}, u32[]{:S(2)}) copy-start(bf16[128,512]{1,0:T(8,128)(2,1)} %refs_4_.4) | copy-start | bytes 393220
  8.2 5.8 %copy-start.4 = (bf16[128,512]{1,0:T(8,128)(2,1)S(1)}, bf16[128,512]{1,0:T(8,128)(2,1)}, u32[]{:S(2)}) copy-start(bf16[128,512]{1,0:T(8,128)(2,1)} %refs_5_.2) | copy-start | bytes 393220
  10.4 6.7 %collective-permute-start.6 = (bf16[128,128]{1,0:T(8,128)(2,1)S(1)}, bf16[128,128]{1,0:T(8,128)(2,1)S(1)}, u32[]{:S(2)}, u32[]{:S(2)}) collective-permute-start(bf16[128,128]{1,0:T(8,128)(2,1)S(1)} %get-tuple-element.40), channel_id=1, source_target_pairs={{0,12},{4,8},{8,4},{12,0},{16,28},{20,24},{24,20},{28,16},{1,13},{... | collective-permute-start | bytes 98312 | tf_op jit(solution)/shard_map/ppermute | solution.py:80
  13.0 4.1 %collective-permute-start.7 = (bf16[128,128]{1,0:T(8,128)(2,1)S(1)}, bf16[128,128]{1,0:T(8,128)(2,1)S(1)}, u32[]{:S(2)}, u32[]{:S(2)}) collective-permute-start(bf16[128,128]{1,0:T(8,128)(2,1)S(1)} %get-tuple-element.41), channel_id=1, source_target_pairs={{0,8},{4,12},{8,0},{12,4},{16,24},{20,28},{24,16},{28,20},{1,9},{5... | collective-permute-start | bytes 98312 | tf_op jit(solution)/shard_map/ppermute | solution.py:80
  13.4 3.9 %collective-permute-start.8 = (bf16[128,128]{1,0:T(8,128)(2,1)S(1)}, bf16[128,128]{1,0:T(8,128)(2,1)S(1)}, u32[]{:S(2)}, u32[]{:S(2)}) collective-permute-start(bf16[128,128]{1,0:T(8,128)(2,1)S(1)} %get-tuple-element.42), channel_id=1, source_target_pairs={{0,4},{4,0},{8,12},{12,8},{16,20},{20,16},{24,28},{28,24},{1,5},{5... | collective-permute-start | bytes 98312 | tf_op jit(solution)/shard_map/ppermute | solution.py:80
  14.5 5.5 %collective-permute-start.9 = (bf16[128,256]{1,0:T(8,128)(2,1)S(1)}, bf16[128,256]{1,0:T(8,128)(2,1)S(1)}, u32[]{:S(2)}, u32[]{:S(2)}) collective-permute-start(bf16[128,256]{1,0:T(8,128)(2,1)S(1)} %get-tuple-element.47), channel_id=1, source_target_pairs={{0,16},{4,20},{8,24},{12,28},{16,0},{20,4},{24,8},{28,12},{1,17},{... | collective-permute-start | bytes 196616 | tf_op jit(solution)/shard_map/ppermute | solution.py:80
  20.6 7.0 %collective-permute-start.10 = (bf16[128,256]{1,0:T(8,128)(2,1)S(1)}, bf16[128,256]{1,0:T(8,128)(2,1)S(1)}, u32[]{:S(2)}, u32[]{:S(2)}) collective-permute-start(bf16[128,256]{1,0:T(8,128)(2,1)S(1)} %get-tuple-element.53), channel_id=1, source_target_pairs={{0,16},{4,20},{8,24},{12,28},{16,0},{20,4},{24,8},{28,12},{1,17},{... | collective-permute-start | bytes 196616 | tf_op jit(solution)/shard_map/ppermute | solution.py:80
  23.1 5.2 %collective-permute-start.14 = (bf16[128,128]{1,0:T(8,128)(2,1)S(1)}, bf16[128,128]{1,0:T(8,128)(2,1)S(1)}, u32[]{:S(2)}, u32[]{:S(2)}) collective-permute-start(bf16[128,128]{1,0:T(8,128)(2,1)S(1)} %get-tuple-element.58), channel_id=1, source_target_pairs={{0,12},{4,8},{8,4},{12,0},{16,28},{20,24},{24,20},{28,16},{1,13},{... | collective-permute-start | bytes 98312 | tf_op jit(solution)/shard_map/ppermute | solution.py:80
  26.1 3.9 %collective-permute-start.15 = (bf16[128,128]{1,0:T(8,128)(2,1)S(1)}, bf16[128,128]{1,0:T(8,128)(2,1)S(1)}, u32[]{:S(2)}, u32[]{:S(2)}) collective-permute-start(bf16[128,128]{1,0:T(8,128)(2,1)S(1)} %get-tuple-element.59), channel_id=1, source_target_pairs={{0,8},{4,12},{8,0},{12,4},{16,24},{20,28},{24,16},{28,20},{1,9},{5... | collective-permute-start | bytes 98312 | tf_op jit(solution)/shard_map/ppermute | solution.py:80
  26.1 3.9 %collective-permute-start.16 = (bf16[128,128]{1,0:T(8,128)(2,1)S(1)}, bf16[128,128]{1,0:T(8,128)(2,1)S(1)}, u32[]{:S(2)}, u32[]{:S(2)}) collective-permute-start(bf16[128,128]{1,0:T(8,128)(2,1)S(1)} %get-tuple-element.60), channel_id=1, source_target_pairs={{0,4},{4,0},{8,12},{12,8},{16,20},{20,16},{24,28},{28,24},{1,5},{5... | collective-permute-start | bytes 98312 | tf_op jit(solution)/shard_map/ppermute | solution.py:80
  30.5 3.6 %collective-permute-start.17 = (bf16[2,128,512]{2,1,0:T(8,128)(2,1)S(1)}, bf16[2,128,512]{2,1,0:T(8,128)(2,1)S(1)}, u32[]{:S(2)}, u32[]{:S(2)}) collective-permute-start(bf16[2,128,512]{2,1,0:T(8,128)(2,1)S(1)} %get-tuple-element.63), channel_id=1, source_target_pairs={{0,1},{1,0},{2,3},{3,2},{4,5},{5,4},{6,7},{7,6},{8,9},{9,8},{10,11... | collective-permute-start | bytes 786440 | tf_op jit(solution)/shard_map/ppermute | solution.py:80
  30.6 6.4 %collective-permute-start.11 = (bf16[3,128,128]{2,1,0:T(8,128)(2,1)S(1)}, bf16[3,128,128]{2,1,0:T(8,128)(2,1)S(1)}, u32[]{:S(2)}, u32[]{:S(2)}) collective-permute-start(bf16[3,128,128]{2,1,0:T(8,128)(2,1)S(1)} %get-tuple-element.54), channel_id=1, source_target_pairs={{0,12},{4,8},{8,4},{12,0},{16,28},{20,24},{24,20},{28,16},{1,13},{... | collective-permute-start | bytes 294920 | tf_op jit(solution)/shard_map/ppermute | solution.py:80
  32.6 5.5 %collective-permute-start.12 = (bf16[3,128,128]{2,1,0:T(8,128)(2,1)S(1)}, bf16[3,128,128]{2,1,0:T(8,128)(2,1)S(1)}, u32[]{:S(2)}, u32[]{:S(2)}) collective-permute-start(bf16[3,128,128]{2,1,0:T(8,128)(2,1)S(1)} %get-tuple-element.55), channel_id=1, source_target_pairs={{0,8},{4,12},{8,0},{12,4},{16,24},{20,28},{24,16},{28,20},{1,9},{5... | collective-permute-start | bytes 294920 | tf_op jit(solution)/shard_map/ppermute | solution.py:80
  32.7 6.0 %collective-permute-start.13 = (bf16[3,128,128]{2,1,0:T(8,128)(2,1)S(1)}, bf16[3,128,128]{2,1,0:T(8,128)(2,1)S(1)}, u32[]{:S(2)}, u32[]{:S(2)}) collective-permute-start(bf16[3,128,128]{2,1,0:T(8,128)(2,1)S(1)} %get-tuple-element.56), channel_id=1, source_target_pairs={{0,4},{4,0},{8,12},{12,8},{16,20},{20,16},{24,28},{28,24},{1,5},{5... | collective-permute-start | bytes 294920 | tf_op jit(solution)/shard_map/ppermute | solution.py:80
  34.2 5.4 %collective-permute-start.18 = (bf16[1,128,512]{2,1,0:T(8,128)(2,1)S(1)}, bf16[1,128,512]{2,1,0:T(8,128)(2,1)S(1)}, u32[]{:S(2)}, u32[]{:S(2)}) collective-permute-start(bf16[1,128,512]{2,1,0:T(8,128)(2,1)S(1)} %fusion), channel_id=1, source_target_pairs={{0,2},{1,3},{2,0},{3,1},{4,6},{5,7},{6,4},{7,5},{8,10},{9,11},{10,... | collective-permute-start | bytes 393224 | tf_op jit(solution)/shard_map/ppermute | solution.py:80

commit v14 on v12

--- a/solution.py
+++ b/solution.py
@@ -178,12 +178,17 @@
     total_ref[...] = bf(mm(qkv_ref[2], kf, TN))
 
 
-def inner_kernel(rows, qkv_ref, om_ref, kf_ref, qf_ref, scores_ref, num_ref):
+def inner_kernel(n, *refs):
+    gm_in, (qkv_ref, om_ref, kf_ref) = refs[:n][::-1], refs[n : n + 3]
+    gm_ref, qf_ref, scores_ref, num_ref = refs[n + 3 :]
     long, dim = num_ref.shape
-    n = long // rows
+    rows = long // n
+    r = member(n)
+    for k in range(n):
+        gm_ref[pl.ds(pl.multiple_of((r ^ k) * rows, 128), rows), :] = gm_in[k][...]
     scale = dim ** (-0.25)
     spans = tiles(long, rows)
-    qf = bf(jnp.exp(mm(qkv_ref[0], om_ref[member(n)]) * scale))
+    qf = bf(jnp.exp(mm(qkv_ref[0], om_ref[r]) * scale))
     qf_ref[...] = qf
     scores = lower(qf, kf_ref[...], spans)
     for (i, j), tile in scores.items():
@@ -193,21 +198,19 @@
 
 
 def turn_kernel(n, *refs):
-    gm_in, (qf_ref, num_ref), earlier = refs[:n][::-1], refs[n : n + 2], refs[n + 2 : -5]
+    gm_ref, qf_ref, num_ref, *earlier = refs[:-5]
     carried_ref, gn_ref, total_ref, mixed_ref, scr = refs[-5:]
     r = member(n)
-    rows = gm_in[0].shape[0]
+    rows = mixed_ref.shape[1]
     places = [
         pl.ds(pl.multiple_of((r ^ k) * rows, 128), rows) for k in range(n)
     ]
-    for k in range(n):
-        scr[places[k], :] = gm_in[k][...]
     carried = sum_of_side(earlier, n, True)
     carried_ref[...] = carried
     num = num_ref[...] + mm(qf_ref[...], carried, NT)
     inv = lax.rsqrt(jnp.mean(num * num, axis=1, keepdims=True) + EPSILON)
     normed = num * inv
-    gm = scr[...].astype(jnp.float32)
+    gm = gm_ref[...].astype(jnp.float32)
     gn = bf((gm - normed * jnp.mean(gm * normed, axis=1, keepdims=True)) * inv)
     gn_ref[...] = gn
     scr[...] = bf(normed)
@@ -310,7 +313,6 @@
     for bit in reversed(bits):
         blocks = blocks + [swap(b, "head", bit) for b in blocks]
         offsets = offsets + [o ^ bit for o in offsets]
-    other_weight = swap(out_weight, "head", 1)
     sends = call(
         functools.partial(pack_kernel, n),
         [struct((3, rows, dim))] * (n - 1),
@@ -338,10 +340,10 @@
         flops=2 * macs, specs=[VMEM] * (n + 3) + [ANY],
     )
     earlier = swap_totals(total, n)
-    qf, scores, num = call(
-        functools.partial(inner_kernel, rows),
-        [struct((long, feats)), struct((long, long)), struct((long, dim), f32)],
-        qkv, feature_proj, kf, flops=4 * macs,
+    gm, qf, scores, num = call(
+        functools.partial(inner_kernel, n),
+        [struct((long, dim)), struct((long, feats)), struct((long, long)), struct((long, dim), f32)],
+        *gm_in, qkv, feature_proj, kf, flops=16 * macs,
     )
     carried, gn, later_total, mixed = call(
         functools.partial(turn_kernel, n),
@@ -351,7 +353,7 @@
             struct((dim, feats)),
             struct((n, rows, dim)),
         ],
-        *gm_in, qf, num, *earlier, flops=2 * macs,
+        gm, qf, num, *earlier, flops=2 * macs,
         scratch=[pltpu.VMEM((long, dim), jnp.bfloat16)],
     )
     after = swap_totals(later_total, n)
@@ -371,6 +373,8 @@
     )
     grads_in = exchange(grads[1:]) + [grads[0]]
 
+    held, _ = lax.optimization_barrier((out_weight, gn))
+    other_weight = swap(held, "head", 1)
     order = [o for o in range(0, split, 2) if not o & 2] + [o for o in range(2, split, 4)]
     own, sent = call(
         functools.partial(mixed_project_kernel, n, order),

time: 41.2 us -> 41 us (level)
  waiting for transfers between devices: 10 us -> 8.27 us
  starting transfers between devices: 23.2 us -> 24.8 us
    ppermute x20, waiting for transfers between devices: 10 us -> 8.27 us  [swap(): return lax.ppermute(array, axis, [(i, i ^ bit) for i in range(size)])]
    ppermute x20, starting transfers between devices: 23.2 us -> 24.8 us  [swap(): return lax.ppermute(array, axis, [(i, i ^ bit) for i in range(size)])]
  transfers between devices with their start and end apart: 20 -> 20, of which waited for: 12 -> 8; matrix products, arithmetic and copies ran while one was open for 0% -> 0% of each run, Pallas kernels for 15% -> 14%
where the time goes in v14:
time: 41 us; the launch traced here: 40.9 us
  starting transfers between devices  24.8 us (60%)
  waiting for transfers between devices  8.27 us (20%)
  Pallas kernels  6.99 us (17%)
  between operations  0.79 us (2%)
    ppermute x20, starting transfers between devices, swap(): return lax.ppermute(array, axis, [(i, i ^ bit) for i in range(size)])  24.8 us
    ppermute x20, waiting for transfers between devices, swap(): return lax.ppermute(array, axis, [(i, i ^ bit) for i in range(size)])  8.27 us
    pallas_call x11, Pallas kernels, call(): pl.pallas_call(body, out_shape=outs, in_specs=specs or [VMEM] * len(args)...  6.99 us
  transfers between devices with their start and end apart: 20, of which 8 were waited for; matrix products, arithmetic and copies ran while one was open for 0% of the time, Pallas kernels for 14%

profile of v14, /device:TPU:0, one launch (start us, length us, event | category | flops | bytes accessed | tf_op | source)
XLA Modules:
  0.0 40.9 jit_solution(8149292864750355477)
XLA Ops:
  0.6 3.0 %collective-permute-start.3 = (bf16[128,512]{1,0:T(8,128)(2,1)}, bf16[128,512]{1,0:T(8,128)(2,1)S(1)}, u32[]{:S(2)}, u32[]{:S(2)}) collective-permute-start(bf16[128,512]{1,0:T(8,128)(2,1)} %refs_0_.1), channel_id=1, source_target_pairs={{0,2},{1,3},{2,0},{3,1},{4,6},{5,7},{6,4},{7,5},{8,10},{9,11},{10,... | collective-permute-start | bytes 393224 | tf_op jit(solution)/shard_map/ppermute | solution.py:80
  3.6 0.0 collective-permute-start.4
  3.6 1.0 %shard_map.93 = (bf16[3,128,128]{2,1,0:T(8,128)(2,1)S(1)}, bf16[3,128,128]{2,1,0:T(8,128)(2,1)S(1)}, bf16[3,128,128]{2,1,0:T(8,128)(2,1)S(1)}) custom-call(bf16[128,512]{1,0:T(8,128)(2,1)} %refs_3_.1, bf16[128,512]{1,0:T(8,128)(2,1)} %refs_4_.4, bf16[128,512]{1,0:T(8,128)(2,1)} %refs_5_.2), custom_call_target="tpu_custom_call" | custom-call | bytes 688128 | tf_op jit(solution)/shard_map/pallas_call | solution.py:29
  4.6 2.6 %collective-permute-start = (bf16[3,128,128]{2,1,0:T(8,128)(2,1)S(1)}, bf16[3,128,128]{2,1,0:T(8,128)(2,1)S(1)}, u32[]{:S(2)}, u32[]{:S(2)}) collective-permute-start(bf16[3,128,128]{2,1,0:T(8,128)(2,1)S(1)} %get-tuple-element.40), channel_id=1, source_target_pairs={{0,12},{4,8},{8,4},{12,0},{16,28},{20,24},{24,20},{28,16},{1,13},{... | collective-permute-start | bytes 294920 | tf_op jit(solution)/shard_map/ppermute | solution.py:80
  7.2 0.4 %collective-permute-start.1 = (bf16[3,128,128]{2,1,0:T(8,128)(2,1)S(1)}, bf16[3,128,128]{2,1,0:T(8,128)(2,1)S(1)}, u32[]{:S(2)}, u32[]{:S(2)}) collective-permute-start(bf16[3,128,128]{2,1,0:T(8,128)(2,1)S(1)} %get-tuple-element.41), channel_id=1, source_target_pairs={{0,8},{4,12},{8,0},{12,4},{16,24},{20,28},{24,16},{28,20},{1,9},{5... | collective-permute-start | bytes 294920 | tf_op jit(solution)/shard_map/ppermute | solution.py:80
  7.7 0.5 %collective-permute-start.2 = (bf16[3,128,128]{2,1,0:T(8,128)(2,1)S(1)}, bf16[3,128,128]{2,1,0:T(8,128)(2,1)S(1)}, u32[]{:S(2)}, u32[]{:S(2)}) collective-permute-start(bf16[3,128,128]{2,1,0:T(8,128)(2,1)S(1)} %get-tuple-element.42), channel_id=1, source_target_pairs={{0,4},{4,0},{8,12},{12,8},{16,20},{20,16},{24,28},{28,24},{1,5},{5... | collective-permute-start | bytes 294920 | tf_op jit(solution)/shard_map/ppermute | solution.py:80
  8.2 0.0 collective-permute-start.5
  8.2 0.0 collective-permute-done.4._.refs_2_
  8.2 0.0 copy-start.1
  8.2 0.0 copy-start.2
  8.2 0.0 copy-start.3
  8.2 0.0 copy-start.4
  8.2 1.3 %collective-permute-done.5.refs_3_ = bf16[128,512]{1,0:T(8,128)(2,1)S(1)} collective-permute-done((bf16[128,512]{1,0:T(8,128)(2,1)S(1)}, bf16[128,512]{1,0:T(8,128)(2,1)S(1)}, u32[]{:S(2)}, u32[]{:S(2)}) %collective-permute-start.5) | collective-permute-done | bytes 131104 | tf_op jit(solution)/shard_map/ppermute | solution.py:80
  9.5 0.9 %shard_map.95 = (bf16[128,128]{1,0:T(8,128)(2,1)S(1)}, bf16[128,128]{1,0:T(8,128)(2,1)S(1)}, bf16[128,128]{1,0:T(8,128)(2,1)S(1)}, bf16[128,128]{1,0:T(8,128)(2,1)S(1)}) custom-call(bf16[128,512]{1,0:T(8,128)(2,1)S(1)} %copy-done.5, bf16[128,512]{1,0:T(8,128)(2,1)S(1)} %collective-permute-done.3.refs_1_, ...), custom_call_target="tpu_custom_call" | custom-call | flops 268435456 | bytes 2756608 | tf_op jit(solution)/shard_map/pallas_call | solution.py:29
  10.4 2.6 %collective-permute-start.6 = (bf16[128,128]{1,0:T(8,128)(2,1)S(1)}, bf16[128,128]{1,0:T(8,128)(2,1)S(1)}, u32[]{:S(2)}, u32[]{:S(2)}) collective-permute-start(bf16[128,128]{1,0:T(8,128)(2,1)S(1)} %get-tuple-element.46), channel_id=1, source_target_pairs={{0,12},{4,8},{8,4},{12,0},{16,28},{20,24},{24,20},{28,16},{1,13},{... | collective-permute-start | bytes 98312 | tf_op jit(solution)/shard_map/ppermute | solution.py:80
  13.0 0.4 %collective-permute-start.7 = (bf16[128,128]{1,0:T(8,128)(2,1)S(1)}, bf16[128,128]{1,0:T(8,128)(2,1)S(1)}, u32[]{:S(2)}, u32[]{:S(2)}) collective-permute-start(bf16[128,128]{1,0:T(8,128)(2,1)S(1)} %get-tuple-element.47), channel_id=1, source_target_pairs={{0,8},{4,12},{8,0},{12,4},{16,24},{20,28},{24,16},{28,20},{1,9},{5... | collective-permute-start | bytes 98312 | tf_op jit(solution)/shard_map/ppermute | solution.py:80
  13.4 0.5 %collective-permute-start.8 = (bf16[128,128]{1,0:T(8,128)(2,1)S(1)}, bf16[128,128]{1,0:T(8,128)(2,1)S(1)}, u32[]{:S(2)}, u32[]{:S(2)}) collective-permute-start(bf16[128,128]{1,0:T(8,128)(2,1)S(1)} %get-tuple-element.48), channel_id=1, source_target_pairs={{0,4},{4,0},{8,12},{12,8},{16,20},{20,16},{24,28},{28,24},{1,5},{5... | collective-permute-start | bytes 98312 | tf_op jit(solution)/shard_map/ppermute | solution.py:80
  14.0 0.0 collective-permute-done.1.refs_1_
  14.0 0.0 collective-permute-done.2.refs_2_
  14.0 0.5 %shard_map.96 = (bf16[3,512,128]{2,1,0:T(8,128)(2,1)S(1)}, bf16[512,256]{1,0:T(8,128)(2,1)S(1)}, bf16[128,256]{1,0:T(8,128)(2,1)S(1)}) custom-call(bf16[3,128,128]{2,1,0:T(8,128)(2,1)S(1)} %collective-permute-done.refs_0_, bf16[3,128,128]{2,1,0:T(8,128)(2,1)S(1)} %collective-permute-done.1.refs_1_, bf16[3,128,128]{2,1,0:T(8,128)(2,1)S(1)} %collective-permute-done.2.refs_2_, ...), custom_call_target="tpu_custom_call" | custom-call | flops 67108864 | bytes 1703936 | tf_op jit(solution)/shard_map/pallas_call | solution.py:29
  14.5 2.7 %collective-permute-start.9 = (bf16[128,256]{1,0:T(8,128)(2,1)S(1)}, bf16[128,256]{1,0:T(8,128)(2,1)S(1)}, u32[]{:S(2)}, u32[]{:S(2)}) collective-permute-start(bf16[128,256]{1,0:T(8,128)(2,1)S(1)} %get-tuple-element.53), channel_id=1, source_target_pairs={{0,16},{4,20},{8,24},{12,28},{16,0},{20,4},{24,8},{28,12},{1,17},{... | collective-permute-start | bytes 196616 | tf_op jit(solution)/shard_map/ppermute | solution.py:80
  17.1 0.0 collective-permute-done.6.refs_0_
  17.1 0.0 collective-permute-done.7.refs_1_
  17.1 0.2 collective-permute-done.8.refs_2_
  17.4 0.5 %shard_map.97 = (bf16[512,128]{1,0:T(8,128)(2,1)S(1)}, bf16[512,256]{1,0:T(8,128)(2,1)S(1)}, bf16[512,512]{1,0:T(8,128)(2,1)S(1)}, f32[512,128]{1,0:T(8,128)S(1)}) custom-call(bf16[128,128]{1,0:T(8,128)(2,1)S(1)} %collective-permute-done.6.refs_0_, bf16[128,128]{1,0:T(8,128)(2,1)S(1)} %collective-permute-done.7.refs_1_, ...), custom_call_target="tpu_custom_call" | custom-call | flops 536870912 | bytes 2228224 | tf_op jit(solution)/shard_map/pallas_call | solution.py:29
  17.9 2.1 %collective-permute-done.9.refs_3_ = bf16[128,256]{1,0:T(8,128)(2,1)S(1)} collective-permute-done((bf16[128,256]{1,0:T(8,128)(2,1)S(1)}, bf16[128,256]{1,0:T(8,128)(2,1)S(1)}, u32[]{:S(2)}, u32[]{:S(2)}) %collective-permute-start.9) | collective-permute-done | bytes 65568 | tf_op jit(solution)/shard_map/ppermute | solution.py:80
  20.0 0.6 %shard_map.98 = (bf16[128,256]{1,0:T(8,128)(2,1)S(1)}, bf16[512,128]{1,0:T(8,128)(2,1)S(1)}, bf16[128,256]{1,0:T(8,128)(2,1)S(1)}, bf16[4,128,128]{2,1,0:T(8,128)(2,1)S(1)}) custom-call(bf16[512,128]{1,0:T(8,128)(2,1)S(1)} %get-tuple-element.51.refs_0_, bf16[512,256]{1,0:T(8,128)(2,1)S(1)} %get-tuple-element.49.refs_1_.qf_ref, ...), custom_call_target="tpu_custom_call" | custom-call | flops 67108864 | bytes 1114112 | tf_op jit(solution)/shard_map/pallas_call | solution.py:29
  20.6 0.1 collective-permute-start.14
  20.7 0.5 %collective-permute-start.10 = (bf16[4,128,128]{2,1,0:T(8,128)(2,1)S(1)}, bf16[4,128,128]{2,1,0:T(8,128)(2,1)S(1)}, u32[]{:S(2)}, u32[]{:S(2)}) collective-permute-start(bf16[4,128,128]{2,1,0:T(8,128)(2,1)S(1)} %get-tuple-element.56.mixed_ref), channel_id=1, source_target_pairs={{0,1},{1,0},{2,3},{3,2},{4,5},{5,4},{6,7},{7,6},{8,9},{9,8},{10,11... | collective-permute-start | bytes 393224 | tf_op jit(solution)/shard_map/ppermute | solution.py:80
  21.2 2.4 %collective-permute-start.15 = (bf16[128,256]{1,0:T(8,128)(2,1)S(1)}, bf16[128,256]{1,0:T(8,128)(2,1)S(1)}, u32[]{:S(2)}, u32[]{:S(2)}) collective-permute-start(bf16[128,256]{1,0:T(8,128)(2,1)S(1)} %get-tuple-element.65), channel_id=1, source_target_pairs={{0,16},{4,20},{8,24},{12,28},{16,0},{20,4},{24,8},{28,12},{1,17},{... | collective-permute-start | bytes 196616 | tf_op jit(solution)/shard_map/ppermute | solution.py:80
  23.6 1.5 %collective-permute-done.10.other_ref = bf16[4,128,128]{2,1,0:T(8,128)(2,1)S(1)} collective-permute-done((bf16[4,128,128]{2,1,0:T(8,128)(2,1)S(1)}, bf16[4,128,128]{2,1,0:T(8,128)(2,1)S(1)}, u32[]{:S(2)}, u32[]{:S(2)}) %collective-permute-start.10) | collective-permute-done | bytes 131104 | tf_op jit(solution)/shard_map/ppermute | solution.py:80
  25.0 1.0 %shard_map.99 = (bf16[512,128]{1,0:T(8,128)(2,1)S(1)}, f32[512,128]{1,0:T(8,128)S(1)}, f32[512,256]{1,0:T(8,128)S(1)}, bf16[2,128,128]{2,1,0:T(8,128)(2,1)S(1)},...) custom-call(bf16[3,512,128]{2,1,0:T(8,128)(2,1)S(1)} %get-tuple-element.44.refs, ...), custom_call_target="tpu_custom_call" | custom-call | flops 268435456 | bytes 3342336 | tf_op jit(solution)/shard_map/pallas_call | solution.py:29
  26.0 2.3 %collective-permute-start.11 = (bf16[2,128,128]{2,1,0:T(8,128)(2,1)S(1)}, bf16[2,128,128]{2,1,0:T(8,128)(2,1)S(1)}, u32[]{:S(2)}, u32[]{:S(2)}) collective-permute-start(bf16[2,128,128]{2,1,0:T(8,128)(2,1)S(1)} %get-tuple-element.57), channel_id=1, source_target_pairs={{0,12},{4,8},{8,4},{12,0},{16,28},{20,24},{24,20},{28,16},{1,13},{... | collective-permute-start | bytes 196616 | tf_op jit(solution)/shard_map/ppermute | solution.py:80
  28.3 0.5 %collective-permute-start.12 = (bf16[2,128,128]{2,1,0:T(8,128)(2,1)S(1)}, bf16[2,128,128]{2,1,0:T(8,128)(2,1)S(1)}, u32[]{:S(2)}, u32[]{:S(2)}) collective-permute-start(bf16[2,128,128]{2,1,0:T(8,128)(2,1)S(1)} %get-tuple-element.58), channel_id=1, source_target_pairs={{0,8},{4,12},{8,0},{12,4},{16,24},{20,28},{24,16},{28,20},{1,9},{5... | collective-permute-start | bytes 196616 | tf_op jit(solution)/shard_map/ppermute | solution.py:80
  28.8 0.7 %collective-permute-start.13 = (bf16[2,128,128]{2,1,0:T(8,128)(2,1)S(1)}, bf16[2,128,128]{2,1,0:T(8,128)(2,1)S(1)}, u32[]{:S(2)}, u32[]{:S(2)}) collective-permute-start(bf16[2,128,128]{2,1,0:T(8,128)(2,1)S(1)} %get-tuple-element.59), channel_id=1, source_target_pairs={{0,4},{4,0},{8,12},{12,8},{16,20},{20,16},{24,28},{28,24},{1,5},{5... | collective-permute-start | bytes 196616 | tf_op jit(solution)/shard_map/ppermute | solution.py:80
  29.5 0.6 %shard_map.100 = (bf16[3,128,128]{2,1,0:T(8,128)(2,1)S(1)}, bf16[3,128,128]{2,1,0:T(8,128)(2,1)S(1)}, bf16[3,128,128]{2,1,0:T(8,128)(2,1)S(1)}, bf16[3,128,128]{2,1,0:T(8,128)(2,1)S(1)}) custom-call(bf16[3,512,128]{2,1,0:T(8,128)(2,1)S(1)} %get-tuple-element.44.refs_4_.qkv_ref, bf16[4,128,256]{2,1,0:T(8,128)(2,1)S(1)} %copy-done.1, ...), custom_call_target="tpu_custom_call" | custom-call | flops 100663296 | bytes 2293760 | tf_op jit(solution)/shard_map/pallas_call | solution.py:29
  30.1 2.4 %collective-permute-start.17 = (bf16[3,128,128]{2,1,0:T(8,128)(2,1)S(1)}, bf16[3,128,128]{2,1,0:T(8,128)(2,1)S(1)}, u32[]{:S(2)}, u32[]{:S(2)}) collective-permute-start(bf16[3,128,128]{2,1,0:T(8,128)(2,1)S(1)} %get-tuple-element.69), channel_id=1, source_target_pairs={{0,12},{4,8},{8,4},{12,0},{16,28},{20,24},{24,20},{28,16},{1,13},{... | collective-permute-start | bytes 294920 | tf_op jit(solution)/shard_map/ppermute | solution.py:80
  32.5 0.7 %collective-permute-start.18 = (bf16[3,128,128]{2,1,0:T(8,128)(2,1)S(1)}, bf16[3,128,128]{2,1,0:T(8,128)(2,1)S(1)}, u32[]{:S(2)}, u32[]{:S(2)}) collective-permute-start(bf16[3,128,128]{2,1,0:T(8,128)(2,1)S(1)} %get-tuple-element.70), channel_id=1, source_target_pairs={{0,8},{4,12},{8,0},{12,4},{16,24},{20,28},{24,16},{28,20},{1,9},{5... | collective-permute-start | bytes 294920 | tf_op jit(solution)/shard_map/ppermute | solution.py:80
  33.2 0.0 collective-permute-done.12.refs_1_
  33.2 1.4 %collective-permute-start.19 = (bf16[3,128,128]{2,1,0:T(8,128)(2,1)S(1)}, bf16[3,128,128]{2,1,0:T(8,128)(2,1)S(1)}, u32[]{:S(2)}, u32[]{:S(2)}) collective-permute-start(bf16[3,128,128]{2,1,0:T(8,128)(2,1)S(1)} %get-tuple-element.71), channel_id=1, source_target_pairs={{0,4},{4,0},{8,12},{12,8},{16,20},{20,16},{24,28},{28,24},{1,5},{5... | collective-permute-start | bytes 294920 | tf_op jit(solution)/shard_map/ppermute | solution.py:80
  34.6 0.5 %shard_map.101 = (f32[1,128,512]{2,1,0:T(8,128)S(1)}, bf16[1,128,512]{2,1,0:T(8,128)(2,1)S(1)}) custom-call(bf16[2,128,128]{2,1,0:T(8,128)(2,1)S(1)} %collective-permute-done.11.refs_0_, bf16[2,128,128]{2,1,0:T(8,128)(2,1)S(1)} %collective-permute-done.12.refs_1_, bf16[2,128,128]{2,1,0:T(8,128)(2,1)S(1)} %collective-permute-done.13.refs_2_, ...), custom_call_target="tpu_custom_call" | custom-call | flops 268435456 | bytes 4947968 | tf_op jit(solution)/shard_map/pallas_call | solution.py:29
  35.1 1.0 %collective-permute-start.16 = (bf16[1,128,512]{2,1,0:T(8,128)(2,1)S(1)}, bf16[1,128,512]{2,1,0:T(8,128)(2,1)S(1)}, u32[]{:S(2)}, u32[]{:S(2)}) collective-permute-start(bf16[1,128,512]{2,1,0:T(8,128)(2,1)S(1)} %get-tuple-element.68), channel_id=1, source_target_pairs={{0,2},{1,3},{2,0},{3,1},{4,6},{5,7},{6,4},{7,5},{8,10},{9,11},{10,... | collective-permute-start | bytes 393224 | tf_op jit(solution)/shard_map/ppermute | solution.py:80
  36.1 0.2 collective-permute-done.17.refs_0_
  36.3 1.0 %collective-permute-done.18.refs_1_ = bf16[3,128,128]{2,1,0:T(8,128)(2,1)S(1)} collective-permute-done((bf16[3,128,128]{2,1,0:T(8,128)(2,1)S(1)}, bf16[3,128,128]{2,1,0:T(8,128)(2,1)S(1)}, u32[]{:S(2)}, u32[]{:S(2)}) %collective-permute-start.18) | collective-permute-done | bytes 98336 | tf_op jit(solution)/shard_map/ppermute | solution.py:80
  37.2 0.6 %collective-permute-done.19.refs_2_ = bf16[3,128,128]{2,1,0:T(8,128)(2,1)S(1)} collective-permute-done((bf16[3,128,128]{2,1,0:T(8,128)(2,1)S(1)}, bf16[3,128,128]{2,1,0:T(8,128)(2,1)S(1)}, u32[]{:S(2)}, u32[]{:S(2)}) %collective-permute-start.19) | collective-permute-done | bytes 98336 | tf_op jit(solution)/shard_map/ppermute | solution.py:80
  37.8 0.8 %shard_map.102 = (bf16[128,512]{1,0:T(8,128)(2,1)}, bf16[128,512]{1,0:T(8,128)(2,1)}, bf16[128,512]{1,0:T(8,128)(2,1)}, f32[8,128]{1,0:T(8,128)S(1)}) custom-call(bf16[3,128,128]{2,1,0:T(8,128)(2,1)S(1)} %collective-permute-done.17.refs_0_, bf16[3,128,128]{2,1,0:T(8,128)(2,1)S(1)} %collective-permute-done.18.refs_1_, ...), custom_call_target="tpu_custom_call" | custom-call | flops 800000000 | bytes 790528 | tf_op jit(solution)/shard_map/pallas_call | solution.py:29
  38.7 1.5 %collective-permute-done.16 = bf16[1,128,512]{2,1,0:T(8,128)(2,1)S(1)} collective-permute-done((bf16[1,128,512]{2,1,0:T(8,128)(2,1)S(1)}, bf16[1,128,512]{2,1,0:T(8,128)(2,1)S(1)}, u32[]{:S(2)}, u32[]{:S(2)}) %collective-permute-start.16) | collective-permute-done | bytes 131104 | tf_op jit(solution)/shard_map/ppermute | solution.py:80
  40.2 0.7 %shard_map.103 = bf16[128,512]{1,0:T(8,128)(2,1)} custom-call(f32[128,512]{1,0:T(8,128)S(1)} %bitcast.2, bf16[128,512]{1,0:T(8,128)(2,1)S(1)} %bitcast.3, f32[8,128]{1,0:T(8,128)S(1)} %get-tuple-element.72._), custom_call_target="tpu_custom_call" | custom-call | bytes 528384 | tf_op jit(solution)/shard_map/pallas_call | solution.py:29
  (15 shorter events, 0.0 us)
Async XLA Ops:
  0.6 7.5 %collective-permute-start.3 = (bf16[128,512]{1,0:T(8,128)(2,1)}, bf16[128,512]{1,0:T(8,128)(2,1)S(1)}, u32[]{:S(2)}, u32[]{:S(2)}) collective-permute-start(bf16[128,512]{1,0:T(8,128)(2,1)} %refs_0_.1), channel_id=1, source_target_pairs={{0,2},{1,3},{2,0},{3,1},{4,6},{5,7},{6,4},{7,5},{8,10},{9,11},{10,... | collective-permute-start | bytes 393224 | tf_op jit(solution)/shard_map/ppermute | solution.py:80
  3.6 4.5 %collective-permute-start.4 = (bf16[128,512]{1,0:T(8,128)(2,1)}, bf16[128,512]{1,0:T(8,128)(2,1)S(1)}, u32[]{:S(2)}, u32[]{:S(2)}) collective-permute-start(bf16[128,512]{1,0:T(8,128)(2,1)} %refs_0_.1), channel_id=1, source_target_pairs={{0,1},{1,0},{2,3},{3,2},{4,5},{5,4},{6,7},{7,6},{8,9},{9,8},{10,11... | collective-permute-start | bytes 393224 | tf_op jit(solution)/shard_map/ppermute | solution.py:80
  4.6 8.8 %collective-permute-start = (bf16[3,128,128]{2,1,0:T(8,128)(2,1)S(1)}, bf16[3,128,128]{2,1,0:T(8,128)(2,1)S(1)}, u32[]{:S(2)}, u32[]{:S(2)}) collective-permute-start(bf16[3,128,128]{2,1,0:T(8,128)(2,1)S(1)} %get-tuple-element.40), channel_id=1, source_target_pairs={{0,12},{4,8},{8,4},{12,0},{16,28},{20,24},{24,20},{28,16},{1,13},{... | collective-permute-start | bytes 294920 | tf_op jit(solution)/shard_map/ppermute | solution.py:80
  7.2 6.7 %collective-permute-start.1 = (bf16[3,128,128]{2,1,0:T(8,128)(2,1)S(1)}, bf16[3,128,128]{2,1,0:T(8,128)(2,1)S(1)}, u32[]{:S(2)}, u32[]{:S(2)}) collective-permute-start(bf16[3,128,128]{2,1,0:T(8,128)(2,1)S(1)} %get-tuple-element.41), channel_id=1, source_target_pairs={{0,8},{4,12},{8,0},{12,4},{16,24},{20,28},{24,16},{28,20},{1,9},{5... | collective-permute-start | bytes 294920 | tf_op jit(solution)/shard_map/ppermute | solution.py:80
  7.7 1.9 %copy-start = (bf16[512,2048]{1,0:T(8,128)(2,1)S(1)}, bf16[512,2048]{1,0:T(8,128)(2,1)}, u32[]{:S(2)}) copy-start(bf16[512,2048]{1,0:T(8,128)(2,1)} %refs_4_.5) | copy-start | bytes 6291460
  7.7 1.9 %copy-start.5 = (bf16[128,512]{1,0:T(8,128)(2,1)S(1)}, bf16[128,512]{1,0:T(8,128)(2,1)}, u32[]{:S(2)}) copy-start(bf16[128,512]{1,0:T(8,128)(2,1)} %refs_0_.1) | copy-start | bytes 393220
  7.7 6.3 %collective-permute-start.2 = (bf16[3,128,128]{2,1,0:T(8,128)(2,1)S(1)}, bf16[3,128,128]{2,1,0:T(8,128)(2,1)S(1)}, u32[]{:S(2)}, u32[]{:S(2)}) collective-permute-start(bf16[3,128,128]{2,1,0:T(8,128)(2,1)S(1)} %get-tuple-element.42), channel_id=1, source_target_pairs={{0,4},{4,0},{8,12},{12,8},{16,20},{20,16},{24,28},{28,24},{1,5},{5... | collective-permute-start | bytes 294920 | tf_op jit(solution)/shard_map/ppermute | solution.py:80
  8.2 1.3 %collective-permute-start.5 = (bf16[128,512]{1,0:T(8,128)(2,1)S(1)}, bf16[128,512]{1,0:T(8,128)(2,1)S(1)}, u32[]{:S(2)}, u32[]{:S(2)}) collective-permute-start(bf16[128,512]{1,0:T(8,128)(2,1)S(1)} %collective-permute-done.3.refs_1_), channel_id=1, source_target_pairs={{0,1},{1,0},{2,3},{3,2},{4,5},{5,4},{6,7},{7,6},{8,9},{9,8},{10,11... | collective-permute-start | bytes 393224 | tf_op jit(solution)/shard_map/ppermute | solution.py:80
  8.2 5.8 %copy-start.1 = (bf16[4,128,256]{2,1,0:T(8,128)(2,1)S(1)}, bf16[4,128,256]{2,1,0:T(8,128)(2,1)}, u32[]{:S(2)}) copy-start(bf16[4,128,256]{2,1,0:T(8,128)(2,1)} %om_ref.3) | copy-start | bytes 786436
  8.2 5.8 %copy-start.2 = (bf16[128,512]{1,0:T(8,128)(2,1)S(1)}, bf16[128,512]{1,0:T(8,128)(2,1)}, u32[]{:S(2)}) copy-start(bf16[128,512]{1,0:T(8,128)(2,1)} %refs_3_.1) | copy-start | bytes 393220
  8.2 5.8 %copy-start.3 = (bf16[128,512]{1,0:T(8,128)(2,1)S(1)}, bf16[128,512]{1,0:T(8,128)(2,1)}, u32[]{:S(2)}) copy-start(bf16[128,512]{1,0:T(8,128)(2,1)} %refs_4_.4) | copy-start | bytes 393220
  8.2 5.8 %copy-start.4 = (bf16[128,512]{1,0:T(8,128)(2,1)S(1)}, bf16[128,512]{1,0:T(8,128)(2,1)}, u32[]{:S(2)}) copy-start(bf16[128,512]{1,0:T(8,128)(2,1)} %refs_5_.2) | copy-start | bytes 393220
  10.4 6.7 %collective-permute-start.6 = (bf16[128,128]{1,0:T(8,128)(2,1)S(1)}, bf16[128,128]{1,0:T(8,128)(2,1)S(1)}, u32[]{:S(2)}, u32[]{:S(2)}) collective-permute-start(bf16[128,128]{1,0:T(8,128)(2,1)S(1)} %get-tuple-element.46), channel_id=1, source_target_pairs={{0,12},{4,8},{8,4},{12,0},{16,28},{20,24},{24,20},{28,16},{1,13},{... | collective-permute-start | bytes 98312 | tf_op jit(solution)/shard_map/ppermute | solution.py:80
  13.0 4.1 %collective-permute-start.7 = (bf16[128,128]{1,0:T(8,128)(2,1)S(1)}, bf16[128,128]{1,0:T(8,128)(2,1)S(1)}, u32[]{:S(2)}, u32[]{:S(2)}) collective-permute-start(bf16[128,128]{1,0:T(8,128)(2,1)S(1)} %get-tuple-element.47), channel_id=1, source_target_pairs={{0,8},{4,12},{8,0},{12,4},{16,24},{20,28},{24,16},{28,20},{1,9},{5... | collective-permute-start | bytes 98312 | tf_op jit(solution)/shard_map/ppermute | solution.py:80
  13.4 3.9 %collective-permute-start.8 = (bf16[128,128]{1,0:T(8,128)(2,1)S(1)}, bf16[128,128]{1,0:T(8,128)(2,1)S(1)}, u32[]{:S(2)}, u32[]{:S(2)}) collective-permute-start(bf16[128,128]{1,0:T(8,128)(2,1)S(1)} %get-tuple-element.48), channel_id=1, source_target_pairs={{0,4},{4,0},{8,12},{12,8},{16,20},{20,16},{24,28},{28,24},{1,5},{5... | collective-permute-start | bytes 98312 | tf_op jit(solution)/shard_map/ppermute | solution.py:80
  14.5 5.5 %collective-permute-start.9 = (bf16[128,256]{1,0:T(8,128)(2,1)S(1)}, bf16[128,256]{1,0:T(8,128)(2,1)S(1)}, u32[]{:S(2)}, u32[]{:S(2)}) collective-permute-start(bf16[128,256]{1,0:T(8,128)(2,1)S(1)} %get-tuple-element.53), channel_id=1, source_target_pairs={{0,16},{4,20},{8,24},{12,28},{16,0},{20,4},{24,8},{28,12},{1,17},{... | collective-permute-start | bytes 196616 | tf_op jit(solution)/shard_map/ppermute | solution.py:80
  20.6 14.0 %collective-permute-start.14 = (bf16[512,2048]{1,0:T(8,128)(2,1)S(1)}, bf16[512,2048]{1,0:T(8,128)(2,1)S(1)}, u32[]{:S(2)}, u32[]{:S(2)}) collective-permute-start(bf16[512,2048]{1,0:T(8,128)(2,1)S(1)} %copy-done), channel_id=1, source_target_pairs={{0,1},{1,0},{2,3},{3,2},{4,5},{5,4},{6,7},{7,6},{8,9},{9,8},{10,11... | collective-permute-start | bytes 6291464 | tf_op jit(solution)/shard_map/ppermute | solution.py:80
  20.7 4.3 %collective-permute-start.10 = (bf16[4,128,128]{2,1,0:T(8,128)(2,1)S(1)}, bf16[4,128,128]{2,1,0:T(8,128)(2,1)S(1)}, u32[]{:S(2)}, u32[]{:S(2)}) collective-permute-start(bf16[4,128,128]{2,1,0:T(8,128)(2,1)S(1)} %get-tuple-element.56.mixed_ref), channel_id=1, source_target_pairs={{0,1},{1,0},{2,3},{3,2},{4,5},{5,4},{6,7},{7,6},{8,9},{9,8},{10,11... | collective-permute-start | bytes 393224 | tf_op jit(solution)/shard_map/ppermute | solution.py:80
  21.2 8.4 %collective-permute-start.15 = (bf16[128,256]{1,0:T(8,128)(2,1)S(1)}, bf16[128,256]{1,0:T(8,128)(2,1)S(1)}, u32[]{:S(2)}, u32[]{:S(2)}) collective-permute-start(bf16[128,256]{1,0:T(8,128)(2,1)S(1)} %get-tuple-element.65), channel_id=1, source_target_pairs={{0,16},{4,20},{8,24},{12,28},{16,0},{20,4},{24,8},{28,12},{1,17},{... | collective-permute-start | bytes 196616 | tf_op jit(solution)/shard_map/ppermute | solution.py:80
  26.0 6.5 %collective-permute-start.11 = (bf16[2,128,128]{2,1,0:T(8,128)(2,1)S(1)}, bf16[2,128,128]{2,1,0:T(8,128)(2,1)S(1)}, u32[]{:S(2)}, u32[]{:S(2)}) collective-permute-start(bf16[2,128,128]{2,1,0:T(8,128)(2,1)S(1)} %get-tuple-element.57), channel_id=1, source_target_pairs={{0,12},{4,8},{8,4},{12,0},{16,28},{20,24},{24,20},{28,16},{1,13},{... | collective-permute-start | bytes 196616 | tf_op jit(solution)/shard_map/ppermute | solution.py:80
  28.3 4.9 %collective-permute-start.12 = (bf16[2,128,128]{2,1,0:T(8,128)(2,1)S(1)}, bf16[2,128,128]{2,1,0:T(8,128)(2,1)S(1)}, u32[]{:S(2)}, u32[]{:S(2)}) collective-permute-start(bf16[2,128,128]{2,1,0:T(8,128)(2,1)S(1)} %get-tuple-element.58), channel_id=1, source_target_pairs={{0,8},{4,12},{8,0},{12,4},{16,24},{20,28},{24,16},{28,20},{1,9},{5... | collective-permute-start | bytes 196616 | tf_op jit(solution)/shard_map/ppermute | solution.py:80
  28.8 5.8 %collective-permute-start.13 = (bf16[2,128,128]{2,1,0:T(8,128)(2,1)S(1)}, bf16[2,128,128]{2,1,0:T(8,128)(2,1)S(1)}, u32[]{:S(2)}, u32[]{:S(2)}) collective-permute-start(bf16[2,128,128]{2,1,0:T(8,128)(2,1)S(1)} %get-tuple-element.59), channel_id=1, source_target_pairs={{0,4},{4,0},{8,12},{12,8},{16,20},{20,16},{24,28},{28,24},{1,5},{5... | collective-permute-start | bytes 196616 | tf_op jit(solution)/shard_map/ppermute | solution.py:80
  30.1 6.2 %collective-permute-start.17 = (bf16[3,128,128]{2,1,0:T(8,128)(2,1)S(1)}, bf16[3,128,128]{2,1,0:T(8,128)(2,1)S(1)}, u32[]{:S(2)}, u32[]{:S(2)}) collective-permute-start(bf16[3,128,128]{2,1,0:T(8,128)(2,1)S(1)} %get-tuple-element.69), channel_id=1, source_target_pairs={{0,12},{4,8},{8,4},{12,0},{16,28},{20,24},{24,20},{28,16},{1,13},{... | collective-permute-start | bytes 294920 | tf_op jit(solution)/shard_map/ppermute | solution.py:80
  32.5 4.8 %collective-permute-start.18 = (bf16[3,128,128]{2,1,0:T(8,128)(2,1)S(1)}, bf16[3,128,128]{2,1,0:T(8,128)(2,1)S(1)}, u32[]{:S(2)}, u32[]{:S(2)}) collective-permute-start(bf16[3,128,128]{2,1,0:T(8,128)(2,1)S(1)} %get-tuple-element.70), channel_id=1, source_target_pairs={{0,8},{4,12},{8,0},{12,4},{16,24},{20,28},{24,16},{28,20},{1,9},{5... | collective-permute-start | bytes 294920 | tf_op jit(solution)/shard_map/ppermute | solution.py:80
  33.2 4.6 %collective-permute-start.19 = (bf16[3,128,128]{2,1,0:T(8,128)(2,1)S(1)}, bf16[3,128,128]{2,1,0:T(8,128)(2,1)S(1)}, u32[]{:S(2)}, u32[]{:S(2)}) collective-permute-start(bf16[3,128,128]{2,1,0:T(8,128)(2,1)S(1)} %get-tuple-element.71), channel_id=1, source_target_pairs={{0,4},{4,0},{8,12},{12,8},{16,20},{20,16},{24,28},{28,24},{1,5},{5... | collective-permute-start | bytes 294920 | tf_op jit(solution)/shard_map/ppermute | solution.py:80
  35.1 5.0 %collective-permute-start.16 = (bf16[1,128,512]{2,1,0:T(8,128)(2,1)S(1)}, bf16[1,128,512]{2,1,0:T(8,128)(2,1)S(1)}, u32[]{:S(2)}, u32[]{:S(2)}) collective-permute-start(bf16[1,128,512]{2,1,0:T(8,128)(2,1)S(1)} %get-tuple-element.68), channel_id=1, source_target_pairs={{0,2},{1,3},{2,0},{3,1},{4,6},{5,7},{6,4},{7,5},{8,10},{9,11},{10,... | collective-permute-start | bytes 393224 | tf_op jit(solution)/shard_map/ppermute | solution.py:80

commit v15 on v13

--- a/solution.py
+++ b/solution.py
@@ -179,8 +179,9 @@
 
 
 def inner_kernel(n, *refs):
-    gm_in, (qkv_ref, om_ref, kf_ref) = refs[:n][::-1], refs[n : n + 3]
-    gm_ref, qf_ref, scores_ref, num_ref = refs[n + 3 :]
+    own, (qkv_ref, om_ref, kf_ref) = refs[: n - 1][::-1], refs[n - 1 : n + 2]
+    gm_in = own[:1] + own
+    gm_ref, qf_ref, scores_ref, num_ref = refs[n + 2 :]
     long, dim = num_ref.shape
     rows = long // n
     r = member(n)
@@ -198,7 +199,7 @@
 
 
 def turn_kernel(n, *refs):
-    gm_ref, qf_ref, num_ref, *earlier = refs[: -n - 4]
+    gm_ref, late_ref, qf_ref, num_ref, *earlier = refs[: -n - 4]
     carried_ref, gn_ref, total_ref = refs[-n - 4 : -n - 1]
     outs, scr = refs[-n - 1 : -1], refs[-1]
     r = member(n)
@@ -206,12 +207,14 @@
     places = [
         pl.ds(pl.multiple_of((r ^ k) * rows, 128), rows) for k in range(n)
     ]
+    scr[...] = gm_ref[...]
+    scr[places[1], :] = late_ref[...]
     carried = sum_of_side(earlier, n, True)
     carried_ref[...] = carried
     num = num_ref[...] + mm(qf_ref[...], carried, NT)
     inv = lax.rsqrt(jnp.mean(num * num, axis=1, keepdims=True) + EPSILON)
     normed = num * inv
-    gm = gm_ref[...].astype(jnp.float32)
+    gm = scr[...].astype(jnp.float32)
     gn = bf((gm - normed * jnp.mean(gm * normed, axis=1, keepdims=True)) * inv)
     gn_ref[...] = gn
     scr[...] = bf(normed)
@@ -340,7 +343,7 @@
     gm, qf, scores, num = call(
         functools.partial(inner_kernel, n),
         [struct((long, dim)), struct((long, feats)), struct((long, long)), struct((long, dim), f32)],
-        *gm_in, qkv, feature_proj, kf, flops=16 * macs,
+        *gm_in[:-2], gm_in[-1], qkv, feature_proj, kf, flops=16 * macs,
     )
     carried, gn, later_total, *mixed_parts = call(
         functools.partial(turn_kernel, n),
@@ -350,7 +353,7 @@
             struct((dim, feats)),
         ]
         + [struct((rows, dim))] * n,
-        gm, qf, num, *earlier, flops=2 * macs,
+        gm, gm_in[-2], qf, num, *earlier, flops=2 * macs,
         scratch=[pltpu.VMEM((long, dim), jnp.bfloat16)],
     )
     after = swap_totals(later_total, n)

time: 40.7 us -> 40 us (0.983)
  starting transfers between devices: 23.4 us -> 22.4 us
    ppermute x19, starting transfers between devices: 23.4 us -> 22.4 us  [swap(): return lax.ppermute(array, axis, [(i, i ^ bit) for i in range(size)])]
  transfers between devices with their start and end apart: 19 -> 19, of which waited for: 8 -> 7; matrix products, arithmetic and copies ran while one was open for 0% -> 0% of each run, Pallas kernels for 11% -> 11%
where the time goes in v15:
time: 40 us; the launch traced here: 39.9 us
  starting transfers between devices  22.4 us (56%)
  waiting for transfers between devices  10.1 us (25%)
  Pallas kernels  6.37 us (16%)
  between operations  0.82 us (2%)
    ppermute x19, starting transfers between devices, swap(): return lax.ppermute(array, axis, [(i, i ^ bit) for i in range(size)])  22.4 us
    ppermute x19, waiting for transfers between devices, swap(): return lax.ppermute(array, axis, [(i, i ^ bit) for i in range(size)])  10.1 us
    pallas_call x10, Pallas kernels, call(): pl.pallas_call(body, out_shape=outs, in_specs=specs or [VMEM] * len(args)...  6.37 us
  transfers between devices with their start and end apart: 19, of which 7 were waited for; matrix products, arithmetic and copies ran while one was open for 0% of the time, Pallas kernels for 11%

profile of v15, /device:TPU:0, one launch (start us, length us, event | category | flops | bytes accessed | tf_op | source)
XLA Modules:
  0.0 39.9 jit_solution(3282844350588578856)
XLA Ops:
  0.6 3.0 %collective-permute-start.3 = (bf16[128,512]{1,0:T(8,128)(2,1)}, bf16[128,512]{1,0:T(8,128)(2,1)S(1)}, u32[]{:S(2)}, u32[]{:S(2)}) collective-permute-start(bf16[128,512]{1,0:T(8,128)(2,1)} %refs_0_.1), channel_id=1, source_target_pairs={{0,2},{1,3},{2,0},{3,1},{4,6},{5,7},{6,4},{7,5},{8,10},{9,11},{10,... | collective-permute-start | bytes 393224 | tf_op jit(solution)/shard_map/ppermute | solution.py:80
  3.6 0.0 collective-permute-start.4
  3.6 1.0 %shard_map.93 = (bf16[3,128,128]{2,1,0:T(8,128)(2,1)S(1)}, bf16[3,128,128]{2,1,0:T(8,128)(2,1)S(1)}, bf16[3,128,128]{2,1,0:T(8,128)(2,1)S(1)}) custom-call(bf16[128,512]{1,0:T(8,128)(2,1)} %refs_3_.1, bf16[128,512]{1,0:T(8,128)(2,1)} %refs_4_.5, bf16[128,512]{1,0:T(8,128)(2,1)} %refs_5_.1), custom_call_target="tpu_custom_call" | custom-call | bytes 688128 | tf_op jit(solution)/shard_map/pallas_call | solution.py:29
  4.6 2.6 %collective-permute-start = (bf16[3,128,128]{2,1,0:T(8,128)(2,1)S(1)}, bf16[3,128,128]{2,1,0:T(8,128)(2,1)S(1)}, u32[]{:S(2)}, u32[]{:S(2)}) collective-permute-start(bf16[3,128,128]{2,1,0:T(8,128)(2,1)S(1)} %get-tuple-element.34), channel_id=1, source_target_pairs={{0,12},{4,8},{8,4},{12,0},{16,28},{20,24},{24,20},{28,16},{1,13},{... | collective-permute-start | bytes 294920 | tf_op jit(solution)/shard_map/ppermute | solution.py:80
  7.2 0.4 %collective-permute-start.1 = (bf16[3,128,128]{2,1,0:T(8,128)(2,1)S(1)}, bf16[3,128,128]{2,1,0:T(8,128)(2,1)S(1)}, u32[]{:S(2)}, u32[]{:S(2)}) collective-permute-start(bf16[3,128,128]{2,1,0:T(8,128)(2,1)S(1)} %get-tuple-element.35), channel_id=1, source_target_pairs={{0,8},{4,12},{8,0},{12,4},{16,24},{20,28},{24,16},{28,20},{1,9},{5... | collective-permute-start | bytes 294920 | tf_op jit(solution)/shard_map/ppermute | solution.py:80
  7.7 0.5 %collective-permute-start.2 = (bf16[3,128,128]{2,1,0:T(8,128)(2,1)S(1)}, bf16[3,128,128]{2,1,0:T(8,128)(2,1)S(1)}, u32[]{:S(2)}, u32[]{:S(2)}) collective-permute-start(bf16[3,128,128]{2,1,0:T(8,128)(2,1)S(1)} %get-tuple-element.36), channel_id=1, source_target_pairs={{0,4},{4,0},{8,12},{12,8},{16,20},{20,16},{24,28},{28,24},{1,5},{5... | collective-permute-start | bytes 294920 | tf_op jit(solution)/shard_map/ppermute | solution.py:80
  8.2 0.0 collective-permute-done.3.refs_1_
  8.2 0.0 collective-permute-start.5
  8.2 0.0 collective-permute-done.4._.refs_2_
  8.2 0.0 copy-start.1
  8.2 0.0 copy-start.2
  8.2 0.0 copy-start.3
  8.2 0.0 copy-start.4
  8.2 1.3 %collective-permute-done.5.refs_3_ = bf16[128,512]{1,0:T(8,128)(2,1)S(1)} collective-permute-done((bf16[128,512]{1,0:T(8,128)(2,1)S(1)}, bf16[128,512]{1,0:T(8,128)(2,1)S(1)}, u32[]{:S(2)}, u32[]{:S(2)}) %collective-permute-start.5) | collective-permute-done | bytes 131104 | tf_op jit(solution)/shard_map/ppermute | solution.py:80
  9.5 0.9 %shard_map.95 = (bf16[128,128]{1,0:T(8,128)(2,1)S(1)}, bf16[128,128]{1,0:T(8,128)(2,1)S(1)}, bf16[128,128]{1,0:T(8,128)(2,1)S(1)}, bf16[128,128]{1,0:T(8,128)(2,1)S(1)}) custom-call(bf16[128,512]{1,0:T(8,128)(2,1)S(1)} %copy-done.5, bf16[128,512]{1,0:T(8,128)(2,1)S(1)} %collective-permute-done.3.refs_1_, ...), custom_call_target="tpu_custom_call" | custom-call | flops 268435456 | bytes 2756608 | tf_op jit(solution)/shard_map/pallas_call | solution.py:29
  10.4 2.6 %collective-permute-start.6 = (bf16[128,128]{1,0:T(8,128)(2,1)S(1)}, bf16[128,128]{1,0:T(8,128)(2,1)S(1)}, u32[]{:S(2)}, u32[]{:S(2)}) collective-permute-start(bf16[128,128]{1,0:T(8,128)(2,1)S(1)} %get-tuple-element.40), channel_id=1, source_target_pairs={{0,12},{4,8},{8,4},{12,0},{16,28},{20,24},{24,20},{28,16},{1,13},{... | collective-permute-start | bytes 98312 | tf_op jit(solution)/shard_map/ppermute | solution.py:80
  13.0 0.4 %collective-permute-start.7 = (bf16[128,128]{1,0:T(8,128)(2,1)S(1)}, bf16[128,128]{1,0:T(8,128)(2,1)S(1)}, u32[]{:S(2)}, u32[]{:S(2)}) collective-permute-start(bf16[128,128]{1,0:T(8,128)(2,1)S(1)} %get-tuple-element.41), channel_id=1, source_target_pairs={{0,8},{4,12},{8,0},{12,4},{16,24},{20,28},{24,16},{28,20},{1,9},{5... | collective-permute-start | bytes 98312 | tf_op jit(solution)/shard_map/ppermute | solution.py:80
  13.4 0.0 collective-permute-done.refs_0_
  13.4 0.0 collective-permute-done.1.refs_1_
  13.5 0.0 collective-permute-done.2.refs_2_
  13.5 0.5 %shard_map.96 = (bf16[3,512,128]{2,1,0:T(8,128)(2,1)S(1)}, bf16[512,256]{1,0:T(8,128)(2,1)S(1)}, bf16[128,256]{1,0:T(8,128)(2,1)S(1)}) custom-call(bf16[3,128,128]{2,1,0:T(8,128)(2,1)S(1)} %collective-permute-done.refs_0_, bf16[3,128,128]{2,1,0:T(8,128)(2,1)S(1)} %collective-permute-done.1.refs_1_, bf16[3,128,128]{2,1,0:T(8,128)(2,1)S(1)} %collective-permute-done.2.refs_2_, ...), custom_call_target="tpu_custom_call" | custom-call | flops 67108864 | bytes 1703936 | tf_op jit(solution)/shard_map/pallas_call | solution.py:29
  14.0 2.7 %collective-permute-start.9 = (bf16[128,256]{1,0:T(8,128)(2,1)S(1)}, bf16[128,256]{1,0:T(8,128)(2,1)S(1)}, u32[]{:S(2)}, u32[]{:S(2)}) collective-permute-start(bf16[128,256]{1,0:T(8,128)(2,1)S(1)} %get-tuple-element.47), channel_id=1, source_target_pairs={{0,16},{4,20},{8,24},{12,28},{16,0},{20,4},{24,8},{28,12},{1,17},{... | collective-permute-start | bytes 196616 | tf_op jit(solution)/shard_map/ppermute | solution.py:80
  16.6 0.9 %collective-permute-start.8 = (bf16[128,128]{1,0:T(8,128)(2,1)S(1)}, bf16[128,128]{1,0:T(8,128)(2,1)S(1)}, u32[]{:S(2)}, u32[]{:S(2)}) collective-permute-start(bf16[128,128]{1,0:T(8,128)(2,1)S(1)} %get-tuple-element.45), channel_id=1, source_target_pairs={{0,4},{4,0},{8,12},{12,8},{16,20},{20,16},{24,28},{28,24},{1,5},{5... | collective-permute-start | bytes 98312 | tf_op jit(solution)/shard_map/ppermute | solution.py:80
  17.6 0.5 %shard_map.97 = (bf16[512,128]{1,0:T(8,128)(2,1)S(1)}, bf16[512,256]{1,0:T(8,128)(2,1)S(1)}, bf16[512,512]{1,0:T(8,128)(2,1)S(1)}, f32[512,128]{1,0:T(8,128)S(1)}) custom-call(bf16[128,128]{1,0:T(8,128)(2,1)S(1)} %collective-permute-done.6.refs_0_, bf16[128,128]{1,0:T(8,128)(2,1)S(1)} %collective-permute-done.7.refs_1_, ...), custom_call_target="tpu_custom_call" | custom-call | flops 536870912 | bytes 2195456 | tf_op jit(solution)/shard_map/pallas_call | solution.py:29
  18.1 2.4 %collective-permute-done.8.refs_1_ = bf16[128,128]{1,0:T(8,128)(2,1)S(1)} collective-permute-done((bf16[128,128]{1,0:T(8,128)(2,1)S(1)}, bf16[128,128]{1,0:T(8,128)(2,1)S(1)}, u32[]{:S(2)}, u32[]{:S(2)}) %collective-permute-start.8) | collective-permute-done | bytes 32800 | tf_op jit(solution)/shard_map/ppermute | solution.py:80
  20.6 0.0 collective-permute-done.9.refs_4_
  20.6 0.6 %shard_map.98 = (bf16[128,256]{1,0:T(8,128)(2,1)S(1)}, bf16[512,128]{1,0:T(8,128)(2,1)S(1)}, bf16[128,256]{1,0:T(8,128)(2,1)S(1)}, bf16[128,128]{1,0:T(8,128)(2,...) custom-call(bf16[512,128]{1,0:T(8,128)(2,1)S(1)} %get-tuple-element.44.refs_0_, ...), custom_call_target="tpu_custom_call" | custom-call | flops 67108864 | bytes 1146880 | tf_op jit(solution)/shard_map/pallas_call | solution.py:29
  21.2 1.4 %collective-permute-start.10 = (bf16[128,256]{1,0:T(8,128)(2,1)S(1)}, bf16[128,256]{1,0:T(8,128)(2,1)S(1)}, u32[]{:S(2)}, u32[]{:S(2)}) collective-permute-start(bf16[128,256]{1,0:T(8,128)(2,1)S(1)} %get-tuple-element.53), channel_id=1, source_target_pairs={{0,16},{4,20},{8,24},{12,28},{16,0},{20,4},{24,8},{28,12},{1,17},{... | collective-permute-start | bytes 196616 | tf_op jit(solution)/shard_map/ppermute | solution.py:80
  22.6 2.9 %collective-permute-start.14 = (bf16[128,128]{1,0:T(8,128)(2,1)S(1)}, bf16[128,128]{1,0:T(8,128)(2,1)S(1)}, u32[]{:S(2)}, u32[]{:S(2)}) collective-permute-start(bf16[128,128]{1,0:T(8,128)(2,1)S(1)} %get-tuple-element.58), channel_id=1, source_target_pairs={{0,12},{4,8},{8,4},{12,0},{16,28},{20,24},{24,20},{28,16},{1,13},{... | collective-permute-start | bytes 98312 | tf_op jit(solution)/shard_map/ppermute | solution.py:80
  25.5 0.7 %collective-permute-start.16 = (bf16[128,128]{1,0:T(8,128)(2,1)S(1)}, bf16[128,128]{1,0:T(8,128)(2,1)S(1)}, u32[]{:S(2)}, u32[]{:S(2)}) collective-permute-start(bf16[128,128]{1,0:T(8,128)(2,1)S(1)} %get-tuple-element.60), channel_id=1, source_target_pairs={{0,4},{4,0},{8,12},{12,8},{16,20},{20,16},{24,28},{28,24},{1,5},{5... | collective-permute-start | bytes 98312 | tf_op jit(solution)/shard_map/ppermute | solution.py:80
  26.2 1.0 %shard_map.99 = (bf16[512,128]{1,0:T(8,128)(2,1)S(1)}, f32[512,128]{1,0:T(8,128)S(1)}, f32[512,256]{1,0:T(8,128)S(1)}) custom-call(bf16[3,512,128]{2,1,0:T(8,128)(2,1)S(1)} %get-tuple-element.38.refs_3_.qkv_ref, bf16[4,128,256]{2,1,0:T(8,128)(2,1)S(1)} %copy-done.1, bf16[512,256]{1,0:T(8,128)(2,1)S(1)} %get-tuple-element.39.refs_5_.kf_ref, ...), custom_call_target="tpu_custom_call" | custom-call | flops 268435456 | bytes 2818048 | tf_op jit(solution)/shard_map/pallas_call | solution.py:29
  27.1 0.0 collective-permute-done.10.rest_0_
  27.1 0.6 %shard_map.100 = (bf16[3,128,128]{2,1,0:T(8,128)(2,1)S(1)}, bf16[3,128,128]{2,1,0:T(8,128)(2,1)S(1)}, bf16[3,128,128]{2,1,0:T(8,128)(2,1)S(1)}, bf16[3,128,128]{2,1,0:T(8,128)(2,1)S(1)}) custom-call(bf16[3,512,128]{2,1,0:T(8,128)(2,1)S(1)} %get-tuple-element.38.refs_3_.qkv_ref, bf16[4,128,256]{2,1,0:T(8,128)(2,1)S(1)} %copy-done.1, ...), custom_call_target="tpu_custom_call" | custom-call | flops 100663296 | bytes 2293760 | tf_op jit(solution)/shard_map/pallas_call | solution.py:29
  27.7 0.0 collective-permute-done.14.refs_0_
  27.8 1.6 %collective-permute-done.15.refs_1_ = bf16[128,128]{1,0:T(8,128)(2,1)S(1)} collective-permute-done((bf16[128,128]{1,0:T(8,128)(2,1)S(1)}, bf16[128,128]{1,0:T(8,128)(2,1)S(1)}, u32[]{:S(2)}, u32[]{:S(2)}) %collective-permute-start.15) | collective-permute-done | bytes 32800 | tf_op jit(solution)/shard_map/ppermute | solution.py:80
  29.4 0.0 collective-permute-done.16.refs_2_
  29.4 0.4 %shard_map.101 = (bf16[2,128,512]{2,1,0:T(8,128)(2,1)S(1)}, bf16[2,128,512]{2,1,0:T(8,128)(2,1)S(1)}) custom-call(bf16[128,128]{1,0:T(8,128)(2,1)S(1)} %collective-permute-done.14.refs_0_, bf16[128,128]{1,0:T(8,128)(2,1)S(1)} %collective-permute-done.15.refs_1_, bf16[128,128]{1,0:T(8,128)(2,1)S(1)} %collective-permute-done.16.refs_2_, ...), custom_call_target="tpu_custom_call" | custom-call | flops 268435456 | bytes 2850816 | tf_op jit(solution)/shard_map/pallas_call | solution.py:29
  29.8 0.1 collective-permute-start.17
  29.9 2.2 %collective-permute-start.11 = (bf16[3,128,128]{2,1,0:T(8,128)(2,1)S(1)}, bf16[3,128,128]{2,1,0:T(8,128)(2,1)S(1)}, u32[]{:S(2)}, u32[]{:S(2)}) collective-permute-start(bf16[3,128,128]{2,1,0:T(8,128)(2,1)S(1)} %get-tuple-element.54), channel_id=1, source_target_pairs={{0,12},{4,8},{8,4},{12,0},{16,28},{20,24},{24,20},{28,16},{1,13},{... | collective-permute-start | bytes 294920 | tf_op jit(solution)/shard_map/ppermute | solution.py:80
  32.1 1.3 %collective-permute-start.13 = (bf16[3,128,128]{2,1,0:T(8,128)(2,1)S(1)}, bf16[3,128,128]{2,1,0:T(8,128)(2,1)S(1)}, u32[]{:S(2)}, u32[]{:S(2)}) collective-permute-start(bf16[3,128,128]{2,1,0:T(8,128)(2,1)S(1)} %get-tuple-element.56), channel_id=1, source_target_pairs={{0,4},{4,0},{8,12},{12,8},{16,20},{20,16},{24,28},{28,24},{1,5},{5... | collective-permute-start | bytes 294920 | tf_op jit(solution)/shard_map/ppermute | solution.py:80
  33.5 0.0 collective-permute-done.17
  33.5 0.1 add_bitcast_fusion
  33.6 0.6 %collective-permute-start.18 = (bf16[1,128,512]{2,1,0:T(8,128)(2,1)S(1)}, bf16[1,128,512]{2,1,0:T(8,128)(2,1)S(1)}, u32[]{:S(2)}, u32[]{:S(2)}) collective-permute-start(bf16[1,128,512]{2,1,0:T(8,128)(2,1)S(1)} %fusion), channel_id=1, source_target_pairs={{0,2},{1,3},{2,0},{3,1},{4,6},{5,7},{6,4},{7,5},{8,10},{9,11},{10,... | collective-permute-start | bytes 393224 | tf_op jit(solution)/shard_map/ppermute | solution.py:80
  34.2 2.1 %collective-permute-done.11.refs_0_ = bf16[3,128,128]{2,1,0:T(8,128)(2,1)S(1)} collective-permute-done((bf16[3,128,128]{2,1,0:T(8,128)(2,1)S(1)}, bf16[3,128,128]{2,1,0:T(8,128)(2,1)S(1)}, u32[]{:S(2)}, u32[]{:S(2)}) %collective-permute-start.11) | collective-permute-done | bytes 98336 | tf_op jit(solution)/shard_map/ppermute | solution.py:80
  36.4 1.1 %collective-permute-done.12.refs_1_ = bf16[3,128,128]{2,1,0:T(8,128)(2,1)S(1)} collective-permute-done((bf16[3,128,128]{2,1,0:T(8,128)(2,1)S(1)}, bf16[3,128,128]{2,1,0:T(8,128)(2,1)S(1)}, u32[]{:S(2)}, u32[]{:S(2)}) %collective-permute-start.12) | collective-permute-done | bytes 98336 | tf_op jit(solution)/shard_map/ppermute | solution.py:80
  37.5 0.6 %collective-permute-done.13.refs_2_ = bf16[3,128,128]{2,1,0:T(8,128)(2,1)S(1)} collective-permute-done((bf16[3,128,128]{2,1,0:T(8,128)(2,1)S(1)}, bf16[3,128,128]{2,1,0:T(8,128)(2,1)S(1)}, u32[]{:S(2)}, u32[]{:S(2)}) %collective-permute-start.13) | collective-permute-done | bytes 98336 | tf_op jit(solution)/shard_map/ppermute | solution.py:80
  38.1 0.8 %collective-permute-done.18 = bf16[1,128,512]{2,1,0:T(8,128)(2,1)S(1)} collective-permute-done((bf16[1,128,512]{2,1,0:T(8,128)(2,1)S(1)}, bf16[1,128,512]{2,1,0:T(8,128)(2,1)S(1)}, u32[]{:S(2)}, u32[]{:S(2)}) %collective-permute-start.18) | collective-permute-done | bytes 131104 | tf_op jit(solution)/shard_map/ppermute | solution.py:80
  38.9 0.9 %shard_map.102 = (bf16[128,512]{1,0:T(8,128)(2,1)}, bf16[128,512]{1,0:T(8,128)(2,1)}, bf16[128,512]{1,0:T(8,128)(2,1)}, bf16[128,512]{1,0:T(8,128)(2,1)}) custom-call(bf16[3,128,128]{2,1,0:T(8,128)(2,1)S(1)} %collective-permute-done.11.refs_0_, bf16[3,128,128]{2,1,0:T(8,128)(2,1)S(1)} %collective-permute-done.12.refs_1_, ...), custom_call_target="tpu_custom_call" | custom-call | bytes 1310720 | tf_op jit(solution)/shard_map/pallas_call | solution.py:29
  (15 shorter events, 0.1 us)
Async XLA Ops:
  0.6 7.5 %collective-permute-start.3 = (bf16[128,512]{1,0:T(8,128)(2,1)}, bf16[128,512]{1,0:T(8,128)(2,1)S(1)}, u32[]{:S(2)}, u32[]{:S(2)}) collective-permute-start(bf16[128,512]{1,0:T(8,128)(2,1)} %refs_0_.1), channel_id=1, source_target_pairs={{0,2},{1,3},{2,0},{3,1},{4,6},{5,7},{6,4},{7,5},{8,10},{9,11},{10,... | collective-permute-start | bytes 393224 | tf_op jit(solution)/shard_map/ppermute | solution.py:80
  3.6 4.5 %collective-permute-start.4 = (bf16[128,512]{1,0:T(8,128)(2,1)}, bf16[128,512]{1,0:T(8,128)(2,1)S(1)}, u32[]{:S(2)}, u32[]{:S(2)}) collective-permute-start(bf16[128,512]{1,0:T(8,128)(2,1)} %refs_0_.1), channel_id=1, source_target_pairs={{0,1},{1,0},{2,3},{3,2},{4,5},{5,4},{6,7},{7,6},{8,9},{9,8},{10,11... | collective-permute-start | bytes 393224 | tf_op jit(solution)/shard_map/ppermute | solution.py:80
  4.6 8.8 %collective-permute-start = (bf16[3,128,128]{2,1,0:T(8,128)(2,1)S(1)}, bf16[3,128,128]{2,1,0:T(8,128)(2,1)S(1)}, u32[]{:S(2)}, u32[]{:S(2)}) collective-permute-start(bf16[3,128,128]{2,1,0:T(8,128)(2,1)S(1)} %get-tuple-element.34), channel_id=1, source_target_pairs={{0,12},{4,8},{8,4},{12,0},{16,28},{20,24},{24,20},{28,16},{1,13},{... | collective-permute-start | bytes 294920 | tf_op jit(solution)/shard_map/ppermute | solution.py:80
  7.2 6.2 %collective-permute-start.1 = (bf16[3,128,128]{2,1,0:T(8,128)(2,1)S(1)}, bf16[3,128,128]{2,1,0:T(8,128)(2,1)S(1)}, u32[]{:S(2)}, u32[]{:S(2)}) collective-permute-start(bf16[3,128,128]{2,1,0:T(8,128)(2,1)S(1)} %get-tuple-element.35), channel_id=1, source_target_pairs={{0,8},{4,12},{8,0},{12,4},{16,24},{20,28},{24,16},{28,20},{1,9},{5... | collective-permute-start | bytes 294920 | tf_op jit(solution)/shard_map/ppermute | solution.py:80
  7.7 1.9 %copy-start = (bf16[512,2048]{1,0:T(8,128)(2,1)S(1)}, bf16[512,2048]{1,0:T(8,128)(2,1)}, u32[]{:S(2)}) copy-start(bf16[512,2048]{1,0:T(8,128)(2,1)} %refs_4_.7) | copy-start | bytes 6291460
  7.7 1.9 %copy-start.5 = (bf16[128,512]{1,0:T(8,128)(2,1)S(1)}, bf16[128,512]{1,0:T(8,128)(2,1)}, u32[]{:S(2)}) copy-start(bf16[128,512]{1,0:T(8,128)(2,1)} %refs_0_.1) | copy-start | bytes 393220
  7.7 5.8 %collective-permute-start.2 = (bf16[3,128,128]{2,1,0:T(8,128)(2,1)S(1)}, bf16[3,128,128]{2,1,0:T(8,128)(2,1)S(1)}, u32[]{:S(2)}, u32[]{:S(2)}) collective-permute-start(bf16[3,128,128]{2,1,0:T(8,128)(2,1)S(1)} %get-tuple-element.36), channel_id=1, source_target_pairs={{0,4},{4,0},{8,12},{12,8},{16,20},{20,16},{24,28},{28,24},{1,5},{5... | collective-permute-start | bytes 294920 | tf_op jit(solution)/shard_map/ppermute | solution.py:80
  8.2 1.3 %collective-permute-start.5 = (bf16[128,512]{1,0:T(8,128)(2,1)S(1)}, bf16[128,512]{1,0:T(8,128)(2,1)S(1)}, u32[]{:S(2)}, u32[]{:S(2)}) collective-permute-start(bf16[128,512]{1,0:T(8,128)(2,1)S(1)} %collective-permute-done.3.refs_1_), channel_id=1, source_target_pairs={{0,1},{1,0},{2,3},{3,2},{4,5},{5,4},{6,7},{7,6},{8,9},{9,8},{10,11... | collective-permute-start | bytes 393224 | tf_op jit(solution)/shard_map/ppermute | solution.py:80
  8.2 5.3 %copy-start.1 = (bf16[4,128,256]{2,1,0:T(8,128)(2,1)S(1)}, bf16[4,128,256]{2,1,0:T(8,128)(2,1)}, u32[]{:S(2)}) copy-start(bf16[4,128,256]{2,1,0:T(8,128)(2,1)} %om_ref.3) | copy-start | bytes 786436
  8.2 5.3 %copy-start.2 = (bf16[128,512]{1,0:T(8,128)(2,1)S(1)}, bf16[128,512]{1,0:T(8,128)(2,1)}, u32[]{:S(2)}) copy-start(bf16[128,512]{1,0:T(8,128)(2,1)} %refs_3_.1) | copy-start | bytes 393220
  8.2 5.3 %copy-start.3 = (bf16[128,512]{1,0:T(8,128)(2,1)S(1)}, bf16[128,512]{1,0:T(8,128)(2,1)}, u32[]{:S(2)}) copy-start(bf16[128,512]{1,0:T(8,128)(2,1)} %refs_4_.5) | copy-start | bytes 393220
  8.2 5.3 %copy-start.4 = (bf16[128,512]{1,0:T(8,128)(2,1)S(1)}, bf16[128,512]{1,0:T(8,128)(2,1)}, u32[]{:S(2)}) copy-start(bf16[128,512]{1,0:T(8,128)(2,1)} %refs_5_.1) | copy-start | bytes 393220
  10.4 7.2 %collective-permute-start.6 = (bf16[128,128]{1,0:T(8,128)(2,1)S(1)}, bf16[128,128]{1,0:T(8,128)(2,1)S(1)}, u32[]{:S(2)}, u32[]{:S(2)}) collective-permute-start(bf16[128,128]{1,0:T(8,128)(2,1)S(1)} %get-tuple-element.40), channel_id=1, source_target_pairs={{0,12},{4,8},{8,4},{12,0},{16,28},{20,24},{24,20},{28,16},{1,13},{... | collective-permute-start | bytes 98312 | tf_op jit(solution)/shard_map/ppermute | solution.py:80
  13.0 4.6 %collective-permute-start.7 = (bf16[128,128]{1,0:T(8,128)(2,1)S(1)}, bf16[128,128]{1,0:T(8,128)(2,1)S(1)}, u32[]{:S(2)}, u32[]{:S(2)}) collective-permute-start(bf16[128,128]{1,0:T(8,128)(2,1)S(1)} %get-tuple-element.41), channel_id=1, source_target_pairs={{0,8},{4,12},{8,0},{12,4},{16,24},{20,28},{24,16},{28,20},{1,9},{5... | collective-permute-start | bytes 98312 | tf_op jit(solution)/shard_map/ppermute | solution.py:80
  14.0 6.6 %collective-permute-start.9 = (bf16[128,256]{1,0:T(8,128)(2,1)S(1)}, bf16[128,256]{1,0:T(8,128)(2,1)S(1)}, u32[]{:S(2)}, u32[]{:S(2)}) collective-permute-start(bf16[128,256]{1,0:T(8,128)(2,1)S(1)} %get-tuple-element.47), channel_id=1, source_target_pairs={{0,16},{4,20},{8,24},{12,28},{16,0},{20,4},{24,8},{28,12},{1,17},{... | collective-permute-start | bytes 196616 | tf_op jit(solution)/shard_map/ppermute | solution.py:80
  16.6 3.9 %collective-permute-start.8 = (bf16[128,128]{1,0:T(8,128)(2,1)S(1)}, bf16[128,128]{1,0:T(8,128)(2,1)S(1)}, u32[]{:S(2)}, u32[]{:S(2)}) collective-permute-start(bf16[128,128]{1,0:T(8,128)(2,1)S(1)} %get-tuple-element.45), channel_id=1, source_target_pairs={{0,4},{4,0},{8,12},{12,8},{16,20},{20,16},{24,28},{28,24},{1,5},{5... | collective-permute-start | bytes 98312 | tf_op jit(solution)/shard_map/ppermute | solution.py:80
  21.2 5.9 %collective-permute-start.10 = (bf16[128,256]{1,0:T(8,128)(2,1)S(1)}, bf16[128,256]{1,0:T(8,128)(2,1)S(1)}, u32[]{:S(2)}, u32[]{:S(2)}) collective-permute-start(bf16[128,256]{1,0:T(8,128)(2,1)S(1)} %get-tuple-element.53), channel_id=1, source_target_pairs={{0,16},{4,20},{8,24},{12,28},{16,0},{20,4},{24,8},{28,12},{1,17},{... | collective-permute-start | bytes 196616 | tf_op jit(solution)/shard_map/ppermute | solution.py:80
  22.6 5.2 %collective-permute-start.14 = (bf16[128,128]{1,0:T(8,128)(2,1)S(1)}, bf16[128,128]{1,0:T(8,128)(2,1)S(1)}, u32[]{:S(2)}, u32[]{:S(2)}) collective-permute-start(bf16[128,128]{1,0:T(8,128)(2,1)S(1)} %get-tuple-element.58), channel_id=1, source_target_pairs={{0,12},{4,8},{8,4},{12,0},{16,28},{20,24},{24,20},{28,16},{1,13},{... | collective-permute-start | bytes 98312 | tf_op jit(solution)/shard_map/ppermute | solution.py:80
  25.5 3.9 %collective-permute-start.15 = (bf16[128,128]{1,0:T(8,128)(2,1)S(1)}, bf16[128,128]{1,0:T(8,128)(2,1)S(1)}, u32[]{:S(2)}, u32[]{:S(2)}) collective-permute-start(bf16[128,128]{1,0:T(8,128)(2,1)S(1)} %get-tuple-element.59), channel_id=1, source_target_pairs={{0,8},{4,12},{8,0},{12,4},{16,24},{20,28},{24,16},{28,20},{1,9},{5... | collective-permute-start | bytes 98312 | tf_op jit(solution)/shard_map/ppermute | solution.py:80
  25.5 3.9 %collective-permute-start.16 = (bf16[128,128]{1,0:T(8,128)(2,1)S(1)}, bf16[128,128]{1,0:T(8,128)(2,1)S(1)}, u32[]{:S(2)}, u32[]{:S(2)}) collective-permute-start(bf16[128,128]{1,0:T(8,128)(2,1)S(1)} %get-tuple-element.60), channel_id=1, source_target_pairs={{0,4},{4,0},{8,12},{12,8},{16,20},{20,16},{24,28},{28,24},{1,5},{5... | collective-permute-start | bytes 98312 | tf_op jit(solution)/shard_map/ppermute | solution.py:80
  29.8 3.6 %collective-permute-start.17 = (bf16[2,128,512]{2,1,0:T(8,128)(2,1)S(1)}, bf16[2,128,512]{2,1,0:T(8,128)(2,1)S(1)}, u32[]{:S(2)}, u32[]{:S(2)}) collective-permute-start(bf16[2,128,512]{2,1,0:T(8,128)(2,1)S(1)} %get-tuple-element.63), channel_id=1, source_target_pairs={{0,1},{1,0},{2,3},{3,2},{4,5},{5,4},{6,7},{7,6},{8,9},{9,8},{10,11... | collective-permute-start | bytes 786440 | tf_op jit(solution)/shard_map/ppermute | solution.py:80
  29.9 6.4 %collective-permute-start.11 = (bf16[3,128,128]{2,1,0:T(8,128)(2,1)S(1)}, bf16[3,128,128]{2,1,0:T(8,128)(2,1)S(1)}, u32[]{:S(2)}, u32[]{:S(2)}) collective-permute-start(bf16[3,128,128]{2,1,0:T(8,128)(2,1)S(1)} %get-tuple-element.54), channel_id=1, source_target_pairs={{0,12},{4,8},{8,4},{12,0},{16,28},{20,24},{24,20},{28,16},{1,13},{... | collective-permute-start | bytes 294920 | tf_op jit(solution)/shard_map/ppermute | solution.py:80
  32.1 5.4 %collective-permute-start.12 = (bf16[3,128,128]{2,1,0:T(8,128)(2,1)S(1)}, bf16[3,128,128]{2,1,0:T(8,128)(2,1)S(1)}, u32[]{:S(2)}, u32[]{:S(2)}) collective-permute-start(bf16[3,128,128]{2,1,0:T(8,128)(2,1)S(1)} %get-tuple-element.55), channel_id=1, source_target_pairs={{0,8},{4,12},{8,0},{12,4},{16,24},{20,28},{24,16},{28,20},{1,9},{5... | collective-permute-start | bytes 294920 | tf_op jit(solution)/shard_map/ppermute | solution.py:80
  32.1 6.0 %collective-permute-start.13 = (bf16[3,128,128]{2,1,0:T(8,128)(2,1)S(1)}, bf16[3,128,128]{2,1,0:T(8,128)(2,1)S(1)}, u32[]{:S(2)}, u32[]{:S(2)}) collective-permute-start(bf16[3,128,128]{2,1,0:T(8,128)(2,1)S(1)} %get-tuple-element.56), channel_id=1, source_target_pairs={{0,4},{4,0},{8,12},{12,8},{16,20},{20,16},{24,28},{28,24},{1,5},{5... | collective-permute-start | bytes 294920 | tf_op jit(solution)/shard_map/ppermute | solution.py:80
  33.6 5.4 %collective-permute-start.18 = (bf16[1,128,512]{2,1,0:T(8,128)(2,1)S(1)}, bf16[1,128,512]{2,1,0:T(8,128)(2,1)S(1)}, u32[]{:S(2)}, u32[]{:S(2)}) collective-permute-start(bf16[1,128,512]{2,1,0:T(8,128)(2,1)S(1)} %fusion), channel_id=1, source_target_pairs={{0,2},{1,3},{2,0},{3,1},{4,6},{5,7},{6,4},{7,5},{8,10},{9,11},{10,... | collective-permute-start | bytes 393224 | tf_op jit(solution)/shard_map/ppermute | solution.py:80

commit v16 on v15

--- a/solution.py
+++ b/solution.py
@@ -131,7 +131,7 @@
     copies = [
         pltpu.make_async_copy(ref.at[:, lane(r ^ k, dim)], out.at[at], sems.at[k - 1, at])
         for k, out in enumerate(outs, 1)
-        for at, ref in enumerate((q_ref, k_ref, v_ref))
+        for at, ref in enumerate((q_ref, k_ref, v_ref)[-out.shape[0] :])
     ]
     for copy in copies:
         copy.start()
@@ -143,58 +143,72 @@
     out_ref[...] = jnp.zeros(out_ref.shape, out_ref.dtype)
 
 
-def grad_mixed_kernel(n, offsets, *refs):
-    blocks, w_ref, outs, scr = refs[: -n - 3], refs[-n - 3], refs[-n - 1 : -1], refs[-1]
-    r, h = member(n), lax.axis_index("head")
+def early_blocks_kernel(offsets, *refs):
+    blocks, w_ref, total_ref = refs[: len(offsets)], refs[-3], refs[-1]
+    h = lax.axis_index("head")
     width = blocks[0].shape[1]
-    dim = outs[0].shape[1]
     total = None
     for offset, ref in zip(offsets, blocks):
         part = mm(ref[...], w_ref[:, lane(h ^ offset, width)], NT)
         total = part if total is None else total + part
-    scr[...] = bf(total)
+    total_ref[...] = total
+
+
+def grad_mixed_kernel(n, offset, q_ref, total_ref, block_ref, w_ref, *refs):
+    outs, scr = refs[:-1], refs[-1]
+    r, h = member(n), lax.axis_index("head")
+    width = block_ref.shape[1]
+    dim = outs[0].shape[2]
+    scr[...] = bf(total_ref[...] + mm(block_ref[...], w_ref[:, lane(h ^ offset, width)], NT))
     for k in range(n):
-        outs[k][...] = scr[:, lane(r ^ k, dim)]
+        outs[k][0] = scr[:, lane(r ^ k, dim)]
+        if k > 1:
+            outs[k][1] = q_ref[:, lane(r ^ k, dim)]
 
 
 def first_kernel(n, *refs):
-    got, own, om_ref = refs[: n - 1][::-1], refs[n - 1 : n + 2], refs[n + 2]
-    qkv_ref, kf_ref, total_ref = refs[n + 4 :]
+    got, own, om_ref = refs[: n - 1][::-1], refs[n - 1 : n + 1], refs[n + 1]
+    kv_ref, kf_ref, total_ref = refs[n + 3 :]
     r = member(n)
     rows, dim = own[0].shape[0], om_ref.shape[1]
     scale = dim ** (-0.25)
     for k in range(n):
         at = pl.ds(pl.multiple_of((r ^ k) * rows, 128), rows)
         if k:
-            qkv_ref[:, at, :] = got[k - 1][...]
+            kv_ref[:, at, :] = got[k - 1][-2:]
         else:
             for i, ref in enumerate(own):
-                qkv_ref[i, at, :] = ref[:, lane(r, dim)]
-    k_all = qkv_ref[1]
+                kv_ref[i, at, :] = ref[:, lane(r, dim)]
+    k_all = kv_ref[0]
     wide = k_all.astype(jnp.float32)
     half_sq = jnp.sum(wide * wide, axis=1, keepdims=True) * (scale * scale * 0.5)
     kf = bf(jnp.exp(mm(k_all, om_ref[r]) * scale - half_sq))
     kf_ref[...] = kf
-    total_ref[...] = bf(mm(qkv_ref[2], kf, TN))
+    total_ref[...] = bf(mm(kv_ref[1], kf, TN))
 
 
 def inner_kernel(n, *refs):
-    own, (qkv_ref, om_ref, kf_ref) = refs[: n - 1][::-1], refs[n - 1 : n + 2]
-    gm_in = own[:1] + own
-    gm_ref, qf_ref, scores_ref, num_ref = refs[n + 2 :]
+    parts, (own_ref, first_ref, kv_ref, om_ref, kf_ref) = refs[: n - 1][::-1], refs[n - 1 : n + 4]
+    gm_ref, qf_ref, scores_ref, num_ref, q_scr = refs[n + 4 :]
     long, dim = num_ref.shape
     rows = long // n
     r = member(n)
-    for k in range(n):
-        gm_ref[pl.ds(pl.multiple_of((r ^ k) * rows, 128), rows), :] = gm_in[k][...]
+    places = [pl.ds(pl.multiple_of((r ^ k) * rows, 128), rows) for k in range(n)]
+    gm_ref[places[0], :] = parts[0][0]
+    q_scr[places[0], :] = own_ref[:, lane(r, dim)]
+    gm_ref[places[1], :] = jnp.zeros((rows, dim), gm_ref.dtype)
+    q_scr[places[1], :] = first_ref[0]
+    for k in range(2, n):
+        gm_ref[places[k], :] = parts[k - 1][0]
+        q_scr[places[k], :] = parts[k - 1][1]
     scale = dim ** (-0.25)
     spans = tiles(long, rows)
-    qf = bf(jnp.exp(mm(qkv_ref[0], om_ref[r]) * scale))
+    qf = bf(jnp.exp(mm(q_scr[...], om_ref[r]) * scale))
     qf_ref[...] = qf
     scores = lower(qf, kf_ref[...], spans)
     for (i, j), tile in scores.items():
         scores_ref[slice(*spans[i]), slice(*spans[j])] = tile
-    for (a, b), part in zip(spans, times(lambda i, j: scores[i, j], qkv_ref[2], spans)):
+    for (a, b), part in zip(spans, times(lambda i, j: scores[i, j], kv_ref[1], spans)):
         num_ref[a:b, :] = part
 
 
@@ -208,7 +222,7 @@
         pl.ds(pl.multiple_of((r ^ k) * rows, 128), rows) for k in range(n)
     ]
     scr[...] = gm_ref[...]
-    scr[places[1], :] = late_ref[...]
+    scr[places[1], :] = late_ref[0]
     carried = sum_of_side(earlier, n, True)
     carried_ref[...] = carried
     num = num_ref[...] + mm(qf_ref[...], carried, NT)
@@ -223,14 +237,14 @@
     total_ref[...] = bf(mm(gn, qf_ref[...], TN))
 
 
-def back_kernel(rows, qkv_ref, om_ref, kf_ref, qf_ref, scores_ref, gn_ref, carried_ref,
+def back_kernel(rows, kv_ref, om_ref, kf_ref, qf_ref, scores_ref, gn_ref, carried_ref,
                 gq_ref, gv_ref, gkf_ref):
     long, dim = gn_ref.shape
     r = member(long // rows)
     scale = dim ** (-0.25)
     spans = tiles(long, rows)
     gn, qf = gn_ref[...], qf_ref[...]
-    gs = lower(gn, qkv_ref[2], spans)
+    gs = lower(gn, kv_ref[1], spans)
     cross = mm(gn, carried_ref[...])
     for (a, b), part in zip(spans, times(lambda i, j: gs[i, j], kf_ref[...], spans)):
         terms = bf((cross[a:b] + part) * qf[a:b].astype(jnp.float32))
@@ -245,17 +259,17 @@
         gv_ref[a:b, :] = part
 
 
-def end_kernel(n, qkv_ref, om_ref, kf_ref, gq_ref, gv_ref, gkf_ref, *rest):
+def end_kernel(n, kv_ref, om_ref, kf_ref, gq_ref, gv_ref, gkf_ref, *rest):
     later, outs, (gk_scr, gv_scr) = rest[: -n - 2], rest[-n - 2 : -2], rest[-2:]
     r, dim = member(n), om_ref.shape[1]
     rows = outs[0].shape[1]
     scale = dim ** (-0.25)
     kf, after = kf_ref[...], sum_of_side(later, n, False)
     gv_scr[...] = bf(gv_ref[...] + mm(kf, after, NT))
-    gkf = gkf_ref[...] + mm(qkv_ref[2], after)
+    gkf = gkf_ref[...] + mm(kv_ref[1], after)
     terms = bf(gkf * kf.astype(jnp.float32))
     total = jnp.sum(terms.astype(jnp.float32), axis=1, keepdims=True)
-    wide = qkv_ref[1].astype(jnp.float32)
+    wide = kv_ref[0].astype(jnp.float32)
     gk_scr[...] = bf(mm(terms, om_ref[r], NT) * scale - total * wide * (scale * scale))
     for k in range(n):
         at = pl.ds(pl.multiple_of((r ^ k) * rows, 128), rows)
@@ -315,35 +329,41 @@
         offsets = offsets + [o ^ bit for o in offsets]
     sends = call(
         functools.partial(pack_kernel, n),
-        [struct((3, rows, dim))] * (n - 1),
+        [struct((3 if k == 1 else 2, rows, dim)) for k in range(1, n)],
         queries, key_vectors, value_vectors,
-        specs=[ANY] * 3, scratch=[pltpu.SemaphoreType.DMA((n - 1, 3))], vmem=53.62,
+        specs=[ANY] * 3, scratch=[pltpu.SemaphoreType.DMA((n - 1, 3))], vmem=53.68,
     )
     got = exchange(sends)
     (mark,) = call(mark_kernel, [struct((8, 128), f32)], blocks[offsets.index(1)], specs=[ANY], flops=10**10)
+    (gm_early,) = call(
+        functools.partial(early_blocks_kernel, offsets[:-1]),
+        [struct((rows, n * dim), f32)],
+        *blocks[:-1], out_weight, mark, flops=2 * rows * out_weight.size,
+        specs=[VMEM] * split + [ANY],
+    )
     gm_parts = call(
-        functools.partial(grad_mixed_kernel, n, offsets),
-        [struct((rows, dim))] * n,
-        *blocks, out_weight, mark, flops=2 * rows * out_weight.size,
-        specs=[VMEM] * (split + 1) + [ANY],
+        functools.partial(grad_mixed_kernel, n, offsets[-1]),
+        [struct((1 if k < 2 else 2, rows, dim)) for k in range(n)],
+        queries, gm_early, blocks[-1], out_weight, flops=2 * rows * out_weight.size,
         scratch=[pltpu.VMEM((rows, n * dim), jnp.bfloat16)],
     )
     gm_in = exchange(gm_parts[1:]) + [gm_parts[0]]
-    qkv, kf, total = call(
+    kv, kf, total = call(
         functools.partial(first_kernel, n),
         [
-            struct((3, long, dim)),
+            struct((2, long, dim)),
             struct((long, feats)),
             struct((dim, feats)),
         ],
-        *got, queries, key_vectors, value_vectors, feature_proj, gm_parts[0],
-        flops=2 * macs, specs=[VMEM] * (n + 3) + [ANY],
+        *got, key_vectors, value_vectors, feature_proj, gm_parts[0],
+        flops=2 * macs, specs=[VMEM] * (n + 2) + [ANY],
     )
     earlier = swap_totals(total, n)
     gm, qf, scores, num = call(
         functools.partial(inner_kernel, n),
         [struct((long, dim)), struct((long, feats)), struct((long, long)), struct((long, dim), f32)],
-        *gm_in[:-2], gm_in[-1], qkv, feature_proj, kf, flops=16 * macs,
+        *gm_in[:-2], gm_in[-1], queries, got[-1], kv, feature_proj, kf, flops=16 * macs,
+        scratch=[pltpu.VMEM((long, dim), jnp.bfloat16)],
     )
     carried, gn, later_total, *mixed_parts = call(
         functools.partial(turn_kernel, n),
@@ -361,12 +381,12 @@
     gq, gv_part, gkf_part = call(
         functools.partial(back_kernel, rows),
         [struct((long, dim)), struct((long, dim), f32), struct((long, feats), f32)],
-        qkv, feature_proj, kf, qf, scores, gn, carried, flops=8 * macs,
+        kv, feature_proj, kf, qf, scores, gn, carried, flops=8 * macs,
     )
     grads = call(
         functools.partial(end_kernel, n),
         [struct((3, rows, dim))] * n,
-        qkv, feature_proj, kf, gq, gv_part, gkf_part, *after, flops=3 * macs,
+        kv, feature_proj, kf, gq, gv_part, gkf_part, *after, flops=3 * macs,
         scratch=[pltpu.VMEM((long, dim), jnp.bfloat16)] * 2,
     )
     grads_in = exchange(grads[1:]) + [grads[0]]

time: 40 us -> 39.3 us (0.982)
  waiting for transfers between devices: 10.1 us -> 8.42 us
  local copies, waits for them, and re-layouts: 0.07 us -> 1.33 us
    ppermute x19, waiting for transfers between devices: 10.1 us -> 8.42 us  [swap(): return lax.ppermute(array, axis, [(i, i ^ bit) for i in range(size)])]
    unnamed x12, local copies, waits for them, and re-layouts: 0.03 us -> 1.29 us
    ppermute x19, starting transfers between devices: 22.4 us -> 22 us  [swap(): return lax.ppermute(array, axis, [(i, i ^ bit) for i in range(size)])]
    pallas_call x10 -> x11, Pallas kernels: 6.37 us -> 6.47 us  [call(): pl.pallas_call(body, out_shape=outs, in_specs=specs or [VMEM] * len(args)...]
where the time goes in v16:
time: 39.3 us; the launch traced here: 39.1 us
  starting transfers between devices  22 us (56%)
  waiting for transfers between devices  8.42 us (21%)
  Pallas kernels  6.47 us (16%)
  local copies, waits for them, and re-layouts  1.33 us (3%)
  between operations  0.81 us (2%)
    ppermute x19, starting transfers between devices, swap(): return lax.ppermute(array, axis, [(i, i ^ bit) for i in range(size)])  22 us
    ppermute x19, waiting for transfers between devices, swap(): return lax.ppermute(array, axis, [(i, i ^ bit) for i in range(size)])  8.42 us
    pallas_call x11, Pallas kernels, call(): pl.pallas_call(body, out_shape=outs, in_specs=specs or [VMEM] * len(args)...  6.47 us
    unnamed x12, local copies, waits for them, and re-layouts  1.29 us
  transfers between devices with their start and end apart: 19, of which 7 were waited for; matrix products, arithmetic and copies ran while one was open for 0% of the time, Pallas kernels for 11%

profile of v16, /device:TPU:0, one launch (start us, length us, event | category | flops | bytes accessed | tf_op | source)
XLA Modules:
  0.0 39.1 jit_solution(2902358513687179443)
XLA Ops:
  0.6 3.0 %collective-permute-start.3 = (bf16[128,512]{1,0:T(8,128)(2,1)}, bf16[128,512]{1,0:T(8,128)(2,1)S(1)}, u32[]{:S(2)}, u32[]{:S(2)}) collective-permute-start(bf16[128,512]{1,0:T(8,128)(2,1)} %refs_0_.1), channel_id=1, source_target_pairs={{0,2},{1,3},{2,0},{3,1},{4,6},{5,7},{6,4},{7,5},{8,10},{9,11},{10,... | collective-permute-start | bytes 393224 | tf_op jit(solution)/shard_map/ppermute | solution.py:80
  3.6 0.0 collective-permute-start.4
  3.6 0.9 %shard_map.93 = (bf16[3,128,128]{2,1,0:T(8,128)(2,1)S(1)}, bf16[2,128,128]{2,1,0:T(8,128)(2,1)S(1)}, bf16[2,128,128]{2,1,0:T(8,128)(2,1)S(1)}) custom-call(bf16[128,512]{1,0:T(8,128)(2,1)} %refs_3_.5, bf16[128,512]{1,0:T(8,128)(2,1)} %refs_3_.4, bf16[128,512]{1,0:T(8,128)(2,1)} %refs_4_.2), custom_call_target="tpu_custom_call" | custom-call | bytes 622592 | tf_op jit(solution)/shard_map/pallas_call | solution.py:29
  4.6 2.6 %collective-permute-start = (bf16[2,128,128]{2,1,0:T(8,128)(2,1)S(1)}, bf16[2,128,128]{2,1,0:T(8,128)(2,1)S(1)}, u32[]{:S(2)}, u32[]{:S(2)}) collective-permute-start(bf16[2,128,128]{2,1,0:T(8,128)(2,1)S(1)} %get-tuple-element.34), channel_id=1, source_target_pairs={{0,12},{4,8},{8,4},{12,0},{16,28},{20,24},{24,20},{28,16},{1,13},{... | collective-permute-start | bytes 196616 | tf_op jit(solution)/shard_map/ppermute | solution.py:80
  7.2 0.4 %collective-permute-start.1 = (bf16[2,128,128]{2,1,0:T(8,128)(2,1)S(1)}, bf16[2,128,128]{2,1,0:T(8,128)(2,1)S(1)}, u32[]{:S(2)}, u32[]{:S(2)}) collective-permute-start(bf16[2,128,128]{2,1,0:T(8,128)(2,1)S(1)} %get-tuple-element.35), channel_id=1, source_target_pairs={{0,8},{4,12},{8,0},{12,4},{16,24},{20,28},{24,16},{28,20},{1,9},{5... | collective-permute-start | bytes 196616 | tf_op jit(solution)/shard_map/ppermute | solution.py:80
  7.6 0.5 %collective-permute-start.2 = (bf16[3,128,128]{2,1,0:T(8,128)(2,1)S(1)}, bf16[3,128,128]{2,1,0:T(8,128)(2,1)S(1)}, u32[]{:S(2)}, u32[]{:S(2)}) collective-permute-start(bf16[3,128,128]{2,1,0:T(8,128)(2,1)S(1)} %get-tuple-element.36), channel_id=1, source_target_pairs={{0,4},{4,0},{8,12},{12,8},{16,20},{20,16},{24,28},{28,24},{1,5},{5... | collective-permute-start | bytes 294920 | tf_op jit(solution)/shard_map/ppermute | solution.py:80
  8.1 0.0 collective-permute-done.3.refs_1_
  8.1 0.0 collective-permute-start.5
  8.1 0.0 collective-permute-done.4._.refs_2_
  8.2 1.1 %copy-done = bf16[512,2048]{1,0:T(8,128)(2,1)S(1)} copy-done((bf16[512,2048]{1,0:T(8,128)(2,1)S(1)}, bf16[512,2048]{1,0:T(8,128)(2,1)}, u32[]{:S(2)}) %copy-start) | copy-done | bytes 2097176
  9.2 0.0 copy-start.4
  9.2 0.7 %shard_map.95.total_ref = f32[128,512]{1,0:T(8,128)S(1)} custom-call(bf16[128,512]{1,0:T(8,128)(2,1)S(1)} %copy-done.5, bf16[128,512]{1,0:T(8,128)(2,1)S(1)} %collective-permute-done.3.refs_1_, bf16[128,512]{1,0:T(8,128)(2,1)S(1)} %collective-permute-done.4._.refs_2_, bf16[512,2048]{1,0:T(8,128)(2,1)S(1)} %copy-done, f32[8,128]{1,0:T(8,128)S(1)} %shard_map.94.refs_4_), custom_call_target="tpu_custom_call" | custom-call | flops 268435456 | bytes 2756608 | tf_op jit(solution)/shard_map/pallas_call | solution.py:29
  9.9 0.0 collective-permute-done.5.block_ref
  9.9 0.2 copy-done.2
  10.1 0.4 shard_map.96
  10.5 2.0 %collective-permute-start.6 = (bf16[2,128,128]{2,1,0:T(8,128)(2,1)S(1)}, bf16[2,128,128]{2,1,0:T(8,128)(2,1)S(1)}, u32[]{:S(2)}, u32[]{:S(2)}) collective-permute-start(bf16[2,128,128]{2,1,0:T(8,128)(2,1)S(1)} %get-tuple-element.40), channel_id=1, source_target_pairs={{0,12},{4,8},{8,4},{12,0},{16,28},{20,24},{24,20},{28,16},{1,13},{... | collective-permute-start | bytes 196616 | tf_op jit(solution)/shard_map/ppermute | solution.py:80
  12.5 0.4 %collective-permute-start.7 = (bf16[2,128,128]{2,1,0:T(8,128)(2,1)S(1)}, bf16[2,128,128]{2,1,0:T(8,128)(2,1)S(1)}, u32[]{:S(2)}, u32[]{:S(2)}) collective-permute-start(bf16[2,128,128]{2,1,0:T(8,128)(2,1)S(1)} %get-tuple-element.41), channel_id=1, source_target_pairs={{0,8},{4,12},{8,0},{12,4},{16,24},{20,28},{24,16},{28,20},{1,9},{5... | collective-permute-start | bytes 196616 | tf_op jit(solution)/shard_map/ppermute | solution.py:80
  12.9 0.0 collective-permute-done.refs_0_
  12.9 0.0 collective-permute-done.1.refs_1_
  13.0 0.5 %shard_map.97 = (bf16[2,512,128]{2,1,0:T(8,128)(2,1)S(1)}, bf16[512,256]{1,0:T(8,128)(2,1)S(1)}, bf16[128,256]{1,0:T(8,128)(2,1)S(1)}) custom-call(bf16[2,128,128]{2,1,0:T(8,128)(2,1)S(1)} %collective-permute-done.refs_0_, bf16[2,128,128]{2,1,0:T(8,128)(2,1)S(1)} %collective-permute-done.1.refs_1_, ...), custom_call_target="tpu_custom_call" | custom-call | flops 67108864 | bytes 1376256 | tf_op jit(solution)/shard_map/pallas_call | solution.py:29
  13.4 2.7 %collective-permute-start.9 = (bf16[128,256]{1,0:T(8,128)(2,1)S(1)}, bf16[128,256]{1,0:T(8,128)(2,1)S(1)}, u32[]{:S(2)}, u32[]{:S(2)}) collective-permute-start(bf16[128,256]{1,0:T(8,128)(2,1)S(1)} %get-tuple-element.47), channel_id=1, source_target_pairs={{0,16},{4,20},{8,24},{12,28},{16,0},{20,4},{24,8},{28,12},{1,17},{... | collective-permute-start | bytes 196616 | tf_op jit(solution)/shard_map/ppermute | solution.py:80
  16.1 1.1 %collective-permute-start.8 = (bf16[1,128,128]{2,1,0:T(8,128)(2,1)S(1)}, bf16[1,128,128]{2,1,0:T(8,128)(2,1)S(1)}, u32[]{:S(2)}, u32[]{:S(2)}) collective-permute-start(bf16[1,128,128]{2,1,0:T(8,128)(2,1)S(1)} %get-tuple-element.45), channel_id=1, source_target_pairs={{0,4},{4,0},{8,12},{12,8},{16,20},{20,16},{24,28},{28,24},{1,5},{5... | collective-permute-start | bytes 98312 | tf_op jit(solution)/shard_map/ppermute | solution.py:80
  17.2 0.0 collective-permute-done.6.refs_0_
  17.2 0.2 collective-permute-done.7.refs_1_
  17.4 0.5 %shard_map.98 = (bf16[512,128]{1,0:T(8,128)(2,1)S(1)}, bf16[512,256]{1,0:T(8,128)(2,1)S(1)}, bf16[512,512]{1,0:T(8,128)(2,1)S(1)}, f32[512,128]{1,0:T(8,128)S(1)}) custom-call(bf16[2,128,128]{2,1,0:T(8,128)(2,1)S(1)} %collective-permute-done.6.refs_0_, bf16[2,128,128]{2,1,0:T(8,128)(2,1)S(1)} %collective-permute-done.7.refs_1_, ...), custom_call_target="tpu_custom_call" | custom-call | flops 536870912 | bytes 2359296 | tf_op jit(solution)/shard_map/pallas_call | solution.py:29
  18.0 2.0 %collective-permute-done.8.refs_1_ = bf16[1,128,128]{2,1,0:T(8,128)(2,1)S(1)} collective-permute-done((bf16[1,128,128]{2,1,0:T(8,128)(2,1)S(1)}, bf16[1,128,128]{2,1,0:T(8,128)(2,1)S(1)}, u32[]{:S(2)}, u32[]{:S(2)}) %collective-permute-start.8) | collective-permute-done | bytes 32800 | tf_op jit(solution)/shard_map/ppermute | solution.py:80
  20.0 0.6 %shard_map.99 = (bf16[128,256]{1,0:T(8,128)(2,1)S(1)}, bf16[512,128]{1,0:T(8,128)(2,1)S(1)}, bf16[128,256]{1,0:T(8,128)(2,1)S(1)}, bf16[128,128]{1,0:T(8,128)(2,...) custom-call(bf16[512,128]{1,0:T(8,128)(2,1)S(1)} %get-tuple-element.44.refs_0_, ...), custom_call_target="tpu_custom_call" | custom-call | flops 67108864 | bytes 1146880 | tf_op jit(solution)/shard_map/pallas_call | solution.py:29
  20.6 1.4 %collective-permute-start.10 = (bf16[128,256]{1,0:T(8,128)(2,1)S(1)}, bf16[128,256]{1,0:T(8,128)(2,1)S(1)}, u32[]{:S(2)}, u32[]{:S(2)}) collective-permute-start(bf16[128,256]{1,0:T(8,128)(2,1)S(1)} %get-tuple-element.53), channel_id=1, source_target_pairs={{0,16},{4,20},{8,24},{12,28},{16,0},{20,4},{24,8},{28,12},{1,17},{... | collective-permute-start | bytes 196616 | tf_op jit(solution)/shard_map/ppermute | solution.py:80
  22.0 2.7 %collective-permute-start.14 = (bf16[128,128]{1,0:T(8,128)(2,1)S(1)}, bf16[128,128]{1,0:T(8,128)(2,1)S(1)}, u32[]{:S(2)}, u32[]{:S(2)}) collective-permute-start(bf16[128,128]{1,0:T(8,128)(2,1)S(1)} %get-tuple-element.58), channel_id=1, source_target_pairs={{0,12},{4,8},{8,4},{12,0},{16,28},{20,24},{24,20},{28,16},{1,13},{... | collective-permute-start | bytes 98312 | tf_op jit(solution)/shard_map/ppermute | solution.py:80
  24.7 0.0 collective-permute-start.15
  24.7 0.9 %collective-permute-start.16 = (bf16[128,128]{1,0:T(8,128)(2,1)S(1)}, bf16[128,128]{1,0:T(8,128)(2,1)S(1)}, u32[]{:S(2)}, u32[]{:S(2)}) collective-permute-start(bf16[128,128]{1,0:T(8,128)(2,1)S(1)} %get-tuple-element.60), channel_id=1, source_target_pairs={{0,4},{4,0},{8,12},{12,8},{16,20},{20,16},{24,28},{28,24},{1,5},{5... | collective-permute-start | bytes 98312 | tf_op jit(solution)/shard_map/ppermute | solution.py:80
  25.6 1.0 %shard_map.100 = (bf16[512,128]{1,0:T(8,128)(2,1)S(1)}, f32[512,128]{1,0:T(8,128)S(1)}, f32[512,256]{1,0:T(8,128)S(1)}) custom-call(bf16[2,512,128]{2,1,0:T(8,128)(2,1)S(1)} %get-tuple-element.38.refs_5_.kv_ref, bf16[4,128,256]{2,1,0:T(8,128)(2,1)S(1)} %copy-done.1, bf16[512,256]{1,0:T(8,128)(2,1)S(1)} %get-tuple-element.39.refs_7_.kf_ref, ...), custom_call_target="tpu_custom_call" | custom-call | flops 268435456 | bytes 2686976 | tf_op jit(solution)/shard_map/pallas_call | solution.py:29
  26.6 0.0 collective-permute-done.10.rest_0_
  26.6 0.6 %shard_map.101 = (bf16[3,128,128]{2,1,0:T(8,128)(2,1)S(1)}, bf16[3,128,128]{2,1,0:T(8,128)(2,1)S(1)}, bf16[3,128,128]{2,1,0:T(8,128)(2,1)S(1)}, bf16[3,128,128]{2,1,0:T(8,128)(2,1)S(1)}) custom-call(bf16[2,512,128]{2,1,0:T(8,128)(2,1)S(1)} %get-tuple-element.38.refs_5_.kv_ref, bf16[4,128,256]{2,1,0:T(8,128)(2,1)S(1)} %copy-done.1, ...), custom_call_target="tpu_custom_call" | custom-call | flops 100663296 | bytes 2162688 | tf_op jit(solution)/shard_map/pallas_call | solution.py:29
  27.2 1.4 %collective-permute-done.15.refs_1_ = bf16[128,128]{1,0:T(8,128)(2,1)S(1)} collective-permute-done((bf16[128,128]{1,0:T(8,128)(2,1)S(1)}, bf16[128,128]{1,0:T(8,128)(2,1)S(1)}, u32[]{:S(2)}, u32[]{:S(2)}) %collective-permute-start.15) | collective-permute-done | bytes 32800 | tf_op jit(solution)/shard_map/ppermute | solution.py:80
  28.6 0.0 collective-permute-done.16.refs_2_
  28.6 0.5 %shard_map.102 = (bf16[2,128,512]{2,1,0:T(8,128)(2,1)S(1)}, bf16[2,128,512]{2,1,0:T(8,128)(2,1)S(1)}) custom-call(bf16[128,128]{1,0:T(8,128)(2,1)S(1)} %collective-permute-done.14.refs_0_, bf16[128,128]{1,0:T(8,128)(2,1)S(1)} %collective-permute-done.15.refs_1_, bf16[128,128]{1,0:T(8,128)(2,1)S(1)} %collective-permute-done.16.refs_2_, ...), custom_call_target="tpu_custom_call" | custom-call | flops 268435456 | bytes 2850816 | tf_op jit(solution)/shard_map/pallas_call | solution.py:29
  29.0 0.1 collective-permute-start.17
  29.1 2.4 %collective-permute-start.11 = (bf16[3,128,128]{2,1,0:T(8,128)(2,1)S(1)}, bf16[3,128,128]{2,1,0:T(8,128)(2,1)S(1)}, u32[]{:S(2)}, u32[]{:S(2)}) collective-permute-start(bf16[3,128,128]{2,1,0:T(8,128)(2,1)S(1)} %get-tuple-element.54), channel_id=1, source_target_pairs={{0,12},{4,8},{8,4},{12,0},{16,28},{20,24},{24,20},{28,16},{1,13},{... | collective-permute-start | bytes 294920 | tf_op jit(solution)/shard_map/ppermute | solution.py:80
  31.6 0.0 collective-permute-start.12
  31.6 1.1 %collective-permute-start.13 = (bf16[3,128,128]{2,1,0:T(8,128)(2,1)S(1)}, bf16[3,128,128]{2,1,0:T(8,128)(2,1)S(1)}, u32[]{:S(2)}, u32[]{:S(2)}) collective-permute-start(bf16[3,128,128]{2,1,0:T(8,128)(2,1)S(1)} %get-tuple-element.56), channel_id=1, source_target_pairs={{0,4},{4,0},{8,12},{12,8},{16,20},{20,16},{24,28},{28,24},{1,5},{5... | collective-permute-start | bytes 294920 | tf_op jit(solution)/shard_map/ppermute | solution.py:80
  32.7 0.1 add_bitcast_fusion
  32.8 0.6 %collective-permute-start.18 = (bf16[1,128,512]{2,1,0:T(8,128)(2,1)S(1)}, bf16[1,128,512]{2,1,0:T(8,128)(2,1)S(1)}, u32[]{:S(2)}, u32[]{:S(2)}) collective-permute-start(bf16[1,128,512]{2,1,0:T(8,128)(2,1)S(1)} %fusion), channel_id=1, source_target_pairs={{0,2},{1,3},{2,0},{3,1},{4,6},{5,7},{6,4},{7,5},{8,10},{9,11},{10,... | collective-permute-start | bytes 393224 | tf_op jit(solution)/shard_map/ppermute | solution.py:80
  33.4 2.2 %collective-permute-done.11.refs_0_ = bf16[3,128,128]{2,1,0:T(8,128)(2,1)S(1)} collective-permute-done((bf16[3,128,128]{2,1,0:T(8,128)(2,1)S(1)}, bf16[3,128,128]{2,1,0:T(8,128)(2,1)S(1)}, u32[]{:S(2)}, u32[]{:S(2)}) %collective-permute-start.11) | collective-permute-done | bytes 98336 | tf_op jit(solution)/shard_map/ppermute | solution.py:80
  35.6 1.2 %collective-permute-done.12.refs_1_ = bf16[3,128,128]{2,1,0:T(8,128)(2,1)S(1)} collective-permute-done((bf16[3,128,128]{2,1,0:T(8,128)(2,1)S(1)}, bf16[3,128,128]{2,1,0:T(8,128)(2,1)S(1)}, u32[]{:S(2)}, u32[]{:S(2)}) %collective-permute-start.12) | collective-permute-done | bytes 98336 | tf_op jit(solution)/shard_map/ppermute | solution.py:80
  36.8 0.5 %collective-permute-done.13.refs_2_ = bf16[3,128,128]{2,1,0:T(8,128)(2,1)S(1)} collective-permute-done((bf16[3,128,128]{2,1,0:T(8,128)(2,1)S(1)}, bf16[3,128,128]{2,1,0:T(8,128)(2,1)S(1)}, u32[]{:S(2)}, u32[]{:S(2)}) %collective-permute-start.13) | collective-permute-done | bytes 98336 | tf_op jit(solution)/shard_map/ppermute | solution.py:80
  37.3 0.8 %collective-permute-done.18 = bf16[1,128,512]{2,1,0:T(8,128)(2,1)S(1)} collective-permute-done((bf16[1,128,512]{2,1,0:T(8,128)(2,1)S(1)}, bf16[1,128,512]{2,1,0:T(8,128)(2,1)S(1)}, u32[]{:S(2)}, u32[]{:S(2)}) %collective-permute-start.18) | collective-permute-done | bytes 131104 | tf_op jit(solution)/shard_map/ppermute | solution.py:80
  38.1 0.9 %shard_map.103 = (bf16[128,512]{1,0:T(8,128)(2,1)}, bf16[128,512]{1,0:T(8,128)(2,1)}, bf16[128,512]{1,0:T(8,128)(2,1)}, bf16[128,512]{1,0:T(8,128)(2,1)}) custom-call(bf16[3,128,128]{2,1,0:T(8,128)(2,1)S(1)} %collective-permute-done.11.refs_0_, bf16[3,128,128]{2,1,0:T(8,128)(2,1)S(1)} %collective-permute-done.12.refs_1_, ...), custom_call_target="tpu_custom_call" | custom-call | bytes 1310720 | tf_op jit(solution)/shard_map/pallas_call | solution.py:29
  (16 shorter events, 0.1 us)
Async XLA Ops:
  0.6 7.5 %collective-permute-start.3 = (bf16[128,512]{1,0:T(8,128)(2,1)}, bf16[128,512]{1,0:T(8,128)(2,1)S(1)}, u32[]{:S(2)}, u32[]{:S(2)}) collective-permute-start(bf16[128,512]{1,0:T(8,128)(2,1)} %refs_0_.1), channel_id=1, source_target_pairs={{0,2},{1,3},{2,0},{3,1},{4,6},{5,7},{6,4},{7,5},{8,10},{9,11},{10,... | collective-permute-start | bytes 393224 | tf_op jit(solution)/shard_map/ppermute | solution.py:80
  3.6 4.5 %collective-permute-start.4 = (bf16[128,512]{1,0:T(8,128)(2,1)}, bf16[128,512]{1,0:T(8,128)(2,1)S(1)}, u32[]{:S(2)}, u32[]{:S(2)}) collective-permute-start(bf16[128,512]{1,0:T(8,128)(2,1)} %refs_0_.1), channel_id=1, source_target_pairs={{0,1},{1,0},{2,3},{3,2},{4,5},{5,4},{6,7},{7,6},{8,9},{9,8},{10,11... | collective-permute-start | bytes 393224 | tf_op jit(solution)/shard_map/ppermute | solution.py:80
  4.6 8.3 %collective-permute-start = (bf16[2,128,128]{2,1,0:T(8,128)(2,1)S(1)}, bf16[2,128,128]{2,1,0:T(8,128)(2,1)S(1)}, u32[]{:S(2)}, u32[]{:S(2)}) collective-permute-start(bf16[2,128,128]{2,1,0:T(8,128)(2,1)S(1)} %get-tuple-element.34), channel_id=1, source_target_pairs={{0,12},{4,8},{8,4},{12,0},{16,28},{20,24},{24,20},{28,16},{1,13},{... | collective-permute-start | bytes 196616 | tf_op jit(solution)/shard_map/ppermute | solution.py:80
  7.2 5.7 %collective-permute-start.1 = (bf16[2,128,128]{2,1,0:T(8,128)(2,1)S(1)}, bf16[2,128,128]{2,1,0:T(8,128)(2,1)S(1)}, u32[]{:S(2)}, u32[]{:S(2)}) collective-permute-start(bf16[2,128,128]{2,1,0:T(8,128)(2,1)S(1)} %get-tuple-element.35), channel_id=1, source_target_pairs={{0,8},{4,12},{8,0},{12,4},{16,24},{20,28},{24,16},{28,20},{1,9},{5... | collective-permute-start | bytes 196616 | tf_op jit(solution)/shard_map/ppermute | solution.py:80
  7.6 1.6 %copy-start = (bf16[512,2048]{1,0:T(8,128)(2,1)S(1)}, bf16[512,2048]{1,0:T(8,128)(2,1)}, u32[]{:S(2)}) copy-start(bf16[512,2048]{1,0:T(8,128)(2,1)} %refs_4_.3) | copy-start | bytes 6291460
  7.6 1.6 %copy-start.5 = (bf16[128,512]{1,0:T(8,128)(2,1)S(1)}, bf16[128,512]{1,0:T(8,128)(2,1)}, u32[]{:S(2)}) copy-start(bf16[128,512]{1,0:T(8,128)(2,1)} %refs_0_.1) | copy-start | bytes 393220
  7.6 5.3 %collective-permute-start.2 = (bf16[3,128,128]{2,1,0:T(8,128)(2,1)S(1)}, bf16[3,128,128]{2,1,0:T(8,128)(2,1)S(1)}, u32[]{:S(2)}, u32[]{:S(2)}) collective-permute-start(bf16[3,128,128]{2,1,0:T(8,128)(2,1)S(1)} %get-tuple-element.36), channel_id=1, source_target_pairs={{0,4},{4,0},{8,12},{12,8},{16,20},{20,16},{24,28},{28,24},{1,5},{5... | collective-permute-start | bytes 294920 | tf_op jit(solution)/shard_map/ppermute | solution.py:80
  8.1 1.8 %collective-permute-start.5 = (bf16[128,512]{1,0:T(8,128)(2,1)S(1)}, bf16[128,512]{1,0:T(8,128)(2,1)S(1)}, u32[]{:S(2)}, u32[]{:S(2)}) collective-permute-start(bf16[128,512]{1,0:T(8,128)(2,1)S(1)} %collective-permute-done.3.refs_1_), channel_id=1, source_target_pairs={{0,1},{1,0},{2,3},{3,2},{4,5},{5,4},{6,7},{7,6},{8,9},{9,8},{10,11... | collective-permute-start | bytes 393224 | tf_op jit(solution)/shard_map/ppermute | solution.py:80
  9.2 0.9 %copy-start.2 = (bf16[128,512]{1,0:T(8,128)(2,1)S(1)}, bf16[128,512]{1,0:T(8,128)(2,1)}, u32[]{:S(2)}) copy-start(bf16[128,512]{1,0:T(8,128)(2,1)} %refs_3_.5) | copy-start | bytes 393220
  9.2 3.7 %copy-start.1 = (bf16[4,128,256]{2,1,0:T(8,128)(2,1)S(1)}, bf16[4,128,256]{2,1,0:T(8,128)(2,1)}, u32[]{:S(2)}) copy-start(bf16[4,128,256]{2,1,0:T(8,128)(2,1)} %om_ref.3) | copy-start | bytes 786436
  9.2 3.7 %copy-start.3 = (bf16[128,512]{1,0:T(8,128)(2,1)S(1)}, bf16[128,512]{1,0:T(8,128)(2,1)}, u32[]{:S(2)}) copy-start(bf16[128,512]{1,0:T(8,128)(2,1)} %refs_3_.4) | copy-start | bytes 393220
  9.2 3.7 %copy-start.4 = (bf16[128,512]{1,0:T(8,128)(2,1)S(1)}, bf16[128,512]{1,0:T(8,128)(2,1)}, u32[]{:S(2)}) copy-start(bf16[128,512]{1,0:T(8,128)(2,1)} %refs_4_.2) | copy-start | bytes 393220
  10.5 6.7 %collective-permute-start.6 = (bf16[2,128,128]{2,1,0:T(8,128)(2,1)S(1)}, bf16[2,128,128]{2,1,0:T(8,128)(2,1)S(1)}, u32[]{:S(2)}, u32[]{:S(2)}) collective-permute-start(bf16[2,128,128]{2,1,0:T(8,128)(2,1)S(1)} %get-tuple-element.40), channel_id=1, source_target_pairs={{0,12},{4,8},{8,4},{12,0},{16,28},{20,24},{24,20},{28,16},{1,13},{... | collective-permute-start | bytes 196616 | tf_op jit(solution)/shard_map/ppermute | solution.py:80
  12.5 5.0 %collective-permute-start.7 = (bf16[2,128,128]{2,1,0:T(8,128)(2,1)S(1)}, bf16[2,128,128]{2,1,0:T(8,128)(2,1)S(1)}, u32[]{:S(2)}, u32[]{:S(2)}) collective-permute-start(bf16[2,128,128]{2,1,0:T(8,128)(2,1)S(1)} %get-tuple-element.41), channel_id=1, source_target_pairs={{0,8},{4,12},{8,0},{12,4},{16,24},{20,28},{24,16},{28,20},{1,9},{5... | collective-permute-start | bytes 196616 | tf_op jit(solution)/shard_map/ppermute | solution.py:80
  13.4 6.6 %collective-permute-start.9 = (bf16[128,256]{1,0:T(8,128)(2,1)S(1)}, bf16[128,256]{1,0:T(8,128)(2,1)S(1)}, u32[]{:S(2)}, u32[]{:S(2)}) collective-permute-start(bf16[128,256]{1,0:T(8,128)(2,1)S(1)} %get-tuple-element.47), channel_id=1, source_target_pairs={{0,16},{4,20},{8,24},{12,28},{16,0},{20,4},{24,8},{28,12},{1,17},{... | collective-permute-start | bytes 196616 | tf_op jit(solution)/shard_map/ppermute | solution.py:80
  16.1 3.9 %collective-permute-start.8 = (bf16[1,128,128]{2,1,0:T(8,128)(2,1)S(1)}, bf16[1,128,128]{2,1,0:T(8,128)(2,1)S(1)}, u32[]{:S(2)}, u32[]{:S(2)}) collective-permute-start(bf16[1,128,128]{2,1,0:T(8,128)(2,1)S(1)} %get-tuple-element.45), channel_id=1, source_target_pairs={{0,4},{4,0},{8,12},{12,8},{16,20},{20,16},{24,28},{28,24},{1,5},{5... | collective-permute-start | bytes 98312 | tf_op jit(solution)/shard_map/ppermute | solution.py:80
  20.6 5.9 %collective-permute-start.10 = (bf16[128,256]{1,0:T(8,128)(2,1)S(1)}, bf16[128,256]{1,0:T(8,128)(2,1)S(1)}, u32[]{:S(2)}, u32[]{:S(2)}) collective-permute-start(bf16[128,256]{1,0:T(8,128)(2,1)S(1)} %get-tuple-element.53), channel_id=1, source_target_pairs={{0,16},{4,20},{8,24},{12,28},{16,0},{20,4},{24,8},{28,12},{1,17},{... | collective-permute-start | bytes 196616 | tf_op jit(solution)/shard_map/ppermute | solution.py:80
  22.0 5.1 %collective-permute-start.14 = (bf16[128,128]{1,0:T(8,128)(2,1)S(1)}, bf16[128,128]{1,0:T(8,128)(2,1)S(1)}, u32[]{:S(2)}, u32[]{:S(2)}) collective-permute-start(bf16[128,128]{1,0:T(8,128)(2,1)S(1)} %get-tuple-element.58), channel_id=1, source_target_pairs={{0,12},{4,8},{8,4},{12,0},{16,28},{20,24},{24,20},{28,16},{1,13},{... | collective-permute-start | bytes 98312 | tf_op jit(solution)/shard_map/ppermute | solution.py:80
  24.7 3.9 %collective-permute-start.15 = (bf16[128,128]{1,0:T(8,128)(2,1)S(1)}, bf16[128,128]{1,0:T(8,128)(2,1)S(1)}, u32[]{:S(2)}, u32[]{:S(2)}) collective-permute-start(bf16[128,128]{1,0:T(8,128)(2,1)S(1)} %get-tuple-element.59), channel_id=1, source_target_pairs={{0,8},{4,12},{8,0},{12,4},{16,24},{20,28},{24,16},{28,20},{1,9},{5... | collective-permute-start | bytes 98312 | tf_op jit(solution)/shard_map/ppermute | solution.py:80
  24.7 3.9 %collective-permute-start.16 = (bf16[128,128]{1,0:T(8,128)(2,1)S(1)}, bf16[128,128]{1,0:T(8,128)(2,1)S(1)}, u32[]{:S(2)}, u32[]{:S(2)}) collective-permute-start(bf16[128,128]{1,0:T(8,128)(2,1)S(1)} %get-tuple-element.60), channel_id=1, source_target_pairs={{0,4},{4,0},{8,12},{12,8},{16,20},{20,16},{24,28},{28,24},{1,5},{5... | collective-permute-start | bytes 98312 | tf_op jit(solution)/shard_map/ppermute | solution.py:80
  29.0 3.6 %collective-permute-start.17 = (bf16[2,128,512]{2,1,0:T(8,128)(2,1)S(1)}, bf16[2,128,512]{2,1,0:T(8,128)(2,1)S(1)}, u32[]{:S(2)}, u32[]{:S(2)}) collective-permute-start(bf16[2,128,512]{2,1,0:T(8,128)(2,1)S(1)} %get-tuple-element.63), channel_id=1, source_target_pairs={{0,1},{1,0},{2,3},{3,2},{4,5},{5,4},{6,7},{7,6},{8,9},{9,8},{10,11... | collective-permute-start | bytes 786440 | tf_op jit(solution)/shard_map/ppermute | solution.py:80
  29.1 6.4 %collective-permute-start.11 = (bf16[3,128,128]{2,1,0:T(8,128)(2,1)S(1)}, bf16[3,128,128]{2,1,0:T(8,128)(2,1)S(1)}, u32[]{:S(2)}, u32[]{:S(2)}) collective-permute-start(bf16[3,128,128]{2,1,0:T(8,128)(2,1)S(1)} %get-tuple-element.54), channel_id=1, source_target_pairs={{0,12},{4,8},{8,4},{12,0},{16,28},{20,24},{24,20},{28,16},{1,13},{... | collective-permute-start | bytes 294920 | tf_op jit(solution)/shard_map/ppermute | solution.py:80
  31.6 5.2 %collective-permute-start.12 = (bf16[3,128,128]{2,1,0:T(8,128)(2,1)S(1)}, bf16[3,128,128]{2,1,0:T(8,128)(2,1)S(1)}, u32[]{:S(2)}, u32[]{:S(2)}) collective-permute-start(bf16[3,128,128]{2,1,0:T(8,128)(2,1)S(1)} %get-tuple-element.55), channel_id=1, source_target_pairs={{0,8},{4,12},{8,0},{12,4},{16,24},{20,28},{24,16},{28,20},{1,9},{5... | collective-permute-start | bytes 294920 | tf_op jit(solution)/shard_map/ppermute | solution.py:80
  31.6 5.8 %collective-permute-start.13 = (bf16[3,128,128]{2,1,0:T(8,128)(2,1)S(1)}, bf16[3,128,128]{2,1,0:T(8,128)(2,1)S(1)}, u32[]{:S(2)}, u32[]{:S(2)}) collective-permute-start(bf16[3,128,128]{2,1,0:T(8,128)(2,1)S(1)} %get-tuple-element.56), channel_id=1, source_target_pairs={{0,4},{4,0},{8,12},{12,8},{16,20},{20,16},{24,28},{28,24},{1,5},{5... | collective-permute-start | bytes 294920 | tf_op jit(solution)/shard_map/ppermute | solution.py:80
  32.8 5.4 %collective-permute-start.18 = (bf16[1,128,512]{2,1,0:T(8,128)(2,1)S(1)}, bf16[1,128,512]{2,1,0:T(8,128)(2,1)S(1)}, u32[]{:S(2)}, u32[]{:S(2)}) collective-permute-start(bf16[1,128,512]{2,1,0:T(8,128)(2,1)S(1)} %fusion), channel_id=1, source_target_pairs={{0,2},{1,3},{2,0},{3,1},{4,6},{5,7},{6,4},{7,5},{8,10},{9,11},{10,... | collective-permute-start | bytes 393224 | tf_op jit(solution)/shard_map/ppermute | solution.py:80

commit v17 on v16

--- a/solution.py
+++ b/solution.py
@@ -23,7 +23,7 @@
     return x.astype(jnp.bfloat16)
 
 
-def call(body, outs, *args, flops=0, specs=None, out_specs=None, scratch=(), vmem=32):
+def call(body, outs, *args, flops=0, specs=None, out_specs=None, scratch=(), vmem=32, aliases=None):
     size = sum(a.size * a.dtype.itemsize for a in args)
     size += sum(o.size * o.dtype.itemsize for o in outs)
     return pl.pallas_call(
@@ -32,6 +32,7 @@
         in_specs=specs or [VMEM] * len(args),
         out_specs=out_specs or [VMEM] * len(outs),
         scratch_shapes=list(scratch),
+        input_output_aliases=aliases or {},
         cost_estimate=pl.CostEstimate(flops=flops, bytes_accessed=size, transcendentals=0),
         compiler_params=pltpu.CompilerParams(vmem_limit_bytes=int(vmem * 1024 * 1024)),
     )(*args)
@@ -84,13 +85,31 @@
     return [1 << b for b in range(size.bit_length() - 1)]
 
 
+def sum_kernel(own_ref, *refs):
+    got, (kept_ref, sent_ref) = refs[:-2], refs[-2:]
+    rows = got[0].shape[1]
+    for i, ref in enumerate(got):
+        at = slice(i * rows, (i + 1) * rows)
+        for j in range(kept_ref.shape[0]):
+            kept_ref[j, at, :] = own_ref[2 * j, at, :].astype(jnp.float32) + ref[
+                2 * j
+            ].astype(jnp.float32)
+            sent_ref[j, at, :] = bf(
+                own_ref[2 * j + 1, at, :].astype(jnp.float32)
+                + ref[2 * j + 1].astype(jnp.float32)
+            )
+
+
 def reduce_blocks(own, sent, bits):
-    got = swap(sent, "head", 1)
-    for bit in bits[1:]:
-        total = own.astype(jnp.float32) + got.astype(jnp.float32)
+    half = struct((own.shape[0] // 2,) + own.shape[1:])
+    got = [swap(x, "head", bits[0]) for x in sent]
+    own, sent = call(sum_kernel, [struct(half.shape, jnp.float32), half], own, *got)
+    got = swap(sent, "head", bits[1])
+    for bit in bits[2:]:
+        total = own + got.astype(jnp.float32)
         pairs = total.reshape((total.shape[0] // 2, 2) + total.shape[1:])
         own, got = pairs[:, 0], swap(bf(pairs[:, 1]), "head", bit)
-    return own[0].astype(jnp.float32), got[0]
+    return own[0], got[0]
 
 
 def member(n):
@@ -279,7 +298,7 @@
 
 
 def mixed_project_kernel(n, offsets, *refs):
-    mixed_in, (w_ref, _, own_ref, sent_ref, scr) = refs[:n][::-1], refs[n:]
+    mixed_in, (w_ref, _, own_ref, *sent, scr) = refs[:n][::-1], refs[n:]
     r, h = member(n), lax.axis_index("head")
     width = own_ref.shape[2]
     dim = mixed_in[0].shape[1]
@@ -292,23 +311,38 @@
         if at < half:
             own_ref[at] = part
         else:
-            sent_ref[at - half] = part
-
-
-def unpack_kernel(n, *refs):
-    got, (part_ref, last_ref) = refs[:n][::-1], refs[n : n + 2]
-    (out_ref, *outs), (scr, sems, last_sem) = refs[n + 2 : -3], refs[-3:]
+            step = sent[0].shape[1]
+            for i, ref in enumerate(sent):
+                ref[at - half] = part[i * step : (i + 1) * step]
+
+
+def unpack_kernel(ks, n, *refs):
+    got, (*outs, sems) = refs[: len(ks)], refs[len(ks) :]
     r = member(n)
     dim = got[0].shape[2]
     copies = [
-        pltpu.make_async_copy(got[k].at[at], out.at[:, lane(r ^ k, dim)], sems.at[k, at])
-        for k in range(n)
+        pltpu.make_async_copy(ref.at[at], out.at[:, lane(r ^ k, dim)], sems.at[i, at])
+        for i, (k, ref) in enumerate(zip(ks, got))
+        for at, out in enumerate(outs)
+    ]
+    for copy in copies:
+        copy.start()
+    for copy in copies:
+        copy.wait()
+
+
+def last_kernel(n, got_ref, part_ref, last_ref, *refs):
+    (out_ref, *outs), (scr, sems) = refs[3:-2], refs[-2:]
+    r = member(n)
+    dim = got_ref.shape[2]
+    copies = [
+        pltpu.make_async_copy(got_ref.at[at], out.at[:, lane(r ^ 1, dim)], sems.at[at])
         for at, out in enumerate(outs)
     ]
     for copy in copies:
         copy.start()
     scr[...] = bf(part_ref[...] + last_ref[...].astype(jnp.float32))
-    copies.append(pltpu.make_async_copy(scr, out_ref, last_sem))
+    copies.append(pltpu.make_async_copy(scr, out_ref, sems.at[3]))
     copies[-1].start()
     for copy in copies:
         copy.wait()
@@ -392,24 +426,30 @@
     grads_in = exchange(grads[1:]) + [grads[0]]
 
     order = [o for o in range(split) if not o & 1] + [o for o in range(split) if o & 1]
-    own, sent = call(
+    own, *sent = call(
         functools.partial(mixed_project_kernel, n, order),
-        [struct((split // 2, rows, width))] * 2,
+        [struct((split // 2, rows, width))]
+        + [struct((split // 2, rows, width))],
         *mixed_in, out_weight, grads[0], flops=2 * rows * out_weight.size,
         specs=[VMEM] * (n + 1) + [ANY],
         scratch=[pltpu.VMEM((rows, n * dim), jnp.bfloat16)],
     )
     part, last = reduce_blocks(own, sent, bits)
+    *early, late, own_grads = grads_in
+    ks = [k for k in range(n - 1, 1, -1)] + [0]
+    arrays = [struct((rows, n * dim))] * 3
+    partial_grads = call(
+        functools.partial(unpack_kernel, ks, n), arrays,
+        *early, own_grads, flops=6 * 10**8,
+        out_specs=[ANY] * 3, scratch=[pltpu.SemaphoreType.DMA((n - 1, 3))],
+    )
     return call(
-        functools.partial(unpack_kernel, n),
-        [struct((rows, width))] + [struct((rows, n * dim))] * 3,
-        *grads_in, part, last,
-        out_specs=[ANY] * 4,
-        scratch=[
-            pltpu.VMEM((rows, width), jnp.bfloat16),
-            pltpu.SemaphoreType.DMA((n, 3)),
-            pltpu.SemaphoreType.DMA,
-        ],
+        functools.partial(last_kernel, n),
+        [struct((rows, width))] + arrays,
+        late, part, last, *partial_grads,
+        specs=[VMEM] * 3 + [ANY] * 3, out_specs=[ANY] * 4,
+        aliases={3: 1, 4: 2, 5: 3},
+        scratch=[pltpu.VMEM((rows, width), jnp.bfloat16), pltpu.SemaphoreType.DMA((4,))],
     )
 
 

time: 39.3 us -> 38.6 us (0.982)
  waiting for transfers between devices: 8.42 us -> 7.14 us
  Pallas kernels: 6.47 us -> 7.14 us
    ppermute x19, waiting for transfers between devices: 8.42 us -> 7.14 us  [swap(): return lax.ppermute(array, axis, [(i, i ^ bit) for i in range(size)])]
    pallas_call x11 -> x13, Pallas kernels: 6.47 us -> 7.14 us  [call(): pl.pallas_call(body, out_shape=outs, in_specs=specs or [VMEM] * len(args)...]
  transfers between devices with their start and end apart: 19 -> 19, of which waited for: 7 -> 5; matrix products, arithmetic and copies ran while one was open for 0% -> 0% of each run, Pallas kernels for 11% -> 14%
where the time goes in v17:
time: 38.6 us; the launch traced here: 38.3 us
  starting transfers between devices  22 us (57%)
  Pallas kernels  7.14 us (18%)
  waiting for transfers between devices  7.14 us (18%)
  local copies, waits for them, and re-layouts  1.29 us (3%)
  between operations  0.82 us (2%)
    ppermute x19, starting transfers between devices, swap(): return lax.ppermute(array, axis, [(i, i ^ bit) for i in range(size)])  22 us
    ppermute x19, waiting for transfers between devices, swap(): return lax.ppermute(array, axis, [(i, i ^ bit) for i in range(size)])  7.14 us
    pallas_call x13, Pallas kernels, call(): pl.pallas_call(body, out_shape=outs, in_specs=specs or [VMEM] * len(args)...  7.14 us
    unnamed x12, local copies, waits for them, and re-layouts  1.29 us
  transfers between devices with their start and end apart: 19, of which 5 were waited for; matrix products, arithmetic and copies ran while one was open for 0% of the time, Pallas kernels for 14%

profile of v17, /device:TPU:0, one launch (start us, length us, event | category | flops | bytes accessed | tf_op | source)
XLA Modules:
  0.0 38.3 jit_solution(17674736045231765511)
XLA Ops:
  0.6 3.0 %collective-permute-start.3 = (bf16[128,512]{1,0:T(8,128)(2,1)}, bf16[128,512]{1,0:T(8,128)(2,1)S(1)}, u32[]{:S(2)}, u32[]{:S(2)}) collective-permute-start(bf16[128,512]{1,0:T(8,128)(2,1)} %refs_0_.1), channel_id=1, source_target_pairs={{0,2},{1,3},{2,0},{3,1},{4,6},{5,7},{6,4},{7,5},{8,10},{9,11},{10,... | collective-permute-start | bytes 393224 | tf_op jit(solution)/shard_map/ppermute | solution.py:81
  3.6 0.9 %shard_map.93 = (bf16[3,128,128]{2,1,0:T(8,128)(2,1)S(1)}, bf16[2,128,128]{2,1,0:T(8,128)(2,1)S(1)}, bf16[2,128,128]{2,1,0:T(8,128)(2,1)S(1)}) custom-call(bf16[128,512]{1,0:T(8,128)(2,1)} %refs_3_.5, bf16[128,512]{1,0:T(8,128)(2,1)} %refs_3_.4, bf16[128,512]{1,0:T(8,128)(2,1)} %refs_4_.2), custom_call_target="tpu_custom_call" | custom-call | bytes 622592 | tf_op jit(solution)/shard_map/pallas_call | solution.py:29
  4.6 2.6 %collective-permute-start = (bf16[2,128,128]{2,1,0:T(8,128)(2,1)S(1)}, bf16[2,128,128]{2,1,0:T(8,128)(2,1)S(1)}, u32[]{:S(2)}, u32[]{:S(2)}) collective-permute-start(bf16[2,128,128]{2,1,0:T(8,128)(2,1)S(1)} %get-tuple-element.39), channel_id=1, source_target_pairs={{0,12},{4,8},{8,4},{12,0},{16,28},{20,24},{24,20},{28,16},{1,13},{... | collective-permute-start | bytes 196616 | tf_op jit(solution)/shard_map/ppermute | solution.py:81
  7.2 0.4 %collective-permute-start.1 = (bf16[2,128,128]{2,1,0:T(8,128)(2,1)S(1)}, bf16[2,128,128]{2,1,0:T(8,128)(2,1)S(1)}, u32[]{:S(2)}, u32[]{:S(2)}) collective-permute-start(bf16[2,128,128]{2,1,0:T(8,128)(2,1)S(1)} %get-tuple-element.40), channel_id=1, source_target_pairs={{0,8},{4,12},{8,0},{12,4},{16,24},{20,28},{24,16},{28,20},{1,9},{5... | collective-permute-start | bytes 196616 | tf_op jit(solution)/shard_map/ppermute | solution.py:81
  7.6 0.5 %collective-permute-start.2 = (bf16[3,128,128]{2,1,0:T(8,128)(2,1)S(1)}, bf16[3,128,128]{2,1,0:T(8,128)(2,1)S(1)}, u32[]{:S(2)}, u32[]{:S(2)}) collective-permute-start(bf16[3,128,128]{2,1,0:T(8,128)(2,1)S(1)} %get-tuple-element.41), channel_id=1, source_target_pairs={{0,4},{4,0},{8,12},{12,8},{16,20},{20,16},{24,28},{28,24},{1,5},{5... | collective-permute-start | bytes 294920 | tf_op jit(solution)/shard_map/ppermute | solution.py:81
  8.1 0.0 collective-permute-done.3.refs_1_
  8.1 0.0 collective-permute-start.5
  8.1 0.0 collective-permute-done.4._.refs_2_
  8.2 1.1 %copy-done = bf16[512,2048]{1,0:T(8,128)(2,1)S(1)} copy-done((bf16[512,2048]{1,0:T(8,128)(2,1)S(1)}, bf16[512,2048]{1,0:T(8,128)(2,1)}, u32[]{:S(2)}) %copy-start) | copy-done | bytes 2097176
  9.2 0.0 copy-start.4
  9.2 0.7 %shard_map.95.total_ref = f32[128,512]{1,0:T(8,128)S(1)} custom-call(bf16[128,512]{1,0:T(8,128)(2,1)S(1)} %copy-done.5, bf16[128,512]{1,0:T(8,128)(2,1)S(1)} %collective-permute-done.3.refs_1_, bf16[128,512]{1,0:T(8,128)(2,1)S(1)} %collective-permute-done.4._.refs_2_, bf16[512,2048]{1,0:T(8,128)(2,1)S(1)} %copy-done, f32[8,128]{1,0:T(8,128)S(1)} %shard_map.94.refs_4_), custom_call_target="tpu_custom_call" | custom-call | flops 268435456 | bytes 2756608 | tf_op jit(solution)/shard_map/pallas_call | solution.py:29
  9.9 0.0 collective-permute-done.5.block_ref
  9.9 0.2 copy-done.2
  10.1 0.4 shard_map.96
  10.5 2.0 %collective-permute-start.6 = (bf16[2,128,128]{2,1,0:T(8,128)(2,1)S(1)}, bf16[2,128,128]{2,1,0:T(8,128)(2,1)S(1)}, u32[]{:S(2)}, u32[]{:S(2)}) collective-permute-start(bf16[2,128,128]{2,1,0:T(8,128)(2,1)S(1)} %get-tuple-element.45), channel_id=1, source_target_pairs={{0,12},{4,8},{8,4},{12,0},{16,28},{20,24},{24,20},{28,16},{1,13},{... | collective-permute-start | bytes 196616 | tf_op jit(solution)/shard_map/ppermute | solution.py:81
  12.5 0.4 %collective-permute-start.7 = (bf16[2,128,128]{2,1,0:T(8,128)(2,1)S(1)}, bf16[2,128,128]{2,1,0:T(8,128)(2,1)S(1)}, u32[]{:S(2)}, u32[]{:S(2)}) collective-permute-start(bf16[2,128,128]{2,1,0:T(8,128)(2,1)S(1)} %get-tuple-element.46), channel_id=1, source_target_pairs={{0,8},{4,12},{8,0},{12,4},{16,24},{20,28},{24,16},{28,20},{1,9},{5... | collective-permute-start | bytes 196616 | tf_op jit(solution)/shard_map/ppermute | solution.py:81
  12.9 0.0 collective-permute-done.refs_0_
  12.9 0.0 collective-permute-done.1.refs_1_
  12.9 0.0 collective-permute-done.2.refs_2_.refs_4_
  13.0 0.5 %shard_map.97 = (bf16[2,512,128]{2,1,0:T(8,128)(2,1)S(1)}, bf16[512,256]{1,0:T(8,128)(2,1)S(1)}, bf16[128,256]{1,0:T(8,128)(2,1)S(1)}) custom-call(bf16[2,128,128]{2,1,0:T(8,128)(2,1)S(1)} %collective-permute-done.refs_0_, bf16[2,128,128]{2,1,0:T(8,128)(2,1)S(1)} %collective-permute-done.1.refs_1_, ...), custom_call_target="tpu_custom_call" | custom-call | flops 67108864 | bytes 1376256 | tf_op jit(solution)/shard_map/pallas_call | solution.py:29
  13.4 2.7 %collective-permute-start.9 = (bf16[128,256]{1,0:T(8,128)(2,1)S(1)}, bf16[128,256]{1,0:T(8,128)(2,1)S(1)}, u32[]{:S(2)}, u32[]{:S(2)}) collective-permute-start(bf16[128,256]{1,0:T(8,128)(2,1)S(1)} %get-tuple-element.52), channel_id=1, source_target_pairs={{0,16},{4,20},{8,24},{12,28},{16,0},{20,4},{24,8},{28,12},{1,17},{... | collective-permute-start | bytes 196616 | tf_op jit(solution)/shard_map/ppermute | solution.py:81
  16.1 1.1 %collective-permute-start.8 = (bf16[1,128,128]{2,1,0:T(8,128)(2,1)S(1)}, bf16[1,128,128]{2,1,0:T(8,128)(2,1)S(1)}, u32[]{:S(2)}, u32[]{:S(2)}) collective-permute-start(bf16[1,128,128]{2,1,0:T(8,128)(2,1)S(1)} %get-tuple-element.50), channel_id=1, source_target_pairs={{0,4},{4,0},{8,12},{12,8},{16,20},{20,16},{24,28},{28,24},{1,5},{5... | collective-permute-start | bytes 98312 | tf_op jit(solution)/shard_map/ppermute | solution.py:81
  17.2 0.2 collective-permute-done.7.refs_1_
  17.4 0.5 %shard_map.98 = (bf16[512,128]{1,0:T(8,128)(2,1)S(1)}, bf16[512,256]{1,0:T(8,128)(2,1)S(1)}, bf16[512,512]{1,0:T(8,128)(2,1)S(1)}, f32[512,128]{1,0:T(8,128)S(1)}) custom-call(bf16[2,128,128]{2,1,0:T(8,128)(2,1)S(1)} %collective-permute-done.6.refs_0_, bf16[2,128,128]{2,1,0:T(8,128)(2,1)S(1)} %collective-permute-done.7.refs_1_, ...), custom_call_target="tpu_custom_call" | custom-call | flops 536870912 | bytes 2359296 | tf_op jit(solution)/shard_map/pallas_call | solution.py:29
  18.0 2.0 %collective-permute-done.8.refs_1_ = bf16[1,128,128]{2,1,0:T(8,128)(2,1)S(1)} collective-permute-done((bf16[1,128,128]{2,1,0:T(8,128)(2,1)S(1)}, bf16[1,128,128]{2,1,0:T(8,128)(2,1)S(1)}, u32[]{:S(2)}, u32[]{:S(2)}) %collective-permute-start.8) | collective-permute-done | bytes 32800 | tf_op jit(solution)/shard_map/ppermute | solution.py:81
  20.0 0.0 collective-permute-done.9.refs_4_
  20.0 0.6 %shard_map.99 = (bf16[128,256]{1,0:T(8,128)(2,1)S(1)}, bf16[512,128]{1,0:T(8,128)(2,1)S(1)}, bf16[128,256]{1,0:T(8,128)(2,1)S(1)}, bf16[128,128]{1,0:T(8,128)(2,...) custom-call(bf16[512,128]{1,0:T(8,128)(2,1)S(1)} %get-tuple-element.49.refs_0_, ...), custom_call_target="tpu_custom_call" | custom-call | flops 67108864 | bytes 1146880 | tf_op jit(solution)/shard_map/pallas_call | solution.py:29
  20.6 1.4 %collective-permute-start.10 = (bf16[128,256]{1,0:T(8,128)(2,1)S(1)}, bf16[128,256]{1,0:T(8,128)(2,1)S(1)}, u32[]{:S(2)}, u32[]{:S(2)}) collective-permute-start(bf16[128,256]{1,0:T(8,128)(2,1)S(1)} %get-tuple-element.58), channel_id=1, source_target_pairs={{0,16},{4,20},{8,24},{12,28},{16,0},{20,4},{24,8},{28,12},{1,17},{... | collective-permute-start | bytes 196616 | tf_op jit(solution)/shard_map/ppermute | solution.py:81
  22.0 2.7 %collective-permute-start.12 = (bf16[128,128]{1,0:T(8,128)(2,1)S(1)}, bf16[128,128]{1,0:T(8,128)(2,1)S(1)}, u32[]{:S(2)}, u32[]{:S(2)}) collective-permute-start(bf16[128,128]{1,0:T(8,128)(2,1)S(1)} %get-tuple-element.60), channel_id=1, source_target_pairs={{0,12},{4,8},{8,4},{12,0},{16,28},{20,24},{24,20},{28,16},{1,13},{... | collective-permute-start | bytes 98312 | tf_op jit(solution)/shard_map/ppermute | solution.py:81
  24.7 0.0 collective-permute-start.13
  24.7 0.9 %collective-permute-start.14 = (bf16[128,128]{1,0:T(8,128)(2,1)S(1)}, bf16[128,128]{1,0:T(8,128)(2,1)S(1)}, u32[]{:S(2)}, u32[]{:S(2)}) collective-permute-start(bf16[128,128]{1,0:T(8,128)(2,1)S(1)} %get-tuple-element.62), channel_id=1, source_target_pairs={{0,4},{4,0},{8,12},{12,8},{16,20},{20,16},{24,28},{28,24},{1,5},{5... | collective-permute-start | bytes 98312 | tf_op jit(solution)/shard_map/ppermute | solution.py:81
  25.6 1.0 %shard_map.100 = (bf16[512,128]{1,0:T(8,128)(2,1)S(1)}, f32[512,128]{1,0:T(8,128)S(1)}, f32[512,256]{1,0:T(8,128)S(1)}) custom-call(bf16[2,512,128]{2,1,0:T(8,128)(2,1)S(1)} %get-tuple-element.43.refs_5_.kv_ref, bf16[4,128,256]{2,1,0:T(8,128)(2,1)S(1)} %copy-done.1, bf16[512,256]{1,0:T(8,128)(2,1)S(1)} %get-tuple-element.44.refs_7_.kf_ref, ...), custom_call_target="tpu_custom_call" | custom-call | flops 268435456 | bytes 2686976 | tf_op jit(solution)/shard_map/pallas_call | solution.py:29
  26.6 0.0 collective-permute-done.10.rest_0_
  26.6 0.6 %shard_map.101 = (bf16[3,128,128]{2,1,0:T(8,128)(2,1)S(1)}, bf16[3,128,128]{2,1,0:T(8,128)(2,1)S(1)}, bf16[3,128,128]{2,1,0:T(8,128)(2,1)S(1)}, bf16[3,128,128]{2,1,0:T(8,128)(2,1)S(1)}) custom-call(bf16[2,512,128]{2,1,0:T(8,128)(2,1)S(1)} %get-tuple-element.43.refs_5_.kv_ref, bf16[4,128,256]{2,1,0:T(8,128)(2,1)S(1)} %copy-done.1, ...), custom_call_target="tpu_custom_call" | custom-call | flops 100663296 | bytes 2162688 | tf_op jit(solution)/shard_map/pallas_call | solution.py:29
  27.2 0.0 collective-permute-done.12.refs_0_
  27.2 1.4 %collective-permute-done.13.refs_1_ = bf16[128,128]{1,0:T(8,128)(2,1)S(1)} collective-permute-done((bf16[128,128]{1,0:T(8,128)(2,1)S(1)}, bf16[128,128]{1,0:T(8,128)(2,1)S(1)}, u32[]{:S(2)}, u32[]{:S(2)}) %collective-permute-start.13) | collective-permute-done | bytes 32800 | tf_op jit(solution)/shard_map/ppermute | solution.py:81
  28.6 0.5 %shard_map.102 = (bf16[2,128,512]{2,1,0:T(8,128)(2,1)S(1)}, bf16[2,128,512]{2,1,0:T(8,128)(2,1)S(1)}) custom-call(bf16[128,128]{1,0:T(8,128)(2,1)S(1)} %collective-permute-done.12.refs_0_, bf16[128,128]{1,0:T(8,128)(2,1)S(1)} %collective-permute-done.13.refs_1_, bf16[128,128]{1,0:T(8,128)(2,1)S(1)} %collective-permute-done.14.refs_2_, ...), custom_call_target="tpu_custom_call" | custom-call | flops 268435456 | bytes 2850816 | tf_op jit(solution)/shard_map/pallas_call | solution.py:29
  29.0 0.1 collective-permute-start.15
  29.1 2.4 %collective-permute-start.17 = (bf16[3,128,128]{2,1,0:T(8,128)(2,1)S(1)}, bf16[3,128,128]{2,1,0:T(8,128)(2,1)S(1)}, u32[]{:S(2)}, u32[]{:S(2)}) collective-permute-start(bf16[3,128,128]{2,1,0:T(8,128)(2,1)S(1)} %get-tuple-element.69), channel_id=1, source_target_pairs={{0,12},{4,8},{8,4},{12,0},{16,28},{20,24},{24,20},{28,16},{1,13},{... | collective-permute-start | bytes 294920 | tf_op jit(solution)/shard_map/ppermute | solution.py:81
  31.6 0.1 shard_map.103
  31.6 1.0 %collective-permute-start.16 = (bf16[1,128,512]{2,1,0:T(8,128)(2,1)S(1)}, bf16[1,128,512]{2,1,0:T(8,128)(2,1)S(1)}, u32[]{:S(2)}, u32[]{:S(2)}) collective-permute-start(bf16[1,128,512]{2,1,0:T(8,128)(2,1)S(1)} %get-tuple-element.68), channel_id=1, source_target_pairs={{0,2},{1,3},{2,0},{3,1},{4,6},{5,7},{6,4},{7,5},{8,10},{9,11},{10,... | collective-permute-start | bytes 393224 | tf_op jit(solution)/shard_map/ppermute | solution.py:81
  32.6 0.7 %collective-permute-start.11 = (bf16[3,128,128]{2,1,0:T(8,128)(2,1)S(1)}, bf16[3,128,128]{2,1,0:T(8,128)(2,1)S(1)}, u32[]{:S(2)}, u32[]{:S(2)}) collective-permute-start(bf16[3,128,128]{2,1,0:T(8,128)(2,1)S(1)} %get-tuple-element.59), channel_id=1, source_target_pairs={{0,4},{4,0},{8,12},{12,8},{16,20},{20,16},{24,28},{28,24},{1,5},{5... | collective-permute-start | bytes 294920 | tf_op jit(solution)/shard_map/ppermute | solution.py:81
  33.3 2.2 %collective-permute-done.17.refs_0_ = bf16[3,128,128]{2,1,0:T(8,128)(2,1)S(1)} collective-permute-done((bf16[3,128,128]{2,1,0:T(8,128)(2,1)S(1)}, bf16[3,128,128]{2,1,0:T(8,128)(2,1)S(1)}, u32[]{:S(2)}, u32[]{:S(2)}) %collective-permute-start.17) | collective-permute-done | bytes 98336 | tf_op jit(solution)/shard_map/ppermute | solution.py:81
  35.6 1.2 %collective-permute-done.18.refs_1_ = bf16[3,128,128]{2,1,0:T(8,128)(2,1)S(1)} collective-permute-done((bf16[3,128,128]{2,1,0:T(8,128)(2,1)S(1)}, bf16[3,128,128]{2,1,0:T(8,128)(2,1)S(1)}, u32[]{:S(2)}, u32[]{:S(2)}) %collective-permute-start.18) | collective-permute-done | bytes 98336 | tf_op jit(solution)/shard_map/ppermute | solution.py:81
  36.8 0.8 %shard_map.104 = (bf16[128,512]{1,0:T(8,128)(2,1)}, bf16[128,512]{1,0:T(8,128)(2,1)}, bf16[128,512]{1,0:T(8,128)(2,1)}) custom-call(bf16[3,128,128]{2,1,0:T(8,128)(2,1)S(1)} %collective-permute-done.17.refs_0_, bf16[3,128,128]{2,1,0:T(8,128)(2,1)S(1)} %collective-permute-done.18.refs_1_, bf16[3,128,128]{2,1,0:T(8,128)(2,1)S(1)} %get-tuple-element.64.refs_5_.refs_2_), custom_call_target="tpu_custom_call" | custom-call | flops 600000000 | bytes 688128 | tf_op jit(solution)/shard_map/pallas_call | solution.py:29
  37.6 0.0 collective-permute-done.11.got_ref
  37.6 0.0 collective-permute-done.16
  37.6 0.7 %shard_map.105 = (bf16[128,512]{1,0:T(8,128)(2,1)}, bf16[128,512]{1,0:T(8,128)(2,1)}, bf16[128,512]{1,0:T(8,128)(2,1)}, bf16[128,512]{1,0:T(8,128)(2,1)}) custom-call(bf16[3,128,128]{2,1,0:T(8,128)(2,1)S(1)} %collective-permute-done.11.got_ref, f32[128,512]{1,0:T(8,128)S(1)} %bitcast.2, ...), custom_call_target="tpu_custom_call", output_to_operand_aliasing={{1}: (3, {}), {2}: (4, {}), {3}: (5, {})} | custom-call | bytes 1409024 | tf_op jit(solution)/shard_map/pallas_call | solution.py:29
  (15 shorter events, 0.0 us)
Async XLA Ops:
  0.6 7.5 %collective-permute-start.3 = (bf16[128,512]{1,0:T(8,128)(2,1)}, bf16[128,512]{1,0:T(8,128)(2,1)S(1)}, u32[]{:S(2)}, u32[]{:S(2)}) collective-permute-start(bf16[128,512]{1,0:T(8,128)(2,1)} %refs_0_.1), channel_id=1, source_target_pairs={{0,2},{1,3},{2,0},{3,1},{4,6},{5,7},{6,4},{7,5},{8,10},{9,11},{10,... | collective-permute-start | bytes 393224 | tf_op jit(solution)/shard_map/ppermute | solution.py:81
  3.6 4.5 %collective-permute-start.4 = (bf16[128,512]{1,0:T(8,128)(2,1)}, bf16[128,512]{1,0:T(8,128)(2,1)S(1)}, u32[]{:S(2)}, u32[]{:S(2)}) collective-permute-start(bf16[128,512]{1,0:T(8,128)(2,1)} %refs_0_.1), channel_id=1, source_target_pairs={{0,1},{1,0},{2,3},{3,2},{4,5},{5,4},{6,7},{7,6},{8,9},{9,8},{10,11... | collective-permute-start | bytes 393224 | tf_op jit(solution)/shard_map/ppermute | solution.py:81
  4.6 8.3 %collective-permute-start = (bf16[2,128,128]{2,1,0:T(8,128)(2,1)S(1)}, bf16[2,128,128]{2,1,0:T(8,128)(2,1)S(1)}, u32[]{:S(2)}, u32[]{:S(2)}) collective-permute-start(bf16[2,128,128]{2,1,0:T(8,128)(2,1)S(1)} %get-tuple-element.39), channel_id=1, source_target_pairs={{0,12},{4,8},{8,4},{12,0},{16,28},{20,24},{24,20},{28,16},{1,13},{... | collective-permute-start | bytes 196616 | tf_op jit(solution)/shard_map/ppermute | solution.py:81
  7.2 5.7 %collective-permute-start.1 = (bf16[2,128,128]{2,1,0:T(8,128)(2,1)S(1)}, bf16[2,128,128]{2,1,0:T(8,128)(2,1)S(1)}, u32[]{:S(2)}, u32[]{:S(2)}) collective-permute-start(bf16[2,128,128]{2,1,0:T(8,128)(2,1)S(1)} %get-tuple-element.40), channel_id=1, source_target_pairs={{0,8},{4,12},{8,0},{12,4},{16,24},{20,28},{24,16},{28,20},{1,9},{5... | collective-permute-start | bytes 196616 | tf_op jit(solution)/shard_map/ppermute | solution.py:81
  7.6 1.6 %copy-start = (bf16[512,2048]{1,0:T(8,128)(2,1)S(1)}, bf16[512,2048]{1,0:T(8,128)(2,1)}, u32[]{:S(2)}) copy-start(bf16[512,2048]{1,0:T(8,128)(2,1)} %refs_4_.3) | copy-start | bytes 6291460
  7.6 1.6 %copy-start.5 = (bf16[128,512]{1,0:T(8,128)(2,1)S(1)}, bf16[128,512]{1,0:T(8,128)(2,1)}, u32[]{:S(2)}) copy-start(bf16[128,512]{1,0:T(8,128)(2,1)} %refs_0_.1) | copy-start | bytes 393220
  7.6 5.3 %collective-permute-start.2 = (bf16[3,128,128]{2,1,0:T(8,128)(2,1)S(1)}, bf16[3,128,128]{2,1,0:T(8,128)(2,1)S(1)}, u32[]{:S(2)}, u32[]{:S(2)}) collective-permute-start(bf16[3,128,128]{2,1,0:T(8,128)(2,1)S(1)} %get-tuple-element.41), channel_id=1, source_target_pairs={{0,4},{4,0},{8,12},{12,8},{16,20},{20,16},{24,28},{28,24},{1,5},{5... | collective-permute-start | bytes 294920 | tf_op jit(solution)/shard_map/ppermute | solution.py:81
  8.1 1.8 %collective-permute-start.5 = (bf16[128,512]{1,0:T(8,128)(2,1)S(1)}, bf16[128,512]{1,0:T(8,128)(2,1)S(1)}, u32[]{:S(2)}, u32[]{:S(2)}) collective-permute-start(bf16[128,512]{1,0:T(8,128)(2,1)S(1)} %collective-permute-done.3.refs_1_), channel_id=1, source_target_pairs={{0,1},{1,0},{2,3},{3,2},{4,5},{5,4},{6,7},{7,6},{8,9},{9,8},{10,11... | collective-permute-start | bytes 393224 | tf_op jit(solution)/shard_map/ppermute | solution.py:81
  9.2 0.9 %copy-start.2 = (bf16[128,512]{1,0:T(8,128)(2,1)S(1)}, bf16[128,512]{1,0:T(8,128)(2,1)}, u32[]{:S(2)}) copy-start(bf16[128,512]{1,0:T(8,128)(2,1)} %refs_3_.5) | copy-start | bytes 393220
  9.2 3.7 %copy-start.1 = (bf16[4,128,256]{2,1,0:T(8,128)(2,1)S(1)}, bf16[4,128,256]{2,1,0:T(8,128)(2,1)}, u32[]{:S(2)}) copy-start(bf16[4,128,256]{2,1,0:T(8,128)(2,1)} %om_ref.3) | copy-start | bytes 786436
  9.2 3.7 %copy-start.3 = (bf16[128,512]{1,0:T(8,128)(2,1)S(1)}, bf16[128,512]{1,0:T(8,128)(2,1)}, u32[]{:S(2)}) copy-start(bf16[128,512]{1,0:T(8,128)(2,1)} %refs_3_.4) | copy-start | bytes 393220
  9.2 3.7 %copy-start.4 = (bf16[128,512]{1,0:T(8,128)(2,1)S(1)}, bf16[128,512]{1,0:T(8,128)(2,1)}, u32[]{:S(2)}) copy-start(bf16[128,512]{1,0:T(8,128)(2,1)} %refs_4_.2) | copy-start | bytes 393220
  10.5 6.7 %collective-permute-start.6 = (bf16[2,128,128]{2,1,0:T(8,128)(2,1)S(1)}, bf16[2,128,128]{2,1,0:T(8,128)(2,1)S(1)}, u32[]{:S(2)}, u32[]{:S(2)}) collective-permute-start(bf16[2,128,128]{2,1,0:T(8,128)(2,1)S(1)} %get-tuple-element.45), channel_id=1, source_target_pairs={{0,12},{4,8},{8,4},{12,0},{16,28},{20,24},{24,20},{28,16},{1,13},{... | collective-permute-start | bytes 196616 | tf_op jit(solution)/shard_map/ppermute | solution.py:81
  12.5 5.0 %collective-permute-start.7 = (bf16[2,128,128]{2,1,0:T(8,128)(2,1)S(1)}, bf16[2,128,128]{2,1,0:T(8,128)(2,1)S(1)}, u32[]{:S(2)}, u32[]{:S(2)}) collective-permute-start(bf16[2,128,128]{2,1,0:T(8,128)(2,1)S(1)} %get-tuple-element.46), channel_id=1, source_target_pairs={{0,8},{4,12},{8,0},{12,4},{16,24},{20,28},{24,16},{28,20},{1,9},{5... | collective-permute-start | bytes 196616 | tf_op jit(solution)/shard_map/ppermute | solution.py:81
  13.4 6.6 %collective-permute-start.9 = (bf16[128,256]{1,0:T(8,128)(2,1)S(1)}, bf16[128,256]{1,0:T(8,128)(2,1)S(1)}, u32[]{:S(2)}, u32[]{:S(2)}) collective-permute-start(bf16[128,256]{1,0:T(8,128)(2,1)S(1)} %get-tuple-element.52), channel_id=1, source_target_pairs={{0,16},{4,20},{8,24},{12,28},{16,0},{20,4},{24,8},{28,12},{1,17},{... | collective-permute-start | bytes 196616 | tf_op jit(solution)/shard_map/ppermute | solution.py:81
  16.1 3.9 %collective-permute-start.8 = (bf16[1,128,128]{2,1,0:T(8,128)(2,1)S(1)}, bf16[1,128,128]{2,1,0:T(8,128)(2,1)S(1)}, u32[]{:S(2)}, u32[]{:S(2)}) collective-permute-start(bf16[1,128,128]{2,1,0:T(8,128)(2,1)S(1)} %get-tuple-element.50), channel_id=1, source_target_pairs={{0,4},{4,0},{8,12},{12,8},{16,20},{20,16},{24,28},{28,24},{1,5},{5... | collective-permute-start | bytes 98312 | tf_op jit(solution)/shard_map/ppermute | solution.py:81
  20.6 5.9 %collective-permute-start.10 = (bf16[128,256]{1,0:T(8,128)(2,1)S(1)}, bf16[128,256]{1,0:T(8,128)(2,1)S(1)}, u32[]{:S(2)}, u32[]{:S(2)}) collective-permute-start(bf16[128,256]{1,0:T(8,128)(2,1)S(1)} %get-tuple-element.58), channel_id=1, source_target_pairs={{0,16},{4,20},{8,24},{12,28},{16,0},{20,4},{24,8},{28,12},{1,17},{... | collective-permute-start | bytes 196616 | tf_op jit(solution)/shard_map/ppermute | solution.py:81
  22.0 5.1 %collective-permute-start.12 = (bf16[128,128]{1,0:T(8,128)(2,1)S(1)}, bf16[128,128]{1,0:T(8,128)(2,1)S(1)}, u32[]{:S(2)}, u32[]{:S(2)}) collective-permute-start(bf16[128,128]{1,0:T(8,128)(2,1)S(1)} %get-tuple-element.60), channel_id=1, source_target_pairs={{0,12},{4,8},{8,4},{12,0},{16,28},{20,24},{24,20},{28,16},{1,13},{... | collective-permute-start | bytes 98312 | tf_op jit(solution)/shard_map/ppermute | solution.py:81
  24.7 3.9 %collective-permute-start.13 = (bf16[128,128]{1,0:T(8,128)(2,1)S(1)}, bf16[128,128]{1,0:T(8,128)(2,1)S(1)}, u32[]{:S(2)}, u32[]{:S(2)}) collective-permute-start(bf16[128,128]{1,0:T(8,128)(2,1)S(1)} %get-tuple-element.61), channel_id=1, source_target_pairs={{0,8},{4,12},{8,0},{12,4},{16,24},{20,28},{24,16},{28,20},{1,9},{5... | collective-permute-start | bytes 98312 | tf_op jit(solution)/shard_map/ppermute | solution.py:81
  24.7 3.9 %collective-permute-start.14 = (bf16[128,128]{1,0:T(8,128)(2,1)S(1)}, bf16[128,128]{1,0:T(8,128)(2,1)S(1)}, u32[]{:S(2)}, u32[]{:S(2)}) collective-permute-start(bf16[128,128]{1,0:T(8,128)(2,1)S(1)} %get-tuple-element.62), channel_id=1, source_target_pairs={{0,4},{4,0},{8,12},{12,8},{16,20},{20,16},{24,28},{28,24},{1,5},{5... | collective-permute-start | bytes 98312 | tf_op jit(solution)/shard_map/ppermute | solution.py:81
  29.0 2.5 %collective-permute-start.15 = (bf16[2,128,512]{2,1,0:T(8,128)(2,1)S(1)}, bf16[2,128,512]{2,1,0:T(8,128)(2,1)S(1)}, u32[]{:S(2)}, u32[]{:S(2)}) collective-permute-start(bf16[2,128,512]{2,1,0:T(8,128)(2,1)S(1)} %get-tuple-element.66), channel_id=1, source_target_pairs={{0,1},{1,0},{2,3},{3,2},{4,5},{5,4},{6,7},{7,6},{8,9},{9,8},{10,11... | collective-permute-start | bytes 786440 | tf_op jit(solution)/shard_map/ppermute | solution.py:81
  29.1 6.4 %collective-permute-start.17 = (bf16[3,128,128]{2,1,0:T(8,128)(2,1)S(1)}, bf16[3,128,128]{2,1,0:T(8,128)(2,1)S(1)}, u32[]{:S(2)}, u32[]{:S(2)}) collective-permute-start(bf16[3,128,128]{2,1,0:T(8,128)(2,1)S(1)} %get-tuple-element.69), channel_id=1, source_target_pairs={{0,12},{4,8},{8,4},{12,0},{16,28},{20,24},{24,20},{28,16},{1,13},{... | collective-permute-start | bytes 294920 | tf_op jit(solution)/shard_map/ppermute | solution.py:81
  31.6 5.2 %collective-permute-start.18 = (bf16[3,128,128]{2,1,0:T(8,128)(2,1)S(1)}, bf16[3,128,128]{2,1,0:T(8,128)(2,1)S(1)}, u32[]{:S(2)}, u32[]{:S(2)}) collective-permute-start(bf16[3,128,128]{2,1,0:T(8,128)(2,1)S(1)} %get-tuple-element.70), channel_id=1, source_target_pairs={{0,8},{4,12},{8,0},{12,4},{16,24},{20,28},{24,16},{28,20},{1,9},{5... | collective-permute-start | bytes 294920 | tf_op jit(solution)/shard_map/ppermute | solution.py:81
  31.6 6.0 %collective-permute-start.16 = (bf16[1,128,512]{2,1,0:T(8,128)(2,1)S(1)}, bf16[1,128,512]{2,1,0:T(8,128)(2,1)S(1)}, u32[]{:S(2)}, u32[]{:S(2)}) collective-permute-start(bf16[1,128,512]{2,1,0:T(8,128)(2,1)S(1)} %get-tuple-element.68), channel_id=1, source_target_pairs={{0,2},{1,3},{2,0},{3,1},{4,6},{5,7},{6,4},{7,5},{8,10},{9,11},{10,... | collective-permute-start | bytes 393224 | tf_op jit(solution)/shard_map/ppermute | solution.py:81
  32.6 4.9 %collective-permute-start.11 = (bf16[3,128,128]{2,1,0:T(8,128)(2,1)S(1)}, bf16[3,128,128]{2,1,0:T(8,128)(2,1)S(1)}, u32[]{:S(2)}, u32[]{:S(2)}) collective-permute-start(bf16[3,128,128]{2,1,0:T(8,128)(2,1)S(1)} %get-tuple-element.59), channel_id=1, source_target_pairs={{0,4},{4,0},{8,12},{12,8},{16,20},{20,16},{24,28},{28,24},{1,5},{5... | collective-permute-start | bytes 294920 | tf_op jit(solution)/shard_map/ppermute | solution.py:81

commit v18 on v17

--- a/solution.py
+++ b/solution.py
@@ -86,7 +86,7 @@
 
 
 def sum_kernel(own_ref, *refs):
-    got, (kept_ref, sent_ref) = refs[:-2], refs[-2:]
+    got, (kept_ref, sent_ref) = refs[:-3], refs[-2:]
     rows = got[0].shape[1]
     for i, ref in enumerate(got):
         at = slice(i * rows, (i + 1) * rows)
@@ -103,7 +103,11 @@
 def reduce_blocks(own, sent, bits):
     half = struct((own.shape[0] // 2,) + own.shape[1:])
     got = [swap(x, "head", bits[0]) for x in sent]
-    own, sent = call(sum_kernel, [struct(half.shape, jnp.float32), half], own, *got)
+    (mark,) = call(mark_kernel, [struct((8, 128), jnp.float32)], own, specs=[ANY], flops=28 * 10**8)
+    own, sent = call(
+        sum_kernel, [struct(half.shape, jnp.float32), half], own, *got, mark,
+        specs=[VMEM] * (1 + len(got)) + [ANY],
+    )
     got = swap(sent, "head", bits[1])
     for bit in bits[2:]:
         total = own + got.astype(jnp.float32)
@@ -440,7 +444,7 @@
     arrays = [struct((rows, n * dim))] * 3
     partial_grads = call(
         functools.partial(unpack_kernel, ks, n), arrays,
-        *early, own_grads, flops=6 * 10**8,
+        *early, own_grads, flops=8 * 10**8,
         out_specs=[ANY] * 3, scratch=[pltpu.SemaphoreType.DMA((n - 1, 3))],
     )
     return call(

time: 38.6 us -> 38.5 us (level)
  waiting for transfers between devices: 7.14 us -> 6.69 us
  starting transfers between devices: 22 us -> 22.4 us
    ppermute x19, waiting for transfers between devices: 7.14 us -> 6.69 us  [swap(): return lax.ppermute(array, axis, [(i, i ^ bit) for i in range(size)])]
    ppermute x19, starting transfers between devices: 22 us -> 22.4 us  [swap(): return lax.ppermute(array, axis, [(i, i ^ bit) for i in range(size)])]
    pallas_call x13 -> x14, Pallas kernels: 7.14 us -> 7.14 us  [call(): pl.pallas_call(body, out_shape=outs, in_specs=specs or [VMEM] * len(args)...]
  transfers between devices with their start and end apart: 19 -> 19, of which waited for: 5 -> 6; matrix products, arithmetic and copies ran while one was open for 0% -> 0% of each run, Pallas kernels for 14% -> 15%
where the time goes in v18:
time: 38.5 us; the launch traced here: 38.3 us
  starting transfers between devices  22.4 us (58%)
  Pallas kernels  7.14 us (19%)
  waiting for transfers between devices  6.69 us (17%)
  local copies, waits for them, and re-layouts  1.29 us (3%)
  between operations  0.82 us (2%)
    ppermute x19, starting transfers between devices, swap(): return lax.ppermute(array, axis, [(i, i ^ bit) for i in range(size)])  22.4 us
    pallas_call x14, Pallas kernels, call(): pl.pallas_call(body, out_shape=outs, in_specs=specs or [VMEM] * len(args)...  7.14 us
    ppermute x19, waiting for transfers between devices, swap(): return lax.ppermute(array, axis, [(i, i ^ bit) for i in range(size)])  6.69 us
    unnamed x12, local copies, waits for them, and re-layouts  1.29 us
  transfers between devices with their start and end apart: 19, of which 6 were waited for; matrix products, arithmetic and copies ran while one was open for 0% of the time, Pallas kernels for 15%

profile of v18, /device:TPU:0, one launch (start us, length us, event | category | flops | bytes accessed | tf_op | source)
XLA Modules:
  0.0 38.3 jit_solution(11988683433068621770)
XLA Ops:
  0.6 3.0 %collective-permute-start.3 = (bf16[128,512]{1,0:T(8,128)(2,1)}, bf16[128,512]{1,0:T(8,128)(2,1)S(1)}, u32[]{:S(2)}, u32[]{:S(2)}) collective-permute-start(bf16[128,512]{1,0:T(8,128)(2,1)} %refs_0_.1), channel_id=1, source_target_pairs={{0,2},{1,3},{2,0},{3,1},{4,6},{5,7},{6,4},{7,5},{8,10},{9,11},{10,... | collective-permute-start | bytes 393224 | tf_op jit(solution)/shard_map/ppermute | solution.py:81
  3.6 0.0 collective-permute-start.4
  3.6 0.9 %shard_map.93 = (bf16[3,128,128]{2,1,0:T(8,128)(2,1)S(1)}, bf16[2,128,128]{2,1,0:T(8,128)(2,1)S(1)}, bf16[2,128,128]{2,1,0:T(8,128)(2,1)S(1)}) custom-call(bf16[128,512]{1,0:T(8,128)(2,1)} %refs_3_.5, bf16[128,512]{1,0:T(8,128)(2,1)} %refs_3_.4, bf16[128,512]{1,0:T(8,128)(2,1)} %refs_4_.2), custom_call_target="tpu_custom_call" | custom-call | bytes 622592 | tf_op jit(solution)/shard_map/pallas_call | solution.py:29
  4.6 2.6 %collective-permute-start = (bf16[2,128,128]{2,1,0:T(8,128)(2,1)S(1)}, bf16[2,128,128]{2,1,0:T(8,128)(2,1)S(1)}, u32[]{:S(2)}, u32[]{:S(2)}) collective-permute-start(bf16[2,128,128]{2,1,0:T(8,128)(2,1)S(1)} %get-tuple-element.39), channel_id=1, source_target_pairs={{0,12},{4,8},{8,4},{12,0},{16,28},{20,24},{24,20},{28,16},{1,13},{... | collective-permute-start | bytes 196616 | tf_op jit(solution)/shard_map/ppermute | solution.py:81
  7.2 0.4 %collective-permute-start.1 = (bf16[2,128,128]{2,1,0:T(8,128)(2,1)S(1)}, bf16[2,128,128]{2,1,0:T(8,128)(2,1)S(1)}, u32[]{:S(2)}, u32[]{:S(2)}) collective-permute-start(bf16[2,128,128]{2,1,0:T(8,128)(2,1)S(1)} %get-tuple-element.40), channel_id=1, source_target_pairs={{0,8},{4,12},{8,0},{12,4},{16,24},{20,28},{24,16},{28,20},{1,9},{5... | collective-permute-start | bytes 196616 | tf_op jit(solution)/shard_map/ppermute | solution.py:81
  7.6 0.5 %collective-permute-start.2 = (bf16[3,128,128]{2,1,0:T(8,128)(2,1)S(1)}, bf16[3,128,128]{2,1,0:T(8,128)(2,1)S(1)}, u32[]{:S(2)}, u32[]{:S(2)}) collective-permute-start(bf16[3,128,128]{2,1,0:T(8,128)(2,1)S(1)} %get-tuple-element.41), channel_id=1, source_target_pairs={{0,4},{4,0},{8,12},{12,8},{16,20},{20,16},{24,28},{28,24},{1,5},{5... | collective-permute-start | bytes 294920 | tf_op jit(solution)/shard_map/ppermute | solution.py:81
  8.1 0.0 collective-permute-done.3.refs_1_
  8.1 0.0 collective-permute-start.5
  8.1 0.0 collective-permute-done.4._.refs_2_
  8.2 1.1 %copy-done = bf16[512,2048]{1,0:T(8,128)(2,1)S(1)} copy-done((bf16[512,2048]{1,0:T(8,128)(2,1)S(1)}, bf16[512,2048]{1,0:T(8,128)(2,1)}, u32[]{:S(2)}) %copy-start) | copy-done | bytes 2097176
  9.2 0.0 copy-start.4
  9.2 0.7 %shard_map.95.total_ref = f32[128,512]{1,0:T(8,128)S(1)} custom-call(bf16[128,512]{1,0:T(8,128)(2,1)S(1)} %copy-done.5, bf16[128,512]{1,0:T(8,128)(2,1)S(1)} %collective-permute-done.3.refs_1_, bf16[128,512]{1,0:T(8,128)(2,1)S(1)} %collective-permute-done.4._.refs_2_, bf16[512,2048]{1,0:T(8,128)(2,1)S(1)} %copy-done, f32[8,128]{1,0:T(8,128)S(1)} %shard_map.94.refs_4_), custom_call_target="tpu_custom_call" | custom-call | flops 268435456 | bytes 2756608 | tf_op jit(solution)/shard_map/pallas_call | solution.py:29
  9.9 0.0 collective-permute-done.5.block_ref
  9.9 0.2 copy-done.2
  10.1 0.4 shard_map.96
  10.5 2.0 %collective-permute-start.6 = (bf16[2,128,128]{2,1,0:T(8,128)(2,1)S(1)}, bf16[2,128,128]{2,1,0:T(8,128)(2,1)S(1)}, u32[]{:S(2)}, u32[]{:S(2)}) collective-permute-start(bf16[2,128,128]{2,1,0:T(8,128)(2,1)S(1)} %get-tuple-element.45), channel_id=1, source_target_pairs={{0,12},{4,8},{8,4},{12,0},{16,28},{20,24},{24,20},{28,16},{1,13},{... | collective-permute-start | bytes 196616 | tf_op jit(solution)/shard_map/ppermute | solution.py:81
  12.5 0.4 %collective-permute-start.7 = (bf16[2,128,128]{2,1,0:T(8,128)(2,1)S(1)}, bf16[2,128,128]{2,1,0:T(8,128)(2,1)S(1)}, u32[]{:S(2)}, u32[]{:S(2)}) collective-permute-start(bf16[2,128,128]{2,1,0:T(8,128)(2,1)S(1)} %get-tuple-element.46), channel_id=1, source_target_pairs={{0,8},{4,12},{8,0},{12,4},{16,24},{20,28},{24,16},{28,20},{1,9},{5... | collective-permute-start | bytes 196616 | tf_op jit(solution)/shard_map/ppermute | solution.py:81
  12.9 0.0 collective-permute-done.refs_0_
  13.0 0.5 %shard_map.97 = (bf16[2,512,128]{2,1,0:T(8,128)(2,1)S(1)}, bf16[512,256]{1,0:T(8,128)(2,1)S(1)}, bf16[128,256]{1,0:T(8,128)(2,1)S(1)}) custom-call(bf16[2,128,128]{2,1,0:T(8,128)(2,1)S(1)} %collective-permute-done.refs_0_, bf16[2,128,128]{2,1,0:T(8,128)(2,1)S(1)} %collective-permute-done.1.refs_1_, ...), custom_call_target="tpu_custom_call" | custom-call | flops 67108864 | bytes 1376256 | tf_op jit(solution)/shard_map/pallas_call | solution.py:29
  13.4 2.7 %collective-permute-start.9 = (bf16[128,256]{1,0:T(8,128)(2,1)S(1)}, bf16[128,256]{1,0:T(8,128)(2,1)S(1)}, u32[]{:S(2)}, u32[]{:S(2)}) collective-permute-start(bf16[128,256]{1,0:T(8,128)(2,1)S(1)} %get-tuple-element.52), channel_id=1, source_target_pairs={{0,16},{4,20},{8,24},{12,28},{16,0},{20,4},{24,8},{28,12},{1,17},{... | collective-permute-start | bytes 196616 | tf_op jit(solution)/shard_map/ppermute | solution.py:81
  16.1 1.1 %collective-permute-start.8 = (bf16[1,128,128]{2,1,0:T(8,128)(2,1)S(1)}, bf16[1,128,128]{2,1,0:T(8,128)(2,1)S(1)}, u32[]{:S(2)}, u32[]{:S(2)}) collective-permute-start(bf16[1,128,128]{2,1,0:T(8,128)(2,1)S(1)} %get-tuple-element.50), channel_id=1, source_target_pairs={{0,4},{4,0},{8,12},{12,8},{16,20},{20,16},{24,28},{28,24},{1,5},{5... | collective-permute-start | bytes 98312 | tf_op jit(solution)/shard_map/ppermute | solution.py:81
  17.2 0.0 collective-permute-done.6.refs_0_
  17.2 0.2 collective-permute-done.7.refs_1_
  17.4 0.5 %shard_map.98 = (bf16[512,128]{1,0:T(8,128)(2,1)S(1)}, bf16[512,256]{1,0:T(8,128)(2,1)S(1)}, bf16[512,512]{1,0:T(8,128)(2,1)S(1)}, f32[512,128]{1,0:T(8,128)S(1)}) custom-call(bf16[2,128,128]{2,1,0:T(8,128)(2,1)S(1)} %collective-permute-done.6.refs_0_, bf16[2,128,128]{2,1,0:T(8,128)(2,1)S(1)} %collective-permute-done.7.refs_1_, ...), custom_call_target="tpu_custom_call" | custom-call | flops 536870912 | bytes 2359296 | tf_op jit(solution)/shard_map/pallas_call | solution.py:29
  18.0 2.0 %collective-permute-done.8.refs_1_ = bf16[1,128,128]{2,1,0:T(8,128)(2,1)S(1)} collective-permute-done((bf16[1,128,128]{2,1,0:T(8,128)(2,1)S(1)}, bf16[1,128,128]{2,1,0:T(8,128)(2,1)S(1)}, u32[]{:S(2)}, u32[]{:S(2)}) %collective-permute-start.8) | collective-permute-done | bytes 32800 | tf_op jit(solution)/shard_map/ppermute | solution.py:81
  20.0 0.6 %shard_map.99 = (bf16[128,256]{1,0:T(8,128)(2,1)S(1)}, bf16[512,128]{1,0:T(8,128)(2,1)S(1)}, bf16[128,256]{1,0:T(8,128)(2,1)S(1)}, bf16[128,128]{1,0:T(8,128)(2,...) custom-call(bf16[512,128]{1,0:T(8,128)(2,1)S(1)} %get-tuple-element.49.refs_0_, ...), custom_call_target="tpu_custom_call" | custom-call | flops 67108864 | bytes 1146880 | tf_op jit(solution)/shard_map/pallas_call | solution.py:29
  20.6 1.4 %collective-permute-start.10 = (bf16[128,256]{1,0:T(8,128)(2,1)S(1)}, bf16[128,256]{1,0:T(8,128)(2,1)S(1)}, u32[]{:S(2)}, u32[]{:S(2)}) collective-permute-start(bf16[128,256]{1,0:T(8,128)(2,1)S(1)} %get-tuple-element.58), channel_id=1, source_target_pairs={{0,16},{4,20},{8,24},{12,28},{16,0},{20,4},{24,8},{28,12},{1,17},{... | collective-permute-start | bytes 196616 | tf_op jit(solution)/shard_map/ppermute | solution.py:81
  22.0 2.7 %collective-permute-start.12 = (bf16[128,128]{1,0:T(8,128)(2,1)S(1)}, bf16[128,128]{1,0:T(8,128)(2,1)S(1)}, u32[]{:S(2)}, u32[]{:S(2)}) collective-permute-start(bf16[128,128]{1,0:T(8,128)(2,1)S(1)} %get-tuple-element.60), channel_id=1, source_target_pairs={{0,12},{4,8},{8,4},{12,0},{16,28},{20,24},{24,20},{28,16},{1,13},{... | collective-permute-start | bytes 98312 | tf_op jit(solution)/shard_map/ppermute | solution.py:81
  24.7 0.0 collective-permute-start.13
  24.7 0.9 %collective-permute-start.14 = (bf16[128,128]{1,0:T(8,128)(2,1)S(1)}, bf16[128,128]{1,0:T(8,128)(2,1)S(1)}, u32[]{:S(2)}, u32[]{:S(2)}) collective-permute-start(bf16[128,128]{1,0:T(8,128)(2,1)S(1)} %get-tuple-element.62), channel_id=1, source_target_pairs={{0,4},{4,0},{8,12},{12,8},{16,20},{20,16},{24,28},{28,24},{1,5},{5... | collective-permute-start | bytes 98312 | tf_op jit(solution)/shard_map/ppermute | solution.py:81
  25.6 1.0 %shard_map.100 = (bf16[512,128]{1,0:T(8,128)(2,1)S(1)}, f32[512,128]{1,0:T(8,128)S(1)}, f32[512,256]{1,0:T(8,128)S(1)}) custom-call(bf16[2,512,128]{2,1,0:T(8,128)(2,1)S(1)} %get-tuple-element.43.refs_5_.kv_ref, bf16[4,128,256]{2,1,0:T(8,128)(2,1)S(1)} %copy-done.1, bf16[512,256]{1,0:T(8,128)(2,1)S(1)} %get-tuple-element.44.refs_7_.kf_ref, ...), custom_call_target="tpu_custom_call" | custom-call | flops 268435456 | bytes 2686976 | tf_op jit(solution)/shard_map/pallas_call | solution.py:29
  26.6 0.6 %shard_map.101 = (bf16[3,128,128]{2,1,0:T(8,128)(2,1)S(1)}, bf16[3,128,128]{2,1,0:T(8,128)(2,1)S(1)}, bf16[3,128,128]{2,1,0:T(8,128)(2,1)S(1)}, bf16[3,128,128]{2,1,0:T(8,128)(2,1)S(1)}) custom-call(bf16[2,512,128]{2,1,0:T(8,128)(2,1)S(1)} %get-tuple-element.43.refs_5_.kv_ref, bf16[4,128,256]{2,1,0:T(8,128)(2,1)S(1)} %copy-done.1, ...), custom_call_target="tpu_custom_call" | custom-call | flops 100663296 | bytes 2162688 | tf_op jit(solution)/shard_map/pallas_call | solution.py:29
  27.2 2.7 %collective-permute-start.17 = (bf16[3,128,128]{2,1,0:T(8,128)(2,1)S(1)}, bf16[3,128,128]{2,1,0:T(8,128)(2,1)S(1)}, u32[]{:S(2)}, u32[]{:S(2)}) collective-permute-start(bf16[3,128,128]{2,1,0:T(8,128)(2,1)S(1)} %get-tuple-element.69), channel_id=1, source_target_pairs={{0,12},{4,8},{8,4},{12,0},{16,28},{20,24},{24,20},{28,16},{1,13},{... | collective-permute-start | bytes 294920 | tf_op jit(solution)/shard_map/ppermute | solution.py:81
  29.8 0.0 collective-permute-start.18
  29.8 0.0 collective-permute-done.12.refs_0_
  29.8 0.0 collective-permute-done.13.refs_1_
  29.8 0.5 %shard_map.102 = (bf16[2,128,512]{2,1,0:T(8,128)(2,1)S(1)}, bf16[2,128,512]{2,1,0:T(8,128)(2,1)S(1)}) custom-call(bf16[128,128]{1,0:T(8,128)(2,1)S(1)} %collective-permute-done.12.refs_0_, bf16[128,128]{1,0:T(8,128)(2,1)S(1)} %collective-permute-done.13.refs_1_, bf16[128,128]{1,0:T(8,128)(2,1)S(1)} %collective-permute-done.14.refs_2_, ...), custom_call_target="tpu_custom_call" | custom-call | flops 268435456 | bytes 2850816 | tf_op jit(solution)/shard_map/pallas_call | solution.py:29
  30.3 0.1 collective-permute-start.15
  30.4 1.5 %collective-permute-done.15.refs_0_ = bf16[2,128,512]{2,1,0:T(8,128)(2,1)S(1)} collective-permute-done((bf16[2,128,512]{2,1,0:T(8,128)(2,1)S(1)}, bf16[2,128,512]{2,1,0:T(8,128)(2,1)S(1)}, u32[]{:S(2)}, u32[]{:S(2)}) %collective-permute-start.15) | collective-permute-done | bytes 262176 | tf_op jit(solution)/shard_map/ppermute | solution.py:81
  31.9 0.1 shard_map.104
  32.0 0.6 %collective-permute-start.16 = (bf16[1,128,512]{2,1,0:T(8,128)(2,1)S(1)}, bf16[1,128,512]{2,1,0:T(8,128)(2,1)S(1)}, u32[]{:S(2)}, u32[]{:S(2)}) collective-permute-start(bf16[1,128,512]{2,1,0:T(8,128)(2,1)S(1)} %get-tuple-element.68), channel_id=1, source_target_pairs={{0,2},{1,3},{2,0},{3,1},{4,6},{5,7},{6,4},{7,5},{8,10},{9,11},{10,... | collective-permute-start | bytes 393224 | tf_op jit(solution)/shard_map/ppermute | solution.py:81
  32.6 1.3 %collective-permute-start.11 = (bf16[3,128,128]{2,1,0:T(8,128)(2,1)S(1)}, bf16[3,128,128]{2,1,0:T(8,128)(2,1)S(1)}, u32[]{:S(2)}, u32[]{:S(2)}) collective-permute-start(bf16[3,128,128]{2,1,0:T(8,128)(2,1)S(1)} %get-tuple-element.59), channel_id=1, source_target_pairs={{0,4},{4,0},{8,12},{12,8},{16,20},{20,16},{24,28},{28,24},{1,5},{5... | collective-permute-start | bytes 294920 | tf_op jit(solution)/shard_map/ppermute | solution.py:81
  33.9 0.0 collective-permute-done.17.refs_0_
  33.9 0.6 %collective-permute-done.18.refs_1_ = bf16[3,128,128]{2,1,0:T(8,128)(2,1)S(1)} collective-permute-done((bf16[3,128,128]{2,1,0:T(8,128)(2,1)S(1)}, bf16[3,128,128]{2,1,0:T(8,128)(2,1)S(1)}, u32[]{:S(2)}, u32[]{:S(2)}) %collective-permute-start.18) | collective-permute-done | bytes 98336 | tf_op jit(solution)/shard_map/ppermute | solution.py:81
  34.4 0.8 %shard_map.105 = (bf16[128,512]{1,0:T(8,128)(2,1)}, bf16[128,512]{1,0:T(8,128)(2,1)}, bf16[128,512]{1,0:T(8,128)(2,1)}) custom-call(bf16[3,128,128]{2,1,0:T(8,128)(2,1)S(1)} %collective-permute-done.17.refs_0_, bf16[3,128,128]{2,1,0:T(8,128)(2,1)S(1)} %collective-permute-done.18.refs_1_, bf16[3,128,128]{2,1,0:T(8,128)(2,1)S(1)} %get-tuple-element.64.refs_5_.refs_2_), custom_call_target="tpu_custom_call" | custom-call | flops 800000000 | bytes 688128 | tf_op jit(solution)/shard_map/pallas_call | solution.py:29
  35.2 2.0 %collective-permute-done.11.got_ref = bf16[3,128,128]{2,1,0:T(8,128)(2,1)S(1)} collective-permute-done((bf16[3,128,128]{2,1,0:T(8,128)(2,1)S(1)}, bf16[3,128,128]{2,1,0:T(8,128)(2,1)S(1)}, u32[]{:S(2)}, u32[]{:S(2)}) %collective-permute-start.11) | collective-permute-done | bytes 98336 | tf_op jit(solution)/shard_map/ppermute | solution.py:81
  37.2 0.4 %collective-permute-done.16 = bf16[1,128,512]{2,1,0:T(8,128)(2,1)S(1)} collective-permute-done((bf16[1,128,512]{2,1,0:T(8,128)(2,1)S(1)}, bf16[1,128,512]{2,1,0:T(8,128)(2,1)S(1)}, u32[]{:S(2)}, u32[]{:S(2)}) %collective-permute-start.16) | collective-permute-done | bytes 131104 | tf_op jit(solution)/shard_map/ppermute | solution.py:81
  37.6 0.7 %shard_map.106 = (bf16[128,512]{1,0:T(8,128)(2,1)}, bf16[128,512]{1,0:T(8,128)(2,1)}, bf16[128,512]{1,0:T(8,128)(2,1)}, bf16[128,512]{1,0:T(8,128)(2,1)}) custom-call(bf16[3,128,128]{2,1,0:T(8,128)(2,1)S(1)} %collective-permute-done.11.got_ref, f32[128,512]{1,0:T(8,128)S(1)} %bitcast.2, ...), custom_call_target="tpu_custom_call", output_to_operand_aliasing={{1}: (3, {}), {2}: (4, {}), {3}: (5, {})} | custom-call | bytes 1409024 | tf_op jit(solution)/shard_map/pallas_call | solution.py:29
  (16 shorter events, 0.0 us)
Async XLA Ops:
  0.6 7.5 %collective-permute-start.3 = (bf16[128,512]{1,0:T(8,128)(2,1)}, bf16[128,512]{1,0:T(8,128)(2,1)S(1)}, u32[]{:S(2)}, u32[]{:S(2)}) collective-permute-start(bf16[128,512]{1,0:T(8,128)(2,1)} %refs_0_.1), channel_id=1, source_target_pairs={{0,2},{1,3},{2,0},{3,1},{4,6},{5,7},{6,4},{7,5},{8,10},{9,11},{10,... | collective-permute-start | bytes 393224 | tf_op jit(solution)/shard_map/ppermute | solution.py:81
  3.6 4.5 %collective-permute-start.4 = (bf16[128,512]{1,0:T(8,128)(2,1)}, bf16[128,512]{1,0:T(8,128)(2,1)S(1)}, u32[]{:S(2)}, u32[]{:S(2)}) collective-permute-start(bf16[128,512]{1,0:T(8,128)(2,1)} %refs_0_.1), channel_id=1, source_target_pairs={{0,1},{1,0},{2,3},{3,2},{4,5},{5,4},{6,7},{7,6},{8,9},{9,8},{10,11... | collective-permute-start | bytes 393224 | tf_op jit(solution)/shard_map/ppermute | solution.py:81
  4.6 8.3 %collective-permute-start = (bf16[2,128,128]{2,1,0:T(8,128)(2,1)S(1)}, bf16[2,128,128]{2,1,0:T(8,128)(2,1)S(1)}, u32[]{:S(2)}, u32[]{:S(2)}) collective-permute-start(bf16[2,128,128]{2,1,0:T(8,128)(2,1)S(1)} %get-tuple-element.39), channel_id=1, source_target_pairs={{0,12},{4,8},{8,4},{12,0},{16,28},{20,24},{24,20},{28,16},{1,13},{... | collective-permute-start | bytes 196616 | tf_op jit(solution)/shard_map/ppermute | solution.py:81
  7.2 5.7 %collective-permute-start.1 = (bf16[2,128,128]{2,1,0:T(8,128)(2,1)S(1)}, bf16[2,128,128]{2,1,0:T(8,128)(2,1)S(1)}, u32[]{:S(2)}, u32[]{:S(2)}) collective-permute-start(bf16[2,128,128]{2,1,0:T(8,128)(2,1)S(1)} %get-tuple-element.40), channel_id=1, source_target_pairs={{0,8},{4,12},{8,0},{12,4},{16,24},{20,28},{24,16},{28,20},{1,9},{5... | collective-permute-start | bytes 196616 | tf_op jit(solution)/shard_map/ppermute | solution.py:81
  7.6 1.6 %copy-start = (bf16[512,2048]{1,0:T(8,128)(2,1)S(1)}, bf16[512,2048]{1,0:T(8,128)(2,1)}, u32[]{:S(2)}) copy-start(bf16[512,2048]{1,0:T(8,128)(2,1)} %refs_4_.3) | copy-start | bytes 6291460
  7.6 1.6 %copy-start.5 = (bf16[128,512]{1,0:T(8,128)(2,1)S(1)}, bf16[128,512]{1,0:T(8,128)(2,1)}, u32[]{:S(2)}) copy-start(bf16[128,512]{1,0:T(8,128)(2,1)} %refs_0_.1) | copy-start | bytes 393220
  7.6 5.3 %collective-permute-start.2 = (bf16[3,128,128]{2,1,0:T(8,128)(2,1)S(1)}, bf16[3,128,128]{2,1,0:T(8,128)(2,1)S(1)}, u32[]{:S(2)}, u32[]{:S(2)}) collective-permute-start(bf16[3,128,128]{2,1,0:T(8,128)(2,1)S(1)} %get-tuple-element.41), channel_id=1, source_target_pairs={{0,4},{4,0},{8,12},{12,8},{16,20},{20,16},{24,28},{28,24},{1,5},{5... | collective-permute-start | bytes 294920 | tf_op jit(solution)/shard_map/ppermute | solution.py:81
  8.1 1.8 %collective-permute-start.5 = (bf16[128,512]{1,0:T(8,128)(2,1)S(1)}, bf16[128,512]{1,0:T(8,128)(2,1)S(1)}, u32[]{:S(2)}, u32[]{:S(2)}) collective-permute-start(bf16[128,512]{1,0:T(8,128)(2,1)S(1)} %collective-permute-done.3.refs_1_), channel_id=1, source_target_pairs={{0,1},{1,0},{2,3},{3,2},{4,5},{5,4},{6,7},{7,6},{8,9},{9,8},{10,11... | collective-permute-start | bytes 393224 | tf_op jit(solution)/shard_map/ppermute | solution.py:81
  9.2 0.9 %copy-start.2 = (bf16[128,512]{1,0:T(8,128)(2,1)S(1)}, bf16[128,512]{1,0:T(8,128)(2,1)}, u32[]{:S(2)}) copy-start(bf16[128,512]{1,0:T(8,128)(2,1)} %refs_3_.5) | copy-start | bytes 393220
  9.2 3.7 %copy-start.1 = (bf16[4,128,256]{2,1,0:T(8,128)(2,1)S(1)}, bf16[4,128,256]{2,1,0:T(8,128)(2,1)}, u32[]{:S(2)}) copy-start(bf16[4,128,256]{2,1,0:T(8,128)(2,1)} %om_ref.3) | copy-start | bytes 786436
  9.2 3.7 %copy-start.3 = (bf16[128,512]{1,0:T(8,128)(2,1)S(1)}, bf16[128,512]{1,0:T(8,128)(2,1)}, u32[]{:S(2)}) copy-start(bf16[128,512]{1,0:T(8,128)(2,1)} %refs_3_.4) | copy-start | bytes 393220
  9.2 3.7 %copy-start.4 = (bf16[128,512]{1,0:T(8,128)(2,1)S(1)}, bf16[128,512]{1,0:T(8,128)(2,1)}, u32[]{:S(2)}) copy-start(bf16[128,512]{1,0:T(8,128)(2,1)} %refs_4_.2) | copy-start | bytes 393220
  10.5 6.7 %collective-permute-start.6 = (bf16[2,128,128]{2,1,0:T(8,128)(2,1)S(1)}, bf16[2,128,128]{2,1,0:T(8,128)(2,1)S(1)}, u32[]{:S(2)}, u32[]{:S(2)}) collective-permute-start(bf16[2,128,128]{2,1,0:T(8,128)(2,1)S(1)} %get-tuple-element.45), channel_id=1, source_target_pairs={{0,12},{4,8},{8,4},{12,0},{16,28},{20,24},{24,20},{28,16},{1,13},{... | collective-permute-start | bytes 196616 | tf_op jit(solution)/shard_map/ppermute | solution.py:81
  12.5 5.0 %collective-permute-start.7 = (bf16[2,128,128]{2,1,0:T(8,128)(2,1)S(1)}, bf16[2,128,128]{2,1,0:T(8,128)(2,1)S(1)}, u32[]{:S(2)}, u32[]{:S(2)}) collective-permute-start(bf16[2,128,128]{2,1,0:T(8,128)(2,1)S(1)} %get-tuple-element.46), channel_id=1, source_target_pairs={{0,8},{4,12},{8,0},{12,4},{16,24},{20,28},{24,16},{28,20},{1,9},{5... | collective-permute-start | bytes 196616 | tf_op jit(solution)/shard_map/ppermute | solution.py:81
  13.4 6.6 %collective-permute-start.9 = (bf16[128,256]{1,0:T(8,128)(2,1)S(1)}, bf16[128,256]{1,0:T(8,128)(2,1)S(1)}, u32[]{:S(2)}, u32[]{:S(2)}) collective-permute-start(bf16[128,256]{1,0:T(8,128)(2,1)S(1)} %get-tuple-element.52), channel_id=1, source_target_pairs={{0,16},{4,20},{8,24},{12,28},{16,0},{20,4},{24,8},{28,12},{1,17},{... | collective-permute-start | bytes 196616 | tf_op jit(solution)/shard_map/ppermute | solution.py:81
  16.1 3.9 %collective-permute-start.8 = (bf16[1,128,128]{2,1,0:T(8,128)(2,1)S(1)}, bf16[1,128,128]{2,1,0:T(8,128)(2,1)S(1)}, u32[]{:S(2)}, u32[]{:S(2)}) collective-permute-start(bf16[1,128,128]{2,1,0:T(8,128)(2,1)S(1)} %get-tuple-element.50), channel_id=1, source_target_pairs={{0,4},{4,0},{8,12},{12,8},{16,20},{20,16},{24,28},{28,24},{1,5},{5... | collective-permute-start | bytes 98312 | tf_op jit(solution)/shard_map/ppermute | solution.py:81
  20.6 5.9 %collective-permute-start.10 = (bf16[128,256]{1,0:T(8,128)(2,1)S(1)}, bf16[128,256]{1,0:T(8,128)(2,1)S(1)}, u32[]{:S(2)}, u32[]{:S(2)}) collective-permute-start(bf16[128,256]{1,0:T(8,128)(2,1)S(1)} %get-tuple-element.58), channel_id=1, source_target_pairs={{0,16},{4,20},{8,24},{12,28},{16,0},{20,4},{24,8},{28,12},{1,17},{... | collective-permute-start | bytes 196616 | tf_op jit(solution)/shard_map/ppermute | solution.py:81
  22.0 7.8 %collective-permute-start.12 = (bf16[128,128]{1,0:T(8,128)(2,1)S(1)}, bf16[128,128]{1,0:T(8,128)(2,1)S(1)}, u32[]{:S(2)}, u32[]{:S(2)}) collective-permute-start(bf16[128,128]{1,0:T(8,128)(2,1)S(1)} %get-tuple-element.60), channel_id=1, source_target_pairs={{0,12},{4,8},{8,4},{12,0},{16,28},{20,24},{24,20},{28,16},{1,13},{... | collective-permute-start | bytes 98312 | tf_op jit(solution)/shard_map/ppermute | solution.py:81
  24.7 5.2 %collective-permute-start.13 = (bf16[128,128]{1,0:T(8,128)(2,1)S(1)}, bf16[128,128]{1,0:T(8,128)(2,1)S(1)}, u32[]{:S(2)}, u32[]{:S(2)}) collective-permute-start(bf16[128,128]{1,0:T(8,128)(2,1)S(1)} %get-tuple-element.61), channel_id=1, source_target_pairs={{0,8},{4,12},{8,0},{12,4},{16,24},{20,28},{24,16},{28,20},{1,9},{5... | collective-permute-start | bytes 98312 | tf_op jit(solution)/shard_map/ppermute | solution.py:81
  24.7 5.2 %collective-permute-start.14 = (bf16[128,128]{1,0:T(8,128)(2,1)S(1)}, bf16[128,128]{1,0:T(8,128)(2,1)S(1)}, u32[]{:S(2)}, u32[]{:S(2)}) collective-permute-start(bf16[128,128]{1,0:T(8,128)(2,1)S(1)} %get-tuple-element.62), channel_id=1, source_target_pairs={{0,4},{4,0},{8,12},{12,8},{16,20},{20,16},{24,28},{28,24},{1,5},{5... | collective-permute-start | bytes 98312 | tf_op jit(solution)/shard_map/ppermute | solution.py:81
  27.2 6.7 %collective-permute-start.17 = (bf16[3,128,128]{2,1,0:T(8,128)(2,1)S(1)}, bf16[3,128,128]{2,1,0:T(8,128)(2,1)S(1)}, u32[]{:S(2)}, u32[]{:S(2)}) collective-permute-start(bf16[3,128,128]{2,1,0:T(8,128)(2,1)S(1)} %get-tuple-element.69), channel_id=1, source_target_pairs={{0,12},{4,8},{8,4},{12,0},{16,28},{20,24},{24,20},{28,16},{1,13},{... | collective-permute-start | bytes 294920 | tf_op jit(solution)/shard_map/ppermute | solution.py:81
  29.8 4.6 %collective-permute-start.18 = (bf16[3,128,128]{2,1,0:T(8,128)(2,1)S(1)}, bf16[3,128,128]{2,1,0:T(8,128)(2,1)S(1)}, u32[]{:S(2)}, u32[]{:S(2)}) collective-permute-start(bf16[3,128,128]{2,1,0:T(8,128)(2,1)S(1)} %get-tuple-element.70), channel_id=1, source_target_pairs={{0,8},{4,12},{8,0},{12,4},{16,24},{20,28},{24,16},{28,20},{1,9},{5... | collective-permute-start | bytes 294920 | tf_op jit(solution)/shard_map/ppermute | solution.py:81
  30.3 1.6 %collective-permute-start.15 = (bf16[2,128,512]{2,1,0:T(8,128)(2,1)S(1)}, bf16[2,128,512]{2,1,0:T(8,128)(2,1)S(1)}, u32[]{:S(2)}, u32[]{:S(2)}) collective-permute-start(bf16[2,128,512]{2,1,0:T(8,128)(2,1)S(1)} %get-tuple-element.66), channel_id=1, source_target_pairs={{0,1},{1,0},{2,3},{3,2},{4,5},{5,4},{6,7},{7,6},{8,9},{9,8},{10,11... | collective-permute-start | bytes 786440 | tf_op jit(solution)/shard_map/ppermute | solution.py:81
  32.0 5.6 %collective-permute-start.16 = (bf16[1,128,512]{2,1,0:T(8,128)(2,1)S(1)}, bf16[1,128,512]{2,1,0:T(8,128)(2,1)S(1)}, u32[]{:S(2)}, u32[]{:S(2)}) collective-permute-start(bf16[1,128,512]{2,1,0:T(8,128)(2,1)S(1)} %get-tuple-element.68), channel_id=1, source_target_pairs={{0,2},{1,3},{2,0},{3,1},{4,6},{5,7},{6,4},{7,5},{8,10},{9,11},{10,... | collective-permute-start | bytes 393224 | tf_op jit(solution)/shard_map/ppermute | solution.py:81
  32.6 4.6 %collective-permute-start.11 = (bf16[3,128,128]{2,1,0:T(8,128)(2,1)S(1)}, bf16[3,128,128]{2,1,0:T(8,128)(2,1)S(1)}, u32[]{:S(2)}, u32[]{:S(2)}) collective-permute-start(bf16[3,128,128]{2,1,0:T(8,128)(2,1)S(1)} %get-tuple-element.59), channel_id=1, source_target_pairs={{0,4},{4,0},{8,12},{12,8},{16,20},{20,16},{24,28},{28,24},{1,5},{5... | collective-permute-start | bytes 294920 | tf_op jit(solution)/shard_map/ppermute | solution.py:81

commit v19 on v17

--- a/solution.py
+++ b/solution.py
@@ -85,31 +85,27 @@
     return [1 << b for b in range(size.bit_length() - 1)]
 
 
-def sum_kernel(own_ref, *refs):
-    got, (kept_ref, sent_ref) = refs[:-2], refs[-2:]
-    rows = got[0].shape[1]
-    for i, ref in enumerate(got):
-        at = slice(i * rows, (i + 1) * rows)
-        for j in range(kept_ref.shape[0]):
-            kept_ref[j, at, :] = own_ref[2 * j, at, :].astype(jnp.float32) + ref[
-                2 * j
-            ].astype(jnp.float32)
-            sent_ref[j, at, :] = bf(
-                own_ref[2 * j + 1, at, :].astype(jnp.float32)
-                + ref[2 * j + 1].astype(jnp.float32)
-            )
-
-
-def reduce_blocks(own, sent, bits):
-    half = struct((own.shape[0] // 2,) + own.shape[1:])
-    got = [swap(x, "head", bits[0]) for x in sent]
-    own, sent = call(sum_kernel, [struct(half.shape, jnp.float32), half], own, *got)
-    got = swap(sent, "head", bits[1])
-    for bit in bits[2:]:
-        total = own + got.astype(jnp.float32)
-        pairs = total.reshape((total.shape[0] // 2, 2) + total.shape[1:])
-        own, got = pairs[:, 0], swap(bf(pairs[:, 1]), "head", bit)
-    return own[0], got[0]
+def sum_kernel(*refs):
+    out_ref = refs[-1]
+    out_ref[...] = bf(sum(ref[...].astype(jnp.float32) for ref in refs[:-2]))
+
+
+def reduce_blocks(parts, bits):
+    held = {o: [part] for o, part in enumerate(parts)}
+    for bit in bits:
+        for o in reversed(range(bit, len(parts), 2 * bit)):
+            block = held[o][0]
+            if bit > 1:
+                (mark,) = call(
+                    mark_kernel, [struct((8, 128), jnp.float32)], block, specs=[ANY],
+                    flops=28 * 10**8,
+                )
+                (block,) = call(
+                    sum_kernel, [struct(block.shape)], *held[o], mark,
+                    specs=[VMEM] * len(held[o]) + [ANY],
+                )
+            held[o ^ bit].append(swap(block, "head", bit))
+    return held[0]
 
 
 def member(n):
@@ -297,23 +293,16 @@
         outs[k][2] = gv_scr[at, :]
 
 
-def mixed_project_kernel(n, offsets, *refs):
-    mixed_in, (w_ref, _, own_ref, *sent, scr) = refs[:n][::-1], refs[n:]
+def mixed_project_kernel(n, *refs):
+    mixed_in, (w_ref, _, *outs, scr) = refs[:n][::-1], refs[n:]
     r, h = member(n), lax.axis_index("head")
-    width = own_ref.shape[2]
+    width = outs[0].shape[1]
     dim = mixed_in[0].shape[1]
-    half = len(offsets) // 2
     for k in range(n):
         scr[:, lane(r ^ k, dim)] = mixed_in[k][...]
     mixed = scr[...]
-    for at, offset in enumerate(offsets):
-        part = bf(mm(mixed, w_ref[:, lane(h ^ offset, width)]))
-        if at < half:
-            own_ref[at] = part
-        else:
-            step = sent[0].shape[1]
-            for i, ref in enumerate(sent):
-                ref[at - half] = part[i * step : (i + 1) * step]
+    for offset in reversed(range(len(outs))):
+        outs[offset][...] = bf(mm(mixed, w_ref[:, lane(h ^ offset, width)]))
 
 
 def unpack_kernel(ks, n, *refs):
@@ -331,8 +320,8 @@
         copy.wait()
 
 
-def last_kernel(n, got_ref, part_ref, last_ref, *refs):
-    (out_ref, *outs), (scr, sems) = refs[3:-2], refs[-2:]
+def last_kernel(n, got_ref, *refs):
+    parts, (out_ref, *outs), (scr, sems) = refs[:-9], refs[-6:-2], refs[-2:]
     r = member(n)
     dim = got_ref.shape[2]
     copies = [
@@ -341,7 +330,7 @@
     ]
     for copy in copies:
         copy.start()
-    scr[...] = bf(part_ref[...] + last_ref[...].astype(jnp.float32))
+    scr[...] = bf(sum(ref[...].astype(jnp.float32) for ref in parts))
     copies.append(pltpu.make_async_copy(scr, out_ref, sems.at[3]))
     copies[-1].start()
     for copy in copies:
@@ -425,30 +414,28 @@
     )
     grads_in = exchange(grads[1:]) + [grads[0]]
 
-    order = [o for o in range(split) if not o & 1] + [o for o in range(split) if o & 1]
-    own, *sent = call(
-        functools.partial(mixed_project_kernel, n, order),
-        [struct((split // 2, rows, width))]
-        + [struct((split // 2, rows, width))],
+    parts = call(
+        functools.partial(mixed_project_kernel, n),
+        [struct((rows, width))] * split,
         *mixed_in, out_weight, grads[0], flops=2 * rows * out_weight.size,
         specs=[VMEM] * (n + 1) + [ANY],
         scratch=[pltpu.VMEM((rows, n * dim), jnp.bfloat16)],
     )
-    part, last = reduce_blocks(own, sent, bits)
+    kept = reduce_blocks(parts, bits)
     *early, late, own_grads = grads_in
     ks = [k for k in range(n - 1, 1, -1)] + [0]
     arrays = [struct((rows, n * dim))] * 3
     partial_grads = call(
         functools.partial(unpack_kernel, ks, n), arrays,
-        *early, own_grads, flops=6 * 10**8,
+        *early, own_grads, flops=8 * 10**8,
         out_specs=[ANY] * 3, scratch=[pltpu.SemaphoreType.DMA((n - 1, 3))],
     )
     return call(
         functools.partial(last_kernel, n),
         [struct((rows, width))] + arrays,
-        late, part, last, *partial_grads,
-        specs=[VMEM] * 3 + [ANY] * 3, out_specs=[ANY] * 4,
-        aliases={3: 1, 4: 2, 5: 3},
+        late, *kept, *partial_grads,
+        specs=[VMEM] * (1 + len(kept)) + [ANY] * 3, out_specs=[ANY] * 4,
+        aliases={1 + len(kept) + i: 1 + i for i in range(3)},
         scratch=[pltpu.VMEM((rows, width), jnp.bfloat16), pltpu.SemaphoreType.DMA((4,))],
     )
 

time: 38.6 us -> 38.3 us (level)
  waiting for transfers between devices: 7.14 us -> 6.02 us
  starting transfers between devices: 22 us -> 22.9 us
    ppermute x19 -> x20, waiting for transfers between devices: 7.14 us -> 6.02 us  [swap(): return lax.ppermute(array, axis, [(i, i ^ bit) for i in range(size)])]
    ppermute x19 -> x20, starting transfers between devices: 22 us -> 22.9 us  [swap(): return lax.ppermute(array, axis, [(i, i ^ bit) for i in range(size)])]
    pallas_call x13 -> x14, Pallas kernels: 7.14 us -> 7.12 us  [call(): pl.pallas_call(body, out_shape=outs, in_specs=specs or [VMEM] * len(args)...]
  transfers between devices with their start and end apart: 19 -> 20, of which waited for: 5 -> 6; matrix products, arithmetic and copies ran while one was open for 0% -> 0% of each run, Pallas kernels for 14% -> 15%
where the time goes in v19:
time: 38.3 us; the launch traced here: 38.1 us
  starting transfers between devices  22.9 us (60%)
  Pallas kernels  7.12 us (19%)
  waiting for transfers between devices  6.02 us (16%)
  local copies, waits for them, and re-layouts  1.29 us (3%)
  between operations  0.82 us (2%)
    ppermute x20, starting transfers between devices, swap(): return lax.ppermute(array, axis, [(i, i ^ bit) for i in range(size)])  22.9 us
    pallas_call x14, Pallas kernels, call(): pl.pallas_call(body, out_shape=outs, in_specs=specs or [VMEM] * len(args)...  7.12 us
    ppermute x20, waiting for transfers between devices, swap(): return lax.ppermute(array, axis, [(i, i ^ bit) for i in range(size)])  6.02 us
    unnamed x12, local copies, waits for them, and re-layouts  1.29 us
  transfers between devices with their start and end apart: 20, of which 6 were waited for; matrix products, arithmetic and copies ran while one was open for 0% of the time, Pallas kernels for 15%

profile of v19, /device:TPU:0, one launch (start us, length us, event | category | flops | bytes accessed | tf_op | source)
XLA Modules:
  0.0 38.1 jit_solution(8598388692033423854)
XLA Ops:
  0.6 3.0 %collective-permute-start.3 = (bf16[128,512]{1,0:T(8,128)(2,1)}, bf16[128,512]{1,0:T(8,128)(2,1)S(1)}, u32[]{:S(2)}, u32[]{:S(2)}) collective-permute-start(bf16[128,512]{1,0:T(8,128)(2,1)} %refs_0_.1), channel_id=1, source_target_pairs={{0,2},{1,3},{2,0},{3,1},{4,6},{5,7},{6,4},{7,5},{8,10},{9,11},{10,... | collective-permute-start | bytes 393224 | tf_op jit(solution)/shard_map/ppermute | solution.py:81
  3.6 0.0 collective-permute-start.4
  3.6 0.9 %shard_map.93 = (bf16[3,128,128]{2,1,0:T(8,128)(2,1)S(1)}, bf16[2,128,128]{2,1,0:T(8,128)(2,1)S(1)}, bf16[2,128,128]{2,1,0:T(8,128)(2,1)S(1)}) custom-call(bf16[128,512]{1,0:T(8,128)(2,1)} %refs_3_.5, bf16[128,512]{1,0:T(8,128)(2,1)} %refs_3_.4, bf16[128,512]{1,0:T(8,128)(2,1)} %refs_4_.2), custom_call_target="tpu_custom_call" | custom-call | bytes 622592 | tf_op jit(solution)/shard_map/pallas_call | solution.py:29
  4.6 2.6 %collective-permute-start = (bf16[2,128,128]{2,1,0:T(8,128)(2,1)S(1)}, bf16[2,128,128]{2,1,0:T(8,128)(2,1)S(1)}, u32[]{:S(2)}, u32[]{:S(2)}) collective-permute-start(bf16[2,128,128]{2,1,0:T(8,128)(2,1)S(1)} %get-tuple-element.39), channel_id=1, source_target_pairs={{0,12},{4,8},{8,4},{12,0},{16,28},{20,24},{24,20},{28,16},{1,13},{... | collective-permute-start | bytes 196616 | tf_op jit(solution)/shard_map/ppermute | solution.py:81
  7.2 0.4 %collective-permute-start.1 = (bf16[2,128,128]{2,1,0:T(8,128)(2,1)S(1)}, bf16[2,128,128]{2,1,0:T(8,128)(2,1)S(1)}, u32[]{:S(2)}, u32[]{:S(2)}) collective-permute-start(bf16[2,128,128]{2,1,0:T(8,128)(2,1)S(1)} %get-tuple-element.40), channel_id=1, source_target_pairs={{0,8},{4,12},{8,0},{12,4},{16,24},{20,28},{24,16},{28,20},{1,9},{5... | collective-permute-start | bytes 196616 | tf_op jit(solution)/shard_map/ppermute | solution.py:81
  7.6 0.5 %collective-permute-start.2 = (bf16[3,128,128]{2,1,0:T(8,128)(2,1)S(1)}, bf16[3,128,128]{2,1,0:T(8,128)(2,1)S(1)}, u32[]{:S(2)}, u32[]{:S(2)}) collective-permute-start(bf16[3,128,128]{2,1,0:T(8,128)(2,1)S(1)} %get-tuple-element.41), channel_id=1, source_target_pairs={{0,4},{4,0},{8,12},{12,8},{16,20},{20,16},{24,28},{28,24},{1,5},{5... | collective-permute-start | bytes 294920 | tf_op jit(solution)/shard_map/ppermute | solution.py:81
  8.1 0.0 collective-permute-done.3.refs_1_
  8.1 0.0 collective-permute-start.5
  8.1 0.0 collective-permute-done.4._.refs_2_
  8.2 1.1 %copy-done = bf16[512,2048]{1,0:T(8,128)(2,1)S(1)} copy-done((bf16[512,2048]{1,0:T(8,128)(2,1)S(1)}, bf16[512,2048]{1,0:T(8,128)(2,1)}, u32[]{:S(2)}) %copy-start) | copy-done | bytes 2097176
  9.2 0.0 copy-start.4
  9.2 0.7 %shard_map.95.total_ref = f32[128,512]{1,0:T(8,128)S(1)} custom-call(bf16[128,512]{1,0:T(8,128)(2,1)S(1)} %copy-done.5, bf16[128,512]{1,0:T(8,128)(2,1)S(1)} %collective-permute-done.3.refs_1_, bf16[128,512]{1,0:T(8,128)(2,1)S(1)} %collective-permute-done.4._.refs_2_, bf16[512,2048]{1,0:T(8,128)(2,1)S(1)} %copy-done, f32[8,128]{1,0:T(8,128)S(1)} %shard_map.94.refs_4_), custom_call_target="tpu_custom_call" | custom-call | flops 268435456 | bytes 2756608 | tf_op jit(solution)/shard_map/pallas_call | solution.py:29
  9.9 0.0 collective-permute-done.5.block_ref
  9.9 0.2 copy-done.2
  10.1 0.4 shard_map.96
  10.5 2.0 %collective-permute-start.6 = (bf16[2,128,128]{2,1,0:T(8,128)(2,1)S(1)}, bf16[2,128,128]{2,1,0:T(8,128)(2,1)S(1)}, u32[]{:S(2)}, u32[]{:S(2)}) collective-permute-start(bf16[2,128,128]{2,1,0:T(8,128)(2,1)S(1)} %get-tuple-element.45), channel_id=1, source_target_pairs={{0,12},{4,8},{8,4},{12,0},{16,28},{20,24},{24,20},{28,16},{1,13},{... | collective-permute-start | bytes 196616 | tf_op jit(solution)/shard_map/ppermute | solution.py:81
  12.5 0.4 %collective-permute-start.7 = (bf16[2,128,128]{2,1,0:T(8,128)(2,1)S(1)}, bf16[2,128,128]{2,1,0:T(8,128)(2,1)S(1)}, u32[]{:S(2)}, u32[]{:S(2)}) collective-permute-start(bf16[2,128,128]{2,1,0:T(8,128)(2,1)S(1)} %get-tuple-element.46), channel_id=1, source_target_pairs={{0,8},{4,12},{8,0},{12,4},{16,24},{20,28},{24,16},{28,20},{1,9},{5... | collective-permute-start | bytes 196616 | tf_op jit(solution)/shard_map/ppermute | solution.py:81
  12.9 0.0 collective-permute-done.1.refs_1_
  12.9 0.0 collective-permute-done.2.refs_2_.refs_4_
  13.0 0.5 %shard_map.97 = (bf16[2,512,128]{2,1,0:T(8,128)(2,1)S(1)}, bf16[512,256]{1,0:T(8,128)(2,1)S(1)}, bf16[128,256]{1,0:T(8,128)(2,1)S(1)}) custom-call(bf16[2,128,128]{2,1,0:T(8,128)(2,1)S(1)} %collective-permute-done.refs_0_, bf16[2,128,128]{2,1,0:T(8,128)(2,1)S(1)} %collective-permute-done.1.refs_1_, ...), custom_call_target="tpu_custom_call" | custom-call | flops 67108864 | bytes 1376256 | tf_op jit(solution)/shard_map/pallas_call | solution.py:29
  13.4 2.7 %collective-permute-start.9 = (bf16[128,256]{1,0:T(8,128)(2,1)S(1)}, bf16[128,256]{1,0:T(8,128)(2,1)S(1)}, u32[]{:S(2)}, u32[]{:S(2)}) collective-permute-start(bf16[128,256]{1,0:T(8,128)(2,1)S(1)} %get-tuple-element.52), channel_id=1, source_target_pairs={{0,16},{4,20},{8,24},{12,28},{16,0},{20,4},{24,8},{28,12},{1,17},{... | collective-permute-start | bytes 196616 | tf_op jit(solution)/shard_map/ppermute | solution.py:81
  16.1 1.1 %collective-permute-start.8 = (bf16[1,128,128]{2,1,0:T(8,128)(2,1)S(1)}, bf16[1,128,128]{2,1,0:T(8,128)(2,1)S(1)}, u32[]{:S(2)}, u32[]{:S(2)}) collective-permute-start(bf16[1,128,128]{2,1,0:T(8,128)(2,1)S(1)} %get-tuple-element.50), channel_id=1, source_target_pairs={{0,4},{4,0},{8,12},{12,8},{16,20},{20,16},{24,28},{28,24},{1,5},{5... | collective-permute-start | bytes 98312 | tf_op jit(solution)/shard_map/ppermute | solution.py:81
  17.2 0.2 collective-permute-done.7.refs_1_
  17.4 0.5 %shard_map.98 = (bf16[512,128]{1,0:T(8,128)(2,1)S(1)}, bf16[512,256]{1,0:T(8,128)(2,1)S(1)}, bf16[512,512]{1,0:T(8,128)(2,1)S(1)}, f32[512,128]{1,0:T(8,128)S(1)}) custom-call(bf16[2,128,128]{2,1,0:T(8,128)(2,1)S(1)} %collective-permute-done.6.refs_0_, bf16[2,128,128]{2,1,0:T(8,128)(2,1)S(1)} %collective-permute-done.7.refs_1_, ...), custom_call_target="tpu_custom_call" | custom-call | flops 536870912 | bytes 2359296 | tf_op jit(solution)/shard_map/pallas_call | solution.py:29
  18.0 2.0 %collective-permute-done.8.refs_1_ = bf16[1,128,128]{2,1,0:T(8,128)(2,1)S(1)} collective-permute-done((bf16[1,128,128]{2,1,0:T(8,128)(2,1)S(1)}, bf16[1,128,128]{2,1,0:T(8,128)(2,1)S(1)}, u32[]{:S(2)}, u32[]{:S(2)}) %collective-permute-start.8) | collective-permute-done | bytes 32800 | tf_op jit(solution)/shard_map/ppermute | solution.py:81
  20.0 0.0 collective-permute-done.9.refs_4_
  20.0 0.6 %shard_map.99 = (bf16[128,256]{1,0:T(8,128)(2,1)S(1)}, bf16[512,128]{1,0:T(8,128)(2,1)S(1)}, bf16[128,256]{1,0:T(8,128)(2,1)S(1)}, bf16[128,128]{1,0:T(8,128)(2,...) custom-call(bf16[512,128]{1,0:T(8,128)(2,1)S(1)} %get-tuple-element.49.refs_0_, ...), custom_call_target="tpu_custom_call" | custom-call | flops 67108864 | bytes 1146880 | tf_op jit(solution)/shard_map/pallas_call | solution.py:29
  20.6 1.4 %collective-permute-start.10 = (bf16[128,256]{1,0:T(8,128)(2,1)S(1)}, bf16[128,256]{1,0:T(8,128)(2,1)S(1)}, u32[]{:S(2)}, u32[]{:S(2)}) collective-permute-start(bf16[128,256]{1,0:T(8,128)(2,1)S(1)} %get-tuple-element.58), channel_id=1, source_target_pairs={{0,16},{4,20},{8,24},{12,28},{16,0},{20,4},{24,8},{28,12},{1,17},{... | collective-permute-start | bytes 196616 | tf_op jit(solution)/shard_map/ppermute | solution.py:81
  22.0 2.7 %collective-permute-start.12 = (bf16[128,128]{1,0:T(8,128)(2,1)S(1)}, bf16[128,128]{1,0:T(8,128)(2,1)S(1)}, u32[]{:S(2)}, u32[]{:S(2)}) collective-permute-start(bf16[128,128]{1,0:T(8,128)(2,1)S(1)} %get-tuple-element.60), channel_id=1, source_target_pairs={{0,12},{4,8},{8,4},{12,0},{16,28},{20,24},{24,20},{28,16},{1,13},{... | collective-permute-start | bytes 98312 | tf_op jit(solution)/shard_map/ppermute | solution.py:81
  24.7 0.9 %collective-permute-start.14 = (bf16[128,128]{1,0:T(8,128)(2,1)S(1)}, bf16[128,128]{1,0:T(8,128)(2,1)S(1)}, u32[]{:S(2)}, u32[]{:S(2)}) collective-permute-start(bf16[128,128]{1,0:T(8,128)(2,1)S(1)} %get-tuple-element.62), channel_id=1, source_target_pairs={{0,4},{4,0},{8,12},{12,8},{16,20},{20,16},{24,28},{28,24},{1,5},{5... | collective-permute-start | bytes 98312 | tf_op jit(solution)/shard_map/ppermute | solution.py:81
  25.6 1.0 %shard_map.100 = (bf16[512,128]{1,0:T(8,128)(2,1)S(1)}, f32[512,128]{1,0:T(8,128)S(1)}, f32[512,256]{1,0:T(8,128)S(1)}) custom-call(bf16[2,512,128]{2,1,0:T(8,128)(2,1)S(1)} %get-tuple-element.43.refs_5_.kv_ref, bf16[4,128,256]{2,1,0:T(8,128)(2,1)S(1)} %copy-done.1, bf16[512,256]{1,0:T(8,128)(2,1)S(1)} %get-tuple-element.44.refs_7_.kf_ref, ...), custom_call_target="tpu_custom_call" | custom-call | flops 268435456 | bytes 2686976 | tf_op jit(solution)/shard_map/pallas_call | solution.py:29
  26.6 0.0 collective-permute-done.10.rest_0_
  26.6 0.6 %shard_map.101 = (bf16[3,128,128]{2,1,0:T(8,128)(2,1)S(1)}, bf16[3,128,128]{2,1,0:T(8,128)(2,1)S(1)}, bf16[3,128,128]{2,1,0:T(8,128)(2,1)S(1)}, bf16[3,128,128]{2,1,0:T(8,128)(2,1)S(1)}) custom-call(bf16[2,512,128]{2,1,0:T(8,128)(2,1)S(1)} %get-tuple-element.43.refs_5_.kv_ref, bf16[4,128,256]{2,1,0:T(8,128)(2,1)S(1)} %copy-done.1, ...), custom_call_target="tpu_custom_call" | custom-call | flops 100663296 | bytes 2162688 | tf_op jit(solution)/shard_map/pallas_call | solution.py:29
  27.2 2.7 %collective-permute-start.18 = (bf16[3,128,128]{2,1,0:T(8,128)(2,1)S(1)}, bf16[3,128,128]{2,1,0:T(8,128)(2,1)S(1)}, u32[]{:S(2)}, u32[]{:S(2)}) collective-permute-start(bf16[3,128,128]{2,1,0:T(8,128)(2,1)S(1)} %get-tuple-element.69), channel_id=1, source_target_pairs={{0,12},{4,8},{8,4},{12,0},{16,28},{20,24},{24,20},{28,16},{1,13},{... | collective-permute-start | bytes 294920 | tf_op jit(solution)/shard_map/ppermute | solution.py:81
  29.8 0.0 collective-permute-done.14.refs_2_
  29.8 0.5 %shard_map.102 = (bf16[128,512]{1,0:T(8,128)(2,1)S(1)}, bf16[128,512]{1,0:T(8,128)(2,1)S(1)}, bf16[128,512]{1,0:T(8,128)(2,1)S(1)}, bf16[128,512]{1,0:T(8,128)(2,1)S(1)}) custom-call(bf16[128,128]{1,0:T(8,128)(2,1)S(1)} %collective-permute-done.12.refs_0_, bf16[128,128]{1,0:T(8,128)(2,1)S(1)} %collective-permute-done.13.refs_1_, ...), custom_call_target="tpu_custom_call" | custom-call | flops 268435456 | bytes 2850816 | tf_op jit(solution)/shard_map/pallas_call | solution.py:29
  30.3 0.1 collective-permute-start.16
  30.4 0.5 %collective-permute-start.15 = (bf16[128,512]{1,0:T(8,128)(2,1)S(1)}, bf16[128,512]{1,0:T(8,128)(2,1)S(1)}, u32[]{:S(2)}, u32[]{:S(2)}) collective-permute-start(bf16[128,512]{1,0:T(8,128)(2,1)S(1)} %get-tuple-element.66), channel_id=1, source_target_pairs={{0,1},{1,0},{2,3},{3,2},{4,5},{5,4},{6,7},{7,6},{8,9},{9,8},{10,11... | collective-permute-start | bytes 393224 | tf_op jit(solution)/shard_map/ppermute | solution.py:81
  30.9 0.8 %collective-permute-done.16.refs_1_ = bf16[128,512]{1,0:T(8,128)(2,1)S(1)} collective-permute-done((bf16[128,512]{1,0:T(8,128)(2,1)S(1)}, bf16[128,512]{1,0:T(8,128)(2,1)S(1)}, u32[]{:S(2)}, u32[]{:S(2)}) %collective-permute-start.16) | collective-permute-done | bytes 131104 | tf_op jit(solution)/shard_map/ppermute | solution.py:81
  31.7 0.6 %collective-permute-start.17 = (bf16[128,512]{1,0:T(8,128)(2,1)S(1)}, bf16[128,512]{1,0:T(8,128)(2,1)S(1)}, u32[]{:S(2)}, u32[]{:S(2)}) collective-permute-start(bf16[128,512]{1,0:T(8,128)(2,1)S(1)} %shard_map.104), channel_id=1, source_target_pairs={{0,2},{1,3},{2,0},{3,1},{4,6},{5,7},{6,4},{7,5},{8,10},{9,11},{10,... | collective-permute-start | bytes 393224 | tf_op jit(solution)/shard_map/ppermute | solution.py:81
  32.3 1.3 %collective-permute-start.11 = (bf16[3,128,128]{2,1,0:T(8,128)(2,1)S(1)}, bf16[3,128,128]{2,1,0:T(8,128)(2,1)S(1)}, u32[]{:S(2)}, u32[]{:S(2)}) collective-permute-start(bf16[3,128,128]{2,1,0:T(8,128)(2,1)S(1)} %get-tuple-element.59), channel_id=1, source_target_pairs={{0,4},{4,0},{8,12},{12,8},{16,20},{20,16},{24,28},{28,24},{1,5},{5... | collective-permute-start | bytes 294920 | tf_op jit(solution)/shard_map/ppermute | solution.py:81
  33.7 0.0 collective-permute-done.18.refs_0_
  33.7 0.8 %collective-permute-done.19.refs_1_ = bf16[3,128,128]{2,1,0:T(8,128)(2,1)S(1)} collective-permute-done((bf16[3,128,128]{2,1,0:T(8,128)(2,1)S(1)}, bf16[3,128,128]{2,1,0:T(8,128)(2,1)S(1)}, u32[]{:S(2)}, u32[]{:S(2)}) %collective-permute-start.19) | collective-permute-done | bytes 98336 | tf_op jit(solution)/shard_map/ppermute | solution.py:81
  34.4 0.8 %shard_map.105 = (bf16[128,512]{1,0:T(8,128)(2,1)}, bf16[128,512]{1,0:T(8,128)(2,1)}, bf16[128,512]{1,0:T(8,128)(2,1)}) custom-call(bf16[3,128,128]{2,1,0:T(8,128)(2,1)S(1)} %collective-permute-done.18.refs_0_, bf16[3,128,128]{2,1,0:T(8,128)(2,1)S(1)} %collective-permute-done.19.refs_1_, bf16[3,128,128]{2,1,0:T(8,128)(2,1)S(1)} %get-tuple-element.64.refs_5_.refs_2_), custom_call_target="tpu_custom_call" | custom-call | flops 800000000 | bytes 688128 | tf_op jit(solution)/shard_map/pallas_call | solution.py:29
  35.2 1.8 %collective-permute-done.11.got_ref = bf16[3,128,128]{2,1,0:T(8,128)(2,1)S(1)} collective-permute-done((bf16[3,128,128]{2,1,0:T(8,128)(2,1)S(1)}, bf16[3,128,128]{2,1,0:T(8,128)(2,1)S(1)}, u32[]{:S(2)}, u32[]{:S(2)}) %collective-permute-start.11) | collective-permute-done | bytes 98336 | tf_op jit(solution)/shard_map/ppermute | solution.py:81
  37.0 0.0 collective-permute-done.15.refs_1_
  37.0 0.4 %collective-permute-done.17.refs_2_ = bf16[128,512]{1,0:T(8,128)(2,1)S(1)} collective-permute-done((bf16[128,512]{1,0:T(8,128)(2,1)S(1)}, bf16[128,512]{1,0:T(8,128)(2,1)S(1)}, u32[]{:S(2)}, u32[]{:S(2)}) %collective-permute-start.17) | collective-permute-done | bytes 131104 | tf_op jit(solution)/shard_map/ppermute | solution.py:81
  37.4 0.7 %shard_map.106 = (bf16[128,512]{1,0:T(8,128)(2,1)}, bf16[128,512]{1,0:T(8,128)(2,1)}, bf16[128,512]{1,0:T(8,128)(2,1)}, bf16[128,512]{1,0:T(8,128)(2,1)}) custom-call(bf16[3,128,128]{2,1,0:T(8,128)(2,1)S(1)} %collective-permute-done.11.got_ref, ...), custom_call_target="tpu_custom_call", output_to_operand_aliasing={{1}: (4, {}), {2}: (5, {}), {3}: (6, {})} | custom-call | bytes 1409024 | tf_op jit(solution)/shard_map/pallas_call | solution.py:29
  (18 shorter events, 0.1 us)
Async XLA Ops:
  0.6 7.5 %collective-permute-start.3 = (bf16[128,512]{1,0:T(8,128)(2,1)}, bf16[128,512]{1,0:T(8,128)(2,1)S(1)}, u32[]{:S(2)}, u32[]{:S(2)}) collective-permute-start(bf16[128,512]{1,0:T(8,128)(2,1)} %refs_0_.1), channel_id=1, source_target_pairs={{0,2},{1,3},{2,0},{3,1},{4,6},{5,7},{6,4},{7,5},{8,10},{9,11},{10,... | collective-permute-start | bytes 393224 | tf_op jit(solution)/shard_map/ppermute | solution.py:81
  3.6 4.5 %collective-permute-start.4 = (bf16[128,512]{1,0:T(8,128)(2,1)}, bf16[128,512]{1,0:T(8,128)(2,1)S(1)}, u32[]{:S(2)}, u32[]{:S(2)}) collective-permute-start(bf16[128,512]{1,0:T(8,128)(2,1)} %refs_0_.1), channel_id=1, source_target_pairs={{0,1},{1,0},{2,3},{3,2},{4,5},{5,4},{6,7},{7,6},{8,9},{9,8},{10,11... | collective-permute-start | bytes 393224 | tf_op jit(solution)/shard_map/ppermute | solution.py:81
  4.6 8.3 %collective-permute-start = (bf16[2,128,128]{2,1,0:T(8,128)(2,1)S(1)}, bf16[2,128,128]{2,1,0:T(8,128)(2,1)S(1)}, u32[]{:S(2)}, u32[]{:S(2)}) collective-permute-start(bf16[2,128,128]{2,1,0:T(8,128)(2,1)S(1)} %get-tuple-element.39), channel_id=1, source_target_pairs={{0,12},{4,8},{8,4},{12,0},{16,28},{20,24},{24,20},{28,16},{1,13},{... | collective-permute-start | bytes 196616 | tf_op jit(solution)/shard_map/ppermute | solution.py:81
  7.2 5.7 %collective-permute-start.1 = (bf16[2,128,128]{2,1,0:T(8,128)(2,1)S(1)}, bf16[2,128,128]{2,1,0:T(8,128)(2,1)S(1)}, u32[]{:S(2)}, u32[]{:S(2)}) collective-permute-start(bf16[2,128,128]{2,1,0:T(8,128)(2,1)S(1)} %get-tuple-element.40), channel_id=1, source_target_pairs={{0,8},{4,12},{8,0},{12,4},{16,24},{20,28},{24,16},{28,20},{1,9},{5... | collective-permute-start | bytes 196616 | tf_op jit(solution)/shard_map/ppermute | solution.py:81
  7.6 1.6 %copy-start = (bf16[512,2048]{1,0:T(8,128)(2,1)S(1)}, bf16[512,2048]{1,0:T(8,128)(2,1)}, u32[]{:S(2)}) copy-start(bf16[512,2048]{1,0:T(8,128)(2,1)} %refs_4_.3) | copy-start | bytes 6291460
  7.6 1.6 %copy-start.5 = (bf16[128,512]{1,0:T(8,128)(2,1)S(1)}, bf16[128,512]{1,0:T(8,128)(2,1)}, u32[]{:S(2)}) copy-start(bf16[128,512]{1,0:T(8,128)(2,1)} %refs_0_.1) | copy-start | bytes 393220
  7.6 5.3 %collective-permute-start.2 = (bf16[3,128,128]{2,1,0:T(8,128)(2,1)S(1)}, bf16[3,128,128]{2,1,0:T(8,128)(2,1)S(1)}, u32[]{:S(2)}, u32[]{:S(2)}) collective-permute-start(bf16[3,128,128]{2,1,0:T(8,128)(2,1)S(1)} %get-tuple-element.41), channel_id=1, source_target_pairs={{0,4},{4,0},{8,12},{12,8},{16,20},{20,16},{24,28},{28,24},{1,5},{5... | collective-permute-start | bytes 294920 | tf_op jit(solution)/shard_map/ppermute | solution.py:81
  8.1 1.8 %collective-permute-start.5 = (bf16[128,512]{1,0:T(8,128)(2,1)S(1)}, bf16[128,512]{1,0:T(8,128)(2,1)S(1)}, u32[]{:S(2)}, u32[]{:S(2)}) collective-permute-start(bf16[128,512]{1,0:T(8,128)(2,1)S(1)} %collective-permute-done.3.refs_1_), channel_id=1, source_target_pairs={{0,1},{1,0},{2,3},{3,2},{4,5},{5,4},{6,7},{7,6},{8,9},{9,8},{10,11... | collective-permute-start | bytes 393224 | tf_op jit(solution)/shard_map/ppermute | solution.py:81
  9.2 0.9 %copy-start.2 = (bf16[128,512]{1,0:T(8,128)(2,1)S(1)}, bf16[128,512]{1,0:T(8,128)(2,1)}, u32[]{:S(2)}) copy-start(bf16[128,512]{1,0:T(8,128)(2,1)} %refs_3_.5) | copy-start | bytes 393220
  9.2 3.7 %copy-start.1 = (bf16[4,128,256]{2,1,0:T(8,128)(2,1)S(1)}, bf16[4,128,256]{2,1,0:T(8,128)(2,1)}, u32[]{:S(2)}) copy-start(bf16[4,128,256]{2,1,0:T(8,128)(2,1)} %om_ref.3) | copy-start | bytes 786436
  9.2 3.7 %copy-start.3 = (bf16[128,512]{1,0:T(8,128)(2,1)S(1)}, bf16[128,512]{1,0:T(8,128)(2,1)}, u32[]{:S(2)}) copy-start(bf16[128,512]{1,0:T(8,128)(2,1)} %refs_3_.4) | copy-start | bytes 393220
  9.2 3.7 %copy-start.4 = (bf16[128,512]{1,0:T(8,128)(2,1)S(1)}, bf16[128,512]{1,0:T(8,128)(2,1)}, u32[]{:S(2)}) copy-start(bf16[128,512]{1,0:T(8,128)(2,1)} %refs_4_.2) | copy-start | bytes 393220
  10.5 6.7 %collective-permute-start.6 = (bf16[2,128,128]{2,1,0:T(8,128)(2,1)S(1)}, bf16[2,128,128]{2,1,0:T(8,128)(2,1)S(1)}, u32[]{:S(2)}, u32[]{:S(2)}) collective-permute-start(bf16[2,128,128]{2,1,0:T(8,128)(2,1)S(1)} %get-tuple-element.45), channel_id=1, source_target_pairs={{0,12},{4,8},{8,4},{12,0},{16,28},{20,24},{24,20},{28,16},{1,13},{... | collective-permute-start | bytes 196616 | tf_op jit(solution)/shard_map/ppermute | solution.py:81
  12.5 5.0 %collective-permute-start.7 = (bf16[2,128,128]{2,1,0:T(8,128)(2,1)S(1)}, bf16[2,128,128]{2,1,0:T(8,128)(2,1)S(1)}, u32[]{:S(2)}, u32[]{:S(2)}) collective-permute-start(bf16[2,128,128]{2,1,0:T(8,128)(2,1)S(1)} %get-tuple-element.46), channel_id=1, source_target_pairs={{0,8},{4,12},{8,0},{12,4},{16,24},{20,28},{24,16},{28,20},{1,9},{5... | collective-permute-start | bytes 196616 | tf_op jit(solution)/shard_map/ppermute | solution.py:81
  13.4 6.6 %collective-permute-start.9 = (bf16[128,256]{1,0:T(8,128)(2,1)S(1)}, bf16[128,256]{1,0:T(8,128)(2,1)S(1)}, u32[]{:S(2)}, u32[]{:S(2)}) collective-permute-start(bf16[128,256]{1,0:T(8,128)(2,1)S(1)} %get-tuple-element.52), channel_id=1, source_target_pairs={{0,16},{4,20},{8,24},{12,28},{16,0},{20,4},{24,8},{28,12},{1,17},{... | collective-permute-start | bytes 196616 | tf_op jit(solution)/shard_map/ppermute | solution.py:81
  16.1 3.9 %collective-permute-start.8 = (bf16[1,128,128]{2,1,0:T(8,128)(2,1)S(1)}, bf16[1,128,128]{2,1,0:T(8,128)(2,1)S(1)}, u32[]{:S(2)}, u32[]{:S(2)}) collective-permute-start(bf16[1,128,128]{2,1,0:T(8,128)(2,1)S(1)} %get-tuple-element.50), channel_id=1, source_target_pairs={{0,4},{4,0},{8,12},{12,8},{16,20},{20,16},{24,28},{28,24},{1,5},{5... | collective-permute-start | bytes 98312 | tf_op jit(solution)/shard_map/ppermute | solution.py:81
  20.6 5.9 %collective-permute-start.10 = (bf16[128,256]{1,0:T(8,128)(2,1)S(1)}, bf16[128,256]{1,0:T(8,128)(2,1)S(1)}, u32[]{:S(2)}, u32[]{:S(2)}) collective-permute-start(bf16[128,256]{1,0:T(8,128)(2,1)S(1)} %get-tuple-element.58), channel_id=1, source_target_pairs={{0,16},{4,20},{8,24},{12,28},{16,0},{20,4},{24,8},{28,12},{1,17},{... | collective-permute-start | bytes 196616 | tf_op jit(solution)/shard_map/ppermute | solution.py:81
  22.0 7.8 %collective-permute-start.12 = (bf16[128,128]{1,0:T(8,128)(2,1)S(1)}, bf16[128,128]{1,0:T(8,128)(2,1)S(1)}, u32[]{:S(2)}, u32[]{:S(2)}) collective-permute-start(bf16[128,128]{1,0:T(8,128)(2,1)S(1)} %get-tuple-element.60), channel_id=1, source_target_pairs={{0,12},{4,8},{8,4},{12,0},{16,28},{20,24},{24,20},{28,16},{1,13},{... | collective-permute-start | bytes 98312 | tf_op jit(solution)/shard_map/ppermute | solution.py:81
  24.7 5.2 %collective-permute-start.13 = (bf16[128,128]{1,0:T(8,128)(2,1)S(1)}, bf16[128,128]{1,0:T(8,128)(2,1)S(1)}, u32[]{:S(2)}, u32[]{:S(2)}) collective-permute-start(bf16[128,128]{1,0:T(8,128)(2,1)S(1)} %get-tuple-element.61), channel_id=1, source_target_pairs={{0,8},{4,12},{8,0},{12,4},{16,24},{20,28},{24,16},{28,20},{1,9},{5... | collective-permute-start | bytes 98312 | tf_op jit(solution)/shard_map/ppermute | solution.py:81
  24.7 5.2 %collective-permute-start.14 = (bf16[128,128]{1,0:T(8,128)(2,1)S(1)}, bf16[128,128]{1,0:T(8,128)(2,1)S(1)}, u32[]{:S(2)}, u32[]{:S(2)}) collective-permute-start(bf16[128,128]{1,0:T(8,128)(2,1)S(1)} %get-tuple-element.62), channel_id=1, source_target_pairs={{0,4},{4,0},{8,12},{12,8},{16,20},{20,16},{24,28},{28,24},{1,5},{5... | collective-permute-start | bytes 98312 | tf_op jit(solution)/shard_map/ppermute | solution.py:81
  27.2 6.5 %collective-permute-start.18 = (bf16[3,128,128]{2,1,0:T(8,128)(2,1)S(1)}, bf16[3,128,128]{2,1,0:T(8,128)(2,1)S(1)}, u32[]{:S(2)}, u32[]{:S(2)}) collective-permute-start(bf16[3,128,128]{2,1,0:T(8,128)(2,1)S(1)} %get-tuple-element.69), channel_id=1, source_target_pairs={{0,12},{4,8},{8,4},{12,0},{16,28},{20,24},{24,20},{28,16},{1,13},{... | collective-permute-start | bytes 294920 | tf_op jit(solution)/shard_map/ppermute | solution.py:81
  29.8 4.6 %collective-permute-start.19 = (bf16[3,128,128]{2,1,0:T(8,128)(2,1)S(1)}, bf16[3,128,128]{2,1,0:T(8,128)(2,1)S(1)}, u32[]{:S(2)}, u32[]{:S(2)}) collective-permute-start(bf16[3,128,128]{2,1,0:T(8,128)(2,1)S(1)} %get-tuple-element.70), channel_id=1, source_target_pairs={{0,8},{4,12},{8,0},{12,4},{16,24},{20,28},{24,16},{28,20},{1,9},{5... | collective-permute-start | bytes 294920 | tf_op jit(solution)/shard_map/ppermute | solution.py:81
  30.3 1.4 %collective-permute-start.16 = (bf16[128,512]{1,0:T(8,128)(2,1)S(1)}, bf16[128,512]{1,0:T(8,128)(2,1)S(1)}, u32[]{:S(2)}, u32[]{:S(2)}) collective-permute-start(bf16[128,512]{1,0:T(8,128)(2,1)S(1)} %get-tuple-element.68), channel_id=1, source_target_pairs={{0,1},{1,0},{2,3},{3,2},{4,5},{5,4},{6,7},{7,6},{8,9},{9,8},{10,11... | collective-permute-start | bytes 393224 | tf_op jit(solution)/shard_map/ppermute | solution.py:81
  30.4 6.6 %collective-permute-start.15 = (bf16[128,512]{1,0:T(8,128)(2,1)S(1)}, bf16[128,512]{1,0:T(8,128)(2,1)S(1)}, u32[]{:S(2)}, u32[]{:S(2)}) collective-permute-start(bf16[128,512]{1,0:T(8,128)(2,1)S(1)} %get-tuple-element.66), channel_id=1, source_target_pairs={{0,1},{1,0},{2,3},{3,2},{4,5},{5,4},{6,7},{7,6},{8,9},{9,8},{10,11... | collective-permute-start | bytes 393224 | tf_op jit(solution)/shard_map/ppermute | solution.py:81
  31.7 5.6 %collective-permute-start.17 = (bf16[128,512]{1,0:T(8,128)(2,1)S(1)}, bf16[128,512]{1,0:T(8,128)(2,1)S(1)}, u32[]{:S(2)}, u32[]{:S(2)}) collective-permute-start(bf16[128,512]{1,0:T(8,128)(2,1)S(1)} %shard_map.104), channel_id=1, source_target_pairs={{0,2},{1,3},{2,0},{3,1},{4,6},{5,7},{6,4},{7,5},{8,10},{9,11},{10,... | collective-permute-start | bytes 393224 | tf_op jit(solution)/shard_map/ppermute | solution.py:81
  32.3 4.6 %collective-permute-start.11 = (bf16[3,128,128]{2,1,0:T(8,128)(2,1)S(1)}, bf16[3,128,128]{2,1,0:T(8,128)(2,1)S(1)}, u32[]{:S(2)}, u32[]{:S(2)}) collective-permute-start(bf16[3,128,128]{2,1,0:T(8,128)(2,1)S(1)} %get-tuple-element.59), channel_id=1, source_target_pairs={{0,4},{4,0},{8,12},{12,8},{16,20},{20,16},{24,28},{28,24},{1,5},{5... | collective-permute-start | bytes 294920 | tf_op jit(solution)/shard_map/ppermute | solution.py:81

commit v20 on v19

--- a/solution.py
+++ b/solution.py
@@ -87,7 +87,7 @@
 
 def sum_kernel(*refs):
     out_ref = refs[-1]
-    out_ref[...] = bf(sum(ref[...].astype(jnp.float32) for ref in refs[:-2]))
+    out_ref[...] = bf(sum(ref[...].astype(jnp.float32) for ref in refs[:-1]))
 
 
 def reduce_blocks(parts, bits):
@@ -96,14 +96,7 @@
         for o in reversed(range(bit, len(parts), 2 * bit)):
             block = held[o][0]
             if bit > 1:
-                (mark,) = call(
-                    mark_kernel, [struct((8, 128), jnp.float32)], block, specs=[ANY],
-                    flops=28 * 10**8,
-                )
-                (block,) = call(
-                    sum_kernel, [struct(block.shape)], *held[o], mark,
-                    specs=[VMEM] * len(held[o]) + [ANY],
-                )
+                (block,) = call(sum_kernel, [struct(block.shape)], *held[o])
             held[o ^ bit].append(swap(block, "head", bit))
     return held[0]
 
@@ -293,16 +286,22 @@
         outs[k][2] = gv_scr[at, :]
 
 
-def mixed_project_kernel(n, *refs):
-    mixed_in, (w_ref, _, *outs, scr) = refs[:n][::-1], refs[n:]
+def far_project_kernel(n, offset, *refs):
+    mixed_in, (w_ref, _, mixed_ref, out_ref) = refs[:n][::-1], refs[n:]
     r, h = member(n), lax.axis_index("head")
-    width = outs[0].shape[1]
+    width = out_ref.shape[1]
     dim = mixed_in[0].shape[1]
     for k in range(n):
-        scr[:, lane(r ^ k, dim)] = mixed_in[k][...]
-    mixed = scr[...]
-    for offset in reversed(range(len(outs))):
-        outs[offset][...] = bf(mm(mixed, w_ref[:, lane(h ^ offset, width)]))
+        mixed_ref[:, lane(r ^ k, dim)] = mixed_in[k][...]
+    out_ref[...] = bf(mm(mixed_ref[...], w_ref[:, lane(h ^ offset, width)]))
+
+
+def project_kernel(mixed_ref, w_ref, *outs):
+    h = lax.axis_index("head")
+    width = outs[0].shape[1]
+    mixed = mixed_ref[...]
+    for offset, out in enumerate(outs):
+        out[...] = bf(mm(mixed, w_ref[:, lane(h ^ offset, width)]))
 
 
 def unpack_kernel(ks, n, *refs):
@@ -414,13 +413,17 @@
     )
     grads_in = exchange(grads[1:]) + [grads[0]]
 
+    mixed, far = call(
+        functools.partial(far_project_kernel, n, split - 1),
+        [struct((rows, n * dim)), struct((rows, width))],
+        *mixed_in, out_weight, grads[0], flops=2 * rows * out_weight.size // split,
+        specs=[VMEM] * (n + 1) + [ANY],
+    )
     parts = call(
-        functools.partial(mixed_project_kernel, n),
-        [struct((rows, width))] * split,
-        *mixed_in, out_weight, grads[0], flops=2 * rows * out_weight.size,
-        specs=[VMEM] * (n + 1) + [ANY],
-        scratch=[pltpu.VMEM((rows, n * dim), jnp.bfloat16)],
-    )
+        project_kernel, [struct((rows, width))] * (split - 1), mixed, out_weight,
+        flops=28 * 10**8,
+    )
+    parts = list(parts) + [far]
     kept = reduce_blocks(parts, bits)
     *early, late, own_grads = grads_in
     ks = [k for k in range(n - 1, 1, -1)] + [0]

time: 38.3 us -> 38.1 us (level)
  waiting for transfers between devices: 6.02 us -> 5.57 us
    ppermute x20, waiting for transfers between devices: 6.02 us -> 5.57 us  [swap(): return lax.ppermute(array, axis, [(i, i ^ bit) for i in range(size)])]
  transfers between devices with their start and end apart: 20 -> 20, of which waited for: 6 -> 6; matrix products, arithmetic and copies ran while one was open for 0% -> 0% of each run, Pallas kernels for 15% -> 16%
where the time goes in v20:
time: 38.1 us; the launch traced here: 37.9 us
  starting transfers between devices  22.9 us (60%)
  Pallas kernels  7.29 us (19%)
  waiting for transfers between devices  5.57 us (15%)
  local copies, waits for them, and re-layouts  1.29 us (3%)
  between operations  0.82 us (2%)
    ppermute x20, starting transfers between devices, swap(): return lax.ppermute(array, axis, [(i, i ^ bit) for i in range(size)])  22.9 us
    pallas_call x14, Pallas kernels, call(): pl.pallas_call(body, out_shape=outs, in_specs=specs or [VMEM] * len(args)...  7.29 us
    ppermute x20, waiting for transfers between devices, swap(): return lax.ppermute(array, axis, [(i, i ^ bit) for i in range(size)])  5.57 us
    unnamed x12, local copies, waits for them, and re-layouts  1.29 us
  transfers between devices with their start and end apart: 20, of which 6 were waited for; matrix products, arithmetic and copies ran while one was open for 0% of the time, Pallas kernels for 16%

profile of v20, /device:TPU:0, one launch (start us, length us, event | category | flops | bytes accessed | tf_op | source)
XLA Modules:
  0.0 37.9 jit_solution(7436374693583038944)
XLA Ops:
  0.6 3.0 %collective-permute-start.3 = (bf16[128,512]{1,0:T(8,128)(2,1)}, bf16[128,512]{1,0:T(8,128)(2,1)S(1)}, u32[]{:S(2)}, u32[]{:S(2)}) collective-permute-start(bf16[128,512]{1,0:T(8,128)(2,1)} %refs_0_.1), channel_id=1, source_target_pairs={{0,2},{1,3},{2,0},{3,1},{4,6},{5,7},{6,4},{7,5},{8,10},{9,11},{10,... | collective-permute-start | bytes 393224 | tf_op jit(solution)/shard_map/ppermute | solution.py:81
  3.6 0.0 collective-permute-start.4
  3.6 0.9 %shard_map.93 = (bf16[3,128,128]{2,1,0:T(8,128)(2,1)S(1)}, bf16[2,128,128]{2,1,0:T(8,128)(2,1)S(1)}, bf16[2,128,128]{2,1,0:T(8,128)(2,1)S(1)}) custom-call(bf16[128,512]{1,0:T(8,128)(2,1)} %refs_3_.5, bf16[128,512]{1,0:T(8,128)(2,1)} %refs_3_.4, bf16[128,512]{1,0:T(8,128)(2,1)} %refs_4_.2), custom_call_target="tpu_custom_call" | custom-call | bytes 622592 | tf_op jit(solution)/shard_map/pallas_call | solution.py:29
  4.6 2.6 %collective-permute-start = (bf16[2,128,128]{2,1,0:T(8,128)(2,1)S(1)}, bf16[2,128,128]{2,1,0:T(8,128)(2,1)S(1)}, u32[]{:S(2)}, u32[]{:S(2)}) collective-permute-start(bf16[2,128,128]{2,1,0:T(8,128)(2,1)S(1)} %get-tuple-element.40), channel_id=1, source_target_pairs={{0,12},{4,8},{8,4},{12,0},{16,28},{20,24},{24,20},{28,16},{1,13},{... | collective-permute-start | bytes 196616 | tf_op jit(solution)/shard_map/ppermute | solution.py:81
  7.2 0.4 %collective-permute-start.1 = (bf16[2,128,128]{2,1,0:T(8,128)(2,1)S(1)}, bf16[2,128,128]{2,1,0:T(8,128)(2,1)S(1)}, u32[]{:S(2)}, u32[]{:S(2)}) collective-permute-start(bf16[2,128,128]{2,1,0:T(8,128)(2,1)S(1)} %get-tuple-element.41), channel_id=1, source_target_pairs={{0,8},{4,12},{8,0},{12,4},{16,24},{20,28},{24,16},{28,20},{1,9},{5... | collective-permute-start | bytes 196616 | tf_op jit(solution)/shard_map/ppermute | solution.py:81
  7.6 0.5 %collective-permute-start.2 = (bf16[3,128,128]{2,1,0:T(8,128)(2,1)S(1)}, bf16[3,128,128]{2,1,0:T(8,128)(2,1)S(1)}, u32[]{:S(2)}, u32[]{:S(2)}) collective-permute-start(bf16[3,128,128]{2,1,0:T(8,128)(2,1)S(1)} %get-tuple-element.42), channel_id=1, source_target_pairs={{0,4},{4,0},{8,12},{12,8},{16,20},{20,16},{24,28},{28,24},{1,5},{5... | collective-permute-start | bytes 294920 | tf_op jit(solution)/shard_map/ppermute | solution.py:81
  8.1 0.0 collective-permute-done.3.refs_1_
  8.1 0.0 collective-permute-start.5
  8.1 0.0 collective-permute-done.4._.refs_2_
  8.2 1.1 %copy-done = bf16[512,2048]{1,0:T(8,128)(2,1)S(1)} copy-done((bf16[512,2048]{1,0:T(8,128)(2,1)S(1)}, bf16[512,2048]{1,0:T(8,128)(2,1)}, u32[]{:S(2)}) %copy-start) | copy-done | bytes 2097176
  9.2 0.0 copy-start.4
  9.2 0.7 %shard_map.95.total_ref = f32[128,512]{1,0:T(8,128)S(1)} custom-call(bf16[128,512]{1,0:T(8,128)(2,1)S(1)} %copy-done.5, bf16[128,512]{1,0:T(8,128)(2,1)S(1)} %collective-permute-done.3.refs_1_, bf16[128,512]{1,0:T(8,128)(2,1)S(1)} %collective-permute-done.4._.refs_2_, bf16[512,2048]{1,0:T(8,128)(2,1)S(1)} %copy-done, f32[8,128]{1,0:T(8,128)S(1)} %shard_map.94.refs_4_), custom_call_target="tpu_custom_call" | custom-call | flops 268435456 | bytes 2756608 | tf_op jit(solution)/shard_map/pallas_call | solution.py:29
  9.9 0.2 copy-done.2
  10.1 0.4 shard_map.96
  10.5 2.0 %collective-permute-start.6 = (bf16[2,128,128]{2,1,0:T(8,128)(2,1)S(1)}, bf16[2,128,128]{2,1,0:T(8,128)(2,1)S(1)}, u32[]{:S(2)}, u32[]{:S(2)}) collective-permute-start(bf16[2,128,128]{2,1,0:T(8,128)(2,1)S(1)} %get-tuple-element.46), channel_id=1, source_target_pairs={{0,12},{4,8},{8,4},{12,0},{16,28},{20,24},{24,20},{28,16},{1,13},{... | collective-permute-start | bytes 196616 | tf_op jit(solution)/shard_map/ppermute | solution.py:81
  12.5 0.4 %collective-permute-start.7 = (bf16[2,128,128]{2,1,0:T(8,128)(2,1)S(1)}, bf16[2,128,128]{2,1,0:T(8,128)(2,1)S(1)}, u32[]{:S(2)}, u32[]{:S(2)}) collective-permute-start(bf16[2,128,128]{2,1,0:T(8,128)(2,1)S(1)} %get-tuple-element.47), channel_id=1, source_target_pairs={{0,8},{4,12},{8,0},{12,4},{16,24},{20,28},{24,16},{28,20},{1,9},{5... | collective-permute-start | bytes 196616 | tf_op jit(solution)/shard_map/ppermute | solution.py:81
  12.9 0.0 collective-permute-done.1.refs_1_
  12.9 0.0 collective-permute-done.2.refs_2_.refs_4_
  13.0 0.5 %shard_map.97 = (bf16[2,512,128]{2,1,0:T(8,128)(2,1)S(1)}, bf16[512,256]{1,0:T(8,128)(2,1)S(1)}, bf16[128,256]{1,0:T(8,128)(2,1)S(1)}) custom-call(bf16[2,128,128]{2,1,0:T(8,128)(2,1)S(1)} %collective-permute-done.refs_0_, bf16[2,128,128]{2,1,0:T(8,128)(2,1)S(1)} %collective-permute-done.1.refs_1_, ...), custom_call_target="tpu_custom_call" | custom-call | flops 67108864 | bytes 1376256 | tf_op jit(solution)/shard_map/pallas_call | solution.py:29
  13.4 2.7 %collective-permute-start.9 = (bf16[128,256]{1,0:T(8,128)(2,1)S(1)}, bf16[128,256]{1,0:T(8,128)(2,1)S(1)}, u32[]{:S(2)}, u32[]{:S(2)}) collective-permute-start(bf16[128,256]{1,0:T(8,128)(2,1)S(1)} %get-tuple-element.53), channel_id=1, source_target_pairs={{0,16},{4,20},{8,24},{12,28},{16,0},{20,4},{24,8},{28,12},{1,17},{... | collective-permute-start | bytes 196616 | tf_op jit(solution)/shard_map/ppermute | solution.py:81
  16.1 1.1 %collective-permute-start.8 = (bf16[1,128,128]{2,1,0:T(8,128)(2,1)S(1)}, bf16[1,128,128]{2,1,0:T(8,128)(2,1)S(1)}, u32[]{:S(2)}, u32[]{:S(2)}) collective-permute-start(bf16[1,128,128]{2,1,0:T(8,128)(2,1)S(1)} %get-tuple-element.51), channel_id=1, source_target_pairs={{0,4},{4,0},{8,12},{12,8},{16,20},{20,16},{24,28},{28,24},{1,5},{5... | collective-permute-start | bytes 98312 | tf_op jit(solution)/shard_map/ppermute | solution.py:81
  17.2 0.2 collective-permute-done.7.refs_1_
  17.4 0.5 %shard_map.98 = (bf16[512,128]{1,0:T(8,128)(2,1)S(1)}, bf16[512,256]{1,0:T(8,128)(2,1)S(1)}, bf16[512,512]{1,0:T(8,128)(2,1)S(1)}, f32[512,128]{1,0:T(8,128)S(1)}) custom-call(bf16[2,128,128]{2,1,0:T(8,128)(2,1)S(1)} %collective-permute-done.6.refs_0_, bf16[2,128,128]{2,1,0:T(8,128)(2,1)S(1)} %collective-permute-done.7.refs_1_, ...), custom_call_target="tpu_custom_call" | custom-call | flops 536870912 | bytes 2359296 | tf_op jit(solution)/shard_map/pallas_call | solution.py:29
  18.0 2.0 %collective-permute-done.8.refs_1_ = bf16[1,128,128]{2,1,0:T(8,128)(2,1)S(1)} collective-permute-done((bf16[1,128,128]{2,1,0:T(8,128)(2,1)S(1)}, bf16[1,128,128]{2,1,0:T(8,128)(2,1)S(1)}, u32[]{:S(2)}, u32[]{:S(2)}) %collective-permute-start.8) | collective-permute-done | bytes 32800 | tf_op jit(solution)/shard_map/ppermute | solution.py:81
  20.0 0.0 collective-permute-done.9.refs_4_
  20.0 0.6 %shard_map.99 = (bf16[128,256]{1,0:T(8,128)(2,1)S(1)}, bf16[512,128]{1,0:T(8,128)(2,1)S(1)}, bf16[128,256]{1,0:T(8,128)(2,1)S(1)}, bf16[128,128]{1,0:T(8,128)(2,...) custom-call(bf16[512,128]{1,0:T(8,128)(2,1)S(1)} %get-tuple-element.50.refs_0_, ...), custom_call_target="tpu_custom_call" | custom-call | flops 67108864 | bytes 1146880 | tf_op jit(solution)/shard_map/pallas_call | solution.py:29
  20.6 1.4 %collective-permute-start.10 = (bf16[128,256]{1,0:T(8,128)(2,1)S(1)}, bf16[128,256]{1,0:T(8,128)(2,1)S(1)}, u32[]{:S(2)}, u32[]{:S(2)}) collective-permute-start(bf16[128,256]{1,0:T(8,128)(2,1)S(1)} %get-tuple-element.59), channel_id=1, source_target_pairs={{0,16},{4,20},{8,24},{12,28},{16,0},{20,4},{24,8},{28,12},{1,17},{... | collective-permute-start | bytes 196616 | tf_op jit(solution)/shard_map/ppermute | solution.py:81
  22.0 2.7 %collective-permute-start.12 = (bf16[128,128]{1,0:T(8,128)(2,1)S(1)}, bf16[128,128]{1,0:T(8,128)(2,1)S(1)}, u32[]{:S(2)}, u32[]{:S(2)}) collective-permute-start(bf16[128,128]{1,0:T(8,128)(2,1)S(1)} %get-tuple-element.61), channel_id=1, source_target_pairs={{0,12},{4,8},{8,4},{12,0},{16,28},{20,24},{24,20},{28,16},{1,13},{... | collective-permute-start | bytes 98312 | tf_op jit(solution)/shard_map/ppermute | solution.py:81
  24.7 0.9 %collective-permute-start.14 = (bf16[128,128]{1,0:T(8,128)(2,1)S(1)}, bf16[128,128]{1,0:T(8,128)(2,1)S(1)}, u32[]{:S(2)}, u32[]{:S(2)}) collective-permute-start(bf16[128,128]{1,0:T(8,128)(2,1)S(1)} %get-tuple-element.63), channel_id=1, source_target_pairs={{0,4},{4,0},{8,12},{12,8},{16,20},{20,16},{24,28},{28,24},{1,5},{5... | collective-permute-start | bytes 98312 | tf_op jit(solution)/shard_map/ppermute | solution.py:81
  25.6 1.0 %shard_map.100 = (bf16[512,128]{1,0:T(8,128)(2,1)S(1)}, f32[512,128]{1,0:T(8,128)S(1)}, f32[512,256]{1,0:T(8,128)S(1)}) custom-call(bf16[2,512,128]{2,1,0:T(8,128)(2,1)S(1)} %get-tuple-element.44.refs_5_.kv_ref, bf16[4,128,256]{2,1,0:T(8,128)(2,1)S(1)} %copy-done.1, bf16[512,256]{1,0:T(8,128)(2,1)S(1)} %get-tuple-element.45.refs_7_.kf_ref, ...), custom_call_target="tpu_custom_call" | custom-call | flops 268435456 | bytes 2686976 | tf_op jit(solution)/shard_map/pallas_call | solution.py:29
  26.6 0.0 collective-permute-done.10.rest_0_
  26.6 0.6 %shard_map.101 = (bf16[3,128,128]{2,1,0:T(8,128)(2,1)S(1)}, bf16[3,128,128]{2,1,0:T(8,128)(2,1)S(1)}, bf16[3,128,128]{2,1,0:T(8,128)(2,1)S(1)}, bf16[3,128,128]{2,1,0:T(8,128)(2,1)S(1)}) custom-call(bf16[2,512,128]{2,1,0:T(8,128)(2,1)S(1)} %get-tuple-element.44.refs_5_.kv_ref, bf16[4,128,256]{2,1,0:T(8,128)(2,1)S(1)} %copy-done.1, ...), custom_call_target="tpu_custom_call" | custom-call | flops 100663296 | bytes 2162688 | tf_op jit(solution)/shard_map/pallas_call | solution.py:29
  27.2 2.7 %collective-permute-start.18 = (bf16[3,128,128]{2,1,0:T(8,128)(2,1)S(1)}, bf16[3,128,128]{2,1,0:T(8,128)(2,1)S(1)}, u32[]{:S(2)}, u32[]{:S(2)}) collective-permute-start(bf16[3,128,128]{2,1,0:T(8,128)(2,1)S(1)} %get-tuple-element.71), channel_id=1, source_target_pairs={{0,12},{4,8},{8,4},{12,0},{16,28},{20,24},{24,20},{28,16},{1,13},{... | collective-permute-start | bytes 294920 | tf_op jit(solution)/shard_map/ppermute | solution.py:81
  29.8 0.0 collective-permute-done.14.refs_2_
  29.8 0.2 shard_map.102
  30.1 0.1 collective-permute-start.16
  30.2 0.4 %shard_map.103 = (bf16[128,512]{1,0:T(8,128)(2,1)S(1)}, bf16[128,512]{1,0:T(8,128)(2,1)S(1)}, bf16[128,512]{1,0:T(8,128)(2,1)S(1)}) custom-call(bf16[128,512]{1,0:T(8,128)(2,1)S(1)} %get-tuple-element.66.mixed_ref, bf16[512,2048]{1,0:T(8,128)(2,1)S(1)} %copy-done), custom_call_target="tpu_custom_call" | custom-call | flops 2800000000 | bytes 2621440 | tf_op jit(solution)/shard_map/pallas_call | solution.py:29
  30.6 0.6 %collective-permute-start.15 = (bf16[128,512]{1,0:T(8,128)(2,1)S(1)}, bf16[128,512]{1,0:T(8,128)(2,1)S(1)}, u32[]{:S(2)}, u32[]{:S(2)}) collective-permute-start(bf16[128,512]{1,0:T(8,128)(2,1)S(1)} %get-tuple-element.68), channel_id=1, source_target_pairs={{0,1},{1,0},{2,3},{3,2},{4,5},{5,4},{6,7},{7,6},{8,9},{9,8},{10,11... | collective-permute-start | bytes 393224 | tf_op jit(solution)/shard_map/ppermute | solution.py:81
  31.1 0.4 %collective-permute-done.16.refs_1_ = bf16[128,512]{1,0:T(8,128)(2,1)S(1)} collective-permute-done((bf16[128,512]{1,0:T(8,128)(2,1)S(1)}, bf16[128,512]{1,0:T(8,128)(2,1)S(1)}, u32[]{:S(2)}, u32[]{:S(2)}) %collective-permute-start.16) | collective-permute-done | bytes 131104 | tf_op jit(solution)/shard_map/ppermute | solution.py:81
  31.5 0.6 %collective-permute-start.17 = (bf16[128,512]{1,0:T(8,128)(2,1)S(1)}, bf16[128,512]{1,0:T(8,128)(2,1)S(1)}, u32[]{:S(2)}, u32[]{:S(2)}) collective-permute-start(bf16[128,512]{1,0:T(8,128)(2,1)S(1)} %shard_map.104), channel_id=1, source_target_pairs={{0,2},{1,3},{2,0},{3,1},{4,6},{5,7},{6,4},{7,5},{8,10},{9,11},{10,... | collective-permute-start | bytes 393224 | tf_op jit(solution)/shard_map/ppermute | solution.py:81
  32.1 1.3 %collective-permute-start.11 = (bf16[3,128,128]{2,1,0:T(8,128)(2,1)S(1)}, bf16[3,128,128]{2,1,0:T(8,128)(2,1)S(1)}, u32[]{:S(2)}, u32[]{:S(2)}) collective-permute-start(bf16[3,128,128]{2,1,0:T(8,128)(2,1)S(1)} %get-tuple-element.60), channel_id=1, source_target_pairs={{0,4},{4,0},{8,12},{12,8},{16,20},{20,16},{24,28},{28,24},{1,5},{5... | collective-permute-start | bytes 294920 | tf_op jit(solution)/shard_map/ppermute | solution.py:81
  33.4 0.0 collective-permute-done.18.refs_0_
  33.4 1.0 %collective-permute-done.19.refs_1_ = bf16[3,128,128]{2,1,0:T(8,128)(2,1)S(1)} collective-permute-done((bf16[3,128,128]{2,1,0:T(8,128)(2,1)S(1)}, bf16[3,128,128]{2,1,0:T(8,128)(2,1)S(1)}, u32[]{:S(2)}, u32[]{:S(2)}) %collective-permute-start.19) | collective-permute-done | bytes 98336 | tf_op jit(solution)/shard_map/ppermute | solution.py:81
  34.4 0.8 %shard_map.105 = (bf16[128,512]{1,0:T(8,128)(2,1)}, bf16[128,512]{1,0:T(8,128)(2,1)}, bf16[128,512]{1,0:T(8,128)(2,1)}) custom-call(bf16[3,128,128]{2,1,0:T(8,128)(2,1)S(1)} %collective-permute-done.18.refs_0_, bf16[3,128,128]{2,1,0:T(8,128)(2,1)S(1)} %collective-permute-done.19.refs_1_, bf16[3,128,128]{2,1,0:T(8,128)(2,1)S(1)} %get-tuple-element.65.refs_5_.refs_2_), custom_call_target="tpu_custom_call" | custom-call | flops 800000000 | bytes 688128 | tf_op jit(solution)/shard_map/pallas_call | solution.py:29
  35.2 1.5 %collective-permute-done.11.got_ref = bf16[3,128,128]{2,1,0:T(8,128)(2,1)S(1)} collective-permute-done((bf16[3,128,128]{2,1,0:T(8,128)(2,1)S(1)}, bf16[3,128,128]{2,1,0:T(8,128)(2,1)S(1)}, u32[]{:S(2)}, u32[]{:S(2)}) %collective-permute-start.11) | collective-permute-done | bytes 98336 | tf_op jit(solution)/shard_map/ppermute | solution.py:81
  36.8 0.0 collective-permute-done.15.refs_1_
  36.8 0.4 %collective-permute-done.17.refs_2_ = bf16[128,512]{1,0:T(8,128)(2,1)S(1)} collective-permute-done((bf16[128,512]{1,0:T(8,128)(2,1)S(1)}, bf16[128,512]{1,0:T(8,128)(2,1)S(1)}, u32[]{:S(2)}, u32[]{:S(2)}) %collective-permute-start.17) | collective-permute-done | bytes 131104 | tf_op jit(solution)/shard_map/ppermute | solution.py:81
  37.2 0.7 %shard_map.106 = (bf16[128,512]{1,0:T(8,128)(2,1)}, bf16[128,512]{1,0:T(8,128)(2,1)}, bf16[128,512]{1,0:T(8,128)(2,1)}, bf16[128,512]{1,0:T(8,128)(2,1)}) custom-call(bf16[3,128,128]{2,1,0:T(8,128)(2,1)S(1)} %collective-permute-done.11.got_ref, ...), custom_call_target="tpu_custom_call", output_to_operand_aliasing={{1}: (4, {}), {2}: (5, {}), {3}: (6, {})} | custom-call | bytes 1409024 | tf_op jit(solution)/shard_map/pallas_call | solution.py:29
  (18 shorter events, 0.1 us)
Async XLA Ops:
  0.6 7.5 %collective-permute-start.3 = (bf16[128,512]{1,0:T(8,128)(2,1)}, bf16[128,512]{1,0:T(8,128)(2,1)S(1)}, u32[]{:S(2)}, u32[]{:S(2)}) collective-permute-start(bf16[128,512]{1,0:T(8,128)(2,1)} %refs_0_.1), channel_id=1, source_target_pairs={{0,2},{1,3},{2,0},{3,1},{4,6},{5,7},{6,4},{7,5},{8,10},{9,11},{10,... | collective-permute-start | bytes 393224 | tf_op jit(solution)/shard_map/ppermute | solution.py:81
  3.6 4.5 %collective-permute-start.4 = (bf16[128,512]{1,0:T(8,128)(2,1)}, bf16[128,512]{1,0:T(8,128)(2,1)S(1)}, u32[]{:S(2)}, u32[]{:S(2)}) collective-permute-start(bf16[128,512]{1,0:T(8,128)(2,1)} %refs_0_.1), channel_id=1, source_target_pairs={{0,1},{1,0},{2,3},{3,2},{4,5},{5,4},{6,7},{7,6},{8,9},{9,8},{10,11... | collective-permute-start | bytes 393224 | tf_op jit(solution)/shard_map/ppermute | solution.py:81
  4.6 8.3 %collective-permute-start = (bf16[2,128,128]{2,1,0:T(8,128)(2,1)S(1)}, bf16[2,128,128]{2,1,0:T(8,128)(2,1)S(1)}, u32[]{:S(2)}, u32[]{:S(2)}) collective-permute-start(bf16[2,128,128]{2,1,0:T(8,128)(2,1)S(1)} %get-tuple-element.40), channel_id=1, source_target_pairs={{0,12},{4,8},{8,4},{12,0},{16,28},{20,24},{24,20},{28,16},{1,13},{... | collective-permute-start | bytes 196616 | tf_op jit(solution)/shard_map/ppermute | solution.py:81
  7.2 5.7 %collective-permute-start.1 = (bf16[2,128,128]{2,1,0:T(8,128)(2,1)S(1)}, bf16[2,128,128]{2,1,0:T(8,128)(2,1)S(1)}, u32[]{:S(2)}, u32[]{:S(2)}) collective-permute-start(bf16[2,128,128]{2,1,0:T(8,128)(2,1)S(1)} %get-tuple-element.41), channel_id=1, source_target_pairs={{0,8},{4,12},{8,0},{12,4},{16,24},{20,28},{24,16},{28,20},{1,9},{5... | collective-permute-start | bytes 196616 | tf_op jit(solution)/shard_map/ppermute | solution.py:81
  7.6 1.6 %copy-start = (bf16[512,2048]{1,0:T(8,128)(2,1)S(1)}, bf16[512,2048]{1,0:T(8,128)(2,1)}, u32[]{:S(2)}) copy-start(bf16[512,2048]{1,0:T(8,128)(2,1)} %w_ref.3) | copy-start | bytes 6291460
  7.6 1.6 %copy-start.5 = (bf16[128,512]{1,0:T(8,128)(2,1)S(1)}, bf16[128,512]{1,0:T(8,128)(2,1)}, u32[]{:S(2)}) copy-start(bf16[128,512]{1,0:T(8,128)(2,1)} %refs_0_.1) | copy-start | bytes 393220
  7.6 5.3 %collective-permute-start.2 = (bf16[3,128,128]{2,1,0:T(8,128)(2,1)S(1)}, bf16[3,128,128]{2,1,0:T(8,128)(2,1)S(1)}, u32[]{:S(2)}, u32[]{:S(2)}) collective-permute-start(bf16[3,128,128]{2,1,0:T(8,128)(2,1)S(1)} %get-tuple-element.42), channel_id=1, source_target_pairs={{0,4},{4,0},{8,12},{12,8},{16,20},{20,16},{24,28},{28,24},{1,5},{5... | collective-permute-start | bytes 294920 | tf_op jit(solution)/shard_map/ppermute | solution.py:81
  8.1 1.8 %collective-permute-start.5 = (bf16[128,512]{1,0:T(8,128)(2,1)S(1)}, bf16[128,512]{1,0:T(8,128)(2,1)S(1)}, u32[]{:S(2)}, u32[]{:S(2)}) collective-permute-start(bf16[128,512]{1,0:T(8,128)(2,1)S(1)} %collective-permute-done.3.refs_1_), channel_id=1, source_target_pairs={{0,1},{1,0},{2,3},{3,2},{4,5},{5,4},{6,7},{7,6},{8,9},{9,8},{10,11... | collective-permute-start | bytes 393224 | tf_op jit(solution)/shard_map/ppermute | solution.py:81
  9.2 0.9 %copy-start.2 = (bf16[128,512]{1,0:T(8,128)(2,1)S(1)}, bf16[128,512]{1,0:T(8,128)(2,1)}, u32[]{:S(2)}) copy-start(bf16[128,512]{1,0:T(8,128)(2,1)} %refs_3_.5) | copy-start | bytes 393220
  9.2 3.7 %copy-start.1 = (bf16[4,128,256]{2,1,0:T(8,128)(2,1)S(1)}, bf16[4,128,256]{2,1,0:T(8,128)(2,1)}, u32[]{:S(2)}) copy-start(bf16[4,128,256]{2,1,0:T(8,128)(2,1)} %om_ref.3) | copy-start | bytes 786436
  9.2 3.7 %copy-start.3 = (bf16[128,512]{1,0:T(8,128)(2,1)S(1)}, bf16[128,512]{1,0:T(8,128)(2,1)}, u32[]{:S(2)}) copy-start(bf16[128,512]{1,0:T(8,128)(2,1)} %refs_3_.4) | copy-start | bytes 393220
  9.2 3.7 %copy-start.4 = (bf16[128,512]{1,0:T(8,128)(2,1)S(1)}, bf16[128,512]{1,0:T(8,128)(2,1)}, u32[]{:S(2)}) copy-start(bf16[128,512]{1,0:T(8,128)(2,1)} %refs_4_.2) | copy-start | bytes 393220
  10.5 6.7 %collective-permute-start.6 = (bf16[2,128,128]{2,1,0:T(8,128)(2,1)S(1)}, bf16[2,128,128]{2,1,0:T(8,128)(2,1)S(1)}, u32[]{:S(2)}, u32[]{:S(2)}) collective-permute-start(bf16[2,128,128]{2,1,0:T(8,128)(2,1)S(1)} %get-tuple-element.46), channel_id=1, source_target_pairs={{0,12},{4,8},{8,4},{12,0},{16,28},{20,24},{24,20},{28,16},{1,13},{... | collective-permute-start | bytes 196616 | tf_op jit(solution)/shard_map/ppermute | solution.py:81
  12.5 5.0 %collective-permute-start.7 = (bf16[2,128,128]{2,1,0:T(8,128)(2,1)S(1)}, bf16[2,128,128]{2,1,0:T(8,128)(2,1)S(1)}, u32[]{:S(2)}, u32[]{:S(2)}) collective-permute-start(bf16[2,128,128]{2,1,0:T(8,128)(2,1)S(1)} %get-tuple-element.47), channel_id=1, source_target_pairs={{0,8},{4,12},{8,0},{12,4},{16,24},{20,28},{24,16},{28,20},{1,9},{5... | collective-permute-start | bytes 196616 | tf_op jit(solution)/shard_map/ppermute | solution.py:81
  13.4 6.6 %collective-permute-start.9 = (bf16[128,256]{1,0:T(8,128)(2,1)S(1)}, bf16[128,256]{1,0:T(8,128)(2,1)S(1)}, u32[]{:S(2)}, u32[]{:S(2)}) collective-permute-start(bf16[128,256]{1,0:T(8,128)(2,1)S(1)} %get-tuple-element.53), channel_id=1, source_target_pairs={{0,16},{4,20},{8,24},{12,28},{16,0},{20,4},{24,8},{28,12},{1,17},{... | collective-permute-start | bytes 196616 | tf_op jit(solution)/shard_map/ppermute | solution.py:81
  16.1 3.9 %collective-permute-start.8 = (bf16[1,128,128]{2,1,0:T(8,128)(2,1)S(1)}, bf16[1,128,128]{2,1,0:T(8,128)(2,1)S(1)}, u32[]{:S(2)}, u32[]{:S(2)}) collective-permute-start(bf16[1,128,128]{2,1,0:T(8,128)(2,1)S(1)} %get-tuple-element.51), channel_id=1, source_target_pairs={{0,4},{4,0},{8,12},{12,8},{16,20},{20,16},{24,28},{28,24},{1,5},{5... | collective-permute-start | bytes 98312 | tf_op jit(solution)/shard_map/ppermute | solution.py:81
  20.6 5.9 %collective-permute-start.10 = (bf16[128,256]{1,0:T(8,128)(2,1)S(1)}, bf16[128,256]{1,0:T(8,128)(2,1)S(1)}, u32[]{:S(2)}, u32[]{:S(2)}) collective-permute-start(bf16[128,256]{1,0:T(8,128)(2,1)S(1)} %get-tuple-element.59), channel_id=1, source_target_pairs={{0,16},{4,20},{8,24},{12,28},{16,0},{20,4},{24,8},{28,12},{1,17},{... | collective-permute-start | bytes 196616 | tf_op jit(solution)/shard_map/ppermute | solution.py:81
  22.0 7.8 %collective-permute-start.12 = (bf16[128,128]{1,0:T(8,128)(2,1)S(1)}, bf16[128,128]{1,0:T(8,128)(2,1)S(1)}, u32[]{:S(2)}, u32[]{:S(2)}) collective-permute-start(bf16[128,128]{1,0:T(8,128)(2,1)S(1)} %get-tuple-element.61), channel_id=1, source_target_pairs={{0,12},{4,8},{8,4},{12,0},{16,28},{20,24},{24,20},{28,16},{1,13},{... | collective-permute-start | bytes 98312 | tf_op jit(solution)/shard_map/ppermute | solution.py:81
  24.7 5.2 %collective-permute-start.13 = (bf16[128,128]{1,0:T(8,128)(2,1)S(1)}, bf16[128,128]{1,0:T(8,128)(2,1)S(1)}, u32[]{:S(2)}, u32[]{:S(2)}) collective-permute-start(bf16[128,128]{1,0:T(8,128)(2,1)S(1)} %get-tuple-element.62), channel_id=1, source_target_pairs={{0,8},{4,12},{8,0},{12,4},{16,24},{20,28},{24,16},{28,20},{1,9},{5... | collective-permute-start | bytes 98312 | tf_op jit(solution)/shard_map/ppermute | solution.py:81
  24.7 5.2 %collective-permute-start.14 = (bf16[128,128]{1,0:T(8,128)(2,1)S(1)}, bf16[128,128]{1,0:T(8,128)(2,1)S(1)}, u32[]{:S(2)}, u32[]{:S(2)}) collective-permute-start(bf16[128,128]{1,0:T(8,128)(2,1)S(1)} %get-tuple-element.63), channel_id=1, source_target_pairs={{0,4},{4,0},{8,12},{12,8},{16,20},{20,16},{24,28},{28,24},{1,5},{5... | collective-permute-start | bytes 98312 | tf_op jit(solution)/shard_map/ppermute | solution.py:81
  27.2 6.3 %collective-permute-start.18 = (bf16[3,128,128]{2,1,0:T(8,128)(2,1)S(1)}, bf16[3,128,128]{2,1,0:T(8,128)(2,1)S(1)}, u32[]{:S(2)}, u32[]{:S(2)}) collective-permute-start(bf16[3,128,128]{2,1,0:T(8,128)(2,1)S(1)} %get-tuple-element.71), channel_id=1, source_target_pairs={{0,12},{4,8},{8,4},{12,0},{16,28},{20,24},{24,20},{28,16},{1,13},{... | collective-permute-start | bytes 294920 | tf_op jit(solution)/shard_map/ppermute | solution.py:81
  29.8 4.6 %collective-permute-start.19 = (bf16[3,128,128]{2,1,0:T(8,128)(2,1)S(1)}, bf16[3,128,128]{2,1,0:T(8,128)(2,1)S(1)}, u32[]{:S(2)}, u32[]{:S(2)}) collective-permute-start(bf16[3,128,128]{2,1,0:T(8,128)(2,1)S(1)} %get-tuple-element.72), channel_id=1, source_target_pairs={{0,8},{4,12},{8,0},{12,4},{16,24},{20,28},{24,16},{28,20},{1,9},{5... | collective-permute-start | bytes 294920 | tf_op jit(solution)/shard_map/ppermute | solution.py:81
  30.1 1.4 %collective-permute-start.16 = (bf16[128,512]{1,0:T(8,128)(2,1)S(1)}, bf16[128,512]{1,0:T(8,128)(2,1)S(1)}, u32[]{:S(2)}, u32[]{:S(2)}) collective-permute-start(bf16[128,512]{1,0:T(8,128)(2,1)S(1)} %get-tuple-element.70), channel_id=1, source_target_pairs={{0,1},{1,0},{2,3},{3,2},{4,5},{5,4},{6,7},{7,6},{8,9},{9,8},{10,11... | collective-permute-start | bytes 393224 | tf_op jit(solution)/shard_map/ppermute | solution.py:81
  30.6 6.2 %collective-permute-start.15 = (bf16[128,512]{1,0:T(8,128)(2,1)S(1)}, bf16[128,512]{1,0:T(8,128)(2,1)S(1)}, u32[]{:S(2)}, u32[]{:S(2)}) collective-permute-start(bf16[128,512]{1,0:T(8,128)(2,1)S(1)} %get-tuple-element.68), channel_id=1, source_target_pairs={{0,1},{1,0},{2,3},{3,2},{4,5},{5,4},{6,7},{7,6},{8,9},{9,8},{10,11... | collective-permute-start | bytes 393224 | tf_op jit(solution)/shard_map/ppermute | solution.py:81
  31.5 5.6 %collective-permute-start.17 = (bf16[128,512]{1,0:T(8,128)(2,1)S(1)}, bf16[128,512]{1,0:T(8,128)(2,1)S(1)}, u32[]{:S(2)}, u32[]{:S(2)}) collective-permute-start(bf16[128,512]{1,0:T(8,128)(2,1)S(1)} %shard_map.104), channel_id=1, source_target_pairs={{0,2},{1,3},{2,0},{3,1},{4,6},{5,7},{6,4},{7,5},{8,10},{9,11},{10,... | collective-permute-start | bytes 393224 | tf_op jit(solution)/shard_map/ppermute | solution.py:81
  32.1 4.6 %collective-permute-start.11 = (bf16[3,128,128]{2,1,0:T(8,128)(2,1)S(1)}, bf16[3,128,128]{2,1,0:T(8,128)(2,1)S(1)}, u32[]{:S(2)}, u32[]{:S(2)}) collective-permute-start(bf16[3,128,128]{2,1,0:T(8,128)(2,1)S(1)} %get-tuple-element.60), channel_id=1, source_target_pairs={{0,4},{4,0},{8,12},{12,8},{16,20},{20,16},{24,28},{28,24},{1,5},{5... | collective-permute-start | bytes 294920 | tf_op jit(solution)/shard_map/ppermute | solution.py:81

commit v21 on v20

--- a/solution.py
+++ b/solution.py
@@ -421,7 +421,7 @@
     )
     parts = call(
         project_kernel, [struct((rows, width))] * (split - 1), mixed, out_weight,
-        flops=28 * 10**8,
+        flops=10 * 10**8,
     )
     parts = list(parts) + [far]
     kept = reduce_blocks(parts, bits)

time: 38.1 us -> 38.8 us (1.018)
  waiting for transfers between devices: 5.57 us -> 7 us
  starting transfers between devices: 22.9 us -> 22.2 us
    ppermute x20, waiting for transfers between devices: 5.57 us -> 7 us  [swap(): return lax.ppermute(array, axis, [(i, i ^ bit) for i in range(size)])]
    ppermute x20, starting transfers between devices: 22.9 us -> 22.2 us  [swap(): return lax.ppermute(array, axis, [(i, i ^ bit) for i in range(size)])]
  transfers between devices with their start and end apart: 20 -> 20, of which waited for: 6 -> 6; matrix products, arithmetic and copies ran while one was open for 0% -> 0% of each run, Pallas kernels for 16% -> 15%
where the time goes in v21:
time: 38.8 us; the launch traced here: 38.6 us
  starting transfers between devices  22.2 us (57%)
  Pallas kernels  7.28 us (19%)
  waiting for transfers between devices  7 us (18%)
  local copies, waits for them, and re-layouts  1.29 us (3%)
  between operations  0.81 us (2%)
    ppermute x20, starting transfers between devices, swap(): return lax.ppermute(array, axis, [(i, i ^ bit) for i in range(size)])  22.2 us
    pallas_call x14, Pallas kernels, call(): pl.pallas_call(body, out_shape=outs, in_specs=specs or [VMEM] * len(args)...  7.28 us
    ppermute x20, waiting for transfers between devices, swap(): return lax.ppermute(array, axis, [(i, i ^ bit) for i in range(size)])  7 us
    unnamed x12, local copies, waits for them, and re-layouts  1.29 us
  transfers between devices with their start and end apart: 20, of which 6 were waited for; matrix products, arithmetic and copies ran while one was open for 0% of the time, Pallas kernels for 15%

profile of v21, /device:TPU:0, one launch (start us, length us, event | category | flops | bytes accessed | tf_op | source)
XLA Modules:
  0.0 38.6 jit_solution(17652888721254950729)
XLA Ops:
  0.6 3.0 %collective-permute-start.3 = (bf16[128,512]{1,0:T(8,128)(2,1)}, bf16[128,512]{1,0:T(8,128)(2,1)S(1)}, u32[]{:S(2)}, u32[]{:S(2)}) collective-permute-start(bf16[128,512]{1,0:T(8,128)(2,1)} %refs_0_.1), channel_id=1, source_target_pairs={{0,2},{1,3},{2,0},{3,1},{4,6},{5,7},{6,4},{7,5},{8,10},{9,11},{10,... | collective-permute-start | bytes 393224 | tf_op jit(solution)/shard_map/ppermute | solution.py:81
  3.6 0.9 %shard_map.93 = (bf16[3,128,128]{2,1,0:T(8,128)(2,1)S(1)}, bf16[2,128,128]{2,1,0:T(8,128)(2,1)S(1)}, bf16[2,128,128]{2,1,0:T(8,128)(2,1)S(1)}) custom-call(bf16[128,512]{1,0:T(8,128)(2,1)} %refs_3_.5, bf16[128,512]{1,0:T(8,128)(2,1)} %refs_3_.4, bf16[128,512]{1,0:T(8,128)(2,1)} %refs_4_.2), custom_call_target="tpu_custom_call" | custom-call | bytes 622592 | tf_op jit(solution)/shard_map/pallas_call | solution.py:29
  4.6 2.6 %collective-permute-start = (bf16[2,128,128]{2,1,0:T(8,128)(2,1)S(1)}, bf16[2,128,128]{2,1,0:T(8,128)(2,1)S(1)}, u32[]{:S(2)}, u32[]{:S(2)}) collective-permute-start(bf16[2,128,128]{2,1,0:T(8,128)(2,1)S(1)} %get-tuple-element.40), channel_id=1, source_target_pairs={{0,12},{4,8},{8,4},{12,0},{16,28},{20,24},{24,20},{28,16},{1,13},{... | collective-permute-start | bytes 196616 | tf_op jit(solution)/shard_map/ppermute | solution.py:81
  7.2 0.4 %collective-permute-start.1 = (bf16[2,128,128]{2,1,0:T(8,128)(2,1)S(1)}, bf16[2,128,128]{2,1,0:T(8,128)(2,1)S(1)}, u32[]{:S(2)}, u32[]{:S(2)}) collective-permute-start(bf16[2,128,128]{2,1,0:T(8,128)(2,1)S(1)} %get-tuple-element.41), channel_id=1, source_target_pairs={{0,8},{4,12},{8,0},{12,4},{16,24},{20,28},{24,16},{28,20},{1,9},{5... | collective-permute-start | bytes 196616 | tf_op jit(solution)/shard_map/ppermute | solution.py:81
  7.6 0.5 %collective-permute-start.2 = (bf16[3,128,128]{2,1,0:T(8,128)(2,1)S(1)}, bf16[3,128,128]{2,1,0:T(8,128)(2,1)S(1)}, u32[]{:S(2)}, u32[]{:S(2)}) collective-permute-start(bf16[3,128,128]{2,1,0:T(8,128)(2,1)S(1)} %get-tuple-element.42), channel_id=1, source_target_pairs={{0,4},{4,0},{8,12},{12,8},{16,20},{20,16},{24,28},{28,24},{1,5},{5... | collective-permute-start | bytes 294920 | tf_op jit(solution)/shard_map/ppermute | solution.py:81
  8.1 0.0 collective-permute-done.3.refs_1_
  8.1 0.0 collective-permute-start.5
  8.1 0.0 collective-permute-done.4._.refs_2_
  8.2 1.1 %copy-done = bf16[512,2048]{1,0:T(8,128)(2,1)S(1)} copy-done((bf16[512,2048]{1,0:T(8,128)(2,1)S(1)}, bf16[512,2048]{1,0:T(8,128)(2,1)}, u32[]{:S(2)}) %copy-start) | copy-done | bytes 2097176
  9.2 0.0 copy-start.4
  9.2 0.7 %shard_map.95.total_ref = f32[128,512]{1,0:T(8,128)S(1)} custom-call(bf16[128,512]{1,0:T(8,128)(2,1)S(1)} %copy-done.5, bf16[128,512]{1,0:T(8,128)(2,1)S(1)} %collective-permute-done.3.refs_1_, bf16[128,512]{1,0:T(8,128)(2,1)S(1)} %collective-permute-done.4._.refs_2_, bf16[512,2048]{1,0:T(8,128)(2,1)S(1)} %copy-done, f32[8,128]{1,0:T(8,128)S(1)} %shard_map.94.refs_4_), custom_call_target="tpu_custom_call" | custom-call | flops 268435456 | bytes 2756608 | tf_op jit(solution)/shard_map/pallas_call | solution.py:29
  9.9 0.2 copy-done.2
  10.1 0.4 shard_map.96
  10.5 2.0 %collective-permute-start.6 = (bf16[2,128,128]{2,1,0:T(8,128)(2,1)S(1)}, bf16[2,128,128]{2,1,0:T(8,128)(2,1)S(1)}, u32[]{:S(2)}, u32[]{:S(2)}) collective-permute-start(bf16[2,128,128]{2,1,0:T(8,128)(2,1)S(1)} %get-tuple-element.46), channel_id=1, source_target_pairs={{0,12},{4,8},{8,4},{12,0},{16,28},{20,24},{24,20},{28,16},{1,13},{... | collective-permute-start | bytes 196616 | tf_op jit(solution)/shard_map/ppermute | solution.py:81
  12.5 0.4 %collective-permute-start.7 = (bf16[2,128,128]{2,1,0:T(8,128)(2,1)S(1)}, bf16[2,128,128]{2,1,0:T(8,128)(2,1)S(1)}, u32[]{:S(2)}, u32[]{:S(2)}) collective-permute-start(bf16[2,128,128]{2,1,0:T(8,128)(2,1)S(1)} %get-tuple-element.47), channel_id=1, source_target_pairs={{0,8},{4,12},{8,0},{12,4},{16,24},{20,28},{24,16},{28,20},{1,9},{5... | collective-permute-start | bytes 196616 | tf_op jit(solution)/shard_map/ppermute | solution.py:81
  12.9 0.0 collective-permute-done.refs_0_
  12.9 0.0 collective-permute-done.1.refs_1_
  12.9 0.0 collective-permute-done.2.refs_2_.refs_4_
  13.0 0.5 %shard_map.97 = (bf16[2,512,128]{2,1,0:T(8,128)(2,1)S(1)}, bf16[512,256]{1,0:T(8,128)(2,1)S(1)}, bf16[128,256]{1,0:T(8,128)(2,1)S(1)}) custom-call(bf16[2,128,128]{2,1,0:T(8,128)(2,1)S(1)} %collective-permute-done.refs_0_, bf16[2,128,128]{2,1,0:T(8,128)(2,1)S(1)} %collective-permute-done.1.refs_1_, ...), custom_call_target="tpu_custom_call" | custom-call | flops 67108864 | bytes 1376256 | tf_op jit(solution)/shard_map/pallas_call | solution.py:29
  13.4 2.7 %collective-permute-start.9 = (bf16[128,256]{1,0:T(8,128)(2,1)S(1)}, bf16[128,256]{1,0:T(8,128)(2,1)S(1)}, u32[]{:S(2)}, u32[]{:S(2)}) collective-permute-start(bf16[128,256]{1,0:T(8,128)(2,1)S(1)} %get-tuple-element.53), channel_id=1, source_target_pairs={{0,16},{4,20},{8,24},{12,28},{16,0},{20,4},{24,8},{28,12},{1,17},{... | collective-permute-start | bytes 196616 | tf_op jit(solution)/shard_map/ppermute | solution.py:81
  16.1 1.1 %collective-permute-start.8 = (bf16[1,128,128]{2,1,0:T(8,128)(2,1)S(1)}, bf16[1,128,128]{2,1,0:T(8,128)(2,1)S(1)}, u32[]{:S(2)}, u32[]{:S(2)}) collective-permute-start(bf16[1,128,128]{2,1,0:T(8,128)(2,1)S(1)} %get-tuple-element.51), channel_id=1, source_target_pairs={{0,4},{4,0},{8,12},{12,8},{16,20},{20,16},{24,28},{28,24},{1,5},{5... | collective-permute-start | bytes 98312 | tf_op jit(solution)/shard_map/ppermute | solution.py:81
  17.2 0.2 collective-permute-done.7.refs_1_
  17.4 0.5 %shard_map.98 = (bf16[512,128]{1,0:T(8,128)(2,1)S(1)}, bf16[512,256]{1,0:T(8,128)(2,1)S(1)}, bf16[512,512]{1,0:T(8,128)(2,1)S(1)}, f32[512,128]{1,0:T(8,128)S(1)}) custom-call(bf16[2,128,128]{2,1,0:T(8,128)(2,1)S(1)} %collective-permute-done.6.refs_0_, bf16[2,128,128]{2,1,0:T(8,128)(2,1)S(1)} %collective-permute-done.7.refs_1_, ...), custom_call_target="tpu_custom_call" | custom-call | flops 536870912 | bytes 2359296 | tf_op jit(solution)/shard_map/pallas_call | solution.py:29
  18.0 2.0 %collective-permute-done.8.refs_1_ = bf16[1,128,128]{2,1,0:T(8,128)(2,1)S(1)} collective-permute-done((bf16[1,128,128]{2,1,0:T(8,128)(2,1)S(1)}, bf16[1,128,128]{2,1,0:T(8,128)(2,1)S(1)}, u32[]{:S(2)}, u32[]{:S(2)}) %collective-permute-start.8) | collective-permute-done | bytes 32800 | tf_op jit(solution)/shard_map/ppermute | solution.py:81
  20.0 0.0 collective-permute-done.9.refs_4_
  20.0 0.6 %shard_map.99 = (bf16[128,256]{1,0:T(8,128)(2,1)S(1)}, bf16[512,128]{1,0:T(8,128)(2,1)S(1)}, bf16[128,256]{1,0:T(8,128)(2,1)S(1)}, bf16[128,128]{1,0:T(8,128)(2,...) custom-call(bf16[512,128]{1,0:T(8,128)(2,1)S(1)} %get-tuple-element.50.refs_0_, ...), custom_call_target="tpu_custom_call" | custom-call | flops 67108864 | bytes 1146880 | tf_op jit(solution)/shard_map/pallas_call | solution.py:29
  20.6 1.4 %collective-permute-start.10 = (bf16[128,256]{1,0:T(8,128)(2,1)S(1)}, bf16[128,256]{1,0:T(8,128)(2,1)S(1)}, u32[]{:S(2)}, u32[]{:S(2)}) collective-permute-start(bf16[128,256]{1,0:T(8,128)(2,1)S(1)} %get-tuple-element.59), channel_id=1, source_target_pairs={{0,16},{4,20},{8,24},{12,28},{16,0},{20,4},{24,8},{28,12},{1,17},{... | collective-permute-start | bytes 196616 | tf_op jit(solution)/shard_map/ppermute | solution.py:81
  22.0 2.7 %collective-permute-start.12 = (bf16[128,128]{1,0:T(8,128)(2,1)S(1)}, bf16[128,128]{1,0:T(8,128)(2,1)S(1)}, u32[]{:S(2)}, u32[]{:S(2)}) collective-permute-start(bf16[128,128]{1,0:T(8,128)(2,1)S(1)} %get-tuple-element.61), channel_id=1, source_target_pairs={{0,12},{4,8},{8,4},{12,0},{16,28},{20,24},{24,20},{28,16},{1,13},{... | collective-permute-start | bytes 98312 | tf_op jit(solution)/shard_map/ppermute | solution.py:81
  24.7 0.9 %collective-permute-start.14 = (bf16[128,128]{1,0:T(8,128)(2,1)S(1)}, bf16[128,128]{1,0:T(8,128)(2,1)S(1)}, u32[]{:S(2)}, u32[]{:S(2)}) collective-permute-start(bf16[128,128]{1,0:T(8,128)(2,1)S(1)} %get-tuple-element.63), channel_id=1, source_target_pairs={{0,4},{4,0},{8,12},{12,8},{16,20},{20,16},{24,28},{28,24},{1,5},{5... | collective-permute-start | bytes 98312 | tf_op jit(solution)/shard_map/ppermute | solution.py:81
  25.6 1.0 %shard_map.100 = (bf16[512,128]{1,0:T(8,128)(2,1)S(1)}, f32[512,128]{1,0:T(8,128)S(1)}, f32[512,256]{1,0:T(8,128)S(1)}) custom-call(bf16[2,512,128]{2,1,0:T(8,128)(2,1)S(1)} %get-tuple-element.44.refs_5_.kv_ref, bf16[4,128,256]{2,1,0:T(8,128)(2,1)S(1)} %copy-done.1, bf16[512,256]{1,0:T(8,128)(2,1)S(1)} %get-tuple-element.45.refs_7_.kf_ref, ...), custom_call_target="tpu_custom_call" | custom-call | flops 268435456 | bytes 2686976 | tf_op jit(solution)/shard_map/pallas_call | solution.py:29
  26.6 0.0 collective-permute-done.10.rest_0_
  26.6 0.6 %shard_map.101 = (bf16[3,128,128]{2,1,0:T(8,128)(2,1)S(1)}, bf16[3,128,128]{2,1,0:T(8,128)(2,1)S(1)}, bf16[3,128,128]{2,1,0:T(8,128)(2,1)S(1)}, bf16[3,128,128]{2,1,0:T(8,128)(2,1)S(1)}) custom-call(bf16[2,512,128]{2,1,0:T(8,128)(2,1)S(1)} %get-tuple-element.44.refs_5_.kv_ref, bf16[4,128,256]{2,1,0:T(8,128)(2,1)S(1)} %copy-done.1, ...), custom_call_target="tpu_custom_call" | custom-call | flops 100663296 | bytes 2162688 | tf_op jit(solution)/shard_map/pallas_call | solution.py:29
  27.2 0.0 collective-permute-done.12.refs_0_
  27.2 1.4 %collective-permute-done.13.refs_1_ = bf16[128,128]{1,0:T(8,128)(2,1)S(1)} collective-permute-done((bf16[128,128]{1,0:T(8,128)(2,1)S(1)}, bf16[128,128]{1,0:T(8,128)(2,1)S(1)}, u32[]{:S(2)}, u32[]{:S(2)}) %collective-permute-start.13) | collective-permute-done | bytes 32800 | tf_op jit(solution)/shard_map/ppermute | solution.py:81
  28.6 0.2 shard_map.102
  28.8 0.1 collective-permute-start.16
  28.9 2.4 %collective-permute-start.18 = (bf16[3,128,128]{2,1,0:T(8,128)(2,1)S(1)}, bf16[3,128,128]{2,1,0:T(8,128)(2,1)S(1)}, u32[]{:S(2)}, u32[]{:S(2)}) collective-permute-start(bf16[3,128,128]{2,1,0:T(8,128)(2,1)S(1)} %get-tuple-element.71), channel_id=1, source_target_pairs={{0,12},{4,8},{8,4},{12,0},{16,28},{20,24},{24,20},{28,16},{1,13},{... | collective-permute-start | bytes 294920 | tf_op jit(solution)/shard_map/ppermute | solution.py:81
  31.4 0.0 collective-permute-start.19
  31.4 0.4 shard_map.103
  31.7 0.2 collective-permute-start.15
  32.0 1.0 %collective-permute-start.17 = (bf16[128,512]{1,0:T(8,128)(2,1)S(1)}, bf16[128,512]{1,0:T(8,128)(2,1)S(1)}, u32[]{:S(2)}, u32[]{:S(2)}) collective-permute-start(bf16[128,512]{1,0:T(8,128)(2,1)S(1)} %shard_map.104), channel_id=1, source_target_pairs={{0,2},{1,3},{2,0},{3,1},{4,6},{5,7},{6,4},{7,5},{8,10},{9,11},{10,... | collective-permute-start | bytes 393224 | tf_op jit(solution)/shard_map/ppermute | solution.py:81
  33.0 0.7 %collective-permute-start.11 = (bf16[3,128,128]{2,1,0:T(8,128)(2,1)S(1)}, bf16[3,128,128]{2,1,0:T(8,128)(2,1)S(1)}, u32[]{:S(2)}, u32[]{:S(2)}) collective-permute-start(bf16[3,128,128]{2,1,0:T(8,128)(2,1)S(1)} %get-tuple-element.60), channel_id=1, source_target_pairs={{0,4},{4,0},{8,12},{12,8},{16,20},{20,16},{24,28},{28,24},{1,5},{5... | collective-permute-start | bytes 294920 | tf_op jit(solution)/shard_map/ppermute | solution.py:81
  33.7 1.6 %collective-permute-done.18.refs_0_ = bf16[3,128,128]{2,1,0:T(8,128)(2,1)S(1)} collective-permute-done((bf16[3,128,128]{2,1,0:T(8,128)(2,1)S(1)}, bf16[3,128,128]{2,1,0:T(8,128)(2,1)S(1)}, u32[]{:S(2)}, u32[]{:S(2)}) %collective-permute-start.18) | collective-permute-done | bytes 98336 | tf_op jit(solution)/shard_map/ppermute | solution.py:81
  35.4 1.2 %collective-permute-done.19.refs_1_ = bf16[3,128,128]{2,1,0:T(8,128)(2,1)S(1)} collective-permute-done((bf16[3,128,128]{2,1,0:T(8,128)(2,1)S(1)}, bf16[3,128,128]{2,1,0:T(8,128)(2,1)S(1)}, u32[]{:S(2)}, u32[]{:S(2)}) %collective-permute-start.19) | collective-permute-done | bytes 98336 | tf_op jit(solution)/shard_map/ppermute | solution.py:81
  36.6 0.8 %shard_map.105 = (bf16[128,512]{1,0:T(8,128)(2,1)}, bf16[128,512]{1,0:T(8,128)(2,1)}, bf16[128,512]{1,0:T(8,128)(2,1)}) custom-call(bf16[3,128,128]{2,1,0:T(8,128)(2,1)S(1)} %collective-permute-done.18.refs_0_, bf16[3,128,128]{2,1,0:T(8,128)(2,1)S(1)} %collective-permute-done.19.refs_1_, bf16[3,128,128]{2,1,0:T(8,128)(2,1)S(1)} %get-tuple-element.65.refs_5_.refs_2_), custom_call_target="tpu_custom_call" | custom-call | flops 800000000 | bytes 688128 | tf_op jit(solution)/shard_map/pallas_call | solution.py:29
  37.4 0.4 %collective-permute-done.11.got_ref = bf16[3,128,128]{2,1,0:T(8,128)(2,1)S(1)} collective-permute-done((bf16[3,128,128]{2,1,0:T(8,128)(2,1)S(1)}, bf16[3,128,128]{2,1,0:T(8,128)(2,1)S(1)}, u32[]{:S(2)}, u32[]{:S(2)}) %collective-permute-start.11) | collective-permute-done | bytes 98336 | tf_op jit(solution)/shard_map/ppermute | solution.py:81
  37.8 0.0 collective-permute-done.17.refs_2_
  37.8 0.7 %shard_map.106 = (bf16[128,512]{1,0:T(8,128)(2,1)}, bf16[128,512]{1,0:T(8,128)(2,1)}, bf16[128,512]{1,0:T(8,128)(2,1)}, bf16[128,512]{1,0:T(8,128)(2,1)}) custom-call(bf16[3,128,128]{2,1,0:T(8,128)(2,1)S(1)} %collective-permute-done.11.got_ref, ...), custom_call_target="tpu_custom_call", output_to_operand_aliasing={{1}: (4, {}), {2}: (5, {}), {3}: (6, {})} | custom-call | bytes 1409024 | tf_op jit(solution)/shard_map/pallas_call | solution.py:29
  (18 shorter events, 0.1 us)
Async XLA Ops:
  0.6 7.5 %collective-permute-start.3 = (bf16[128,512]{1,0:T(8,128)(2,1)}, bf16[128,512]{1,0:T(8,128)(2,1)S(1)}, u32[]{:S(2)}, u32[]{:S(2)}) collective-permute-start(bf16[128,512]{1,0:T(8,128)(2,1)} %refs_0_.1), channel_id=1, source_target_pairs={{0,2},{1,3},{2,0},{3,1},{4,6},{5,7},{6,4},{7,5},{8,10},{9,11},{10,... | collective-permute-start | bytes 393224 | tf_op jit(solution)/shard_map/ppermute | solution.py:81
  3.6 4.5 %collective-permute-start.4 = (bf16[128,512]{1,0:T(8,128)(2,1)}, bf16[128,512]{1,0:T(8,128)(2,1)S(1)}, u32[]{:S(2)}, u32[]{:S(2)}) collective-permute-start(bf16[128,512]{1,0:T(8,128)(2,1)} %refs_0_.1), channel_id=1, source_target_pairs={{0,1},{1,0},{2,3},{3,2},{4,5},{5,4},{6,7},{7,6},{8,9},{9,8},{10,11... | collective-permute-start | bytes 393224 | tf_op jit(solution)/shard_map/ppermute | solution.py:81
  4.6 8.3 %collective-permute-start = (bf16[2,128,128]{2,1,0:T(8,128)(2,1)S(1)}, bf16[2,128,128]{2,1,0:T(8,128)(2,1)S(1)}, u32[]{:S(2)}, u32[]{:S(2)}) collective-permute-start(bf16[2,128,128]{2,1,0:T(8,128)(2,1)S(1)} %get-tuple-element.40), channel_id=1, source_target_pairs={{0,12},{4,8},{8,4},{12,0},{16,28},{20,24},{24,20},{28,16},{1,13},{... | collective-permute-start | bytes 196616 | tf_op jit(solution)/shard_map/ppermute | solution.py:81
  7.2 5.7 %collective-permute-start.1 = (bf16[2,128,128]{2,1,0:T(8,128)(2,1)S(1)}, bf16[2,128,128]{2,1,0:T(8,128)(2,1)S(1)}, u32[]{:S(2)}, u32[]{:S(2)}) collective-permute-start(bf16[2,128,128]{2,1,0:T(8,128)(2,1)S(1)} %get-tuple-element.41), channel_id=1, source_target_pairs={{0,8},{4,12},{8,0},{12,4},{16,24},{20,28},{24,16},{28,20},{1,9},{5... | collective-permute-start | bytes 196616 | tf_op jit(solution)/shard_map/ppermute | solution.py:81
  7.6 1.6 %copy-start = (bf16[512,2048]{1,0:T(8,128)(2,1)S(1)}, bf16[512,2048]{1,0:T(8,128)(2,1)}, u32[]{:S(2)}) copy-start(bf16[512,2048]{1,0:T(8,128)(2,1)} %w_ref.3) | copy-start | bytes 6291460
  7.6 1.6 %copy-start.5 = (bf16[128,512]{1,0:T(8,128)(2,1)S(1)}, bf16[128,512]{1,0:T(8,128)(2,1)}, u32[]{:S(2)}) copy-start(bf16[128,512]{1,0:T(8,128)(2,1)} %refs_0_.1) | copy-start | bytes 393220
  7.6 5.3 %collective-permute-start.2 = (bf16[3,128,128]{2,1,0:T(8,128)(2,1)S(1)}, bf16[3,128,128]{2,1,0:T(8,128)(2,1)S(1)}, u32[]{:S(2)}, u32[]{:S(2)}) collective-permute-start(bf16[3,128,128]{2,1,0:T(8,128)(2,1)S(1)} %get-tuple-element.42), channel_id=1, source_target_pairs={{0,4},{4,0},{8,12},{12,8},{16,20},{20,16},{24,28},{28,24},{1,5},{5... | collective-permute-start | bytes 294920 | tf_op jit(solution)/shard_map/ppermute | solution.py:81
  8.1 1.8 %collective-permute-start.5 = (bf16[128,512]{1,0:T(8,128)(2,1)S(1)}, bf16[128,512]{1,0:T(8,128)(2,1)S(1)}, u32[]{:S(2)}, u32[]{:S(2)}) collective-permute-start(bf16[128,512]{1,0:T(8,128)(2,1)S(1)} %collective-permute-done.3.refs_1_), channel_id=1, source_target_pairs={{0,1},{1,0},{2,3},{3,2},{4,5},{5,4},{6,7},{7,6},{8,9},{9,8},{10,11... | collective-permute-start | bytes 393224 | tf_op jit(solution)/shard_map/ppermute | solution.py:81
  9.2 0.9 %copy-start.2 = (bf16[128,512]{1,0:T(8,128)(2,1)S(1)}, bf16[128,512]{1,0:T(8,128)(2,1)}, u32[]{:S(2)}) copy-start(bf16[128,512]{1,0:T(8,128)(2,1)} %refs_3_.5) | copy-start | bytes 393220
  9.2 3.7 %copy-start.1 = (bf16[4,128,256]{2,1,0:T(8,128)(2,1)S(1)}, bf16[4,128,256]{2,1,0:T(8,128)(2,1)}, u32[]{:S(2)}) copy-start(bf16[4,128,256]{2,1,0:T(8,128)(2,1)} %om_ref.3) | copy-start | bytes 786436
  9.2 3.7 %copy-start.3 = (bf16[128,512]{1,0:T(8,128)(2,1)S(1)}, bf16[128,512]{1,0:T(8,128)(2,1)}, u32[]{:S(2)}) copy-start(bf16[128,512]{1,0:T(8,128)(2,1)} %refs_3_.4) | copy-start | bytes 393220
  9.2 3.7 %copy-start.4 = (bf16[128,512]{1,0:T(8,128)(2,1)S(1)}, bf16[128,512]{1,0:T(8,128)(2,1)}, u32[]{:S(2)}) copy-start(bf16[128,512]{1,0:T(8,128)(2,1)} %refs_4_.2) | copy-start | bytes 393220
  10.5 6.7 %collective-permute-start.6 = (bf16[2,128,128]{2,1,0:T(8,128)(2,1)S(1)}, bf16[2,128,128]{2,1,0:T(8,128)(2,1)S(1)}, u32[]{:S(2)}, u32[]{:S(2)}) collective-permute-start(bf16[2,128,128]{2,1,0:T(8,128)(2,1)S(1)} %get-tuple-element.46), channel_id=1, source_target_pairs={{0,12},{4,8},{8,4},{12,0},{16,28},{20,24},{24,20},{28,16},{1,13},{... | collective-permute-start | bytes 196616 | tf_op jit(solution)/shard_map/ppermute | solution.py:81
  12.5 5.0 %collective-permute-start.7 = (bf16[2,128,128]{2,1,0:T(8,128)(2,1)S(1)}, bf16[2,128,128]{2,1,0:T(8,128)(2,1)S(1)}, u32[]{:S(2)}, u32[]{:S(2)}) collective-permute-start(bf16[2,128,128]{2,1,0:T(8,128)(2,1)S(1)} %get-tuple-element.47), channel_id=1, source_target_pairs={{0,8},{4,12},{8,0},{12,4},{16,24},{20,28},{24,16},{28,20},{1,9},{5... | collective-permute-start | bytes 196616 | tf_op jit(solution)/shard_map/ppermute | solution.py:81
  13.4 6.6 %collective-permute-start.9 = (bf16[128,256]{1,0:T(8,128)(2,1)S(1)}, bf16[128,256]{1,0:T(8,128)(2,1)S(1)}, u32[]{:S(2)}, u32[]{:S(2)}) collective-permute-start(bf16[128,256]{1,0:T(8,128)(2,1)S(1)} %get-tuple-element.53), channel_id=1, source_target_pairs={{0,16},{4,20},{8,24},{12,28},{16,0},{20,4},{24,8},{28,12},{1,17},{... | collective-permute-start | bytes 196616 | tf_op jit(solution)/shard_map/ppermute | solution.py:81
  16.1 3.9 %collective-permute-start.8 = (bf16[1,128,128]{2,1,0:T(8,128)(2,1)S(1)}, bf16[1,128,128]{2,1,0:T(8,128)(2,1)S(1)}, u32[]{:S(2)}, u32[]{:S(2)}) collective-permute-start(bf16[1,128,128]{2,1,0:T(8,128)(2,1)S(1)} %get-tuple-element.51), channel_id=1, source_target_pairs={{0,4},{4,0},{8,12},{12,8},{16,20},{20,16},{24,28},{28,24},{1,5},{5... | collective-permute-start | bytes 98312 | tf_op jit(solution)/shard_map/ppermute | solution.py:81
  20.6 5.9 %collective-permute-start.10 = (bf16[128,256]{1,0:T(8,128)(2,1)S(1)}, bf16[128,256]{1,0:T(8,128)(2,1)S(1)}, u32[]{:S(2)}, u32[]{:S(2)}) collective-permute-start(bf16[128,256]{1,0:T(8,128)(2,1)S(1)} %get-tuple-element.59), channel_id=1, source_target_pairs={{0,16},{4,20},{8,24},{12,28},{16,0},{20,4},{24,8},{28,12},{1,17},{... | collective-permute-start | bytes 196616 | tf_op jit(solution)/shard_map/ppermute | solution.py:81
  22.0 5.1 %collective-permute-start.12 = (bf16[128,128]{1,0:T(8,128)(2,1)S(1)}, bf16[128,128]{1,0:T(8,128)(2,1)S(1)}, u32[]{:S(2)}, u32[]{:S(2)}) collective-permute-start(bf16[128,128]{1,0:T(8,128)(2,1)S(1)} %get-tuple-element.61), channel_id=1, source_target_pairs={{0,12},{4,8},{8,4},{12,0},{16,28},{20,24},{24,20},{28,16},{1,13},{... | collective-permute-start | bytes 98312 | tf_op jit(solution)/shard_map/ppermute | solution.py:81
  24.7 3.9 %collective-permute-start.13 = (bf16[128,128]{1,0:T(8,128)(2,1)S(1)}, bf16[128,128]{1,0:T(8,128)(2,1)S(1)}, u32[]{:S(2)}, u32[]{:S(2)}) collective-permute-start(bf16[128,128]{1,0:T(8,128)(2,1)S(1)} %get-tuple-element.62), channel_id=1, source_target_pairs={{0,8},{4,12},{8,0},{12,4},{16,24},{20,28},{24,16},{28,20},{1,9},{5... | collective-permute-start | bytes 98312 | tf_op jit(solution)/shard_map/ppermute | solution.py:81
  24.7 3.9 %collective-permute-start.14 = (bf16[128,128]{1,0:T(8,128)(2,1)S(1)}, bf16[128,128]{1,0:T(8,128)(2,1)S(1)}, u32[]{:S(2)}, u32[]{:S(2)}) collective-permute-start(bf16[128,128]{1,0:T(8,128)(2,1)S(1)} %get-tuple-element.63), channel_id=1, source_target_pairs={{0,4},{4,0},{8,12},{12,8},{16,20},{20,16},{24,28},{28,24},{1,5},{5... | collective-permute-start | bytes 98312 | tf_op jit(solution)/shard_map/ppermute | solution.py:81
  28.8 3.2 %collective-permute-start.16 = (bf16[128,512]{1,0:T(8,128)(2,1)S(1)}, bf16[128,512]{1,0:T(8,128)(2,1)S(1)}, u32[]{:S(2)}, u32[]{:S(2)}) collective-permute-start(bf16[128,512]{1,0:T(8,128)(2,1)S(1)} %get-tuple-element.70), channel_id=1, source_target_pairs={{0,1},{1,0},{2,3},{3,2},{4,5},{5,4},{6,7},{7,6},{8,9},{9,8},{10,11... | collective-permute-start | bytes 393224 | tf_op jit(solution)/shard_map/ppermute | solution.py:81
  28.9 6.4 %collective-permute-start.18 = (bf16[3,128,128]{2,1,0:T(8,128)(2,1)S(1)}, bf16[3,128,128]{2,1,0:T(8,128)(2,1)S(1)}, u32[]{:S(2)}, u32[]{:S(2)}) collective-permute-start(bf16[3,128,128]{2,1,0:T(8,128)(2,1)S(1)} %get-tuple-element.71), channel_id=1, source_target_pairs={{0,12},{4,8},{8,4},{12,0},{16,28},{20,24},{24,20},{28,16},{1,13},{... | collective-permute-start | bytes 294920 | tf_op jit(solution)/shard_map/ppermute | solution.py:81
  31.4 5.2 %collective-permute-start.19 = (bf16[3,128,128]{2,1,0:T(8,128)(2,1)S(1)}, bf16[3,128,128]{2,1,0:T(8,128)(2,1)S(1)}, u32[]{:S(2)}, u32[]{:S(2)}) collective-permute-start(bf16[3,128,128]{2,1,0:T(8,128)(2,1)S(1)} %get-tuple-element.72), channel_id=1, source_target_pairs={{0,8},{4,12},{8,0},{12,4},{16,24},{20,28},{24,16},{28,20},{1,9},{5... | collective-permute-start | bytes 294920 | tf_op jit(solution)/shard_map/ppermute | solution.py:81
  31.7 6.0 %collective-permute-start.15 = (bf16[128,512]{1,0:T(8,128)(2,1)S(1)}, bf16[128,512]{1,0:T(8,128)(2,1)S(1)}, u32[]{:S(2)}, u32[]{:S(2)}) collective-permute-start(bf16[128,512]{1,0:T(8,128)(2,1)S(1)} %get-tuple-element.68), channel_id=1, source_target_pairs={{0,1},{1,0},{2,3},{3,2},{4,5},{5,4},{6,7},{7,6},{8,9},{9,8},{10,11... | collective-permute-start | bytes 393224 | tf_op jit(solution)/shard_map/ppermute | solution.py:81
  32.0 5.8 %collective-permute-start.17 = (bf16[128,512]{1,0:T(8,128)(2,1)S(1)}, bf16[128,512]{1,0:T(8,128)(2,1)S(1)}, u32[]{:S(2)}, u32[]{:S(2)}) collective-permute-start(bf16[128,512]{1,0:T(8,128)(2,1)S(1)} %shard_map.104), channel_id=1, source_target_pairs={{0,2},{1,3},{2,0},{3,1},{4,6},{5,7},{6,4},{7,5},{8,10},{9,11},{10,... | collective-permute-start | bytes 393224 | tf_op jit(solution)/shard_map/ppermute | solution.py:81
  33.0 4.8 %collective-permute-start.11 = (bf16[3,128,128]{2,1,0:T(8,128)(2,1)S(1)}, bf16[3,128,128]{2,1,0:T(8,128)(2,1)S(1)}, u32[]{:S(2)}, u32[]{:S(2)}) collective-permute-start(bf16[3,128,128]{2,1,0:T(8,128)(2,1)S(1)} %get-tuple-element.60), channel_id=1, source_target_pairs={{0,4},{4,0},{8,12},{12,8},{16,20},{20,16},{24,28},{28,24},{1,5},{5... | collective-permute-start | bytes 294920 | tf_op jit(solution)/shard_map/ppermute | solution.py:81
